TPU v7x, 32 devices: a whole 2x2x4 slice. The times are simulated.
32 devices in a mesh: req: 8 (over y, x, core), head: 4 (over z).
Axes of the slice: x: 2, y: 2, z: 4, core: 2. Of those that a mesh axis runs over, the one named last changes fastest.
Arguments:
- tokens: bfloat16 [32, 7168], P('req'), may hold values from -6 to 6
- norm_gain: float32 [7168], replicated, may hold values from 0.5 to 1.5
- norm_shift: float32 [7168], replicated, may hold values from -3 to 3
- qkv_weight: bfloat16 [7168, 56, 384], P('req', 'head'), may hold values from -0.0625 to 0.0625
- qkv_bias: float32 [56, 384], P('head'), may hold values from -3 to 3
- out_weight: bfloat16 [56, 128, 7168], P('head', 'req'), may hold values from -0.09375 to 0.09375
- out_bias: float32 [7168], replicated, may hold values from -3 to 3
- key_pool: bfloat16 [160, 64, 7168], P('req', None, 'head'), may hold values from -256 to 256
- value_pool: bfloat16 [160, 64, 7168], P('req', None, 'head'), may hold values from -6 to 6
- lengths: int32 [32], P('req'), may hold values from 1 to 1023, as said below
- page_table: int32 [32, 16], P('req'), may hold values from 0 to 19, as said below
- new_slot: int32 [32], P('req'), may hold values from 0 to 31, as said below
- new_page: int32 [32], P('req'), may hold values from 0 to 19, as said below
Outputs:
- hidden_out: bfloat16 [32, 7168], P('req', 'head')
- key_out: bfloat16 [160, 64, 7168], P('req', None, 'head')
- value_out: bfloat16 [160, 64, 7168], P('req', None, 'head')
Inputs may be any that keep to these rules, and one draw needn't show every extreme that they name: `lengths`: A request with length under 64 uses one page; the others use 16 pages. A device holds at most one request of length 64 or more. `page_table`: local pages of the request's device; the used entries (the first (lengths + 64) // 64 of a row) of all requests of one device are distinct. `new_slot`: A permutation of the slots. Every device has exactly one request whose new slot lies on another device, and it has length under 64; every device receives exactly one such request into the slot its own leaving request frees; the others keep their slot. `new_page`: for a moving request, a local page of its new device that no request uses before the move; for the others, page_table[s, 0].
All inputs are finite; a program needn't handle non-finite values.
Results may differ from a plain program's by a relative error of at most 0.012.
Values may be sent and summed in bfloat16 or wider, within the bound.
No kernel may reach another device: no remote copies, remote signals or barrier semaphores. Data moves between devices by JAX's collectives and lax.ppermute only.
A program may use at most 192 MiB of HBM per device.

v0:
```python
import jax
import jax.numpy as jnp
from jax import lax
from jax.sharding import PartitionSpec as P

EPSILON = 1e-05


def layer_norm(tokens, norm_gain, norm_shift):
    values_f = tokens.astype(jnp.float32)
    average = jnp.mean(values_f, axis=1, keepdims=True)
    centered = values_f - average
    variance = jnp.mean(centered * centered, axis=1, keepdims=True)
    return (centered * lax.rsqrt(variance + EPSILON) * norm_gain + norm_shift).astype(jnp.bfloat16)


def regroup_heads(attended):
    return lax.all_to_all(attended, "req", split_axis=2, concat_axis=0, tiled=True)


def body(
    tokens,
    norm_gain,
    norm_shift,
    qkv_weight,
    qkv_bias,
    out_weight,
    out_bias,
    key_pool,
    value_pool,
    lengths,
    page_table,
    new_slot,
    new_page,
):
    groups = lax.axis_size("req")
    head_groups = lax.axis_size("head")
    here = lax.axis_index("req")
    column_block = lax.axis_index("head")
    slot_count = tokens.shape[0]
    total_slots = slot_count * groups
    page_count = key_pool.shape[0]
    page_size = key_pool.shape[1]
    feature_width = key_pool.shape[2]
    local_heads = qkv_weight.shape[1]
    head_size = qkv_weight.shape[2] // 3
    head_share = out_weight.shape[1]
    max_pages = page_table.shape[1]
    slot_range = jnp.arange(slot_count, dtype=jnp.int32)
    normed = layer_norm(tokens, norm_gain, norm_shift)
    spread = lax.all_to_all(normed, "req", split_axis=1, concat_axis=0, tiled=True)
    slot_all, page_all, length_all = (
        lax.all_gather(new_slot, "req", axis=0, tiled=True),
        lax.all_gather(new_page, "req", axis=0, tiled=True),
        lax.all_gather(lengths, "req", axis=0, tiled=True),
    )
    anchor = (
        jnp.zeros((total_slots,), jnp.int32)
        .at[slot_all]
        .set(jnp.arange(total_slots, dtype=jnp.int32))
    )
    spread_new = spread[anchor]
    projected = (
        lax.psum_scatter(
            jnp.einsum("td,dhc->thc", spread_new, qkv_weight, preferred_element_type=jnp.float32),
            "req",
            scatter_dimension=0,
            tiled=True,
        )
        + qkv_bias
    )
    query = (projected[:, :, :head_size] * head_size ** (-0.5)).astype(jnp.bfloat16)
    key_new = projected[:, :, head_size : 2 * head_size].astype(jnp.bfloat16)
    value_new = projected[:, :, 2 * head_size :].astype(jnp.bfloat16)
    token_part = lax.dynamic_slice_in_dim(tokens, column_block * feature_width, feature_width, 1)
    target_device = new_slot // slot_count
    moving = target_device != here
    single = jnp.sum(jnp.where(moving, slot_range, 0))
    single_page = page_table[single, 0]
    arrived_keys, arrived_values, arrived_rows = (
        lax.all_gather(key_pool[single_page][None], "req", axis=0, tiled=True),
        lax.all_gather(value_pool[single_page][None], "req", axis=0, tiled=True),
        lax.all_gather(token_part[single][None], "req", axis=0, tiled=True),
    )
    mine = here * slot_count + slot_range
    source_slot = anchor[mine]
    source_device = source_slot // slot_count
    incoming = source_device != here
    dest_page = page_all[source_slot]
    write_index = jnp.where(incoming, dest_page, page_count)
    key_moved = key_pool.at[write_index].set(arrived_keys[source_device], mode="drop")
    value_moved = value_pool.at[write_index].set(arrived_values[source_device], mode="drop")
    residual = jnp.where(incoming[:, None], arrived_rows[source_device], token_part).astype(
        jnp.float32
    )
    row_page = jnp.where(incoming[:, None], dest_page[:, None], page_table)
    length_new = length_all[source_slot]
    page_slot = jnp.take_along_axis(row_page, (length_new // page_size)[:, None], axis=1)[:, 0]
    offset = length_new % page_size
    key_out = key_moved.at[page_slot, offset].set(key_new.reshape(slot_count, feature_width))
    value_out = value_moved.at[page_slot, offset].set(value_new.reshape(slot_count, feature_width))
    block_pages = min(max_pages, max(1, 512 // page_size))
    block_keys = block_pages * page_size
    positions = jnp.arange(max_pages * page_size, dtype=jnp.int32)
    valid = (positions[None, :] <= length_new[:, None])[:, None, :]
    turns = (jnp.max(length_new // page_size + 1) + block_pages - 1) // block_pages

    def fetch(pool, block_index):
        pages_here = lax.dynamic_slice_in_dim(row_page, block_index * block_pages, block_pages, 1)
        return pool[pages_here].reshape(slot_count, block_keys, local_heads, head_size)

    def score_block(block_index, buffer):
        block_scores = jnp.einsum(
            "shc,sthc->sht", query, fetch(key_out, block_index), preferred_element_type=jnp.float32
        )
        return lax.dynamic_update_slice_in_dim(buffer, block_scores, block_index * block_keys, 2)

    start_scores = jnp.full((slot_count, local_heads, max_pages * page_size), -1e30, jnp.float32)
    scores = lax.fori_loop(0, turns, score_block, start_scores)
    masked = jnp.where(valid, scores, -1e30)
    peak = jnp.max(masked, axis=2, keepdims=True)
    weights = jnp.where(valid, jnp.exp(masked - peak), 0.0)
    denom = jnp.sum(weights, axis=2)
    probs = weights.astype(jnp.bfloat16)

    def mix_block(block_index, summed):
        block_probs = lax.dynamic_slice_in_dim(probs, block_index * block_keys, block_keys, 2)
        return summed + jnp.einsum(
            "sht,sthc->shc",
            block_probs,
            fetch(value_out, block_index),
            preferred_element_type=jnp.float32,
        )

    mixed = lax.fori_loop(
        0, turns, mix_block, jnp.zeros((slot_count, local_heads, head_size), jnp.float32)
    )
    attended = (mixed / denom[:, :, None]).astype(jnp.bfloat16)
    bias_part = lax.dynamic_slice_in_dim(out_bias, column_block * feature_width, feature_width, 0)
    weight_tiles = out_weight.reshape(local_heads, head_share, head_groups, feature_width)
    gathered = regroup_heads(attended)
    token_tiles = gathered.reshape(groups, slot_count, local_heads, head_share)
    block_total = slot_count * lax.axis_size(("req", "head")) // slot_count
    index = jnp.arange(block_total, dtype=jnp.int32)
    chosen_tokens = jnp.take(token_tiles, index // head_groups, axis=0)
    chosen_weight = jnp.take(weight_tiles, index % head_groups, axis=2)
    term = jnp.einsum(
        "bsjc,jcbf->bsf", chosen_tokens, chosen_weight, preferred_element_type=jnp.float32
    )
    summed_out = lax.psum_scatter(
        term.reshape(slot_count * lax.axis_size(("req", "head")), feature_width),
        ("req", "head"),
        scatter_dimension=0,
        tiled=True,
    )
    hidden_out = (summed_out + bias_part + residual).astype(jnp.bfloat16)
    return (hidden_out, key_out, value_out)


def solution(mesh):
    in_specs = (
        P("req", None),
        P(),
        P(),
        P("req", "head", None),
        P("head", None),
        P("head", "req", None),
        P(),
        P("req", None, "head"),
        P("req", None, "head"),
        P("req"),
        P("req", None),
        P("req"),
        P("req"),
    )
    out_specs = (P("req", "head"), P("req", None, "head"), P("req", None, "head"))
    return jax.shard_map(body, mesh=mesh, in_specs=in_specs, out_specs=out_specs, check_vma=False)
```

profile of v0, /device:TPU:0, one launch (start us, length us, event | category | flops | bytes accessed | tf_op | source)
XLA Modules:
  0.0 409.3 jit_solution(10917934267618278864)
XLA Ops:
  7.3 5.0 %copy.115 = bf16[20,64,1792]{2,1,0:T(8,128)(2,1)} copy(bf16[20,64,1792]{2,1,0:T(8,128)(2,1)} %param.24) | data formatting | bytes 9175040
  12.3 2.1 copy.116
  14.9 0.7 fusion.29
  15.6 5.2 %all-to-all-start = ((bf16[4,8,896]{2,0,1:T(4,128)(2,1)}), bf16[4,8,896]{2,0,1:T(4,128)(2,1)S(1)}, u32[]{:S(2)}, u32[]{:S(2)}) async-start(bf16[4,8,896]{2,0,1:T(4,128)(2,1)} %bitcast.18), calls=%async_computation | async-start | bytes 114688 | tf_op jit(solution)/shard_map/all_to_all | solution.py:51
  22.8 8.4 %all-reduce.5 = (s32[32]{0:T(128)S(1)}, s32[32]{0:T(128)S(1)}, s32[32]{0:T(128)S(1)}) all-reduce(s32[32]{0:T(128)S(1)} %dynamic-update-slice, s32[32]{0:T(128)S(1)} %dynamic-update-slice.1, s32[32]{0:T(128)S(1)} %dynamic-update-slice.2), channel_id=1, replica_groups=mesh['req'=8,'head'=4] {'req'}, use_global_device_ids=true, to_apply=%add | all-reduce | flops 96 | bytes 768
  31.3 0.7 scatter_custom_fusion
  32.7 6.0 %fusion.30 = f32[32,14,384]{2,0,1:T(8,128)} fusion(bf16[896,14,384]{2,0,1:T(8,128)(2,1)} %param.20, bf16[32,896]{1,0:T(8,128)(2,1)S(1)} %gather_fusion.6), kind=kOutput, calls=%fused_computation.57 | convolution fusion | flops 308281344 | bytes 10379264 | tf_op jit(solution)/shard_map/td,dhc->thc/dot_general | solution.py:65
  43.8 1.6 constant_dynamic-slice_fusion.1
  45.5 1.7 constant_dynamic-slice_fusion
  47.2 0.6 gather_fusion.2
  47.9 0.6 gather_fusion.3
  48.6 0.6 add_reduce_fusion
  50.7 0.6 gather_fusion.11
  52.0 41.8 %all-reduce.9.cloned.1.call-done = f32[32,14,384]{2,0,1:T(8,128)} async-done(((f32[32,14,384]{2,0,1:T(8,128)}), f32[32,14,384]{2,0,1:T(8,128)}) %all-reduce.9.cloned.1.call-update) | async-done | bytes 688144
  93.8 1.0 fusion.49
  94.8 27.2 %all-gather.4.cloned.1.call-done = bf16[8,64,1792]{2,1,0:T(8,128)(2,1)} async-done(((bf16[1,64,1792]{2,1,0:T(8,128)(2,1)}), bf16[8,64,1792]{2,1,0:T(8,128)(2,1)}) %all-gather.4.cloned.1.call-update) | async-done | bytes 1835024 | tf_op jit(solution)/shard_map/all_gather | solution.py:81
  122.0 2.1 gather_fusion.5
  124.1 2.6 scatter_fusion
  126.7 2.3 scatter_fusion.1
  129.0 51.9 %while.20 = (s32[]{:T(128)}, f32[4,14,1024]{2,1,0:T(8,128)S(1)}, s32[]{:T(128)}, s32[4,16]{1,0:T(4,128)S(1)}, bf16[20,64,1792]{2,1,0:T(8,128)(2,1)}, /*index=5*/...) while((s32[]{:T(128)}, f32[4,14,1024]{2,1,0:T(8,128)S(1)}, ...), condition=%wide.region_9.10_spmd, body=%wide.region_8.9_spmd.sunk | while | flops 7341162 | bytes 37080024 | solution.py:119
  129.2 6.4 %gather_fusion = bf16[32,64,1792]{2,1,0:T(8,128)(2,1)} fusion(bf16[20,64,1792]{2,1,0:T(8,128)(2,1)} %get-tuple-element.247, s32[1024]{0:T(1024)S(1)} %pad_clamp_fusion.10), kind=kCustom, calls=%fused_computation.clone.1 | custom fusion | bytes 14680192 | tf_op jit(solution)/shard_map/while/body/gather | solution.py:110
  135.7 13.5 %reshape.627 = bf16[4,512,14,128]{3,2,1,0:T(8,128)(2,1)} reshape(bf16[32,64,1792]{2,1,0:T(8,128)(2,1)} %gather_fusion) | data formatting | bytes 14680064 | tf_op jit(solution)/shard_map/while/body/reshape | solution.py:110
  149.2 5.8 %fusion.61 = f32[4,14,1,512]{3,2,1,0:T(1,128)S(1)} fusion(bf16[4,512,14,128]{3,2,1,0:T(8,128)(2,1)} %reshape.627, bf16[4,14,128,1]{2,1,0,3:T(8,128)(2,1)S(1)} %bitcast.122), kind=kOutput, calls=%fused_computation.17.clone.1 | convolution fusion | flops 7340032 | bytes 7469056 | tf_op jit(solution)/shard_map/while/body/shc,sthc->sht/dot_general | solution.py:113
  155.3 6.3 %gather_fusion = bf16[32,64,1792]{2,1,0:T(8,128)(2,1)} fusion(bf16[20,64,1792]{2,1,0:T(8,128)(2,1)} %get-tuple-element.247, s32[1024]{0:T(1024)S(1)} %pad_clamp_fusion.10), kind=kCustom, calls=%fused_computation.clone.1 | custom fusion | bytes 14680192 | tf_op jit(solution)/shard_map/while/body/gather | solution.py:110
  161.6 13.5 %reshape.627 = bf16[4,512,14,128]{3,2,1,0:T(8,128)(2,1)} reshape(bf16[32,64,1792]{2,1,0:T(8,128)(2,1)} %gather_fusion) | data formatting | bytes 14680064 | tf_op jit(solution)/shard_map/while/body/reshape | solution.py:110
  175.1 5.8 %fusion.61 = f32[4,14,1,512]{3,2,1,0:T(1,128)S(1)} fusion(bf16[4,512,14,128]{3,2,1,0:T(8,128)(2,1)} %reshape.627, bf16[4,14,128,1]{2,1,0,3:T(8,128)(2,1)S(1)} %bitcast.122), kind=kOutput, calls=%fused_computation.17.clone.1 | convolution fusion | flops 7340032 | bytes 7469056 | tf_op jit(solution)/shard_map/while/body/shc,sthc->sht/dot_general | solution.py:113
  181.0 2.1 gather_fusion.7
  183.1 2.6 scatter_fusion.2
  185.9 2.3 scatter_fusion.3
  188.2 51.3 %while.21 = (s32[]{:T(128)}, f32[4,14,128]{2,1,0:T(8,128)S(1)}, s32[]{:T(128)}, bf16[4,14,1024]{2,1,0:T(8,128)(2,1)S(1)}, s32[4,16]{1,0:T(4,128)S(1)}, /*index=5...) while((s32[]{:T(128)}, f32[4,14,128]{2,1,0:T(8,128)S(1)}, ...), condition=%wide.region_14.15_spmd, body=%wide.region_13.14_spmd.sunk | while | flops 7348330 | bytes 36991960 | solution.py:135
  188.4 6.3 %gather_fusion.1 = bf16[32,64,1792]{2,1,0:T(8,128)(2,1)} fusion(bf16[20,64,1792]{2,1,0:T(8,128)(2,1)} %get-tuple-element.284, s32[1024]{0:T(1024)S(1)} %pad_clamp_fusion.11), kind=kCustom, calls=%fused_computation.1.clone.1 | custom fusion | bytes 14680192 | tf_op jit(solution)/shard_map/while/body/gather | solution.py:110
  194.7 13.5 %reshape.631 = bf16[4,512,14,128]{3,2,1,0:T(8,128)(2,1)} reshape(bf16[32,64,1792]{2,1,0:T(8,128)(2,1)} %gather_fusion.1) | data formatting | bytes 14680064 | tf_op jit(solution)/shard_map/while/body/reshape | solution.py:110
  208.2 5.6 %fusion.64 = f32[4,14,1,128]{3,2,1,0:T(1,128)S(1)} fusion(bf16[4,512,14,128]{3,2,1,0:T(8,128)(2,1)} %reshape.631, bf16[4,14,512,1]{2,1,0,3:T(8,128)(2,1)S(1)} %dynamic-slice_bitcast_fusion.3), kind=kOutput, calls=%fused_computation.23.clone.1 | convolution fusion | flops 7340032 | bytes 7426048 | tf_op jit(solution)/shard_map/while/body/sht,sthc->shc/dot_general | solution.py:128
  214.0 6.3 %gather_fusion.1 = bf16[32,64,1792]{2,1,0:T(8,128)(2,1)} fusion(bf16[20,64,1792]{2,1,0:T(8,128)(2,1)} %get-tuple-element.284, s32[1024]{0:T(1024)S(1)} %pad_clamp_fusion.11), kind=kCustom, calls=%fused_computation.1.clone.1 | custom fusion | bytes 14680192 | tf_op jit(solution)/shard_map/while/body/gather | solution.py:110
  220.3 13.5 %reshape.631 = bf16[4,512,14,128]{3,2,1,0:T(8,128)(2,1)} reshape(bf16[32,64,1792]{2,1,0:T(8,128)(2,1)} %gather_fusion.1) | data formatting | bytes 14680064 | tf_op jit(solution)/shard_map/while/body/reshape | solution.py:110
  233.9 5.6 %fusion.64 = f32[4,14,1,128]{3,2,1,0:T(1,128)S(1)} fusion(bf16[4,512,14,128]{3,2,1,0:T(8,128)(2,1)} %reshape.631, bf16[4,14,512,1]{2,1,0,3:T(8,128)(2,1)S(1)} %dynamic-slice_bitcast_fusion.3), kind=kOutput, calls=%fused_computation.23.clone.1 | convolution fusion | flops 7340032 | bytes 7426048 | tf_op jit(solution)/shard_map/while/body/sht,sthc->shc/dot_general | solution.py:128
  239.7 0.8 reshape.614
  240.5 3.3 all-to-all-start.1
  243.9 2.1 copy.67
  246.1 10.0 %gather_fusion.9 = bf16[32,14,16,1792]{3,2,1,0:T(8,128)(2,1)} fusion(bf16[14,16,4,1792]{3,1,2,0:T(8,128)(2,1)S(1)} %bitcast.115, s32[1024]{0:T(1024)S(1)} %pad_clamp_fusion.2), kind=kCustom, calls=%fused_computation.9 | custom fusion | bytes 51380352 | tf_op jit(solution)/shard_map/jit(_take)/gather | solution.py:146
  256.7 1.0 gather_fusion.8
  257.7 11.4 %fusion.12 = f32[32,4,1792]{2,1,0:T(4,128)S(1)} fusion(bf16[32,14,16,1792]{3,2,1,0:T(8,128)(2,1)} %gather_fusion.9, pred[32]{0:T(512)(128)(4,1)S(1)} %get-tuple-element.139, bf16[32,4,14,16]{3,1,2,0:T(4,128)(2,1)S(1)} %gather_fusion.8, pred[32]{0:T(512)(128)(4,1)S(1)} %get-tuple-element.140), kind=kOutput, calls=%fused_computation.37 | convolution fusion | flops 115634176 | bytes 26665024 | tf_op jit(solution)/shard_map/bsjc,jcbf->bsf/dot_general | solution.py:147
  269.1 1.3 reshape.445
  270.4 0.8 dynamic-slice_bitcast_fusion.1
  271.2 9.6 %all-gather = bf16[8,1,1792]{2,1,0:T(2,128)(2,1)S(1)} all-gather(bf16[1,1,1792]{2,1,0:T(2,128)(2,1)S(1)} %dynamic-slice_bitcast_fusion.1), channel_id=1, replica_groups=mesh['req'=8,'head'=4] {'req'}, dimensions={0}, use_global_device_ids=true | all-gather | bytes 32256 | tf_op jit(solution)/shard_map/all_gather | solution.py:83
  281.3 0.8 dynamic_slice.30
  282.1 119.2 %all-reduce.11.cloned.1.call-done = f32[128,1792]{1,0:T(8,128)} async-done(((f32[128,1792]{1,0:T(8,128)}), f32[128,1792]{1,0:T(8,128)}) %all-reduce.11.cloned.1.call-update) | async-done | bytes 917520
  401.3 1.5 fusion.34
  (103 shorter events, 7.2 us)
Async XLA Ops:
  7.2 13.7 %copy-start.7 = (u32[32]{0:T(128)S(1)}, u32[32]{0:T(128)}, u32[]{:S(2)}) copy-start(u32[32]{0:T(128)} %constant.273) | copy-start | bytes 388
  7.2 7.3 %copy-start.1 = (bf16[4,7168]{1,0:T(4,128)(2,1)S(1)}, bf16[4,7168]{1,0:T(4,128)(2,1)}, u32[]{:S(2)}) copy-start(bf16[4,7168]{1,0:T(4,128)(2,1)} %param.17) | copy-start | bytes 172036
  7.2 7.7 %copy-start.3 = (f32[7168]{0:T(1024)S(1)}, f32[7168]{0:T(1024)}, u32[]{:S(2)}) copy-start(f32[7168]{0:T(1024)} %param.18) | copy-start | bytes 86020
  7.2 7.7 %copy-start.2 = (f32[7168]{0:T(1024)S(1)}, f32[7168]{0:T(1024)}, u32[]{:S(2)}) copy-start(f32[7168]{0:T(1024)} %param.19) | copy-start | bytes 86020
  7.2 5.1 %copy-start = (bf16[20,64,1792]{2,1,0:T(8,128)(2,1)S(1)}, bf16[20,64,1792]{2,1,0:T(8,128)(2,1)}, u32[]{:S(2)}) copy-start(bf16[20,64,1792]{2,1,0:T(8,128)(2,1)} %param.25) | copy-start | bytes 13762564
  7.2 14.9 %copy-start.9 = (s32[4]{0:T(128)S(1)}, s32[4]{0:T(128)}, u32[]{:S(2)}) copy-start(s32[4]{0:T(128)} %param.26) | copy-start | bytes 52
  7.2 15.1 %copy-start.11 = (s32[4]{0:T(128)S(1)}, s32[4]{0:T(128)}, u32[]{:S(2)}) copy-start(s32[4]{0:T(128)} %param.28) | copy-start | bytes 52
  7.2 15.4 %copy-start.10 = (s32[4]{0:T(128)S(1)}, s32[4]{0:T(128)}, u32[]{:S(2)}) copy-start(s32[4]{0:T(128)} %param.29) | copy-start | bytes 52
  14.4 26.9 %copy-start.8 = (s32[4,16]{1,0:T(4,128)S(1)}, s32[4,16]{1,0:T(4,128)}, u32[]{:S(2)}) copy-start(s32[4,16]{1,0:T(4,128)} %param.27) | copy-start | bytes 772
  15.6 16.3 %all-to-all-start = ((bf16[4,8,896]{2,0,1:T(4,128)(2,1)}), bf16[4,8,896]{2,0,1:T(4,128)(2,1)S(1)}, u32[]{:S(2)}, u32[]{:S(2)}) async-start(bf16[4,8,896]{2,0,1:T(4,128)(2,1)} %bitcast.18), calls=%async_computation | async-start | bytes 114688 | tf_op jit(solution)/shard_map/all_to_all | solution.py:51
  20.8 73.0 %all-reduce.9.cloned.1.call-start = ((), (), s32[]{:S(2)}) async-start(), calls=%async_computation.4 | async-start | bytes 1376256
  32.6 61.1 %copy-start.4 = (f32[14,384]{1,0:T(8,128)S(1)}, f32[14,384]{1,0:T(8,128)}, u32[]{:S(2)}) copy-start(f32[14,384]{1,0:T(8,128)} %param.21) | copy-start | bytes 64516
  38.7 83.4 %all-gather.4.cloned.1.call-start = ((), (), s32[]{:S(2)}) async-start(), calls=%async_computation.2 | async-start | bytes 2064384 | tf_op jit(solution)/shard_map/all_gather | solution.py:81
  45.5 135.5 %all-gather.6.cloned.1.call-start = ((), (), s32[]{:S(2)}) async-start(), calls=%async_computation.3 | async-start | bytes 2064384 | tf_op jit(solution)/shard_map/all_gather | solution.py:82
  47.9 46.9 %copy-start.5 = (pred[4]{0:T(512)(128)(4,1)}, pred[4]{0:T(512)(128)(4,1)S(1)}, u32[]{:S(2)}) copy-start(pred[4]{0:T(512)(128)(4,1)S(1)} %fusion.42) | copy-start | bytes 16
  240.5 15.5 %all-to-all-start.1 = ((bf16[8,2,448]{2,1,0:T(2,128)(2,1)}), bf16[8,2,448]{2,1,0:T(2,128)(2,1)S(1)}, u32[]{:S(2)}, u32[]{:S(2)}) async-start(bf16[8,2,448]{2,1,0:T(2,128)(2,1)} %reshape.614), calls=%async_computation.1 | async-start | bytes 32768 | tf_op jit(solution)/shard_map/all_to_all | solution.py:18
  243.9 157.4 %all-reduce.11.cloned.1.call-start = ((), (), s32[]{:S(2)}) async-start(), calls=%async_computation.5 | async-start | bytes 1835008
  257.6 143.7 %copy-start.6 = (pred[4]{0:T(512)(128)(4,1)S(1)}, pred[4]{0:T(512)(128)(4,1)}, u32[]{:S(2)}) copy-start(pred[4]{0:T(512)(128)(4,1)} %copy-done.5) | copy-start | bytes 16
Sparse Core Ops, SparseCore 0:
  38.8 54.9 all-reduce.8
  95.8 26.1 all-gather.3
  124.1 26.7 all-gather.5
  270.5 130.7 all-reduce.10
where the time goes:
time: 412 us; the launch traced here: 409 us
  waiting for transfers between devices  188 us (46%)
  local copies, waits for them, and re-layouts  128 us (31%)
  matrix products  40.2 us (10%)
  between operations  20 us (5%)
  blocking collectives  18 us (4%)
  starting transfers between devices  8.65 us (2%)
  other arithmetic  5.85 us (1%)
    unnamed x6, waiting for transfers between devices  161 us
    reshape x4, local copies, waits for them, and re-layouts, fetch(): pool[pages_here].reshape(slot_count, block_keys, local_heads, head_size)  54.1 us
    all_gather x1, waiting for transfers between devices, body(): lax.all_gather(key_pool[single_page][None], 'req', axis=0, tiled=True)  27.2 us
    gather x4, local copies, waits for them, and re-layouts, fetch(): pool[pages_here].reshape(slot_count, block_keys, local_heads, head_size)  25.4 us
    dot_general x2, matrix products, score_block(): jnp.einsum('shc,sthc->sht', query, fetch(key_out, block_index), preferred...  11.6 us
    dot_general x1, matrix products, body(): jnp.einsum('bsjc,jcbf->bsf', chosen_tokens, chosen_weight, preferred_elem...  11.4 us
    dot_general x2, matrix products, mix_block(): jnp.einsum('sht,sthc->shc', block_probs, fetch(value_out, block_index), p...  11.1 us
    unnamed x35, local copies, waits for them, and re-layouts  10.4 us
  transfers between devices with their start and end apart: 6, of which 3 were waited for; matrix products, arithmetic and copies ran while one was open for 21% of the time, Pallas kernels for 0%

commit v1 on v0

v1 whole, which is shorter than its diff:
```python
import functools

import jax
import jax.numpy as jnp
from jax import lax
from jax.experimental import pallas as pl
from jax.experimental.pallas import tpu as pltpu
from jax.sharding import PartitionSpec as P

EPSILON = 1e-05
F32 = jnp.float32
BF16 = jnp.bfloat16
LANES = 128
META = 128
PACK = 256
VMEM = pl.BlockSpec(memory_space=pltpu.VMEM)
SMEM = pl.BlockSpec(memory_space=pltpu.SMEM)
ANY = pl.BlockSpec(memory_space=pl.ANY)
LIMIT = 56 * 1024 * 1024


def cost(flops, moved):
    return pl.CostEstimate(flops=flops, bytes_accessed=moved, transcendentals=0)


def layer_norm(tokens, norm_gain, norm_shift):
    values_f = tokens.astype(F32)
    average = jnp.mean(values_f, axis=1, keepdims=True)
    centered = values_f - average
    variance = jnp.mean(centered * centered, axis=1, keepdims=True)
    return (centered * lax.rsqrt(variance + EPSILON) * norm_gain + norm_shift).astype(BF16)


def swap(value, axis, step):
    size = lax.axis_size(axis)
    return lax.ppermute(value, axis, [(i, i ^ step) for i in range(size)])


def relative(blocks, index):
    size = blocks.shape[0]
    tail = blocks.shape[1:]
    bits = size.bit_length() - 1
    split = blocks.reshape((2,) * bits + tail)
    for bit in range(bits):
        axis = bits - 1 - bit
        split = jnp.where((index >> bit) & 1 == 1, jnp.flip(split, axis), split)
    return split.reshape((size,) + tail)


def spread_pairs(keep, send):
    got = swap(send, "req", 1)
    chips = keep.shape[0]
    return [jnp.stack([keep[0], got[0]])] + [
        swap(jnp.stack([keep[d], got[d]]), "req", 2 * d) for d in range(1, chips)
    ]


def copy_pools(key_pool, value_pool):
    pages = key_pool.shape[0]
    parts = 4
    step = pages // parts

    def kernel(key_ref, value_ref, key_out, value_out, sems):
        copies = [
            pltpu.make_async_copy(
                source.at[pl.ds(i * step, step)], target.at[pl.ds(i * step, step)], sems.at[n, i]
            )
            for n, (source, target) in enumerate(((key_ref, key_out), (value_ref, value_out)))
            for i in range(parts)
        ]
        for copy in copies:
            copy.start()
        for copy in copies:
            copy.wait()

    shape = jax.ShapeDtypeStruct(key_pool.shape, key_pool.dtype)
    return pl.pallas_call(
        kernel,
        out_shape=(shape, shape),
        in_specs=[ANY, ANY],
        out_specs=(ANY, ANY),
        scratch_shapes=[pltpu.SemaphoreType.DMA((2, parts))],
        compiler_params=pltpu.CompilerParams(vmem_limit_bytes=LIMIT),
        cost_estimate=cost(0, 4 * key_pool.size * 2),
        name="copy_pools",
    )(key_pool, value_pool)


def pick_page(key_pool, value_pool, page):
    shape = (2,) + key_pool.shape[1:]

    def kernel(page_ref, key_ref, value_ref, out_ref, sems):
        copies = [
            pltpu.make_async_copy(source.at[page_ref[0]], out_ref.at[n], sems.at[n])
            for n, source in enumerate((key_ref, value_ref))
        ]
        for copy in copies:
            copy.start()
        for copy in copies:
            copy.wait()

    return pl.pallas_call(
        kernel,
        out_shape=jax.ShapeDtypeStruct(shape, key_pool.dtype),
        in_specs=[SMEM, ANY, ANY],
        out_specs=ANY,
        scratch_shapes=[pltpu.SemaphoreType.DMA((2,))],
        compiler_params=pltpu.CompilerParams(vmem_limit_bytes=LIMIT),
        cost_estimate=cost(0, 4 * key_pool.shape[1] * key_pool.shape[2] * 2),
        name="pick_page",
    )(page, key_pool, value_pool)


def choose_page(which, candidates):
    def kernel(which_ref, *refs):
        out_ref, sem = refs[-2:]
        for n, candidate in enumerate(refs[:-2]):

            @pl.when(which_ref[0] == n)
            def _():
                copy = pltpu.make_async_copy(candidate, out_ref, sem)
                copy.start()
                copy.wait()

    one = candidates[0]
    return pl.pallas_call(
        kernel,
        out_shape=jax.ShapeDtypeStruct(one.shape, one.dtype),
        in_specs=[SMEM] + [ANY] * len(candidates),
        out_specs=ANY,
        scratch_shapes=[pltpu.SemaphoreType.DMA],
        compiler_params=pltpu.CompilerParams(vmem_limit_bytes=LIMIT),
        cost_estimate=cost(0, 4 * one.size),
        name="choose_page",
    )(which, *candidates)


def project(blocks, weight):
    chips = len(blocks)
    slots = blocks[0].shape[1]
    heads, depth, width = weight.shape
    per = 2 if heads % 2 == 0 else 1
    rows = chips * 2 * slots

    def kernel(*refs):
        block_refs = refs[:chips]
        weight_ref, keep_ref, send_ref, left = refs[chips:]

        @pl.when(pl.program_id(0) == 0)
        def _():
            for d in range(chips):
                for e in range(2):
                    row = (d * 2 + e) * slots
                    left[row : row + slots, :] = block_refs[d][e][:, :depth].astype(F32)

        lhs = left[...].astype(BF16)
        for j in range(per):
            total = jnp.dot(lhs, weight_ref[j], preferred_element_type=F32)
            for d in range(chips):
                row = d * 2 * slots
                columns = slice(j * width, (j + 1) * width)
                keep_ref[d, :, columns] = total[row : row + slots]
                send_ref[d, :, columns] = total[row + slots : row + 2 * slots]

    shape = jax.ShapeDtypeStruct((chips, slots, heads * width), F32)
    out_spec = pl.BlockSpec((chips, slots, per * width), lambda i: (0, 0, i))
    return pl.pallas_call(
        kernel,
        grid=(heads // per,),
        out_shape=(shape, shape),
        in_specs=[VMEM] * chips + [pl.BlockSpec((per, depth, width), lambda i: (i, 0, 0))],
        out_specs=(out_spec, out_spec),
        scratch_shapes=[pltpu.VMEM((rows, depth), F32)],
        compiler_params=pltpu.CompilerParams(vmem_limit_bytes=LIMIT),
        cost_estimate=cost(2 * rows * weight.size, 2 * weight.size),
        name="project",
    )(*blocks, weight)


def attend(numbers, page_table, sums, bias, tokens, key_pool, value_pool, key_out, value_out):
    parts = len(sums)
    slots = sums[0].shape[0]
    pages, page, width = key_pool.shape
    head = LANES
    heads = width // head
    max_pages = page_table.shape[1]
    chunk_pages = 4
    chunk = chunk_pages * page
    chunks = max_pages // chunk_pages
    long_rows = max_pages * page
    short_rows = slots * page
    groups = 2 * parts
    share = head // groups
    per = LANES // share
    tall = 16
    strips = width // PACK
    scale = head ** (-0.5)

    def kernel(*refs):
        numbers_ref, table_ref = refs[:2]
        sum_refs = refs[2 : 2 + parts]
        (bias_ref, token_ref, key_ref, value_ref, _, _, pack_keep, pack_send, key_out_ref, value_out_ref) = refs[
            2 + parts : 12 + parts
        ]
        key_buffer, value_buffer, score_buffer, mix_buffer, sems, out_sems = refs[12 + parts :]
        leaving = numbers_ref[slots]
        here = numbers_ref[slots + 1]
        column_block = numbers_ref[slots + 2]
        lengths = [numbers_ref[s] for s in range(slots)]
        long_slot = jnp.int32(0)
        long_length = jnp.int32(-1)
        for s in range(slots):
            is_long = lengths[s] >= page
            long_slot = jnp.where(is_long, s, long_slot)
            long_length = jnp.where(is_long, lengths[s], long_length)
        turns = (long_length + chunk) // chunk

        pairs = ((key_ref, key_buffer), (value_ref, value_buffer))

        def short_copies(n):
            source, buffer = pairs[n]
            return [
                pltpu.make_async_copy(
                    source.at[table_ref[s, 0]], buffer.at[pl.ds(long_rows + s * page, page)], sems.at[n, chunks]
                )
                for s in range(slots)
            ]

        def long_copies(n, c):
            source, buffer = pairs[n]
            return [
                pltpu.make_async_copy(
                    source.at[table_ref[long_slot, c * chunk_pages + i]],
                    buffer.at[pl.ds((c * chunk_pages + i) * page, page)],
                    sems.at[n, c],
                )
                for i in range(chunk_pages)
            ]

        for n in range(2):
            for copy in short_copies(n):
                copy.start()
            for c in range(chunks):

                @pl.when(c < turns)
                def _():
                    for copy in long_copies(n, c):
                        copy.start()

        total = sum_refs[0][...]
        for ref in sum_refs[1:]:
            total = total + ref[...].astype(F32)
        total = total + bias_ref[...]

        def third(k):
            return jnp.concatenate(
                [total[:, (3 * h + k) * head : (3 * h + k + 1) * head] for h in range(heads)], axis=1
            )

        query = (third(0) * scale).astype(BF16).astype(F32)
        new_rows = (third(1).astype(BF16).astype(F32), third(2).astype(BF16).astype(F32))

        lane_head = lax.broadcasted_iota(jnp.int32, (tall, width), 1) // head
        on_head = lane_head == lax.broadcasted_iota(jnp.int32, (tall, width), 0)

        def blocked(row):
            return jnp.where(on_head, jnp.broadcast_to(row, (tall, width)), 0.0).astype(BF16)

        def append(n, s, base, offset, out_ref):
            _, buffer = pairs[n]
            first = pl.multiple_of(offset // 16 * 16, 16)
            place = pl.ds(pl.multiple_of(base + first, 16), 16)
            old = buffer[place, :].astype(F32)
            row = lax.broadcasted_iota(jnp.int32, (16, width), 0)
            fresh = jnp.where(row == offset - first, jnp.broadcast_to(new_rows[n][s : s + 1], (16, width)), old)
            buffer[place, :] = fresh.astype(BF16)

        def out_copy(n, s):
            _, buffer = pairs[n]
            out_ref = (key_out_ref, value_out_ref)[n]
            length = lengths[s]
            is_long = length >= page
            within = length % page // 16 * 16
            base = jnp.where(is_long, length // page * page, long_rows + s * page)
            return pltpu.make_async_copy(
                buffer.at[pl.ds(pl.multiple_of(base + within, 16), 16)],
                out_ref.at[table_ref[s, length // page], pl.ds(pl.multiple_of(within, 16), 16)],
                out_sems.at[n, s],
            )

        def append_short(n):
            for s in range(slots):

                @pl.when(lengths[s] < page)
                def _():
                    append(n, s, long_rows + s * page, lengths[s], None)

        def append_long(n):
            for s in range(slots):

                @pl.when(lengths[s] >= page)
                def _():
                    append(n, s, 0, lengths[s], None)

        def softmax(scores, valid):
            masked = jnp.where(valid, scores, -1e30)
            peak = jnp.max(masked, axis=1, keepdims=True)
            weights = jnp.where(valid, jnp.exp(masked - peak), 0.0)
            return weights.astype(BF16), jnp.sum(weights, axis=1, keepdims=True)

        across = (((1,), (1,)), ((), ()))
        for copy in short_copies(0):
            copy.wait()
        append_short(0)
        short_query = jnp.concatenate([blocked(query[s : s + 1]) for s in range(slots)], axis=0)
        short_scores = lax.dot_general(
            short_query, key_buffer[long_rows:, :], across, preferred_element_type=F32
        )
        size = (slots * tall, short_rows)
        row_slot = lax.broadcasted_iota(jnp.int32, size, 0) // tall
        column = lax.broadcasted_iota(jnp.int32, size, 1)
        limit = jnp.zeros(size, jnp.int32)
        for s in range(slots):
            limit = jnp.where(row_slot == s, jnp.minimum(lengths[s], page - 1), limit)
        in_slot = row_slot == column // page
        short_probs, short_denom = softmax(short_scores, in_slot & (column % page <= limit))

        long_row = jnp.zeros((1, width), F32)
        for s in range(slots):
            long_row = jnp.where(long_slot == s, query[s : s + 1], long_row)
        long_query = blocked(long_row)
        for c in range(chunks):

            @pl.when(c < turns)
            def _():
                for copy in long_copies(0, c):
                    copy.wait()

        append_long(0)
        score_buffer[...] = jnp.full(score_buffer.shape, -1e30, F32)
        for c in range(chunks):

            @pl.when(c < turns)
            def _():
                score_buffer[:, c * chunk : (c + 1) * chunk] = lax.dot_general(
                    long_query, key_buffer[c * chunk : (c + 1) * chunk, :], across, preferred_element_type=F32
                )

        position = lax.broadcasted_iota(jnp.int32, (tall, long_rows), 1)
        long_probs, long_denom = softmax(score_buffer[...], position <= jnp.maximum(long_length, 0))

        for copy in short_copies(1):
            copy.wait()
        append_short(1)
        short_mix = jnp.dot(short_probs, value_buffer[long_rows:, :], preferred_element_type=F32) / short_denom
        mix_buffer[...] = jnp.zeros(mix_buffer.shape, F32)
        for c in range(chunks):

            @pl.when(c < turns)
            def _():
                for copy in long_copies(1, c):
                    copy.wait()

        append_long(1)
        for n in range(2):
            for s in range(slots):

                @pl.when(leaving != s)
                def _():
                    out_copy(n, s).start()

        for c in range(chunks):

            @pl.when(c < turns)
            def _():
                mix_buffer[...] += jnp.dot(
                    long_probs[:, c * chunk : (c + 1) * chunk],
                    value_buffer[c * chunk : (c + 1) * chunk, :],
                    preferred_element_type=F32,
                )

        def fold(mixed):
            return jnp.sum(jnp.where(on_head, mixed, 0.0), axis=0, keepdims=True)

        long_mix = fold(mix_buffer[...] / long_denom)
        rows = []
        for s in range(slots):
            row = fold(short_mix[s * tall : (s + 1) * tall])
            rows.append(jnp.where(lengths[s] >= page, long_mix, row))
        high = -(-slots // 8) * 8
        attended = jnp.concatenate(rows + [jnp.zeros((high - slots, width), F32)], axis=0)

        token = token_ref[:, pl.ds(pl.multiple_of(column_block * width, LANES), width)].astype(F32)
        extra = []
        for source in new_rows + (token,):
            one = jnp.zeros((1, width), F32)
            for s in range(slots):
                one = jnp.where(leaving == s, source[s : s + 1], one)
            extra += [one[:, i * PACK : (i + 1) * PACK] for i in range(strips)]
        extra = jnp.concatenate(extra + [jnp.zeros((pack_rows(slots, strips) - high - 3 * strips, PACK), F32)], axis=0)

        lane = lax.broadcasted_iota(jnp.int32, (high, LANES), 1) // share
        for k in range(groups):
            wanted = here ^ k
            tiles = [jnp.zeros((high, LANES), F32) for _ in range(PACK // LANES)]
            for h in range(heads):
                place = h % per
                shift = lax.rem((place - wanted) * share + 2 * LANES, LANES)
                turned = pltpu.roll(attended[:, h * head : (h + 1) * head], shift, 1)
                tiles[h // per] = jnp.where(lane == place, turned, tiles[h // per])
            block = jnp.concatenate([jnp.concatenate(tiles, axis=1), extra], axis=0).astype(BF16)
            (pack_keep, pack_send)[k % 2][k // 2] = block

        for n in range(2):
            for s in range(slots):

                @pl.when(leaving != s)
                def _():
                    out_copy(n, s).wait()

    packed = jax.ShapeDtypeStruct((parts, pack_rows(slots, strips), PACK), BF16)
    pool_shape = jax.ShapeDtypeStruct(key_pool.shape, key_pool.dtype)
    return pl.pallas_call(
        kernel,
        out_shape=(packed, packed, pool_shape, pool_shape),
        in_specs=[SMEM, SMEM] + [VMEM] * (parts + 2) + [ANY] * 4,
        out_specs=(VMEM, VMEM, ANY, ANY),
        scratch_shapes=[
            pltpu.VMEM((long_rows + short_rows, width), BF16),
            pltpu.VMEM((long_rows + short_rows, width), BF16),
            pltpu.VMEM((tall, long_rows), F32),
            pltpu.VMEM((tall, width), F32),
            pltpu.SemaphoreType.DMA((2, chunks + 1)),
            pltpu.SemaphoreType.DMA((2, slots)),
        ],
        input_output_aliases={6 + parts: 2, 7 + parts: 3},
        compiler_params=pltpu.CompilerParams(vmem_limit_bytes=LIMIT),
        cost_estimate=cost(4 * tall * (long_rows + short_rows) * width, 4 * (long_rows + short_rows) * width),
        name="attend",
    )(numbers, page_table, *sums, bias, tokens, key_pool, value_pool, key_out, value_out)


def pack_rows(slots, strips):
    need = -(-slots // 8) * 8 + 3 * strips
    return -(-need // 16) * 16


def out_project(column_block, order, blocks, weight, pieces):
    chips = len(blocks)
    depth, width = weight.shape
    rows, high = order.shape[0], order.shape[1] // (2 * chips)
    half = rows // 2
    piece = width // pieces

    def kernel(column_ref, order_ref, *refs):
        block_refs = refs[:chips]
        weight_ref, keep_ref, send_ref, left = refs[chips:]

        @pl.when(pl.program_id(0) == 0)
        def _():
            gathered = jnp.concatenate(
                [block_refs[d][e, :high, :].astype(F32) for d in range(chips) for e in range(2)], axis=0
            ).astype(BF16)
            left[...] = jnp.dot(order_ref[...], gathered, preferred_element_type=F32)

        total = jnp.dot(left[:, :depth].astype(BF16), weight_ref[...], preferred_element_type=F32)
        keep_ref[0] = total[:half]
        send_ref[0] = total[half:]

    shape = jax.ShapeDtypeStruct((pieces, half, piece), F32)
    out_spec = pl.BlockSpec((1, half, piece), lambda j, c: (j, 0, 0))
    whole = lambda shape: pl.BlockSpec(shape, lambda j, c: (0,) * len(shape))
    return pl.pallas_call(
        kernel,
        out_shape=(shape, shape),
        grid_spec=pltpu.PrefetchScalarGridSpec(
            num_scalar_prefetch=1,
            grid=(pieces,),
            in_specs=[whole(order.shape)]
            + [whole(block.shape) for block in blocks]
            + [pl.BlockSpec((depth, piece), lambda j, c: (0, j ^ c[0]))],
            out_specs=(out_spec, out_spec),
            scratch_shapes=[pltpu.VMEM((rows, PACK), F32)],
        ),
        compiler_params=pltpu.CompilerParams(vmem_limit_bytes=LIMIT),
        cost_estimate=cost(2 * rows * weight.size, 2 * weight.size),
        name="out_project",
    )(column_block, order, *blocks, weight)


def place_page(numbers, new_rows, candidates, key_out, value_out):
    count = len(candidates)
    page, width = key_out.shape[1:]

    def kernel(numbers_ref, rows_ref, *refs):
        candidate_refs = refs[:count]
        _, _, key_ref, value_ref, buffer, sem, out_sems = refs[count:]
        for n in range(count):

            @pl.when(numbers_ref[0] == n)
            def _():
                copy = pltpu.make_async_copy(candidate_refs[n], buffer, sem)
                copy.start()
                copy.wait()

        offset = numbers_ref[2]
        first = pl.multiple_of(offset // 16 * 16, 16)
        row = lax.broadcasted_iota(jnp.int32, (16, width), 0)
        for n in range(2):
            old = buffer[n, pl.ds(first, 16), :].astype(F32)
            new = jnp.broadcast_to(rows_ref[n : n + 1, :].astype(F32), (16, width))
            buffer[n, pl.ds(first, 16), :] = jnp.where(row == offset - first, new, old).astype(BF16)
        copies = [
            pltpu.make_async_copy(buffer.at[n], target.at[numbers_ref[1]], out_sems.at[n])
            for n, target in enumerate((key_ref, value_ref))
        ]
        for copy in copies:
            copy.start()
        for copy in copies:
            copy.wait()

    shape = jax.ShapeDtypeStruct(key_out.shape, key_out.dtype)
    return pl.pallas_call(
        kernel,
        out_shape=(shape, shape),
        in_specs=[SMEM, VMEM] + [ANY] * (count + 2),
        out_specs=(ANY, ANY),
        scratch_shapes=[
            pltpu.VMEM((2, page, width), BF16),
            pltpu.SemaphoreType.DMA,
            pltpu.SemaphoreType.DMA((2,)),
        ],
        input_output_aliases={2 + count: 0, 3 + count: 1},
        compiler_params=pltpu.CompilerParams(vmem_limit_bytes=LIMIT),
        cost_estimate=cost(0, 8 * page * width * 2),
        name="place_page",
    )(numbers, new_rows, *candidates, key_out, value_out)


def body(
    tokens,
    norm_gain,
    norm_shift,
    qkv_weight,
    qkv_bias,
    out_weight,
    out_bias,
    key_pool,
    value_pool,
    lengths,
    page_table,
    new_slot,
    new_page,
):
    groups = lax.axis_size("req")
    head_groups = lax.axis_size("head")
    here = lax.axis_index("req")
    column_block = lax.axis_index("head")
    slots = tokens.shape[0]
    chips = groups // 2
    page_size, width = key_pool.shape[1:]
    depth = qkv_weight.shape[0]
    local_heads = qkv_weight.shape[1]
    slot_range = jnp.arange(slots, dtype=jnp.int32)
    target_device = new_slot // slots
    leaving = jnp.sum(jnp.where(target_device != here, slot_range, 0))

    mine = pick_page(key_pool, value_pool, page_table[leaving, :1])

    normed = layer_norm(tokens, norm_gain, norm_shift)
    table = jnp.stack(
        [target_device, new_slot % slots, new_page, lengths % page_size], axis=1
    ).astype(BF16)
    table = jnp.pad(table, ((0, 0), (0, META - table.shape[1])))
    features = normed.reshape(slots, groups, depth).transpose(1, 0, 2)
    blocks = jnp.concatenate(
        [relative(features, here), jnp.broadcast_to(table[None], (groups, slots, META))], axis=2
    ).reshape(chips, 2, slots, depth + META)
    spread = spread_pairs(blocks[:, 0], blocks[:, 1])
    candidates = [mine] + [swap(mine, "req", 2 * d) for d in range(1, chips)]

    told = jnp.stack(spread)[..., depth : depth + 4].astype(jnp.int32).reshape(groups, slots, 4)
    places = jnp.arange(groups, dtype=jnp.int32)
    goal = told[..., 0] ^ here
    for_me = (goal == 0) & (places[:, None] != 0)
    for_other = (goal == 1) & (places[:, None] != 1)
    pick = lambda mask, values: jnp.sum(jnp.where(mask, values, 0))
    source = pick(for_me, places[:, None])
    source_other = pick(for_other, places[:, None])
    arrived_page = pick(for_me, told[..., 2])
    arrived_length = pick(for_me, told[..., 3])
    high = -(-slots // 8) * 8
    goal_row = (goal % 2) * (chips * slots) + (goal // 2) * slots + told[..., 1]
    goal_row = jnp.pad(goal_row, ((0, 0), (0, high - slots)), constant_values=-1).reshape(-1)
    order = (
        jnp.arange(groups * slots, dtype=jnp.int32)[:, None] == goal_row[None, :]
    ).astype(BF16)

    keep, send = project(spread, jnp.transpose(qkv_weight, (1, 0, 2)))
    total = keep + swap(send, "req", 1)
    sums = [total[0]] + [swap(total[d], "req", 2 * d) for d in range(1, chips)]

    key_copy, value_copy = copy_pools(key_pool, value_pool)
    numbers = jnp.concatenate([lengths, jnp.stack([leaving, here, column_block])])
    pack_keep, pack_send, key_out, value_out = attend(
        numbers,
        page_table,
        sums,
        qkv_bias.reshape(1, -1),
        tokens,
        key_pool,
        value_pool,
        key_copy,
        value_copy,
    )
    packs = spread_pairs(pack_keep, pack_send)

    which = jnp.where(source_other % 2 == 0, source_other // 2, 0)
    from_other = swap(choose_page(which[None], candidates), "req", 1)

    strips = width // PACK
    rows = lax.dynamic_index_in_dim(
        jnp.stack(packs).reshape(groups, -1, PACK), source, 0, keepdims=False
    )
    arrived_rows = rows[high : high + 3 * strips].reshape(3, width)
    arrived = jnp.where(source % 2 == 0, source // 2, chips)
    key_out, value_out = place_page(
        jnp.stack([arrived, arrived_page, arrived_length]),
        arrived_rows[:2],
        candidates + [from_other],
        key_out,
        value_out,
    )

    keep, send = out_project(
        column_block[None],
        order,
        packs,
        out_weight.reshape(-1, out_weight.shape[2]),
        head_groups,
    )
    total = (keep + swap(send, "req", 1)).reshape(head_groups, chips, slots, width)
    summed = total[:, 0]
    for d in range(1, chips):
        summed = summed + swap(total[:, d].astype(BF16), "req", 2 * d).astype(F32)
    hidden = summed[0]
    for j in range(1, head_groups):
        hidden = hidden + swap(summed[j].astype(BF16), "head", j).astype(F32)
    token_part = lax.dynamic_slice_in_dim(tokens, column_block * width, width, 1)
    residual = jnp.where((slot_range == leaving)[:, None], arrived_rows[2:3], token_part)
    bias_part = lax.dynamic_slice_in_dim(out_bias, column_block * width, width, 0)
    hidden_out = (hidden + bias_part + residual.astype(F32)).astype(BF16)
    return (hidden_out, key_out, value_out)


def solution(mesh):
    in_specs = (
        P("req", None),
        P(),
        P(),
        P("req", "head", None),
        P("head", None),
        P("head", "req", None),
        P(),
        P("req", None, "head"),
        P("req", None, "head"),
        P("req"),
        P("req", None),
        P("req"),
        P("req"),
    )
    out_specs = (P("req", "head"), P("req", None, "head"), P("req", None, "head"))
    return jax.shard_map(body, mesh=mesh, in_specs=in_specs, out_specs=out_specs, check_vma=False)
```

time: 412 us -> 402 us (0.976)
  Pallas kernels: 0 us -> 330 us
  waiting for transfers between devices: 188 us -> 11.3 us
  local copies, waits for them, and re-layouts: 128 us -> 9.03 us
  matrix products: 40.2 us -> 0 us
  starting transfers between devices: 8.65 us -> 27.5 us
  blocking collectives: 18 us -> 0 us
  between operations: 20 us -> 9.33 us
  other arithmetic: 5.85 us -> 14.4 us
    pallas_call x0 -> x7, Pallas kernels: none -> 330 us  [the longest x1 279 us: copy_pools(): pl.pallas_call(kernel, out_shape=(shape, shape), in_specs=[ANY, ANY], out...]
    unnamed x6 -> x0, waiting for transfers between devices: 161 us -> none
    reshape x7 -> x2, local copies, waits for them, and re-layouts: 57.6 us -> 0.14 us  [the longest x1 0.13 us: body(): (keep + swap(send, 'req', 1)).reshape(head_groups, chips, slots, width)]
    gather x14 -> x0, local copies, waits for them, and re-layouts: 44.4 us -> none  [the longest x4 25.4 us: fetch(): pool[pages_here].reshape(slot_count, block_keys, local_heads, head_size)]
    dot_general x6 -> x0, matrix products: 40.2 us -> none  [the longest x2 11.6 us: score_block(): jnp.einsum('shc,sthc->sht', query, fetch(key_out, block_index), preferred...]
    ppermute x0 -> x23, starting transfers between devices: none -> 27.5 us  [swap(): return lax.ppermute(value, axis, [(i, i ^ step) for i in range(size)])]
    all_gather x2 -> x0, waiting for transfers between devices: 27.3 us -> none  [the longest x1 27.2 us: body(): lax.all_gather(key_pool[single_page][None], 'req', axis=0, tiled=True)]
    ppermute x0 -> x23, waiting for transfers between devices: none -> 11.3 us  [swap(): return lax.ppermute(value, axis, [(i, i ^ step) for i in range(size)])]
  transfers between devices with their start and end apart: 6 -> 23, of which waited for: 3 -> 10; matrix products, arithmetic and copies ran while one was open for 21% -> 4% of each run, Pallas kernels for 0% -> 78%
where the time goes in v1:
time: 402 us; the launch traced here: 401 us
  Pallas kernels  330 us (82%)
  starting transfers between devices  27.5 us (7%)
  other arithmetic  14.4 us (4%)
  waiting for transfers between devices  11.3 us (3%)
  between operations  9.33 us (2%)
  local copies, waits for them, and re-layouts  9.03 us (2%)
    pallas_call x1, Pallas kernels, copy_pools(): pl.pallas_call(kernel, out_shape=(shape, shape), in_specs=[ANY, ANY], out...  279 us
    ppermute x23, starting transfers between devices, swap(): return lax.ppermute(value, axis, [(i, i ^ step) for i in range(size)])  27.5 us
    pallas_call x1, Pallas kernels, pick_page(): pl.pallas_call(kernel, out_shape=jax.ShapeDtypeStruct(shape, key_pool.dty...  15.7 us
    pallas_call x1, Pallas kernels, choose_page(): pl.pallas_call(kernel, out_shape=jax.ShapeDtypeStruct(one.shape, one.dtyp...  15 us
    ppermute x23, waiting for transfers between devices, swap(): return lax.ppermute(value, axis, [(i, i ^ step) for i in range(size)])  11.3 us
  transfers between devices with their start and end apart: 23, of which 10 were waited for; matrix products, arithmetic and copies ran while one was open for 4% of the time, Pallas kernels for 78%

profile of v1, /device:TPU:0, one launch (start us, length us, event | category | flops | bytes accessed | tf_op | source)
XLA Modules:
  0.0 401.2 jit_solution(10544159822040638923)
XLA Ops:
  0.6 1.3 fusion.35
  3.5 1.2 constant_dynamic-slice_fusion.1
  4.8 15.7 %pick_page.1.refs_0_ = bf16[2,64,1792]{2,1,0:T(8,128)(2,1)} custom-call(s32[1]{0:T(128)} %bitcast.42.page_ref, bf16[20,64,1792]{2,1,0:T(8,128)(2,1)} %key_ref.3, bf16[20,64,1792]{2,1,0:T(8,128)(2,1)} %value_ref.3), custom_call_target="tpu_custom_call" | custom-call | bytes 917504 | tf_op jit(solution)/shard_map/pick_page/pallas_call | solution.py:102
  20.5 3.0 collective-permute-start.19
  23.5 1.5 collective-permute-start.20
  26.1 1.1 pad_add_fusion.refs_0_
  27.2 279.1 %copy_pools.1 = (bf16[20,64,1792]{2,1,0:T(8,128)(2,1)}, bf16[20,64,1792]{2,1,0:T(8,128)(2,1)}) custom-call(bf16[20,64,1792]{2,1,0:T(8,128)(2,1)} %key_ref.3, bf16[20,64,1792]{2,1,0:T(8,128)(2,1)} %value_ref.3), custom_call_target="tpu_custom_call" | custom-call | bytes 18350080 | tf_op jit(solution)/shard_map/copy_pools/pallas_call | solution.py:77
  306.3 0.6 copy.35
  307.1 2.0 collective-permute-start.2
  309.2 1.6 collective-permute-start.1
  311.9 1.1 collective-permute-done.1.refs_1_
  313.6 7.6 %project.1 = (f32[4,4,5376]{2,1,0:T(4,128)}, f32[4,4,5376]{2,1,0:T(4,128)}) custom-call(bf16[2,4,1024]{2,1,0:T(4,128)(2,1)} %get-tuple-element.66.refs_0_, bf16[2,4,1024]{2,1,0:T(4,128)(2,1)} %copy-done.14, bf16[2,4,1024]{2,1,0:T(4,128)(2,1)} %copy-done.13, bf16[2,4,1024]{2,1,0:T(4,128)(2,1)} %copy-done.12, bf16[14,896,384]{2,1,0:T(8,128)(2,1)} %bitcast.95), custom_call_target="tpu_custom_call" | custom-call | flops 308281344 | bytes 9633792 | tf_op jit(solution)/shard_map/project/pallas_call | solution.py:167
  321.2 0.7 fusion.23
  322.4 0.7 select_reduce_fusion
  323.3 1.1 add.107
  324.3 0.7 slice_bitcast_fusion.1
  325.0 1.5 collective-permute-start.5
  327.0 1.5 collective-permute-start.7
  329.1 0.8 collective-permute-done.5.refs_3_
  330.0 3.1 collective-permute-done.6.refs_4_
  333.0 0.6 copy-done.10
  333.7 5.2 %attend.1 = (bf16[4,32,256]{2,1,0:T(8,128)(2,1)}, bf16[4,32,256]{2,1,0:T(8,128)(2,1)}, bf16[20,64,1792]{2,1,0:T(8,128)(2,1)}, bf16[20,64,1792]{2,1,0:T(8,128)(2,1)}) custom-call(s32[7]{0:T(128)} %pad_add_fusion.refs_0_, s32[4,16]{1,0:T(4,128)} %refs_1_.1, f32[4,5376]{1,0:T(4,128)} %get-tuple-element.41.refs_2_, ...), custom_call_target="tpu_custom_call", output_to_operand_aliasing={{2}: (10, {}), {3}: (11, {})} | custom-call | flops 146800640 | bytes 9175040 | tf_op jit(solution)/shard_map/attend/pallas_call | solution.py:423
  338.9 1.0 collective-permute-start.8
  339.9 0.8 fusion.41
  341.0 2.7 collective-permute-start.9
  344.1 1.5 collective-permute-start.11
  345.6 0.6 fusion.38
  346.2 1.5 collective-permute-start.21
  348.0 1.0 collective-permute-done.11.refs_3_
  349.6 4.4 %out_project.1 = (f32[4,16,1792]{2,1,0:T(8,128)}, f32[4,16,1792]{2,1,0:T(8,128)}) custom-call(s32[1]{0:T(128)} %bitcast.column_ref, bf16[32,64]{1,0:T(8,128)(2,1)} %fusion.18.order_ref, bf16[2,32,256]{2,1,0:T(8,128)(2,1)} %get-tuple-element.61.refs_0_, bf16[2,32,256]{2,1,0:T(8,128)(2,1)} %copy-done.6, bf16[2,32,256]{2,1,0:T(8,128)(2,1)} %copy-done.7, ...), custom_call_target="tpu_custom_call" | custom-call | flops 102760448 | bytes 3211264 | tf_op jit(solution)/shard_map/out_project/pallas_call | solution.py:473
  354.5 0.8 dynamic_slice.13
  355.3 0.7 select_reduce_fusion.2
  362.7 1.9 pad_add_fusion.1.numbers_ref
  364.6 0.7 copy-done.1
  365.7 15.0 %choose_page.1 = bf16[2,64,1792]{2,1,0:T(8,128)(2,1)} custom-call(s32[1]{0:T(128)} %bitcast.43.which_ref, bf16[2,64,1792]{2,1,0:T(8,128)(2,1)} %pick_page.1.refs_0_, bf16[2,64,1792]{2,1,0:T(8,128)(2,1)} %copy-done.1, bf16[2,64,1792]{2,1,0:T(8,128)(2,1)} %copy-done.2, bf16[2,64,1792]{2,1,0:T(8,128)(2,1)} %copy-done.3), custom_call_target="tpu_custom_call" | custom-call | bytes 917504 | tf_op jit(solution)/shard_map/choose_page/pallas_call | solution.py:126
  381.3 0.8 pad_maximum_fusion
  382.1 1.1 add.108
  383.4 1.5 collective-permute-start.15
  384.9 2.1 collective-permute-start.14
  387.0 1.6 collective-permute-done.15
  388.6 0.8 collective-permute-done.14
  389.5 1.7 collective-permute-done.13
  391.3 3.7 collective-permute-start.18
  395.0 0.8 collective-permute-start.16
  395.8 0.6 slice.179.rows_ref
  396.4 0.8 copy-done.5
  397.2 2.6 place_page.1
  399.8 1.4 fusion.16
  (105 shorter events, 8.0 us)
Async XLA Ops:
  4.7 20.3 %copy-start.18 = (s32[4]{0:T(128)S(1)}, s32[4]{0:T(128)}, u32[]{:S(2)}) copy-start(s32[4]{0:T(128)} %param.22) | copy-start | bytes 52
  4.7 20.3 %copy-start.19 = (s32[4]{0:T(128)S(1)}, s32[4]{0:T(128)}, u32[]{:S(2)}) copy-start(s32[4]{0:T(128)} %param.25) | copy-start | bytes 52
  4.7 20.4 %copy-start.4 = (bf16[4,7168]{1,0:T(4,128)(2,1)S(1)}, bf16[4,7168]{1,0:T(4,128)(2,1)}, u32[]{:S(2)}) copy-start(bf16[4,7168]{1,0:T(4,128)(2,1)} %refs_7_.1) | copy-start | bytes 172036
  4.7 20.9 %copy-start.15 = (f32[7168]{0:T(1024)S(1)}, f32[7168]{0:T(1024)}, u32[]{:S(2)}) copy-start(f32[7168]{0:T(1024)} %param.15) | copy-start | bytes 86020
  4.8 20.9 %copy-start.16 = (f32[7168]{0:T(1024)S(1)}, f32[7168]{0:T(1024)}, u32[]{:S(2)}) copy-start(f32[7168]{0:T(1024)} %param.14) | copy-start | bytes 86020
  20.5 344.1 %collective-permute-start.19 = (bf16[2,64,1792]{2,1,0:T(8,128)(2,1)}, bf16[2,64,1792]{2,1,0:T(8,128)(2,1)S(1)}, u32[]{:S(2)}, u32[]{:S(2)}) collective-permute-start(bf16[2,64,1792]{2,1,0:T(8,128)(2,1)} %pick_page.1.refs_0_), channel_id=1, source_target_pairs={{0,8},{4,12},{8,0},{12,4},{16,24},{20,28},{24,16},{28,20},{1,9},{5... | collective-permute-start | bytes 1376264 | tf_op jit(solution)/shard_map/ppermute | solution.py:36
  23.5 341.1 %collective-permute-start.20 = (bf16[2,64,1792]{2,1,0:T(8,128)(2,1)}, bf16[2,64,1792]{2,1,0:T(8,128)(2,1)S(1)}, u32[]{:S(2)}, u32[]{:S(2)}) collective-permute-start(bf16[2,64,1792]{2,1,0:T(8,128)(2,1)} %pick_page.1.refs_0_), channel_id=1, source_target_pairs={{0,16},{4,20},{8,24},{12,28},{16,0},{20,4},{24,8},{28,12},{1,17},{... | collective-permute-start | bytes 1376264 | tf_op jit(solution)/shard_map/ppermute | solution.py:36
  26.0 281.0 %collective-permute-start = (bf16[4,4,1024]{2,1,0:T(4,128)(2,1)S(1)}, bf16[4,4,1024]{2,1,0:T(4,128)(2,1)S(1)}, u32[]{:S(2)}, u32[]{:S(2)}) collective-permute-start(bf16[4,4,1024]{2,1,0:T(4,128)(2,1)S(1)} %fusion.10), channel_id=1, source_target_pairs={{0,4},{4,0},{8,12},{12,8},{16,20},{20,16},{24,28},{28,24},{1,5},{5... | collective-permute-start | bytes 98312 | tf_op jit(solution)/shard_map/ppermute | solution.py:36
  27.2 279.1 %copy-start.17 = (f32[14,384]{1,0:T(8,128)S(1)}, f32[14,384]{1,0:T(8,128)}, u32[]{:S(2)}) copy-start(f32[14,384]{1,0:T(8,128)} %param.17) | copy-start | bytes 64516
  307.0 4.9 %collective-permute-start.3 = (bf16[2,4,1024]{2,1,0:T(4,128)(2,1)S(1)}, bf16[2,4,1024]{2,1,0:T(4,128)(2,1)S(1)}, u32[]{:S(2)}, u32[]{:S(2)}) collective-permute-start(bf16[2,4,1024]{2,1,0:T(4,128)(2,1)S(1)} %pad_maximum_fusion.8), channel_id=1, source_target_pairs={{0,24},{4,28},{8,16},{12,20},{16,8},{20,12},{24,0},{28,4},{1,25},{... | collective-permute-start | bytes 49160 | tf_op jit(solution)/shard_map/ppermute | solution.py:36
  307.1 4.8 %collective-permute-start.2 = (bf16[2,4,1024]{2,1,0:T(4,128)(2,1)S(1)}, bf16[2,4,1024]{2,1,0:T(4,128)(2,1)S(1)}, u32[]{:S(2)}, u32[]{:S(2)}) collective-permute-start(bf16[2,4,1024]{2,1,0:T(4,128)(2,1)S(1)} %pad_maximum_fusion.7), channel_id=1, source_target_pairs={{0,16},{4,20},{8,24},{12,28},{16,0},{20,4},{24,8},{28,12},{1,17},{... | collective-permute-start | bytes 49160 | tf_op jit(solution)/shard_map/ppermute | solution.py:36
  309.2 3.8 collective-permute-start.1
  311.9 1.1 copy-start.12
  311.9 1.1 copy-start.13
  313.0 0.6 copy-start.14
  321.2 2.0 collective-permute-start.4
  325.0 4.9 %collective-permute-start.5 = (f32[4,5376]{1,0:T(4,128)S(1)}, f32[4,5376]{1,0:T(4,128)S(1)}, u32[]{:S(2)}, u32[]{:S(2)}) collective-permute-start(f32[4,5376]{1,0:T(4,128)S(1)} %get-tuple-element.40), channel_id=1, source_target_pairs={{0,8},{4,12},{8,0},{12,4},{16,24},{20,28},{24,16},{28,20},{1,9},{5... | collective-permute-start | bytes 258056 | tf_op jit(solution)/shard_map/ppermute | solution.py:36
  326.5 6.5 %collective-permute-start.6 = (f32[4,5376]{1,0:T(4,128)S(1)}, f32[4,5376]{1,0:T(4,128)S(1)}, u32[]{:S(2)}, u32[]{:S(2)}) collective-permute-start(f32[4,5376]{1,0:T(4,128)S(1)} %get-tuple-element.39), channel_id=1, source_target_pairs={{0,16},{4,20},{8,24},{12,28},{16,0},{20,4},{24,8},{28,12},{1,17},{... | collective-permute-start | bytes 258056 | tf_op jit(solution)/shard_map/ppermute | solution.py:36
  327.0 6.0 %collective-permute-start.7 = (f32[4,5376]{1,0:T(4,128)S(1)}, f32[4,5376]{1,0:T(4,128)S(1)}, u32[]{:S(2)}, u32[]{:S(2)}) collective-permute-start(f32[4,5376]{1,0:T(4,128)S(1)} %get-tuple-element.38), channel_id=1, source_target_pairs={{0,24},{4,28},{8,16},{12,20},{16,8},{20,12},{24,0},{28,4},{1,25},{... | collective-permute-start | bytes 258056 | tf_op jit(solution)/shard_map/ppermute | solution.py:36
  330.0 3.1 copy-start.9
  333.0 0.6 copy-start.10
  333.0 0.7 copy-start.11
  333.7 12.5 %copy-start = (bf16[2,64,1792]{2,1,0:T(8,128)(2,1)S(1)}, bf16[2,64,1792]{2,1,0:T(8,128)(2,1)}, u32[]{:S(2)}) copy-start(bf16[2,64,1792]{2,1,0:T(8,128)(2,1)} %pick_page.1.refs_0_) | copy-start | bytes 1376260
  338.9 2.1 collective-permute-start.8
  341.0 5.2 %collective-permute-start.9 = (bf16[2,32,256]{2,1,0:T(8,128)(2,1)S(1)}, bf16[2,32,256]{2,1,0:T(8,128)(2,1)S(1)}, u32[]{:S(2)}, u32[]{:S(2)}) collective-permute-start(bf16[2,32,256]{2,1,0:T(8,128)(2,1)S(1)} %pad_maximum_fusion.2), channel_id=1, source_target_pairs={{0,8},{4,12},{8,0},{12,4},{16,24},{20,28},{24,16},{28,20},{1,9},{5... | collective-permute-start | bytes 98312 | tf_op jit(solution)/shard_map/ppermute | solution.py:36
  343.7 4.3 %collective-permute-start.10 = (bf16[2,32,256]{2,1,0:T(8,128)(2,1)S(1)}, bf16[2,32,256]{2,1,0:T(8,128)(2,1)S(1)}, u32[]{:S(2)}, u32[]{:S(2)}) collective-permute-start(bf16[2,32,256]{2,1,0:T(8,128)(2,1)S(1)} %pad_maximum_fusion.3), channel_id=1, source_target_pairs={{0,16},{4,20},{8,24},{12,28},{16,0},{20,4},{24,8},{28,12},{1,17},{... | collective-permute-start | bytes 98312 | tf_op jit(solution)/shard_map/ppermute | solution.py:36
  344.1 4.8 %collective-permute-start.11 = (bf16[2,32,256]{2,1,0:T(8,128)(2,1)S(1)}, bf16[2,32,256]{2,1,0:T(8,128)(2,1)S(1)}, u32[]{:S(2)}, u32[]{:S(2)}) collective-permute-start(bf16[2,32,256]{2,1,0:T(8,128)(2,1)S(1)} %pad_maximum_fusion.4), channel_id=1, source_target_pairs={{0,24},{4,28},{8,16},{12,20},{16,8},{20,12},{24,0},{28,4},{1,25},{... | collective-permute-start | bytes 98312 | tf_op jit(solution)/shard_map/ppermute | solution.py:36
  346.2 2.7 copy-start.6
  346.2 18.4 %collective-permute-start.21 = (bf16[2,64,1792]{2,1,0:T(8,128)(2,1)S(1)}, bf16[2,64,1792]{2,1,0:T(8,128)(2,1)S(1)}, u32[]{:S(2)}, u32[]{:S(2)}) collective-permute-start(bf16[2,64,1792]{2,1,0:T(8,128)(2,1)S(1)} %copy-done), channel_id=1, source_target_pairs={{0,24},{4,28},{8,16},{12,20},{16,8},{20,12},{24,0},{28,4},{1,25},{... | collective-permute-start | bytes 1376264 | tf_op jit(solution)/shard_map/ppermute | solution.py:36
  348.0 1.0 copy-start.7
  348.9 0.6 copy-start.8
  354.0 28.1 %collective-permute-start.12 = (f32[4,16,1792]{2,1,0:T(8,128)}, f32[4,16,1792]{2,1,0:T(8,128)S(1)}, u32[]{:S(2)}, u32[]{:S(2)}) collective-permute-start(f32[4,16,1792]{2,1,0:T(8,128)} %get-tuple-element.22), channel_id=1, source_target_pairs={{0,4},{4,0},{8,12},{12,8},{16,20},{20,16},{24,28},{28,24},{1,5},{5... | collective-permute-start | bytes 1376264 | tf_op jit(solution)/shard_map/ppermute | solution.py:36
  364.6 0.8 copy-start.1
  364.6 0.9 copy-start.2
  364.6 1.1 copy-start.3
  380.7 15.7 %collective-permute-start.22 = (bf16[2,64,1792]{2,1,0:T(8,128)(2,1)}, bf16[2,64,1792]{2,1,0:T(8,128)(2,1)S(1)}, u32[]{:S(2)}, u32[]{:S(2)}) collective-permute-start(bf16[2,64,1792]{2,1,0:T(8,128)(2,1)} %choose_page.1), channel_id=1, source_target_pairs={{0,4},{4,0},{8,12},{12,8},{16,20},{20,16},{24,28},{28,24},{1,5},{5... | collective-permute-start | bytes 1376264 | tf_op jit(solution)/shard_map/ppermute | solution.py:36
  383.4 5.2 %collective-permute-start.15 = (bf16[4,4,1792]{2,1,0:T(4,128)(2,1)S(1)}, bf16[4,4,1792]{2,1,0:T(4,128)(2,1)S(1)}, u32[]{:S(2)}, u32[]{:S(2)}) collective-permute-start(bf16[4,4,1792]{2,1,0:T(4,128)(2,1)S(1)} %get-tuple-element.43), channel_id=1, source_target_pairs={{0,24},{4,28},{8,16},{12,20},{16,8},{20,12},{24,0},{28,4},{1,25},{... | collective-permute-start | bytes 172040 | tf_op jit(solution)/shard_map/ppermute | solution.py:36
  384.9 4.6 %collective-permute-start.14 = (bf16[4,4,1792]{2,1,0:T(4,128)(2,1)S(1)}, bf16[4,4,1792]{2,1,0:T(4,128)(2,1)S(1)}, u32[]{:S(2)}, u32[]{:S(2)}) collective-permute-start(bf16[4,4,1792]{2,1,0:T(4,128)(2,1)S(1)} %get-tuple-element.44), channel_id=1, source_target_pairs={{0,16},{4,20},{8,24},{12,28},{16,0},{20,4},{24,8},{28,12},{1,17},{... | collective-permute-start | bytes 172040 | tf_op jit(solution)/shard_map/ppermute | solution.py:36
  387.0 4.2 %collective-permute-start.13 = (bf16[4,4,1792]{2,1,0:T(4,128)(2,1)S(1)}, bf16[4,4,1792]{2,1,0:T(4,128)(2,1)S(1)}, u32[]{:S(2)}, u32[]{:S(2)}) collective-permute-start(bf16[4,4,1792]{2,1,0:T(4,128)(2,1)S(1)} %get-tuple-element.42), channel_id=1, source_target_pairs={{0,8},{4,12},{8,0},{12,4},{16,24},{20,28},{24,16},{28,20},{1,9},{5... | collective-permute-start | bytes 172040 | tf_op jit(solution)/shard_map/ppermute | solution.py:36
  391.3 8.5 %collective-permute-start.18 = (bf16[4,1792]{1,0:T(4,128)(2,1)S(1)}, bf16[4,1792]{1,0:T(4,128)(2,1)S(1)}, u32[]{:S(2)}, u32[]{:S(2)}) collective-permute-start(bf16[4,1792]{1,0:T(4,128)(2,1)S(1)} %get-tuple-element.58), channel_id=1, source_target_pairs={{0,3},{1,2},{2,1},{3,0},{4,7},{5,6},{6,5},{7,4},{8,11},{9,10},{10,... | collective-permute-start | bytes 43016 | tf_op jit(solution)/shard_map/ppermute | solution.py:36
  395.0 4.8 %collective-permute-start.17 = (bf16[4,1792]{1,0:T(4,128)(2,1)S(1)}, bf16[4,1792]{1,0:T(4,128)(2,1)S(1)}, u32[]{:S(2)}, u32[]{:S(2)}) collective-permute-start(bf16[4,1792]{1,0:T(4,128)(2,1)S(1)} %get-tuple-element.59), channel_id=1, source_target_pairs={{0,2},{1,3},{2,0},{3,1},{4,6},{5,7},{6,4},{7,5},{8,10},{9,11},{10,... | collective-permute-start | bytes 43016 | tf_op jit(solution)/shard_map/ppermute | solution.py:36
  395.0 4.8 %collective-permute-start.16 = (bf16[4,1792]{1,0:T(4,128)(2,1)S(1)}, bf16[4,1792]{1,0:T(4,128)(2,1)S(1)}, u32[]{:S(2)}, u32[]{:S(2)}) collective-permute-start(bf16[4,1792]{1,0:T(4,128)(2,1)S(1)} %get-tuple-element.57), channel_id=1, source_target_pairs={{0,1},{1,0},{2,3},{3,2},{4,5},{5,4},{6,7},{7,6},{8,9},{9,8},{10,11... | collective-permute-start | bytes 43016 | tf_op jit(solution)/shard_map/ppermute | solution.py:36
  396.4 0.8 copy-start.5

commit v2 on v1

--- a/solution.py
+++ b/solution.py
@@ -16,7 +16,7 @@
 VMEM = pl.BlockSpec(memory_space=pltpu.VMEM)
 SMEM = pl.BlockSpec(memory_space=pltpu.SMEM)
 ANY = pl.BlockSpec(memory_space=pl.ANY)
-LIMIT = 56 * 1024 * 1024
+MIB = 1024 * 1024
 
 
 def cost(flops, moved):
@@ -57,21 +57,27 @@
 
 def copy_pools(key_pool, value_pool):
     pages = key_pool.shape[0]
-    parts = 4
+    parts = 5 if pages % 5 == 0 else 1
     step = pages // parts
 
-    def kernel(key_ref, value_ref, key_out, value_out, sems):
-        copies = [
-            pltpu.make_async_copy(
-                source.at[pl.ds(i * step, step)], target.at[pl.ds(i * step, step)], sems.at[n, i]
-            )
-            for n, (source, target) in enumerate(((key_ref, key_out), (value_ref, value_out)))
-            for i in range(parts)
+    def kernel(key_ref, value_ref, key_out, value_out, buffer, in_sems, out_sems):
+        steps = [(n, i, pl.ds(i * step, step)) for i in range(parts) for n in range(2)]
+        sources, targets = (key_ref, value_ref), (key_out, value_out)
+        reads = [
+            pltpu.make_async_copy(sources[n].at[place], buffer.at[n, place], in_sems.at[n, i])
+            for n, i, place in steps
         ]
-        for copy in copies:
-            copy.start()
-        for copy in copies:
-            copy.wait()
+        writes = [
+            pltpu.make_async_copy(buffer.at[n, place], targets[n].at[place], out_sems.at[n, i])
+            for n, i, place in steps
+        ]
+        for read in reads:
+            read.start()
+        for read, write in zip(reads, writes):
+            read.wait()
+            write.start()
+        for write in writes:
+            write.wait()
 
     shape = jax.ShapeDtypeStruct(key_pool.shape, key_pool.dtype)
     return pl.pallas_call(
@@ -79,8 +85,12 @@
         out_shape=(shape, shape),
         in_specs=[ANY, ANY],
         out_specs=(ANY, ANY),
-        scratch_shapes=[pltpu.SemaphoreType.DMA((2, parts))],
-        compiler_params=pltpu.CompilerParams(vmem_limit_bytes=LIMIT),
+        scratch_shapes=[
+            pltpu.VMEM((2,) + key_pool.shape, key_pool.dtype),
+            pltpu.SemaphoreType.DMA((2, parts)),
+            pltpu.SemaphoreType.DMA((2, parts)),
+        ],
+        compiler_params=pltpu.CompilerParams(vmem_limit_bytes=11 * MIB),
         cost_estimate=cost(0, 4 * key_pool.size * 2),
         name="copy_pools",
     )(key_pool, value_pool)
@@ -103,9 +113,9 @@
         kernel,
         out_shape=jax.ShapeDtypeStruct(shape, key_pool.dtype),
         in_specs=[SMEM, ANY, ANY],
-        out_specs=ANY,
+        out_specs=VMEM,
         scratch_shapes=[pltpu.SemaphoreType.DMA((2,))],
-        compiler_params=pltpu.CompilerParams(vmem_limit_bytes=LIMIT),
+        compiler_params=pltpu.CompilerParams(vmem_limit_bytes=2 * MIB),
         cost_estimate=cost(0, 4 * key_pool.shape[1] * key_pool.shape[2] * 2),
         name="pick_page",
     )(page, key_pool, value_pool)
@@ -127,9 +137,9 @@
         kernel,
         out_shape=jax.ShapeDtypeStruct(one.shape, one.dtype),
         in_specs=[SMEM] + [ANY] * len(candidates),
-        out_specs=ANY,
+        out_specs=VMEM,
         scratch_shapes=[pltpu.SemaphoreType.DMA],
-        compiler_params=pltpu.CompilerParams(vmem_limit_bytes=LIMIT),
+        compiler_params=pltpu.CompilerParams(vmem_limit_bytes=2 * MIB),
         cost_estimate=cost(0, 4 * one.size),
         name="choose_page",
     )(which, *candidates)
@@ -171,7 +181,7 @@
         in_specs=[VMEM] * chips + [pl.BlockSpec((per, depth, width), lambda i: (i, 0, 0))],
         out_specs=(out_spec, out_spec),
         scratch_shapes=[pltpu.VMEM((rows, depth), F32)],
-        compiler_params=pltpu.CompilerParams(vmem_limit_bytes=LIMIT),
+        compiler_params=pltpu.CompilerParams(vmem_limit_bytes=8 * MIB),
         cost_estimate=cost(2 * rows * weight.size, 2 * weight.size),
         name="project",
     )(*blocks, weight)
@@ -434,7 +444,7 @@
             pltpu.SemaphoreType.DMA((2, slots)),
         ],
         input_output_aliases={6 + parts: 2, 7 + parts: 3},
-        compiler_params=pltpu.CompilerParams(vmem_limit_bytes=LIMIT),
+        compiler_params=pltpu.CompilerParams(vmem_limit_bytes=18 * MIB),
         cost_estimate=cost(4 * tall * (long_rows + short_rows) * width, 4 * (long_rows + short_rows) * width),
         name="attend",
     )(numbers, page_table, *sums, bias, tokens, key_pool, value_pool, key_out, value_out)
@@ -482,7 +492,7 @@
             out_specs=(out_spec, out_spec),
             scratch_shapes=[pltpu.VMEM((rows, PACK), F32)],
         ),
-        compiler_params=pltpu.CompilerParams(vmem_limit_bytes=LIMIT),
+        compiler_params=pltpu.CompilerParams(vmem_limit_bytes=8 * MIB),
         cost_estimate=cost(2 * rows * weight.size, 2 * weight.size),
         name="out_project",
     )(column_block, order, *blocks, weight)
@@ -531,7 +541,7 @@
             pltpu.SemaphoreType.DMA((2,)),
         ],
         input_output_aliases={2 + count: 0, 3 + count: 1},
-        compiler_params=pltpu.CompilerParams(vmem_limit_bytes=LIMIT),
+        compiler_params=pltpu.CompilerParams(vmem_limit_bytes=2 * MIB),
         cost_estimate=cost(0, 8 * page * width * 2),
         name="place_page",
     )(numbers, new_rows, *candidates, key_out, value_out)

time: 402 us -> 112 us (0.28)
  Pallas kernels: 330 us -> 19.3 us
  local copies, waits for them, and re-layouts: 9.03 us -> 21.9 us
  starting transfers between devices: 27.5 us -> 37.6 us
  other arithmetic: 14.4 us -> 9.44 us
    pallas_call x1, Pallas kernels: 279 us -> 5.93 us  [copy_pools(): pl.pallas_call(kernel, out_shape=(shape, shape), in_specs=[ANY, ANY], out...]
    pallas_call x1, Pallas kernels: 15 us -> 0.32 us  [choose_page(): pl.pallas_call(kernel, out_shape=jax.ShapeDtypeStruct(one.shape, one.dtyp...]
    pallas_call x1, Pallas kernels: 15.7 us -> 1.32 us  [pick_page(): pl.pallas_call(kernel, out_shape=jax.ShapeDtypeStruct(shape, key_pool.dty...]
    unnamed x44 -> x36, local copies, waits for them, and re-layouts: 4.59 us -> 17.8 us
    ppermute x23, starting transfers between devices: 27.5 us -> 37.6 us  [swap(): return lax.ppermute(value, axis, [(i, i ^ step) for i in range(size)])]
    pallas_call x1, Pallas kernels: 7.65 us -> 2.43 us  [project(): pl.pallas_call(kernel, grid=(heads // per,), out_shape=(shape, shape), in...]
  transfers between devices with their start and end apart: 23 -> 23, of which waited for: 10 -> 10; matrix products, arithmetic and copies ran while one was open for 4% -> 10% of each run, Pallas kernels for 78% -> 16%
where the time goes in v2:
time: 112 us; the launch traced here: 111 us
  starting transfers between devices  37.6 us (34%)
  local copies, waits for them, and re-layouts  21.9 us (20%)
  Pallas kernels  19.3 us (17%)
  waiting for transfers between devices  13.2 us (12%)
  other arithmetic  9.44 us (8%)
  between operations  9.1 us (8%)
    ppermute x23, starting transfers between devices, swap(): return lax.ppermute(value, axis, [(i, i ^ step) for i in range(size)])  37.6 us
    unnamed x36, local copies, waits for them, and re-layouts  17.8 us
    ppermute x23, waiting for transfers between devices, swap(): return lax.ppermute(value, axis, [(i, i ^ step) for i in range(size)])  13.2 us
    pallas_call x1, Pallas kernels, copy_pools(): pl.pallas_call(kernel, out_shape=(shape, shape), in_specs=[ANY, ANY], out...  5.93 us
    pallas_call x1, Pallas kernels, attend(): pl.pallas_call(kernel, out_shape=(packed, packed, pool_shape, pool_shape)...  5.19 us
    pallas_call x1, Pallas kernels, project(): pl.pallas_call(kernel, grid=(heads // per,), out_shape=(shape, shape), in...  2.43 us
    pallas_call x1, Pallas kernels, out_project(): pl.pallas_call(kernel, out_shape=(shape, shape), grid_spec=pltpu.Prefetch...  2.41 us
  transfers between devices with their start and end apart: 23, of which 10 were waited for; matrix products, arithmetic and copies ran while one was open for 10% of the time, Pallas kernels for 16%

profile of v2, /device:TPU:0, one launch (start us, length us, event | category | flops | bytes accessed | tf_op | source)
XLA Modules:
  0.0 110.5 jit_solution(12321006540885316323)
XLA Ops:
  0.6 1.3 %fusion.35 = (s32[]{:T(128)}, s32[4]{0:T(128)S(1)}, bf16[4,1]{0,1:T(2,128)(2,1)S(1)}) fusion(s32[]{:T(128)} %axis_index.25, s32[4]{0:T(128)} %param.24), kind=kLoop, calls=%fused_computation.102 | loop fusion | flops 91 | bytes 48 | tf_op jit(solution)/shard_map/reduce_sum | solution.py:576
  3.9 1.2 %constant_dynamic-slice_fusion.1 = s32[1,1]{1,0:T(1,128)} fusion(s32[4,16]{1,0:T(4,128)} %refs_1_.1, s32[]{:T(128)S(6)} %select_n.125), kind=kLoop, calls=%fused_computation.96 | loop fusion | bytes 12 | tf_op jit(solution)/shard_map/dynamic_slice | solution.py:578
  5.1 2.3 %copy-done = bf16[20,64,1792]{2,1,0:T(8,128)(2,1)S(1)} copy-done((bf16[20,64,1792]{2,1,0:T(8,128)(2,1)S(1)}, bf16[20,64,1792]{2,1,0:T(8,128)(2,1)}, u32[]{:S(2)}) %copy-start) | copy-done | bytes 4587544
  7.4 2.3 %copy-done.3 = bf16[20,64,1792]{2,1,0:T(8,128)(2,1)S(1)} copy-done((bf16[20,64,1792]{2,1,0:T(8,128)(2,1)S(1)}, bf16[20,64,1792]{2,1,0:T(8,128)(2,1)}, u32[]{:S(2)}) %copy-start.3) | copy-done | bytes 4587544
  9.7 1.3 %pick_page.1.refs_0_ = bf16[2,64,1792]{2,1,0:T(8,128)(2,1)S(1)} custom-call(s32[1]{0:T(128)} %bitcast.42.page_ref, bf16[20,64,1792]{2,1,0:T(8,128)(2,1)S(1)} %copy-done, bf16[20,64,1792]{2,1,0:T(8,128)(2,1)S(1)} %copy-done.3), custom_call_target="tpu_custom_call" | custom-call | bytes 917504 | tf_op jit(solution)/shard_map/pick_page/pallas_call | solution.py:112
  11.0 3.0 %collective-permute-start.19 = (bf16[2,64,1792]{2,1,0:T(8,128)(2,1)S(1)}, bf16[2,64,1792]{2,1,0:T(8,128)(2,1)S(1)}, u32[]{:S(2)}, u32[]{:S(2)}) collective-permute-start(bf16[2,64,1792]{2,1,0:T(8,128)(2,1)S(1)} %pick_page.1.refs_0_), channel_id=1, source_target_pairs={{0,8},{4,12},{8,0},{12,4},{16,24},{20,28},{24,16},{28,20},{1,9},{5... | collective-permute-start | bytes 1376264 | tf_op jit(solution)/shard_map/ppermute | solution.py:36
  14.0 1.5 %collective-permute-start.20 = (bf16[2,64,1792]{2,1,0:T(8,128)(2,1)S(1)}, bf16[2,64,1792]{2,1,0:T(8,128)(2,1)S(1)}, u32[]{:S(2)}, u32[]{:S(2)}) collective-permute-start(bf16[2,64,1792]{2,1,0:T(8,128)(2,1)S(1)} %pick_page.1.refs_0_), channel_id=1, source_target_pairs={{0,16},{4,20},{8,24},{12,28},{16,0},{20,4},{24,8},{28,12},{1,17},{... | collective-permute-start | bytes 1376264 | tf_op jit(solution)/shard_map/ppermute | solution.py:36
  16.6 0.7 pad_add_fusion.refs_0_
  17.3 2.3 %copy-done.1 = bf16[20,64,1792]{2,1,0:T(8,128)(2,1)S(1)} copy-done((bf16[20,64,1792]{2,1,0:T(8,128)(2,1)S(1)}, bf16[20,64,1792]{2,1,0:T(8,128)(2,1)}, u32[]{:S(2)}) %copy-start.1) | copy-done | bytes 4587544
  19.6 2.3 %copy-done.4 = bf16[20,64,1792]{2,1,0:T(8,128)(2,1)S(1)} copy-done((bf16[20,64,1792]{2,1,0:T(8,128)(2,1)S(1)}, bf16[20,64,1792]{2,1,0:T(8,128)(2,1)}, u32[]{:S(2)}) %copy-start.4) | copy-done | bytes 4587544
  21.9 5.9 %copy_pools.1 = (bf16[20,64,1792]{2,1,0:T(8,128)(2,1)}, bf16[20,64,1792]{2,1,0:T(8,128)(2,1)}) custom-call(bf16[20,64,1792]{2,1,0:T(8,128)(2,1)S(1)} %copy-done.1, bf16[20,64,1792]{2,1,0:T(8,128)(2,1)S(1)} %copy-done.4), custom_call_target="tpu_custom_call" | custom-call | bytes 18350080 | tf_op jit(solution)/shard_map/copy_pools/pallas_call | solution.py:83
  28.1 2.0 %collective-permute-start.2 = (bf16[2,4,1024]{2,1,0:T(4,128)(2,1)S(1)}, bf16[2,4,1024]{2,1,0:T(4,128)(2,1)S(1)}, u32[]{:S(2)}, u32[]{:S(2)}) collective-permute-start(bf16[2,4,1024]{2,1,0:T(4,128)(2,1)S(1)} %pad_maximum_fusion.7), channel_id=1, source_target_pairs={{0,16},{4,20},{8,24},{12,28},{16,0},{20,4},{24,8},{28,12},{1,17},{... | collective-permute-start | bytes 49160 | tf_op jit(solution)/shard_map/ppermute | solution.py:36
  30.1 1.6 %collective-permute-start.1 = (bf16[2,4,1024]{2,1,0:T(4,128)(2,1)S(1)}, bf16[2,4,1024]{2,1,0:T(4,128)(2,1)S(1)}, u32[]{:S(2)}, u32[]{:S(2)}) collective-permute-start(bf16[2,4,1024]{2,1,0:T(4,128)(2,1)S(1)} %pad_maximum_fusion.6), channel_id=1, source_target_pairs={{0,8},{4,12},{8,0},{12,4},{16,24},{20,28},{24,16},{28,20},{1,9},{5... | collective-permute-start | bytes 49160 | tf_op jit(solution)/shard_map/ppermute | solution.py:36
  31.7 1.1 %collective-permute-done.3.refs_3_ = bf16[2,4,1024]{2,1,0:T(4,128)(2,1)S(1)} collective-permute-done((bf16[2,4,1024]{2,1,0:T(4,128)(2,1)S(1)}, bf16[2,4,1024]{2,1,0:T(4,128)(2,1)S(1)}, u32[]{:S(2)}, u32[]{:S(2)}) %collective-permute-start.3) | collective-permute-done | bytes 16416 | tf_op jit(solution)/shard_map/ppermute | solution.py:36
  32.8 1.1 collective-permute-done.1.refs_1_
  33.9 3.7 %copy-done.6 = bf16[896,14,384]{2,0,1:T(8,128)(2,1)S(1)} copy-done((bf16[896,14,384]{2,0,1:T(8,128)(2,1)S(1)}, bf16[896,14,384]{2,0,1:T(8,128)(2,1)}, u32[]{:S(2)}) %copy-start.6) | copy-done | bytes 9633816
  37.7 2.4 %project.1 = (f32[4,4,5376]{2,1,0:T(4,128)S(1)}, f32[4,4,5376]{2,1,0:T(4,128)S(1)}) custom-call(bf16[2,4,1024]{2,1,0:T(4,128)(2,1)S(1)} %get-tuple-element.66.refs_0_, bf16[2,4,1024]{2,1,0:T(4,128)(2,1)S(1)} %collective-permute-done.1.refs_1_, bf16[2,4,1024]{2,1,0:T(4,128)(2,1)S(1)} %collective-permute-done.2.refs_2_, ...), custom_call_target="tpu_custom_call" | custom-call | flops 308281344 | bytes 9633792 | tf_op jit(solution)/shard_map/project/pallas_call | solution.py:177
  40.6 0.7 select_reduce_fusion
  41.9 1.6 %collective-permute-start.5 = (f32[4,5376]{1,0:T(4,128)S(1)}, f32[4,5376]{1,0:T(4,128)S(1)}, u32[]{:S(2)}, u32[]{:S(2)}) collective-permute-start(f32[4,5376]{1,0:T(4,128)S(1)} %get-tuple-element.40), channel_id=1, source_target_pairs={{0,8},{4,12},{8,0},{12,4},{16,24},{20,28},{24,16},{28,20},{1,9},{5... | collective-permute-start | bytes 258056 | tf_op jit(solution)/shard_map/ppermute | solution.py:36
  44.0 1.5 %collective-permute-start.7 = (f32[4,5376]{1,0:T(4,128)S(1)}, f32[4,5376]{1,0:T(4,128)S(1)}, u32[]{:S(2)}, u32[]{:S(2)}) collective-permute-start(f32[4,5376]{1,0:T(4,128)S(1)} %get-tuple-element.38), channel_id=1, source_target_pairs={{0,24},{4,28},{8,16},{12,20},{16,8},{20,12},{24,0},{28,4},{1,25},{... | collective-permute-start | bytes 258056 | tf_op jit(solution)/shard_map/ppermute | solution.py:36
  45.5 1.1 collective-permute-done.5.refs_3_
  46.6 3.2 %collective-permute-done.6.refs_4_ = f32[4,5376]{1,0:T(4,128)S(1)} collective-permute-done((f32[4,5376]{1,0:T(4,128)S(1)}, f32[4,5376]{1,0:T(4,128)S(1)}, u32[]{:S(2)}, u32[]{:S(2)}) %collective-permute-start.6) | collective-permute-done | bytes 86048 | tf_op jit(solution)/shard_map/ppermute | solution.py:36
  49.8 2.3 %copy-done.2 = bf16[20,64,1792]{2,1,0:T(8,128)(2,1)S(1)} copy-done((bf16[20,64,1792]{2,1,0:T(8,128)(2,1)S(1)}, bf16[20,64,1792]{2,1,0:T(8,128)(2,1)}, u32[]{:S(2)}) %copy-start.2) | copy-done | bytes 4587544
  52.1 2.3 %copy-done.5 = bf16[20,64,1792]{2,1,0:T(8,128)(2,1)S(1)} copy-done((bf16[20,64,1792]{2,1,0:T(8,128)(2,1)S(1)}, bf16[20,64,1792]{2,1,0:T(8,128)(2,1)}, u32[]{:S(2)}) %copy-start.5) | copy-done | bytes 4587544
  54.4 5.2 %attend.1 = (bf16[4,32,256]{2,1,0:T(8,128)(2,1)S(1)}, bf16[4,32,256]{2,1,0:T(8,128)(2,1)S(1)}, bf16[20,64,1792]{2,1,0:T(8,128)(2,1)}, bf16[20,64,1792]{2,1,0:T(8,128)(2,1)}) custom-call(s32[7]{0:T(128)S(1)} %pad_add_fusion.refs_0_, s32[4,16]{1,0:T(4,128)S(1)} %copy-done.9, ...), custom_call_target="tpu_custom_call", output_to_operand_aliasing={{2}: (10, {}), {3}: (11, {})} | custom-call | flops 146800640 | bytes 9175040 | tf_op jit(solution)/shard_map/attend/pallas_call | solution.py:433
  59.6 9.9 %collective-permute-start.8 = (bf16[4,32,256]{2,1,0:T(8,128)(2,1)S(1)}, bf16[4,32,256]{2,1,0:T(8,128)(2,1)S(1)}, u32[]{:S(2)}, u32[]{:S(2)}) collective-permute-start(bf16[4,32,256]{2,1,0:T(8,128)(2,1)S(1)} %get-tuple-element.20), channel_id=1, source_target_pairs={{0,4},{4,0},{8,12},{12,8},{16,20},{20,16},{24,28},{28,24},{1,5},{5... | collective-permute-start | bytes 196616 | tf_op jit(solution)/shard_map/ppermute | solution.py:36
  69.5 0.9 collective-permute-done.8
  70.4 1.5 %collective-permute-start.9 = (bf16[2,32,256]{2,1,0:T(8,128)(2,1)S(1)}, bf16[2,32,256]{2,1,0:T(8,128)(2,1)S(1)}, u32[]{:S(2)}, u32[]{:S(2)}) collective-permute-start(bf16[2,32,256]{2,1,0:T(8,128)(2,1)S(1)} %pad_maximum_fusion.2), channel_id=1, source_target_pairs={{0,8},{4,12},{8,0},{12,4},{16,24},{20,28},{24,16},{28,20},{1,9},{5... | collective-permute-start | bytes 98312 | tf_op jit(solution)/shard_map/ppermute | solution.py:36
  72.0 2.4 %collective-permute-start.10 = (bf16[2,32,256]{2,1,0:T(8,128)(2,1)S(1)}, bf16[2,32,256]{2,1,0:T(8,128)(2,1)S(1)}, u32[]{:S(2)}, u32[]{:S(2)}) collective-permute-start(bf16[2,32,256]{2,1,0:T(8,128)(2,1)S(1)} %pad_maximum_fusion.3), channel_id=1, source_target_pairs={{0,16},{4,20},{8,24},{12,28},{16,0},{20,4},{24,8},{28,12},{1,17},{... | collective-permute-start | bytes 98312 | tf_op jit(solution)/shard_map/ppermute | solution.py:36
  74.4 3.3 %collective-permute-start.21 = (bf16[2,64,1792]{2,1,0:T(8,128)(2,1)S(1)}, bf16[2,64,1792]{2,1,0:T(8,128)(2,1)S(1)}, u32[]{:S(2)}, u32[]{:S(2)}) collective-permute-start(bf16[2,64,1792]{2,1,0:T(8,128)(2,1)S(1)} %pick_page.1.refs_0_), channel_id=1, source_target_pairs={{0,24},{4,28},{8,16},{12,20},{16,8},{20,12},{24,0},{28,4},{1,25},{... | collective-permute-start | bytes 1376264 | tf_op jit(solution)/shard_map/ppermute | solution.py:36
  77.7 1.9 %collective-permute-done.11.refs_3_ = bf16[2,32,256]{2,1,0:T(8,128)(2,1)S(1)} collective-permute-done((bf16[2,32,256]{2,1,0:T(8,128)(2,1)S(1)}, bf16[2,32,256]{2,1,0:T(8,128)(2,1)S(1)}, u32[]{:S(2)}, u32[]{:S(2)}) %collective-permute-start.11) | collective-permute-done | bytes 32800 | tf_op jit(solution)/shard_map/ppermute | solution.py:36
  79.6 2.4 %out_project.1 = (f32[4,16,1792]{2,1,0:T(8,128)S(1)}, f32[4,16,1792]{2,1,0:T(8,128)}) custom-call(s32[1]{0:T(128)} %bitcast.column_ref, bf16[32,64]{1,0:T(8,128)(2,1)S(1)} %fusion.18.order_ref, bf16[2,32,256]{2,1,0:T(8,128)(2,1)S(1)} %get-tuple-element.61.refs_0_, bf16[2,32,256]{2,1,0:T(8,128)(2,1)S(1)} %collective-permute-done.9.refs_1_, ...), custom_call_target="tpu_custom_call" | custom-call | flops 102760448 | bytes 3211264 | tf_op jit(solution)/shard_map/out_project/pallas_call | solution.py:483
  82.0 0.6 iota_compare_fusion.3
  82.6 0.8 dynamic_slice.13
  83.4 0.7 select_reduce_fusion.2
  90.3 1.4 %pad_add_fusion.1.numbers_ref = s32[3]{0:T(128)S(1)} fusion(s32[1]{0:T(128)} %bitcast.41, s32[1]{0:T(128)} %bitcast.40, s32[1]{0:T(128)} %bitcast.39), kind=kLoop, calls=%fused_computation.105 | loop fusion | flops 6 | bytes 24 | tf_op jit(solution)/shard_map/stack | solution.py:638
  92.0 0.6 collective-permute-start.22
  92.6 1.9 %add.108 = f32[4,16,1792]{2,1,0:T(8,128)} add(f32[4,16,1792]{2,1,0:T(8,128)S(1)} %get-tuple-element.21, f32[4,16,1792]{2,1,0:T(8,128)} %collective-permute-done.12) | non-fusion elementwise | flops 114688 | bytes 1376256 | tf_op jit(solution)/shard_map/add | solution.py:652
  94.6 1.1 %reshape.90 = f32[4,4,4,1792]{3,2,1,0:T(4,128)S(1)} reshape(f32[4,16,1792]{2,1,0:T(8,128)} %add.108) | data formatting | bytes 917504 | tf_op jit(solution)/shard_map/reshape | solution.py:652
  95.9 1.3 %collective-permute-start.14 = (bf16[4,4,1792]{2,1,0:T(4,128)(2,1)S(1)}, bf16[4,4,1792]{2,1,0:T(4,128)(2,1)S(1)}, u32[]{:S(2)}, u32[]{:S(2)}) collective-permute-start(bf16[4,4,1792]{2,1,0:T(4,128)(2,1)S(1)} %get-tuple-element.44), channel_id=1, source_target_pairs={{0,16},{4,20},{8,24},{12,28},{16,0},{20,4},{24,8},{28,12},{1,17},{... | collective-permute-start | bytes 172040 | tf_op jit(solution)/shard_map/ppermute | solution.py:36
  97.2 2.2 %collective-permute-start.13 = (bf16[4,4,1792]{2,1,0:T(4,128)(2,1)S(1)}, bf16[4,4,1792]{2,1,0:T(4,128)(2,1)S(1)}, u32[]{:S(2)}, u32[]{:S(2)}) collective-permute-start(bf16[4,4,1792]{2,1,0:T(4,128)(2,1)S(1)} %get-tuple-element.42), channel_id=1, source_target_pairs={{0,8},{4,12},{8,0},{12,4},{16,24},{20,28},{24,16},{28,20},{1,9},{5... | collective-permute-start | bytes 172040 | tf_op jit(solution)/shard_map/ppermute | solution.py:36
  99.3 1.9 %collective-permute-done.15 = bf16[4,4,1792]{2,1,0:T(4,128)(2,1)S(1)} collective-permute-done((bf16[4,4,1792]{2,1,0:T(4,128)(2,1)S(1)}, bf16[4,4,1792]{2,1,0:T(4,128)(2,1)S(1)}, u32[]{:S(2)}, u32[]{:S(2)}) %collective-permute-start.15) | collective-permute-done | bytes 57376 | tf_op jit(solution)/shard_map/ppermute | solution.py:36
  101.6 3.7 %collective-permute-start.18 = (bf16[4,1792]{1,0:T(4,128)(2,1)S(1)}, bf16[4,1792]{1,0:T(4,128)(2,1)S(1)}, u32[]{:S(2)}, u32[]{:S(2)}) collective-permute-start(bf16[4,1792]{1,0:T(4,128)(2,1)S(1)} %get-tuple-element.58), channel_id=1, source_target_pairs={{0,3},{1,2},{2,1},{3,0},{4,7},{5,6},{6,5},{7,4},{8,11},{9,10},{10,... | collective-permute-start | bytes 43016 | tf_op jit(solution)/shard_map/ppermute | solution.py:36
  105.2 0.8 collective-permute-start.16
  106.0 0.7 constant_dynamic-slice_fusion
  106.8 1.7 %place_page.1 = (bf16[20,64,1792]{2,1,0:T(8,128)(2,1)}, bf16[20,64,1792]{2,1,0:T(8,128)(2,1)}) custom-call(s32[3]{0:T(128)S(1)} %pad_add_fusion.1.numbers_ref, bf16[2,1792]{1,0:T(2,128)(2,1)S(1)} %slice.179.rows_ref, bf16[2,64,1792]{2,1,0:T(8,128)(2,1)S(1)} %pick_page.1.refs_0_, ...), custom_call_target="tpu_custom_call", output_to_operand_aliasing={{0}: (7, {}), {1}: (8, {})} | custom-call | bytes 1835008 | tf_op jit(solution)/shard_map/place_page/pallas_call | solution.py:533
  108.5 1.4 %collective-permute-done.17 = bf16[4,1792]{1,0:T(4,128)(2,1)S(1)} collective-permute-done((bf16[4,1792]{1,0:T(4,128)(2,1)S(1)}, bf16[4,1792]{1,0:T(4,128)(2,1)S(1)}, u32[]{:S(2)}, u32[]{:S(2)}) %collective-permute-start.17) | collective-permute-done | bytes 14368 | tf_op jit(solution)/shard_map/ppermute | solution.py:36
  109.9 0.7 fusion.16
  (97 shorter events, 3.8 us)
Async XLA Ops:
  5.1 2.3 %copy-start = (bf16[20,64,1792]{2,1,0:T(8,128)(2,1)S(1)}, bf16[20,64,1792]{2,1,0:T(8,128)(2,1)}, u32[]{:S(2)}) copy-start(bf16[20,64,1792]{2,1,0:T(8,128)(2,1)} %key_ref.3) | copy-start | bytes 13762564
  7.4 2.3 %copy-start.3 = (bf16[20,64,1792]{2,1,0:T(8,128)(2,1)S(1)}, bf16[20,64,1792]{2,1,0:T(8,128)(2,1)}, u32[]{:S(2)}) copy-start(bf16[20,64,1792]{2,1,0:T(8,128)(2,1)} %value_ref.3) | copy-start | bytes 13762564
  9.7 5.9 %copy-start.14 = (s32[4]{0:T(128)S(1)}, s32[4]{0:T(128)}, u32[]{:S(2)}) copy-start(s32[4]{0:T(128)} %param.22) | copy-start | bytes 52
  9.7 5.9 %copy-start.15 = (s32[4]{0:T(128)S(1)}, s32[4]{0:T(128)}, u32[]{:S(2)}) copy-start(s32[4]{0:T(128)} %param.25) | copy-start | bytes 52
  9.7 6.0 %copy-start.8 = (bf16[4,7168]{1,0:T(4,128)(2,1)S(1)}, bf16[4,7168]{1,0:T(4,128)(2,1)}, u32[]{:S(2)}) copy-start(bf16[4,7168]{1,0:T(4,128)(2,1)} %refs_7_.1) | copy-start | bytes 172036
  9.7 6.5 %copy-start.11 = (f32[7168]{0:T(1024)S(1)}, f32[7168]{0:T(1024)}, u32[]{:S(2)}) copy-start(f32[7168]{0:T(1024)} %param.15) | copy-start | bytes 86020
  9.7 6.5 %copy-start.12 = (f32[7168]{0:T(1024)S(1)}, f32[7168]{0:T(1024)}, u32[]{:S(2)}) copy-start(f32[7168]{0:T(1024)} %param.14) | copy-start | bytes 86020
  11.0 80.7 %collective-permute-start.19 = (bf16[2,64,1792]{2,1,0:T(8,128)(2,1)S(1)}, bf16[2,64,1792]{2,1,0:T(8,128)(2,1)S(1)}, u32[]{:S(2)}, u32[]{:S(2)}) collective-permute-start(bf16[2,64,1792]{2,1,0:T(8,128)(2,1)S(1)} %pick_page.1.refs_0_), channel_id=1, source_target_pairs={{0,8},{4,12},{8,0},{12,4},{16,24},{20,28},{24,16},{28,20},{1,9},{5... | collective-permute-start | bytes 1376264 | tf_op jit(solution)/shard_map/ppermute | solution.py:36
  14.0 77.7 %collective-permute-start.20 = (bf16[2,64,1792]{2,1,0:T(8,128)(2,1)S(1)}, bf16[2,64,1792]{2,1,0:T(8,128)(2,1)S(1)}, u32[]{:S(2)}, u32[]{:S(2)}) collective-permute-start(bf16[2,64,1792]{2,1,0:T(8,128)(2,1)S(1)} %pick_page.1.refs_0_), channel_id=1, source_target_pairs={{0,16},{4,20},{8,24},{12,28},{16,0},{20,4},{24,8},{28,12},{1,17},{... | collective-permute-start | bytes 1376264 | tf_op jit(solution)/shard_map/ppermute | solution.py:36
  16.5 11.4 %collective-permute-start = (bf16[4,4,1024]{2,1,0:T(4,128)(2,1)S(1)}, bf16[4,4,1024]{2,1,0:T(4,128)(2,1)S(1)}, u32[]{:S(2)}, u32[]{:S(2)}) collective-permute-start(bf16[4,4,1024]{2,1,0:T(4,128)(2,1)S(1)} %fusion.10), channel_id=1, source_target_pairs={{0,4},{4,0},{8,12},{12,8},{16,20},{20,16},{24,28},{28,24},{1,5},{5... | collective-permute-start | bytes 98312 | tf_op jit(solution)/shard_map/ppermute | solution.py:36
  17.3 2.3 %copy-start.1 = (bf16[20,64,1792]{2,1,0:T(8,128)(2,1)S(1)}, bf16[20,64,1792]{2,1,0:T(8,128)(2,1)}, u32[]{:S(2)}) copy-start(bf16[20,64,1792]{2,1,0:T(8,128)(2,1)} %key_ref.3) | copy-start | bytes 13762564
  19.6 2.3 %copy-start.4 = (bf16[20,64,1792]{2,1,0:T(8,128)(2,1)S(1)}, bf16[20,64,1792]{2,1,0:T(8,128)(2,1)}, u32[]{:S(2)}) copy-start(bf16[20,64,1792]{2,1,0:T(8,128)(2,1)} %value_ref.3) | copy-start | bytes 13762564
  21.9 5.9 %copy-start.13 = (f32[14,384]{1,0:T(8,128)S(1)}, f32[14,384]{1,0:T(8,128)}, u32[]{:S(2)}) copy-start(f32[14,384]{1,0:T(8,128)} %param.17) | copy-start | bytes 64516
  28.0 4.9 %collective-permute-start.3 = (bf16[2,4,1024]{2,1,0:T(4,128)(2,1)S(1)}, bf16[2,4,1024]{2,1,0:T(4,128)(2,1)S(1)}, u32[]{:S(2)}, u32[]{:S(2)}) collective-permute-start(bf16[2,4,1024]{2,1,0:T(4,128)(2,1)S(1)} %pad_maximum_fusion.8), channel_id=1, source_target_pairs={{0,24},{4,28},{8,16},{12,20},{16,8},{20,12},{24,0},{28,4},{1,25},{... | collective-permute-start | bytes 49160 | tf_op jit(solution)/shard_map/ppermute | solution.py:36
  28.1 4.8 %collective-permute-start.2 = (bf16[2,4,1024]{2,1,0:T(4,128)(2,1)S(1)}, bf16[2,4,1024]{2,1,0:T(4,128)(2,1)S(1)}, u32[]{:S(2)}, u32[]{:S(2)}) collective-permute-start(bf16[2,4,1024]{2,1,0:T(4,128)(2,1)S(1)} %pad_maximum_fusion.7), channel_id=1, source_target_pairs={{0,16},{4,20},{8,24},{12,28},{16,0},{20,4},{24,8},{28,12},{1,17},{... | collective-permute-start | bytes 49160 | tf_op jit(solution)/shard_map/ppermute | solution.py:36
  30.1 3.8 %collective-permute-start.1 = (bf16[2,4,1024]{2,1,0:T(4,128)(2,1)S(1)}, bf16[2,4,1024]{2,1,0:T(4,128)(2,1)S(1)}, u32[]{:S(2)}, u32[]{:S(2)}) collective-permute-start(bf16[2,4,1024]{2,1,0:T(4,128)(2,1)S(1)} %pad_maximum_fusion.6), channel_id=1, source_target_pairs={{0,8},{4,12},{8,0},{12,4},{16,24},{20,28},{24,16},{28,20},{1,9},{5... | collective-permute-start | bytes 49160 | tf_op jit(solution)/shard_map/ppermute | solution.py:36
  33.9 3.7 %copy-start.6 = (bf16[896,14,384]{2,0,1:T(8,128)(2,1)S(1)}, bf16[896,14,384]{2,0,1:T(8,128)(2,1)}, u32[]{:S(2)}) copy-start(bf16[896,14,384]{2,0,1:T(8,128)(2,1)} %param.16) | copy-start | bytes 28901380
  37.7 12.2 %copy-start.9 = (s32[4,16]{1,0:T(4,128)S(1)}, s32[4,16]{1,0:T(4,128)}, u32[]{:S(2)}) copy-start(s32[4,16]{1,0:T(4,128)} %refs_1_.1) | copy-start | bytes 772
  40.1 1.7 %collective-permute-start.4 = (f32[4,4,5376]{2,1,0:T(4,128)S(1)}, f32[4,4,5376]{2,1,0:T(4,128)S(1)}, u32[]{:S(2)}, u32[]{:S(2)}) collective-permute-start(f32[4,4,5376]{2,1,0:T(4,128)S(1)} %get-tuple-element.16), channel_id=1, source_target_pairs={{0,4},{4,0},{8,12},{12,8},{16,20},{20,16},{24,28},{28,24},{1,5},{5... | collective-permute-start | bytes 1032200 | tf_op jit(solution)/shard_map/ppermute | solution.py:36
  41.9 4.6 %collective-permute-start.5 = (f32[4,5376]{1,0:T(4,128)S(1)}, f32[4,5376]{1,0:T(4,128)S(1)}, u32[]{:S(2)}, u32[]{:S(2)}) collective-permute-start(f32[4,5376]{1,0:T(4,128)S(1)} %get-tuple-element.40), channel_id=1, source_target_pairs={{0,8},{4,12},{8,0},{12,4},{16,24},{20,28},{24,16},{28,20},{1,9},{5... | collective-permute-start | bytes 258056 | tf_op jit(solution)/shard_map/ppermute | solution.py:36
  43.5 6.3 %collective-permute-start.6 = (f32[4,5376]{1,0:T(4,128)S(1)}, f32[4,5376]{1,0:T(4,128)S(1)}, u32[]{:S(2)}, u32[]{:S(2)}) collective-permute-start(f32[4,5376]{1,0:T(4,128)S(1)} %get-tuple-element.39), channel_id=1, source_target_pairs={{0,16},{4,20},{8,24},{12,28},{16,0},{20,4},{24,8},{28,12},{1,17},{... | collective-permute-start | bytes 258056 | tf_op jit(solution)/shard_map/ppermute | solution.py:36
  44.0 5.8 %collective-permute-start.7 = (f32[4,5376]{1,0:T(4,128)S(1)}, f32[4,5376]{1,0:T(4,128)S(1)}, u32[]{:S(2)}, u32[]{:S(2)}) collective-permute-start(f32[4,5376]{1,0:T(4,128)S(1)} %get-tuple-element.38), channel_id=1, source_target_pairs={{0,24},{4,28},{8,16},{12,20},{16,8},{20,12},{24,0},{28,4},{1,25},{... | collective-permute-start | bytes 258056 | tf_op jit(solution)/shard_map/ppermute | solution.py:36
  49.8 2.3 %copy-start.2 = (bf16[20,64,1792]{2,1,0:T(8,128)(2,1)S(1)}, bf16[20,64,1792]{2,1,0:T(8,128)(2,1)}, u32[]{:S(2)}) copy-start(bf16[20,64,1792]{2,1,0:T(8,128)(2,1)} %key_ref.3) | copy-start | bytes 13762564
  52.1 2.3 %copy-start.5 = (bf16[20,64,1792]{2,1,0:T(8,128)(2,1)S(1)}, bf16[20,64,1792]{2,1,0:T(8,128)(2,1)}, u32[]{:S(2)}) copy-start(bf16[20,64,1792]{2,1,0:T(8,128)(2,1)} %value_ref.3) | copy-start | bytes 13762564
  54.4 25.1 %copy-start.7 = (bf16[14,16,7168]{2,1,0:T(8,128)(2,1)S(1)}, bf16[14,16,7168]{2,1,0:T(8,128)(2,1)}, u32[]{:S(2)}) copy-start(bf16[14,16,7168]{2,1,0:T(8,128)(2,1)} %param.18) | copy-start | bytes 9633796
  59.6 10.8 %collective-permute-start.8 = (bf16[4,32,256]{2,1,0:T(8,128)(2,1)S(1)}, bf16[4,32,256]{2,1,0:T(8,128)(2,1)S(1)}, u32[]{:S(2)}, u32[]{:S(2)}) collective-permute-start(bf16[4,32,256]{2,1,0:T(8,128)(2,1)S(1)} %get-tuple-element.20), channel_id=1, source_target_pairs={{0,4},{4,0},{8,12},{12,8},{16,20},{20,16},{24,28},{28,24},{1,5},{5... | collective-permute-start | bytes 196616 | tf_op jit(solution)/shard_map/ppermute | solution.py:36
  70.4 4.0 %collective-permute-start.9 = (bf16[2,32,256]{2,1,0:T(8,128)(2,1)S(1)}, bf16[2,32,256]{2,1,0:T(8,128)(2,1)S(1)}, u32[]{:S(2)}, u32[]{:S(2)}) collective-permute-start(bf16[2,32,256]{2,1,0:T(8,128)(2,1)S(1)} %pad_maximum_fusion.2), channel_id=1, source_target_pairs={{0,8},{4,12},{8,0},{12,4},{16,24},{20,28},{24,16},{28,20},{1,9},{5... | collective-permute-start | bytes 98312 | tf_op jit(solution)/shard_map/ppermute | solution.py:36
  72.0 5.8 %collective-permute-start.10 = (bf16[2,32,256]{2,1,0:T(8,128)(2,1)S(1)}, bf16[2,32,256]{2,1,0:T(8,128)(2,1)S(1)}, u32[]{:S(2)}, u32[]{:S(2)}) collective-permute-start(bf16[2,32,256]{2,1,0:T(8,128)(2,1)S(1)} %pad_maximum_fusion.3), channel_id=1, source_target_pairs={{0,16},{4,20},{8,24},{12,28},{16,0},{20,4},{24,8},{28,12},{1,17},{... | collective-permute-start | bytes 98312 | tf_op jit(solution)/shard_map/ppermute | solution.py:36
  74.4 5.2 %collective-permute-start.11 = (bf16[2,32,256]{2,1,0:T(8,128)(2,1)S(1)}, bf16[2,32,256]{2,1,0:T(8,128)(2,1)S(1)}, u32[]{:S(2)}, u32[]{:S(2)}) collective-permute-start(bf16[2,32,256]{2,1,0:T(8,128)(2,1)S(1)} %pad_maximum_fusion.4), channel_id=1, source_target_pairs={{0,24},{4,28},{8,16},{12,20},{16,8},{20,12},{24,0},{28,4},{1,25},{... | collective-permute-start | bytes 98312 | tf_op jit(solution)/shard_map/ppermute | solution.py:36
  74.4 17.3 %collective-permute-start.21 = (bf16[2,64,1792]{2,1,0:T(8,128)(2,1)S(1)}, bf16[2,64,1792]{2,1,0:T(8,128)(2,1)S(1)}, u32[]{:S(2)}, u32[]{:S(2)}) collective-permute-start(bf16[2,64,1792]{2,1,0:T(8,128)(2,1)S(1)} %pick_page.1.refs_0_), channel_id=1, source_target_pairs={{0,24},{4,28},{8,16},{12,20},{16,8},{20,12},{24,0},{28,4},{1,25},{... | collective-permute-start | bytes 1376264 | tf_op jit(solution)/shard_map/ppermute | solution.py:36
  82.0 10.6 %collective-permute-start.12 = (f32[4,16,1792]{2,1,0:T(8,128)}, f32[4,16,1792]{2,1,0:T(8,128)}, u32[]{:S(2)}, u32[]{:S(2)}) collective-permute-start(f32[4,16,1792]{2,1,0:T(8,128)} %get-tuple-element.22), channel_id=1, source_target_pairs={{0,4},{4,0},{8,12},{12,8},{16,20},{20,16},{24,28},{28,24},{1,5},{5... | collective-permute-start | bytes 1376264 | tf_op jit(solution)/shard_map/ppermute | solution.py:36
  92.0 14.8 %collective-permute-start.22 = (bf16[2,64,1792]{2,1,0:T(8,128)(2,1)S(1)}, bf16[2,64,1792]{2,1,0:T(8,128)(2,1)S(1)}, u32[]{:S(2)}, u32[]{:S(2)}) collective-permute-start(bf16[2,64,1792]{2,1,0:T(8,128)(2,1)S(1)} %choose_page.1), channel_id=1, source_target_pairs={{0,4},{4,0},{8,12},{12,8},{16,20},{20,16},{24,28},{28,24},{1,5},{5... | collective-permute-start | bytes 1376264 | tf_op jit(solution)/shard_map/ppermute | solution.py:36
  92.6 8.6 %copy-start.10 = (bf16[4,2,32,256]{3,2,1,0:T(8,128)(2,1)}, bf16[4,2,32,256]{3,2,1,0:T(8,128)(2,1)S(1)}, u32[]{:S(2)}) copy-start(bf16[4,2,32,256]{3,2,1,0:T(8,128)(2,1)S(1)} %pad_maximum_fusion) | copy-start | bytes 393220
  95.8 5.4 %collective-permute-start.15 = (bf16[4,4,1792]{2,1,0:T(4,128)(2,1)S(1)}, bf16[4,4,1792]{2,1,0:T(4,128)(2,1)S(1)}, u32[]{:S(2)}, u32[]{:S(2)}) collective-permute-start(bf16[4,4,1792]{2,1,0:T(4,128)(2,1)S(1)} %get-tuple-element.43), channel_id=1, source_target_pairs={{0,24},{4,28},{8,16},{12,20},{16,8},{20,12},{24,0},{28,4},{1,25},{... | collective-permute-start | bytes 172040 | tf_op jit(solution)/shard_map/ppermute | solution.py:36
  95.9 5.3 %collective-permute-start.14 = (bf16[4,4,1792]{2,1,0:T(4,128)(2,1)S(1)}, bf16[4,4,1792]{2,1,0:T(4,128)(2,1)S(1)}, u32[]{:S(2)}, u32[]{:S(2)}) collective-permute-start(bf16[4,4,1792]{2,1,0:T(4,128)(2,1)S(1)} %get-tuple-element.44), channel_id=1, source_target_pairs={{0,16},{4,20},{8,24},{12,28},{16,0},{20,4},{24,8},{28,12},{1,17},{... | collective-permute-start | bytes 172040 | tf_op jit(solution)/shard_map/ppermute | solution.py:36
  97.2 4.3 %collective-permute-start.13 = (bf16[4,4,1792]{2,1,0:T(4,128)(2,1)S(1)}, bf16[4,4,1792]{2,1,0:T(4,128)(2,1)S(1)}, u32[]{:S(2)}, u32[]{:S(2)}) collective-permute-start(bf16[4,4,1792]{2,1,0:T(4,128)(2,1)S(1)} %get-tuple-element.42), channel_id=1, source_target_pairs={{0,8},{4,12},{8,0},{12,4},{16,24},{20,28},{24,16},{28,20},{1,9},{5... | collective-permute-start | bytes 172040 | tf_op jit(solution)/shard_map/ppermute | solution.py:36
  101.6 6.9 %collective-permute-start.18 = (bf16[4,1792]{1,0:T(4,128)(2,1)S(1)}, bf16[4,1792]{1,0:T(4,128)(2,1)S(1)}, u32[]{:S(2)}, u32[]{:S(2)}) collective-permute-start(bf16[4,1792]{1,0:T(4,128)(2,1)S(1)} %get-tuple-element.58), channel_id=1, source_target_pairs={{0,3},{1,2},{2,1},{3,0},{4,7},{5,6},{6,5},{7,4},{8,11},{9,10},{10,... | collective-permute-start | bytes 43016 | tf_op jit(solution)/shard_map/ppermute | solution.py:36
  105.2 4.6 %collective-permute-start.17 = (bf16[4,1792]{1,0:T(4,128)(2,1)S(1)}, bf16[4,1792]{1,0:T(4,128)(2,1)S(1)}, u32[]{:S(2)}, u32[]{:S(2)}) collective-permute-start(bf16[4,1792]{1,0:T(4,128)(2,1)S(1)} %get-tuple-element.59), channel_id=1, source_target_pairs={{0,2},{1,3},{2,0},{3,1},{4,6},{5,7},{6,4},{7,5},{8,10},{9,11},{10,... | collective-permute-start | bytes 43016 | tf_op jit(solution)/shard_map/ppermute | solution.py:36
  105.2 4.6 %collective-permute-start.16 = (bf16[4,1792]{1,0:T(4,128)(2,1)S(1)}, bf16[4,1792]{1,0:T(4,128)(2,1)S(1)}, u32[]{:S(2)}, u32[]{:S(2)}) collective-permute-start(bf16[4,1792]{1,0:T(4,128)(2,1)S(1)} %get-tuple-element.57), channel_id=1, source_target_pairs={{0,1},{1,0},{2,3},{3,2},{4,5},{5,4},{6,7},{7,6},{8,9},{9,8},{10,11... | collective-permute-start | bytes 43016 | tf_op jit(solution)/shard_map/ppermute | solution.py:36

commit v3 on v2

--- a/solution.py
+++ b/solution.py
@@ -16,35 +16,17 @@
 VMEM = pl.BlockSpec(memory_space=pltpu.VMEM)
 SMEM = pl.BlockSpec(memory_space=pltpu.SMEM)
 ANY = pl.BlockSpec(memory_space=pl.ANY)
+HBM = pl.BlockSpec(memory_space=pltpu.HBM)
 MIB = 1024 * 1024
 
 
 def cost(flops, moved):
     return pl.CostEstimate(flops=flops, bytes_accessed=moved, transcendentals=0)
-
-
-def layer_norm(tokens, norm_gain, norm_shift):
-    values_f = tokens.astype(F32)
-    average = jnp.mean(values_f, axis=1, keepdims=True)
-    centered = values_f - average
-    variance = jnp.mean(centered * centered, axis=1, keepdims=True)
-    return (centered * lax.rsqrt(variance + EPSILON) * norm_gain + norm_shift).astype(BF16)
 
 
 def swap(value, axis, step):
     size = lax.axis_size(axis)
     return lax.ppermute(value, axis, [(i, i ^ step) for i in range(size)])
-
-
-def relative(blocks, index):
-    size = blocks.shape[0]
-    tail = blocks.shape[1:]
-    bits = size.bit_length() - 1
-    split = blocks.reshape((2,) * bits + tail)
-    for bit in range(bits):
-        axis = bits - 1 - bit
-        split = jnp.where((index >> bit) & 1 == 1, jnp.flip(split, axis), split)
-    return split.reshape((size,) + tail)
 
 
 def spread_pairs(keep, send):
@@ -55,21 +37,20 @@
     ]
 
 
-def copy_pools(key_pool, value_pool):
-    pages = key_pool.shape[0]
+def copy_pool(pool, after):
+    pages = pool.shape[0]
     parts = 5 if pages % 5 == 0 else 1
     step = pages // parts
 
-    def kernel(key_ref, value_ref, key_out, value_out, buffer, in_sems, out_sems):
-        steps = [(n, i, pl.ds(i * step, step)) for i in range(parts) for n in range(2)]
-        sources, targets = (key_ref, value_ref), (key_out, value_out)
+    def kernel(pool_ref, _, out_ref, buffer, in_sems, out_sems):
+        places = [pl.ds(i * step, step) for i in range(parts)]
         reads = [
-            pltpu.make_async_copy(sources[n].at[place], buffer.at[n, place], in_sems.at[n, i])
-            for n, i, place in steps
+            pltpu.make_async_copy(pool_ref.at[place], buffer.at[place], in_sems.at[i])
+            for i, place in enumerate(places)
         ]
         writes = [
-            pltpu.make_async_copy(buffer.at[n, place], targets[n].at[place], out_sems.at[n, i])
-            for n, i, place in steps
+            pltpu.make_async_copy(buffer.at[place], out_ref.at[place], out_sems.at[i])
+            for i, place in enumerate(places)
         ]
         for read in reads:
             read.start()
@@ -79,54 +60,116 @@
         for write in writes:
             write.wait()
 
-    shape = jax.ShapeDtypeStruct(key_pool.shape, key_pool.dtype)
     return pl.pallas_call(
         kernel,
-        out_shape=(shape, shape),
-        in_specs=[ANY, ANY],
-        out_specs=(ANY, ANY),
+        out_shape=jax.ShapeDtypeStruct(pool.shape, pool.dtype),
+        in_specs=[HBM, ANY],
+        out_specs=HBM,
         scratch_shapes=[
-            pltpu.VMEM((2,) + key_pool.shape, key_pool.dtype),
-            pltpu.SemaphoreType.DMA((2, parts)),
-            pltpu.SemaphoreType.DMA((2, parts)),
+            pltpu.VMEM(pool.shape, pool.dtype),
+            pltpu.SemaphoreType.DMA((parts,)),
+            pltpu.SemaphoreType.DMA((parts,)),
         ],
-        compiler_params=pltpu.CompilerParams(vmem_limit_bytes=11 * MIB),
-        cost_estimate=cost(0, 4 * key_pool.size * 2),
-        name="copy_pools",
-    )(key_pool, value_pool)
-
-
-def pick_page(key_pool, value_pool, page):
-    shape = (2,) + key_pool.shape[1:]
-
-    def kernel(page_ref, key_ref, value_ref, out_ref, sems):
+        compiler_params=pltpu.CompilerParams(vmem_limit_bytes=6 * MIB),
+        cost_estimate=cost(0, 2 * pool.size * 2),
+        name="copy_pool",
+    )(pool, after)
+
+
+def leaving_slot(new_slot_ref, slots, here):
+    leaving = jnp.int32(0)
+    for s in range(slots):
+        leaving = jnp.where(new_slot_ref[s] // slots != here, s, leaving)
+    return leaving
+
+
+def prepare(tokens, gain, shift, lengths, page_table, new_slot, new_page, key_pool, value_pool):
+    groups = lax.axis_size("req")
+    chips = groups // 2
+    slots, model = tokens.shape
+    depth = model // groups
+    page, width = key_pool.shape[1:]
+
+    def kernel(
+        token_ref, gain_ref, shift_ref, length_ref, table_ref, slot_ref, page_ref, key_ref, value_ref,
+        keep_ref, send_ref, out_ref, normed, sems,
+    ):
+        here = lax.axis_index("req")
+        leaving = leaving_slot(slot_ref, slots, here)
         copies = [
-            pltpu.make_async_copy(source.at[page_ref[0]], out_ref.at[n], sems.at[n])
+            pltpu.make_async_copy(source.at[table_ref[leaving, 0]], out_ref.at[n], sems.at[n])
             for n, source in enumerate((key_ref, value_ref))
         ]
         for copy in copies:
             copy.start()
+        values = token_ref[...].astype(F32)
+        average = jnp.mean(values, axis=1, keepdims=True)
+        centered = values - average
+        variance = jnp.mean(centered * centered, axis=1, keepdims=True)
+        rows = centered * lax.rsqrt(variance + EPSILON) * gain_ref[...] + shift_ref[...]
+        normed[...] = rows.astype(BF16).astype(F32)
+        row = lax.broadcasted_iota(jnp.int32, (slots, META), 0)
+        lane = lax.broadcasted_iota(jnp.int32, (slots, META), 1)
+        told = jnp.zeros((slots, META), F32)
+        for s in range(slots):
+            slot = slot_ref[s]
+            numbers = (slot // slots, slot % slots, page_ref[s], length_ref[s] % page)
+            for j, number in enumerate(numbers):
+                told = jnp.where((row == s) & (lane == j), number.astype(F32), told)
+        told = told.astype(BF16)
+        for k in range(groups):
+            first = (here ^ k) * depth
+            if depth % LANES == 0:
+                block = normed[:, pl.ds(pl.multiple_of(first, LANES), depth)]
+            else:
+                block = pltpu.roll(normed[...], lax.rem(model - first, model), 1)[:, :depth]
+            target = (keep_ref, send_ref)[k % 2]
+            target[k // 2, :, :META] = told
+            target[k // 2, :, META:] = block.astype(BF16)
         for copy in copies:
             copy.wait()
 
+    blocks = jax.ShapeDtypeStruct((chips, slots, META + depth), BF16)
     return pl.pallas_call(
         kernel,
-        out_shape=jax.ShapeDtypeStruct(shape, key_pool.dtype),
-        in_specs=[SMEM, ANY, ANY],
-        out_specs=VMEM,
-        scratch_shapes=[pltpu.SemaphoreType.DMA((2,))],
-        compiler_params=pltpu.CompilerParams(vmem_limit_bytes=2 * MIB),
-        cost_estimate=cost(0, 4 * key_pool.shape[1] * key_pool.shape[2] * 2),
-        name="pick_page",
-    )(page, key_pool, value_pool)
-
-
-def choose_page(which, candidates):
-    def kernel(which_ref, *refs):
-        out_ref, sem = refs[-2:]
-        for n, candidate in enumerate(refs[:-2]):
-
-            @pl.when(which_ref[0] == n)
+        out_shape=(blocks, blocks, jax.ShapeDtypeStruct((2, page, width), key_pool.dtype)),
+        in_specs=[VMEM] * 3 + [SMEM] * 4 + [HBM] * 2,
+        out_specs=(VMEM, VMEM, VMEM),
+        scratch_shapes=[pltpu.VMEM((slots, model), F32), pltpu.SemaphoreType.DMA((2,))],
+        compiler_params=pltpu.CompilerParams(vmem_limit_bytes=4 * MIB),
+        cost_estimate=cost(0, 8 * page * width),
+        name="prepare",
+    )(tokens, gain, shift, lengths, page_table, new_slot, new_page, key_pool, value_pool)
+
+
+def arrivals(block_refs, here, wanted):
+    slots = block_refs[0].shape[1]
+    lane = lax.broadcasted_iota(jnp.int32, (slots, META), 1)
+    found = jnp.zeros((slots, META), F32)
+    goal = (here ^ wanted).astype(F32)
+    for d, ref in enumerate(block_refs):
+        for e in range(2):
+            k = 2 * d + e
+            if k == wanted:
+                continue
+            told = ref[e, :, :META].astype(F32)
+            numbered = jnp.where(lane == 4, float(k), told)
+            found = jnp.where(told[:, :1] == goal, numbered, found)
+    pick = lambda j: jnp.sum(jnp.where(lane == j, found, 0.0)).astype(jnp.int32)
+    return pick(4), pick(2), pick(3)
+
+
+def choose_page(spread, candidates):
+    chips = len(spread)
+
+    def kernel(*refs):
+        block_refs, candidate_refs = refs[:chips], refs[chips : 2 * chips]
+        out_ref, sem = refs[2 * chips :]
+        source = arrivals(block_refs, lax.axis_index("req"), 1)[0]
+        which = jnp.where(source % 2 == 0, source // 2, 0)
+        for n, candidate in enumerate(candidate_refs):
+
+            @pl.when(which == n)
             def _():
                 copy = pltpu.make_async_copy(candidate, out_ref, sem)
                 copy.start()
@@ -136,13 +179,13 @@
     return pl.pallas_call(
         kernel,
         out_shape=jax.ShapeDtypeStruct(one.shape, one.dtype),
-        in_specs=[SMEM] + [ANY] * len(candidates),
+        in_specs=[VMEM] * chips + [ANY] * chips,
         out_specs=VMEM,
         scratch_shapes=[pltpu.SemaphoreType.DMA],
         compiler_params=pltpu.CompilerParams(vmem_limit_bytes=2 * MIB),
         cost_estimate=cost(0, 4 * one.size),
         name="choose_page",
-    )(which, *candidates)
+    )(*spread, *candidates)
 
 
 def project(blocks, weight):
@@ -161,7 +204,7 @@
             for d in range(chips):
                 for e in range(2):
                     row = (d * 2 + e) * slots
-                    left[row : row + slots, :] = block_refs[d][e][:, :depth].astype(F32)
+                    left[row : row + slots, :] = block_refs[d][e, :, META:].astype(F32)
 
         lhs = left[...].astype(BF16)
         for j in range(per):
@@ -187,7 +230,36 @@
     )(*blocks, weight)
 
 
-def attend(numbers, page_table, sums, bias, tokens, key_pool, value_pool, key_out, value_out):
+def combine(keep, got):
+    chips, slots, width = keep.shape
+    heads = width // (3 * LANES)
+
+    def kernel(keep_ref, got_ref, own_ref, *message_refs):
+        own_ref[...] = keep_ref[0] + got_ref[0]
+        for d in range(1, chips):
+            for h in range(heads):
+                total = keep_ref[d, :, 3 * h * LANES : 3 * (h + 1) * LANES] + got_ref[d, :, 3 * h * LANES : 3 * (h + 1) * LANES]
+                query = total[:, :LANES]
+                high = query.astype(BF16)
+                low = (query - high.astype(F32)).astype(BF16)
+                base = 4 * h * LANES
+                message_refs[d - 1][:, base : base + LANES] = high
+                message_refs[d - 1][:, base + LANES : base + 2 * LANES] = low
+                message_refs[d - 1][:, base + 2 * LANES : base + 4 * LANES] = total[:, LANES:].astype(BF16)
+
+    message = jax.ShapeDtypeStruct((slots, 4 * heads * LANES), BF16)
+    return pl.pallas_call(
+        kernel,
+        out_shape=(jax.ShapeDtypeStruct((slots, width), F32),) + (message,) * (chips - 1),
+        in_specs=[VMEM, VMEM],
+        out_specs=(VMEM,) * chips,
+        compiler_params=pltpu.CompilerParams(vmem_limit_bytes=8 * MIB),
+        cost_estimate=cost(0, 8 * keep.size),
+        name="combine",
+    )(keep, got)
+
+
+def attend(lengths, new_slot, page_table, sums, bias, tokens, key_pool, value_pool, key_out, value_out):
     parts = len(sums)
     slots = sums[0].shape[0]
     pages, page, width = key_pool.shape
@@ -207,16 +279,16 @@
     scale = head ** (-0.5)
 
     def kernel(*refs):
-        numbers_ref, table_ref = refs[:2]
-        sum_refs = refs[2 : 2 + parts]
+        length_ref, slot_ref, table_ref = refs[:3]
+        sum_refs = refs[3 : 3 + parts]
         (bias_ref, token_ref, key_ref, value_ref, _, _, pack_keep, pack_send, key_out_ref, value_out_ref) = refs[
-            2 + parts : 12 + parts
+            3 + parts : 13 + parts
         ]
-        key_buffer, value_buffer, score_buffer, mix_buffer, sems, out_sems = refs[12 + parts :]
-        leaving = numbers_ref[slots]
-        here = numbers_ref[slots + 1]
-        column_block = numbers_ref[slots + 2]
-        lengths = [numbers_ref[s] for s in range(slots)]
+        key_buffer, value_buffer, score_buffer, mix_buffer, sems, out_sems = refs[13 + parts :]
+        here = lax.axis_index("req")
+        column_block = lax.axis_index("head")
+        leaving = leaving_slot(slot_ref, slots, here)
+        lengths = [length_ref[s] for s in range(slots)]
         long_slot = jnp.int32(0)
         long_length = jnp.int32(-1)
         for s in range(slots):
@@ -257,15 +329,20 @@
                     for copy in long_copies(n, c):
                         copy.start()
 
-        total = sum_refs[0][...]
-        for ref in sum_refs[1:]:
-            total = total + ref[...].astype(F32)
-        total = total + bias_ref[...]
+        total = sum_refs[0][...] + bias_ref[...]
 
         def third(k):
-            return jnp.concatenate(
-                [total[:, (3 * h + k) * head : (3 * h + k + 1) * head] for h in range(heads)], axis=1
-            )
+            columns = []
+            for h in range(heads):
+                one = total[:, (3 * h + k) * head : (3 * h + k + 1) * head]
+                for ref in sum_refs[1:]:
+                    base = 4 * h * head
+                    if k == 0:
+                        one = one + ref[:, base : base + head].astype(F32) + ref[:, base + head : base + 2 * head].astype(F32)
+                    else:
+                        one = one + ref[:, base + (k + 1) * head : base + (k + 2) * head].astype(F32)
+                columns.append(one)
+            return jnp.concatenate(columns, axis=1)
 
         query = (third(0) * scale).astype(BF16).astype(F32)
         new_rows = (third(1).astype(BF16).astype(F32), third(2).astype(BF16).astype(F32))
@@ -409,7 +486,14 @@
             extra += [one[:, i * PACK : (i + 1) * PACK] for i in range(strips)]
         extra = jnp.concatenate(extra + [jnp.zeros((pack_rows(slots, strips) - high - 3 * strips, PACK), F32)], axis=0)
 
-        lane = lax.broadcasted_iota(jnp.int32, (high, LANES), 1) // share
+        row_at = lax.broadcasted_iota(jnp.int32, (high, LANES), 0)
+        lane_at = lax.broadcasted_iota(jnp.int32, (high, LANES), 1)
+        goal_device = jnp.full((high, LANES), -1.0, F32)
+        goal_slot = jnp.zeros((high, LANES), F32)
+        for s in range(slots):
+            goal_device = jnp.where(row_at == s, (slot_ref[s] // slots).astype(F32), goal_device)
+            goal_slot = jnp.where(row_at == s, (slot_ref[s] % slots).astype(F32), goal_slot)
+        lane = lane_at // share
         for k in range(groups):
             wanted = here ^ k
             tiles = [jnp.zeros((high, LANES), F32) for _ in range(PACK // LANES)]
@@ -418,6 +502,7 @@
                 shift = lax.rem((place - wanted) * share + 2 * LANES, LANES)
                 turned = pltpu.roll(attended[:, h * head : (h + 1) * head], shift, 1)
                 tiles[h // per] = jnp.where(lane == place, turned, tiles[h // per])
+            tiles[-1] = jnp.where(lane_at == LANES - 2, goal_device, jnp.where(lane_at == LANES - 1, goal_slot, tiles[-1]))
             block = jnp.concatenate([jnp.concatenate(tiles, axis=1), extra], axis=0).astype(BF16)
             (pack_keep, pack_send)[k % 2][k // 2] = block
 
@@ -433,8 +518,8 @@
     return pl.pallas_call(
         kernel,
         out_shape=(packed, packed, pool_shape, pool_shape),
-        in_specs=[SMEM, SMEM] + [VMEM] * (parts + 2) + [ANY] * 4,
-        out_specs=(VMEM, VMEM, ANY, ANY),
+        in_specs=[SMEM] * 3 + [VMEM] * (parts + 2) + [HBM] * 4,
+        out_specs=(VMEM, VMEM, HBM, HBM),
         scratch_shapes=[
             pltpu.VMEM((long_rows + short_rows, width), BF16),
             pltpu.VMEM((long_rows + short_rows, width), BF16),
@@ -443,11 +528,11 @@
             pltpu.SemaphoreType.DMA((2, chunks + 1)),
             pltpu.SemaphoreType.DMA((2, slots)),
         ],
-        input_output_aliases={6 + parts: 2, 7 + parts: 3},
+        input_output_aliases={7 + parts: 2, 8 + parts: 3},
         compiler_params=pltpu.CompilerParams(vmem_limit_bytes=18 * MIB),
         cost_estimate=cost(4 * tall * (long_rows + short_rows) * width, 4 * (long_rows + short_rows) * width),
         name="attend",
-    )(numbers, page_table, *sums, bias, tokens, key_pool, value_pool, key_out, value_out)
+    )(lengths, new_slot, page_table, *sums, bias, tokens, key_pool, value_pool, key_out, value_out)
 
 
 def pack_rows(slots, strips):
@@ -455,14 +540,14 @@
     return -(-need // 16) * 16
 
 
-def out_project(column_block, order, blocks, weight, pieces):
+def out_project(column_block, blocks, weight, pieces, slots):
     chips = len(blocks)
     depth, width = weight.shape
-    rows, high = order.shape[0], order.shape[1] // (2 * chips)
-    half = rows // 2
+    high = -(-slots // 8) * 8
+    rows = 2 * chips * slots
     piece = width // pieces
 
-    def kernel(column_ref, order_ref, *refs):
+    def kernel(column_ref, *refs):
         block_refs = refs[:chips]
         weight_ref, keep_ref, send_ref, left = refs[chips:]
 
@@ -470,24 +555,32 @@
         def _():
             gathered = jnp.concatenate(
                 [block_refs[d][e, :high, :].astype(F32) for d in range(chips) for e in range(2)], axis=0
-            ).astype(BF16)
-            left[...] = jnp.dot(order_ref[...], gathered, preferred_element_type=F32)
+            )
+            goal = gathered[:, PACK - 2 : PACK - 1].astype(jnp.int32)
+            place = goal ^ lax.axis_index("req")
+            row = (place % 2) * (chips * slots) + (place // 2) * slots + gathered[:, PACK - 1 :].astype(jnp.int32)
+            row = jnp.where(goal < 0, -1, row)
+            size = (gathered.shape[0], rows)
+            order = jnp.where(lax.broadcasted_iota(jnp.int32, size, 1) == row, 1.0, 0.0)
+            left[...] = lax.dot_general(
+                order.astype(BF16), gathered.astype(BF16), (((0,), (0,)), ((), ())), preferred_element_type=F32
+            )
 
         total = jnp.dot(left[:, :depth].astype(BF16), weight_ref[...], preferred_element_type=F32)
-        keep_ref[0] = total[:half]
-        send_ref[0] = total[half:]
-
-    shape = jax.ShapeDtypeStruct((pieces, half, piece), F32)
-    out_spec = pl.BlockSpec((1, half, piece), lambda j, c: (j, 0, 0))
+        for d in range(chips):
+            keep_ref[d, 0] = total[d * slots : (d + 1) * slots]
+            send_ref[d, 0] = total[(chips + d) * slots : (chips + d + 1) * slots].astype(BF16)
+
+    shape = (chips, pieces, slots, piece)
+    out_spec = pl.BlockSpec((chips, 1, slots, piece), lambda j, c: (0, j, 0, 0))
     whole = lambda shape: pl.BlockSpec(shape, lambda j, c: (0,) * len(shape))
     return pl.pallas_call(
         kernel,
-        out_shape=(shape, shape),
+        out_shape=(jax.ShapeDtypeStruct(shape, F32), jax.ShapeDtypeStruct(shape, BF16)),
         grid_spec=pltpu.PrefetchScalarGridSpec(
             num_scalar_prefetch=1,
             grid=(pieces,),
-            in_specs=[whole(order.shape)]
-            + [whole(block.shape) for block in blocks]
+            in_specs=[whole(block.shape) for block in blocks]
             + [pl.BlockSpec((depth, piece), lambda j, c: (0, j ^ c[0]))],
             out_specs=(out_spec, out_spec),
             scratch_shapes=[pltpu.VMEM((rows, PACK), F32)],
@@ -495,33 +588,60 @@
         compiler_params=pltpu.CompilerParams(vmem_limit_bytes=8 * MIB),
         cost_estimate=cost(2 * rows * weight.size, 2 * weight.size),
         name="out_project",
-    )(column_block, order, *blocks, weight)
-
-
-def place_page(numbers, new_rows, candidates, key_out, value_out):
+    )(column_block, *blocks, weight)
+
+
+def place_page(new_slot, spread, packs, tokens, out_bias, candidates, key_out, value_out):
+    chips = len(spread)
     count = len(candidates)
     page, width = key_out.shape[1:]
-
-    def kernel(numbers_ref, rows_ref, *refs):
-        candidate_refs = refs[:count]
-        _, _, key_ref, value_ref, buffer, sem, out_sems = refs[count:]
+    slots = tokens.shape[0]
+    high = -(-slots // 8) * 8
+    strips = width // PACK
+
+    def kernel(slot_ref, *refs):
+        block_refs, pack_refs = refs[:chips], refs[chips : 2 * chips]
+        token_ref, bias_ref = refs[2 * chips : 2 * chips + 2]
+        candidate_refs = refs[2 * chips + 2 : 2 * chips + 2 + count]
+        _, _, base_ref, key_ref, value_ref, buffer, arrived, sem, out_sems = refs[2 * chips + 2 + count :]
+        here = lax.axis_index("req")
+        column = pl.multiple_of(lax.axis_index("head") * width, LANES)
+        source, page_at, offset = arrivals(block_refs, here, 0)
+        which = jnp.where(source % 2 == 0, source // 2, chips)
         for n in range(count):
 
-            @pl.when(numbers_ref[0] == n)
+            @pl.when(which == n)
             def _():
                 copy = pltpu.make_async_copy(candidate_refs[n], buffer, sem)
                 copy.start()
-                copy.wait()
-
-        offset = numbers_ref[2]
+
+        for d in range(chips):
+            for e in range(2):
+
+                @pl.when(source == 2 * d + e)
+                def _():
+                    arrived[...] = pack_refs[d][e].astype(F32)
+
+        def fresh(n):
+            strip = high + n * strips
+            return jnp.concatenate([arrived[strip + i : strip + i + 1, :] for i in range(strips)], axis=1)
+
+        at = lax.broadcasted_iota(jnp.int32, (slots, width), 0)
+        token = jnp.where(
+            at == leaving_slot(slot_ref, slots, here),
+            jnp.broadcast_to(fresh(2), (slots, width)),
+            token_ref[:, pl.ds(column, width)].astype(F32),
+        )
+        base_ref[...] = token + bias_ref[:, pl.ds(column, width)]
+        pltpu.make_async_copy(candidate_refs[0], buffer, sem).wait()
         first = pl.multiple_of(offset // 16 * 16, 16)
         row = lax.broadcasted_iota(jnp.int32, (16, width), 0)
         for n in range(2):
             old = buffer[n, pl.ds(first, 16), :].astype(F32)
-            new = jnp.broadcast_to(rows_ref[n : n + 1, :].astype(F32), (16, width))
+            new = jnp.broadcast_to(fresh(n), (16, width))
             buffer[n, pl.ds(first, 16), :] = jnp.where(row == offset - first, new, old).astype(BF16)
         copies = [
-            pltpu.make_async_copy(buffer.at[n], target.at[numbers_ref[1]], out_sems.at[n])
+            pltpu.make_async_copy(buffer.at[n], target.at[page_at], out_sems.at[n])
             for n, target in enumerate((key_ref, value_ref))
         ]
         for copy in copies:
@@ -532,19 +652,20 @@
     shape = jax.ShapeDtypeStruct(key_out.shape, key_out.dtype)
     return pl.pallas_call(
         kernel,
-        out_shape=(shape, shape),
-        in_specs=[SMEM, VMEM] + [ANY] * (count + 2),
-        out_specs=(ANY, ANY),
+        out_shape=(jax.ShapeDtypeStruct((slots, width), F32), shape, shape),
+        in_specs=[SMEM] + [VMEM] * (2 * chips + 2) + [ANY] * count + [HBM] * 2,
+        out_specs=(VMEM, HBM, HBM),
         scratch_shapes=[
             pltpu.VMEM((2, page, width), BF16),
+            pltpu.VMEM(packs[0].shape[1:], F32),
             pltpu.SemaphoreType.DMA,
             pltpu.SemaphoreType.DMA((2,)),
         ],
-        input_output_aliases={2 + count: 0, 3 + count: 1},
-        compiler_params=pltpu.CompilerParams(vmem_limit_bytes=2 * MIB),
-        cost_estimate=cost(0, 8 * page * width * 2),
+        input_output_aliases={2 * chips + 3 + count: 1, 2 * chips + 4 + count: 2},
+        compiler_params=pltpu.CompilerParams(vmem_limit_bytes=4 * MIB),
+        cost_estimate=cost(0, 8 * page * width),
         name="place_page",
-    )(numbers, new_rows, *candidates, key_out, value_out)
+    )(new_slot, *spread, *packs, tokens, out_bias, *candidates, key_out, value_out)
 
 
 def body(
@@ -564,56 +685,29 @@
 ):
     groups = lax.axis_size("req")
     head_groups = lax.axis_size("head")
-    here = lax.axis_index("req")
     column_block = lax.axis_index("head")
     slots = tokens.shape[0]
     chips = groups // 2
-    page_size, width = key_pool.shape[1:]
-    depth = qkv_weight.shape[0]
-    local_heads = qkv_weight.shape[1]
-    slot_range = jnp.arange(slots, dtype=jnp.int32)
-    target_device = new_slot // slots
-    leaving = jnp.sum(jnp.where(target_device != here, slot_range, 0))
-
-    mine = pick_page(key_pool, value_pool, page_table[leaving, :1])
-
-    normed = layer_norm(tokens, norm_gain, norm_shift)
-    table = jnp.stack(
-        [target_device, new_slot % slots, new_page, lengths % page_size], axis=1
-    ).astype(BF16)
-    table = jnp.pad(table, ((0, 0), (0, META - table.shape[1])))
-    features = normed.reshape(slots, groups, depth).transpose(1, 0, 2)
-    blocks = jnp.concatenate(
-        [relative(features, here), jnp.broadcast_to(table[None], (groups, slots, META))], axis=2
-    ).reshape(chips, 2, slots, depth + META)
-    spread = spread_pairs(blocks[:, 0], blocks[:, 1])
+
+    keep, send, mine = prepare(
+        tokens, norm_gain[None], norm_shift[None], lengths, page_table, new_slot, new_page, key_pool, value_pool
+    )
+    got = swap(send, "req", 1)
+    spread = [jnp.stack([keep[0], got[0]])] + [
+        swap(jnp.stack([keep[d], got[d]]), "req", 2 * d) for d in range(1, chips)
+    ]
+    key_copy = copy_pool(key_pool, got)
     candidates = [mine] + [swap(mine, "req", 2 * d) for d in range(1, chips)]
 
-    told = jnp.stack(spread)[..., depth : depth + 4].astype(jnp.int32).reshape(groups, slots, 4)
-    places = jnp.arange(groups, dtype=jnp.int32)
-    goal = told[..., 0] ^ here
-    for_me = (goal == 0) & (places[:, None] != 0)
-    for_other = (goal == 1) & (places[:, None] != 1)
-    pick = lambda mask, values: jnp.sum(jnp.where(mask, values, 0))
-    source = pick(for_me, places[:, None])
-    source_other = pick(for_other, places[:, None])
-    arrived_page = pick(for_me, told[..., 2])
-    arrived_length = pick(for_me, told[..., 3])
-    high = -(-slots // 8) * 8
-    goal_row = (goal % 2) * (chips * slots) + (goal // 2) * slots + told[..., 1]
-    goal_row = jnp.pad(goal_row, ((0, 0), (0, high - slots)), constant_values=-1).reshape(-1)
-    order = (
-        jnp.arange(groups * slots, dtype=jnp.int32)[:, None] == goal_row[None, :]
-    ).astype(BF16)
-
     keep, send = project(spread, jnp.transpose(qkv_weight, (1, 0, 2)))
-    total = keep + swap(send, "req", 1)
-    sums = [total[0]] + [swap(total[d], "req", 2 * d) for d in range(1, chips)]
-
-    key_copy, value_copy = copy_pools(key_pool, value_pool)
-    numbers = jnp.concatenate([lengths, jnp.stack([leaving, here, column_block])])
+    got = swap(send, "req", 1)
+    own, *messages = combine(keep, got)
+    sums = [own] + [swap(messages[d - 1], "req", 2 * d) for d in range(1, chips)]
+    value_copy = copy_pool(value_pool, own)
+
     pack_keep, pack_send, key_out, value_out = attend(
-        numbers,
+        lengths,
+        new_slot,
         page_table,
         sums,
         qkv_bias.reshape(1, -1),
@@ -625,41 +719,22 @@
     )
     packs = spread_pairs(pack_keep, pack_send)
 
-    which = jnp.where(source_other % 2 == 0, source_other // 2, 0)
-    from_other = swap(choose_page(which[None], candidates), "req", 1)
-
-    strips = width // PACK
-    rows = lax.dynamic_index_in_dim(
-        jnp.stack(packs).reshape(groups, -1, PACK), source, 0, keepdims=False
+    from_other = swap(choose_page(spread, candidates), "req", 1)
+
+    keep, send = out_project(
+        column_block[None], packs, out_weight.reshape(-1, out_weight.shape[2]), head_groups, slots
     )
-    arrived_rows = rows[high : high + 3 * strips].reshape(3, width)
-    arrived = jnp.where(source % 2 == 0, source // 2, chips)
-    key_out, value_out = place_page(
-        jnp.stack([arrived, arrived_page, arrived_length]),
-        arrived_rows[:2],
-        candidates + [from_other],
-        key_out,
-        value_out,
+    base, key_out, value_out = place_page(
+        new_slot, spread, packs, tokens, out_bias[None], candidates + [from_other], key_out, value_out
     )
-
-    keep, send = out_project(
-        column_block[None],
-        order,
-        packs,
-        out_weight.reshape(-1, out_weight.shape[2]),
-        head_groups,
-    )
-    total = (keep + swap(send, "req", 1)).reshape(head_groups, chips, slots, width)
-    summed = total[:, 0]
+    total = keep + swap(send, "req", 1).astype(F32)
+    summed = total[0]
     for d in range(1, chips):
-        summed = summed + swap(total[:, d].astype(BF16), "req", 2 * d).astype(F32)
+        summed = summed + swap(total[d].astype(BF16), "req", 2 * d).astype(F32)
     hidden = summed[0]
     for j in range(1, head_groups):
         hidden = hidden + swap(summed[j].astype(BF16), "head", j).astype(F32)
-    token_part = lax.dynamic_slice_in_dim(tokens, column_block * width, width, 1)
-    residual = jnp.where((slot_range == leaving)[:, None], arrived_rows[2:3], token_part)
-    bias_part = lax.dynamic_slice_in_dim(out_bias, column_block * width, width, 0)
-    hidden_out = (hidden + bias_part + residual.astype(F32)).astype(BF16)
+    hidden_out = (hidden + base).astype(BF16)
     return (hidden_out, key_out, value_out)
 
 

time: 112 us -> 105 us (0.938); the launches traced: 111 us -> 105 us
  waiting for transfers between devices: 13.2 us -> 29.9 us
  other arithmetic: 9.44 us -> 0.94 us
  between operations: 9.1 us -> 1.01 us
  local copies, waits for them, and re-layouts: 21.9 us -> 15.8 us
    ppermute x23, waiting for transfers between devices: 13.2 us -> 29.9 us  [swap(): return lax.ppermute(value, axis, [(i, i ^ step) for i in range(size)])]
    reduce_sum x5 -> x0, other arithmetic: 3.13 us -> none  [the longest x2 1.39 us: body(): pick = lambda mask, values: jnp.sum(jnp.where(mask, values, 0))]
    unnamed x36 -> x43, local copies, waits for them, and re-layouts: 17.8 us -> 15.7 us
    add x2 -> x0, other arithmetic: 2.02 us -> none  [the longest x1 1.93 us: body(): keep + swap(send, 'req', 1)]
    dynamic_slice x2 -> x0, local copies, waits for them, and re-layouts: 1.99 us -> none  [the longest x1 1.2 us: body(): mine = pick_page(key_pool, value_pool, page_table[leaving, :1])]
    another operation x7 -> x6, other arithmetic: 1.48 us -> 0.29 us  [the longest x1 1.35 us: body(): jnp.stack([arrived, arrived_page, arrived_length])]
    reshape x2 -> x0, local copies, waits for them, and re-layouts: 1.16 us -> none  [the longest x1 1.15 us: body(): (keep + swap(send, 'req', 1)).reshape(head_groups, chips, slots, width)]
    pallas_call x4 -> x6, Pallas kernels: 11.3 us -> 12.2 us  [the longest x2 6.86 us: copy_pool(): pl.pallas_call(kernel, out_shape=jax.ShapeDtypeStruct(pool.shape, pool.dt...]
  transfers between devices with their start and end apart: 23 -> 23, of which waited for: 10 -> 11; matrix products, arithmetic and copies ran while one was open for 10% -> 0% of each run, Pallas kernels for 16% -> 9%
where the time goes in v3:
time: 105 us
  starting transfers between devices  36.8 us (35%)
  waiting for transfers between devices  29.9 us (28%)
  Pallas kernels  20.4 us (19%)
  local copies, waits for them, and re-layouts  15.8 us (15%)
    ppermute x23, starting transfers between devices, swap(): return lax.ppermute(value, axis, [(i, i ^ step) for i in range(size)])  36.8 us
    ppermute x23, waiting for transfers between devices, swap(): return lax.ppermute(value, axis, [(i, i ^ step) for i in range(size)])  29.9 us
    unnamed x43, local copies, waits for them, and re-layouts  15.7 us
    pallas_call x2, Pallas kernels, copy_pool(): pl.pallas_call(kernel, out_shape=jax.ShapeDtypeStruct(pool.shape, pool.dt...  6.86 us
    pallas_call x1, Pallas kernels, attend(): pl.pallas_call(kernel, out_shape=(packed, packed, pool_shape, pool_shape)...  5.29 us
    pallas_call x1, Pallas kernels, project(): pl.pallas_call(kernel, grid=(heads // per,), out_shape=(shape, shape), in...  2.38 us
  transfers between devices with their start and end apart: 23, of which 11 were waited for; matrix products, arithmetic and copies ran while one was open for 0% of the time, Pallas kernels for 9%

profile of v3, /device:TPU:0, one launch (start us, length us, event | category | flops | bytes accessed | tf_op | source)
XLA Modules:
  0.0 104.8 jit_solution(8045304168146512405)
XLA Ops:
  0.6 2.3 %copy-done = bf16[20,64,1792]{2,1,0:T(8,128)(2,1)S(1)} copy-done((bf16[20,64,1792]{2,1,0:T(8,128)(2,1)S(1)}, bf16[20,64,1792]{2,1,0:T(8,128)(2,1)}, u32[]{:S(2)}) %copy-start) | copy-done | bytes 4587544
  2.9 2.3 %copy-done.2 = bf16[20,64,1792]{2,1,0:T(8,128)(2,1)S(1)} copy-done((bf16[20,64,1792]{2,1,0:T(8,128)(2,1)S(1)}, bf16[20,64,1792]{2,1,0:T(8,128)(2,1)}, u32[]{:S(2)}) %copy-start.2) | copy-done | bytes 4587544
  5.2 0.8 copy-done.6
  6.1 0.7 copy-done.8
  6.8 0.7 copy-done.9
  7.6 0.7 copy-done.11
  8.2 0.7 copy-done.13
  8.9 0.7 copy-done.15
  9.5 0.7 copy-done.17
  10.2 1.6 %prepare.1 = (bf16[4,4,1024]{2,1,0:T(4,128)(2,1)S(1)}, bf16[4,4,1024]{2,1,0:T(4,128)(2,1)S(1)}, bf16[2,64,1792]{2,1,0:T(8,128)(2,1)S(1)}) custom-call(bf16[4,7168]{1,0:T(4,128)(2,1)S(1)} %copy-done.6, f32[1,7168]{1,0:T(1,128)S(1)} %bitcast.47, f32[1,7168]{1,0:T(1,128)S(1)} %bitcast.48, s32[4]{0:T(128)S(1)} %copy-done.15, s32[4,16]{1,0:T(4,128)S(1)} %copy-done.11, ...), custom_call_target="tpu_custom_call" | custom-call | bytes 917504 | tf_op jit(solution)/shard_map/prepare/pallas_call | solution.py:133
  11.8 0.5 collective-permute-start
  12.3 0.8 collective-permute-done._
  13.2 2.9 %collective-permute-start.1 = (bf16[2,4,1024]{2,1,0:T(4,128)(2,1)S(1)}, bf16[2,4,1024]{2,1,0:T(4,128)(2,1)S(1)}, u32[]{:S(2)}, u32[]{:S(2)}) collective-permute-start(bf16[2,4,1024]{2,1,0:T(4,128)(2,1)S(1)} %pad_maximum_fusion.5), channel_id=1, source_target_pairs={{0,8},{4,12},{8,0},{12,4},{16,24},{20,28},{24,16},{28,20},{1,9},{5... | collective-permute-start | bytes 49160 | tf_op jit(solution)/shard_map/ppermute | solution.py:29
  16.1 1.6 %collective-permute-start.2 = (bf16[2,4,1024]{2,1,0:T(4,128)(2,1)S(1)}, bf16[2,4,1024]{2,1,0:T(4,128)(2,1)S(1)}, u32[]{:S(2)}, u32[]{:S(2)}) collective-permute-start(bf16[2,4,1024]{2,1,0:T(4,128)(2,1)S(1)} %pad_maximum_fusion.6), channel_id=1, source_target_pairs={{0,16},{4,20},{8,24},{12,28},{16,0},{20,4},{24,8},{28,12},{1,17},{... | collective-permute-start | bytes 49160 | tf_op jit(solution)/shard_map/ppermute | solution.py:29
  17.8 2.1 %collective-permute-done.2.refs_2_ = bf16[2,4,1024]{2,1,0:T(4,128)(2,1)S(1)} collective-permute-done((bf16[2,4,1024]{2,1,0:T(4,128)(2,1)S(1)}, bf16[2,4,1024]{2,1,0:T(4,128)(2,1)S(1)}, u32[]{:S(2)}, u32[]{:S(2)}) %collective-permute-start.2) | collective-permute-done | bytes 16416 | tf_op jit(solution)/shard_map/ppermute | solution.py:29
  19.9 2.5 %collective-permute-done.3.refs_3_ = bf16[2,4,1024]{2,1,0:T(4,128)(2,1)S(1)} collective-permute-done((bf16[2,4,1024]{2,1,0:T(4,128)(2,1)S(1)}, bf16[2,4,1024]{2,1,0:T(4,128)(2,1)S(1)}, u32[]{:S(2)}, u32[]{:S(2)}) %collective-permute-start.3) | collective-permute-done | bytes 16416 | tf_op jit(solution)/shard_map/ppermute | solution.py:29
  22.4 3.7 %copy-done.4 = bf16[896,14,384]{2,0,1:T(8,128)(2,1)S(1)} copy-done((bf16[896,14,384]{2,0,1:T(8,128)(2,1)S(1)}, bf16[896,14,384]{2,0,1:T(8,128)(2,1)}, u32[]{:S(2)}) %copy-start.4) | copy-done | bytes 9633816
  26.2 2.4 %project.1 = (f32[4,4,5376]{2,1,0:T(4,128)S(1)}, f32[4,4,5376]{2,1,0:T(4,128)S(1)}) custom-call(bf16[2,4,1024]{2,1,0:T(4,128)(2,1)S(1)} %pad_maximum_fusion.4.refs_0_, bf16[2,4,1024]{2,1,0:T(4,128)(2,1)S(1)} %collective-permute-done.1.refs_1_, bf16[2,4,1024]{2,1,0:T(4,128)(2,1)S(1)} %collective-permute-done.2.refs_2_, ...), custom_call_target="tpu_custom_call" | custom-call | flops 308281344 | bytes 9633792 | tf_op jit(solution)/shard_map/project/pallas_call | solution.py:220
  28.6 1.6 %collective-permute-done.4.got_ref = f32[4,4,5376]{2,1,0:T(4,128)S(1)} collective-permute-done((f32[4,4,5376]{2,1,0:T(4,128)S(1)}, f32[4,4,5376]{2,1,0:T(4,128)S(1)}, u32[]{:S(2)}, u32[]{:S(2)}) %collective-permute-start.4) | collective-permute-done | bytes 344096 | tf_op jit(solution)/shard_map/ppermute | solution.py:29
  30.3 0.6 collective-permute-start.5
  31.0 2.9 %collective-permute-start.7 = (bf16[4,7168]{1,0:T(4,128)(2,1)S(1)}, bf16[4,7168]{1,0:T(4,128)(2,1)S(1)}, u32[]{:S(2)}, u32[]{:S(2)}) collective-permute-start(bf16[4,7168]{1,0:T(4,128)(2,1)S(1)} %get-tuple-element.28), channel_id=1, source_target_pairs={{0,24},{4,28},{8,16},{12,20},{16,8},{20,12},{24,0},{28,4},{1,25},{... | collective-permute-start | bytes 172040 | tf_op jit(solution)/shard_map/ppermute | solution.py:29
  33.9 2.3 %copy-done.1 = bf16[20,64,1792]{2,1,0:T(8,128)(2,1)S(1)} copy-done((bf16[20,64,1792]{2,1,0:T(8,128)(2,1)S(1)}, bf16[20,64,1792]{2,1,0:T(8,128)(2,1)}, u32[]{:S(2)}) %copy-start.1) | copy-done | bytes 4587544
  36.2 3.5 %copy_pool.2.refs_11_ = bf16[20,64,1792]{2,1,0:T(8,128)(2,1)} custom-call(bf16[20,64,1792]{2,1,0:T(8,128)(2,1)S(1)} %copy-done.1, bf16[4,4,1024]{2,1,0:T(4,128)(2,1)S(1)} %collective-permute-done._), custom_call_target="tpu_custom_call" | custom-call | bytes 9175040 | tf_op jit(solution)/shard_map/copy_pool/pallas_call | solution.py:63
  39.8 3.3 %copy_pool.3.refs_12_ = bf16[20,64,1792]{2,1,0:T(8,128)(2,1)} custom-call(bf16[20,64,1792]{2,1,0:T(8,128)(2,1)S(1)} %copy-done.3, f32[4,5376]{1,0:T(4,128)S(1)} %get-tuple-element.25._.refs_3_), custom_call_target="tpu_custom_call" | custom-call | bytes 9175040 | tf_op jit(solution)/shard_map/copy_pool/pallas_call | solution.py:63
  43.3 5.3 %attend.1 = (bf16[4,32,256]{2,1,0:T(8,128)(2,1)S(1)}, bf16[4,32,256]{2,1,0:T(8,128)(2,1)S(1)}, bf16[20,64,1792]{2,1,0:T(8,128)(2,1)}, bf16[20,64,1792]{2,1,0:T(8,128)(2,1)}) custom-call(s32[4]{0:T(128)S(1)} %copy-done.16, s32[4]{0:T(128)S(1)} %copy-done.14, s32[4,16]{1,0:T(4,128)S(1)} %copy-done.12, ...), custom_call_target="tpu_custom_call", output_to_operand_aliasing={{2}: (11, {}), {3}: (12, {})} | custom-call | flops 146800640 | bytes 9175040 | tf_op jit(solution)/shard_map/attend/pallas_call | solution.py:518
  48.6 11.0 %collective-permute-start.8 = (bf16[4,32,256]{2,1,0:T(8,128)(2,1)S(1)}, bf16[4,32,256]{2,1,0:T(8,128)(2,1)S(1)}, u32[]{:S(2)}, u32[]{:S(2)}) collective-permute-start(bf16[4,32,256]{2,1,0:T(8,128)(2,1)S(1)} %get-tuple-element.30), channel_id=1, source_target_pairs={{0,4},{4,0},{8,12},{12,8},{16,20},{20,16},{24,28},{28,24},{1,5},{5... | collective-permute-start | bytes 196616 | tf_op jit(solution)/shard_map/ppermute | solution.py:29
  59.6 0.9 collective-permute-done.8
  60.5 1.7 %collective-permute-start.9 = (bf16[2,32,256]{2,1,0:T(8,128)(2,1)S(1)}, bf16[2,32,256]{2,1,0:T(8,128)(2,1)S(1)}, u32[]{:S(2)}, u32[]{:S(2)}) collective-permute-start(bf16[2,32,256]{2,1,0:T(8,128)(2,1)S(1)} %pad_maximum_fusion.1), channel_id=1, source_target_pairs={{0,8},{4,12},{8,0},{12,4},{16,24},{20,28},{24,16},{28,20},{1,9},{5... | collective-permute-start | bytes 98312 | tf_op jit(solution)/shard_map/ppermute | solution.py:29
  62.3 1.8 %collective-permute-start.11 = (bf16[2,32,256]{2,1,0:T(8,128)(2,1)S(1)}, bf16[2,32,256]{2,1,0:T(8,128)(2,1)S(1)}, u32[]{:S(2)}, u32[]{:S(2)}) collective-permute-start(bf16[2,32,256]{2,1,0:T(8,128)(2,1)S(1)} %pad_maximum_fusion.3), channel_id=1, source_target_pairs={{0,24},{4,28},{8,16},{12,20},{16,8},{20,12},{24,0},{28,4},{1,25},{... | collective-permute-start | bytes 98312 | tf_op jit(solution)/shard_map/ppermute | solution.py:29
  64.1 0.4 collective-permute-done.9.refs_1_.refs_5_
  64.5 1.8 %collective-permute-done.10.refs_2_.refs_6_ = bf16[2,32,256]{2,1,0:T(8,128)(2,1)S(1)} collective-permute-done((bf16[2,32,256]{2,1,0:T(8,128)(2,1)S(1)}, bf16[2,32,256]{2,1,0:T(8,128)(2,1)S(1)}, u32[]{:S(2)}, u32[]{:S(2)}) %collective-permute-start.10) | collective-permute-done | bytes 32800 | tf_op jit(solution)/shard_map/ppermute | solution.py:29
  66.4 0.7 collective-permute-done.11.refs_3_.refs_7_
  67.1 1.8 %out_project.1 = (f32[4,4,4,1792]{3,2,1,0:T(4,128)S(1)}, bf16[4,4,4,1792]{3,2,1,0:T(4,128)(2,1)S(1)}) custom-call(s32[1]{0:T(128)} %bitcast.column_ref, bf16[2,32,256]{2,1,0:T(8,128)(2,1)S(1)} %pad_maximum_fusion.refs_0_.refs_4_, bf16[2,32,256]{2,1,0:T(8,128)(2,1)S(1)} %collective-permute-done.9.refs_1_.refs_5_, ...), custom_call_target="tpu_custom_call" | custom-call | flops 102760448 | bytes 3211264 | tf_op jit(solution)/shard_map/out_project/pallas_call | solution.py:577
  68.9 2.0 %collective-permute-start.19 = (bf16[2,64,1792]{2,1,0:T(8,128)(2,1)S(1)}, bf16[2,64,1792]{2,1,0:T(8,128)(2,1)S(1)}, u32[]{:S(2)}, u32[]{:S(2)}) collective-permute-start(bf16[2,64,1792]{2,1,0:T(8,128)(2,1)S(1)} %get-tuple-element.33.refs_4_.refs_10_), channel_id=1, source_target_pairs={{0,8},{4,12},{8,0},{12,4},{16,24},{20,28},{24,16},{28,20},{1,9},{5... | collective-permute-start | bytes 1376264 | tf_op jit(solution)/shard_map/ppermute | solution.py:29
  70.9 0.5 collective-permute-start.20
  71.4 1.1 %collective-permute-start.21 = (bf16[2,64,1792]{2,1,0:T(8,128)(2,1)S(1)}, bf16[2,64,1792]{2,1,0:T(8,128)(2,1)S(1)}, u32[]{:S(2)}, u32[]{:S(2)}) collective-permute-start(bf16[2,64,1792]{2,1,0:T(8,128)(2,1)S(1)} %get-tuple-element.33.refs_4_.refs_10_), channel_id=1, source_target_pairs={{0,24},{4,28},{8,16},{12,20},{16,8},{20,12},{24,0},{28,4},{1,25},{... | collective-permute-start | bytes 1376264 | tf_op jit(solution)/shard_map/ppermute | solution.py:29
  72.5 0.2 fusion.10
  72.7 1.9 %collective-permute-start.15 = (bf16[4,4,1792]{2,1,0:T(4,128)(2,1)S(1)}, bf16[4,4,1792]{2,1,0:T(4,128)(2,1)S(1)}, u32[]{:S(2)}, u32[]{:S(2)}) collective-permute-start(bf16[4,4,1792]{2,1,0:T(4,128)(2,1)S(1)} %get-tuple-element.44), channel_id=1, source_target_pairs={{0,24},{4,28},{8,16},{12,20},{16,8},{20,12},{24,0},{28,4},{1,25},{... | collective-permute-start | bytes 172040 | tf_op jit(solution)/shard_map/ppermute | solution.py:29
  74.6 1.6 %collective-permute-start.14 = (bf16[4,4,1792]{2,1,0:T(4,128)(2,1)S(1)}, bf16[4,4,1792]{2,1,0:T(4,128)(2,1)S(1)}, u32[]{:S(2)}, u32[]{:S(2)}) collective-permute-start(bf16[4,4,1792]{2,1,0:T(4,128)(2,1)S(1)} %get-tuple-element.45), channel_id=1, source_target_pairs={{0,16},{4,20},{8,24},{12,28},{16,0},{20,4},{24,8},{28,12},{1,17},{... | collective-permute-start | bytes 172040 | tf_op jit(solution)/shard_map/ppermute | solution.py:29
  76.2 6.1 %collective-permute-done.19.refs_5_.refs_11_ = bf16[2,64,1792]{2,1,0:T(8,128)(2,1)S(1)} collective-permute-done((bf16[2,64,1792]{2,1,0:T(8,128)(2,1)S(1)}, bf16[2,64,1792]{2,1,0:T(8,128)(2,1)S(1)}, u32[]{:S(2)}, u32[]{:S(2)}) %collective-permute-start.19) | collective-permute-done | bytes 458784 | tf_op jit(solution)/shard_map/ppermute | solution.py:29
  82.3 1.9 %collective-permute-start.13 = (bf16[4,4,1792]{2,1,0:T(4,128)(2,1)S(1)}, bf16[4,4,1792]{2,1,0:T(4,128)(2,1)S(1)}, u32[]{:S(2)}, u32[]{:S(2)}) collective-permute-start(bf16[4,4,1792]{2,1,0:T(4,128)(2,1)S(1)} %get-tuple-element.43), channel_id=1, source_target_pairs={{0,8},{4,12},{8,0},{12,4},{16,24},{20,28},{24,16},{28,20},{1,9},{5... | collective-permute-start | bytes 172040 | tf_op jit(solution)/shard_map/ppermute | solution.py:29
  84.3 10.9 %collective-permute-done.20.refs_6_.refs_12_ = bf16[2,64,1792]{2,1,0:T(8,128)(2,1)S(1)} collective-permute-done((bf16[2,64,1792]{2,1,0:T(8,128)(2,1)S(1)}, bf16[2,64,1792]{2,1,0:T(8,128)(2,1)S(1)}, u32[]{:S(2)}, u32[]{:S(2)}) %collective-permute-start.20) | collective-permute-done | bytes 458784 | tf_op jit(solution)/shard_map/ppermute | solution.py:29
  95.2 0.5 choose_page.1
  95.9 3.7 %collective-permute-start.18 = (bf16[4,1792]{1,0:T(4,128)(2,1)S(1)}, bf16[4,1792]{1,0:T(4,128)(2,1)S(1)}, u32[]{:S(2)}, u32[]{:S(2)}) collective-permute-start(bf16[4,1792]{1,0:T(4,128)(2,1)S(1)} %get-tuple-element.55), channel_id=1, source_target_pairs={{0,3},{1,2},{2,1},{3,0},{4,7},{5,6},{6,5},{7,4},{8,11},{9,10},{10,... | collective-permute-start | bytes 43016 | tf_op jit(solution)/shard_map/ppermute | solution.py:29
  99.6 0.8 collective-permute-start.16
  100.4 1.9 %place_page.1 = (f32[4,1792]{1,0:T(4,128)S(1)}, bf16[20,64,1792]{2,1,0:T(8,128)(2,1)}, bf16[20,64,1792]{2,1,0:T(8,128)(2,1)}) custom-call(s32[4]{0:T(128)S(1)} %copy-done.14, bf16[2,4,1024]{2,1,0:T(4,128)(2,1)S(1)} %pad_maximum_fusion.4.refs_0_, ...), custom_call_target="tpu_custom_call", output_to_operand_aliasing={{1}: (16, {}), {2}: (17, {})} | custom-call | bytes 917504 | tf_op jit(solution)/shard_map/place_page/pallas_call | solution.py:653
  102.3 1.9 %collective-permute-done.17 = bf16[4,1792]{1,0:T(4,128)(2,1)S(1)} collective-permute-done((bf16[4,1792]{1,0:T(4,128)(2,1)S(1)}, bf16[4,1792]{1,0:T(4,128)(2,1)S(1)}, u32[]{:S(2)}, u32[]{:S(2)}) %collective-permute-start.17) | collective-permute-done | bytes 14368 | tf_op jit(solution)/shard_map/ppermute | solution.py:29
  104.2 0.6 fusion.7
  (68 shorter events, 0.9 us)
Async XLA Ops:
  0.6 2.3 %copy-start = (bf16[20,64,1792]{2,1,0:T(8,128)(2,1)S(1)}, bf16[20,64,1792]{2,1,0:T(8,128)(2,1)}, u32[]{:S(2)}) copy-start(bf16[20,64,1792]{2,1,0:T(8,128)(2,1)} %refs_9_.1) | copy-start | bytes 13762564
  2.9 2.3 %copy-start.2 = (bf16[20,64,1792]{2,1,0:T(8,128)(2,1)S(1)}, bf16[20,64,1792]{2,1,0:T(8,128)(2,1)}, u32[]{:S(2)}) copy-start(bf16[20,64,1792]{2,1,0:T(8,128)(2,1)} %refs_10_.1) | copy-start | bytes 13762564
  5.2 0.8 copy-start.6
  6.1 0.7 copy-start.8
  6.8 0.7 copy-start.9
  7.5 0.7 copy-start.11
  8.2 0.7 copy-start.13
  8.9 0.7 copy-start.15
  9.5 0.7 copy-start.17
  11.8 1.4 %collective-permute-start = (bf16[4,4,1024]{2,1,0:T(4,128)(2,1)S(1)}, bf16[4,4,1024]{2,1,0:T(4,128)(2,1)S(1)}, u32[]{:S(2)}, u32[]{:S(2)}) collective-permute-start(bf16[4,4,1024]{2,1,0:T(4,128)(2,1)S(1)} %get-tuple-element.22), channel_id=1, source_target_pairs={{0,4},{4,0},{8,12},{12,8},{16,20},{20,16},{24,28},{28,24},{1,5},{5... | collective-permute-start | bytes 98312 | tf_op jit(solution)/shard_map/ppermute | solution.py:29
  13.2 4.6 %collective-permute-start.1 = (bf16[2,4,1024]{2,1,0:T(4,128)(2,1)S(1)}, bf16[2,4,1024]{2,1,0:T(4,128)(2,1)S(1)}, u32[]{:S(2)}, u32[]{:S(2)}) collective-permute-start(bf16[2,4,1024]{2,1,0:T(4,128)(2,1)S(1)} %pad_maximum_fusion.5), channel_id=1, source_target_pairs={{0,8},{4,12},{8,0},{12,4},{16,24},{20,28},{24,16},{28,20},{1,9},{5... | collective-permute-start | bytes 49160 | tf_op jit(solution)/shard_map/ppermute | solution.py:29
  16.1 3.8 %collective-permute-start.2 = (bf16[2,4,1024]{2,1,0:T(4,128)(2,1)S(1)}, bf16[2,4,1024]{2,1,0:T(4,128)(2,1)S(1)}, u32[]{:S(2)}, u32[]{:S(2)}) collective-permute-start(bf16[2,4,1024]{2,1,0:T(4,128)(2,1)S(1)} %pad_maximum_fusion.6), channel_id=1, source_target_pairs={{0,16},{4,20},{8,24},{12,28},{16,0},{20,4},{24,8},{28,12},{1,17},{... | collective-permute-start | bytes 49160 | tf_op jit(solution)/shard_map/ppermute | solution.py:29
  17.7 4.7 %collective-permute-start.3 = (bf16[2,4,1024]{2,1,0:T(4,128)(2,1)S(1)}, bf16[2,4,1024]{2,1,0:T(4,128)(2,1)S(1)}, u32[]{:S(2)}, u32[]{:S(2)}) collective-permute-start(bf16[2,4,1024]{2,1,0:T(4,128)(2,1)S(1)} %pad_maximum_fusion.7), channel_id=1, source_target_pairs={{0,24},{4,28},{8,16},{12,20},{16,8},{20,12},{24,0},{28,4},{1,25},{... | collective-permute-start | bytes 49160 | tf_op jit(solution)/shard_map/ppermute | solution.py:29
  22.4 3.7 %copy-start.4 = (bf16[896,14,384]{2,0,1:T(8,128)(2,1)S(1)}, bf16[896,14,384]{2,0,1:T(8,128)(2,1)}, u32[]{:S(2)}) copy-start(bf16[896,14,384]{2,0,1:T(8,128)(2,1)} %param.16) | copy-start | bytes 28901380
  26.2 7.7 %copy-start.18 = (f32[14,384]{1,0:T(8,128)S(1)}, f32[14,384]{1,0:T(8,128)}, u32[]{:S(2)}) copy-start(f32[14,384]{1,0:T(8,128)} %param.17) | copy-start | bytes 64516
  28.6 1.7 %collective-permute-start.4 = (f32[4,4,5376]{2,1,0:T(4,128)S(1)}, f32[4,4,5376]{2,1,0:T(4,128)S(1)}, u32[]{:S(2)}, u32[]{:S(2)}) collective-permute-start(f32[4,4,5376]{2,1,0:T(4,128)S(1)} %get-tuple-element.24), channel_id=1, source_target_pairs={{0,4},{4,0},{8,12},{12,8},{16,20},{20,16},{24,28},{28,24},{1,5},{5... | collective-permute-start | bytes 1032200 | tf_op jit(solution)/shard_map/ppermute | solution.py:29
  30.3 12.8 %collective-permute-start.5 = (bf16[4,7168]{1,0:T(4,128)(2,1)S(1)}, bf16[4,7168]{1,0:T(4,128)(2,1)S(1)}, u32[]{:S(2)}, u32[]{:S(2)}) collective-permute-start(bf16[4,7168]{1,0:T(4,128)(2,1)S(1)} %get-tuple-element.26), channel_id=1, source_target_pairs={{0,8},{4,12},{8,0},{12,4},{16,24},{20,28},{24,16},{28,20},{1,9},{5... | collective-permute-start | bytes 172040 | tf_op jit(solution)/shard_map/ppermute | solution.py:29
  30.9 12.3 %collective-permute-start.6 = (bf16[4,7168]{1,0:T(4,128)(2,1)S(1)}, bf16[4,7168]{1,0:T(4,128)(2,1)S(1)}, u32[]{:S(2)}, u32[]{:S(2)}) collective-permute-start(bf16[4,7168]{1,0:T(4,128)(2,1)S(1)} %get-tuple-element.27), channel_id=1, source_target_pairs={{0,16},{4,20},{8,24},{12,28},{16,0},{20,4},{24,8},{28,12},{1,17},{... | collective-permute-start | bytes 172040 | tf_op jit(solution)/shard_map/ppermute | solution.py:29
  31.0 12.2 %collective-permute-start.7 = (bf16[4,7168]{1,0:T(4,128)(2,1)S(1)}, bf16[4,7168]{1,0:T(4,128)(2,1)S(1)}, u32[]{:S(2)}, u32[]{:S(2)}) collective-permute-start(bf16[4,7168]{1,0:T(4,128)(2,1)S(1)} %get-tuple-element.28), channel_id=1, source_target_pairs={{0,24},{4,28},{8,16},{12,20},{16,8},{20,12},{24,0},{28,4},{1,25},{... | collective-permute-start | bytes 172040 | tf_op jit(solution)/shard_map/ppermute | solution.py:29
  33.9 2.3 %copy-start.1 = (bf16[20,64,1792]{2,1,0:T(8,128)(2,1)S(1)}, bf16[20,64,1792]{2,1,0:T(8,128)(2,1)}, u32[]{:S(2)}) copy-start(bf16[20,64,1792]{2,1,0:T(8,128)(2,1)} %refs_9_.1) | copy-start | bytes 13762564
  36.2 3.5 %copy-start.3 = (bf16[20,64,1792]{2,1,0:T(8,128)(2,1)S(1)}, bf16[20,64,1792]{2,1,0:T(8,128)(2,1)}, u32[]{:S(2)}) copy-start(bf16[20,64,1792]{2,1,0:T(8,128)(2,1)} %refs_10_.1) | copy-start | bytes 13762564
  36.2 7.0 %slice-start = ((s8[4587520]{0:T(1024)(128)(4,1)}), s8[4194304]{0:T(1024)(128)(4,1)S(1)}, s32[]{:S(2)}) async-start(s8[4587520]{0:T(1024)(128)(4,1)} %bitcast.42), calls=%async_computation | async-start | bytes 8388608
  39.8 3.4 %slice-start.1 = ((s8[4587520]{0:T(1024)(128)(4,1)}), s8[393216]{0:T(1024)(128)(4,1)S(1)}, s32[]{:S(2)}) async-start(s8[4587520]{0:T(1024)(128)(4,1)} %bitcast.42), calls=%async_computation.1 | async-start | bytes 786432
  39.8 3.4 %copy-start.7 = (bf16[4,7168]{1,0:T(4,128)(2,1)S(1)}, bf16[4,7168]{1,0:T(4,128)(2,1)}, u32[]{:S(2)}) copy-start(bf16[4,7168]{1,0:T(4,128)(2,1)} %refs_8_.3) | copy-start | bytes 172036
  39.8 3.4 %copy-start.12 = (s32[4,16]{1,0:T(4,128)S(1)}, s32[4,16]{1,0:T(4,128)}, u32[]{:S(2)}) copy-start(s32[4,16]{1,0:T(4,128)} %refs_2_.1) | copy-start | bytes 772
  39.8 3.4 %copy-start.14 = (s32[4]{0:T(128)S(1)}, s32[4]{0:T(128)}, u32[]{:S(2)}) copy-start(s32[4]{0:T(128)} %slot_ref.3) | copy-start | bytes 52
  39.8 3.4 %copy-start.16 = (s32[4]{0:T(128)S(1)}, s32[4]{0:T(128)}, u32[]{:S(2)}) copy-start(s32[4]{0:T(128)} %refs_0_.1) | copy-start | bytes 52
  43.3 23.8 %copy-start.5 = (bf16[14,16,7168]{2,1,0:T(8,128)(2,1)S(1)}, bf16[14,16,7168]{2,1,0:T(8,128)(2,1)}, u32[]{:S(2)}) copy-start(bf16[14,16,7168]{2,1,0:T(8,128)(2,1)} %param.18) | copy-start | bytes 9633796
  48.6 51.8 %copy-start.10 = (f32[7168]{0:T(1024)S(1)}, f32[7168]{0:T(1024)}, u32[]{:S(2)}) copy-start(f32[7168]{0:T(1024)} %param.19) | copy-start | bytes 86020
  48.6 11.9 %collective-permute-start.8 = (bf16[4,32,256]{2,1,0:T(8,128)(2,1)S(1)}, bf16[4,32,256]{2,1,0:T(8,128)(2,1)S(1)}, u32[]{:S(2)}, u32[]{:S(2)}) collective-permute-start(bf16[4,32,256]{2,1,0:T(8,128)(2,1)S(1)} %get-tuple-element.30), channel_id=1, source_target_pairs={{0,4},{4,0},{8,12},{12,8},{16,20},{20,16},{24,28},{28,24},{1,5},{5... | collective-permute-start | bytes 196616 | tf_op jit(solution)/shard_map/ppermute | solution.py:29
  60.5 4.0 %collective-permute-start.9 = (bf16[2,32,256]{2,1,0:T(8,128)(2,1)S(1)}, bf16[2,32,256]{2,1,0:T(8,128)(2,1)S(1)}, u32[]{:S(2)}, u32[]{:S(2)}) collective-permute-start(bf16[2,32,256]{2,1,0:T(8,128)(2,1)S(1)} %pad_maximum_fusion.1), channel_id=1, source_target_pairs={{0,8},{4,12},{8,0},{12,4},{16,24},{20,28},{24,16},{28,20},{1,9},{5... | collective-permute-start | bytes 98312 | tf_op jit(solution)/shard_map/ppermute | solution.py:29
  62.2 4.2 %collective-permute-start.10 = (bf16[2,32,256]{2,1,0:T(8,128)(2,1)S(1)}, bf16[2,32,256]{2,1,0:T(8,128)(2,1)S(1)}, u32[]{:S(2)}, u32[]{:S(2)}) collective-permute-start(bf16[2,32,256]{2,1,0:T(8,128)(2,1)S(1)} %pad_maximum_fusion.2), channel_id=1, source_target_pairs={{0,16},{4,20},{8,24},{12,28},{16,0},{20,4},{24,8},{28,12},{1,17},{... | collective-permute-start | bytes 98312 | tf_op jit(solution)/shard_map/ppermute | solution.py:29
  62.3 4.8 %collective-permute-start.11 = (bf16[2,32,256]{2,1,0:T(8,128)(2,1)S(1)}, bf16[2,32,256]{2,1,0:T(8,128)(2,1)S(1)}, u32[]{:S(2)}, u32[]{:S(2)}) collective-permute-start(bf16[2,32,256]{2,1,0:T(8,128)(2,1)S(1)} %pad_maximum_fusion.3), channel_id=1, source_target_pairs={{0,24},{4,28},{8,16},{12,20},{16,8},{20,12},{24,0},{28,4},{1,25},{... | collective-permute-start | bytes 98312 | tf_op jit(solution)/shard_map/ppermute | solution.py:29
  68.9 3.6 %collective-permute-start.12 = (bf16[4,4,4,1792]{3,2,1,0:T(4,128)(2,1)S(1)}, bf16[4,4,4,1792]{3,2,1,0:T(4,128)(2,1)S(1)}, u32[]{:S(2)}, u32[]{:S(2)}) collective-permute-start(bf16[4,4,4,1792]{3,2,1,0:T(4,128)(2,1)S(1)} %get-tuple-element.32), channel_id=1, source_target_pairs={{0,4},{4,0},{8,12},{12,8},{16,20},{20,16},{24,28},{28,24},{1,5},{5... | collective-permute-start | bytes 688136 | tf_op jit(solution)/shard_map/ppermute | solution.py:29
  68.9 13.4 %collective-permute-start.19 = (bf16[2,64,1792]{2,1,0:T(8,128)(2,1)S(1)}, bf16[2,64,1792]{2,1,0:T(8,128)(2,1)S(1)}, u32[]{:S(2)}, u32[]{:S(2)}) collective-permute-start(bf16[2,64,1792]{2,1,0:T(8,128)(2,1)S(1)} %get-tuple-element.33.refs_4_.refs_10_), channel_id=1, source_target_pairs={{0,8},{4,12},{8,0},{12,4},{16,24},{20,28},{24,16},{28,20},{1,9},{5... | collective-permute-start | bytes 1376264 | tf_op jit(solution)/shard_map/ppermute | solution.py:29
  70.9 24.3 %collective-permute-start.20 = (bf16[2,64,1792]{2,1,0:T(8,128)(2,1)S(1)}, bf16[2,64,1792]{2,1,0:T(8,128)(2,1)S(1)}, u32[]{:S(2)}, u32[]{:S(2)}) collective-permute-start(bf16[2,64,1792]{2,1,0:T(8,128)(2,1)S(1)} %get-tuple-element.33.refs_4_.refs_10_), channel_id=1, source_target_pairs={{0,16},{4,20},{8,24},{12,28},{16,0},{20,4},{24,8},{28,12},{1,17},{... | collective-permute-start | bytes 1376264 | tf_op jit(solution)/shard_map/ppermute | solution.py:29
  71.4 23.8 %collective-permute-start.21 = (bf16[2,64,1792]{2,1,0:T(8,128)(2,1)S(1)}, bf16[2,64,1792]{2,1,0:T(8,128)(2,1)S(1)}, u32[]{:S(2)}, u32[]{:S(2)}) collective-permute-start(bf16[2,64,1792]{2,1,0:T(8,128)(2,1)S(1)} %get-tuple-element.33.refs_4_.refs_10_), channel_id=1, source_target_pairs={{0,24},{4,28},{8,16},{12,20},{16,8},{20,12},{24,0},{28,4},{1,25},{... | collective-permute-start | bytes 1376264 | tf_op jit(solution)/shard_map/ppermute | solution.py:29
  72.7 23.1 %collective-permute-start.15 = (bf16[4,4,1792]{2,1,0:T(4,128)(2,1)S(1)}, bf16[4,4,1792]{2,1,0:T(4,128)(2,1)S(1)}, u32[]{:S(2)}, u32[]{:S(2)}) collective-permute-start(bf16[4,4,1792]{2,1,0:T(4,128)(2,1)S(1)} %get-tuple-element.44), channel_id=1, source_target_pairs={{0,24},{4,28},{8,16},{12,20},{16,8},{20,12},{24,0},{28,4},{1,25},{... | collective-permute-start | bytes 172040 | tf_op jit(solution)/shard_map/ppermute | solution.py:29
  74.6 21.2 %collective-permute-start.14 = (bf16[4,4,1792]{2,1,0:T(4,128)(2,1)S(1)}, bf16[4,4,1792]{2,1,0:T(4,128)(2,1)S(1)}, u32[]{:S(2)}, u32[]{:S(2)}) collective-permute-start(bf16[4,4,1792]{2,1,0:T(4,128)(2,1)S(1)} %get-tuple-element.45), channel_id=1, source_target_pairs={{0,16},{4,20},{8,24},{12,28},{16,0},{20,4},{24,8},{28,12},{1,17},{... | collective-permute-start | bytes 172040 | tf_op jit(solution)/shard_map/ppermute | solution.py:29
  82.3 13.5 %collective-permute-start.13 = (bf16[4,4,1792]{2,1,0:T(4,128)(2,1)S(1)}, bf16[4,4,1792]{2,1,0:T(4,128)(2,1)S(1)}, u32[]{:S(2)}, u32[]{:S(2)}) collective-permute-start(bf16[4,4,1792]{2,1,0:T(4,128)(2,1)S(1)} %get-tuple-element.43), channel_id=1, source_target_pairs={{0,8},{4,12},{8,0},{12,4},{16,24},{20,28},{24,16},{28,20},{1,9},{5... | collective-permute-start | bytes 172040 | tf_op jit(solution)/shard_map/ppermute | solution.py:29
  95.7 4.7 %collective-permute-start.22 = (bf16[2,64,1792]{2,1,0:T(8,128)(2,1)S(1)}, bf16[2,64,1792]{2,1,0:T(8,128)(2,1)S(1)}, u32[]{:S(2)}, u32[]{:S(2)}) collective-permute-start(bf16[2,64,1792]{2,1,0:T(8,128)(2,1)S(1)} %choose_page.1), channel_id=1, source_target_pairs={{0,4},{4,0},{8,12},{12,8},{16,20},{20,16},{24,28},{28,24},{1,5},{5... | collective-permute-start | bytes 1376264 | tf_op jit(solution)/shard_map/ppermute | solution.py:29
  95.9 6.4 %collective-permute-start.18 = (bf16[4,1792]{1,0:T(4,128)(2,1)S(1)}, bf16[4,1792]{1,0:T(4,128)(2,1)S(1)}, u32[]{:S(2)}, u32[]{:S(2)}) collective-permute-start(bf16[4,1792]{1,0:T(4,128)(2,1)S(1)} %get-tuple-element.55), channel_id=1, source_target_pairs={{0,3},{1,2},{2,1},{3,0},{4,7},{5,6},{6,5},{7,4},{8,11},{9,10},{10,... | collective-permute-start | bytes 43016 | tf_op jit(solution)/shard_map/ppermute | solution.py:29
  99.6 4.6 %collective-permute-start.17 = (bf16[4,1792]{1,0:T(4,128)(2,1)S(1)}, bf16[4,1792]{1,0:T(4,128)(2,1)S(1)}, u32[]{:S(2)}, u32[]{:S(2)}) collective-permute-start(bf16[4,1792]{1,0:T(4,128)(2,1)S(1)} %get-tuple-element.56), channel_id=1, source_target_pairs={{0,2},{1,3},{2,0},{3,1},{4,6},{5,7},{6,4},{7,5},{8,10},{9,11},{10,... | collective-permute-start | bytes 43016 | tf_op jit(solution)/shard_map/ppermute | solution.py:29
  99.6 4.6 %collective-permute-start.16 = (bf16[4,1792]{1,0:T(4,128)(2,1)S(1)}, bf16[4,1792]{1,0:T(4,128)(2,1)S(1)}, u32[]{:S(2)}, u32[]{:S(2)}) collective-permute-start(bf16[4,1792]{1,0:T(4,128)(2,1)S(1)} %get-tuple-element.54), channel_id=1, source_target_pairs={{0,1},{1,0},{2,3},{3,2},{4,5},{5,4},{6,7},{7,6},{8,9},{9,8},{10,11... | collective-permute-start | bytes 43016 | tf_op jit(solution)/shard_map/ppermute | solution.py:29

commit v4 on v3

--- a/solution.py
+++ b/solution.py
@@ -37,43 +37,86 @@
     ]
 
 
-def copy_pool(pool, after):
-    pages = pool.shape[0]
-    parts = 5 if pages % 5 == 0 else 1
+def in_hbm(*arrays):
+    return [pltpu.with_memory_space_constraint(array, pltpu.HBM) for array in arrays]
+
+
+def stage(arrays, after, name):
+    count = len(arrays)
+    parts = 4
+
+    def kernel(*refs):
+        sources, targets, sems = refs[:count], refs[count + 1 : 2 * count + 1], refs[-1]
+        copies = []
+        for n in range(count):
+            step = -(-arrays[n].shape[0] // parts)
+            for i, first in enumerate(range(0, arrays[n].shape[0], step)):
+                place = pl.ds(first, min(step, arrays[n].shape[0] - first))
+                copies.append(pltpu.make_async_copy(sources[n].at[place], targets[n].at[place], sems.at[n, i]))
+        for copy in copies:
+            copy.start()
+        for copy in copies:
+            copy.wait()
+
+    size = sum(array.size * 2 for array in arrays)
+    return pl.pallas_call(
+        kernel,
+        out_shape=tuple(jax.ShapeDtypeStruct(array.shape, array.dtype) for array in arrays),
+        in_specs=[HBM] * count + [ANY],
+        out_specs=(VMEM,) * count,
+        scratch_shapes=[pltpu.SemaphoreType.DMA((count, parts))],
+        compiler_params=pltpu.CompilerParams(vmem_limit_bytes=size + 2 * MIB),
+        cost_estimate=cost(0, size),
+        name=name,
+    )(*in_hbm(*arrays), after)
+
+
+def write_pools(lengths, new_slot, page_table, patches, key_pool, value_pool, after):
+    pages, page, width = key_pool.shape
+    slots, tall = patches.shape[1:3]
+    parts = 4
     step = pages // parts
 
-    def kernel(pool_ref, _, out_ref, buffer, in_sems, out_sems):
-        places = [pl.ds(i * step, step) for i in range(parts)]
-        reads = [
-            pltpu.make_async_copy(pool_ref.at[place], buffer.at[place], in_sems.at[i])
-            for i, place in enumerate(places)
+    def kernel(length_ref, slot_ref, table_ref, patch_ref, key_ref, value_ref, _, key_out, value_out, sems, patch_sems):
+        leaving = leaving_slot(slot_ref, slots, lax.axis_index("req"))
+        pairs = ((key_ref, key_out), (value_ref, value_out))
+        copies = [
+            pltpu.make_async_copy(source.at[pl.ds(i * step, step)], target.at[pl.ds(i * step, step)], sems.at[n, i])
+            for n, (source, target) in enumerate(pairs)
+            for i in range(parts)
         ]
-        writes = [
-            pltpu.make_async_copy(buffer.at[place], out_ref.at[place], out_sems.at[i])
-            for i, place in enumerate(places)
-        ]
-        for read in reads:
-            read.start()
-        for read, write in zip(reads, writes):
-            read.wait()
-            write.start()
-        for write in writes:
-            write.wait()
-
-    return pl.pallas_call(
-        kernel,
-        out_shape=jax.ShapeDtypeStruct(pool.shape, pool.dtype),
-        in_specs=[HBM, ANY],
-        out_specs=HBM,
-        scratch_shapes=[
-            pltpu.VMEM(pool.shape, pool.dtype),
-            pltpu.SemaphoreType.DMA((parts,)),
-            pltpu.SemaphoreType.DMA((parts,)),
-        ],
-        compiler_params=pltpu.CompilerParams(vmem_limit_bytes=6 * MIB),
-        cost_estimate=cost(0, 2 * pool.size * 2),
-        name="copy_pool",
-    )(pool, after)
+        for copy in copies:
+            copy.start()
+        for copy in copies:
+            copy.wait()
+
+        def patch(n, s):
+            length = length_ref[s]
+            first = pl.multiple_of(length % page // tall * tall, tall)
+            return pltpu.make_async_copy(
+                patch_ref.at[n, s], pairs[n][1].at[table_ref[s, length // page], pl.ds(first, tall)], patch_sems.at[n, s]
+            )
+
+        for act in ("start", "wait"):
+            for n in range(2):
+                for s in range(slots):
+
+                    @pl.when(leaving != s)
+                    def _():
+                        copy = patch(n, s)
+                        copy.start() if act == "start" else copy.wait()
+
+    shape = jax.ShapeDtypeStruct(key_pool.shape, key_pool.dtype)
+    return pl.pallas_call(
+        kernel,
+        out_shape=(shape, shape),
+        in_specs=[SMEM] * 3 + [VMEM] * 3 + [ANY],
+        out_specs=(HBM, HBM),
+        scratch_shapes=[pltpu.SemaphoreType.DMA((2, parts)), pltpu.SemaphoreType.DMA((2, slots))],
+        compiler_params=pltpu.CompilerParams(vmem_limit_bytes=14 * MIB),
+        cost_estimate=cost(0, 4 * key_pool.size),
+        name="write_pools",
+    )(lengths, new_slot, page_table, patches, key_pool, value_pool, after)
 
 
 def leaving_slot(new_slot_ref, slots, here):
@@ -139,7 +182,7 @@
         compiler_params=pltpu.CompilerParams(vmem_limit_bytes=4 * MIB),
         cost_estimate=cost(0, 8 * page * width),
         name="prepare",
-    )(tokens, gain, shift, lengths, page_table, new_slot, new_page, key_pool, value_pool)
+    )(*in_hbm(tokens, gain, shift, lengths, page_table, new_slot, new_page, key_pool, value_pool))
 
 
 def arrivals(block_refs, here, wanted):
@@ -198,33 +241,30 @@
     def kernel(*refs):
         block_refs = refs[:chips]
         weight_ref, keep_ref, send_ref, left = refs[chips:]
-
-        @pl.when(pl.program_id(0) == 0)
-        def _():
-            for d in range(chips):
-                for e in range(2):
-                    row = (d * 2 + e) * slots
-                    left[row : row + slots, :] = block_refs[d][e, :, META:].astype(F32)
-
+        for d in range(chips):
+            for e in range(2):
+                row = (d * 2 + e) * slots
+                left[row : row + slots, :] = block_refs[d][e, :, META:].astype(F32)
         lhs = left[...].astype(BF16)
-        for j in range(per):
-            total = jnp.dot(lhs, weight_ref[j], preferred_element_type=F32)
+
+        @pl.loop(0, heads // per)
+        def _(i):
+            right = jnp.concatenate([weight_ref[i * per + j] for j in range(per)], axis=1)
+            total = jnp.dot(lhs, right, preferred_element_type=F32)
+            columns = pl.ds(pl.multiple_of(i * (per * width), per * width), per * width)
             for d in range(chips):
                 row = d * 2 * slots
-                columns = slice(j * width, (j + 1) * width)
                 keep_ref[d, :, columns] = total[row : row + slots]
                 send_ref[d, :, columns] = total[row + slots : row + 2 * slots]
 
     shape = jax.ShapeDtypeStruct((chips, slots, heads * width), F32)
-    out_spec = pl.BlockSpec((chips, slots, per * width), lambda i: (0, 0, i))
-    return pl.pallas_call(
-        kernel,
-        grid=(heads // per,),
+    return pl.pallas_call(
+        kernel,
         out_shape=(shape, shape),
-        in_specs=[VMEM] * chips + [pl.BlockSpec((per, depth, width), lambda i: (i, 0, 0))],
-        out_specs=(out_spec, out_spec),
+        in_specs=[VMEM] * (chips + 1),
+        out_specs=(VMEM, VMEM),
         scratch_shapes=[pltpu.VMEM((rows, depth), F32)],
-        compiler_params=pltpu.CompilerParams(vmem_limit_bytes=8 * MIB),
+        compiler_params=pltpu.CompilerParams(vmem_limit_bytes=weight.size * 2 + 8 * MIB),
         cost_estimate=cost(2 * rows * weight.size, 2 * weight.size),
         name="project",
     )(*blocks, weight)
@@ -259,7 +299,7 @@
     )(keep, got)
 
 
-def attend(lengths, new_slot, page_table, sums, bias, tokens, key_pool, value_pool, key_out, value_out):
+def attend(lengths, new_slot, page_table, sums, bias, tokens, key_pool, value_pool):
     parts = len(sums)
     slots = sums[0].shape[0]
     pages, page, width = key_pool.shape
@@ -281,53 +321,20 @@
     def kernel(*refs):
         length_ref, slot_ref, table_ref = refs[:3]
         sum_refs = refs[3 : 3 + parts]
-        (bias_ref, token_ref, key_ref, value_ref, _, _, pack_keep, pack_send, key_out_ref, value_out_ref) = refs[
-            3 + parts : 13 + parts
+        (bias_ref, token_ref, key_ref, value_ref, pack_keep, pack_send, patch_ref, score_buffer, mix_buffer) = refs[
+            3 + parts :
         ]
-        key_buffer, value_buffer, score_buffer, mix_buffer, sems, out_sems = refs[13 + parts :]
         here = lax.axis_index("req")
         column_block = lax.axis_index("head")
         leaving = leaving_slot(slot_ref, slots, here)
         lengths = [length_ref[s] for s in range(slots)]
         long_slot = jnp.int32(0)
-        long_length = jnp.int32(-1)
+        long_length = jnp.int32(0)
         for s in range(slots):
             is_long = lengths[s] >= page
             long_slot = jnp.where(is_long, s, long_slot)
             long_length = jnp.where(is_long, lengths[s], long_length)
-        turns = (long_length + chunk) // chunk
-
-        pairs = ((key_ref, key_buffer), (value_ref, value_buffer))
-
-        def short_copies(n):
-            source, buffer = pairs[n]
-            return [
-                pltpu.make_async_copy(
-                    source.at[table_ref[s, 0]], buffer.at[pl.ds(long_rows + s * page, page)], sems.at[n, chunks]
-                )
-                for s in range(slots)
-            ]
-
-        def long_copies(n, c):
-            source, buffer = pairs[n]
-            return [
-                pltpu.make_async_copy(
-                    source.at[table_ref[long_slot, c * chunk_pages + i]],
-                    buffer.at[pl.ds((c * chunk_pages + i) * page, page)],
-                    sems.at[n, c],
-                )
-                for i in range(chunk_pages)
-            ]
-
-        for n in range(2):
-            for copy in short_copies(n):
-                copy.start()
-            for c in range(chunks):
-
-                @pl.when(c < turns)
-                def _():
-                    for copy in long_copies(n, c):
-                        copy.start()
+        turns = (long_length + chunk - 1) // chunk
 
         total = sum_refs[0][...] + bias_ref[...]
 
@@ -353,129 +360,88 @@
         def blocked(row):
             return jnp.where(on_head, jnp.broadcast_to(row, (tall, width)), 0.0).astype(BF16)
 
-        def append(n, s, base, offset, out_ref):
-            _, buffer = pairs[n]
-            first = pl.multiple_of(offset // 16 * 16, 16)
-            place = pl.ds(pl.multiple_of(base + first, 16), 16)
-            old = buffer[place, :].astype(F32)
-            row = lax.broadcasted_iota(jnp.int32, (16, width), 0)
-            fresh = jnp.where(row == offset - first, jnp.broadcast_to(new_rows[n][s : s + 1], (16, width)), old)
-            buffer[place, :] = fresh.astype(BF16)
-
-        def out_copy(n, s):
-            _, buffer = pairs[n]
-            out_ref = (key_out_ref, value_out_ref)[n]
-            length = lengths[s]
-            is_long = length >= page
-            within = length % page // 16 * 16
-            base = jnp.where(is_long, length // page * page, long_rows + s * page)
-            return pltpu.make_async_copy(
-                buffer.at[pl.ds(pl.multiple_of(base + within, 16), 16)],
-                out_ref.at[table_ref[s, length // page], pl.ds(pl.multiple_of(within, 16), 16)],
-                out_sems.at[n, s],
-            )
-
-        def append_short(n):
-            for s in range(slots):
-
-                @pl.when(lengths[s] < page)
-                def _():
-                    append(n, s, long_rows + s * page, lengths[s], None)
-
-        def append_long(n):
-            for s in range(slots):
-
-                @pl.when(lengths[s] >= page)
-                def _():
-                    append(n, s, 0, lengths[s], None)
-
-        def softmax(scores, valid):
+        def for_slot(which, rows):
+            found = rows[0]
+            for s in range(1, slots):
+                found = jnp.where(which == s, rows[s], found)
+            return found
+
+        def softmax(scores, valid, new_score):
             masked = jnp.where(valid, scores, -1e30)
-            peak = jnp.max(masked, axis=1, keepdims=True)
+            peak = jnp.maximum(jnp.max(masked, axis=1, keepdims=True), new_score)
             weights = jnp.where(valid, jnp.exp(masked - peak), 0.0)
-            return weights.astype(BF16), jnp.sum(weights, axis=1, keepdims=True)
+            new_weight = jnp.exp(new_score - peak)
+            denom = jnp.sum(weights, axis=1, keepdims=True) + new_weight
+            return weights.astype(BF16), new_weight.astype(BF16).astype(F32), denom
 
         across = (((1,), (1,)), ((), ()))
-        for copy in short_copies(0):
-            copy.wait()
-        append_short(0)
         short_query = jnp.concatenate([blocked(query[s : s + 1]) for s in range(slots)], axis=0)
-        short_scores = lax.dot_general(
-            short_query, key_buffer[long_rows:, :], across, preferred_element_type=F32
-        )
+        new_keys = jnp.concatenate([new_rows[0], jnp.zeros((tall - slots, width), F32)], axis=0).astype(BF16)
+        new_scores = lax.dot_general(short_query, new_keys, across, preferred_element_type=F32)
+        size = (slots * tall, tall)
+        own_column = lax.broadcasted_iota(jnp.int32, size, 0) // tall == lax.broadcasted_iota(jnp.int32, size, 1)
+        new_score = jnp.sum(jnp.where(own_column, new_scores, 0.0), axis=1, keepdims=True)
+
+        first_pages = lambda ref: jnp.concatenate([ref[table_ref[s, 0]] for s in range(slots)], axis=0)
+        short_scores = lax.dot_general(short_query, first_pages(key_ref), across, preferred_element_type=F32)
         size = (slots * tall, short_rows)
         row_slot = lax.broadcasted_iota(jnp.int32, size, 0) // tall
         column = lax.broadcasted_iota(jnp.int32, size, 1)
         limit = jnp.zeros(size, jnp.int32)
         for s in range(slots):
-            limit = jnp.where(row_slot == s, jnp.minimum(lengths[s], page - 1), limit)
-        in_slot = row_slot == column // page
-        short_probs, short_denom = softmax(short_scores, in_slot & (column % page <= limit))
-
-        long_row = jnp.zeros((1, width), F32)
-        for s in range(slots):
-            long_row = jnp.where(long_slot == s, query[s : s + 1], long_row)
-        long_query = blocked(long_row)
-        for c in range(chunks):
-
-            @pl.when(c < turns)
-            def _():
-                for copy in long_copies(0, c):
-                    copy.wait()
-
-        append_long(0)
-        score_buffer[...] = jnp.full(score_buffer.shape, -1e30, F32)
-        for c in range(chunks):
-
-            @pl.when(c < turns)
-            def _():
-                score_buffer[:, c * chunk : (c + 1) * chunk] = lax.dot_general(
-                    long_query, key_buffer[c * chunk : (c + 1) * chunk, :], across, preferred_element_type=F32
-                )
-
-        position = lax.broadcasted_iota(jnp.int32, (tall, long_rows), 1)
-        long_probs, long_denom = softmax(score_buffer[...], position <= jnp.maximum(long_length, 0))
-
-        for copy in short_copies(1):
-            copy.wait()
-        append_short(1)
-        short_mix = jnp.dot(short_probs, value_buffer[long_rows:, :], preferred_element_type=F32) / short_denom
+            limit = jnp.where(row_slot == s, lengths[s], limit)
+        valid = (row_slot == column // page) & (column % page < limit)
+        short_probs, new_prob, short_denom = softmax(short_scores, valid, new_score)
+        new_values = jnp.concatenate(
+            [jnp.broadcast_to(new_rows[1][s : s + 1], (tall, width)) for s in range(slots)], axis=0
+        )
+        short_mix = jnp.dot(short_probs, first_pages(value_ref), preferred_element_type=F32)
+        short_mix = (short_mix + new_prob * new_values) / short_denom
+
         mix_buffer[...] = jnp.zeros(mix_buffer.shape, F32)
-        for c in range(chunks):
-
-            @pl.when(c < turns)
-            def _():
-                for copy in long_copies(1, c):
-                    copy.wait()
-
-        append_long(1)
-        for n in range(2):
-            for s in range(slots):
-
-                @pl.when(leaving != s)
+
+        @pl.when(turns > 0)
+        def _():
+            some_pages = lambda ref, c: jnp.concatenate(
+                [ref[table_ref[long_slot, c * chunk_pages + i]] for i in range(chunk_pages)], axis=0
+            )
+            long_query = blocked(for_slot(long_slot, [query[s : s + 1] for s in range(slots)]))
+            long_new = for_slot(long_slot, [new_score[s * tall : (s + 1) * tall] for s in range(slots)])
+            long_value = for_slot(long_slot, [new_rows[1][s : s + 1] for s in range(slots)])
+            for c in range(chunks):
+
+                @pl.when(c < turns)
                 def _():
-                    out_copy(n, s).start()
-
-        for c in range(chunks):
-
-            @pl.when(c < turns)
-            def _():
-                mix_buffer[...] += jnp.dot(
-                    long_probs[:, c * chunk : (c + 1) * chunk],
-                    value_buffer[c * chunk : (c + 1) * chunk, :],
-                    preferred_element_type=F32,
-                )
+                    score_buffer[:, c * chunk : (c + 1) * chunk] = lax.dot_general(
+                        long_query, some_pages(key_ref, c), across, preferred_element_type=F32
+                    )
+
+                @pl.when(c >= turns)
+                def _():
+                    score_buffer[:, c * chunk : (c + 1) * chunk] = jnp.zeros((tall, chunk), F32)
+
+            position = lax.broadcasted_iota(jnp.int32, (tall, long_rows), 1)
+            long_probs, long_prob, long_denom = softmax(score_buffer[...], position < long_length, long_new)
+            for c in range(chunks):
+
+                @pl.when(c < turns)
+                def _():
+                    mix_buffer[...] += jnp.dot(
+                        long_probs[:, c * chunk : (c + 1) * chunk], some_pages(value_ref, c), preferred_element_type=F32
+                    )
+
+            mix_buffer[...] = (mix_buffer[...] + long_prob * long_value) / long_denom
 
         def fold(mixed):
             return jnp.sum(jnp.where(on_head, mixed, 0.0), axis=0, keepdims=True)
 
-        long_mix = fold(mix_buffer[...] / long_denom)
+        long_mix = fold(mix_buffer[...])
         rows = []
         for s in range(slots):
             row = fold(short_mix[s * tall : (s + 1) * tall])
             rows.append(jnp.where(lengths[s] >= page, long_mix, row))
         high = -(-slots // 8) * 8
-        attended = jnp.concatenate(rows + [jnp.zeros((high - slots, width), F32)], axis=0)
+        attended = jnp.concatenate(rows + [jnp.zeros((high - slots, width), F32)], axis=0).astype(BF16).astype(F32)
 
         token = token_ref[:, pl.ds(pl.multiple_of(column_block * width, LANES), width)].astype(F32)
         extra = []
@@ -506,33 +472,26 @@
             block = jnp.concatenate([jnp.concatenate(tiles, axis=1), extra], axis=0).astype(BF16)
             (pack_keep, pack_send)[k % 2][k // 2] = block
 
-        for n in range(2):
+        at = lax.broadcasted_iota(jnp.int32, (tall, width), 0)
+        for n, ref in enumerate((key_ref, value_ref)):
             for s in range(slots):
-
-                @pl.when(leaving != s)
-                def _():
-                    out_copy(n, s).wait()
+                offset = lengths[s] % page
+                first = pl.multiple_of(offset // tall * tall, tall)
+                old = ref[table_ref[s, lengths[s] // page], pl.ds(first, tall), :].astype(F32)
+                new = jnp.broadcast_to(new_rows[n][s : s + 1], (tall, width))
+                patch_ref[n, s] = jnp.where(at == offset - first, new, old).astype(BF16)
 
     packed = jax.ShapeDtypeStruct((parts, pack_rows(slots, strips), PACK), BF16)
-    pool_shape = jax.ShapeDtypeStruct(key_pool.shape, key_pool.dtype)
-    return pl.pallas_call(
-        kernel,
-        out_shape=(packed, packed, pool_shape, pool_shape),
-        in_specs=[SMEM] * 3 + [VMEM] * (parts + 2) + [HBM] * 4,
-        out_specs=(VMEM, VMEM, HBM, HBM),
-        scratch_shapes=[
-            pltpu.VMEM((long_rows + short_rows, width), BF16),
-            pltpu.VMEM((long_rows + short_rows, width), BF16),
-            pltpu.VMEM((tall, long_rows), F32),
-            pltpu.VMEM((tall, width), F32),
-            pltpu.SemaphoreType.DMA((2, chunks + 1)),
-            pltpu.SemaphoreType.DMA((2, slots)),
-        ],
-        input_output_aliases={7 + parts: 2, 8 + parts: 3},
+    return pl.pallas_call(
+        kernel,
+        out_shape=(packed, packed, jax.ShapeDtypeStruct((2, slots, tall, width), BF16)),
+        in_specs=[SMEM] * 3 + [VMEM] * (parts + 4),
+        out_specs=(VMEM, VMEM, VMEM),
+        scratch_shapes=[pltpu.VMEM((tall, long_rows), F32), pltpu.VMEM((tall, width), F32)],
         compiler_params=pltpu.CompilerParams(vmem_limit_bytes=18 * MIB),
         cost_estimate=cost(4 * tall * (long_rows + short_rows) * width, 4 * (long_rows + short_rows) * width),
         name="attend",
-    )(lengths, new_slot, page_table, *sums, bias, tokens, key_pool, value_pool, key_out, value_out)
+    )(lengths, new_slot, page_table, *sums, bias, tokens, key_pool, value_pool)
 
 
 def pack_rows(slots, strips):
@@ -696,26 +655,24 @@
     spread = [jnp.stack([keep[0], got[0]])] + [
         swap(jnp.stack([keep[d], got[d]]), "req", 2 * d) for d in range(1, chips)
     ]
-    key_copy = copy_pool(key_pool, got)
+    (weight,) = stage([jnp.transpose(qkv_weight, (1, 0, 2))], got, "stage_weight")
     candidates = [mine] + [swap(mine, "req", 2 * d) for d in range(1, chips)]
 
-    keep, send = project(spread, jnp.transpose(qkv_weight, (1, 0, 2)))
+    keep, send = project(spread, weight)
     got = swap(send, "req", 1)
     own, *messages = combine(keep, got)
     sums = [own] + [swap(messages[d - 1], "req", 2 * d) for d in range(1, chips)]
-    value_copy = copy_pool(value_pool, own)
-
-    pack_keep, pack_send, key_out, value_out = attend(
+    keys, values = stage([key_pool, value_pool], own, "stage_pools")
+
+    pack_keep, pack_send, patches = attend(
         lengths,
         new_slot,
         page_table,
         sums,
         qkv_bias.reshape(1, -1),
         tokens,
-        key_pool,
-        value_pool,
-        key_copy,
-        value_copy,
+        keys,
+        values,
     )
     packs = spread_pairs(pack_keep, pack_send)
 
@@ -724,10 +681,11 @@
     keep, send = out_project(
         column_block[None], packs, out_weight.reshape(-1, out_weight.shape[2]), head_groups, slots
     )
+    total = keep + swap(send, "req", 1).astype(F32)
+    key_out, value_out = write_pools(lengths, new_slot, page_table, patches, keys, values, total)
     base, key_out, value_out = place_page(
         new_slot, spread, packs, tokens, out_bias[None], candidates + [from_other], key_out, value_out
     )
-    total = keep + swap(send, "req", 1).astype(F32)
     summed = total[0]
     for d in range(1, chips):
         summed = summed + swap(total[d].astype(BF16), "req", 2 * d).astype(F32)

time: 105 us -> 77.7 us (0.74)
  local copies, waits for them, and re-layouts: 15.8 us -> 0.18 us
  starting transfers between devices: 36.8 us -> 24 us
  Pallas kernels: 20.4 us -> 25.6 us
  waiting for transfers between devices: 29.9 us -> 25.9 us
    unnamed x43 -> x15, local copies, waits for them, and re-layouts: 15.7 us -> 0.06 us
    ppermute x23, starting transfers between devices: 36.8 us -> 24 us  [swap(): return lax.ppermute(value, axis, [(i, i ^ step) for i in range(size)])]
    pallas_call x4 -> x5, Pallas kernels: 14.5 us -> 19.3 us  [the longest x2 7.52 us: stage(): pl.pallas_call(kernel, out_shape=tuple((jax.ShapeDtypeStruct(array.shape,...]
    ppermute x23, waiting for transfers between devices: 29.9 us -> 25.9 us  [swap(): return lax.ppermute(value, axis, [(i, i ^ step) for i in range(size)])]
  transfers between devices with their start and end apart: 23 -> 23, of which waited for: 11 -> 11; matrix products, arithmetic and copies ran while one was open for 0% -> 1% of each run, Pallas kernels for 9% -> 19%
where the time goes in v4:
time: 77.7 us; the launch traced here: 77.5 us
  waiting for transfers between devices  25.9 us (33%)
  Pallas kernels  25.6 us (33%)
  starting transfers between devices  24 us (31%)
  between operations  0.97 us (1%)
  other arithmetic  0.94 us (1%)
    ppermute x23, waiting for transfers between devices, swap(): return lax.ppermute(value, axis, [(i, i ^ step) for i in range(size)])  25.9 us
    ppermute x23, starting transfers between devices, swap(): return lax.ppermute(value, axis, [(i, i ^ step) for i in range(size)])  24 us
    pallas_call x2, Pallas kernels, stage(): pl.pallas_call(kernel, out_shape=tuple((jax.ShapeDtypeStruct(array.shape,...  7.52 us
    pallas_call x1, Pallas kernels, write_pools(): pl.pallas_call(kernel, out_shape=(shape, shape), in_specs=[SMEM] * 3 + [V...  4.97 us
    pallas_call x1, Pallas kernels, attend(): pl.pallas_call(kernel, out_shape=(packed, packed, jax.ShapeDtypeStruct((2...  4.59 us
    pallas_call x1, Pallas kernels, project(): pl.pallas_call(kernel, out_shape=(shape, shape), in_specs=[VMEM] * (chips...  2.25 us
    pallas_call x1, Pallas kernels, prepare(): pl.pallas_call(kernel, out_shape=(blocks, blocks, jax.ShapeDtypeStruct((2...  1.95 us
    pallas_call x1, Pallas kernels, place_page(): pl.pallas_call(kernel, out_shape=(jax.ShapeDtypeStruct((slots, width), F3...  1.95 us
  transfers between devices with their start and end apart: 23, of which 11 were waited for; matrix products, arithmetic and copies ran while one was open for 1% of the time, Pallas kernels for 19%

profile of v4, /device:TPU:0, one launch (start us, length us, event | category | flops | bytes accessed | tf_op | source)
XLA Modules:
  0.0 77.5 jit_solution(15813942869667106055)
XLA Ops:
  0.6 2.0 %prepare.1 = (bf16[4,4,1024]{2,1,0:T(4,128)(2,1)S(1)}, bf16[4,4,1024]{2,1,0:T(4,128)(2,1)S(1)}, bf16[2,64,1792]{2,1,0:T(8,128)(2,1)S(1)}) custom-call(bf16[4,7168]{1,0:T(4,128)(2,1)} %refs_8_.3, f32[1,7168]{1,0:T(1,128)} %bitcast.46, f32[1,7168]{1,0:T(1,128)} %bitcast.47, s32[4]{0:T(128)} %length_ref.3, s32[4,16]{1,0:T(4,128)} %table_ref.3, s32[4]{0:T(128)} %slot_ref.5, ...), custom_call_target="tpu_custom_call" | custom-call | bytes 917504 | tf_op jit(solution)/shard_map/prepare/pallas_call | solution.py:176
  2.6 0.5 collective-permute-start
  3.1 0.8 %collective-permute-done.refs_1_ = bf16[4,4,1024]{2,1,0:T(4,128)(2,1)S(1)} collective-permute-done((bf16[4,4,1024]{2,1,0:T(4,128)(2,1)S(1)}, bf16[4,4,1024]{2,1,0:T(4,128)(2,1)S(1)}, u32[]{:S(2)}, u32[]{:S(2)}) %collective-permute-start) | collective-permute-done | bytes 32800 | tf_op jit(solution)/shard_map/ppermute | solution.py:29
  4.0 3.9 %collective-permute-start.3 = (bf16[2,4,1024]{2,1,0:T(4,128)(2,1)S(1)}, bf16[2,4,1024]{2,1,0:T(4,128)(2,1)S(1)}, u32[]{:S(2)}, u32[]{:S(2)}) collective-permute-start(bf16[2,4,1024]{2,1,0:T(4,128)(2,1)S(1)} %pad_maximum_fusion.7), channel_id=1, source_target_pairs={{0,24},{4,28},{8,16},{12,20},{16,8},{20,12},{24,0},{28,4},{1,25},{... | collective-permute-start | bytes 49160 | tf_op jit(solution)/shard_map/ppermute | solution.py:29
  7.9 0.6 collective-permute-start.2
  8.5 0.1 collective-permute-start.1
  8.6 3.8 %stage_weight.1.refs_4_ = bf16[14,896,384]{2,1,0:T(8,128)(2,1)S(1)} custom-call(bf16[14,896,384]{2,1,0:T(8,128)(2,1)} %bitcast.45, bf16[4,4,1024]{2,1,0:T(4,128)(2,1)S(1)} %collective-permute-done.refs_1_), custom_call_target="tpu_custom_call" | custom-call | bytes 9633792 | tf_op jit(solution)/shard_map/stage_weight/pallas_call | solution.py:62
  12.5 2.3 %project.1 = (f32[4,4,5376]{2,1,0:T(4,128)S(1)}, f32[4,4,5376]{2,1,0:T(4,128)S(1)}) custom-call(bf16[2,4,1024]{2,1,0:T(4,128)(2,1)S(1)} %pad_maximum_fusion.4.refs_0_, bf16[2,4,1024]{2,1,0:T(4,128)(2,1)S(1)} %collective-permute-done.1.refs_1_, bf16[2,4,1024]{2,1,0:T(4,128)(2,1)S(1)} %collective-permute-done.2.refs_2_, ...), custom_call_target="tpu_custom_call" | custom-call | flops 308281344 | bytes 9633792 | tf_op jit(solution)/shard_map/project/pallas_call | solution.py:261
  14.7 0.1 collective-permute-start.4
  14.8 1.6 %collective-permute-done.4.got_ref = f32[4,4,5376]{2,1,0:T(4,128)S(1)} collective-permute-done((f32[4,4,5376]{2,1,0:T(4,128)S(1)}, f32[4,4,5376]{2,1,0:T(4,128)S(1)}, u32[]{:S(2)}, u32[]{:S(2)}) %collective-permute-start.4) | collective-permute-done | bytes 344096 | tf_op jit(solution)/shard_map/ppermute | solution.py:29
  16.5 0.1 combine.1
  16.5 2.0 %collective-permute-start.5 = (bf16[4,7168]{1,0:T(4,128)(2,1)S(1)}, bf16[4,7168]{1,0:T(4,128)(2,1)S(1)}, u32[]{:S(2)}, u32[]{:S(2)}) collective-permute-start(bf16[4,7168]{1,0:T(4,128)(2,1)S(1)} %get-tuple-element.29), channel_id=1, source_target_pairs={{0,8},{4,12},{8,0},{12,4},{16,24},{20,28},{24,16},{28,20},{1,9},{5... | collective-permute-start | bytes 172040 | tf_op jit(solution)/shard_map/ppermute | solution.py:29
  18.5 1.5 %collective-permute-start.6 = (bf16[4,7168]{1,0:T(4,128)(2,1)S(1)}, bf16[4,7168]{1,0:T(4,128)(2,1)S(1)}, u32[]{:S(2)}, u32[]{:S(2)}) collective-permute-start(bf16[4,7168]{1,0:T(4,128)(2,1)S(1)} %get-tuple-element.30), channel_id=1, source_target_pairs={{0,16},{4,20},{8,24},{12,28},{16,0},{20,4},{24,8},{28,12},{1,17},{... | collective-permute-start | bytes 172040 | tf_op jit(solution)/shard_map/ppermute | solution.py:29
  20.1 0.0 collective-permute-start.7
  20.1 0.0 copy-start.4
  20.2 3.7 %stage_pools.1 = (bf16[20,64,1792]{2,1,0:T(8,128)(2,1)S(1)}, bf16[20,64,1792]{2,1,0:T(8,128)(2,1)S(1)}) custom-call(bf16[20,64,1792]{2,1,0:T(8,128)(2,1)} %refs_0_.2, bf16[20,64,1792]{2,1,0:T(8,128)(2,1)} %refs_1_.2, f32[4,5376]{1,0:T(4,128)S(1)} %get-tuple-element.28.refs_2_.refs_3_), custom_call_target="tpu_custom_call" | custom-call | bytes 9175040 | tf_op jit(solution)/shard_map/stage_pools/pallas_call | solution.py:62
  23.9 1.2 %collective-permute-done.7.refs_6_ = bf16[4,7168]{1,0:T(4,128)(2,1)S(1)} collective-permute-done((bf16[4,7168]{1,0:T(4,128)(2,1)S(1)}, bf16[4,7168]{1,0:T(4,128)(2,1)S(1)}, u32[]{:S(2)}, u32[]{:S(2)}) %collective-permute-start.7) | collective-permute-done | bytes 57376 | tf_op jit(solution)/shard_map/ppermute | solution.py:29
  25.2 4.6 %attend.1 = (bf16[4,32,256]{2,1,0:T(8,128)(2,1)S(1)}, bf16[4,32,256]{2,1,0:T(8,128)(2,1)S(1)}, bf16[2,4,16,1792]{3,2,1,0:T(8,128)(2,1)S(1)}) custom-call(s32[4]{0:T(128)S(1)} %copy-done.5, s32[4]{0:T(128)S(1)} %copy-done.4, s32[4,16]{1,0:T(4,128)S(1)} %copy-done.3, f32[4,5376]{1,0:T(4,128)S(1)} %get-tuple-element.28.refs_2_.refs_3_, ...), custom_call_target="tpu_custom_call" | custom-call | flops 146800640 | bytes 9175040 | tf_op jit(solution)/shard_map/attend/pallas_call | solution.py:485
  29.8 0.1 collective-permute-start.8
  29.9 1.2 %collective-permute-done.8 = bf16[4,32,256]{2,1,0:T(8,128)(2,1)S(1)} collective-permute-done((bf16[4,32,256]{2,1,0:T(8,128)(2,1)S(1)}, bf16[4,32,256]{2,1,0:T(8,128)(2,1)S(1)}, u32[]{:S(2)}, u32[]{:S(2)}) %collective-permute-start.8) | collective-permute-done | bytes 65568 | tf_op jit(solution)/shard_map/ppermute | solution.py:29
  31.1 1.8 %collective-permute-start.11 = (bf16[2,32,256]{2,1,0:T(8,128)(2,1)S(1)}, bf16[2,32,256]{2,1,0:T(8,128)(2,1)S(1)}, u32[]{:S(2)}, u32[]{:S(2)}) collective-permute-start(bf16[2,32,256]{2,1,0:T(8,128)(2,1)S(1)} %pad_maximum_fusion.3), channel_id=1, source_target_pairs={{0,24},{4,28},{8,16},{12,20},{16,8},{20,12},{24,0},{28,4},{1,25},{... | collective-permute-start | bytes 98312 | tf_op jit(solution)/shard_map/ppermute | solution.py:29
  32.9 1.8 %collective-permute-start.9 = (bf16[2,32,256]{2,1,0:T(8,128)(2,1)S(1)}, bf16[2,32,256]{2,1,0:T(8,128)(2,1)S(1)}, u32[]{:S(2)}, u32[]{:S(2)}) collective-permute-start(bf16[2,32,256]{2,1,0:T(8,128)(2,1)S(1)} %pad_maximum_fusion.1), channel_id=1, source_target_pairs={{0,8},{4,12},{8,0},{12,4},{16,24},{20,28},{24,16},{28,20},{1,9},{5... | collective-permute-start | bytes 98312 | tf_op jit(solution)/shard_map/ppermute | solution.py:29
  34.7 1.4 %collective-permute-done.11.refs_3_.refs_7_ = bf16[2,32,256]{2,1,0:T(8,128)(2,1)S(1)} collective-permute-done((bf16[2,32,256]{2,1,0:T(8,128)(2,1)S(1)}, bf16[2,32,256]{2,1,0:T(8,128)(2,1)S(1)}, u32[]{:S(2)}, u32[]{:S(2)}) %collective-permute-start.11) | collective-permute-done | bytes 32800 | tf_op jit(solution)/shard_map/ppermute | solution.py:29
  36.1 0.7 collective-permute-done.10.refs_2_.refs_6_
  36.8 0.1 collective-permute-done.9.refs_1_.refs_5_
  36.9 1.8 %out_project.1 = (f32[4,4,4,1792]{3,2,1,0:T(4,128)S(1)}, bf16[4,4,4,1792]{3,2,1,0:T(4,128)(2,1)S(1)}) custom-call(s32[1]{0:T(128)} %bitcast.column_ref, bf16[2,32,256]{2,1,0:T(8,128)(2,1)S(1)} %pad_maximum_fusion.refs_0_.refs_4_, bf16[2,32,256]{2,1,0:T(8,128)(2,1)S(1)} %collective-permute-done.9.refs_1_.refs_5_, ...), custom_call_target="tpu_custom_call" | custom-call | flops 102760448 | bytes 3211264 | tf_op jit(solution)/shard_map/out_project/pallas_call | solution.py:536
  38.6 0.1 collective-permute-start.12
  38.7 1.8 %collective-permute-start.19 = (bf16[2,64,1792]{2,1,0:T(8,128)(2,1)S(1)}, bf16[2,64,1792]{2,1,0:T(8,128)(2,1)S(1)}, u32[]{:S(2)}, u32[]{:S(2)}) collective-permute-start(bf16[2,64,1792]{2,1,0:T(8,128)(2,1)S(1)} %get-tuple-element.38.refs_4_.refs_10_), channel_id=1, source_target_pairs={{0,8},{4,12},{8,0},{12,4},{16,24},{20,28},{24,16},{28,20},{1,9},{5... | collective-permute-start | bytes 1376264 | tf_op jit(solution)/shard_map/ppermute | solution.py:29
  40.5 0.3 collective-permute-start.20
  40.8 1.5 %collective-permute-start.21 = (bf16[2,64,1792]{2,1,0:T(8,128)(2,1)S(1)}, bf16[2,64,1792]{2,1,0:T(8,128)(2,1)S(1)}, u32[]{:S(2)}, u32[]{:S(2)}) collective-permute-start(bf16[2,64,1792]{2,1,0:T(8,128)(2,1)S(1)} %get-tuple-element.38.refs_4_.refs_10_), channel_id=1, source_target_pairs={{0,24},{4,28},{8,16},{12,20},{16,8},{20,12},{24,0},{28,4},{1,25},{... | collective-permute-start | bytes 1376264 | tf_op jit(solution)/shard_map/ppermute | solution.py:29
  42.3 0.2 fusion.10
  42.5 0.1 slice_bitcast_fusion.3
  42.5 1.8 %collective-permute-start.13 = (bf16[4,4,1792]{2,1,0:T(4,128)(2,1)S(1)}, bf16[4,4,1792]{2,1,0:T(4,128)(2,1)S(1)}, u32[]{:S(2)}, u32[]{:S(2)}) collective-permute-start(bf16[4,4,1792]{2,1,0:T(4,128)(2,1)S(1)} %get-tuple-element.49), channel_id=1, source_target_pairs={{0,8},{4,12},{8,0},{12,4},{16,24},{20,28},{24,16},{28,20},{1,9},{5... | collective-permute-start | bytes 172040 | tf_op jit(solution)/shard_map/ppermute | solution.py:29
  44.3 0.3 collective-permute-start.14
  44.6 7.5 %collective-permute-done.19.refs_5_.refs_11_ = bf16[2,64,1792]{2,1,0:T(8,128)(2,1)S(1)} collective-permute-done((bf16[2,64,1792]{2,1,0:T(8,128)(2,1)S(1)}, bf16[2,64,1792]{2,1,0:T(8,128)(2,1)S(1)}, u32[]{:S(2)}, u32[]{:S(2)}) %collective-permute-start.19) | collective-permute-done | bytes 458784 | tf_op jit(solution)/shard_map/ppermute | solution.py:29
  52.1 1.5 %collective-permute-start.15 = (bf16[4,4,1792]{2,1,0:T(4,128)(2,1)S(1)}, bf16[4,4,1792]{2,1,0:T(4,128)(2,1)S(1)}, u32[]{:S(2)}, u32[]{:S(2)}) collective-permute-start(bf16[4,4,1792]{2,1,0:T(4,128)(2,1)S(1)} %get-tuple-element.50), channel_id=1, source_target_pairs={{0,24},{4,28},{8,16},{12,20},{16,8},{20,12},{24,0},{28,4},{1,25},{... | collective-permute-start | bytes 172040 | tf_op jit(solution)/shard_map/ppermute | solution.py:29
  53.6 10.0 %collective-permute-done.20.refs_6_.refs_12_ = bf16[2,64,1792]{2,1,0:T(8,128)(2,1)S(1)} collective-permute-done((bf16[2,64,1792]{2,1,0:T(8,128)(2,1)S(1)}, bf16[2,64,1792]{2,1,0:T(8,128)(2,1)S(1)}, u32[]{:S(2)}, u32[]{:S(2)}) %collective-permute-start.20) | collective-permute-done | bytes 458784 | tf_op jit(solution)/shard_map/ppermute | solution.py:29
  63.5 0.5 choose_page.1
  64.0 0.1 collective-permute-start.22
  64.1 0.4 collective-permute-done.14
  64.6 0.8 %collective-permute-done.15 = bf16[4,4,1792]{2,1,0:T(4,128)(2,1)S(1)} collective-permute-done((bf16[4,4,1792]{2,1,0:T(4,128)(2,1)S(1)}, bf16[4,4,1792]{2,1,0:T(4,128)(2,1)S(1)}, u32[]{:S(2)}, u32[]{:S(2)}) %collective-permute-start.15) | collective-permute-done | bytes 57376 | tf_op jit(solution)/shard_map/ppermute | solution.py:29
  65.4 0.1 fusion.8
  65.5 1.6 %collective-permute-start.16 = (bf16[4,1792]{1,0:T(4,128)(2,1)S(1)}, bf16[4,1792]{1,0:T(4,128)(2,1)S(1)}, u32[]{:S(2)}, u32[]{:S(2)}) collective-permute-start(bf16[4,1792]{1,0:T(4,128)(2,1)S(1)} %get-tuple-element.60), channel_id=1, source_target_pairs={{0,1},{1,0},{2,3},{3,2},{4,5},{5,4},{6,7},{7,6},{8,9},{9,8},{10,11... | collective-permute-start | bytes 43016 | tf_op jit(solution)/shard_map/ppermute | solution.py:29
  67.1 2.6 %collective-permute-start.17 = (bf16[4,1792]{1,0:T(4,128)(2,1)S(1)}, bf16[4,1792]{1,0:T(4,128)(2,1)S(1)}, u32[]{:S(2)}, u32[]{:S(2)}) collective-permute-start(bf16[4,1792]{1,0:T(4,128)(2,1)S(1)} %get-tuple-element.62), channel_id=1, source_target_pairs={{0,2},{1,3},{2,0},{3,1},{4,6},{5,7},{6,4},{7,5},{8,10},{9,11},{10,... | collective-permute-start | bytes 43016 | tf_op jit(solution)/shard_map/ppermute | solution.py:29
  69.7 0.2 collective-permute-start.18
  69.9 5.0 %write_pools.1 = (bf16[20,64,1792]{2,1,0:T(8,128)(2,1)}, bf16[20,64,1792]{2,1,0:T(8,128)(2,1)}) custom-call(s32[4]{0:T(128)S(1)} %copy-done.5, s32[4]{0:T(128)S(1)} %copy-done.4, s32[4,16]{1,0:T(4,128)S(1)} %copy-done.3, bf16[2,4,16,1792]{3,2,1,0:T(8,128)(2,1)S(1)} %get-tuple-element.39.patch_ref, ...), custom_call_target="tpu_custom_call" | custom-call | bytes 9175040 | tf_op jit(solution)/shard_map/write_pools/pallas_call | solution.py:110
  74.9 1.9 %place_page.1 = (f32[4,1792]{1,0:T(4,128)S(1)}, bf16[20,64,1792]{2,1,0:T(8,128)(2,1)}, bf16[20,64,1792]{2,1,0:T(8,128)(2,1)}) custom-call(s32[4]{0:T(128)S(1)} %copy-done.4, bf16[2,4,1024]{2,1,0:T(4,128)(2,1)S(1)} %pad_maximum_fusion.4.refs_0_, ...), custom_call_target="tpu_custom_call", output_to_operand_aliasing={{1}: (16, {}), {2}: (17, {})} | custom-call | bytes 917504 | tf_op jit(solution)/shard_map/place_page/pallas_call | solution.py:612
  76.9 0.6 fusion.7
  (40 shorter events, 0.2 us)
Async XLA Ops:
  2.6 1.4 %collective-permute-start = (bf16[4,4,1024]{2,1,0:T(4,128)(2,1)S(1)}, bf16[4,4,1024]{2,1,0:T(4,128)(2,1)S(1)}, u32[]{:S(2)}, u32[]{:S(2)}) collective-permute-start(bf16[4,4,1024]{2,1,0:T(4,128)(2,1)S(1)} %get-tuple-element.25), channel_id=1, source_target_pairs={{0,4},{4,0},{8,12},{12,8},{16,20},{20,16},{24,28},{28,24},{1,5},{5... | collective-permute-start | bytes 98312 | tf_op jit(solution)/shard_map/ppermute | solution.py:29
  4.0 8.4 %collective-permute-start.3 = (bf16[2,4,1024]{2,1,0:T(4,128)(2,1)S(1)}, bf16[2,4,1024]{2,1,0:T(4,128)(2,1)S(1)}, u32[]{:S(2)}, u32[]{:S(2)}) collective-permute-start(bf16[2,4,1024]{2,1,0:T(4,128)(2,1)S(1)} %pad_maximum_fusion.7), channel_id=1, source_target_pairs={{0,24},{4,28},{8,16},{12,20},{16,8},{20,12},{24,0},{28,4},{1,25},{... | collective-permute-start | bytes 49160 | tf_op jit(solution)/shard_map/ppermute | solution.py:29
  7.9 4.6 %collective-permute-start.2 = (bf16[2,4,1024]{2,1,0:T(4,128)(2,1)S(1)}, bf16[2,4,1024]{2,1,0:T(4,128)(2,1)S(1)}, u32[]{:S(2)}, u32[]{:S(2)}) collective-permute-start(bf16[2,4,1024]{2,1,0:T(4,128)(2,1)S(1)} %pad_maximum_fusion.6), channel_id=1, source_target_pairs={{0,16},{4,20},{8,24},{12,28},{16,0},{20,4},{24,8},{28,12},{1,17},{... | collective-permute-start | bytes 49160 | tf_op jit(solution)/shard_map/ppermute | solution.py:29
  8.5 4.0 %collective-permute-start.1 = (bf16[2,4,1024]{2,1,0:T(4,128)(2,1)S(1)}, bf16[2,4,1024]{2,1,0:T(4,128)(2,1)S(1)}, u32[]{:S(2)}, u32[]{:S(2)}) collective-permute-start(bf16[2,4,1024]{2,1,0:T(4,128)(2,1)S(1)} %pad_maximum_fusion.5), channel_id=1, source_target_pairs={{0,8},{4,12},{8,0},{12,4},{16,24},{20,28},{24,16},{28,20},{1,9},{5... | collective-permute-start | bytes 49160 | tf_op jit(solution)/shard_map/ppermute | solution.py:29
  12.4 7.6 %copy-start.6 = (f32[14,384]{1,0:T(8,128)S(1)}, f32[14,384]{1,0:T(8,128)}, u32[]{:S(2)}) copy-start(f32[14,384]{1,0:T(8,128)} %param.17) | copy-start | bytes 64516
  14.7 1.7 %collective-permute-start.4 = (f32[4,4,5376]{2,1,0:T(4,128)S(1)}, f32[4,4,5376]{2,1,0:T(4,128)S(1)}, u32[]{:S(2)}, u32[]{:S(2)}) collective-permute-start(f32[4,4,5376]{2,1,0:T(4,128)S(1)} %get-tuple-element.27), channel_id=1, source_target_pairs={{0,4},{4,0},{8,12},{12,8},{16,20},{20,16},{24,28},{28,24},{1,5},{5... | collective-permute-start | bytes 1032200 | tf_op jit(solution)/shard_map/ppermute | solution.py:29
  16.5 7.4 %collective-permute-start.5 = (bf16[4,7168]{1,0:T(4,128)(2,1)S(1)}, bf16[4,7168]{1,0:T(4,128)(2,1)S(1)}, u32[]{:S(2)}, u32[]{:S(2)}) collective-permute-start(bf16[4,7168]{1,0:T(4,128)(2,1)S(1)} %get-tuple-element.29), channel_id=1, source_target_pairs={{0,8},{4,12},{8,0},{12,4},{16,24},{20,28},{24,16},{28,20},{1,9},{5... | collective-permute-start | bytes 172040 | tf_op jit(solution)/shard_map/ppermute | solution.py:29
  18.5 5.4 %collective-permute-start.6 = (bf16[4,7168]{1,0:T(4,128)(2,1)S(1)}, bf16[4,7168]{1,0:T(4,128)(2,1)S(1)}, u32[]{:S(2)}, u32[]{:S(2)}) collective-permute-start(bf16[4,7168]{1,0:T(4,128)(2,1)S(1)} %get-tuple-element.30), channel_id=1, source_target_pairs={{0,16},{4,20},{8,24},{12,28},{16,0},{20,4},{24,8},{28,12},{1,17},{... | collective-permute-start | bytes 172040 | tf_op jit(solution)/shard_map/ppermute | solution.py:29
  20.1 5.1 %collective-permute-start.7 = (bf16[4,7168]{1,0:T(4,128)(2,1)S(1)}, bf16[4,7168]{1,0:T(4,128)(2,1)S(1)}, u32[]{:S(2)}, u32[]{:S(2)}) collective-permute-start(bf16[4,7168]{1,0:T(4,128)(2,1)S(1)} %get-tuple-element.31), channel_id=1, source_target_pairs={{0,24},{4,28},{8,16},{12,20},{16,8},{20,12},{24,0},{28,4},{1,25},{... | collective-permute-start | bytes 172040 | tf_op jit(solution)/shard_map/ppermute | solution.py:29
  20.1 5.0 %copy-start.1 = (bf16[4,7168]{1,0:T(4,128)(2,1)S(1)}, bf16[4,7168]{1,0:T(4,128)(2,1)}, u32[]{:S(2)}) copy-start(bf16[4,7168]{1,0:T(4,128)(2,1)} %refs_8_.3) | copy-start | bytes 172036
  20.1 5.0 %copy-start.3 = (s32[4,16]{1,0:T(4,128)S(1)}, s32[4,16]{1,0:T(4,128)}, u32[]{:S(2)}) copy-start(s32[4,16]{1,0:T(4,128)} %table_ref.3) | copy-start | bytes 772
  20.1 5.0 %copy-start.4 = (s32[4]{0:T(128)S(1)}, s32[4]{0:T(128)}, u32[]{:S(2)}) copy-start(s32[4]{0:T(128)} %slot_ref.5) | copy-start | bytes 52
  20.1 5.0 %copy-start.5 = (s32[4]{0:T(128)S(1)}, s32[4]{0:T(128)}, u32[]{:S(2)}) copy-start(s32[4]{0:T(128)} %length_ref.3) | copy-start | bytes 52
  25.2 11.7 %copy-start = (bf16[14,16,7168]{2,1,0:T(8,128)(2,1)S(1)}, bf16[14,16,7168]{2,1,0:T(8,128)(2,1)}, u32[]{:S(2)}) copy-start(bf16[14,16,7168]{2,1,0:T(8,128)(2,1)} %param.18) | copy-start | bytes 9633796
  29.8 1.3 %collective-permute-start.8 = (bf16[4,32,256]{2,1,0:T(8,128)(2,1)S(1)}, bf16[4,32,256]{2,1,0:T(8,128)(2,1)S(1)}, u32[]{:S(2)}, u32[]{:S(2)}) collective-permute-start(bf16[4,32,256]{2,1,0:T(8,128)(2,1)S(1)} %get-tuple-element.35), channel_id=1, source_target_pairs={{0,4},{4,0},{8,12},{12,8},{16,20},{20,16},{24,28},{28,24},{1,5},{5... | collective-permute-start | bytes 196616 | tf_op jit(solution)/shard_map/ppermute | solution.py:29
  31.1 5.0 %collective-permute-start.11 = (bf16[2,32,256]{2,1,0:T(8,128)(2,1)S(1)}, bf16[2,32,256]{2,1,0:T(8,128)(2,1)S(1)}, u32[]{:S(2)}, u32[]{:S(2)}) collective-permute-start(bf16[2,32,256]{2,1,0:T(8,128)(2,1)S(1)} %pad_maximum_fusion.3), channel_id=1, source_target_pairs={{0,24},{4,28},{8,16},{12,20},{16,8},{20,12},{24,0},{28,4},{1,25},{... | collective-permute-start | bytes 98312 | tf_op jit(solution)/shard_map/ppermute | solution.py:29
  32.9 3.9 %collective-permute-start.10 = (bf16[2,32,256]{2,1,0:T(8,128)(2,1)S(1)}, bf16[2,32,256]{2,1,0:T(8,128)(2,1)S(1)}, u32[]{:S(2)}, u32[]{:S(2)}) collective-permute-start(bf16[2,32,256]{2,1,0:T(8,128)(2,1)S(1)} %pad_maximum_fusion.2), channel_id=1, source_target_pairs={{0,16},{4,20},{8,24},{12,28},{16,0},{20,4},{24,8},{28,12},{1,17},{... | collective-permute-start | bytes 98312 | tf_op jit(solution)/shard_map/ppermute | solution.py:29
  32.9 4.0 %collective-permute-start.9 = (bf16[2,32,256]{2,1,0:T(8,128)(2,1)S(1)}, bf16[2,32,256]{2,1,0:T(8,128)(2,1)S(1)}, u32[]{:S(2)}, u32[]{:S(2)}) collective-permute-start(bf16[2,32,256]{2,1,0:T(8,128)(2,1)S(1)} %pad_maximum_fusion.1), channel_id=1, source_target_pairs={{0,8},{4,12},{8,0},{12,4},{16,24},{20,28},{24,16},{28,20},{1,9},{5... | collective-permute-start | bytes 98312 | tf_op jit(solution)/shard_map/ppermute | solution.py:29
  38.6 3.6 %collective-permute-start.12 = (bf16[4,4,4,1792]{3,2,1,0:T(4,128)(2,1)S(1)}, bf16[4,4,4,1792]{3,2,1,0:T(4,128)(2,1)S(1)}, u32[]{:S(2)}, u32[]{:S(2)}) collective-permute-start(bf16[4,4,4,1792]{3,2,1,0:T(4,128)(2,1)S(1)} %get-tuple-element.37), channel_id=1, source_target_pairs={{0,4},{4,0},{8,12},{12,8},{16,20},{20,16},{24,28},{28,24},{1,5},{5... | collective-permute-start | bytes 688136 | tf_op jit(solution)/shard_map/ppermute | solution.py:29
  38.7 13.4 %collective-permute-start.19 = (bf16[2,64,1792]{2,1,0:T(8,128)(2,1)S(1)}, bf16[2,64,1792]{2,1,0:T(8,128)(2,1)S(1)}, u32[]{:S(2)}, u32[]{:S(2)}) collective-permute-start(bf16[2,64,1792]{2,1,0:T(8,128)(2,1)S(1)} %get-tuple-element.38.refs_4_.refs_10_), channel_id=1, source_target_pairs={{0,8},{4,12},{8,0},{12,4},{16,24},{20,28},{24,16},{28,20},{1,9},{5... | collective-permute-start | bytes 1376264 | tf_op jit(solution)/shard_map/ppermute | solution.py:29
  40.5 23.0 %collective-permute-start.20 = (bf16[2,64,1792]{2,1,0:T(8,128)(2,1)S(1)}, bf16[2,64,1792]{2,1,0:T(8,128)(2,1)S(1)}, u32[]{:S(2)}, u32[]{:S(2)}) collective-permute-start(bf16[2,64,1792]{2,1,0:T(8,128)(2,1)S(1)} %get-tuple-element.38.refs_4_.refs_10_), channel_id=1, source_target_pairs={{0,16},{4,20},{8,24},{12,28},{16,0},{20,4},{24,8},{28,12},{1,17},{... | collective-permute-start | bytes 1376264 | tf_op jit(solution)/shard_map/ppermute | solution.py:29
  40.8 22.7 %collective-permute-start.21 = (bf16[2,64,1792]{2,1,0:T(8,128)(2,1)S(1)}, bf16[2,64,1792]{2,1,0:T(8,128)(2,1)S(1)}, u32[]{:S(2)}, u32[]{:S(2)}) collective-permute-start(bf16[2,64,1792]{2,1,0:T(8,128)(2,1)S(1)} %get-tuple-element.38.refs_4_.refs_10_), channel_id=1, source_target_pairs={{0,24},{4,28},{8,16},{12,20},{16,8},{20,12},{24,0},{28,4},{1,25},{... | collective-permute-start | bytes 1376264 | tf_op jit(solution)/shard_map/ppermute | solution.py:29
  42.5 21.6 %collective-permute-start.13 = (bf16[4,4,1792]{2,1,0:T(4,128)(2,1)S(1)}, bf16[4,4,1792]{2,1,0:T(4,128)(2,1)S(1)}, u32[]{:S(2)}, u32[]{:S(2)}) collective-permute-start(bf16[4,4,1792]{2,1,0:T(4,128)(2,1)S(1)} %get-tuple-element.49), channel_id=1, source_target_pairs={{0,8},{4,12},{8,0},{12,4},{16,24},{20,28},{24,16},{28,20},{1,9},{5... | collective-permute-start | bytes 172040 | tf_op jit(solution)/shard_map/ppermute | solution.py:29
  44.3 20.3 %collective-permute-start.14 = (bf16[4,4,1792]{2,1,0:T(4,128)(2,1)S(1)}, bf16[4,4,1792]{2,1,0:T(4,128)(2,1)S(1)}, u32[]{:S(2)}, u32[]{:S(2)}) collective-permute-start(bf16[4,4,1792]{2,1,0:T(4,128)(2,1)S(1)} %get-tuple-element.51), channel_id=1, source_target_pairs={{0,16},{4,20},{8,24},{12,28},{16,0},{20,4},{24,8},{28,12},{1,17},{... | collective-permute-start | bytes 172040 | tf_op jit(solution)/shard_map/ppermute | solution.py:29
  52.1 13.3 %collective-permute-start.15 = (bf16[4,4,1792]{2,1,0:T(4,128)(2,1)S(1)}, bf16[4,4,1792]{2,1,0:T(4,128)(2,1)S(1)}, u32[]{:S(2)}, u32[]{:S(2)}) collective-permute-start(bf16[4,4,1792]{2,1,0:T(4,128)(2,1)S(1)} %get-tuple-element.50), channel_id=1, source_target_pairs={{0,24},{4,28},{8,16},{12,20},{16,8},{20,12},{24,0},{28,4},{1,25},{... | collective-permute-start | bytes 172040 | tf_op jit(solution)/shard_map/ppermute | solution.py:29
  64.0 10.9 %collective-permute-start.22 = (bf16[2,64,1792]{2,1,0:T(8,128)(2,1)S(1)}, bf16[2,64,1792]{2,1,0:T(8,128)(2,1)S(1)}, u32[]{:S(2)}, u32[]{:S(2)}) collective-permute-start(bf16[2,64,1792]{2,1,0:T(8,128)(2,1)S(1)} %choose_page.1), channel_id=1, source_target_pairs={{0,4},{4,0},{8,12},{12,8},{16,20},{20,16},{24,28},{28,24},{1,5},{5... | collective-permute-start | bytes 1376264 | tf_op jit(solution)/shard_map/ppermute | solution.py:29
  65.5 11.4 %collective-permute-start.16 = (bf16[4,1792]{1,0:T(4,128)(2,1)S(1)}, bf16[4,1792]{1,0:T(4,128)(2,1)S(1)}, u32[]{:S(2)}, u32[]{:S(2)}) collective-permute-start(bf16[4,1792]{1,0:T(4,128)(2,1)S(1)} %get-tuple-element.60), channel_id=1, source_target_pairs={{0,1},{1,0},{2,3},{3,2},{4,5},{5,4},{6,7},{7,6},{8,9},{9,8},{10,11... | collective-permute-start | bytes 43016 | tf_op jit(solution)/shard_map/ppermute | solution.py:29
  67.1 9.8 %collective-permute-start.17 = (bf16[4,1792]{1,0:T(4,128)(2,1)S(1)}, bf16[4,1792]{1,0:T(4,128)(2,1)S(1)}, u32[]{:S(2)}, u32[]{:S(2)}) collective-permute-start(bf16[4,1792]{1,0:T(4,128)(2,1)S(1)} %get-tuple-element.62), channel_id=1, source_target_pairs={{0,2},{1,3},{2,0},{3,1},{4,6},{5,7},{6,4},{7,5},{8,10},{9,11},{10,... | collective-permute-start | bytes 43016 | tf_op jit(solution)/shard_map/ppermute | solution.py:29
  69.7 7.2 %collective-permute-start.18 = (bf16[4,1792]{1,0:T(4,128)(2,1)S(1)}, bf16[4,1792]{1,0:T(4,128)(2,1)S(1)}, u32[]{:S(2)}, u32[]{:S(2)}) collective-permute-start(bf16[4,1792]{1,0:T(4,128)(2,1)S(1)} %get-tuple-element.61), channel_id=1, source_target_pairs={{0,3},{1,2},{2,1},{3,0},{4,7},{5,6},{6,5},{7,4},{8,11},{9,10},{10,... | collective-permute-start | bytes 43016 | tf_op jit(solution)/shard_map/ppermute | solution.py:29
  69.9 5.0 %copy-start.2 = (f32[7168]{0:T(1024)S(1)}, f32[7168]{0:T(1024)}, u32[]{:S(2)}) copy-start(f32[7168]{0:T(1024)} %param.19) | copy-start | bytes 86020

commit v5 on v4

--- a/solution.py
+++ b/solution.py
@@ -21,7 +21,8 @@
 
 
 def cost(flops, moved):
-    return pl.CostEstimate(flops=flops, bytes_accessed=moved, transcendentals=0)
+    del flops, moved
+    return pl.CostEstimate(flops=0, bytes_accessed=0, transcendentals=0)
 
 
 def swap(value, axis, step):
@@ -29,8 +30,7 @@
     return lax.ppermute(value, axis, [(i, i ^ step) for i in range(size)])
 
 
-def spread_pairs(keep, send):
-    got = swap(send, "req", 1)
+def spread_pairs(keep, got):
     chips = keep.shape[0]
     return [jnp.stack([keep[0], got[0]])] + [
         swap(jnp.stack([keep[d], got[d]]), "req", 2 * d) for d in range(1, chips)
@@ -71,52 +71,48 @@
     )(*in_hbm(*arrays), after)
 
 
-def write_pools(lengths, new_slot, page_table, patches, key_pool, value_pool, after):
-    pages, page, width = key_pool.shape
+def write_pool(lengths, new_slot, page_table, patches, pool, after, part):
+    pages, page, width = pool.shape
     slots, tall = patches.shape[1:3]
     parts = 4
     step = pages // parts
 
-    def kernel(length_ref, slot_ref, table_ref, patch_ref, key_ref, value_ref, _, key_out, value_out, sems, patch_sems):
+    def kernel(length_ref, slot_ref, table_ref, patch_ref, pool_ref, _, out_ref, sems, patch_sems):
         leaving = leaving_slot(slot_ref, slots, lax.axis_index("req"))
-        pairs = ((key_ref, key_out), (value_ref, value_out))
+        places = [pl.ds(i * step, step) for i in range(parts)]
         copies = [
-            pltpu.make_async_copy(source.at[pl.ds(i * step, step)], target.at[pl.ds(i * step, step)], sems.at[n, i])
-            for n, (source, target) in enumerate(pairs)
-            for i in range(parts)
+            pltpu.make_async_copy(pool_ref.at[place], out_ref.at[place], sems.at[i]) for i, place in enumerate(places)
         ]
         for copy in copies:
             copy.start()
         for copy in copies:
             copy.wait()
 
-        def patch(n, s):
+        def patch(s):
             length = length_ref[s]
             first = pl.multiple_of(length % page // tall * tall, tall)
             return pltpu.make_async_copy(
-                patch_ref.at[n, s], pairs[n][1].at[table_ref[s, length // page], pl.ds(first, tall)], patch_sems.at[n, s]
+                patch_ref.at[part, s], out_ref.at[table_ref[s, length // page], pl.ds(first, tall)], patch_sems.at[s]
             )
 
         for act in ("start", "wait"):
-            for n in range(2):
-                for s in range(slots):
-
-                    @pl.when(leaving != s)
-                    def _():
-                        copy = patch(n, s)
-                        copy.start() if act == "start" else copy.wait()
-
-    shape = jax.ShapeDtypeStruct(key_pool.shape, key_pool.dtype)
-    return pl.pallas_call(
-        kernel,
-        out_shape=(shape, shape),
-        in_specs=[SMEM] * 3 + [VMEM] * 3 + [ANY],
-        out_specs=(HBM, HBM),
-        scratch_shapes=[pltpu.SemaphoreType.DMA((2, parts)), pltpu.SemaphoreType.DMA((2, slots))],
-        compiler_params=pltpu.CompilerParams(vmem_limit_bytes=14 * MIB),
-        cost_estimate=cost(0, 4 * key_pool.size),
-        name="write_pools",
-    )(lengths, new_slot, page_table, patches, key_pool, value_pool, after)
+            for s in range(slots):
+
+                @pl.when(leaving != s)
+                def _():
+                    copy = patch(s)
+                    copy.start() if act == "start" else copy.wait()
+
+    return pl.pallas_call(
+        kernel,
+        out_shape=jax.ShapeDtypeStruct(pool.shape, pool.dtype),
+        in_specs=[SMEM] * 3 + [VMEM] * 2 + [ANY],
+        out_specs=HBM,
+        scratch_shapes=[pltpu.SemaphoreType.DMA((parts,)), pltpu.SemaphoreType.DMA((slots,))],
+        compiler_params=pltpu.CompilerParams(vmem_limit_bytes=8 * MIB),
+        cost_estimate=cost(0, 2 * pool.size),
+        name="write_pool",
+    )(lengths, new_slot, page_table, patches, pool, after)
 
 
 def leaving_slot(new_slot_ref, slots, here):
@@ -132,17 +128,21 @@
     slots, model = tokens.shape
     depth = model // groups
     page, width = key_pool.shape[1:]
+    half = page // 2
 
     def kernel(
         token_ref, gain_ref, shift_ref, length_ref, table_ref, slot_ref, page_ref, key_ref, value_ref,
-        keep_ref, send_ref, out_ref, normed, sems,
+        keep_ref, send_ref, keep_half, send_half, normed, sems,
     ):
         here = lax.axis_index("req")
         leaving = leaving_slot(slot_ref, slots, here)
-        copies = [
-            pltpu.make_async_copy(source.at[table_ref[leaving, 0]], out_ref.at[n], sems.at[n])
-            for n, source in enumerate((key_ref, value_ref))
-        ]
+        copies = []
+        for n, source in enumerate((key_ref, value_ref)):
+            for e, target in enumerate((keep_half, send_half)):
+                rows = pl.ds(pl.multiple_of((here % 2 ^ e) * half, half), half)
+                copies.append(
+                    pltpu.make_async_copy(source.at[table_ref[leaving, 0], rows], target.at[n], sems.at[n, e])
+                )
         for copy in copies:
             copy.start()
         values = token_ref[...].astype(F32)
@@ -173,12 +173,13 @@
             copy.wait()
 
     blocks = jax.ShapeDtypeStruct((chips, slots, META + depth), BF16)
-    return pl.pallas_call(
-        kernel,
-        out_shape=(blocks, blocks, jax.ShapeDtypeStruct((2, page, width), key_pool.dtype)),
+    halves = jax.ShapeDtypeStruct((2, half, width), key_pool.dtype)
+    return pl.pallas_call(
+        kernel,
+        out_shape=(blocks, blocks, halves, halves),
         in_specs=[VMEM] * 3 + [SMEM] * 4 + [HBM] * 2,
-        out_specs=(VMEM, VMEM, VMEM),
-        scratch_shapes=[pltpu.VMEM((slots, model), F32), pltpu.SemaphoreType.DMA((2,))],
+        out_specs=(VMEM,) * 4,
+        scratch_shapes=[pltpu.VMEM((slots, model), F32), pltpu.SemaphoreType.DMA((2, 2))],
         compiler_params=pltpu.CompilerParams(vmem_limit_bytes=4 * MIB),
         cost_estimate=cost(0, 8 * page * width),
         name="prepare",
@@ -198,37 +199,91 @@
             told = ref[e, :, :META].astype(F32)
             numbered = jnp.where(lane == 4, float(k), told)
             found = jnp.where(told[:, :1] == goal, numbered, found)
-    pick = lambda j: jnp.sum(jnp.where(lane == j, found, 0.0)).astype(jnp.int32)
-    return pick(4), pick(2), pick(3)
-
-
-def choose_page(spread, candidates):
+    return lambda j: jnp.sum(jnp.where(lane == j, found, 0.0)).astype(jnp.int32)
+
+
+def row_length(chips):
+    return 1 << (chips.bit_length() // 2)
+
+
+def turn_pages(spread, halves):
     chips = len(spread)
+    across = row_length(chips)
+    down = chips // across
+    shape = halves[0].shape
 
     def kernel(*refs):
-        block_refs, candidate_refs = refs[:chips], refs[chips : 2 * chips]
-        out_ref, sem = refs[2 * chips :]
-        source = arrivals(block_refs, lax.axis_index("req"), 1)[0]
-        which = jnp.where(source % 2 == 0, source // 2, 0)
-        for n, candidate in enumerate(candidate_refs):
-
-            @pl.when(which == n)
+        block_refs, half_refs = refs[:chips], refs[chips : chips + across]
+        out_refs, sems = refs[chips + across : -1], refs[-1]
+        here = lax.axis_index("req")
+        waits = []
+        for row in range(1, down):
+            for j in range(2):
+                source = arrivals(block_refs, here, 2 * across * row + j)(4)
+                place = jnp.where(source < 2 * across, source, 0)
+                for d in range(across):
+                    for e in range(2):
+                        copy = pltpu.make_async_copy(half_refs[d].at[e], out_refs[row - 1].at[j], sems.at[row - 1, j])
+
+                        @pl.when(place == 2 * d + e)
+                        def _():
+                            copy.start()
+
+                waits.append(copy)
+        for copy in waits:
+            copy.wait()
+
+    one = jax.ShapeDtypeStruct(shape, halves[0].dtype)
+    return pl.pallas_call(
+        kernel,
+        out_shape=(one,) * (down - 1),
+        in_specs=[VMEM] * chips + [ANY] * across,
+        out_specs=(VMEM,) * (down - 1),
+        scratch_shapes=[pltpu.SemaphoreType.DMA((down - 1, 2))],
+        compiler_params=pltpu.CompilerParams(vmem_limit_bytes=down * 2 * MIB),
+        cost_estimate=cost(0, 4 * halves[0].size),
+        name="turn_pages",
+    )(*spread, *halves)
+
+
+def start_half(source, across, core, half_refs, turned_refs, target, sem):
+    place = jnp.where(source < 2 * across, source, 2 * across + source // (2 * across))
+    for d, ref in enumerate(half_refs):
+        for e in range(2):
+
+            @pl.when(place == 2 * d + e)
             def _():
-                copy = pltpu.make_async_copy(candidate, out_ref, sem)
-                copy.start()
-                copy.wait()
-
-    one = candidates[0]
-    return pl.pallas_call(
-        kernel,
-        out_shape=jax.ShapeDtypeStruct(one.shape, one.dtype),
-        in_specs=[VMEM] * chips + [ANY] * chips,
+                pltpu.make_async_copy(ref.at[e], target, sem).start()
+
+    for row, ref in enumerate(turned_refs):
+
+        @pl.when(place == 2 * across + row + 1)
+        def _():
+            pltpu.make_async_copy(ref.at[core], target, sem).start()
+
+
+def choose_half(spread, halves, turned):
+    chips, across, rows = len(spread), len(halves), len(turned)
+
+    def kernel(*refs):
+        block_refs, half_refs = refs[:chips], refs[chips : chips + across]
+        turned_refs = refs[chips + across : chips + across + rows]
+        out_ref, sem = refs[chips + across + rows :]
+        source = arrivals(block_refs, lax.axis_index("req"), 1)(4)
+        start_half(source, across, 1, half_refs, turned_refs, out_ref, sem)
+        pltpu.make_async_copy(half_refs[0].at[0], out_ref, sem).wait()
+
+    shape = halves[0].shape[1:]
+    return pl.pallas_call(
+        kernel,
+        out_shape=jax.ShapeDtypeStruct(shape, halves[0].dtype),
+        in_specs=[VMEM] * chips + [ANY] * (across + rows),
         out_specs=VMEM,
         scratch_shapes=[pltpu.SemaphoreType.DMA],
         compiler_params=pltpu.CompilerParams(vmem_limit_bytes=2 * MIB),
-        cost_estimate=cost(0, 4 * one.size),
-        name="choose_page",
-    )(*spread, *candidates)
+        cost_estimate=cost(0, 2 * halves[0].size),
+        name="choose_half",
+    )(*spread, *halves, *turned)
 
 
 def project(blocks, weight):
@@ -299,7 +354,7 @@
     )(keep, got)
 
 
-def attend(lengths, new_slot, page_table, sums, bias, tokens, key_pool, value_pool):
+def attend(lengths, new_slot, page_table, sums, bias, tokens, key_pool, value_pool, after):
     parts = len(sums)
     slots = sums[0].shape[0]
     pages, page, width = key_pool.shape
@@ -321,7 +376,7 @@
     def kernel(*refs):
         length_ref, slot_ref, table_ref = refs[:3]
         sum_refs = refs[3 : 3 + parts]
-        (bias_ref, token_ref, key_ref, value_ref, pack_keep, pack_send, patch_ref, score_buffer, mix_buffer) = refs[
+        (bias_ref, token_ref, key_ref, value_ref, _, pack_keep, pack_send, patch_ref, score_buffer, mix_buffer) = refs[
             3 + parts :
         ]
         here = lax.axis_index("req")
@@ -485,13 +540,13 @@
     return pl.pallas_call(
         kernel,
         out_shape=(packed, packed, jax.ShapeDtypeStruct((2, slots, tall, width), BF16)),
-        in_specs=[SMEM] * 3 + [VMEM] * (parts + 4),
+        in_specs=[SMEM] * 3 + [VMEM] * (parts + 4) + [ANY],
         out_specs=(VMEM, VMEM, VMEM),
         scratch_shapes=[pltpu.VMEM((tall, long_rows), F32), pltpu.VMEM((tall, width), F32)],
         compiler_params=pltpu.CompilerParams(vmem_limit_bytes=18 * MIB),
         cost_estimate=cost(4 * tall * (long_rows + short_rows) * width, 4 * (long_rows + short_rows) * width),
         name="attend",
-    )(lengths, new_slot, page_table, *sums, bias, tokens, key_pool, value_pool)
+    )(lengths, new_slot, page_table, *sums, bias, tokens, key_pool, value_pool, after)
 
 
 def pack_rows(slots, strips):
@@ -499,7 +554,7 @@
     return -(-need // 16) * 16
 
 
-def out_project(column_block, blocks, weight, pieces, slots):
+def out_project(column_block, blocks, weight, pieces, slots, *after):
     chips = len(blocks)
     depth, width = weight.shape
     high = -(-slots // 8) * 8
@@ -508,7 +563,8 @@
 
     def kernel(column_ref, *refs):
         block_refs = refs[:chips]
-        weight_ref, keep_ref, send_ref, left = refs[chips:]
+        weight_ref = refs[chips]
+        keep_ref, send_ref, left = refs[chips + 1 + len(after) :]
 
         @pl.when(pl.program_id(0) == 0)
         def _():
@@ -540,20 +596,22 @@
             num_scalar_prefetch=1,
             grid=(pieces,),
             in_specs=[whole(block.shape) for block in blocks]
-            + [pl.BlockSpec((depth, piece), lambda j, c: (0, j ^ c[0]))],
+            + [pl.BlockSpec((depth, piece), lambda j, c: (0, j ^ c[0]))]
+            + [HBM] * min(1, len(after)) + [ANY] * (len(after) - 1),
             out_specs=(out_spec, out_spec),
             scratch_shapes=[pltpu.VMEM((rows, PACK), F32)],
         ),
         compiler_params=pltpu.CompilerParams(vmem_limit_bytes=8 * MIB),
         cost_estimate=cost(2 * rows * weight.size, 2 * weight.size),
         name="out_project",
-    )(column_block, *blocks, weight)
-
-
-def place_page(new_slot, spread, packs, tokens, out_bias, candidates, key_out, value_out):
-    chips = len(spread)
-    count = len(candidates)
+    )(column_block, *blocks, weight, *after)
+
+
+def place_page(new_slot, spread, packs, tokens, out_bias, halves, turned, from_other, key_out, value_out):
+    chips, across, rows = len(spread), len(halves), len(turned)
+    count = across + rows + 1
     page, width = key_out.shape[1:]
+    half = page // 2
     slots = tokens.shape[0]
     high = -(-slots // 8) * 8
     strips = width // PACK
@@ -561,18 +619,20 @@
     def kernel(slot_ref, *refs):
         block_refs, pack_refs = refs[:chips], refs[chips : 2 * chips]
         token_ref, bias_ref = refs[2 * chips : 2 * chips + 2]
-        candidate_refs = refs[2 * chips + 2 : 2 * chips + 2 + count]
-        _, _, base_ref, key_ref, value_ref, buffer, arrived, sem, out_sems = refs[2 * chips + 2 + count :]
+        half_refs = refs[2 * chips + 2 : 2 * chips + 2 + across]
+        turned_refs = refs[2 * chips + 2 + across : 2 * chips + 2 + across + rows]
+        other_ref = refs[2 * chips + 1 + count]
+        _, _, base_ref, key_ref, value_ref, buffer, arrived, sems, out_sems = refs[2 * chips + 2 + count :]
         here = lax.axis_index("req")
         column = pl.multiple_of(lax.axis_index("head") * width, LANES)
-        source, page_at, offset = arrivals(block_refs, here, 0)
-        which = jnp.where(source % 2 == 0, source // 2, chips)
-        for n in range(count):
-
-            @pl.when(which == n)
-            def _():
-                copy = pltpu.make_async_copy(candidate_refs[n], buffer, sem)
-                copy.start()
+        pick = arrivals(block_refs, here, 0)
+        source, page_at, offset = pick(4), pick(2), pick(3)
+        targets = [
+            buffer.at[:, pl.ds(pl.multiple_of((here % 2 ^ e) * half, half), half)] for e in range(2)
+        ]
+        start_half(source, across, 0, half_refs, turned_refs, targets[0], sems.at[0])
+        from_core = pltpu.make_async_copy(other_ref, targets[1], sems.at[1])
+        from_core.start()
 
         for d in range(chips):
             for e in range(2):
@@ -592,7 +652,8 @@
             token_ref[:, pl.ds(column, width)].astype(F32),
         )
         base_ref[...] = token + bias_ref[:, pl.ds(column, width)]
-        pltpu.make_async_copy(candidate_refs[0], buffer, sem).wait()
+        pltpu.make_async_copy(half_refs[0].at[0], targets[0], sems.at[0]).wait()
+        from_core.wait()
         first = pl.multiple_of(offset // 16 * 16, 16)
         row = lax.broadcasted_iota(jnp.int32, (16, width), 0)
         for n in range(2):
@@ -617,14 +678,14 @@
         scratch_shapes=[
             pltpu.VMEM((2, page, width), BF16),
             pltpu.VMEM(packs[0].shape[1:], F32),
-            pltpu.SemaphoreType.DMA,
+            pltpu.SemaphoreType.DMA((2,)),
             pltpu.SemaphoreType.DMA((2,)),
         ],
         input_output_aliases={2 * chips + 3 + count: 1, 2 * chips + 4 + count: 2},
         compiler_params=pltpu.CompilerParams(vmem_limit_bytes=4 * MIB),
         cost_estimate=cost(0, 8 * page * width),
         name="place_page",
-    )(new_slot, *spread, *packs, tokens, out_bias, *candidates, key_out, value_out)
+    )(new_slot, *spread, *packs, tokens, out_bias, *halves, *turned, from_other, key_out, value_out)
 
 
 def body(
@@ -648,15 +709,17 @@
     slots = tokens.shape[0]
     chips = groups // 2
 
-    keep, send, mine = prepare(
+    keep, send, keep_half, send_half = prepare(
         tokens, norm_gain[None], norm_shift[None], lengths, page_table, new_slot, new_page, key_pool, value_pool
     )
     got = swap(send, "req", 1)
-    spread = [jnp.stack([keep[0], got[0]])] + [
-        swap(jnp.stack([keep[d], got[d]]), "req", 2 * d) for d in range(1, chips)
-    ]
+    spread = spread_pairs(keep, got)
     (weight,) = stage([jnp.transpose(qkv_weight, (1, 0, 2))], got, "stage_weight")
-    candidates = [mine] + [swap(mine, "req", 2 * d) for d in range(1, chips)]
+    across = row_length(chips)
+    halves = [jnp.stack([keep_half, swap(send_half, "req", 1)])]
+    halves += [swap(halves[0], "req", 2 * d) for d in range(1, across)]
+    turning = turn_pages(spread, halves)
+    turned = [swap(one, "req", 2 * across * (row + 1)) for row, one in enumerate(turning)]
 
     keep, send = project(spread, weight)
     got = swap(send, "req", 1)
@@ -673,22 +736,26 @@
         tokens,
         keys,
         values,
+        turning[0],
     )
-    packs = spread_pairs(pack_keep, pack_send)
-
-    from_other = swap(choose_page(spread, candidates), "req", 1)
+    packs_got = swap(pack_send, "req", 1)
+    packs = spread_pairs(pack_keep, packs_got)
+
+    from_other = swap(choose_half(spread, halves, turned), "req", 1)
+    key_out = write_pool(lengths, new_slot, page_table, patches, keys, packs_got, 0)
 
     keep, send = out_project(
-        column_block[None], packs, out_weight.reshape(-1, out_weight.shape[2]), head_groups, slots
+        column_block[None], packs, out_weight.reshape(-1, out_weight.shape[2]), head_groups, slots, *in_hbm(key_out), turned[0]
     )
     total = keep + swap(send, "req", 1).astype(F32)
-    key_out, value_out = write_pools(lengths, new_slot, page_table, patches, keys, values, total)
-    base, key_out, value_out = place_page(
-        new_slot, spread, packs, tokens, out_bias[None], candidates + [from_other], key_out, value_out
-    )
+    value_out = write_pool(lengths, new_slot, page_table, patches, values, total, 1)
     summed = total[0]
     for d in range(1, chips):
         summed = summed + swap(total[d].astype(BF16), "req", 2 * d).astype(F32)
+    summed, value_out = lax.optimization_barrier((summed, value_out))
+    base, key_out, value_out = place_page(
+        new_slot, spread, packs, tokens, out_bias[None], halves, turned, from_other, key_out, value_out
+    )
     hidden = summed[0]
     for j in range(1, head_groups):
         hidden = hidden + swap(summed[j].astype(BF16), "head", j).astype(F32)

time: 77.7 us -> 62.6 us (0.81)
  waiting for transfers between devices: 25.9 us -> 7.66 us
  Pallas kernels: 25.6 us -> 28.6 us
    ppermute x23, waiting for transfers between devices: 25.9 us -> 7.66 us  [swap(): return lax.ppermute(value, axis, [(i, i ^ step) for i in range(size)])]
    pallas_call x3 -> x5, Pallas kernels: 7.44 us -> 10.5 us  [the longest x2 6.88 us: write_pool(): pl.pallas_call(kernel, out_shape=jax.ShapeDtypeStruct(pool.shape, pool.dt...]
  transfers between devices with their start and end apart: 23 -> 23, of which waited for: 11 -> 6; matrix products, arithmetic and copies ran while one was open for 1% -> 0% of each run, Pallas kernels for 19% -> 40%
where the time goes in v5:
time: 62.6 us; the launch traced here: 62.4 us
  Pallas kernels  28.6 us (46%)
  starting transfers between devices  23.9 us (38%)
  waiting for transfers between devices  7.66 us (12%)
  between operations  1.07 us (2%)
  other arithmetic  1 us (2%)
    ppermute x23, starting transfers between devices, swap(): return lax.ppermute(value, axis, [(i, i ^ step) for i in range(size)])  23.9 us
    ppermute x23, waiting for transfers between devices, swap(): return lax.ppermute(value, axis, [(i, i ^ step) for i in range(size)])  7.66 us
    pallas_call x2, Pallas kernels, stage(): pl.pallas_call(kernel, out_shape=tuple((jax.ShapeDtypeStruct(array.shape,...  7.52 us
    pallas_call x2, Pallas kernels, write_pool(): pl.pallas_call(kernel, out_shape=jax.ShapeDtypeStruct(pool.shape, pool.dt...  6.88 us
    pallas_call x1, Pallas kernels, attend(): pl.pallas_call(kernel, out_shape=(packed, packed, jax.ShapeDtypeStruct((2...  4.59 us
    pallas_call x1, Pallas kernels, project(): pl.pallas_call(kernel, out_shape=(shape, shape), in_specs=[VMEM] * (chips...  2.25 us
    pallas_call x1, Pallas kernels, prepare(): pl.pallas_call(kernel, out_shape=(blocks, blocks, halves, halves), in_spe...  1.99 us
    pallas_call x1, Pallas kernels, place_page(): pl.pallas_call(kernel, out_shape=(jax.ShapeDtypeStruct((slots, width), F3...  1.97 us
  transfers between devices with their start and end apart: 23, of which 6 were waited for; matrix products, arithmetic and copies ran while one was open for 0% of the time, Pallas kernels for 40%

profile of v5, /device:TPU:0, one launch (start us, length us, event | category | flops | bytes accessed | tf_op | source)
XLA Modules:
  0.0 62.4 jit_solution(13637909047391665775)
XLA Ops:
  0.6 2.0 %prepare.1 = (bf16[4,4,1024]{2,1,0:T(4,128)(2,1)S(1)}, bf16[4,4,1024]{2,1,0:T(4,128)(2,1)S(1)}, bf16[2,32,1792]{2,1,0:T(8,128)(2,1)S(1)}, bf16[2,32,1792]{2,1,0:T(8,128)(2,1)S(1)}) custom-call(bf16[4,7168]{1,0:T(4,128)(2,1)} %refs_8_.3, f32[1,7168]{1,0:T(1,128)} %bitcast.47, f32[1,7168]{1,0:T(1,128)} %bitcast.48, s32[4]{0:T(128)} %length_ref.5, ...), custom_call_target="tpu_custom_call" | custom-call | tf_op jit(solution)/shard_map/prepare/pallas_call | solution.py:177
  2.6 0.5 collective-permute-start
  3.1 0.1 collective-permute-start.8
  3.2 0.8 %collective-permute-done.refs_1_ = bf16[4,4,1024]{2,1,0:T(4,128)(2,1)S(1)} collective-permute-done((bf16[4,4,1024]{2,1,0:T(4,128)(2,1)S(1)}, bf16[4,4,1024]{2,1,0:T(4,128)(2,1)S(1)}, u32[]{:S(2)}, u32[]{:S(2)}) %collective-permute-start) | collective-permute-done | bytes 32800 | tf_op jit(solution)/shard_map/ppermute | solution.py:30
  4.0 2.9 %collective-permute-start.1 = (bf16[2,4,1024]{2,1,0:T(4,128)(2,1)S(1)}, bf16[2,4,1024]{2,1,0:T(4,128)(2,1)S(1)}, u32[]{:S(2)}, u32[]{:S(2)}) collective-permute-start(bf16[2,4,1024]{2,1,0:T(4,128)(2,1)S(1)} %pad_maximum_fusion.6), channel_id=1, source_target_pairs={{0,8},{4,12},{8,0},{12,4},{16,24},{20,28},{24,16},{28,20},{1,9},{5... | collective-permute-start | bytes 49160 | tf_op jit(solution)/shard_map/ppermute | solution.py:30
  7.0 1.6 %collective-permute-start.2 = (bf16[2,4,1024]{2,1,0:T(4,128)(2,1)S(1)}, bf16[2,4,1024]{2,1,0:T(4,128)(2,1)S(1)}, u32[]{:S(2)}, u32[]{:S(2)}) collective-permute-start(bf16[2,4,1024]{2,1,0:T(4,128)(2,1)S(1)} %pad_maximum_fusion.7), channel_id=1, source_target_pairs={{0,16},{4,20},{8,24},{12,28},{16,0},{20,4},{24,8},{28,12},{1,17},{... | collective-permute-start | bytes 49160 | tf_op jit(solution)/shard_map/ppermute | solution.py:30
  8.6 0.1 collective-permute-start.3
  8.7 2.0 %collective-permute-start.9 = (bf16[2,2,32,1792]{3,2,1,0:T(8,128)(2,1)S(1)}, bf16[2,2,32,1792]{3,2,1,0:T(8,128)(2,1)S(1)}, u32[]{:S(2)}, u32[]{:S(2)}) collective-permute-start(bf16[2,2,32,1792]{3,2,1,0:T(8,128)(2,1)S(1)} %pad_maximum_fusion.refs_4_.refs_10_), channel_id=1, source_target_pairs={{0,8},{4,12},{8,0},{12,4},{16,24},{20,28},{24,16},{28,20},{1,9},{5... | collective-permute-start | bytes 1376264 | tf_op jit(solution)/shard_map/ppermute | solution.py:30
  10.7 3.8 %stage_weight.1.refs_4_ = bf16[14,896,384]{2,1,0:T(8,128)(2,1)S(1)} custom-call(bf16[14,896,384]{2,1,0:T(8,128)(2,1)} %bitcast.45, bf16[4,4,1024]{2,1,0:T(4,128)(2,1)S(1)} %collective-permute-done.refs_1_), custom_call_target="tpu_custom_call" | custom-call | tf_op jit(solution)/shard_map/stage_weight/pallas_call | solution.py:62
  14.5 0.0 copy-start.6
  14.6 2.3 %project.1 = (f32[4,4,5376]{2,1,0:T(4,128)S(1)}, f32[4,4,5376]{2,1,0:T(4,128)S(1)}) custom-call(bf16[2,4,1024]{2,1,0:T(4,128)(2,1)S(1)} %pad_maximum_fusion.5.refs_0_, bf16[2,4,1024]{2,1,0:T(4,128)(2,1)S(1)} %collective-permute-done.1.refs_1_, bf16[2,4,1024]{2,1,0:T(4,128)(2,1)S(1)} %collective-permute-done.2.refs_2_, ...), custom_call_target="tpu_custom_call" | custom-call | tf_op jit(solution)/shard_map/project/pallas_call | solution.py:316
  16.8 0.1 collective-permute-start.4
  16.9 1.6 %collective-permute-done.4.got_ref = f32[4,4,5376]{2,1,0:T(4,128)S(1)} collective-permute-done((f32[4,4,5376]{2,1,0:T(4,128)S(1)}, f32[4,4,5376]{2,1,0:T(4,128)S(1)}, u32[]{:S(2)}, u32[]{:S(2)}) %collective-permute-start.4) | collective-permute-done | bytes 344096 | tf_op jit(solution)/shard_map/ppermute | solution.py:30
  18.6 0.1 combine.1
  18.6 0.1 collective-permute-start.5
  18.8 2.0 %collective-permute-start.6 = (bf16[4,7168]{1,0:T(4,128)(2,1)S(1)}, bf16[4,7168]{1,0:T(4,128)(2,1)S(1)}, u32[]{:S(2)}, u32[]{:S(2)}) collective-permute-start(bf16[4,7168]{1,0:T(4,128)(2,1)S(1)} %get-tuple-element.31), channel_id=1, source_target_pairs={{0,16},{4,20},{8,24},{12,28},{16,0},{20,4},{24,8},{28,12},{1,17},{... | collective-permute-start | bytes 172040 | tf_op jit(solution)/shard_map/ppermute | solution.py:30
  20.8 1.4 %collective-permute-start.7 = (bf16[4,7168]{1,0:T(4,128)(2,1)S(1)}, bf16[4,7168]{1,0:T(4,128)(2,1)S(1)}, u32[]{:S(2)}, u32[]{:S(2)}) collective-permute-start(bf16[4,7168]{1,0:T(4,128)(2,1)S(1)} %get-tuple-element.32), channel_id=1, source_target_pairs={{0,24},{4,28},{8,16},{12,20},{16,8},{20,12},{24,0},{28,4},{1,25},{... | collective-permute-start | bytes 172040 | tf_op jit(solution)/shard_map/ppermute | solution.py:30
  22.2 0.0 copy-start.1
  22.2 0.0 copy-start.2
  22.3 3.7 %stage_pools.1 = (bf16[20,64,1792]{2,1,0:T(8,128)(2,1)S(1)}, bf16[20,64,1792]{2,1,0:T(8,128)(2,1)S(1)}) custom-call(bf16[20,64,1792]{2,1,0:T(8,128)(2,1)} %refs_0_.2, bf16[20,64,1792]{2,1,0:T(8,128)(2,1)} %refs_1_.2, f32[4,5376]{1,0:T(4,128)S(1)} %get-tuple-element.29.refs_2_.refs_3_), custom_call_target="tpu_custom_call" | custom-call | tf_op jit(solution)/shard_map/stage_pools/pallas_call | solution.py:62
  26.0 1.1 %turn_pages.1.refs_11_ = bf16[2,2,32,1792]{3,2,1,0:T(8,128)(2,1)S(1)} custom-call(bf16[2,4,1024]{2,1,0:T(4,128)(2,1)S(1)} %pad_maximum_fusion.5.refs_0_, bf16[2,4,1024]{2,1,0:T(4,128)(2,1)S(1)} %collective-permute-done.1.refs_1_, bf16[2,4,1024]{2,1,0:T(4,128)(2,1)S(1)} %collective-permute-done.2.refs_2_, ...), custom_call_target="tpu_custom_call" | custom-call | tf_op jit(solution)/shard_map/turn_pages/pallas_call | solution.py:237
  27.1 1.6 %collective-permute-start.14 = (bf16[2,2,32,1792]{3,2,1,0:T(8,128)(2,1)S(1)}, bf16[2,2,32,1792]{3,2,1,0:T(8,128)(2,1)S(1)}, u32[]{:S(2)}, u32[]{:S(2)}) collective-permute-start(bf16[2,2,32,1792]{3,2,1,0:T(8,128)(2,1)S(1)} %turn_pages.1.refs_11_), channel_id=1, source_target_pairs={{0,16},{4,20},{8,24},{12,28},{16,0},{20,4},{24,8},{28,12},{1,17},{... | collective-permute-start | bytes 1376264 | tf_op jit(solution)/shard_map/ppermute | solution.py:30
  28.7 4.6 %attend.1 = (bf16[4,32,256]{2,1,0:T(8,128)(2,1)S(1)}, bf16[4,32,256]{2,1,0:T(8,128)(2,1)S(1)}, bf16[2,4,16,1792]{3,2,1,0:T(8,128)(2,1)S(1)}) custom-call(s32[4]{0:T(128)S(1)} %copy-done.5, s32[4]{0:T(128)S(1)} %copy-done.4, s32[4,16]{1,0:T(4,128)S(1)} %copy-done.2, f32[4,5376]{1,0:T(4,128)S(1)} %get-tuple-element.29.refs_2_.refs_3_, ...), custom_call_target="tpu_custom_call" | custom-call | tf_op jit(solution)/shard_map/attend/pallas_call | solution.py:540
  33.3 0.1 collective-permute-start.10
  33.4 1.2 %collective-permute-done.10._ = bf16[4,32,256]{2,1,0:T(8,128)(2,1)S(1)} collective-permute-done((bf16[4,32,256]{2,1,0:T(8,128)(2,1)S(1)}, bf16[4,32,256]{2,1,0:T(8,128)(2,1)S(1)}, u32[]{:S(2)}, u32[]{:S(2)}) %collective-permute-start.10) | collective-permute-done | bytes 65568 | tf_op jit(solution)/shard_map/ppermute | solution.py:30
  34.6 0.1 collective-permute-start.11
  34.7 0.1 collective-permute-start.12
  34.8 3.4 %collective-permute-start.13 = (bf16[2,32,256]{2,1,0:T(8,128)(2,1)S(1)}, bf16[2,32,256]{2,1,0:T(8,128)(2,1)S(1)}, u32[]{:S(2)}, u32[]{:S(2)}) collective-permute-start(bf16[2,32,256]{2,1,0:T(8,128)(2,1)S(1)} %pad_maximum_fusion.4), channel_id=1, source_target_pairs={{0,24},{4,28},{8,16},{12,20},{16,8},{20,12},{24,0},{28,4},{1,25},{... | collective-permute-start | bytes 98312 | tf_op jit(solution)/shard_map/ppermute | solution.py:30
  38.2 3.4 %write_pool.2.refs_5_.refs_14_ = bf16[20,64,1792]{2,1,0:T(8,128)(2,1)} custom-call(s32[4]{0:T(128)S(1)} %copy-done.5, s32[4]{0:T(128)S(1)} %copy-done.4, s32[4,16]{1,0:T(4,128)S(1)} %copy-done.2, bf16[2,4,16,1792]{3,2,1,0:T(8,128)(2,1)S(1)} %get-tuple-element.39.patch_ref, bf16[20,64,1792]{2,1,0:T(8,128)(2,1)S(1)} %get-tuple-element.33.refs_9_.pool_ref, ...), custom_call_target="tpu_custom_call" | custom-call | tf_op jit(solution)/shard_map/write_pool/pallas_call | solution.py:106
  41.7 1.8 %out_project.1 = (f32[4,4,4,1792]{3,2,1,0:T(4,128)S(1)}, bf16[4,4,4,1792]{3,2,1,0:T(4,128)(2,1)S(1)}) custom-call(s32[1]{0:T(128)} %bitcast.column_ref, bf16[2,32,256]{2,1,0:T(8,128)(2,1)S(1)} %pad_maximum_fusion.1.refs_0_.refs_4_, bf16[2,32,256]{2,1,0:T(8,128)(2,1)S(1)} %collective-permute-done.11.refs_1_.refs_5_, ...), custom_call_target="tpu_custom_call" | custom-call | tf_op jit(solution)/shard_map/out_project/pallas_call | solution.py:592
  43.5 0.1 collective-permute-start.15
  43.6 1.5 %collective-permute-done.15 = bf16[4,4,4,1792]{3,2,1,0:T(4,128)(2,1)S(1)} collective-permute-done((bf16[4,4,4,1792]{3,2,1,0:T(4,128)(2,1)S(1)}, bf16[4,4,4,1792]{3,2,1,0:T(4,128)(2,1)S(1)}, u32[]{:S(2)}, u32[]{:S(2)}) %collective-permute-start.15) | collective-permute-done | bytes 229408 | tf_op jit(solution)/shard_map/ppermute | solution.py:30
  45.0 0.2 fusion.7
  45.2 0.1 slice_bitcast_fusion.3
  45.3 0.2 collective-permute-start.16
  45.4 1.5 %collective-permute-start.18 = (bf16[4,4,1792]{2,1,0:T(4,128)(2,1)S(1)}, bf16[4,4,1792]{2,1,0:T(4,128)(2,1)S(1)}, u32[]{:S(2)}, u32[]{:S(2)}) collective-permute-start(bf16[4,4,1792]{2,1,0:T(4,128)(2,1)S(1)} %get-tuple-element.50), channel_id=1, source_target_pairs={{0,24},{4,28},{8,16},{12,20},{16,8},{20,12},{24,0},{28,4},{1,25},{... | collective-permute-start | bytes 172040 | tf_op jit(solution)/shard_map/ppermute | solution.py:30
  46.9 1.9 %collective-permute-start.17 = (bf16[4,4,1792]{2,1,0:T(4,128)(2,1)S(1)}, bf16[4,4,1792]{2,1,0:T(4,128)(2,1)S(1)}, u32[]{:S(2)}, u32[]{:S(2)}) collective-permute-start(bf16[4,4,1792]{2,1,0:T(4,128)(2,1)S(1)} %get-tuple-element.51), channel_id=1, source_target_pairs={{0,16},{4,20},{8,24},{12,28},{16,0},{20,4},{24,8},{28,12},{1,17},{... | collective-permute-start | bytes 172040 | tf_op jit(solution)/shard_map/ppermute | solution.py:30
  48.8 0.5 choose_half.1
  49.4 0.1 collective-permute-start.22
  49.5 3.4 %write_pool.3.refs_15_ = bf16[20,64,1792]{2,1,0:T(8,128)(2,1)} custom-call(s32[4]{0:T(128)S(1)} %copy-done.5, s32[4]{0:T(128)S(1)} %copy-done.4, s32[4,16]{1,0:T(4,128)S(1)} %copy-done.2, bf16[2,4,16,1792]{3,2,1,0:T(8,128)(2,1)S(1)} %get-tuple-element.39.patch_ref, bf16[20,64,1792]{2,1,0:T(8,128)(2,1)S(1)} %get-tuple-element.34.refs_10_.pool_ref, ...), custom_call_target="tpu_custom_call" | custom-call | tf_op jit(solution)/shard_map/write_pool/pallas_call | solution.py:106
  53.0 0.1 fusion.2
  53.1 1.6 %collective-permute-start.19 = (bf16[4,1792]{1,0:T(4,128)(2,1)S(1)}, bf16[4,1792]{1,0:T(4,128)(2,1)S(1)}, u32[]{:S(2)}, u32[]{:S(2)}) collective-permute-start(bf16[4,1792]{1,0:T(4,128)(2,1)S(1)} %get-tuple-element.60), channel_id=1, source_target_pairs={{0,1},{1,0},{2,3},{3,2},{4,5},{5,4},{6,7},{7,6},{8,9},{9,8},{10,11... | collective-permute-start | bytes 43016 | tf_op jit(solution)/shard_map/ppermute | solution.py:30
  54.7 2.5 %collective-permute-start.21 = (bf16[4,1792]{1,0:T(4,128)(2,1)S(1)}, bf16[4,1792]{1,0:T(4,128)(2,1)S(1)}, u32[]{:S(2)}, u32[]{:S(2)}) collective-permute-start(bf16[4,1792]{1,0:T(4,128)(2,1)S(1)} %get-tuple-element.61), channel_id=1, source_target_pairs={{0,3},{1,2},{2,1},{3,0},{4,7},{5,6},{6,5},{7,4},{8,11},{9,10},{10,... | collective-permute-start | bytes 43016 | tf_op jit(solution)/shard_map/ppermute | solution.py:30
  57.2 0.1 collective-permute-start.20
  57.3 2.0 %place_page.1 = (f32[4,1792]{1,0:T(4,128)S(1)}, bf16[20,64,1792]{2,1,0:T(8,128)(2,1)}, bf16[20,64,1792]{2,1,0:T(8,128)(2,1)}) custom-call(s32[4]{0:T(128)S(1)} %copy-done.4, bf16[2,4,1024]{2,1,0:T(4,128)(2,1)S(1)} %pad_maximum_fusion.5.refs_0_, ...), custom_call_target="tpu_custom_call", output_to_operand_aliasing={{1}: (15, {}), {2}: (16, {})} | custom-call | tf_op jit(solution)/shard_map/place_page/pallas_call | solution.py:673
  59.3 0.9 %collective-permute-done.21 = bf16[4,1792]{1,0:T(4,128)(2,1)S(1)} collective-permute-done((bf16[4,1792]{1,0:T(4,128)(2,1)S(1)}, bf16[4,1792]{1,0:T(4,128)(2,1)S(1)}, u32[]{:S(2)}, u32[]{:S(2)}) %collective-permute-start.21) | collective-permute-done | bytes 14368 | tf_op jit(solution)/shard_map/ppermute | solution.py:30
  60.2 1.6 %collective-permute-done.20 = bf16[4,1792]{1,0:T(4,128)(2,1)S(1)} collective-permute-done((bf16[4,1792]{1,0:T(4,128)(2,1)S(1)}, bf16[4,1792]{1,0:T(4,128)(2,1)S(1)}, u32[]{:S(2)}, u32[]{:S(2)}) %collective-permute-start.20) | collective-permute-done | bytes 14368 | tf_op jit(solution)/shard_map/ppermute | solution.py:30
  61.8 0.6 fusion.6
  (44 shorter events, 0.3 us)
Async XLA Ops:
  2.6 1.4 %collective-permute-start = (bf16[4,4,1024]{2,1,0:T(4,128)(2,1)S(1)}, bf16[4,4,1024]{2,1,0:T(4,128)(2,1)S(1)}, u32[]{:S(2)}, u32[]{:S(2)}) collective-permute-start(bf16[4,4,1024]{2,1,0:T(4,128)(2,1)S(1)} %get-tuple-element.26), channel_id=1, source_target_pairs={{0,4},{4,0},{8,12},{12,8},{16,20},{20,16},{24,28},{28,24},{1,5},{5... | collective-permute-start | bytes 98312 | tf_op jit(solution)/shard_map/ppermute | solution.py:30
  3.1 5.5 %collective-permute-start.8 = (bf16[2,32,1792]{2,1,0:T(8,128)(2,1)S(1)}, bf16[2,32,1792]{2,1,0:T(8,128)(2,1)S(1)}, u32[]{:S(2)}, u32[]{:S(2)}) collective-permute-start(bf16[2,32,1792]{2,1,0:T(8,128)(2,1)S(1)} %get-tuple-element.36), channel_id=1, source_target_pairs={{0,4},{4,0},{8,12},{12,8},{16,20},{20,16},{24,28},{28,24},{1,5},{5... | collective-permute-start | bytes 688136 | tf_op jit(solution)/shard_map/ppermute | solution.py:30
  4.0 10.5 %collective-permute-start.1 = (bf16[2,4,1024]{2,1,0:T(4,128)(2,1)S(1)}, bf16[2,4,1024]{2,1,0:T(4,128)(2,1)S(1)}, u32[]{:S(2)}, u32[]{:S(2)}) collective-permute-start(bf16[2,4,1024]{2,1,0:T(4,128)(2,1)S(1)} %pad_maximum_fusion.6), channel_id=1, source_target_pairs={{0,8},{4,12},{8,0},{12,4},{16,24},{20,28},{24,16},{28,20},{1,9},{5... | collective-permute-start | bytes 49160 | tf_op jit(solution)/shard_map/ppermute | solution.py:30
  7.0 7.6 %collective-permute-start.2 = (bf16[2,4,1024]{2,1,0:T(4,128)(2,1)S(1)}, bf16[2,4,1024]{2,1,0:T(4,128)(2,1)S(1)}, u32[]{:S(2)}, u32[]{:S(2)}) collective-permute-start(bf16[2,4,1024]{2,1,0:T(4,128)(2,1)S(1)} %pad_maximum_fusion.7), channel_id=1, source_target_pairs={{0,16},{4,20},{8,24},{12,28},{16,0},{20,4},{24,8},{28,12},{1,17},{... | collective-permute-start | bytes 49160 | tf_op jit(solution)/shard_map/ppermute | solution.py:30
  8.6 6.0 %collective-permute-start.3 = (bf16[2,4,1024]{2,1,0:T(4,128)(2,1)S(1)}, bf16[2,4,1024]{2,1,0:T(4,128)(2,1)S(1)}, u32[]{:S(2)}, u32[]{:S(2)}) collective-permute-start(bf16[2,4,1024]{2,1,0:T(4,128)(2,1)S(1)} %pad_maximum_fusion.8), channel_id=1, source_target_pairs={{0,24},{4,28},{8,16},{12,20},{16,8},{20,12},{24,0},{28,4},{1,25},{... | collective-permute-start | bytes 49160 | tf_op jit(solution)/shard_map/ppermute | solution.py:30
  8.7 17.3 %collective-permute-start.9 = (bf16[2,2,32,1792]{3,2,1,0:T(8,128)(2,1)S(1)}, bf16[2,2,32,1792]{3,2,1,0:T(8,128)(2,1)S(1)}, u32[]{:S(2)}, u32[]{:S(2)}) collective-permute-start(bf16[2,2,32,1792]{3,2,1,0:T(8,128)(2,1)S(1)} %pad_maximum_fusion.refs_4_.refs_10_), channel_id=1, source_target_pairs={{0,8},{4,12},{8,0},{12,4},{16,24},{20,28},{24,16},{28,20},{1,9},{5... | collective-permute-start | bytes 1376264 | tf_op jit(solution)/shard_map/ppermute | solution.py:30
  14.5 7.6 %copy-start.6 = (f32[14,384]{1,0:T(8,128)S(1)}, f32[14,384]{1,0:T(8,128)}, u32[]{:S(2)}) copy-start(f32[14,384]{1,0:T(8,128)} %param.17) | copy-start | bytes 64516
  16.8 1.7 %collective-permute-start.4 = (f32[4,4,5376]{2,1,0:T(4,128)S(1)}, f32[4,4,5376]{2,1,0:T(4,128)S(1)}, u32[]{:S(2)}, u32[]{:S(2)}) collective-permute-start(f32[4,4,5376]{2,1,0:T(4,128)S(1)} %get-tuple-element.28), channel_id=1, source_target_pairs={{0,4},{4,0},{8,12},{12,8},{16,20},{20,16},{24,28},{28,24},{1,5},{5... | collective-permute-start | bytes 1032200 | tf_op jit(solution)/shard_map/ppermute | solution.py:30
  18.6 10.0 %collective-permute-start.5 = (bf16[4,7168]{1,0:T(4,128)(2,1)S(1)}, bf16[4,7168]{1,0:T(4,128)(2,1)S(1)}, u32[]{:S(2)}, u32[]{:S(2)}) collective-permute-start(bf16[4,7168]{1,0:T(4,128)(2,1)S(1)} %get-tuple-element.30), channel_id=1, source_target_pairs={{0,8},{4,12},{8,0},{12,4},{16,24},{20,28},{24,16},{28,20},{1,9},{5... | collective-permute-start | bytes 172040 | tf_op jit(solution)/shard_map/ppermute | solution.py:30
  18.8 9.9 %collective-permute-start.6 = (bf16[4,7168]{1,0:T(4,128)(2,1)S(1)}, bf16[4,7168]{1,0:T(4,128)(2,1)S(1)}, u32[]{:S(2)}, u32[]{:S(2)}) collective-permute-start(bf16[4,7168]{1,0:T(4,128)(2,1)S(1)} %get-tuple-element.31), channel_id=1, source_target_pairs={{0,16},{4,20},{8,24},{12,28},{16,0},{20,4},{24,8},{28,12},{1,17},{... | collective-permute-start | bytes 172040 | tf_op jit(solution)/shard_map/ppermute | solution.py:30
  20.8 7.9 %collective-permute-start.7 = (bf16[4,7168]{1,0:T(4,128)(2,1)S(1)}, bf16[4,7168]{1,0:T(4,128)(2,1)S(1)}, u32[]{:S(2)}, u32[]{:S(2)}) collective-permute-start(bf16[4,7168]{1,0:T(4,128)(2,1)S(1)} %get-tuple-element.32), channel_id=1, source_target_pairs={{0,24},{4,28},{8,16},{12,20},{16,8},{20,12},{24,0},{28,4},{1,25},{... | collective-permute-start | bytes 172040 | tf_op jit(solution)/shard_map/ppermute | solution.py:30
  22.2 6.5 %copy-start.1 = (bf16[4,7168]{1,0:T(4,128)(2,1)S(1)}, bf16[4,7168]{1,0:T(4,128)(2,1)}, u32[]{:S(2)}) copy-start(bf16[4,7168]{1,0:T(4,128)(2,1)} %refs_8_.3) | copy-start | bytes 172036
  22.2 6.5 %copy-start.2 = (s32[4,16]{1,0:T(4,128)S(1)}, s32[4,16]{1,0:T(4,128)}, u32[]{:S(2)}) copy-start(s32[4,16]{1,0:T(4,128)} %table_ref.5) | copy-start | bytes 772
  22.2 6.5 %copy-start.4 = (s32[4]{0:T(128)S(1)}, s32[4]{0:T(128)}, u32[]{:S(2)}) copy-start(s32[4]{0:T(128)} %slot_ref.7) | copy-start | bytes 52
  22.2 6.4 %copy-start.5 = (s32[4]{0:T(128)S(1)}, s32[4]{0:T(128)}, u32[]{:S(2)}) copy-start(s32[4]{0:T(128)} %length_ref.5) | copy-start | bytes 52
  27.1 14.6 %collective-permute-start.14 = (bf16[2,2,32,1792]{3,2,1,0:T(8,128)(2,1)S(1)}, bf16[2,2,32,1792]{3,2,1,0:T(8,128)(2,1)S(1)}, u32[]{:S(2)}, u32[]{:S(2)}) collective-permute-start(bf16[2,2,32,1792]{3,2,1,0:T(8,128)(2,1)S(1)} %turn_pages.1.refs_11_), channel_id=1, source_target_pairs={{0,16},{4,20},{8,24},{12,28},{16,0},{20,4},{24,8},{28,12},{1,17},{... | collective-permute-start | bytes 1376264 | tf_op jit(solution)/shard_map/ppermute | solution.py:30
  33.3 1.3 %collective-permute-start.10 = (bf16[4,32,256]{2,1,0:T(8,128)(2,1)S(1)}, bf16[4,32,256]{2,1,0:T(8,128)(2,1)S(1)}, u32[]{:S(2)}, u32[]{:S(2)}) collective-permute-start(bf16[4,32,256]{2,1,0:T(8,128)(2,1)S(1)} %get-tuple-element.38), channel_id=1, source_target_pairs={{0,4},{4,0},{8,12},{12,8},{16,20},{20,16},{24,28},{28,24},{1,5},{5... | collective-permute-start | bytes 196616 | tf_op jit(solution)/shard_map/ppermute | solution.py:30
  34.6 7.0 %collective-permute-start.11 = (bf16[2,32,256]{2,1,0:T(8,128)(2,1)S(1)}, bf16[2,32,256]{2,1,0:T(8,128)(2,1)S(1)}, u32[]{:S(2)}, u32[]{:S(2)}) collective-permute-start(bf16[2,32,256]{2,1,0:T(8,128)(2,1)S(1)} %pad_maximum_fusion.2), channel_id=1, source_target_pairs={{0,8},{4,12},{8,0},{12,4},{16,24},{20,28},{24,16},{28,20},{1,9},{5... | collective-permute-start | bytes 98312 | tf_op jit(solution)/shard_map/ppermute | solution.py:30
  34.7 6.9 %collective-permute-start.12 = (bf16[2,32,256]{2,1,0:T(8,128)(2,1)S(1)}, bf16[2,32,256]{2,1,0:T(8,128)(2,1)S(1)}, u32[]{:S(2)}, u32[]{:S(2)}) collective-permute-start(bf16[2,32,256]{2,1,0:T(8,128)(2,1)S(1)} %pad_maximum_fusion.3), channel_id=1, source_target_pairs={{0,16},{4,20},{8,24},{12,28},{16,0},{20,4},{24,8},{28,12},{1,17},{... | collective-permute-start | bytes 98312 | tf_op jit(solution)/shard_map/ppermute | solution.py:30
  34.8 6.9 %collective-permute-start.13 = (bf16[2,32,256]{2,1,0:T(8,128)(2,1)S(1)}, bf16[2,32,256]{2,1,0:T(8,128)(2,1)S(1)}, u32[]{:S(2)}, u32[]{:S(2)}) collective-permute-start(bf16[2,32,256]{2,1,0:T(8,128)(2,1)S(1)} %pad_maximum_fusion.4), channel_id=1, source_target_pairs={{0,24},{4,28},{8,16},{12,20},{16,8},{20,12},{24,0},{28,4},{1,25},{... | collective-permute-start | bytes 98312 | tf_op jit(solution)/shard_map/ppermute | solution.py:30
  38.2 3.5 %copy-start = (bf16[14,16,7168]{2,1,0:T(8,128)(2,1)S(1)}, bf16[14,16,7168]{2,1,0:T(8,128)(2,1)}, u32[]{:S(2)}) copy-start(bf16[14,16,7168]{2,1,0:T(8,128)(2,1)} %param.18) | copy-start | bytes 9633796
  43.5 1.6 %collective-permute-start.15 = (bf16[4,4,4,1792]{3,2,1,0:T(4,128)(2,1)S(1)}, bf16[4,4,4,1792]{3,2,1,0:T(4,128)(2,1)S(1)}, u32[]{:S(2)}, u32[]{:S(2)}) collective-permute-start(bf16[4,4,4,1792]{3,2,1,0:T(4,128)(2,1)S(1)} %get-tuple-element.41), channel_id=1, source_target_pairs={{0,4},{4,0},{8,12},{12,8},{16,20},{20,16},{24,28},{28,24},{1,5},{5... | collective-permute-start | bytes 688136 | tf_op jit(solution)/shard_map/ppermute | solution.py:30
  45.3 7.6 %collective-permute-start.16 = (bf16[4,4,1792]{2,1,0:T(4,128)(2,1)S(1)}, bf16[4,4,1792]{2,1,0:T(4,128)(2,1)S(1)}, u32[]{:S(2)}, u32[]{:S(2)}) collective-permute-start(bf16[4,4,1792]{2,1,0:T(4,128)(2,1)S(1)} %get-tuple-element.49), channel_id=1, source_target_pairs={{0,8},{4,12},{8,0},{12,4},{16,24},{20,28},{24,16},{28,20},{1,9},{5... | collective-permute-start | bytes 172040 | tf_op jit(solution)/shard_map/ppermute | solution.py:30
  45.4 7.5 %collective-permute-start.18 = (bf16[4,4,1792]{2,1,0:T(4,128)(2,1)S(1)}, bf16[4,4,1792]{2,1,0:T(4,128)(2,1)S(1)}, u32[]{:S(2)}, u32[]{:S(2)}) collective-permute-start(bf16[4,4,1792]{2,1,0:T(4,128)(2,1)S(1)} %get-tuple-element.50), channel_id=1, source_target_pairs={{0,24},{4,28},{8,16},{12,20},{16,8},{20,12},{24,0},{28,4},{1,25},{... | collective-permute-start | bytes 172040 | tf_op jit(solution)/shard_map/ppermute | solution.py:30
  46.9 6.0 %collective-permute-start.17 = (bf16[4,4,1792]{2,1,0:T(4,128)(2,1)S(1)}, bf16[4,4,1792]{2,1,0:T(4,128)(2,1)S(1)}, u32[]{:S(2)}, u32[]{:S(2)}) collective-permute-start(bf16[4,4,1792]{2,1,0:T(4,128)(2,1)S(1)} %get-tuple-element.51), channel_id=1, source_target_pairs={{0,16},{4,20},{8,24},{12,28},{16,0},{20,4},{24,8},{28,12},{1,17},{... | collective-permute-start | bytes 172040 | tf_op jit(solution)/shard_map/ppermute | solution.py:30
  49.4 7.9 %collective-permute-start.22 = (bf16[2,32,1792]{2,1,0:T(8,128)(2,1)S(1)}, bf16[2,32,1792]{2,1,0:T(8,128)(2,1)S(1)}, u32[]{:S(2)}, u32[]{:S(2)}) collective-permute-start(bf16[2,32,1792]{2,1,0:T(8,128)(2,1)S(1)} %choose_half.1), channel_id=1, source_target_pairs={{0,4},{4,0},{8,12},{12,8},{16,20},{20,16},{24,28},{28,24},{1,5},{5... | collective-permute-start | bytes 688136 | tf_op jit(solution)/shard_map/ppermute | solution.py:30
  49.5 7.9 %copy-start.3 = (f32[7168]{0:T(1024)S(1)}, f32[7168]{0:T(1024)}, u32[]{:S(2)}) copy-start(f32[7168]{0:T(1024)} %param.19) | copy-start | bytes 86020
  53.1 6.2 %collective-permute-start.19 = (bf16[4,1792]{1,0:T(4,128)(2,1)S(1)}, bf16[4,1792]{1,0:T(4,128)(2,1)S(1)}, u32[]{:S(2)}, u32[]{:S(2)}) collective-permute-start(bf16[4,1792]{1,0:T(4,128)(2,1)S(1)} %get-tuple-element.60), channel_id=1, source_target_pairs={{0,1},{1,0},{2,3},{3,2},{4,5},{5,4},{6,7},{7,6},{8,9},{9,8},{10,11... | collective-permute-start | bytes 43016 | tf_op jit(solution)/shard_map/ppermute | solution.py:30
  54.7 5.5 %collective-permute-start.21 = (bf16[4,1792]{1,0:T(4,128)(2,1)S(1)}, bf16[4,1792]{1,0:T(4,128)(2,1)S(1)}, u32[]{:S(2)}, u32[]{:S(2)}) collective-permute-start(bf16[4,1792]{1,0:T(4,128)(2,1)S(1)} %get-tuple-element.61), channel_id=1, source_target_pairs={{0,3},{1,2},{2,1},{3,0},{4,7},{5,6},{6,5},{7,4},{8,11},{9,10},{10,... | collective-permute-start | bytes 43016 | tf_op jit(solution)/shard_map/ppermute | solution.py:30
  57.2 4.6 %collective-permute-start.20 = (bf16[4,1792]{1,0:T(4,128)(2,1)S(1)}, bf16[4,1792]{1,0:T(4,128)(2,1)S(1)}, u32[]{:S(2)}, u32[]{:S(2)}) collective-permute-start(bf16[4,1792]{1,0:T(4,128)(2,1)S(1)} %get-tuple-element.62), channel_id=1, source_target_pairs={{0,2},{1,3},{2,0},{3,1},{4,6},{5,7},{6,4},{7,5},{8,10},{9,11},{10,... | collective-permute-start | bytes 43016 | tf_op jit(solution)/shard_map/ppermute | solution.py:30

commit v6 on v5

--- a/solution.py
+++ b/solution.py
@@ -41,44 +41,11 @@
     return [pltpu.with_memory_space_constraint(array, pltpu.HBM) for array in arrays]
 
 
-def stage(arrays, after, name):
-    count = len(arrays)
+def write_pool(pool, after):
     parts = 4
-
-    def kernel(*refs):
-        sources, targets, sems = refs[:count], refs[count + 1 : 2 * count + 1], refs[-1]
-        copies = []
-        for n in range(count):
-            step = -(-arrays[n].shape[0] // parts)
-            for i, first in enumerate(range(0, arrays[n].shape[0], step)):
-                place = pl.ds(first, min(step, arrays[n].shape[0] - first))
-                copies.append(pltpu.make_async_copy(sources[n].at[place], targets[n].at[place], sems.at[n, i]))
-        for copy in copies:
-            copy.start()
-        for copy in copies:
-            copy.wait()
-
-    size = sum(array.size * 2 for array in arrays)
-    return pl.pallas_call(
-        kernel,
-        out_shape=tuple(jax.ShapeDtypeStruct(array.shape, array.dtype) for array in arrays),
-        in_specs=[HBM] * count + [ANY],
-        out_specs=(VMEM,) * count,
-        scratch_shapes=[pltpu.SemaphoreType.DMA((count, parts))],
-        compiler_params=pltpu.CompilerParams(vmem_limit_bytes=size + 2 * MIB),
-        cost_estimate=cost(0, size),
-        name=name,
-    )(*in_hbm(*arrays), after)
-
-
-def write_pool(lengths, new_slot, page_table, patches, pool, after, part):
-    pages, page, width = pool.shape
-    slots, tall = patches.shape[1:3]
-    parts = 4
-    step = pages // parts
-
-    def kernel(length_ref, slot_ref, table_ref, patch_ref, pool_ref, _, out_ref, sems, patch_sems):
-        leaving = leaving_slot(slot_ref, slots, lax.axis_index("req"))
+    step = pool.shape[0] // parts
+
+    def kernel(pool_ref, _, out_ref, sems):
         places = [pl.ds(i * step, step) for i in range(parts)]
         copies = [
             pltpu.make_async_copy(pool_ref.at[place], out_ref.at[place], sems.at[i]) for i, place in enumerate(places)
@@ -88,31 +55,16 @@
         for copy in copies:
             copy.wait()
 
-        def patch(s):
-            length = length_ref[s]
-            first = pl.multiple_of(length % page // tall * tall, tall)
-            return pltpu.make_async_copy(
-                patch_ref.at[part, s], out_ref.at[table_ref[s, length // page], pl.ds(first, tall)], patch_sems.at[s]
-            )
-
-        for act in ("start", "wait"):
-            for s in range(slots):
-
-                @pl.when(leaving != s)
-                def _():
-                    copy = patch(s)
-                    copy.start() if act == "start" else copy.wait()
-
     return pl.pallas_call(
         kernel,
         out_shape=jax.ShapeDtypeStruct(pool.shape, pool.dtype),
-        in_specs=[SMEM] * 3 + [VMEM] * 2 + [ANY],
+        in_specs=[VMEM, ANY],
         out_specs=HBM,
-        scratch_shapes=[pltpu.SemaphoreType.DMA((parts,)), pltpu.SemaphoreType.DMA((slots,))],
+        scratch_shapes=[pltpu.SemaphoreType.DMA((parts,))],
         compiler_params=pltpu.CompilerParams(vmem_limit_bytes=8 * MIB),
         cost_estimate=cost(0, 2 * pool.size),
         name="write_pool",
-    )(lengths, new_slot, page_table, patches, pool, after)
+    )(pool, after)
 
 
 def leaving_slot(new_slot_ref, slots, here):
@@ -554,60 +506,51 @@
     return -(-need // 16) * 16
 
 
-def out_project(column_block, blocks, weight, pieces, slots, *after):
+def out_project(blocks, weight, pieces, slots, *after):
     chips = len(blocks)
     depth, width = weight.shape
     high = -(-slots // 8) * 8
     rows = 2 * chips * slots
     piece = width // pieces
 
-    def kernel(column_ref, *refs):
-        block_refs = refs[:chips]
-        weight_ref = refs[chips]
-        keep_ref, send_ref, left = refs[chips + 1 + len(after) :]
-
-        @pl.when(pl.program_id(0) == 0)
-        def _():
-            gathered = jnp.concatenate(
-                [block_refs[d][e, :high, :].astype(F32) for d in range(chips) for e in range(2)], axis=0
+    def kernel(*refs):
+        block_refs, weight_ref = refs[:chips], refs[chips]
+        keep_ref, send_ref = refs[chips + 1 + len(after) :]
+        gathered = jnp.concatenate(
+            [block_refs[d][e, :high, :].astype(F32) for d in range(chips) for e in range(2)], axis=0
+        )
+        goal = gathered[:, PACK - 2 : PACK - 1].astype(jnp.int32)
+        place = goal ^ lax.axis_index("req")
+        row = (place % 2) * (chips * slots) + (place // 2) * slots + gathered[:, PACK - 1 :].astype(jnp.int32)
+        row = jnp.where(goal < 0, -1, row)
+        size = (gathered.shape[0], rows)
+        order = jnp.where(lax.broadcasted_iota(jnp.int32, size, 1) == row, 1.0, 0.0)
+        left = lax.dot_general(
+            order.astype(BF16), gathered.astype(BF16), (((0,), (0,)), ((), ())), preferred_element_type=F32
+        )
+        left = left[:, :depth].astype(BF16)
+        for j in range(pieces):
+            first = (lax.axis_index("head") ^ j) * piece
+            total = jnp.dot(
+                left, weight_ref[:, pl.ds(pl.multiple_of(first, LANES), piece)], preferred_element_type=F32
             )
-            goal = gathered[:, PACK - 2 : PACK - 1].astype(jnp.int32)
-            place = goal ^ lax.axis_index("req")
-            row = (place % 2) * (chips * slots) + (place // 2) * slots + gathered[:, PACK - 1 :].astype(jnp.int32)
-            row = jnp.where(goal < 0, -1, row)
-            size = (gathered.shape[0], rows)
-            order = jnp.where(lax.broadcasted_iota(jnp.int32, size, 1) == row, 1.0, 0.0)
-            left[...] = lax.dot_general(
-                order.astype(BF16), gathered.astype(BF16), (((0,), (0,)), ((), ())), preferred_element_type=F32
-            )
-
-        total = jnp.dot(left[:, :depth].astype(BF16), weight_ref[...], preferred_element_type=F32)
-        for d in range(chips):
-            keep_ref[d, 0] = total[d * slots : (d + 1) * slots]
-            send_ref[d, 0] = total[(chips + d) * slots : (chips + d + 1) * slots].astype(BF16)
+            for d in range(chips):
+                keep_ref[d, j] = total[d * slots : (d + 1) * slots]
+                send_ref[d, j] = total[(chips + d) * slots : (chips + d + 1) * slots].astype(BF16)
 
     shape = (chips, pieces, slots, piece)
-    out_spec = pl.BlockSpec((chips, 1, slots, piece), lambda j, c: (0, j, 0, 0))
-    whole = lambda shape: pl.BlockSpec(shape, lambda j, c: (0,) * len(shape))
     return pl.pallas_call(
         kernel,
         out_shape=(jax.ShapeDtypeStruct(shape, F32), jax.ShapeDtypeStruct(shape, BF16)),
-        grid_spec=pltpu.PrefetchScalarGridSpec(
-            num_scalar_prefetch=1,
-            grid=(pieces,),
-            in_specs=[whole(block.shape) for block in blocks]
-            + [pl.BlockSpec((depth, piece), lambda j, c: (0, j ^ c[0]))]
-            + [HBM] * min(1, len(after)) + [ANY] * (len(after) - 1),
-            out_specs=(out_spec, out_spec),
-            scratch_shapes=[pltpu.VMEM((rows, PACK), F32)],
-        ),
-        compiler_params=pltpu.CompilerParams(vmem_limit_bytes=8 * MIB),
+        in_specs=[VMEM] * (chips + 1) + [HBM] * min(1, len(after)) + [ANY] * (len(after) - 1),
+        out_specs=(VMEM, VMEM),
+        compiler_params=pltpu.CompilerParams(vmem_limit_bytes=10 * MIB),
         cost_estimate=cost(2 * rows * weight.size, 2 * weight.size),
         name="out_project",
-    )(column_block, *blocks, weight, *after)
-
-
-def place_page(new_slot, spread, packs, tokens, out_bias, halves, turned, from_other, key_out, value_out):
+    )(*blocks, weight, *after)
+
+
+def place_page(lengths, new_slot, page_table, patches, spread, packs, tokens, out_bias, halves, turned, from_other, key_out, value_out):
     chips, across, rows = len(spread), len(halves), len(turned)
     count = across + rows + 1
     page, width = key_out.shape[1:]
@@ -616,14 +559,31 @@
     high = -(-slots // 8) * 8
     strips = width // PACK
 
-    def kernel(slot_ref, *refs):
+    tall = patches.shape[2]
+
+    def kernel(length_ref, slot_ref, table_ref, patch_ref, *refs):
         block_refs, pack_refs = refs[:chips], refs[chips : 2 * chips]
         token_ref, bias_ref = refs[2 * chips : 2 * chips + 2]
         half_refs = refs[2 * chips + 2 : 2 * chips + 2 + across]
         turned_refs = refs[2 * chips + 2 + across : 2 * chips + 2 + across + rows]
         other_ref = refs[2 * chips + 1 + count]
-        _, _, base_ref, key_ref, value_ref, buffer, arrived, sems, out_sems = refs[2 * chips + 2 + count :]
+        _, _, base_ref, key_ref, value_ref, buffer, arrived, sems, out_sems, patch_sems = refs[2 * chips + 2 + count :]
         here = lax.axis_index("req")
+        leaving = leaving_slot(slot_ref, slots, here)
+
+        def patch(n, s):
+            length = length_ref[s]
+            first = pl.multiple_of(length % page // tall * tall, tall)
+            target = (key_ref, value_ref)[n].at[table_ref[s, length // page], pl.ds(first, tall)]
+            return pltpu.make_async_copy(patch_ref.at[n, s], target, patch_sems.at[n, s])
+
+        for n in range(2):
+            for s in range(slots):
+
+                @pl.when(leaving != s)
+                def _():
+                    patch(n, s).start()
+
         column = pl.multiple_of(lax.axis_index("head") * width, LANES)
         pick = arrivals(block_refs, here, 0)
         source, page_at, offset = pick(4), pick(2), pick(3)
@@ -647,7 +607,7 @@
 
         at = lax.broadcasted_iota(jnp.int32, (slots, width), 0)
         token = jnp.where(
-            at == leaving_slot(slot_ref, slots, here),
+            at == leaving,
             jnp.broadcast_to(fresh(2), (slots, width)),
             token_ref[:, pl.ds(column, width)].astype(F32),
         )
@@ -666,6 +626,13 @@
         ]
         for copy in copies:
             copy.start()
+        for n in range(2):
+            for s in range(slots):
+
+                @pl.when(leaving != s)
+                def _():
+                    patch(n, s).wait()
+
         for copy in copies:
             copy.wait()
 
@@ -673,19 +640,22 @@
     return pl.pallas_call(
         kernel,
         out_shape=(jax.ShapeDtypeStruct((slots, width), F32), shape, shape),
-        in_specs=[SMEM] + [VMEM] * (2 * chips + 2) + [ANY] * count + [HBM] * 2,
+        in_specs=[SMEM] * 3 + [VMEM] * (2 * chips + 3) + [ANY] * count + [HBM] * 2,
         out_specs=(VMEM, HBM, HBM),
         scratch_shapes=[
             pltpu.VMEM((2, page, width), BF16),
             pltpu.VMEM(packs[0].shape[1:], F32),
             pltpu.SemaphoreType.DMA((2,)),
             pltpu.SemaphoreType.DMA((2,)),
+            pltpu.SemaphoreType.DMA((2, slots)),
         ],
-        input_output_aliases={2 * chips + 3 + count: 1, 2 * chips + 4 + count: 2},
+        input_output_aliases={2 * chips + 6 + count: 1, 2 * chips + 7 + count: 2},
         compiler_params=pltpu.CompilerParams(vmem_limit_bytes=4 * MIB),
         cost_estimate=cost(0, 8 * page * width),
         name="place_page",
-    )(new_slot, *spread, *packs, tokens, out_bias, *halves, *turned, from_other, key_out, value_out)
+    )(
+        lengths, new_slot, page_table, patches, *spread, *packs, tokens, out_bias, *halves, *turned, from_other, key_out, value_out
+    )
 
 
 def body(
@@ -705,7 +675,6 @@
 ):
     groups = lax.axis_size("req")
     head_groups = lax.axis_size("head")
-    column_block = lax.axis_index("head")
     slots = tokens.shape[0]
     chips = groups // 2
 
@@ -714,18 +683,16 @@
     )
     got = swap(send, "req", 1)
     spread = spread_pairs(keep, got)
-    (weight,) = stage([jnp.transpose(qkv_weight, (1, 0, 2))], got, "stage_weight")
     across = row_length(chips)
     halves = [jnp.stack([keep_half, swap(send_half, "req", 1)])]
     halves += [swap(halves[0], "req", 2 * d) for d in range(1, across)]
     turning = turn_pages(spread, halves)
     turned = [swap(one, "req", 2 * across * (row + 1)) for row, one in enumerate(turning)]
 
-    keep, send = project(spread, weight)
+    keep, send = project(spread, jnp.transpose(qkv_weight, (1, 0, 2)))
     got = swap(send, "req", 1)
     own, *messages = combine(keep, got)
     sums = [own] + [swap(messages[d - 1], "req", 2 * d) for d in range(1, chips)]
-    keys, values = stage([key_pool, value_pool], own, "stage_pools")
 
     pack_keep, pack_send, patches = attend(
         lengths,
@@ -734,27 +701,39 @@
         sums,
         qkv_bias.reshape(1, -1),
         tokens,
-        keys,
-        values,
+        key_pool,
+        value_pool,
         turning[0],
     )
     packs_got = swap(pack_send, "req", 1)
     packs = spread_pairs(pack_keep, packs_got)
 
     from_other = swap(choose_half(spread, halves, turned), "req", 1)
-    key_out = write_pool(lengths, new_slot, page_table, patches, keys, packs_got, 0)
+    key_out = write_pool(key_pool, packs_got)
 
     keep, send = out_project(
-        column_block[None], packs, out_weight.reshape(-1, out_weight.shape[2]), head_groups, slots, *in_hbm(key_out), turned[0]
+        packs, out_weight.reshape(-1, out_weight.shape[2]), head_groups, slots, *in_hbm(key_out), turned[0]
     )
     total = keep + swap(send, "req", 1).astype(F32)
-    value_out = write_pool(lengths, new_slot, page_table, patches, values, total, 1)
+    value_out = write_pool(value_pool, total)
     summed = total[0]
     for d in range(1, chips):
         summed = summed + swap(total[d].astype(BF16), "req", 2 * d).astype(F32)
     summed, value_out = lax.optimization_barrier((summed, value_out))
     base, key_out, value_out = place_page(
-        new_slot, spread, packs, tokens, out_bias[None], halves, turned, from_other, key_out, value_out
+        lengths,
+        new_slot,
+        page_table,
+        patches,
+        spread,
+        packs,
+        tokens,
+        out_bias[None],
+        halves,
+        turned,
+        from_other,
+        key_out,
+        value_out,
     )
     hidden = summed[0]
     for j in range(1, head_groups):

time: 62.6 us -> 58.3 us (0.931)
  Pallas kernels: 28.6 us -> 15.9 us
  waiting for transfers between devices: 7.66 us -> 12.9 us
  starting transfers between devices: 23.9 us -> 26.9 us
    pallas_call x2 -> x0, Pallas kernels: 7.52 us -> none  [stage(): pl.pallas_call(kernel, out_shape=tuple((jax.ShapeDtypeStruct(array.shape,...]
    ppermute x23, waiting for transfers between devices: 7.66 us -> 12.9 us  [swap(): return lax.ppermute(value, axis, [(i, i ^ step) for i in range(size)])]
    ppermute x23, starting transfers between devices: 23.9 us -> 26.9 us  [swap(): return lax.ppermute(value, axis, [(i, i ^ step) for i in range(size)])]
    pallas_call x1, Pallas kernels: 4.59 us -> 1.96 us  [attend(): pl.pallas_call(kernel, out_shape=(packed, packed, jax.ShapeDtypeStruct((2...]
    pallas_call x2, Pallas kernels: 6.88 us -> 4.54 us  [write_pool(): pl.pallas_call(kernel, out_shape=jax.ShapeDtypeStruct(pool.shape, pool.dt...]
    pallas_call x1, Pallas kernels: 1.78 us -> 0.96 us  [out_project(): pl.pallas_call(kernel, out_shape=(jax.ShapeDtypeStruct(shape, F32), jax.S...]
  transfers between devices with their start and end apart: 23 -> 23, of which waited for: 6 -> 12; matrix products, arithmetic and copies ran while one was open for 0% -> 1% of each run, Pallas kernels for 40% -> 22%
where the time goes in v6:
time: 58.3 us; the launch traced here: 58.1 us
  starting transfers between devices  26.9 us (46%)
  Pallas kernels  15.9 us (27%)
  waiting for transfers between devices  12.9 us (22%)
  other arithmetic  1.01 us (2%)
  between operations  1.01 us (2%)
    ppermute x23, starting transfers between devices, swap(): return lax.ppermute(value, axis, [(i, i ^ step) for i in range(size)])  26.9 us
    ppermute x23, waiting for transfers between devices, swap(): return lax.ppermute(value, axis, [(i, i ^ step) for i in range(size)])  12.9 us
    pallas_call x2, Pallas kernels, write_pool(): pl.pallas_call(kernel, out_shape=jax.ShapeDtypeStruct(pool.shape, pool.dt...  4.54 us
    pallas_call x1, Pallas kernels, prepare(): pl.pallas_call(kernel, out_shape=(blocks, blocks, halves, halves), in_spe...  2.33 us
    pallas_call x1, Pallas kernels, project(): pl.pallas_call(kernel, out_shape=(shape, shape), in_specs=[VMEM] * (chips...  2.25 us
    pallas_call x1, Pallas kernels, place_page(): pl.pallas_call(kernel, out_shape=(jax.ShapeDtypeStruct((slots, width), F3...  2.2 us
    pallas_call x1, Pallas kernels, attend(): pl.pallas_call(kernel, out_shape=(packed, packed, jax.ShapeDtypeStruct((2...  1.96 us
  transfers between devices with their start and end apart: 23, of which 12 were waited for; matrix products, arithmetic and copies ran while one was open for 1% of the time, Pallas kernels for 22%

profile of v6, /device:TPU:0, one launch (start us, length us, event | category | flops | bytes accessed | tf_op | source)
XLA Modules:
  0.0 58.1 jit_solution(3950273374150933177)
XLA Ops:
  0.6 2.3 %prepare.1 = (bf16[4,4,1024]{2,1,0:T(4,128)(2,1)S(1)}, bf16[4,4,1024]{2,1,0:T(4,128)(2,1)S(1)}, bf16[2,32,1792]{2,1,0:T(8,128)(2,1)S(1)}, bf16[2,32,1792]{2,1,0:T(8,128)(2,1)S(1)}) custom-call(bf16[4,7168]{1,0:T(4,128)(2,1)} %refs_8_.3, f32[1,7168]{1,0:T(1,128)} %bitcast.48, f32[1,7168]{1,0:T(1,128)} %bitcast.49, s32[4]{0:T(128)} %length_ref.3, ...), custom_call_target="tpu_custom_call" | custom-call | tf_op jit(solution)/shard_map/prepare/pallas_call | solution.py:129
  3.0 0.5 collective-permute-start
  3.5 0.1 collective-permute-start.8
  3.6 0.8 %collective-permute-done = bf16[4,4,1024]{2,1,0:T(4,128)(2,1)S(1)} collective-permute-done((bf16[4,4,1024]{2,1,0:T(4,128)(2,1)S(1)}, bf16[4,4,1024]{2,1,0:T(4,128)(2,1)S(1)}, u32[]{:S(2)}, u32[]{:S(2)}) %collective-permute-start) | collective-permute-done | bytes 32800 | tf_op jit(solution)/shard_map/ppermute | solution.py:30
  4.4 2.9 %collective-permute-start.1 = (bf16[2,4,1024]{2,1,0:T(4,128)(2,1)S(1)}, bf16[2,4,1024]{2,1,0:T(4,128)(2,1)S(1)}, u32[]{:S(2)}, u32[]{:S(2)}) collective-permute-start(bf16[2,4,1024]{2,1,0:T(4,128)(2,1)S(1)} %pad_maximum_fusion.6), channel_id=1, source_target_pairs={{0,8},{4,12},{8,0},{12,4},{16,24},{20,28},{24,16},{28,20},{1,9},{5... | collective-permute-start | bytes 49160 | tf_op jit(solution)/shard_map/ppermute | solution.py:30
  7.3 1.6 %collective-permute-start.2 = (bf16[2,4,1024]{2,1,0:T(4,128)(2,1)S(1)}, bf16[2,4,1024]{2,1,0:T(4,128)(2,1)S(1)}, u32[]{:S(2)}, u32[]{:S(2)}) collective-permute-start(bf16[2,4,1024]{2,1,0:T(4,128)(2,1)S(1)} %pad_maximum_fusion.7), channel_id=1, source_target_pairs={{0,16},{4,20},{8,24},{12,28},{16,0},{20,4},{24,8},{28,12},{1,17},{... | collective-permute-start | bytes 49160 | tf_op jit(solution)/shard_map/ppermute | solution.py:30
  8.9 0.1 collective-permute-start.3
  9.1 2.0 %collective-permute-start.9 = (bf16[2,2,32,1792]{3,2,1,0:T(8,128)(2,1)S(1)}, bf16[2,2,32,1792]{3,2,1,0:T(8,128)(2,1)S(1)}, u32[]{:S(2)}, u32[]{:S(2)}) collective-permute-start(bf16[2,2,32,1792]{3,2,1,0:T(8,128)(2,1)S(1)} %pad_maximum_fusion.refs_4_.refs_10_), channel_id=1, source_target_pairs={{0,8},{4,12},{8,0},{12,4},{16,24},{20,28},{24,16},{28,20},{1,9},{5... | collective-permute-start | bytes 1376264 | tf_op jit(solution)/shard_map/ppermute | solution.py:30
  11.1 2.7 %collective-permute-done.3.refs_3_ = bf16[2,4,1024]{2,1,0:T(4,128)(2,1)S(1)} collective-permute-done((bf16[2,4,1024]{2,1,0:T(4,128)(2,1)S(1)}, bf16[2,4,1024]{2,1,0:T(4,128)(2,1)S(1)}, u32[]{:S(2)}, u32[]{:S(2)}) %collective-permute-start.3) | collective-permute-done | bytes 16416 | tf_op jit(solution)/shard_map/ppermute | solution.py:30
  13.9 2.3 %project.1 = (f32[4,4,5376]{2,1,0:T(4,128)S(1)}, f32[4,4,5376]{2,1,0:T(4,128)S(1)}) custom-call(bf16[2,4,1024]{2,1,0:T(4,128)(2,1)S(1)} %pad_maximum_fusion.5.refs_0_, bf16[2,4,1024]{2,1,0:T(4,128)(2,1)S(1)} %collective-permute-done.1.refs_1_, bf16[2,4,1024]{2,1,0:T(4,128)(2,1)S(1)} %collective-permute-done.2.refs_2_, ...), custom_call_target="tpu_custom_call" | custom-call | tf_op jit(solution)/shard_map/project/pallas_call | solution.py:268
  16.1 0.1 collective-permute-start.4
  16.2 1.6 %collective-permute-done.4.got_ref = f32[4,4,5376]{2,1,0:T(4,128)S(1)} collective-permute-done((f32[4,4,5376]{2,1,0:T(4,128)S(1)}, f32[4,4,5376]{2,1,0:T(4,128)S(1)}, u32[]{:S(2)}, u32[]{:S(2)}) %collective-permute-start.4) | collective-permute-done | bytes 344096 | tf_op jit(solution)/shard_map/ppermute | solution.py:30
  17.8 0.1 combine.1
  17.9 0.6 %collective-permute-start.5 = (bf16[4,7168]{1,0:T(4,128)(2,1)S(1)}, bf16[4,7168]{1,0:T(4,128)(2,1)S(1)}, u32[]{:S(2)}, u32[]{:S(2)}) collective-permute-start(bf16[4,7168]{1,0:T(4,128)(2,1)S(1)} %get-tuple-element.28), channel_id=1, source_target_pairs={{0,8},{4,12},{8,0},{12,4},{16,24},{20,28},{24,16},{28,20},{1,9},{5... | collective-permute-start | bytes 172040 | tf_op jit(solution)/shard_map/ppermute | solution.py:30
  18.5 0.1 collective-permute-start.6
  18.6 2.9 %collective-permute-start.7 = (bf16[4,7168]{1,0:T(4,128)(2,1)S(1)}, bf16[4,7168]{1,0:T(4,128)(2,1)S(1)}, u32[]{:S(2)}, u32[]{:S(2)}) collective-permute-start(bf16[4,7168]{1,0:T(4,128)(2,1)S(1)} %get-tuple-element.30), channel_id=1, source_target_pairs={{0,24},{4,28},{8,16},{12,20},{16,8},{20,12},{24,0},{28,4},{1,25},{... | collective-permute-start | bytes 172040 | tf_op jit(solution)/shard_map/ppermute | solution.py:30
  21.5 0.4 collective-permute-done.9.refs_5_.refs_11_
  21.9 1.0 %turn_pages.1.refs_11_ = bf16[2,2,32,1792]{3,2,1,0:T(8,128)(2,1)S(1)} custom-call(bf16[2,4,1024]{2,1,0:T(4,128)(2,1)S(1)} %pad_maximum_fusion.5.refs_0_, bf16[2,4,1024]{2,1,0:T(4,128)(2,1)S(1)} %collective-permute-done.1.refs_1_, bf16[2,4,1024]{2,1,0:T(4,128)(2,1)S(1)} %collective-permute-done.2.refs_2_, ...), custom_call_target="tpu_custom_call" | custom-call | tf_op jit(solution)/shard_map/turn_pages/pallas_call | solution.py:189
  22.9 2.4 %collective-permute-start.14 = (bf16[2,2,32,1792]{3,2,1,0:T(8,128)(2,1)S(1)}, bf16[2,2,32,1792]{3,2,1,0:T(8,128)(2,1)S(1)}, u32[]{:S(2)}, u32[]{:S(2)}) collective-permute-start(bf16[2,2,32,1792]{3,2,1,0:T(8,128)(2,1)S(1)} %turn_pages.1.refs_11_), channel_id=1, source_target_pairs={{0,16},{4,20},{8,24},{12,28},{16,0},{20,4},{24,8},{28,12},{1,17},{... | collective-permute-start | bytes 1376264 | tf_op jit(solution)/shard_map/ppermute | solution.py:30
  25.5 2.0 %attend.1 = (bf16[4,32,256]{2,1,0:T(8,128)(2,1)S(1)}, bf16[4,32,256]{2,1,0:T(8,128)(2,1)S(1)}, bf16[2,4,16,1792]{3,2,1,0:T(8,128)(2,1)S(1)}) custom-call(s32[4]{0:T(128)S(1)} %copy-done.6, s32[4]{0:T(128)S(1)} %copy-done.7, s32[4,16]{1,0:T(4,128)S(1)} %copy-done.5, f32[4,5376]{1,0:T(4,128)S(1)} %get-tuple-element.27.refs_3_, ...), custom_call_target="tpu_custom_call" | custom-call | tf_op jit(solution)/shard_map/attend/pallas_call | solution.py:492
  27.4 0.1 collective-permute-start.10
  27.5 1.2 %collective-permute-done.10._ = bf16[4,32,256]{2,1,0:T(8,128)(2,1)S(1)} collective-permute-done((bf16[4,32,256]{2,1,0:T(8,128)(2,1)S(1)}, bf16[4,32,256]{2,1,0:T(8,128)(2,1)S(1)}, u32[]{:S(2)}, u32[]{:S(2)}) %collective-permute-start.10) | collective-permute-done | bytes 65568 | tf_op jit(solution)/shard_map/ppermute | solution.py:30
  28.8 4.2 %collective-permute-start.11 = (bf16[2,32,256]{2,1,0:T(8,128)(2,1)S(1)}, bf16[2,32,256]{2,1,0:T(8,128)(2,1)S(1)}, u32[]{:S(2)}, u32[]{:S(2)}) collective-permute-start(bf16[2,32,256]{2,1,0:T(8,128)(2,1)S(1)} %pad_maximum_fusion.2), channel_id=1, source_target_pairs={{0,8},{4,12},{8,0},{12,4},{16,24},{20,28},{24,16},{28,20},{1,9},{5... | collective-permute-start | bytes 98312 | tf_op jit(solution)/shard_map/ppermute | solution.py:30
  33.0 1.5 %collective-permute-start.13 = (bf16[2,32,256]{2,1,0:T(8,128)(2,1)S(1)}, bf16[2,32,256]{2,1,0:T(8,128)(2,1)S(1)}, u32[]{:S(2)}, u32[]{:S(2)}) collective-permute-start(bf16[2,32,256]{2,1,0:T(8,128)(2,1)S(1)} %pad_maximum_fusion.4), channel_id=1, source_target_pairs={{0,24},{4,28},{8,16},{12,20},{16,8},{20,12},{24,0},{28,4},{1,25},{... | collective-permute-start | bytes 98312 | tf_op jit(solution)/shard_map/ppermute | solution.py:30
  34.5 2.4 %write_pool.2.refs_5_.refs_14_ = bf16[20,64,1792]{2,1,0:T(8,128)(2,1)} custom-call(bf16[20,64,1792]{2,1,0:T(8,128)(2,1)S(1)} %bitcast.41, bf16[4,32,256]{2,1,0:T(8,128)(2,1)S(1)} %collective-permute-done.10._), custom_call_target="tpu_custom_call" | custom-call | tf_op jit(solution)/shard_map/write_pool/pallas_call | solution.py:58
  36.9 0.2 collective-permute-done.12.refs_2_.refs_6_
  37.1 0.7 %collective-permute-done.13.refs_3_.refs_7_ = bf16[2,32,256]{2,1,0:T(8,128)(2,1)S(1)} collective-permute-done((bf16[2,32,256]{2,1,0:T(8,128)(2,1)S(1)}, bf16[2,32,256]{2,1,0:T(8,128)(2,1)S(1)}, u32[]{:S(2)}, u32[]{:S(2)}) %collective-permute-start.13) | collective-permute-done | bytes 32800 | tf_op jit(solution)/shard_map/ppermute | solution.py:30
  37.9 0.2 copy-done.2
  38.1 1.0 %out_project.1 = (f32[4,4,4,1792]{3,2,1,0:T(4,128)S(1)}, bf16[4,4,4,1792]{3,2,1,0:T(4,128)(2,1)S(1)}) custom-call(bf16[2,32,256]{2,1,0:T(8,128)(2,1)S(1)} %pad_maximum_fusion.1.refs_0_.refs_4_, bf16[2,32,256]{2,1,0:T(8,128)(2,1)S(1)} %collective-permute-done.11.refs_1_.refs_5_, bf16[2,32,256]{2,1,0:T(8,128)(2,1)S(1)} %collective-permute-done.12.refs_2_.refs_6_, ...), custom_call_target="tpu_custom_call" | custom-call | tf_op jit(solution)/shard_map/out_project/pallas_call | solution.py:542
  39.1 0.1 collective-permute-start.15
  39.1 1.5 %collective-permute-done.15 = bf16[4,4,4,1792]{3,2,1,0:T(4,128)(2,1)S(1)} collective-permute-done((bf16[4,4,4,1792]{3,2,1,0:T(4,128)(2,1)S(1)}, bf16[4,4,4,1792]{3,2,1,0:T(4,128)(2,1)S(1)}, u32[]{:S(2)}, u32[]{:S(2)}) %collective-permute-start.15) | collective-permute-done | bytes 229408 | tf_op jit(solution)/shard_map/ppermute | solution.py:30
  40.6 0.2 fusion.7
  40.8 0.1 slice_bitcast_fusion.3
  40.8 2.0 %collective-permute-start.16 = (bf16[4,4,1792]{2,1,0:T(4,128)(2,1)S(1)}, bf16[4,4,1792]{2,1,0:T(4,128)(2,1)S(1)}, u32[]{:S(2)}, u32[]{:S(2)}) collective-permute-start(bf16[4,4,1792]{2,1,0:T(4,128)(2,1)S(1)} %get-tuple-element.45), channel_id=1, source_target_pairs={{0,8},{4,12},{8,0},{12,4},{16,24},{20,28},{24,16},{28,20},{1,9},{5... | collective-permute-start | bytes 172040 | tf_op jit(solution)/shard_map/ppermute | solution.py:30
  42.8 1.3 %collective-permute-start.18 = (bf16[4,4,1792]{2,1,0:T(4,128)(2,1)S(1)}, bf16[4,4,1792]{2,1,0:T(4,128)(2,1)S(1)}, u32[]{:S(2)}, u32[]{:S(2)}) collective-permute-start(bf16[4,4,1792]{2,1,0:T(4,128)(2,1)S(1)} %get-tuple-element.46), channel_id=1, source_target_pairs={{0,24},{4,28},{8,16},{12,20},{16,8},{20,12},{24,0},{28,4},{1,25},{... | collective-permute-start | bytes 172040 | tf_op jit(solution)/shard_map/ppermute | solution.py:30
  44.1 0.3 collective-permute-start.17
  44.4 0.5 choose_half.1
  44.9 0.1 collective-permute-start.22
  45.0 2.2 %write_pool.3.refs_15_ = bf16[20,64,1792]{2,1,0:T(8,128)(2,1)} custom-call(bf16[20,64,1792]{2,1,0:T(8,128)(2,1)S(1)} %copy-done, f32[4,4,4,1792]{3,2,1,0:T(4,128)S(1)} %get-tuple-element.44._), custom_call_target="tpu_custom_call" | custom-call | tf_op jit(solution)/shard_map/write_pool/pallas_call | solution.py:58
  47.2 0.8 %collective-permute-done.18 = bf16[4,4,1792]{2,1,0:T(4,128)(2,1)S(1)} collective-permute-done((bf16[4,4,1792]{2,1,0:T(4,128)(2,1)S(1)}, bf16[4,4,1792]{2,1,0:T(4,128)(2,1)S(1)}, u32[]{:S(2)}, u32[]{:S(2)}) %collective-permute-start.18) | collective-permute-done | bytes 57376 | tf_op jit(solution)/shard_map/ppermute | solution.py:30
  48.0 0.7 %collective-permute-done.17 = bf16[4,4,1792]{2,1,0:T(4,128)(2,1)S(1)} collective-permute-done((bf16[4,4,1792]{2,1,0:T(4,128)(2,1)S(1)}, bf16[4,4,1792]{2,1,0:T(4,128)(2,1)S(1)}, u32[]{:S(2)}, u32[]{:S(2)}) %collective-permute-start.17) | collective-permute-done | bytes 57376 | tf_op jit(solution)/shard_map/ppermute | solution.py:30
  48.8 1.6 %collective-permute-start.19 = (bf16[4,1792]{1,0:T(4,128)(2,1)S(1)}, bf16[4,1792]{1,0:T(4,128)(2,1)S(1)}, u32[]{:S(2)}, u32[]{:S(2)}) collective-permute-start(bf16[4,1792]{1,0:T(4,128)(2,1)S(1)} %get-tuple-element.56), channel_id=1, source_target_pairs={{0,1},{1,0},{2,3},{3,2},{4,5},{5,4},{6,7},{7,6},{8,9},{9,8},{10,11... | collective-permute-start | bytes 43016 | tf_op jit(solution)/shard_map/ppermute | solution.py:30
  50.4 2.5 %collective-permute-start.21 = (bf16[4,1792]{1,0:T(4,128)(2,1)S(1)}, bf16[4,1792]{1,0:T(4,128)(2,1)S(1)}, u32[]{:S(2)}, u32[]{:S(2)}) collective-permute-start(bf16[4,1792]{1,0:T(4,128)(2,1)S(1)} %get-tuple-element.57), channel_id=1, source_target_pairs={{0,3},{1,2},{2,1},{3,0},{4,7},{5,6},{6,5},{7,4},{8,11},{9,10},{10,... | collective-permute-start | bytes 43016 | tf_op jit(solution)/shard_map/ppermute | solution.py:30
  52.9 0.1 collective-permute-start.20
  53.0 2.2 %place_page.1 = (f32[4,1792]{1,0:T(4,128)S(1)}, bf16[20,64,1792]{2,1,0:T(8,128)(2,1)}, bf16[20,64,1792]{2,1,0:T(8,128)(2,1)}) custom-call(s32[4]{0:T(128)S(1)} %copy-done.6, s32[4]{0:T(128)S(1)} %copy-done.7, s32[4,16]{1,0:T(4,128)S(1)} %copy-done.5, ...), custom_call_target="tpu_custom_call", output_to_operand_aliasing={{1}: (18, {}), {2}: (19, {})} | custom-call | tf_op jit(solution)/shard_map/place_page/pallas_call | solution.py:640
  55.2 0.7 %collective-permute-done.21 = bf16[4,1792]{1,0:T(4,128)(2,1)S(1)} collective-permute-done((bf16[4,1792]{1,0:T(4,128)(2,1)S(1)}, bf16[4,1792]{1,0:T(4,128)(2,1)S(1)}, u32[]{:S(2)}, u32[]{:S(2)}) %collective-permute-start.21) | collective-permute-done | bytes 14368 | tf_op jit(solution)/shard_map/ppermute | solution.py:30
  55.9 1.6 %collective-permute-done.20 = bf16[4,1792]{1,0:T(4,128)(2,1)S(1)} collective-permute-done((bf16[4,1792]{1,0:T(4,128)(2,1)S(1)}, bf16[4,1792]{1,0:T(4,128)(2,1)S(1)}, u32[]{:S(2)}, u32[]{:S(2)}) %collective-permute-start.20) | collective-permute-done | bytes 14368 | tf_op jit(solution)/shard_map/ppermute | solution.py:30
  57.5 0.6 %fusion.6 = bf16[4,1792]{1,0:T(4,128)(2,1)} fusion(f32[4,1792]{1,0:T(4,128)S(1)} %get-tuple-element.40, bf16[4,1792]{1,0:T(4,128)(2,1)S(1)} %collective-permute-done.21, bf16[4,1792]{1,0:T(4,128)(2,1)S(1)} %collective-permute-done.20, bf16[4,1792]{1,0:T(4,128)(2,1)S(1)} %collective-permute-done.19, f32[4,4,1792]{2,1,0:T(4,128)S(1)} %fusion.2), kind=kLoop, calls=%fused_computation.17 | loop fusion | flops 57344 | bytes 114688 | tf_op jit(solution)/shard_map/convert_element_type | solution.py:741
  (51 shorter events, 0.4 us)
Async XLA Ops:
  0.6 13.2 %copy-start.1 = (bf16[896,14,384]{2,0,1:T(8,128)(2,1)S(1)}, bf16[896,14,384]{2,0,1:T(8,128)(2,1)}, u32[]{:S(2)}) copy-start(bf16[896,14,384]{2,0,1:T(8,128)(2,1)} %param.16) | copy-start | bytes 28901380
  3.0 1.4 %collective-permute-start = (bf16[4,4,1024]{2,1,0:T(4,128)(2,1)S(1)}, bf16[4,4,1024]{2,1,0:T(4,128)(2,1)S(1)}, u32[]{:S(2)}, u32[]{:S(2)}) collective-permute-start(bf16[4,4,1024]{2,1,0:T(4,128)(2,1)S(1)} %get-tuple-element.24), channel_id=1, source_target_pairs={{0,4},{4,0},{8,12},{12,8},{16,20},{20,16},{24,28},{28,24},{1,5},{5... | collective-permute-start | bytes 98312 | tf_op jit(solution)/shard_map/ppermute | solution.py:30
  3.5 5.5 %collective-permute-start.8 = (bf16[2,32,1792]{2,1,0:T(8,128)(2,1)S(1)}, bf16[2,32,1792]{2,1,0:T(8,128)(2,1)S(1)}, u32[]{:S(2)}, u32[]{:S(2)}) collective-permute-start(bf16[2,32,1792]{2,1,0:T(8,128)(2,1)S(1)} %get-tuple-element.32), channel_id=1, source_target_pairs={{0,4},{4,0},{8,12},{12,8},{16,20},{20,16},{24,28},{28,24},{1,5},{5... | collective-permute-start | bytes 688136 | tf_op jit(solution)/shard_map/ppermute | solution.py:30
  4.4 6.7 %collective-permute-start.1 = (bf16[2,4,1024]{2,1,0:T(4,128)(2,1)S(1)}, bf16[2,4,1024]{2,1,0:T(4,128)(2,1)S(1)}, u32[]{:S(2)}, u32[]{:S(2)}) collective-permute-start(bf16[2,4,1024]{2,1,0:T(4,128)(2,1)S(1)} %pad_maximum_fusion.6), channel_id=1, source_target_pairs={{0,8},{4,12},{8,0},{12,4},{16,24},{20,28},{24,16},{28,20},{1,9},{5... | collective-permute-start | bytes 49160 | tf_op jit(solution)/shard_map/ppermute | solution.py:30
  7.3 3.8 %collective-permute-start.2 = (bf16[2,4,1024]{2,1,0:T(4,128)(2,1)S(1)}, bf16[2,4,1024]{2,1,0:T(4,128)(2,1)S(1)}, u32[]{:S(2)}, u32[]{:S(2)}) collective-permute-start(bf16[2,4,1024]{2,1,0:T(4,128)(2,1)S(1)} %pad_maximum_fusion.7), channel_id=1, source_target_pairs={{0,16},{4,20},{8,24},{12,28},{16,0},{20,4},{24,8},{28,12},{1,17},{... | collective-permute-start | bytes 49160 | tf_op jit(solution)/shard_map/ppermute | solution.py:30
  8.9 4.9 %collective-permute-start.3 = (bf16[2,4,1024]{2,1,0:T(4,128)(2,1)S(1)}, bf16[2,4,1024]{2,1,0:T(4,128)(2,1)S(1)}, u32[]{:S(2)}, u32[]{:S(2)}) collective-permute-start(bf16[2,4,1024]{2,1,0:T(4,128)(2,1)S(1)} %pad_maximum_fusion.8), channel_id=1, source_target_pairs={{0,24},{4,28},{8,16},{12,20},{16,8},{20,12},{24,0},{28,4},{1,25},{... | collective-permute-start | bytes 49160 | tf_op jit(solution)/shard_map/ppermute | solution.py:30
  9.1 12.8 %collective-permute-start.9 = (bf16[2,2,32,1792]{3,2,1,0:T(8,128)(2,1)S(1)}, bf16[2,2,32,1792]{3,2,1,0:T(8,128)(2,1)S(1)}, u32[]{:S(2)}, u32[]{:S(2)}) collective-permute-start(bf16[2,2,32,1792]{3,2,1,0:T(8,128)(2,1)S(1)} %pad_maximum_fusion.refs_4_.refs_10_), channel_id=1, source_target_pairs={{0,8},{4,12},{8,0},{12,4},{16,24},{20,28},{24,16},{28,20},{1,9},{5... | collective-permute-start | bytes 1376264 | tf_op jit(solution)/shard_map/ppermute | solution.py:30
  13.8 11.6 %slice-start = ((s8[4587520]{0:T(1024)(128)(4,1)}), s8[4194304]{0:T(1024)(128)(4,1)S(1)}, s32[]{:S(2)}) async-start(s8[4587520]{0:T(1024)(128)(4,1)} %bitcast.40), calls=%async_computation | async-start | bytes 8388608
  13.8 7.7 %copy-start.8 = (f32[14,384]{1,0:T(8,128)S(1)}, f32[14,384]{1,0:T(8,128)}, u32[]{:S(2)}) copy-start(f32[14,384]{1,0:T(8,128)} %param.17) | copy-start | bytes 64516
  13.8 11.6 %slice-start.1 = ((s8[4587520]{0:T(1024)(128)(4,1)}), s8[393216]{0:T(1024)(128)(4,1)S(1)}, s32[]{:S(2)}) async-start(s8[4587520]{0:T(1024)(128)(4,1)} %bitcast.40), calls=%async_computation.1 | async-start | bytes 786432
  13.8 11.6 %copy-start = (bf16[20,64,1792]{2,1,0:T(8,128)(2,1)S(1)}, bf16[20,64,1792]{2,1,0:T(8,128)(2,1)}, u32[]{:S(2)}) copy-start(bf16[20,64,1792]{2,1,0:T(8,128)(2,1)} %pool_ref.3) | copy-start | bytes 13762564
  13.8 11.6 %copy-start.3 = (bf16[4,7168]{1,0:T(4,128)(2,1)S(1)}, bf16[4,7168]{1,0:T(4,128)(2,1)}, u32[]{:S(2)}) copy-start(bf16[4,7168]{1,0:T(4,128)(2,1)} %refs_8_.3) | copy-start | bytes 172036
  13.8 11.6 %copy-start.5 = (s32[4,16]{1,0:T(4,128)S(1)}, s32[4,16]{1,0:T(4,128)}, u32[]{:S(2)}) copy-start(s32[4,16]{1,0:T(4,128)} %table_ref.3) | copy-start | bytes 772
  13.8 11.6 %copy-start.6 = (s32[4]{0:T(128)S(1)}, s32[4]{0:T(128)}, u32[]{:S(2)}) copy-start(s32[4]{0:T(128)} %length_ref.3) | copy-start | bytes 52
  13.9 11.6 %copy-start.7 = (s32[4]{0:T(128)S(1)}, s32[4]{0:T(128)}, u32[]{:S(2)}) copy-start(s32[4]{0:T(128)} %slot_ref.3) | copy-start | bytes 52
  16.1 1.7 %collective-permute-start.4 = (f32[4,4,5376]{2,1,0:T(4,128)S(1)}, f32[4,4,5376]{2,1,0:T(4,128)S(1)}, u32[]{:S(2)}, u32[]{:S(2)}) collective-permute-start(f32[4,4,5376]{2,1,0:T(4,128)S(1)} %get-tuple-element.26), channel_id=1, source_target_pairs={{0,4},{4,0},{8,12},{12,8},{16,20},{20,16},{24,28},{28,24},{1,5},{5... | collective-permute-start | bytes 1032200 | tf_op jit(solution)/shard_map/ppermute | solution.py:30
  17.9 7.5 %collective-permute-start.5 = (bf16[4,7168]{1,0:T(4,128)(2,1)S(1)}, bf16[4,7168]{1,0:T(4,128)(2,1)S(1)}, u32[]{:S(2)}, u32[]{:S(2)}) collective-permute-start(bf16[4,7168]{1,0:T(4,128)(2,1)S(1)} %get-tuple-element.28), channel_id=1, source_target_pairs={{0,8},{4,12},{8,0},{12,4},{16,24},{20,28},{24,16},{28,20},{1,9},{5... | collective-permute-start | bytes 172040 | tf_op jit(solution)/shard_map/ppermute | solution.py:30
  18.5 6.9 %collective-permute-start.6 = (bf16[4,7168]{1,0:T(4,128)(2,1)S(1)}, bf16[4,7168]{1,0:T(4,128)(2,1)S(1)}, u32[]{:S(2)}, u32[]{:S(2)}) collective-permute-start(bf16[4,7168]{1,0:T(4,128)(2,1)S(1)} %get-tuple-element.29), channel_id=1, source_target_pairs={{0,16},{4,20},{8,24},{12,28},{16,0},{20,4},{24,8},{28,12},{1,17},{... | collective-permute-start | bytes 172040 | tf_op jit(solution)/shard_map/ppermute | solution.py:30
  18.6 6.8 %collective-permute-start.7 = (bf16[4,7168]{1,0:T(4,128)(2,1)S(1)}, bf16[4,7168]{1,0:T(4,128)(2,1)S(1)}, u32[]{:S(2)}, u32[]{:S(2)}) collective-permute-start(bf16[4,7168]{1,0:T(4,128)(2,1)S(1)} %get-tuple-element.30), channel_id=1, source_target_pairs={{0,24},{4,28},{8,16},{12,20},{16,8},{20,12},{24,0},{28,4},{1,25},{... | collective-permute-start | bytes 172040 | tf_op jit(solution)/shard_map/ppermute | solution.py:30
  22.9 14.9 %collective-permute-start.14 = (bf16[2,2,32,1792]{3,2,1,0:T(8,128)(2,1)S(1)}, bf16[2,2,32,1792]{3,2,1,0:T(8,128)(2,1)S(1)}, u32[]{:S(2)}, u32[]{:S(2)}) collective-permute-start(bf16[2,2,32,1792]{3,2,1,0:T(8,128)(2,1)S(1)} %turn_pages.1.refs_11_), channel_id=1, source_target_pairs={{0,16},{4,20},{8,24},{12,28},{16,0},{20,4},{24,8},{28,12},{1,17},{... | collective-permute-start | bytes 1376264 | tf_op jit(solution)/shard_map/ppermute | solution.py:30
  27.4 1.3 %collective-permute-start.10 = (bf16[4,32,256]{2,1,0:T(8,128)(2,1)S(1)}, bf16[4,32,256]{2,1,0:T(8,128)(2,1)S(1)}, u32[]{:S(2)}, u32[]{:S(2)}) collective-permute-start(bf16[4,32,256]{2,1,0:T(8,128)(2,1)S(1)} %get-tuple-element.34), channel_id=1, source_target_pairs={{0,4},{4,0},{8,12},{12,8},{16,20},{20,16},{24,28},{28,24},{1,5},{5... | collective-permute-start | bytes 196616 | tf_op jit(solution)/shard_map/ppermute | solution.py:30
  28.8 8.1 %collective-permute-start.11 = (bf16[2,32,256]{2,1,0:T(8,128)(2,1)S(1)}, bf16[2,32,256]{2,1,0:T(8,128)(2,1)S(1)}, u32[]{:S(2)}, u32[]{:S(2)}) collective-permute-start(bf16[2,32,256]{2,1,0:T(8,128)(2,1)S(1)} %pad_maximum_fusion.2), channel_id=1, source_target_pairs={{0,8},{4,12},{8,0},{12,4},{16,24},{20,28},{24,16},{28,20},{1,9},{5... | collective-permute-start | bytes 98312 | tf_op jit(solution)/shard_map/ppermute | solution.py:30
  33.0 4.2 %collective-permute-start.12 = (bf16[2,32,256]{2,1,0:T(8,128)(2,1)S(1)}, bf16[2,32,256]{2,1,0:T(8,128)(2,1)S(1)}, u32[]{:S(2)}, u32[]{:S(2)}) collective-permute-start(bf16[2,32,256]{2,1,0:T(8,128)(2,1)S(1)} %pad_maximum_fusion.3), channel_id=1, source_target_pairs={{0,16},{4,20},{8,24},{12,28},{16,0},{20,4},{24,8},{28,12},{1,17},{... | collective-permute-start | bytes 98312 | tf_op jit(solution)/shard_map/ppermute | solution.py:30
  33.0 4.9 %collective-permute-start.13 = (bf16[2,32,256]{2,1,0:T(8,128)(2,1)S(1)}, bf16[2,32,256]{2,1,0:T(8,128)(2,1)S(1)}, u32[]{:S(2)}, u32[]{:S(2)}) collective-permute-start(bf16[2,32,256]{2,1,0:T(8,128)(2,1)S(1)} %pad_maximum_fusion.4), channel_id=1, source_target_pairs={{0,24},{4,28},{8,16},{12,20},{16,8},{20,12},{24,0},{28,4},{1,25},{... | collective-permute-start | bytes 98312 | tf_op jit(solution)/shard_map/ppermute | solution.py:30
  34.5 3.6 %copy-start.2 = (bf16[14,16,7168]{2,1,0:T(8,128)(2,1)S(1)}, bf16[14,16,7168]{2,1,0:T(8,128)(2,1)}, u32[]{:S(2)}) copy-start(bf16[14,16,7168]{2,1,0:T(8,128)(2,1)} %param.18) | copy-start | bytes 9633796
  39.1 1.6 %collective-permute-start.15 = (bf16[4,4,4,1792]{3,2,1,0:T(4,128)(2,1)S(1)}, bf16[4,4,4,1792]{3,2,1,0:T(4,128)(2,1)S(1)}, u32[]{:S(2)}, u32[]{:S(2)}) collective-permute-start(bf16[4,4,4,1792]{3,2,1,0:T(4,128)(2,1)S(1)} %get-tuple-element.36), channel_id=1, source_target_pairs={{0,4},{4,0},{8,12},{12,8},{16,20},{20,16},{24,28},{28,24},{1,5},{5... | collective-permute-start | bytes 688136 | tf_op jit(solution)/shard_map/ppermute | solution.py:30
  40.8 6.4 %collective-permute-start.16 = (bf16[4,4,1792]{2,1,0:T(4,128)(2,1)S(1)}, bf16[4,4,1792]{2,1,0:T(4,128)(2,1)S(1)}, u32[]{:S(2)}, u32[]{:S(2)}) collective-permute-start(bf16[4,4,1792]{2,1,0:T(4,128)(2,1)S(1)} %get-tuple-element.45), channel_id=1, source_target_pairs={{0,8},{4,12},{8,0},{12,4},{16,24},{20,28},{24,16},{28,20},{1,9},{5... | collective-permute-start | bytes 172040 | tf_op jit(solution)/shard_map/ppermute | solution.py:30
  42.8 5.1 %collective-permute-start.18 = (bf16[4,4,1792]{2,1,0:T(4,128)(2,1)S(1)}, bf16[4,4,1792]{2,1,0:T(4,128)(2,1)S(1)}, u32[]{:S(2)}, u32[]{:S(2)}) collective-permute-start(bf16[4,4,1792]{2,1,0:T(4,128)(2,1)S(1)} %get-tuple-element.46), channel_id=1, source_target_pairs={{0,24},{4,28},{8,16},{12,20},{16,8},{20,12},{24,0},{28,4},{1,25},{... | collective-permute-start | bytes 172040 | tf_op jit(solution)/shard_map/ppermute | solution.py:30
  44.1 4.6 %collective-permute-start.17 = (bf16[4,4,1792]{2,1,0:T(4,128)(2,1)S(1)}, bf16[4,4,1792]{2,1,0:T(4,128)(2,1)S(1)}, u32[]{:S(2)}, u32[]{:S(2)}) collective-permute-start(bf16[4,4,1792]{2,1,0:T(4,128)(2,1)S(1)} %get-tuple-element.47), channel_id=1, source_target_pairs={{0,16},{4,20},{8,24},{12,28},{16,0},{20,4},{24,8},{28,12},{1,17},{... | collective-permute-start | bytes 172040 | tf_op jit(solution)/shard_map/ppermute | solution.py:30
  44.9 8.1 %collective-permute-start.22 = (bf16[2,32,1792]{2,1,0:T(8,128)(2,1)S(1)}, bf16[2,32,1792]{2,1,0:T(8,128)(2,1)S(1)}, u32[]{:S(2)}, u32[]{:S(2)}) collective-permute-start(bf16[2,32,1792]{2,1,0:T(8,128)(2,1)S(1)} %choose_half.1), channel_id=1, source_target_pairs={{0,4},{4,0},{8,12},{12,8},{16,20},{20,16},{24,28},{28,24},{1,5},{5... | collective-permute-start | bytes 688136 | tf_op jit(solution)/shard_map/ppermute | solution.py:30
  45.0 8.0 %copy-start.4 = (f32[7168]{0:T(1024)S(1)}, f32[7168]{0:T(1024)}, u32[]{:S(2)}) copy-start(f32[7168]{0:T(1024)} %param.19) | copy-start | bytes 86020
  48.8 6.5 %collective-permute-start.19 = (bf16[4,1792]{1,0:T(4,128)(2,1)S(1)}, bf16[4,1792]{1,0:T(4,128)(2,1)S(1)}, u32[]{:S(2)}, u32[]{:S(2)}) collective-permute-start(bf16[4,1792]{1,0:T(4,128)(2,1)S(1)} %get-tuple-element.56), channel_id=1, source_target_pairs={{0,1},{1,0},{2,3},{3,2},{4,5},{5,4},{6,7},{7,6},{8,9},{9,8},{10,11... | collective-permute-start | bytes 43016 | tf_op jit(solution)/shard_map/ppermute | solution.py:30
  50.4 5.5 %collective-permute-start.21 = (bf16[4,1792]{1,0:T(4,128)(2,1)S(1)}, bf16[4,1792]{1,0:T(4,128)(2,1)S(1)}, u32[]{:S(2)}, u32[]{:S(2)}) collective-permute-start(bf16[4,1792]{1,0:T(4,128)(2,1)S(1)} %get-tuple-element.57), channel_id=1, source_target_pairs={{0,3},{1,2},{2,1},{3,0},{4,7},{5,6},{6,5},{7,4},{8,11},{9,10},{10,... | collective-permute-start | bytes 43016 | tf_op jit(solution)/shard_map/ppermute | solution.py:30
  52.9 4.6 %collective-permute-start.20 = (bf16[4,1792]{1,0:T(4,128)(2,1)S(1)}, bf16[4,1792]{1,0:T(4,128)(2,1)S(1)}, u32[]{:S(2)}, u32[]{:S(2)}) collective-permute-start(bf16[4,1792]{1,0:T(4,128)(2,1)S(1)} %get-tuple-element.58), channel_id=1, source_target_pairs={{0,2},{1,3},{2,0},{3,1},{4,6},{5,7},{6,4},{7,5},{8,10},{9,11},{10,... | collective-permute-start | bytes 43016 | tf_op jit(solution)/shard_map/ppermute | solution.py:30

commit v7 on v6

--- a/solution.py
+++ b/solution.py
@@ -39,32 +39,6 @@
 
 def in_hbm(*arrays):
     return [pltpu.with_memory_space_constraint(array, pltpu.HBM) for array in arrays]
-
-
-def write_pool(pool, after):
-    parts = 4
-    step = pool.shape[0] // parts
-
-    def kernel(pool_ref, _, out_ref, sems):
-        places = [pl.ds(i * step, step) for i in range(parts)]
-        copies = [
-            pltpu.make_async_copy(pool_ref.at[place], out_ref.at[place], sems.at[i]) for i, place in enumerate(places)
-        ]
-        for copy in copies:
-            copy.start()
-        for copy in copies:
-            copy.wait()
-
-    return pl.pallas_call(
-        kernel,
-        out_shape=jax.ShapeDtypeStruct(pool.shape, pool.dtype),
-        in_specs=[VMEM, ANY],
-        out_specs=HBM,
-        scratch_shapes=[pltpu.SemaphoreType.DMA((parts,))],
-        compiler_params=pltpu.CompilerParams(vmem_limit_bytes=8 * MIB),
-        cost_estimate=cost(0, 2 * pool.size),
-        name="write_pool",
-    )(pool, after)
 
 
 def leaving_slot(new_slot_ref, slots, here):
@@ -142,15 +116,13 @@
     slots = block_refs[0].shape[1]
     lane = lax.broadcasted_iota(jnp.int32, (slots, META), 1)
     found = jnp.zeros((slots, META), F32)
-    goal = (here ^ wanted).astype(F32)
+    goal = here ^ wanted
     for d, ref in enumerate(block_refs):
         for e in range(2):
             k = 2 * d + e
-            if k == wanted:
-                continue
             told = ref[e, :, :META].astype(F32)
             numbered = jnp.where(lane == 4, float(k), told)
-            found = jnp.where(told[:, :1] == goal, numbered, found)
+            found = jnp.where(told[:, :1] == jnp.where(wanted == k, -1, goal).astype(F32), numbered, found)
     return lambda j: jnp.sum(jnp.where(lane == j, found, 0.0)).astype(jnp.int32)
 
 
@@ -158,20 +130,56 @@
     return 1 << (chips.bit_length() // 2)
 
 
-def turn_pages(spread, halves):
+def swap_pages(value, chips, along_row, step):
+    across = row_length(chips)
+    square = across * across == chips
+    steps = [2 * step if along_row == (device % 2 == 0 or not square) else 2 * across * step for device in range(2 * chips)]
+    return lax.ppermute(value, "req", [(i, i ^ steps[i]) for i in range(2 * chips)])
+
+
+def find_sources(spread, after):
     chips = len(spread)
     across = row_length(chips)
     down = chips // across
+
+    def kernel(*refs):
+        block_refs, out_ref = refs[:chips], refs[-1]
+        here = lax.axis_index("req")
+        turned = (here % 2 == 1) & (across == down)
+        for row in range(down):
+            for j in range(2):
+                pick = arrivals(block_refs, here, jnp.where(turned, 2 * row, 2 * across * row) + j)
+                source = pick(4)
+                chip = source // 2
+                chip = jnp.where(turned, chip % across * across + chip // across, chip)
+                out_ref[2 * row + j] = 2 * chip + source % 2
+                if row == 0 and j == 0:
+                    out_ref[2 * down] = pick(2)
+                    out_ref[2 * down + 1] = pick(3)
+                    out_ref[2 * down + 2] = source
+
+    return pl.pallas_call(
+        kernel,
+        out_shape=jax.ShapeDtypeStruct((2 * down + 3,), jnp.int32),
+        in_specs=[VMEM] * chips + [ANY],
+        out_specs=SMEM,
+        compiler_params=pltpu.CompilerParams(vmem_limit_bytes=2 * MIB),
+        cost_estimate=cost(0, 0),
+        name="find_sources",
+    )(*spread, after)
+
+
+def turn_pages(sources, halves, chips):
+    across = len(halves)
+    down = chips // across
     shape = halves[0].shape
 
-    def kernel(*refs):
-        block_refs, half_refs = refs[:chips], refs[chips : chips + across]
-        out_refs, sems = refs[chips + across : -1], refs[-1]
-        here = lax.axis_index("req")
+    def kernel(source_ref, *refs):
+        half_refs, out_refs, sems = refs[:across], refs[across:-1], refs[-1]
         waits = []
         for row in range(1, down):
             for j in range(2):
-                source = arrivals(block_refs, here, 2 * across * row + j)(4)
+                source = source_ref[2 * row + j]
                 place = jnp.where(source < 2 * across, source, 0)
                 for d in range(across):
                     for e in range(2):
@@ -189,13 +197,13 @@
     return pl.pallas_call(
         kernel,
         out_shape=(one,) * (down - 1),
-        in_specs=[VMEM] * chips + [ANY] * across,
+        in_specs=[SMEM] + [ANY] * across,
         out_specs=(VMEM,) * (down - 1),
         scratch_shapes=[pltpu.SemaphoreType.DMA((down - 1, 2))],
         compiler_params=pltpu.CompilerParams(vmem_limit_bytes=down * 2 * MIB),
         cost_estimate=cost(0, 4 * halves[0].size),
         name="turn_pages",
-    )(*spread, *halves)
+    )(sources, *halves)
 
 
 def start_half(source, across, core, half_refs, turned_refs, target, sem):
@@ -214,31 +222,29 @@
             pltpu.make_async_copy(ref.at[core], target, sem).start()
 
 
-def choose_half(spread, halves, turned):
-    chips, across, rows = len(spread), len(halves), len(turned)
-
-    def kernel(*refs):
-        block_refs, half_refs = refs[:chips], refs[chips : chips + across]
-        turned_refs = refs[chips + across : chips + across + rows]
-        out_ref, sem = refs[chips + across + rows :]
-        source = arrivals(block_refs, lax.axis_index("req"), 1)(4)
-        start_half(source, across, 1, half_refs, turned_refs, out_ref, sem)
+def choose_half(sources, halves, turned):
+    across, rows = len(halves), len(turned)
+
+    def kernel(source_ref, *refs):
+        half_refs, turned_refs = refs[:across], refs[across : across + rows]
+        out_ref, sem = refs[across + rows :]
+        start_half(source_ref[1], across, 1, half_refs, turned_refs, out_ref, sem)
         pltpu.make_async_copy(half_refs[0].at[0], out_ref, sem).wait()
 
     shape = halves[0].shape[1:]
     return pl.pallas_call(
         kernel,
         out_shape=jax.ShapeDtypeStruct(shape, halves[0].dtype),
-        in_specs=[VMEM] * chips + [ANY] * (across + rows),
+        in_specs=[SMEM] + [ANY] * (across + rows),
         out_specs=VMEM,
         scratch_shapes=[pltpu.SemaphoreType.DMA],
         compiler_params=pltpu.CompilerParams(vmem_limit_bytes=2 * MIB),
         cost_estimate=cost(0, 2 * halves[0].size),
         name="choose_half",
-    )(*spread, *halves, *turned)
-
-
-def project(blocks, weight):
+    )(sources, *halves, *turned)
+
+
+def project(blocks, weight, later):
     chips = len(blocks)
     slots = blocks[0].shape[1]
     heads, depth, width = weight.shape
@@ -247,7 +253,9 @@
 
     def kernel(*refs):
         block_refs = refs[:chips]
-        weight_ref, keep_ref, send_ref, left = refs[chips:]
+        weight_ref, later_ref, keep_ref, send_ref, later_out, left, sem = refs[chips:]
+        copy = pltpu.make_async_copy(later_ref, later_out, sem)
+        copy.start()
         for d in range(chips):
             for e in range(2):
                 row = (d * 2 + e) * slots
@@ -264,24 +272,26 @@
                 keep_ref[d, :, columns] = total[row : row + slots]
                 send_ref[d, :, columns] = total[row + slots : row + 2 * slots]
 
+        copy.wait()
+
     shape = jax.ShapeDtypeStruct((chips, slots, heads * width), F32)
     return pl.pallas_call(
         kernel,
-        out_shape=(shape, shape),
-        in_specs=[VMEM] * (chips + 1),
-        out_specs=(VMEM, VMEM),
-        scratch_shapes=[pltpu.VMEM((rows, depth), F32)],
-        compiler_params=pltpu.CompilerParams(vmem_limit_bytes=weight.size * 2 + 8 * MIB),
+        out_shape=(shape, shape, jax.ShapeDtypeStruct(later.shape, later.dtype)),
+        in_specs=[VMEM] * (chips + 1) + [HBM],
+        out_specs=(VMEM, VMEM, VMEM),
+        scratch_shapes=[pltpu.VMEM((rows, depth), F32), pltpu.SemaphoreType.DMA],
+        compiler_params=pltpu.CompilerParams(vmem_limit_bytes=weight.size * 2 + 12 * MIB),
         cost_estimate=cost(2 * rows * weight.size, 2 * weight.size),
         name="project",
-    )(*blocks, weight)
-
-
-def combine(keep, got):
+    )(*blocks, weight, *in_hbm(later))
+
+
+def combine(keep, got, after):
     chips, slots, width = keep.shape
     heads = width // (3 * LANES)
 
-    def kernel(keep_ref, got_ref, own_ref, *message_refs):
+    def kernel(keep_ref, got_ref, _, own_ref, *message_refs):
         own_ref[...] = keep_ref[0] + got_ref[0]
         for d in range(1, chips):
             for h in range(heads):
@@ -298,12 +308,12 @@
     return pl.pallas_call(
         kernel,
         out_shape=(jax.ShapeDtypeStruct((slots, width), F32),) + (message,) * (chips - 1),
-        in_specs=[VMEM, VMEM],
+        in_specs=[VMEM, VMEM, ANY],
         out_specs=(VMEM,) * chips,
         compiler_params=pltpu.CompilerParams(vmem_limit_bytes=8 * MIB),
         cost_estimate=cost(0, 8 * keep.size),
         name="combine",
-    )(keep, got)
+    )(keep, got, after)
 
 
 def attend(lengths, new_slot, page_table, sums, bias, tokens, key_pool, value_pool, after):
@@ -328,9 +338,18 @@
     def kernel(*refs):
         length_ref, slot_ref, table_ref = refs[:3]
         sum_refs = refs[3 : 3 + parts]
-        (bias_ref, token_ref, key_ref, value_ref, _, pack_keep, pack_send, patch_ref, score_buffer, mix_buffer) = refs[
-            3 + parts :
+        (bias_ref, token_ref, key_ref, value_ref, _, pack_keep, pack_send, patch_ref, key_out, value_out) = refs[
+            3 + parts : 13 + parts
         ]
+        score_buffer, mix_buffer, out_sems = refs[13 + parts :]
+        step = pages // 4
+        writes = [
+            pltpu.make_async_copy(source.at[pl.ds(i * step, step)], target.at[pl.ds(i * step, step)], out_sems.at[n, i])
+            for n, (source, target) in enumerate(((key_ref, key_out), (value_ref, value_out)))
+            for i in range(4)
+        ]
+        for write in writes:
+            write.start()
         here = lax.axis_index("req")
         column_block = lax.axis_index("head")
         leaving = leaving_slot(slot_ref, slots, here)
@@ -459,23 +478,23 @@
             extra += [one[:, i * PACK : (i + 1) * PACK] for i in range(strips)]
         extra = jnp.concatenate(extra + [jnp.zeros((pack_rows(slots, strips) - high - 3 * strips, PACK), F32)], axis=0)
 
+        lane = lax.broadcasted_iota(jnp.int32, (high, LANES), 1)
         row_at = lax.broadcasted_iota(jnp.int32, (high, LANES), 0)
-        lane_at = lax.broadcasted_iota(jnp.int32, (high, LANES), 1)
-        goal_device = jnp.full((high, LANES), -1.0, F32)
-        goal_slot = jnp.zeros((high, LANES), F32)
+        goal = jnp.full((high, LANES), -1.0, F32)
         for s in range(slots):
-            goal_device = jnp.where(row_at == s, (slot_ref[s] // slots).astype(F32), goal_device)
-            goal_slot = jnp.where(row_at == s, (slot_ref[s] % slots).astype(F32), goal_slot)
-        lane = lane_at // share
+            device, slot = slot_ref[s] // slots, slot_ref[s] % slots
+            number = jnp.where(lane % share == share - 1, slot, device).astype(F32)
+            goal = jnp.where(row_at == s, number, goal)
+        turned = [
+            pltpu.roll(attended[:, h * head : (h + 1) * head], h % per * share, 1) if h % per else attended[:, h * head : (h + 1) * head]
+            for h in range(heads)
+        ]
         for k in range(groups):
-            wanted = here ^ k
+            count = lax.rem(lane // share - (here ^ k) + per, per)
             tiles = [jnp.zeros((high, LANES), F32) for _ in range(PACK // LANES)]
             for h in range(heads):
-                place = h % per
-                shift = lax.rem((place - wanted) * share + 2 * LANES, LANES)
-                turned = pltpu.roll(attended[:, h * head : (h + 1) * head], shift, 1)
-                tiles[h // per] = jnp.where(lane == place, turned, tiles[h // per])
-            tiles[-1] = jnp.where(lane_at == LANES - 2, goal_device, jnp.where(lane_at == LANES - 1, goal_slot, tiles[-1]))
+                tiles[h // per] = jnp.where(count == h % per, turned[h], tiles[h // per])
+            tiles[-1] = jnp.where((count == per - 1) & (lane % share >= share - 2), goal, tiles[-1])
             block = jnp.concatenate([jnp.concatenate(tiles, axis=1), extra], axis=0).astype(BF16)
             (pack_keep, pack_send)[k % 2][k // 2] = block
 
@@ -488,13 +507,21 @@
                 new = jnp.broadcast_to(new_rows[n][s : s + 1], (tall, width))
                 patch_ref[n, s] = jnp.where(at == offset - first, new, old).astype(BF16)
 
+        for write in writes:
+            write.wait()
+
     packed = jax.ShapeDtypeStruct((parts, pack_rows(slots, strips), PACK), BF16)
-    return pl.pallas_call(
-        kernel,
-        out_shape=(packed, packed, jax.ShapeDtypeStruct((2, slots, tall, width), BF16)),
+    pool = jax.ShapeDtypeStruct(key_pool.shape, key_pool.dtype)
+    return pl.pallas_call(
+        kernel,
+        out_shape=(packed, packed, jax.ShapeDtypeStruct((2, slots, tall, width), BF16), pool, pool),
         in_specs=[SMEM] * 3 + [VMEM] * (parts + 4) + [ANY],
-        out_specs=(VMEM, VMEM, VMEM),
-        scratch_shapes=[pltpu.VMEM((tall, long_rows), F32), pltpu.VMEM((tall, width), F32)],
+        out_specs=(VMEM, VMEM, VMEM, HBM, HBM),
+        scratch_shapes=[
+            pltpu.VMEM((tall, long_rows), F32),
+            pltpu.VMEM((tall, width), F32),
+            pltpu.SemaphoreType.DMA((2, 4)),
+        ],
         compiler_params=pltpu.CompilerParams(vmem_limit_bytes=18 * MIB),
         cost_estimate=cost(4 * tall * (long_rows + short_rows) * width, 4 * (long_rows + short_rows) * width),
         name="attend",
@@ -519,8 +546,14 @@
         gathered = jnp.concatenate(
             [block_refs[d][e, :high, :].astype(F32) for d in range(chips) for e in range(2)], axis=0
         )
+        here = lax.axis_index("req")
+        share = LANES // (2 * chips)
+        back = lax.rem(LANES - here * share, LANES)
+        gathered = jnp.concatenate(
+            [pltpu.roll(gathered[:, first : first + LANES], back, 1) for first in range(0, PACK, LANES)], axis=1
+        )
         goal = gathered[:, PACK - 2 : PACK - 1].astype(jnp.int32)
-        place = goal ^ lax.axis_index("req")
+        place = goal ^ here
         row = (place % 2) * (chips * slots) + (place // 2) * slots + gathered[:, PACK - 1 :].astype(jnp.int32)
         row = jnp.where(goal < 0, -1, row)
         size = (gathered.shape[0], rows)
@@ -542,7 +575,7 @@
     return pl.pallas_call(
         kernel,
         out_shape=(jax.ShapeDtypeStruct(shape, F32), jax.ShapeDtypeStruct(shape, BF16)),
-        in_specs=[VMEM] * (chips + 1) + [HBM] * min(1, len(after)) + [ANY] * (len(after) - 1),
+        in_specs=[VMEM] * (chips + 1) + [ANY] * len(after),
         out_specs=(VMEM, VMEM),
         compiler_params=pltpu.CompilerParams(vmem_limit_bytes=10 * MIB),
         cost_estimate=cost(2 * rows * weight.size, 2 * weight.size),
@@ -550,8 +583,9 @@
     )(*blocks, weight, *after)
 
 
-def place_page(lengths, new_slot, page_table, patches, spread, packs, tokens, out_bias, halves, turned, from_other, key_out, value_out):
-    chips, across, rows = len(spread), len(halves), len(turned)
+def place_page(lengths, new_slot, page_table, sources, patches, packs, tokens, out_bias, halves, turned, from_other, key_out, value_out):
+    chips, across, rows = len(packs), len(halves), len(turned)
+    down = chips // across
     count = across + rows + 1
     page, width = key_out.shape[1:]
     half = page // 2
@@ -561,13 +595,13 @@
 
     tall = patches.shape[2]
 
-    def kernel(length_ref, slot_ref, table_ref, patch_ref, *refs):
-        block_refs, pack_refs = refs[:chips], refs[chips : 2 * chips]
-        token_ref, bias_ref = refs[2 * chips : 2 * chips + 2]
-        half_refs = refs[2 * chips + 2 : 2 * chips + 2 + across]
-        turned_refs = refs[2 * chips + 2 + across : 2 * chips + 2 + across + rows]
-        other_ref = refs[2 * chips + 1 + count]
-        _, _, base_ref, key_ref, value_ref, buffer, arrived, sems, out_sems, patch_sems = refs[2 * chips + 2 + count :]
+    def kernel(length_ref, slot_ref, table_ref, source_ref, patch_ref, *refs):
+        pack_refs = refs[:chips]
+        token_ref, bias_ref = refs[chips : chips + 2]
+        half_refs = refs[chips + 2 : chips + 2 + across]
+        turned_refs = refs[chips + 2 + across : chips + 2 + across + rows]
+        other_ref = refs[chips + 1 + count]
+        _, _, base_ref, key_ref, value_ref, buffer, arrived, sems, out_sems, patch_sems = refs[chips + 2 + count :]
         here = lax.axis_index("req")
         leaving = leaving_slot(slot_ref, slots, here)
 
@@ -585,12 +619,11 @@
                     patch(n, s).start()
 
         column = pl.multiple_of(lax.axis_index("head") * width, LANES)
-        pick = arrivals(block_refs, here, 0)
-        source, page_at, offset = pick(4), pick(2), pick(3)
+        page_at, offset, source = source_ref[2 * down], source_ref[2 * down + 1], source_ref[2 * down + 2]
         targets = [
             buffer.at[:, pl.ds(pl.multiple_of((here % 2 ^ e) * half, half), half)] for e in range(2)
         ]
-        start_half(source, across, 0, half_refs, turned_refs, targets[0], sems.at[0])
+        start_half(source_ref[0], across, 0, half_refs, turned_refs, targets[0], sems.at[0])
         from_core = pltpu.make_async_copy(other_ref, targets[1], sems.at[1])
         from_core.start()
 
@@ -640,7 +673,7 @@
     return pl.pallas_call(
         kernel,
         out_shape=(jax.ShapeDtypeStruct((slots, width), F32), shape, shape),
-        in_specs=[SMEM] * 3 + [VMEM] * (2 * chips + 3) + [ANY] * count + [HBM] * 2,
+        in_specs=[SMEM] * 4 + [VMEM] * (chips + 3) + [ANY] * count + [HBM] * 2,
         out_specs=(VMEM, HBM, HBM),
         scratch_shapes=[
             pltpu.VMEM((2, page, width), BF16),
@@ -649,12 +682,12 @@
             pltpu.SemaphoreType.DMA((2,)),
             pltpu.SemaphoreType.DMA((2, slots)),
         ],
-        input_output_aliases={2 * chips + 6 + count: 1, 2 * chips + 7 + count: 2},
+        input_output_aliases={chips + 7 + count: 1, chips + 8 + count: 2},
         compiler_params=pltpu.CompilerParams(vmem_limit_bytes=4 * MIB),
         cost_estimate=cost(0, 8 * page * width),
         name="place_page",
     )(
-        lengths, new_slot, page_table, patches, *spread, *packs, tokens, out_bias, *halves, *turned, from_other, key_out, value_out
+        lengths, new_slot, page_table, sources, patches, *packs, tokens, out_bias, *halves, *turned, from_other, key_out, value_out
     )
 
 
@@ -685,16 +718,17 @@
     spread = spread_pairs(keep, got)
     across = row_length(chips)
     halves = [jnp.stack([keep_half, swap(send_half, "req", 1)])]
-    halves += [swap(halves[0], "req", 2 * d) for d in range(1, across)]
-    turning = turn_pages(spread, halves)
-    turned = [swap(one, "req", 2 * across * (row + 1)) for row, one in enumerate(turning)]
-
-    keep, send = project(spread, jnp.transpose(qkv_weight, (1, 0, 2)))
+    halves += [swap_pages(halves[0], chips, True, d) for d in range(1, across)]
+    flat = out_weight.reshape(-1, out_weight.shape[2])
+    keep, send, staged = project(spread, jnp.transpose(qkv_weight, (1, 0, 2)), flat)
     got = swap(send, "req", 1)
-    own, *messages = combine(keep, got)
+    sources = find_sources(spread, keep)
+    own, *messages = combine(keep, got, sources)
+    turning = turn_pages(sources, halves, chips)
+    turned = [swap_pages(one, chips, False, row + 1) for row, one in enumerate(turning)]
     sums = [own] + [swap(messages[d - 1], "req", 2 * d) for d in range(1, chips)]
 
-    pack_keep, pack_send, patches = attend(
+    pack_keep, pack_send, patches, key_out, value_out = attend(
         lengths,
         new_slot,
         page_table,
@@ -708,24 +742,21 @@
     packs_got = swap(pack_send, "req", 1)
     packs = spread_pairs(pack_keep, packs_got)
 
-    from_other = swap(choose_half(spread, halves, turned), "req", 1)
-    key_out = write_pool(key_pool, packs_got)
+    from_other = swap(choose_half(sources, halves, turned), "req", 1)
 
     keep, send = out_project(
-        packs, out_weight.reshape(-1, out_weight.shape[2]), head_groups, slots, *in_hbm(key_out), turned[0]
+        packs, staged, head_groups, slots, turned[0]
     )
     total = keep + swap(send, "req", 1).astype(F32)
-    value_out = write_pool(value_pool, total)
     summed = total[0]
     for d in range(1, chips):
         summed = summed + swap(total[d].astype(BF16), "req", 2 * d).astype(F32)
-    summed, value_out = lax.optimization_barrier((summed, value_out))
     base, key_out, value_out = place_page(
         lengths,
         new_slot,
         page_table,
+        sources,
         patches,
-        spread,
         packs,
         tokens,
         out_bias[None],

time: 58.3 us -> 57.1 us (0.979)
  starting transfers between devices: 26.9 us -> 24.2 us
  waiting for transfers between devices: 12.9 us -> 14.9 us
    ppermute x23 -> x21, starting transfers between devices: 26.9 us -> 20.6 us  [swap(): return lax.ppermute(value, axis, [(i, i ^ step) for i in range(size)])]
    ppermute x0 -> x2, starting transfers between devices: none -> 3.62 us  [swap_pages(): lax.ppermute(value, 'req', [(i, i ^ steps[i]) for i in range(2 * chips)])]
    pallas_call x4 -> x3, Pallas kernels: 7.84 us -> 4.35 us  [the longest x1 2.28 us: project(): pl.pallas_call(kernel, out_shape=(shape, shape, jax.ShapeDtypeStruct(late...]
    pallas_call x1, Pallas kernels: 1.96 us -> 5.03 us  [attend(): pl.pallas_call(kernel, out_shape=(packed, packed, jax.ShapeDtypeStruct((2...]
    ppermute x23 -> x21, waiting for transfers between devices: 12.9 us -> 14.9 us  [swap(): return lax.ppermute(value, axis, [(i, i ^ step) for i in range(size)])]
  transfers between devices with their start and end apart: 23 -> 23, of which waited for: 12 -> 13; matrix products, arithmetic and copies ran while one was open for 1% -> 0% of each run, Pallas kernels for 22% -> 22%
where the time goes in v7:
time: 57.1 us; the launch traced here: 57 us
  starting transfers between devices  24.2 us (42%)
  Pallas kernels  15.7 us (27%)
  waiting for transfers between devices  14.9 us (26%)
  other arithmetic  0.98 us (2%)
  between operations  0.98 us (2%)
    ppermute x21, starting transfers between devices, swap(): return lax.ppermute(value, axis, [(i, i ^ step) for i in range(size)])  20.6 us
    ppermute x21, waiting for transfers between devices, swap(): return lax.ppermute(value, axis, [(i, i ^ step) for i in range(size)])  14.9 us
    pallas_call x1, Pallas kernels, attend(): pl.pallas_call(kernel, out_shape=(packed, packed, jax.ShapeDtypeStruct((2...  5.03 us
    ppermute x2, starting transfers between devices, swap_pages(): lax.ppermute(value, 'req', [(i, i ^ steps[i]) for i in range(2 * chips)])  3.62 us
    pallas_call x1, Pallas kernels, prepare(): pl.pallas_call(kernel, out_shape=(blocks, blocks, halves, halves), in_spe...  2.33 us
    pallas_call x1, Pallas kernels, project(): pl.pallas_call(kernel, out_shape=(shape, shape, jax.ShapeDtypeStruct(late...  2.28 us
    pallas_call x1, Pallas kernels, place_page(): pl.pallas_call(kernel, out_shape=(jax.ShapeDtypeStruct((slots, width), F3...  2.03 us
    pallas_call x1, Pallas kernels, turn_pages(): pl.pallas_call(kernel, out_shape=(one,) * (down - 1), in_specs=[SMEM] + [...  1.2 us
  transfers between devices with their start and end apart: 23, of which 13 were waited for; matrix products, arithmetic and copies ran while one was open for 0% of the time, Pallas kernels for 22%

profile of v7, /device:TPU:0, one launch (start us, length us, event | category | flops | bytes accessed | tf_op | source)
XLA Modules:
  0.0 57.0 jit_solution(12005883438605295261)
XLA Ops:
  0.6 2.3 %prepare.1 = (bf16[4,4,1024]{2,1,0:T(4,128)(2,1)S(1)}, bf16[4,4,1024]{2,1,0:T(4,128)(2,1)S(1)}, bf16[2,32,1792]{2,1,0:T(8,128)(2,1)S(1)}, bf16[2,32,1792]{2,1,0:T(8,128)(2,1)S(1)}) custom-call(bf16[4,7168]{1,0:T(4,128)(2,1)} %refs_4_.1, f32[1,7168]{1,0:T(1,128)} %bitcast.53, f32[1,7168]{1,0:T(1,128)} %bitcast.54, s32[4]{0:T(128)} %length_ref.3, ...), custom_call_target="tpu_custom_call" | custom-call | tf_op jit(solution)/shard_map/prepare/pallas_call | solution.py:103
  3.0 0.5 collective-permute-start
  3.5 0.1 collective-permute-start.8
  3.6 0.8 %collective-permute-done = bf16[4,4,1024]{2,1,0:T(4,128)(2,1)S(1)} collective-permute-done((bf16[4,4,1024]{2,1,0:T(4,128)(2,1)S(1)}, bf16[4,4,1024]{2,1,0:T(4,128)(2,1)S(1)}, u32[]{:S(2)}, u32[]{:S(2)}) %collective-permute-start) | collective-permute-done | bytes 32800 | tf_op jit(solution)/shard_map/ppermute | solution.py:30
  4.4 3.9 %collective-permute-start.3 = (bf16[2,4,1024]{2,1,0:T(4,128)(2,1)S(1)}, bf16[2,4,1024]{2,1,0:T(4,128)(2,1)S(1)}, u32[]{:S(2)}, u32[]{:S(2)}) collective-permute-start(bf16[2,4,1024]{2,1,0:T(4,128)(2,1)S(1)} %pad_maximum_fusion.8), channel_id=1, source_target_pairs={{0,24},{4,28},{8,16},{12,20},{16,8},{20,12},{24,0},{28,4},{1,25},{... | collective-permute-start | bytes 49160 | tf_op jit(solution)/shard_map/ppermute | solution.py:30
  8.3 0.6 %collective-permute-start.2 = (bf16[2,4,1024]{2,1,0:T(4,128)(2,1)S(1)}, bf16[2,4,1024]{2,1,0:T(4,128)(2,1)S(1)}, u32[]{:S(2)}, u32[]{:S(2)}) collective-permute-start(bf16[2,4,1024]{2,1,0:T(4,128)(2,1)S(1)} %pad_maximum_fusion.7), channel_id=1, source_target_pairs={{0,16},{4,20},{8,24},{12,28},{16,0},{20,4},{24,8},{28,12},{1,17},{... | collective-permute-start | bytes 49160 | tf_op jit(solution)/shard_map/ppermute | solution.py:30
  8.9 0.1 collective-permute-start.1
  9.1 2.0 %collective-permute-start.9 = (bf16[2,2,32,1792]{3,2,1,0:T(8,128)(2,1)S(1)}, bf16[2,2,32,1792]{3,2,1,0:T(8,128)(2,1)S(1)}, u32[]{:S(2)}, u32[]{:S(2)}) collective-permute-start(bf16[2,2,32,1792]{3,2,1,0:T(8,128)(2,1)S(1)} %pad_maximum_fusion.refs_0_.refs_6_), channel_id=1, source_target_pairs={{0,8},{4,20},{8,0},{12,28},{16,24},{20,4},{24,16},{28,12},{1,9},{5... | collective-permute-start | bytes 1376264 | tf_op jit(solution)/shard_map/ppermute | solution.py:137
  11.1 1.1 %collective-permute-done.2.refs_2_ = bf16[2,4,1024]{2,1,0:T(4,128)(2,1)S(1)} collective-permute-done((bf16[2,4,1024]{2,1,0:T(4,128)(2,1)S(1)}, bf16[2,4,1024]{2,1,0:T(4,128)(2,1)S(1)}, u32[]{:S(2)}, u32[]{:S(2)}) %collective-permute-start.2) | collective-permute-done | bytes 16416 | tf_op jit(solution)/shard_map/ppermute | solution.py:30
  12.2 0.4 collective-permute-done.1.refs_1_
  12.8 2.3 %project.1 = (f32[4,4,5376]{2,1,0:T(4,128)S(1)}, f32[4,4,5376]{2,1,0:T(4,128)S(1)}, bf16[224,7168]{1,0:T(8,128)(2,1)S(1)}) custom-call(bf16[2,4,1024]{2,1,0:T(4,128)(2,1)S(1)} %pad_maximum_fusion.5.refs_0_, bf16[2,4,1024]{2,1,0:T(4,128)(2,1)S(1)} %collective-permute-done.1.refs_1_, bf16[2,4,1024]{2,1,0:T(4,128)(2,1)S(1)} %collective-permute-done.2.refs_2_, ...), custom_call_target="tpu_custom_call" | custom-call | tf_op jit(solution)/shard_map/project/pallas_call | solution.py:278
  15.0 0.1 collective-permute-start.4
  15.1 0.9 %find_sources.1._.source_ref = s32[7]{0:T(128)S(1)} custom-call(bf16[2,4,1024]{2,1,0:T(4,128)(2,1)S(1)} %pad_maximum_fusion.5.refs_0_, bf16[2,4,1024]{2,1,0:T(4,128)(2,1)S(1)} %collective-permute-done.1.refs_1_, bf16[2,4,1024]{2,1,0:T(4,128)(2,1)S(1)} %collective-permute-done.2.refs_2_, bf16[2,4,1024]{2,1,0:T(4,128)(2,1)S(1)} %collective-permute-done.3.refs_3_, ...), custom_call_target="tpu_custom_call" | custom-call | tf_op jit(solution)/shard_map/find_sources/pallas_call | solution.py:161
  16.0 0.8 %collective-permute-done.4.got_ref = f32[4,4,5376]{2,1,0:T(4,128)S(1)} collective-permute-done((f32[4,4,5376]{2,1,0:T(4,128)S(1)}, f32[4,4,5376]{2,1,0:T(4,128)S(1)}, u32[]{:S(2)}, u32[]{:S(2)}) %collective-permute-start.4) | collective-permute-done | bytes 344096 | tf_op jit(solution)/shard_map/ppermute | solution.py:30
  16.8 0.1 combine.1
  16.8 0.1 collective-permute-start.5
  17.0 2.0 %collective-permute-start.6 = (bf16[4,7168]{1,0:T(4,128)(2,1)S(1)}, bf16[4,7168]{1,0:T(4,128)(2,1)S(1)}, u32[]{:S(2)}, u32[]{:S(2)}) collective-permute-start(bf16[4,7168]{1,0:T(4,128)(2,1)S(1)} %get-tuple-element.30), channel_id=1, source_target_pairs={{0,16},{4,20},{8,24},{12,28},{16,0},{20,4},{24,8},{28,12},{1,17},{... | collective-permute-start | bytes 172040 | tf_op jit(solution)/shard_map/ppermute | solution.py:30
  18.9 1.4 %collective-permute-start.7 = (bf16[4,7168]{1,0:T(4,128)(2,1)S(1)}, bf16[4,7168]{1,0:T(4,128)(2,1)S(1)}, u32[]{:S(2)}, u32[]{:S(2)}) collective-permute-start(bf16[4,7168]{1,0:T(4,128)(2,1)S(1)} %get-tuple-element.31), channel_id=1, source_target_pairs={{0,24},{4,28},{8,16},{12,20},{16,8},{20,12},{24,0},{28,4},{1,25},{... | collective-permute-start | bytes 172040 | tf_op jit(solution)/shard_map/ppermute | solution.py:30
  20.4 1.2 %turn_pages.1.refs_11_ = bf16[2,2,32,1792]{3,2,1,0:T(8,128)(2,1)S(1)} custom-call(s32[7]{0:T(128)S(1)} %find_sources.1._.source_ref, bf16[2,2,32,1792]{3,2,1,0:T(8,128)(2,1)S(1)} %pad_maximum_fusion.refs_0_.refs_6_, bf16[2,2,32,1792]{3,2,1,0:T(8,128)(2,1)S(1)} %collective-permute-done.9.refs_1_.refs_7_), custom_call_target="tpu_custom_call" | custom-call | tf_op jit(solution)/shard_map/turn_pages/pallas_call | solution.py:197
  21.6 1.6 %collective-permute-start.14 = (bf16[2,2,32,1792]{3,2,1,0:T(8,128)(2,1)S(1)}, bf16[2,2,32,1792]{3,2,1,0:T(8,128)(2,1)S(1)}, u32[]{:S(2)}, u32[]{:S(2)}) collective-permute-start(bf16[2,2,32,1792]{3,2,1,0:T(8,128)(2,1)S(1)} %turn_pages.1.refs_11_), channel_id=1, source_target_pairs={{0,16},{4,12},{8,24},{12,4},{16,0},{20,28},{24,8},{28,20},{1,17},{... | collective-permute-start | bytes 1376264 | tf_op jit(solution)/shard_map/ppermute | solution.py:137
  23.2 0.8 %collective-permute-done.7.refs_6_ = bf16[4,7168]{1,0:T(4,128)(2,1)S(1)} collective-permute-done((bf16[4,7168]{1,0:T(4,128)(2,1)S(1)}, bf16[4,7168]{1,0:T(4,128)(2,1)S(1)}, u32[]{:S(2)}, u32[]{:S(2)}) %collective-permute-start.7) | collective-permute-done | bytes 57376 | tf_op jit(solution)/shard_map/ppermute | solution.py:30
  24.1 5.0 %attend.1 = (bf16[4,32,256]{2,1,0:T(8,128)(2,1)S(1)}, bf16[4,32,256]{2,1,0:T(8,128)(2,1)S(1)}, bf16[2,4,16,1792]{3,2,1,0:T(8,128)(2,1)S(1)}, bf16[20,64,1792]{2,1,0:T(8,128)(2,1)}, bf16[20,64,1792]{2,1,0:T(8,128)(2,1)}) custom-call(s32[4]{0:T(128)S(1)} %copy-done.4, s32[4]{0:T(128)S(1)} %copy-done.5, s32[4,16]{1,0:T(4,128)S(1)} %copy-done.3, ...), custom_call_target="tpu_custom_call" | custom-call | tf_op jit(solution)/shard_map/attend/pallas_call | solution.py:515
  29.1 0.1 collective-permute-start.10
  29.2 1.2 %collective-permute-done.10 = bf16[4,32,256]{2,1,0:T(8,128)(2,1)S(1)} collective-permute-done((bf16[4,32,256]{2,1,0:T(8,128)(2,1)S(1)}, bf16[4,32,256]{2,1,0:T(8,128)(2,1)S(1)}, u32[]{:S(2)}, u32[]{:S(2)}) %collective-permute-start.10) | collective-permute-done | bytes 65568 | tf_op jit(solution)/shard_map/ppermute | solution.py:30
  30.5 2.1 %collective-permute-start.13 = (bf16[2,32,256]{2,1,0:T(8,128)(2,1)S(1)}, bf16[2,32,256]{2,1,0:T(8,128)(2,1)S(1)}, u32[]{:S(2)}, u32[]{:S(2)}) collective-permute-start(bf16[2,32,256]{2,1,0:T(8,128)(2,1)S(1)} %pad_maximum_fusion.4), channel_id=1, source_target_pairs={{0,24},{4,28},{8,16},{12,20},{16,8},{20,12},{24,0},{28,4},{1,25},{... | collective-permute-start | bytes 98312 | tf_op jit(solution)/shard_map/ppermute | solution.py:30
  32.6 1.4 %collective-permute-start.12 = (bf16[2,32,256]{2,1,0:T(8,128)(2,1)S(1)}, bf16[2,32,256]{2,1,0:T(8,128)(2,1)S(1)}, u32[]{:S(2)}, u32[]{:S(2)}) collective-permute-start(bf16[2,32,256]{2,1,0:T(8,128)(2,1)S(1)} %pad_maximum_fusion.3), channel_id=1, source_target_pairs={{0,16},{4,20},{8,24},{12,28},{16,0},{20,4},{24,8},{28,12},{1,17},{... | collective-permute-start | bytes 98312 | tf_op jit(solution)/shard_map/ppermute | solution.py:30
  34.1 1.3 %collective-permute-done.13.refs_3_ = bf16[2,32,256]{2,1,0:T(8,128)(2,1)S(1)} collective-permute-done((bf16[2,32,256]{2,1,0:T(8,128)(2,1)S(1)}, bf16[2,32,256]{2,1,0:T(8,128)(2,1)S(1)}, u32[]{:S(2)}, u32[]{:S(2)}) %collective-permute-start.13) | collective-permute-done | bytes 32800 | tf_op jit(solution)/shard_map/ppermute | solution.py:30
  35.4 1.1 %collective-permute-done.12.refs_2_ = bf16[2,32,256]{2,1,0:T(8,128)(2,1)S(1)} collective-permute-done((bf16[2,32,256]{2,1,0:T(8,128)(2,1)S(1)}, bf16[2,32,256]{2,1,0:T(8,128)(2,1)S(1)}, u32[]{:S(2)}, u32[]{:S(2)}) %collective-permute-start.12) | collective-permute-done | bytes 32800 | tf_op jit(solution)/shard_map/ppermute | solution.py:30
  36.5 1.4 %collective-permute-done.11.refs_1_ = bf16[2,32,256]{2,1,0:T(8,128)(2,1)S(1)} collective-permute-done((bf16[2,32,256]{2,1,0:T(8,128)(2,1)S(1)}, bf16[2,32,256]{2,1,0:T(8,128)(2,1)S(1)}, u32[]{:S(2)}, u32[]{:S(2)}) %collective-permute-start.11) | collective-permute-done | bytes 32800 | tf_op jit(solution)/shard_map/ppermute | solution.py:30
  37.9 1.0 %out_project.1 = (f32[4,4,4,1792]{3,2,1,0:T(4,128)S(1)}, bf16[4,4,4,1792]{3,2,1,0:T(4,128)(2,1)S(1)}) custom-call(bf16[2,32,256]{2,1,0:T(8,128)(2,1)S(1)} %pad_maximum_fusion.1.refs_0_, bf16[2,32,256]{2,1,0:T(8,128)(2,1)S(1)} %collective-permute-done.11.refs_1_, bf16[2,32,256]{2,1,0:T(8,128)(2,1)S(1)} %collective-permute-done.12.refs_2_, ...), custom_call_target="tpu_custom_call" | custom-call | tf_op jit(solution)/shard_map/out_project/pallas_call | solution.py:575
  39.0 0.1 collective-permute-start.15
  39.0 1.5 %collective-permute-done.15 = bf16[4,4,4,1792]{3,2,1,0:T(4,128)(2,1)S(1)} collective-permute-done((bf16[4,4,4,1792]{3,2,1,0:T(4,128)(2,1)S(1)}, bf16[4,4,4,1792]{3,2,1,0:T(4,128)(2,1)S(1)}, u32[]{:S(2)}, u32[]{:S(2)}) %collective-permute-start.15) | collective-permute-done | bytes 229408 | tf_op jit(solution)/shard_map/ppermute | solution.py:30
  40.5 0.2 fusion.10
  40.7 0.1 slice_bitcast_fusion.3
  40.8 0.1 collective-permute-start.16
  40.9 0.7 %collective-permute-start.17 = (bf16[4,4,1792]{2,1,0:T(4,128)(2,1)S(1)}, bf16[4,4,1792]{2,1,0:T(4,128)(2,1)S(1)}, u32[]{:S(2)}, u32[]{:S(2)}) collective-permute-start(bf16[4,4,1792]{2,1,0:T(4,128)(2,1)S(1)} %get-tuple-element.51), channel_id=1, source_target_pairs={{0,16},{4,20},{8,24},{12,28},{16,0},{20,4},{24,8},{28,12},{1,17},{... | collective-permute-start | bytes 172040 | tf_op jit(solution)/shard_map/ppermute | solution.py:30
  41.5 2.8 %collective-permute-start.18 = (bf16[4,4,1792]{2,1,0:T(4,128)(2,1)S(1)}, bf16[4,4,1792]{2,1,0:T(4,128)(2,1)S(1)}, u32[]{:S(2)}, u32[]{:S(2)}) collective-permute-start(bf16[4,4,1792]{2,1,0:T(4,128)(2,1)S(1)} %get-tuple-element.50), channel_id=1, source_target_pairs={{0,24},{4,28},{8,16},{12,20},{16,8},{20,12},{24,0},{28,4},{1,25},{... | collective-permute-start | bytes 172040 | tf_op jit(solution)/shard_map/ppermute | solution.py:30
  44.3 0.9 %choose_half.1 = bf16[2,32,1792]{2,1,0:T(8,128)(2,1)S(1)} custom-call(s32[7]{0:T(128)S(1)} %find_sources.1._.source_ref, bf16[2,2,32,1792]{3,2,1,0:T(8,128)(2,1)S(1)} %pad_maximum_fusion.refs_0_.refs_6_, bf16[2,2,32,1792]{3,2,1,0:T(8,128)(2,1)S(1)} %collective-permute-done.9.refs_1_.refs_7_, ...), custom_call_target="tpu_custom_call" | custom-call | tf_op jit(solution)/shard_map/choose_half/pallas_call | solution.py:235
  45.2 0.1 collective-permute-start.22
  45.3 0.1 collective-permute-done.17
  45.4 1.2 %collective-permute-done.18 = bf16[4,4,1792]{2,1,0:T(4,128)(2,1)S(1)} collective-permute-done((bf16[4,4,1792]{2,1,0:T(4,128)(2,1)S(1)}, bf16[4,4,1792]{2,1,0:T(4,128)(2,1)S(1)}, u32[]{:S(2)}, u32[]{:S(2)}) %collective-permute-start.18) | collective-permute-done | bytes 57376 | tf_op jit(solution)/shard_map/ppermute | solution.py:30
  46.6 0.1 fusion.8
  46.7 1.5 %collective-permute-start.19 = (bf16[4,1792]{1,0:T(4,128)(2,1)S(1)}, bf16[4,1792]{1,0:T(4,128)(2,1)S(1)}, u32[]{:S(2)}, u32[]{:S(2)}) collective-permute-start(bf16[4,1792]{1,0:T(4,128)(2,1)S(1)} %get-tuple-element.60), channel_id=1, source_target_pairs={{0,1},{1,0},{2,3},{3,2},{4,5},{5,4},{6,7},{7,6},{8,9},{9,8},{10,11... | collective-permute-start | bytes 43016 | tf_op jit(solution)/shard_map/ppermute | solution.py:30
  48.2 2.6 %collective-permute-start.20 = (bf16[4,1792]{1,0:T(4,128)(2,1)S(1)}, bf16[4,1792]{1,0:T(4,128)(2,1)S(1)}, u32[]{:S(2)}, u32[]{:S(2)}) collective-permute-start(bf16[4,1792]{1,0:T(4,128)(2,1)S(1)} %get-tuple-element.62), channel_id=1, source_target_pairs={{0,2},{1,3},{2,0},{3,1},{4,6},{5,7},{6,4},{7,5},{8,10},{9,11},{10,... | collective-permute-start | bytes 43016 | tf_op jit(solution)/shard_map/ppermute | solution.py:30
  50.8 0.3 collective-permute-start.21
  51.2 2.0 %place_page.1 = (f32[4,1792]{1,0:T(4,128)S(1)}, bf16[20,64,1792]{2,1,0:T(8,128)(2,1)}, bf16[20,64,1792]{2,1,0:T(8,128)(2,1)}) custom-call(s32[4]{0:T(128)S(1)} %copy-done.4, s32[4]{0:T(128)S(1)} %copy-done.5, s32[4,16]{1,0:T(4,128)S(1)} %copy-done.3, s32[7]{0:T(128)S(1)} %find_sources.1._.source_ref, ...), custom_call_target="tpu_custom_call", output_to_operand_aliasing={{1}: (15, {}), {2}: (16, {})} | custom-call | tf_op jit(solution)/shard_map/place_page/pallas_call | solution.py:673
  53.2 3.1 %collective-permute-done.21 = bf16[4,1792]{1,0:T(4,128)(2,1)S(1)} collective-permute-done((bf16[4,1792]{1,0:T(4,128)(2,1)S(1)}, bf16[4,1792]{1,0:T(4,128)(2,1)S(1)}, u32[]{:S(2)}, u32[]{:S(2)}) %collective-permute-start.21) | collective-permute-done | bytes 14368 | tf_op jit(solution)/shard_map/ppermute | solution.py:30
  56.4 0.6 %fusion.7 = bf16[4,1792]{1,0:T(4,128)(2,1)} fusion(f32[4,1792]{1,0:T(4,128)S(1)} %get-tuple-element.42, f32[4,4,1792]{2,1,0:T(4,128)S(1)} %get-tuple-element.46, bf16[4,1792]{1,0:T(4,128)(2,1)S(1)} %collective-permute-done.21, bf16[4,1792]{1,0:T(4,128)(2,1)S(1)} %collective-permute-done.20, bf16[4,1792]{1,0:T(4,128)(2,1)S(1)} %collective-permute-done.19), kind=kLoop, calls=%fused_computation.18 | loop fusion | flops 57344 | bytes 114688 | tf_op jit(solution)/shard_map/convert_element_type | solution.py:772
  (50 shorter events, 0.3 us)
Async XLA Ops:
  0.6 12.0 %copy-start = (bf16[896,14,384]{2,0,1:T(8,128)(2,1)S(1)}, bf16[896,14,384]{2,0,1:T(8,128)(2,1)}, u32[]{:S(2)}) copy-start(bf16[896,14,384]{2,0,1:T(8,128)(2,1)} %param.16) | copy-start | bytes 28901380
  3.0 1.4 %collective-permute-start = (bf16[4,4,1024]{2,1,0:T(4,128)(2,1)S(1)}, bf16[4,4,1024]{2,1,0:T(4,128)(2,1)S(1)}, u32[]{:S(2)}, u32[]{:S(2)}) collective-permute-start(bf16[4,4,1024]{2,1,0:T(4,128)(2,1)S(1)} %get-tuple-element.25), channel_id=1, source_target_pairs={{0,4},{4,0},{8,12},{12,8},{16,20},{20,16},{24,28},{28,24},{1,5},{5... | collective-permute-start | bytes 98312 | tf_op jit(solution)/shard_map/ppermute | solution.py:30
  3.5 5.5 %collective-permute-start.8 = (bf16[2,32,1792]{2,1,0:T(8,128)(2,1)S(1)}, bf16[2,32,1792]{2,1,0:T(8,128)(2,1)S(1)}, u32[]{:S(2)}, u32[]{:S(2)}) collective-permute-start(bf16[2,32,1792]{2,1,0:T(8,128)(2,1)S(1)} %get-tuple-element.33), channel_id=1, source_target_pairs={{0,4},{4,0},{8,12},{12,8},{16,20},{20,16},{24,28},{28,24},{1,5},{5... | collective-permute-start | bytes 688136 | tf_op jit(solution)/shard_map/ppermute | solution.py:30
  4.4 6.7 %collective-permute-start.3 = (bf16[2,4,1024]{2,1,0:T(4,128)(2,1)S(1)}, bf16[2,4,1024]{2,1,0:T(4,128)(2,1)S(1)}, u32[]{:S(2)}, u32[]{:S(2)}) collective-permute-start(bf16[2,4,1024]{2,1,0:T(4,128)(2,1)S(1)} %pad_maximum_fusion.8), channel_id=1, source_target_pairs={{0,24},{4,28},{8,16},{12,20},{16,8},{20,12},{24,0},{28,4},{1,25},{... | collective-permute-start | bytes 49160 | tf_op jit(solution)/shard_map/ppermute | solution.py:30
  8.3 3.9 %collective-permute-start.2 = (bf16[2,4,1024]{2,1,0:T(4,128)(2,1)S(1)}, bf16[2,4,1024]{2,1,0:T(4,128)(2,1)S(1)}, u32[]{:S(2)}, u32[]{:S(2)}) collective-permute-start(bf16[2,4,1024]{2,1,0:T(4,128)(2,1)S(1)} %pad_maximum_fusion.7), channel_id=1, source_target_pairs={{0,16},{4,20},{8,24},{12,28},{16,0},{20,4},{24,8},{28,12},{1,17},{... | collective-permute-start | bytes 49160 | tf_op jit(solution)/shard_map/ppermute | solution.py:30
  8.9 3.8 %collective-permute-start.1 = (bf16[2,4,1024]{2,1,0:T(4,128)(2,1)S(1)}, bf16[2,4,1024]{2,1,0:T(4,128)(2,1)S(1)}, u32[]{:S(2)}, u32[]{:S(2)}) collective-permute-start(bf16[2,4,1024]{2,1,0:T(4,128)(2,1)S(1)} %pad_maximum_fusion.6), channel_id=1, source_target_pairs={{0,8},{4,12},{8,0},{12,4},{16,24},{20,28},{24,16},{28,20},{1,9},{5... | collective-permute-start | bytes 49160 | tf_op jit(solution)/shard_map/ppermute | solution.py:30
  9.1 11.4 %collective-permute-start.9 = (bf16[2,2,32,1792]{3,2,1,0:T(8,128)(2,1)S(1)}, bf16[2,2,32,1792]{3,2,1,0:T(8,128)(2,1)S(1)}, u32[]{:S(2)}, u32[]{:S(2)}) collective-permute-start(bf16[2,2,32,1792]{3,2,1,0:T(8,128)(2,1)S(1)} %pad_maximum_fusion.refs_0_.refs_6_), channel_id=1, source_target_pairs={{0,8},{4,20},{8,0},{12,28},{16,24},{20,4},{24,16},{28,12},{1,9},{5... | collective-permute-start | bytes 1376264 | tf_op jit(solution)/shard_map/ppermute | solution.py:137
  12.7 11.4 %slice-start = ((s8[4587520]{0:T(1024)(128)(4,1)}), s8[4194304]{0:T(1024)(128)(4,1)S(1)}, s32[]{:S(2)}) async-start(s8[4587520]{0:T(1024)(128)(4,1)} %bitcast.43), calls=%async_computation | async-start | bytes 8388608
  12.7 11.4 %slice-start.2 = ((s8[4587520]{0:T(1024)(128)(4,1)}), s8[4194304]{0:T(1024)(128)(4,1)S(1)}, s32[]{:S(2)}) async-start(s8[4587520]{0:T(1024)(128)(4,1)} %bitcast.45), calls=%async_computation.2 | async-start | bytes 8388608
  12.7 7.7 %copy-start.6 = (f32[14,384]{1,0:T(8,128)S(1)}, f32[14,384]{1,0:T(8,128)}, u32[]{:S(2)}) copy-start(f32[14,384]{1,0:T(8,128)} %param.17) | copy-start | bytes 64516
  12.7 11.3 %slice-start.1 = ((s8[4587520]{0:T(1024)(128)(4,1)}), s8[393216]{0:T(1024)(128)(4,1)S(1)}, s32[]{:S(2)}) async-start(s8[4587520]{0:T(1024)(128)(4,1)} %bitcast.43), calls=%async_computation.1 | async-start | bytes 786432
  12.7 11.3 %slice-start.3 = ((s8[4587520]{0:T(1024)(128)(4,1)}), s8[393216]{0:T(1024)(128)(4,1)S(1)}, s32[]{:S(2)}) async-start(s8[4587520]{0:T(1024)(128)(4,1)} %bitcast.45), calls=%async_computation.3 | async-start | bytes 786432
  12.7 11.3 %copy-start.1 = (bf16[4,7168]{1,0:T(4,128)(2,1)S(1)}, bf16[4,7168]{1,0:T(4,128)(2,1)}, u32[]{:S(2)}) copy-start(bf16[4,7168]{1,0:T(4,128)(2,1)} %refs_4_.1) | copy-start | bytes 172036
  12.7 11.3 %copy-start.3 = (s32[4,16]{1,0:T(4,128)S(1)}, s32[4,16]{1,0:T(4,128)}, u32[]{:S(2)}) copy-start(s32[4,16]{1,0:T(4,128)} %table_ref.3) | copy-start | bytes 772
  12.7 11.3 %copy-start.4 = (s32[4]{0:T(128)S(1)}, s32[4]{0:T(128)}, u32[]{:S(2)}) copy-start(s32[4]{0:T(128)} %length_ref.3) | copy-start | bytes 52
  12.7 11.3 %copy-start.5 = (s32[4]{0:T(128)S(1)}, s32[4]{0:T(128)}, u32[]{:S(2)}) copy-start(s32[4]{0:T(128)} %slot_ref.3) | copy-start | bytes 52
  15.0 1.7 %collective-permute-start.4 = (f32[4,4,5376]{2,1,0:T(4,128)S(1)}, f32[4,4,5376]{2,1,0:T(4,128)S(1)}, u32[]{:S(2)}, u32[]{:S(2)}) collective-permute-start(f32[4,4,5376]{2,1,0:T(4,128)S(1)} %get-tuple-element.27), channel_id=1, source_target_pairs={{0,4},{4,0},{8,12},{12,8},{16,20},{20,16},{24,28},{28,24},{1,5},{5... | collective-permute-start | bytes 1032200 | tf_op jit(solution)/shard_map/ppermute | solution.py:30
  16.8 6.4 %collective-permute-start.5 = (bf16[4,7168]{1,0:T(4,128)(2,1)S(1)}, bf16[4,7168]{1,0:T(4,128)(2,1)S(1)}, u32[]{:S(2)}, u32[]{:S(2)}) collective-permute-start(bf16[4,7168]{1,0:T(4,128)(2,1)S(1)} %get-tuple-element.29), channel_id=1, source_target_pairs={{0,8},{4,12},{8,0},{12,4},{16,24},{20,28},{24,16},{28,20},{1,9},{5... | collective-permute-start | bytes 172040 | tf_op jit(solution)/shard_map/ppermute | solution.py:30
  17.0 6.3 %collective-permute-start.6 = (bf16[4,7168]{1,0:T(4,128)(2,1)S(1)}, bf16[4,7168]{1,0:T(4,128)(2,1)S(1)}, u32[]{:S(2)}, u32[]{:S(2)}) collective-permute-start(bf16[4,7168]{1,0:T(4,128)(2,1)S(1)} %get-tuple-element.30), channel_id=1, source_target_pairs={{0,16},{4,20},{8,24},{12,28},{16,0},{20,4},{24,8},{28,12},{1,17},{... | collective-permute-start | bytes 172040 | tf_op jit(solution)/shard_map/ppermute | solution.py:30
  18.9 5.1 %collective-permute-start.7 = (bf16[4,7168]{1,0:T(4,128)(2,1)S(1)}, bf16[4,7168]{1,0:T(4,128)(2,1)S(1)}, u32[]{:S(2)}, u32[]{:S(2)}) collective-permute-start(bf16[4,7168]{1,0:T(4,128)(2,1)S(1)} %get-tuple-element.31), channel_id=1, source_target_pairs={{0,24},{4,28},{8,16},{12,20},{16,8},{20,12},{24,0},{28,4},{1,25},{... | collective-permute-start | bytes 172040 | tf_op jit(solution)/shard_map/ppermute | solution.py:30
  21.6 16.3 %collective-permute-start.14 = (bf16[2,2,32,1792]{3,2,1,0:T(8,128)(2,1)S(1)}, bf16[2,2,32,1792]{3,2,1,0:T(8,128)(2,1)S(1)}, u32[]{:S(2)}, u32[]{:S(2)}) collective-permute-start(bf16[2,2,32,1792]{3,2,1,0:T(8,128)(2,1)S(1)} %turn_pages.1.refs_11_), channel_id=1, source_target_pairs={{0,16},{4,12},{8,24},{12,4},{16,0},{20,28},{24,8},{28,20},{1,17},{... | collective-permute-start | bytes 1376264 | tf_op jit(solution)/shard_map/ppermute | solution.py:137
  29.1 22.0 %copy-start.2 = (f32[7168]{0:T(1024)S(1)}, f32[7168]{0:T(1024)}, u32[]{:S(2)}) copy-start(f32[7168]{0:T(1024)} %param.19) | copy-start | bytes 86020
  29.1 1.3 %collective-permute-start.10 = (bf16[4,32,256]{2,1,0:T(8,128)(2,1)S(1)}, bf16[4,32,256]{2,1,0:T(8,128)(2,1)S(1)}, u32[]{:S(2)}, u32[]{:S(2)}) collective-permute-start(bf16[4,32,256]{2,1,0:T(8,128)(2,1)S(1)} %get-tuple-element.35), channel_id=1, source_target_pairs={{0,4},{4,0},{8,12},{12,8},{16,20},{20,16},{24,28},{28,24},{1,5},{5... | collective-permute-start | bytes 196616 | tf_op jit(solution)/shard_map/ppermute | solution.py:30
  30.5 4.9 %collective-permute-start.13 = (bf16[2,32,256]{2,1,0:T(8,128)(2,1)S(1)}, bf16[2,32,256]{2,1,0:T(8,128)(2,1)S(1)}, u32[]{:S(2)}, u32[]{:S(2)}) collective-permute-start(bf16[2,32,256]{2,1,0:T(8,128)(2,1)S(1)} %pad_maximum_fusion.4), channel_id=1, source_target_pairs={{0,24},{4,28},{8,16},{12,20},{16,8},{20,12},{24,0},{28,4},{1,25},{... | collective-permute-start | bytes 98312 | tf_op jit(solution)/shard_map/ppermute | solution.py:30
  32.6 3.9 %collective-permute-start.12 = (bf16[2,32,256]{2,1,0:T(8,128)(2,1)S(1)}, bf16[2,32,256]{2,1,0:T(8,128)(2,1)S(1)}, u32[]{:S(2)}, u32[]{:S(2)}) collective-permute-start(bf16[2,32,256]{2,1,0:T(8,128)(2,1)S(1)} %pad_maximum_fusion.3), channel_id=1, source_target_pairs={{0,16},{4,20},{8,24},{12,28},{16,0},{20,4},{24,8},{28,12},{1,17},{... | collective-permute-start | bytes 98312 | tf_op jit(solution)/shard_map/ppermute | solution.py:30
  34.0 3.9 %collective-permute-start.11 = (bf16[2,32,256]{2,1,0:T(8,128)(2,1)S(1)}, bf16[2,32,256]{2,1,0:T(8,128)(2,1)S(1)}, u32[]{:S(2)}, u32[]{:S(2)}) collective-permute-start(bf16[2,32,256]{2,1,0:T(8,128)(2,1)S(1)} %pad_maximum_fusion.2), channel_id=1, source_target_pairs={{0,8},{4,12},{8,0},{12,4},{16,24},{20,28},{24,16},{28,20},{1,9},{5... | collective-permute-start | bytes 98312 | tf_op jit(solution)/shard_map/ppermute | solution.py:30
  39.0 1.6 %collective-permute-start.15 = (bf16[4,4,4,1792]{3,2,1,0:T(4,128)(2,1)S(1)}, bf16[4,4,4,1792]{3,2,1,0:T(4,128)(2,1)S(1)}, u32[]{:S(2)}, u32[]{:S(2)}) collective-permute-start(bf16[4,4,4,1792]{3,2,1,0:T(4,128)(2,1)S(1)} %get-tuple-element.38), channel_id=1, source_target_pairs={{0,4},{4,0},{8,12},{12,8},{16,20},{20,16},{24,28},{28,24},{1,5},{5... | collective-permute-start | bytes 688136 | tf_op jit(solution)/shard_map/ppermute | solution.py:30
  40.8 4.5 %collective-permute-start.16 = (bf16[4,4,1792]{2,1,0:T(4,128)(2,1)S(1)}, bf16[4,4,1792]{2,1,0:T(4,128)(2,1)S(1)}, u32[]{:S(2)}, u32[]{:S(2)}) collective-permute-start(bf16[4,4,1792]{2,1,0:T(4,128)(2,1)S(1)} %get-tuple-element.49), channel_id=1, source_target_pairs={{0,8},{4,12},{8,0},{12,4},{16,24},{20,28},{24,16},{28,20},{1,9},{5... | collective-permute-start | bytes 172040 | tf_op jit(solution)/shard_map/ppermute | solution.py:30
  40.9 4.5 %collective-permute-start.17 = (bf16[4,4,1792]{2,1,0:T(4,128)(2,1)S(1)}, bf16[4,4,1792]{2,1,0:T(4,128)(2,1)S(1)}, u32[]{:S(2)}, u32[]{:S(2)}) collective-permute-start(bf16[4,4,1792]{2,1,0:T(4,128)(2,1)S(1)} %get-tuple-element.51), channel_id=1, source_target_pairs={{0,16},{4,20},{8,24},{12,28},{16,0},{20,4},{24,8},{28,12},{1,17},{... | collective-permute-start | bytes 172040 | tf_op jit(solution)/shard_map/ppermute | solution.py:30
  41.5 5.1 %collective-permute-start.18 = (bf16[4,4,1792]{2,1,0:T(4,128)(2,1)S(1)}, bf16[4,4,1792]{2,1,0:T(4,128)(2,1)S(1)}, u32[]{:S(2)}, u32[]{:S(2)}) collective-permute-start(bf16[4,4,1792]{2,1,0:T(4,128)(2,1)S(1)} %get-tuple-element.50), channel_id=1, source_target_pairs={{0,24},{4,28},{8,16},{12,20},{16,8},{20,12},{24,0},{28,4},{1,25},{... | collective-permute-start | bytes 172040 | tf_op jit(solution)/shard_map/ppermute | solution.py:30
  45.2 6.0 %collective-permute-start.22 = (bf16[2,32,1792]{2,1,0:T(8,128)(2,1)S(1)}, bf16[2,32,1792]{2,1,0:T(8,128)(2,1)S(1)}, u32[]{:S(2)}, u32[]{:S(2)}) collective-permute-start(bf16[2,32,1792]{2,1,0:T(8,128)(2,1)S(1)} %choose_half.1), channel_id=1, source_target_pairs={{0,4},{4,0},{8,12},{12,8},{16,20},{20,16},{24,28},{28,24},{1,5},{5... | collective-permute-start | bytes 688136 | tf_op jit(solution)/shard_map/ppermute | solution.py:30
  46.7 6.5 %collective-permute-start.19 = (bf16[4,1792]{1,0:T(4,128)(2,1)S(1)}, bf16[4,1792]{1,0:T(4,128)(2,1)S(1)}, u32[]{:S(2)}, u32[]{:S(2)}) collective-permute-start(bf16[4,1792]{1,0:T(4,128)(2,1)S(1)} %get-tuple-element.60), channel_id=1, source_target_pairs={{0,1},{1,0},{2,3},{3,2},{4,5},{5,4},{6,7},{7,6},{8,9},{9,8},{10,11... | collective-permute-start | bytes 43016 | tf_op jit(solution)/shard_map/ppermute | solution.py:30
  48.2 5.0 %collective-permute-start.20 = (bf16[4,1792]{1,0:T(4,128)(2,1)S(1)}, bf16[4,1792]{1,0:T(4,128)(2,1)S(1)}, u32[]{:S(2)}, u32[]{:S(2)}) collective-permute-start(bf16[4,1792]{1,0:T(4,128)(2,1)S(1)} %get-tuple-element.62), channel_id=1, source_target_pairs={{0,2},{1,3},{2,0},{3,1},{4,6},{5,7},{6,4},{7,5},{8,10},{9,11},{10,... | collective-permute-start | bytes 43016 | tf_op jit(solution)/shard_map/ppermute | solution.py:30
  50.8 5.5 %collective-permute-start.21 = (bf16[4,1792]{1,0:T(4,128)(2,1)S(1)}, bf16[4,1792]{1,0:T(4,128)(2,1)S(1)}, u32[]{:S(2)}, u32[]{:S(2)}) collective-permute-start(bf16[4,1792]{1,0:T(4,128)(2,1)S(1)} %get-tuple-element.61), channel_id=1, source_target_pairs={{0,3},{1,2},{2,1},{3,0},{4,7},{5,6},{6,5},{7,4},{8,11},{9,10},{10,... | collective-permute-start | bytes 43016 | tf_op jit(solution)/shard_map/ppermute | solution.py:30

commit v8 on v7

--- a/solution.py
+++ b/solution.py
@@ -39,6 +39,32 @@
 
 def in_hbm(*arrays):
     return [pltpu.with_memory_space_constraint(array, pltpu.HBM) for array in arrays]
+
+
+def write_pool(pool, after):
+    parts = 4
+    step = pool.shape[0] // parts
+
+    def kernel(pool_ref, _, out_ref, sems):
+        places = [pl.ds(i * step, step) for i in range(parts)]
+        copies = [
+            pltpu.make_async_copy(pool_ref.at[place], out_ref.at[place], sems.at[i]) for i, place in enumerate(places)
+        ]
+        for copy in copies:
+            copy.start()
+        for copy in copies:
+            copy.wait()
+
+    return pl.pallas_call(
+        kernel,
+        out_shape=jax.ShapeDtypeStruct(pool.shape, pool.dtype),
+        in_specs=[VMEM, ANY],
+        out_specs=HBM,
+        scratch_shapes=[pltpu.SemaphoreType.DMA((parts,))],
+        compiler_params=pltpu.CompilerParams(vmem_limit_bytes=8 * MIB),
+        cost_estimate=cost(0, 2 * pool.size),
+        name="write_pool",
+    )(pool, after)
 
 
 def leaving_slot(new_slot_ref, slots, here):
@@ -145,6 +171,9 @@
     def kernel(*refs):
         block_refs, out_ref = refs[:chips], refs[-1]
         here = lax.axis_index("req")
+        lane = lax.broadcasted_iota(jnp.int32, (8, LANES), 1)
+        found = jnp.zeros((8, LANES), F32)
+        put = lambda j, number: jnp.where(lane == j, number.astype(F32), found)
         turned = (here % 2 == 1) & (across == down)
         for row in range(down):
             for j in range(2):
@@ -152,96 +181,97 @@
                 source = pick(4)
                 chip = source // 2
                 chip = jnp.where(turned, chip % across * across + chip // across, chip)
-                out_ref[2 * row + j] = 2 * chip + source % 2
+                found = put(2 * row + j, 2 * chip + source % 2)
                 if row == 0 and j == 0:
-                    out_ref[2 * down] = pick(2)
-                    out_ref[2 * down + 1] = pick(3)
-                    out_ref[2 * down + 2] = source
-
-    return pl.pallas_call(
-        kernel,
-        out_shape=jax.ShapeDtypeStruct((2 * down + 3,), jnp.int32),
+                    found = put(2 * down, pick(2))
+                    found = put(2 * down + 1, pick(3))
+                    found = put(2 * down + 2, source)
+        out_ref[...] = found
+
+    return pl.pallas_call(
+        kernel,
+        out_shape=jax.ShapeDtypeStruct((8, LANES), F32),
         in_specs=[VMEM] * chips + [ANY],
-        out_specs=SMEM,
+        out_specs=VMEM,
         compiler_params=pltpu.CompilerParams(vmem_limit_bytes=2 * MIB),
         cost_estimate=cost(0, 0),
         name="find_sources",
     )(*spread, after)
 
 
+def number_at(source_ref, j):
+    lane = lax.broadcasted_iota(jnp.int32, (1, LANES), 1)
+    return jnp.sum(jnp.where(lane == j, source_ref[:1, :], 0.0)).astype(jnp.int32)
+
+
 def turn_pages(sources, halves, chips):
     across = len(halves)
     down = chips // across
     shape = halves[0].shape
 
     def kernel(source_ref, *refs):
-        half_refs, out_refs, sems = refs[:across], refs[across:-1], refs[-1]
-        waits = []
+        half_refs, out_refs = refs[:across], refs[across:]
         for row in range(1, down):
             for j in range(2):
-                source = source_ref[2 * row + j]
+                source = number_at(source_ref, 2 * row + j)
                 place = jnp.where(source < 2 * across, source, 0)
                 for d in range(across):
                     for e in range(2):
-                        copy = pltpu.make_async_copy(half_refs[d].at[e], out_refs[row - 1].at[j], sems.at[row - 1, j])
 
                         @pl.when(place == 2 * d + e)
                         def _():
-                            copy.start()
-
-                waits.append(copy)
-        for copy in waits:
-            copy.wait()
+                            out_refs[row - 1][j] = half_refs[d][e]
 
     one = jax.ShapeDtypeStruct(shape, halves[0].dtype)
     return pl.pallas_call(
         kernel,
         out_shape=(one,) * (down - 1),
-        in_specs=[SMEM] + [ANY] * across,
+        in_specs=[VMEM] * (1 + across),
         out_specs=(VMEM,) * (down - 1),
-        scratch_shapes=[pltpu.SemaphoreType.DMA((down - 1, 2))],
-        compiler_params=pltpu.CompilerParams(vmem_limit_bytes=down * 2 * MIB),
+        compiler_params=pltpu.CompilerParams(vmem_limit_bytes=(across + down) * MIB),
         cost_estimate=cost(0, 4 * halves[0].size),
         name="turn_pages",
     )(sources, *halves)
 
 
-def start_half(source, across, core, half_refs, turned_refs, target, sem):
+def with_half(source, across, core, half_refs, turned_refs, use):
     place = jnp.where(source < 2 * across, source, 2 * across + source // (2 * across))
     for d, ref in enumerate(half_refs):
         for e in range(2):
 
             @pl.when(place == 2 * d + e)
             def _():
-                pltpu.make_async_copy(ref.at[e], target, sem).start()
+                use(ref.at[e])
 
     for row, ref in enumerate(turned_refs):
 
         @pl.when(place == 2 * across + row + 1)
         def _():
-            pltpu.make_async_copy(ref.at[core], target, sem).start()
-
-
-def choose_half(sources, halves, turned):
+            use(ref.at[core])
+
+
+def choose_half(sources, halves, turned, after):
     across, rows = len(halves), len(turned)
 
     def kernel(source_ref, *refs):
         half_refs, turned_refs = refs[:across], refs[across : across + rows]
-        out_ref, sem = refs[across + rows :]
-        start_half(source_ref[1], across, 1, half_refs, turned_refs, out_ref, sem)
-        pltpu.make_async_copy(half_refs[0].at[0], out_ref, sem).wait()
+        out_ref = refs[-1]
+
+        def use(ref):
+            out_ref[...] = ref[...]
+
+        with_half(number_at(source_ref, 1), across, 1, half_refs, turned_refs, use)
 
     shape = halves[0].shape[1:]
     return pl.pallas_call(
         kernel,
         out_shape=jax.ShapeDtypeStruct(shape, halves[0].dtype),
-        in_specs=[SMEM] + [ANY] * (across + rows),
+        in_specs=[VMEM] * (1 + across + rows) + [ANY],
         out_specs=VMEM,
-        scratch_shapes=[pltpu.SemaphoreType.DMA],
-        compiler_params=pltpu.CompilerParams(vmem_limit_bytes=2 * MIB),
+        compiler_params=pltpu.CompilerParams(vmem_limit_bytes=(1 + across + rows) * MIB),
         cost_estimate=cost(0, 2 * halves[0].size),
         name="choose_half",
-    )(sources, *halves, *turned)
+    )(sources, *halves, *turned, after)
 
 
 def project(blocks, weight, later):
@@ -338,14 +368,13 @@
     def kernel(*refs):
         length_ref, slot_ref, table_ref = refs[:3]
         sum_refs = refs[3 : 3 + parts]
-        (bias_ref, token_ref, key_ref, value_ref, _, pack_keep, pack_send, patch_ref, key_out, value_out) = refs[
-            3 + parts : 13 + parts
+        (bias_ref, token_ref, key_ref, value_ref, _, pack_keep, pack_send, patch_ref, value_out) = refs[
+            3 + parts : 12 + parts
         ]
-        score_buffer, mix_buffer, out_sems = refs[13 + parts :]
+        score_buffer, mix_buffer, out_sems = refs[12 + parts :]
         step = pages // 4
         writes = [
-            pltpu.make_async_copy(source.at[pl.ds(i * step, step)], target.at[pl.ds(i * step, step)], out_sems.at[n, i])
-            for n, (source, target) in enumerate(((key_ref, key_out), (value_ref, value_out)))
+            pltpu.make_async_copy(value_ref.at[pl.ds(i * step, step)], value_out.at[pl.ds(i * step, step)], out_sems.at[i])
             for i in range(4)
         ]
         for write in writes:
@@ -514,13 +543,13 @@
     pool = jax.ShapeDtypeStruct(key_pool.shape, key_pool.dtype)
     return pl.pallas_call(
         kernel,
-        out_shape=(packed, packed, jax.ShapeDtypeStruct((2, slots, tall, width), BF16), pool, pool),
+        out_shape=(packed, packed, jax.ShapeDtypeStruct((2, slots, tall, width), BF16), pool),
         in_specs=[SMEM] * 3 + [VMEM] * (parts + 4) + [ANY],
-        out_specs=(VMEM, VMEM, VMEM, HBM, HBM),
+        out_specs=(VMEM, VMEM, VMEM, HBM),
         scratch_shapes=[
             pltpu.VMEM((tall, long_rows), F32),
             pltpu.VMEM((tall, width), F32),
-            pltpu.SemaphoreType.DMA((2, 4)),
+            pltpu.SemaphoreType.DMA((4,)),
         ],
         compiler_params=pltpu.CompilerParams(vmem_limit_bytes=18 * MIB),
         cost_estimate=cost(4 * tall * (long_rows + short_rows) * width, 4 * (long_rows + short_rows) * width),
@@ -575,7 +604,7 @@
     return pl.pallas_call(
         kernel,
         out_shape=(jax.ShapeDtypeStruct(shape, F32), jax.ShapeDtypeStruct(shape, BF16)),
-        in_specs=[VMEM] * (chips + 1) + [ANY] * len(after),
+        in_specs=[VMEM] * (chips + 1) + [HBM] * min(1, len(after)) + [ANY] * (len(after) - 1),
         out_specs=(VMEM, VMEM),
         compiler_params=pltpu.CompilerParams(vmem_limit_bytes=10 * MIB),
         cost_estimate=cost(2 * rows * weight.size, 2 * weight.size),
@@ -601,7 +630,7 @@
         half_refs = refs[chips + 2 : chips + 2 + across]
         turned_refs = refs[chips + 2 + across : chips + 2 + across + rows]
         other_ref = refs[chips + 1 + count]
-        _, _, base_ref, key_ref, value_ref, buffer, arrived, sems, out_sems, patch_sems = refs[chips + 2 + count :]
+        _, _, base_ref, key_ref, value_ref, buffer, arrived, out_sems, patch_sems = refs[chips + 2 + count :]
         here = lax.axis_index("req")
         leaving = leaving_slot(slot_ref, slots, here)
 
@@ -619,14 +648,14 @@
                     patch(n, s).start()
 
         column = pl.multiple_of(lax.axis_index("head") * width, LANES)
-        page_at, offset, source = source_ref[2 * down], source_ref[2 * down + 1], source_ref[2 * down + 2]
-        targets = [
-            buffer.at[:, pl.ds(pl.multiple_of((here % 2 ^ e) * half, half), half)] for e in range(2)
-        ]
-        start_half(source_ref[0], across, 0, half_refs, turned_refs, targets[0], sems.at[0])
-        from_core = pltpu.make_async_copy(other_ref, targets[1], sems.at[1])
-        from_core.start()
-
+        page_at, offset, source = [number_at(source_ref, 2 * down + j) for j in range(3)]
+        own_rows, other_rows = [pl.ds(pl.multiple_of((here % 2 ^ e) * half, half), half) for e in range(2)]
+
+        def use(ref):
+            buffer[:, own_rows, :] = ref[...]
+
+        with_half(number_at(source_ref, 0), across, 0, half_refs, turned_refs, use)
+        buffer[:, other_rows, :] = other_ref[...]
         for d in range(chips):
             for e in range(2):
 
@@ -645,8 +674,6 @@
             token_ref[:, pl.ds(column, width)].astype(F32),
         )
         base_ref[...] = token + bias_ref[:, pl.ds(column, width)]
-        pltpu.make_async_copy(half_refs[0].at[0], targets[0], sems.at[0]).wait()
-        from_core.wait()
         first = pl.multiple_of(offset // 16 * 16, 16)
         row = lax.broadcasted_iota(jnp.int32, (16, width), 0)
         for n in range(2):
@@ -673,17 +700,16 @@
     return pl.pallas_call(
         kernel,
         out_shape=(jax.ShapeDtypeStruct((slots, width), F32), shape, shape),
-        in_specs=[SMEM] * 4 + [VMEM] * (chips + 3) + [ANY] * count + [HBM] * 2,
+        in_specs=[SMEM] * 3 + [VMEM] * (chips + 4 + count) + [HBM] * 2,
         out_specs=(VMEM, HBM, HBM),
         scratch_shapes=[
             pltpu.VMEM((2, page, width), BF16),
             pltpu.VMEM(packs[0].shape[1:], F32),
             pltpu.SemaphoreType.DMA((2,)),
-            pltpu.SemaphoreType.DMA((2,)),
             pltpu.SemaphoreType.DMA((2, slots)),
         ],
         input_output_aliases={chips + 7 + count: 1, chips + 8 + count: 2},
-        compiler_params=pltpu.CompilerParams(vmem_limit_bytes=4 * MIB),
+        compiler_params=pltpu.CompilerParams(vmem_limit_bytes=(6 + count) * MIB),
         cost_estimate=cost(0, 8 * page * width),
         name="place_page",
     )(
@@ -728,7 +754,7 @@
     turned = [swap_pages(one, chips, False, row + 1) for row, one in enumerate(turning)]
     sums = [own] + [swap(messages[d - 1], "req", 2 * d) for d in range(1, chips)]
 
-    pack_keep, pack_send, patches, key_out, value_out = attend(
+    pack_keep, pack_send, patches, value_out = attend(
         lengths,
         new_slot,
         page_table,
@@ -741,13 +767,14 @@
     )
     packs_got = swap(pack_send, "req", 1)
     packs = spread_pairs(pack_keep, packs_got)
-
-    from_other = swap(choose_half(sources, halves, turned), "req", 1)
+    key_out = write_pool(key_pool, packs_got)
+
 
     keep, send = out_project(
-        packs, staged, head_groups, slots, turned[0]
+        packs, staged, head_groups, slots, *in_hbm(key_out), turned[0]
     )
     total = keep + swap(send, "req", 1).astype(F32)
+    from_other = swap(choose_half(sources, halves, turned, keep), "req", 1)
     summed = total[0]
     for d in range(1, chips):
         summed = summed + swap(total[d].astype(BF16), "req", 2 * d).astype(F32)
@@ -766,6 +793,7 @@
         key_out,
         value_out,
     )
+    summed, base = lax.optimization_barrier((summed, base))
     hidden = summed[0]
     for j in range(1, head_groups):
         hidden = hidden + swap(summed[j].astype(BF16), "head", j).astype(F32)

time: 57.1 us -> 56.4 us (0.988)
  Pallas kernels: 15.7 us -> 14.9 us
    ppermute x2, starting transfers between devices: 3.62 us -> 2.58 us  [swap_pages(): lax.ppermute(value, 'req', [(i, i ^ steps[i]) for i in range(2 * chips)])]
    ppermute x21, starting transfers between devices: 20.6 us -> 21.5 us  [swap(): return lax.ppermute(value, axis, [(i, i ^ step) for i in range(size)])]
    pallas_call x1, Pallas kernels: 0.88 us -> 0.16 us  [choose_half(): pl.pallas_call(kernel, out_shape=jax.ShapeDtypeStruct(shape, halves[0].dt...]
    pallas_call x2 -> x3, Pallas kernels: 2.07 us -> 2.74 us  [the longest x1 2.17 us: write_pool(): pl.pallas_call(kernel, out_shape=jax.ShapeDtypeStruct(pool.shape, pool.dt...]
  transfers between devices with their start and end apart: 23 -> 23, of which waited for: 13 -> 13; matrix products, arithmetic and copies ran while one was open for 0% -> 1% of each run, Pallas kernels for 22% -> 20%
where the time goes in v8:
time: 56.4 us
  starting transfers between devices  24.1 us (43%)
  waiting for transfers between devices  15.2 us (27%)
  Pallas kernels  14.9 us (26%)
  other arithmetic  1 us (2%)
  between operations  0.99 us (2%)
    ppermute x21, starting transfers between devices, swap(): return lax.ppermute(value, axis, [(i, i ^ step) for i in range(size)])  21.5 us
    ppermute x21, waiting for transfers between devices, swap(): return lax.ppermute(value, axis, [(i, i ^ step) for i in range(size)])  15.2 us
    pallas_call x1, Pallas kernels, attend(): pl.pallas_call(kernel, out_shape=(packed, packed, jax.ShapeDtypeStruct((2...  4.52 us
    ppermute x2, starting transfers between devices, swap_pages(): lax.ppermute(value, 'req', [(i, i ^ steps[i]) for i in range(2 * chips)])  2.58 us
    pallas_call x1, Pallas kernels, prepare(): pl.pallas_call(kernel, out_shape=(blocks, blocks, halves, halves), in_spe...  2.33 us
    pallas_call x1, Pallas kernels, project(): pl.pallas_call(kernel, out_shape=(shape, shape, jax.ShapeDtypeStruct(late...  2.28 us
    pallas_call x1, Pallas kernels, write_pool(): pl.pallas_call(kernel, out_shape=jax.ShapeDtypeStruct(pool.shape, pool.dt...  2.17 us
    pallas_call x1, Pallas kernels, place_page(): pl.pallas_call(kernel, out_shape=(jax.ShapeDtypeStruct((slots, width), F3...  1.76 us
  transfers between devices with their start and end apart: 23, of which 13 were waited for; matrix products, arithmetic and copies ran while one was open for 1% of the time, Pallas kernels for 20%

profile of v8, /device:TPU:0, one launch (start us, length us, event | category | flops | bytes accessed | tf_op | source)
XLA Modules:
  0.0 56.4 jit_solution(14793577402333592628)
XLA Ops:
  0.6 2.3 %prepare.1 = (bf16[4,4,1024]{2,1,0:T(4,128)(2,1)S(1)}, bf16[4,4,1024]{2,1,0:T(4,128)(2,1)S(1)}, bf16[2,32,1792]{2,1,0:T(8,128)(2,1)S(1)}, bf16[2,32,1792]{2,1,0:T(8,128)(2,1)S(1)}) custom-call(bf16[4,7168]{1,0:T(4,128)(2,1)} %refs_4_.1, f32[1,7168]{1,0:T(1,128)} %bitcast.50, f32[1,7168]{1,0:T(1,128)} %bitcast.51, s32[4]{0:T(128)} %length_ref.3, ...), custom_call_target="tpu_custom_call" | custom-call | tf_op jit(solution)/shard_map/prepare/pallas_call | solution.py:129
  3.0 0.5 collective-permute-start
  3.5 0.1 collective-permute-start.8
  3.6 0.8 %collective-permute-done = bf16[4,4,1024]{2,1,0:T(4,128)(2,1)S(1)} collective-permute-done((bf16[4,4,1024]{2,1,0:T(4,128)(2,1)S(1)}, bf16[4,4,1024]{2,1,0:T(4,128)(2,1)S(1)}, u32[]{:S(2)}, u32[]{:S(2)}) %collective-permute-start) | collective-permute-done | bytes 32800 | tf_op jit(solution)/shard_map/ppermute | solution.py:30
  4.4 2.9 %collective-permute-start.1 = (bf16[2,4,1024]{2,1,0:T(4,128)(2,1)S(1)}, bf16[2,4,1024]{2,1,0:T(4,128)(2,1)S(1)}, u32[]{:S(2)}, u32[]{:S(2)}) collective-permute-start(bf16[2,4,1024]{2,1,0:T(4,128)(2,1)S(1)} %pad_maximum_fusion.6), channel_id=1, source_target_pairs={{0,8},{4,12},{8,0},{12,4},{16,24},{20,28},{24,16},{28,20},{1,9},{5... | collective-permute-start | bytes 49160 | tf_op jit(solution)/shard_map/ppermute | solution.py:30
  7.3 1.6 %collective-permute-start.2 = (bf16[2,4,1024]{2,1,0:T(4,128)(2,1)S(1)}, bf16[2,4,1024]{2,1,0:T(4,128)(2,1)S(1)}, u32[]{:S(2)}, u32[]{:S(2)}) collective-permute-start(bf16[2,4,1024]{2,1,0:T(4,128)(2,1)S(1)} %pad_maximum_fusion.7), channel_id=1, source_target_pairs={{0,16},{4,20},{8,24},{12,28},{16,0},{20,4},{24,8},{28,12},{1,17},{... | collective-permute-start | bytes 49160 | tf_op jit(solution)/shard_map/ppermute | solution.py:30
  8.9 0.1 collective-permute-start.3
  9.1 2.0 %collective-permute-start.9 = (bf16[2,2,32,1792]{3,2,1,0:T(8,128)(2,1)S(1)}, bf16[2,2,32,1792]{3,2,1,0:T(8,128)(2,1)S(1)}, u32[]{:S(2)}, u32[]{:S(2)}) collective-permute-start(bf16[2,2,32,1792]{3,2,1,0:T(8,128)(2,1)S(1)} %pad_maximum_fusion.refs_0_.refs_6_), channel_id=1, source_target_pairs={{0,8},{4,20},{8,0},{12,28},{16,24},{20,4},{24,16},{28,12},{1,9},{5... | collective-permute-start | bytes 1376264 | tf_op jit(solution)/shard_map/ppermute | solution.py:163
  11.1 2.6 %collective-permute-done.3.refs_3_ = bf16[2,4,1024]{2,1,0:T(4,128)(2,1)S(1)} collective-permute-done((bf16[2,4,1024]{2,1,0:T(4,128)(2,1)S(1)}, bf16[2,4,1024]{2,1,0:T(4,128)(2,1)S(1)}, u32[]{:S(2)}, u32[]{:S(2)}) %collective-permute-start.3) | collective-permute-done | bytes 16416 | tf_op jit(solution)/shard_map/ppermute | solution.py:30
  13.8 2.3 %project.1 = (f32[4,4,5376]{2,1,0:T(4,128)S(1)}, f32[4,4,5376]{2,1,0:T(4,128)S(1)}, bf16[224,7168]{1,0:T(8,128)(2,1)S(1)}) custom-call(bf16[2,4,1024]{2,1,0:T(4,128)(2,1)S(1)} %pad_maximum_fusion.5.refs_0_, bf16[2,4,1024]{2,1,0:T(4,128)(2,1)S(1)} %collective-permute-done.1.refs_1_, bf16[2,4,1024]{2,1,0:T(4,128)(2,1)S(1)} %collective-permute-done.2.refs_2_, ...), custom_call_target="tpu_custom_call" | custom-call | tf_op jit(solution)/shard_map/project/pallas_call | solution.py:308
  16.1 0.1 collective-permute-start.4
  16.2 0.3 find_sources.1._.source_ref
  16.5 1.4 %collective-permute-done.4.got_ref = f32[4,4,5376]{2,1,0:T(4,128)S(1)} collective-permute-done((f32[4,4,5376]{2,1,0:T(4,128)S(1)}, f32[4,4,5376]{2,1,0:T(4,128)S(1)}, u32[]{:S(2)}, u32[]{:S(2)}) %collective-permute-start.4) | collective-permute-done | bytes 344096 | tf_op jit(solution)/shard_map/ppermute | solution.py:30
  17.8 0.1 combine.1
  17.9 0.6 %collective-permute-start.5 = (bf16[4,7168]{1,0:T(4,128)(2,1)S(1)}, bf16[4,7168]{1,0:T(4,128)(2,1)S(1)}, u32[]{:S(2)}, u32[]{:S(2)}) collective-permute-start(bf16[4,7168]{1,0:T(4,128)(2,1)S(1)} %get-tuple-element.30), channel_id=1, source_target_pairs={{0,8},{4,12},{8,0},{12,4},{16,24},{20,28},{24,16},{28,20},{1,9},{5... | collective-permute-start | bytes 172040 | tf_op jit(solution)/shard_map/ppermute | solution.py:30
  18.5 2.9 %collective-permute-start.7 = (bf16[4,7168]{1,0:T(4,128)(2,1)S(1)}, bf16[4,7168]{1,0:T(4,128)(2,1)S(1)}, u32[]{:S(2)}, u32[]{:S(2)}) collective-permute-start(bf16[4,7168]{1,0:T(4,128)(2,1)S(1)} %get-tuple-element.32), channel_id=1, source_target_pairs={{0,24},{4,28},{8,16},{12,20},{16,8},{20,12},{24,0},{28,4},{1,25},{... | collective-permute-start | bytes 172040 | tf_op jit(solution)/shard_map/ppermute | solution.py:30
  21.5 0.3 turn_pages.1.refs_11_
  21.8 0.6 %collective-permute-start.14 = (bf16[2,2,32,1792]{3,2,1,0:T(8,128)(2,1)S(1)}, bf16[2,2,32,1792]{3,2,1,0:T(8,128)(2,1)S(1)}, u32[]{:S(2)}, u32[]{:S(2)}) collective-permute-start(bf16[2,2,32,1792]{3,2,1,0:T(8,128)(2,1)S(1)} %turn_pages.1.refs_11_), channel_id=1, source_target_pairs={{0,16},{4,12},{8,24},{12,4},{16,0},{20,28},{24,8},{28,20},{1,17},{... | collective-permute-start | bytes 1376264 | tf_op jit(solution)/shard_map/ppermute | solution.py:163
  22.4 1.4 %collective-permute-done.6.refs_5_ = bf16[4,7168]{1,0:T(4,128)(2,1)S(1)} collective-permute-done((bf16[4,7168]{1,0:T(4,128)(2,1)S(1)}, bf16[4,7168]{1,0:T(4,128)(2,1)S(1)}, u32[]{:S(2)}, u32[]{:S(2)}) %collective-permute-start.6) | collective-permute-done | bytes 57376 | tf_op jit(solution)/shard_map/ppermute | solution.py:30
  23.9 4.5 %attend.1 = (bf16[4,32,256]{2,1,0:T(8,128)(2,1)S(1)}, bf16[4,32,256]{2,1,0:T(8,128)(2,1)S(1)}, bf16[2,4,16,1792]{3,2,1,0:T(8,128)(2,1)S(1)}, bf16[20,64,1792]{2,1,0:T(8,128)(2,1)}) custom-call(s32[4]{0:T(128)S(1)} %copy-done.4, s32[4]{0:T(128)S(1)} %copy-done.5, s32[4,16]{1,0:T(4,128)S(1)} %copy-done.3, f32[4,5376]{1,0:T(4,128)S(1)} %get-tuple-element.29.refs_3_, ...), custom_call_target="tpu_custom_call" | custom-call | tf_op jit(solution)/shard_map/attend/pallas_call | solution.py:544
  28.4 0.1 collective-permute-start.10
  28.5 1.2 %collective-permute-done.10._ = bf16[4,32,256]{2,1,0:T(8,128)(2,1)S(1)} collective-permute-done((bf16[4,32,256]{2,1,0:T(8,128)(2,1)S(1)}, bf16[4,32,256]{2,1,0:T(8,128)(2,1)S(1)}, u32[]{:S(2)}, u32[]{:S(2)}) %collective-permute-start.10) | collective-permute-done | bytes 65568 | tf_op jit(solution)/shard_map/ppermute | solution.py:30
  29.7 2.5 %collective-permute-start.11 = (bf16[2,32,256]{2,1,0:T(8,128)(2,1)S(1)}, bf16[2,32,256]{2,1,0:T(8,128)(2,1)S(1)}, u32[]{:S(2)}, u32[]{:S(2)}) collective-permute-start(bf16[2,32,256]{2,1,0:T(8,128)(2,1)S(1)} %pad_maximum_fusion.2), channel_id=1, source_target_pairs={{0,8},{4,12},{8,0},{12,4},{16,24},{20,28},{24,16},{28,20},{1,9},{5... | collective-permute-start | bytes 98312 | tf_op jit(solution)/shard_map/ppermute | solution.py:30
  32.2 0.5 collective-permute-start.12
  32.7 1.1 %collective-permute-start.13 = (bf16[2,32,256]{2,1,0:T(8,128)(2,1)S(1)}, bf16[2,32,256]{2,1,0:T(8,128)(2,1)S(1)}, u32[]{:S(2)}, u32[]{:S(2)}) collective-permute-start(bf16[2,32,256]{2,1,0:T(8,128)(2,1)S(1)} %pad_maximum_fusion.4), channel_id=1, source_target_pairs={{0,24},{4,28},{8,16},{12,20},{16,8},{20,12},{24,0},{28,4},{1,25},{... | collective-permute-start | bytes 98312 | tf_op jit(solution)/shard_map/ppermute | solution.py:30
  33.8 2.2 %write_pool.1.refs_5_.refs_10_ = bf16[20,64,1792]{2,1,0:T(8,128)(2,1)} custom-call(bf16[20,64,1792]{2,1,0:T(8,128)(2,1)S(1)} %bitcast.41, bf16[4,32,256]{2,1,0:T(8,128)(2,1)S(1)} %collective-permute-done.10._), custom_call_target="tpu_custom_call" | custom-call | tf_op jit(solution)/shard_map/write_pool/pallas_call | solution.py:58
  36.0 0.5 collective-permute-done.12.refs_2_
  36.5 1.0 %collective-permute-done.13.refs_3_ = bf16[2,32,256]{2,1,0:T(8,128)(2,1)S(1)} collective-permute-done((bf16[2,32,256]{2,1,0:T(8,128)(2,1)S(1)}, bf16[2,32,256]{2,1,0:T(8,128)(2,1)S(1)}, u32[]{:S(2)}, u32[]{:S(2)}) %collective-permute-start.13) | collective-permute-done | bytes 32800 | tf_op jit(solution)/shard_map/ppermute | solution.py:30
  37.6 1.0 %out_project.1 = (f32[4,4,4,1792]{3,2,1,0:T(4,128)S(1)}, bf16[4,4,4,1792]{3,2,1,0:T(4,128)(2,1)S(1)}) custom-call(bf16[2,32,256]{2,1,0:T(8,128)(2,1)S(1)} %pad_maximum_fusion.1.refs_0_, bf16[2,32,256]{2,1,0:T(8,128)(2,1)S(1)} %collective-permute-done.11.refs_1_, bf16[2,32,256]{2,1,0:T(8,128)(2,1)S(1)} %collective-permute-done.12.refs_2_, ...), custom_call_target="tpu_custom_call" | custom-call | tf_op jit(solution)/shard_map/out_project/pallas_call | solution.py:604
  38.6 0.1 collective-permute-start.15
  38.7 0.2 choose_half.1
  38.8 0.6 collective-permute-start.19
  39.4 0.7 %collective-permute-done.15 = bf16[4,4,4,1792]{3,2,1,0:T(4,128)(2,1)S(1)} collective-permute-done((bf16[4,4,4,1792]{3,2,1,0:T(4,128)(2,1)S(1)}, bf16[4,4,4,1792]{3,2,1,0:T(4,128)(2,1)S(1)}, u32[]{:S(2)}, u32[]{:S(2)}) %collective-permute-start.15) | collective-permute-done | bytes 229408 | tf_op jit(solution)/shard_map/ppermute | solution.py:30
  40.2 0.2 fusion.7
  40.3 0.1 slice_bitcast_fusion.3
  40.4 1.1 %collective-permute-start.18 = (bf16[4,4,1792]{2,1,0:T(4,128)(2,1)S(1)}, bf16[4,4,1792]{2,1,0:T(4,128)(2,1)S(1)}, u32[]{:S(2)}, u32[]{:S(2)}) collective-permute-start(bf16[4,4,1792]{2,1,0:T(4,128)(2,1)S(1)} %get-tuple-element.50), channel_id=1, source_target_pairs={{0,24},{4,28},{8,16},{12,20},{16,8},{20,12},{24,0},{28,4},{1,25},{... | collective-permute-start | bytes 172040 | tf_op jit(solution)/shard_map/ppermute | solution.py:30
  41.5 1.7 %collective-permute-start.17 = (bf16[4,4,1792]{2,1,0:T(4,128)(2,1)S(1)}, bf16[4,4,1792]{2,1,0:T(4,128)(2,1)S(1)}, u32[]{:S(2)}, u32[]{:S(2)}) collective-permute-start(bf16[4,4,1792]{2,1,0:T(4,128)(2,1)S(1)} %get-tuple-element.51), channel_id=1, source_target_pairs={{0,16},{4,20},{8,24},{12,28},{16,0},{20,4},{24,8},{28,12},{1,17},{... | collective-permute-start | bytes 172040 | tf_op jit(solution)/shard_map/ppermute | solution.py:30
  43.2 0.7 %collective-permute-start.16 = (bf16[4,4,1792]{2,1,0:T(4,128)(2,1)S(1)}, bf16[4,4,1792]{2,1,0:T(4,128)(2,1)S(1)}, u32[]{:S(2)}, u32[]{:S(2)}) collective-permute-start(bf16[4,4,1792]{2,1,0:T(4,128)(2,1)S(1)} %get-tuple-element.49), channel_id=1, source_target_pairs={{0,8},{4,12},{8,0},{12,4},{16,24},{20,28},{24,16},{28,20},{1,9},{5... | collective-permute-start | bytes 172040 | tf_op jit(solution)/shard_map/ppermute | solution.py:30
  43.9 1.8 %place_page.1 = (f32[4,1792]{1,0:T(4,128)S(1)}, bf16[20,64,1792]{2,1,0:T(8,128)(2,1)}, bf16[20,64,1792]{2,1,0:T(8,128)(2,1)}) custom-call(s32[4]{0:T(128)S(1)} %copy-done.4, s32[4]{0:T(128)S(1)} %copy-done.5, s32[4,16]{1,0:T(4,128)S(1)} %copy-done.3, f32[8,128]{1,0:T(8,128)S(1)} %find_sources.1._.source_ref, ...), custom_call_target="tpu_custom_call", output_to_operand_aliasing={{1}: (15, {}), {2}: (16, {})} | custom-call | tf_op jit(solution)/shard_map/place_page/pallas_call | solution.py:700
  45.7 0.1 collective-permute-done.18
  45.8 0.6 %collective-permute-done.17 = bf16[4,4,1792]{2,1,0:T(4,128)(2,1)S(1)} collective-permute-done((bf16[4,4,1792]{2,1,0:T(4,128)(2,1)S(1)}, bf16[4,4,1792]{2,1,0:T(4,128)(2,1)S(1)}, u32[]{:S(2)}, u32[]{:S(2)}) %collective-permute-start.17) | collective-permute-done | bytes 57376 | tf_op jit(solution)/shard_map/ppermute | solution.py:30
  46.4 1.0 %collective-permute-done.16 = bf16[4,4,1792]{2,1,0:T(4,128)(2,1)S(1)} collective-permute-done((bf16[4,4,1792]{2,1,0:T(4,128)(2,1)S(1)}, bf16[4,4,1792]{2,1,0:T(4,128)(2,1)S(1)}, u32[]{:S(2)}, u32[]{:S(2)}) %collective-permute-start.16) | collective-permute-done | bytes 57376 | tf_op jit(solution)/shard_map/ppermute | solution.py:30
  47.4 0.1 fusion.2
  47.5 3.7 %collective-permute-start.22 = (bf16[4,1792]{1,0:T(4,128)(2,1)S(1)}, bf16[4,1792]{1,0:T(4,128)(2,1)S(1)}, u32[]{:S(2)}, u32[]{:S(2)}) collective-permute-start(bf16[4,1792]{1,0:T(4,128)(2,1)S(1)} %get-tuple-element.61), channel_id=1, source_target_pairs={{0,3},{1,2},{2,1},{3,0},{4,7},{5,6},{6,5},{7,4},{8,11},{9,10},{10,... | collective-permute-start | bytes 43016 | tf_op jit(solution)/shard_map/ppermute | solution.py:30
  51.2 0.8 %collective-permute-start.20 = (bf16[4,1792]{1,0:T(4,128)(2,1)S(1)}, bf16[4,1792]{1,0:T(4,128)(2,1)S(1)}, u32[]{:S(2)}, u32[]{:S(2)}) collective-permute-start(bf16[4,1792]{1,0:T(4,128)(2,1)S(1)} %get-tuple-element.60), channel_id=1, source_target_pairs={{0,1},{1,0},{2,3},{3,2},{4,5},{5,4},{6,7},{7,6},{8,9},{9,8},{10,11... | collective-permute-start | bytes 43016 | tf_op jit(solution)/shard_map/ppermute | solution.py:30
  52.0 1.1 %collective-permute-done.22 = bf16[4,1792]{1,0:T(4,128)(2,1)S(1)} collective-permute-done((bf16[4,1792]{1,0:T(4,128)(2,1)S(1)}, bf16[4,1792]{1,0:T(4,128)(2,1)S(1)}, u32[]{:S(2)}, u32[]{:S(2)}) %collective-permute-start.22) | collective-permute-done | bytes 14368 | tf_op jit(solution)/shard_map/ppermute | solution.py:30
  53.1 2.7 %collective-permute-done.21 = bf16[4,1792]{1,0:T(4,128)(2,1)S(1)} collective-permute-done((bf16[4,1792]{1,0:T(4,128)(2,1)S(1)}, bf16[4,1792]{1,0:T(4,128)(2,1)S(1)}, u32[]{:S(2)}, u32[]{:S(2)}) %collective-permute-start.21) | collective-permute-done | bytes 14368 | tf_op jit(solution)/shard_map/ppermute | solution.py:30
  55.8 0.6 %fusion.6 = bf16[4,1792]{1,0:T(4,128)(2,1)} fusion(f32[4,1792]{1,0:T(4,128)S(1)} %get-tuple-element.44, bf16[4,1792]{1,0:T(4,128)(2,1)S(1)} %collective-permute-done.22, bf16[4,1792]{1,0:T(4,128)(2,1)S(1)} %collective-permute-done.21, bf16[4,1792]{1,0:T(4,128)(2,1)S(1)} %collective-permute-done.20, f32[4,4,1792]{2,1,0:T(4,128)S(1)} %fusion.2), kind=kLoop, calls=%fused_computation.17 | loop fusion | flops 57344 | bytes 114688 | tf_op jit(solution)/shard_map/convert_element_type | solution.py:800
  (52 shorter events, 0.4 us)
Async XLA Ops:
  0.6 13.1 %copy-start = (bf16[896,14,384]{2,0,1:T(8,128)(2,1)S(1)}, bf16[896,14,384]{2,0,1:T(8,128)(2,1)}, u32[]{:S(2)}) copy-start(bf16[896,14,384]{2,0,1:T(8,128)(2,1)} %param.16) | copy-start | bytes 28901380
  3.0 1.4 %collective-permute-start = (bf16[4,4,1024]{2,1,0:T(4,128)(2,1)S(1)}, bf16[4,4,1024]{2,1,0:T(4,128)(2,1)S(1)}, u32[]{:S(2)}, u32[]{:S(2)}) collective-permute-start(bf16[4,4,1024]{2,1,0:T(4,128)(2,1)S(1)} %get-tuple-element.26), channel_id=1, source_target_pairs={{0,4},{4,0},{8,12},{12,8},{16,20},{20,16},{24,28},{28,24},{1,5},{5... | collective-permute-start | bytes 98312 | tf_op jit(solution)/shard_map/ppermute | solution.py:30
  3.5 5.5 %collective-permute-start.8 = (bf16[2,32,1792]{2,1,0:T(8,128)(2,1)S(1)}, bf16[2,32,1792]{2,1,0:T(8,128)(2,1)S(1)}, u32[]{:S(2)}, u32[]{:S(2)}) collective-permute-start(bf16[2,32,1792]{2,1,0:T(8,128)(2,1)S(1)} %get-tuple-element.34), channel_id=1, source_target_pairs={{0,4},{4,0},{8,12},{12,8},{16,20},{20,16},{24,28},{28,24},{1,5},{5... | collective-permute-start | bytes 688136 | tf_op jit(solution)/shard_map/ppermute | solution.py:30
  4.4 6.7 %collective-permute-start.1 = (bf16[2,4,1024]{2,1,0:T(4,128)(2,1)S(1)}, bf16[2,4,1024]{2,1,0:T(4,128)(2,1)S(1)}, u32[]{:S(2)}, u32[]{:S(2)}) collective-permute-start(bf16[2,4,1024]{2,1,0:T(4,128)(2,1)S(1)} %pad_maximum_fusion.6), channel_id=1, source_target_pairs={{0,8},{4,12},{8,0},{12,4},{16,24},{20,28},{24,16},{28,20},{1,9},{5... | collective-permute-start | bytes 49160 | tf_op jit(solution)/shard_map/ppermute | solution.py:30
  7.3 3.8 %collective-permute-start.2 = (bf16[2,4,1024]{2,1,0:T(4,128)(2,1)S(1)}, bf16[2,4,1024]{2,1,0:T(4,128)(2,1)S(1)}, u32[]{:S(2)}, u32[]{:S(2)}) collective-permute-start(bf16[2,4,1024]{2,1,0:T(4,128)(2,1)S(1)} %pad_maximum_fusion.7), channel_id=1, source_target_pairs={{0,16},{4,20},{8,24},{12,28},{16,0},{20,4},{24,8},{28,12},{1,17},{... | collective-permute-start | bytes 49160 | tf_op jit(solution)/shard_map/ppermute | solution.py:30
  8.9 4.8 %collective-permute-start.3 = (bf16[2,4,1024]{2,1,0:T(4,128)(2,1)S(1)}, bf16[2,4,1024]{2,1,0:T(4,128)(2,1)S(1)}, u32[]{:S(2)}, u32[]{:S(2)}) collective-permute-start(bf16[2,4,1024]{2,1,0:T(4,128)(2,1)S(1)} %pad_maximum_fusion.8), channel_id=1, source_target_pairs={{0,24},{4,28},{8,16},{12,20},{16,8},{20,12},{24,0},{28,4},{1,25},{... | collective-permute-start | bytes 49160 | tf_op jit(solution)/shard_map/ppermute | solution.py:30
  9.1 12.4 %collective-permute-start.9 = (bf16[2,2,32,1792]{3,2,1,0:T(8,128)(2,1)S(1)}, bf16[2,2,32,1792]{3,2,1,0:T(8,128)(2,1)S(1)}, u32[]{:S(2)}, u32[]{:S(2)}) collective-permute-start(bf16[2,2,32,1792]{3,2,1,0:T(8,128)(2,1)S(1)} %pad_maximum_fusion.refs_0_.refs_6_), channel_id=1, source_target_pairs={{0,8},{4,20},{8,0},{12,28},{16,24},{20,4},{24,16},{28,12},{1,9},{5... | collective-permute-start | bytes 1376264 | tf_op jit(solution)/shard_map/ppermute | solution.py:163
  13.7 10.0 %slice-start = ((s8[4587520]{0:T(1024)(128)(4,1)}), s8[4194304]{0:T(1024)(128)(4,1)S(1)}, s32[]{:S(2)}) async-start(s8[4587520]{0:T(1024)(128)(4,1)} %bitcast.40), calls=%async_computation | async-start | bytes 8388608
  13.7 10.0 %slice-start.2 = ((s8[4587520]{0:T(1024)(128)(4,1)}), s8[4194304]{0:T(1024)(128)(4,1)S(1)}, s32[]{:S(2)}) async-start(s8[4587520]{0:T(1024)(128)(4,1)} %bitcast.42), calls=%async_computation.2 | async-start | bytes 8388608
  13.7 7.7 %copy-start.6 = (f32[14,384]{1,0:T(8,128)S(1)}, f32[14,384]{1,0:T(8,128)}, u32[]{:S(2)}) copy-start(f32[14,384]{1,0:T(8,128)} %param.17) | copy-start | bytes 64516
  13.7 10.0 %slice-start.1 = ((s8[4587520]{0:T(1024)(128)(4,1)}), s8[393216]{0:T(1024)(128)(4,1)S(1)}, s32[]{:S(2)}) async-start(s8[4587520]{0:T(1024)(128)(4,1)} %bitcast.40), calls=%async_computation.1 | async-start | bytes 786432
  13.8 10.0 %slice-start.3 = ((s8[4587520]{0:T(1024)(128)(4,1)}), s8[393216]{0:T(1024)(128)(4,1)S(1)}, s32[]{:S(2)}) async-start(s8[4587520]{0:T(1024)(128)(4,1)} %bitcast.42), calls=%async_computation.3 | async-start | bytes 786432
  13.8 10.0 %copy-start.1 = (bf16[4,7168]{1,0:T(4,128)(2,1)S(1)}, bf16[4,7168]{1,0:T(4,128)(2,1)}, u32[]{:S(2)}) copy-start(bf16[4,7168]{1,0:T(4,128)(2,1)} %refs_4_.1) | copy-start | bytes 172036
  13.8 10.0 %copy-start.3 = (s32[4,16]{1,0:T(4,128)S(1)}, s32[4,16]{1,0:T(4,128)}, u32[]{:S(2)}) copy-start(s32[4,16]{1,0:T(4,128)} %table_ref.3) | copy-start | bytes 772
  13.8 10.0 %copy-start.4 = (s32[4]{0:T(128)S(1)}, s32[4]{0:T(128)}, u32[]{:S(2)}) copy-start(s32[4]{0:T(128)} %length_ref.3) | copy-start | bytes 52
  13.8 10.0 %copy-start.5 = (s32[4]{0:T(128)S(1)}, s32[4]{0:T(128)}, u32[]{:S(2)}) copy-start(s32[4]{0:T(128)} %slot_ref.3) | copy-start | bytes 52
  16.1 1.7 %collective-permute-start.4 = (f32[4,4,5376]{2,1,0:T(4,128)S(1)}, f32[4,4,5376]{2,1,0:T(4,128)S(1)}, u32[]{:S(2)}, u32[]{:S(2)}) collective-permute-start(f32[4,4,5376]{2,1,0:T(4,128)S(1)} %get-tuple-element.28), channel_id=1, source_target_pairs={{0,4},{4,0},{8,12},{12,8},{16,20},{20,16},{24,28},{28,24},{1,5},{5... | collective-permute-start | bytes 1032200 | tf_op jit(solution)/shard_map/ppermute | solution.py:30
  17.9 4.5 %collective-permute-start.5 = (bf16[4,7168]{1,0:T(4,128)(2,1)S(1)}, bf16[4,7168]{1,0:T(4,128)(2,1)S(1)}, u32[]{:S(2)}, u32[]{:S(2)}) collective-permute-start(bf16[4,7168]{1,0:T(4,128)(2,1)S(1)} %get-tuple-element.30), channel_id=1, source_target_pairs={{0,8},{4,12},{8,0},{12,4},{16,24},{20,28},{24,16},{28,20},{1,9},{5... | collective-permute-start | bytes 172040 | tf_op jit(solution)/shard_map/ppermute | solution.py:30
  18.5 5.3 %collective-permute-start.6 = (bf16[4,7168]{1,0:T(4,128)(2,1)S(1)}, bf16[4,7168]{1,0:T(4,128)(2,1)S(1)}, u32[]{:S(2)}, u32[]{:S(2)}) collective-permute-start(bf16[4,7168]{1,0:T(4,128)(2,1)S(1)} %get-tuple-element.31), channel_id=1, source_target_pairs={{0,16},{4,20},{8,24},{12,28},{16,0},{20,4},{24,8},{28,12},{1,17},{... | collective-permute-start | bytes 172040 | tf_op jit(solution)/shard_map/ppermute | solution.py:30
  18.5 5.2 %collective-permute-start.7 = (bf16[4,7168]{1,0:T(4,128)(2,1)S(1)}, bf16[4,7168]{1,0:T(4,128)(2,1)S(1)}, u32[]{:S(2)}, u32[]{:S(2)}) collective-permute-start(bf16[4,7168]{1,0:T(4,128)(2,1)S(1)} %get-tuple-element.32), channel_id=1, source_target_pairs={{0,24},{4,28},{8,16},{12,20},{16,8},{20,12},{24,0},{28,4},{1,25},{... | collective-permute-start | bytes 172040 | tf_op jit(solution)/shard_map/ppermute | solution.py:30
  21.8 15.8 %collective-permute-start.14 = (bf16[2,2,32,1792]{3,2,1,0:T(8,128)(2,1)S(1)}, bf16[2,2,32,1792]{3,2,1,0:T(8,128)(2,1)S(1)}, u32[]{:S(2)}, u32[]{:S(2)}) collective-permute-start(bf16[2,2,32,1792]{3,2,1,0:T(8,128)(2,1)S(1)} %turn_pages.1.refs_11_), channel_id=1, source_target_pairs={{0,16},{4,12},{8,24},{12,4},{16,0},{20,28},{24,8},{28,20},{1,17},{... | collective-permute-start | bytes 1376264 | tf_op jit(solution)/shard_map/ppermute | solution.py:163
  28.4 1.3 %collective-permute-start.10 = (bf16[4,32,256]{2,1,0:T(8,128)(2,1)S(1)}, bf16[4,32,256]{2,1,0:T(8,128)(2,1)S(1)}, u32[]{:S(2)}, u32[]{:S(2)}) collective-permute-start(bf16[4,32,256]{2,1,0:T(8,128)(2,1)S(1)} %get-tuple-element.36), channel_id=1, source_target_pairs={{0,4},{4,0},{8,12},{12,8},{16,20},{20,16},{24,28},{28,24},{1,5},{5... | collective-permute-start | bytes 196616 | tf_op jit(solution)/shard_map/ppermute | solution.py:30
  29.7 6.3 %collective-permute-start.11 = (bf16[2,32,256]{2,1,0:T(8,128)(2,1)S(1)}, bf16[2,32,256]{2,1,0:T(8,128)(2,1)S(1)}, u32[]{:S(2)}, u32[]{:S(2)}) collective-permute-start(bf16[2,32,256]{2,1,0:T(8,128)(2,1)S(1)} %pad_maximum_fusion.2), channel_id=1, source_target_pairs={{0,8},{4,12},{8,0},{12,4},{16,24},{20,28},{24,16},{28,20},{1,9},{5... | collective-permute-start | bytes 98312 | tf_op jit(solution)/shard_map/ppermute | solution.py:30
  32.2 4.3 %collective-permute-start.12 = (bf16[2,32,256]{2,1,0:T(8,128)(2,1)S(1)}, bf16[2,32,256]{2,1,0:T(8,128)(2,1)S(1)}, u32[]{:S(2)}, u32[]{:S(2)}) collective-permute-start(bf16[2,32,256]{2,1,0:T(8,128)(2,1)S(1)} %pad_maximum_fusion.3), channel_id=1, source_target_pairs={{0,16},{4,20},{8,24},{12,28},{16,0},{20,4},{24,8},{28,12},{1,17},{... | collective-permute-start | bytes 98312 | tf_op jit(solution)/shard_map/ppermute | solution.py:30
  32.7 4.8 %collective-permute-start.13 = (bf16[2,32,256]{2,1,0:T(8,128)(2,1)S(1)}, bf16[2,32,256]{2,1,0:T(8,128)(2,1)S(1)}, u32[]{:S(2)}, u32[]{:S(2)}) collective-permute-start(bf16[2,32,256]{2,1,0:T(8,128)(2,1)S(1)} %pad_maximum_fusion.4), channel_id=1, source_target_pairs={{0,24},{4,28},{8,16},{12,20},{16,8},{20,12},{24,0},{28,4},{1,25},{... | collective-permute-start | bytes 98312 | tf_op jit(solution)/shard_map/ppermute | solution.py:30
  37.6 6.4 %copy-start.2 = (f32[7168]{0:T(1024)S(1)}, f32[7168]{0:T(1024)}, u32[]{:S(2)}) copy-start(f32[7168]{0:T(1024)} %param.19) | copy-start | bytes 86020
  38.6 1.6 %collective-permute-start.15 = (bf16[4,4,4,1792]{3,2,1,0:T(4,128)(2,1)S(1)}, bf16[4,4,4,1792]{3,2,1,0:T(4,128)(2,1)S(1)}, u32[]{:S(2)}, u32[]{:S(2)}) collective-permute-start(bf16[4,4,4,1792]{3,2,1,0:T(4,128)(2,1)S(1)} %get-tuple-element.39), channel_id=1, source_target_pairs={{0,4},{4,0},{8,12},{12,8},{16,20},{20,16},{24,28},{28,24},{1,5},{5... | collective-permute-start | bytes 688136 | tf_op jit(solution)/shard_map/ppermute | solution.py:30
  38.8 5.1 %collective-permute-start.19 = (bf16[2,32,1792]{2,1,0:T(8,128)(2,1)S(1)}, bf16[2,32,1792]{2,1,0:T(8,128)(2,1)S(1)}, u32[]{:S(2)}, u32[]{:S(2)}) collective-permute-start(bf16[2,32,1792]{2,1,0:T(8,128)(2,1)S(1)} %choose_half.1), channel_id=1, source_target_pairs={{0,4},{4,0},{8,12},{12,8},{16,20},{20,16},{24,28},{28,24},{1,5},{5... | collective-permute-start | bytes 688136 | tf_op jit(solution)/shard_map/ppermute | solution.py:30
  40.4 5.4 %collective-permute-start.18 = (bf16[4,4,1792]{2,1,0:T(4,128)(2,1)S(1)}, bf16[4,4,1792]{2,1,0:T(4,128)(2,1)S(1)}, u32[]{:S(2)}, u32[]{:S(2)}) collective-permute-start(bf16[4,4,1792]{2,1,0:T(4,128)(2,1)S(1)} %get-tuple-element.50), channel_id=1, source_target_pairs={{0,24},{4,28},{8,16},{12,20},{16,8},{20,12},{24,0},{28,4},{1,25},{... | collective-permute-start | bytes 172040 | tf_op jit(solution)/shard_map/ppermute | solution.py:30
  41.5 4.9 %collective-permute-start.17 = (bf16[4,4,1792]{2,1,0:T(4,128)(2,1)S(1)}, bf16[4,4,1792]{2,1,0:T(4,128)(2,1)S(1)}, u32[]{:S(2)}, u32[]{:S(2)}) collective-permute-start(bf16[4,4,1792]{2,1,0:T(4,128)(2,1)S(1)} %get-tuple-element.51), channel_id=1, source_target_pairs={{0,16},{4,20},{8,24},{12,28},{16,0},{20,4},{24,8},{28,12},{1,17},{... | collective-permute-start | bytes 172040 | tf_op jit(solution)/shard_map/ppermute | solution.py:30
  43.2 4.2 %collective-permute-start.16 = (bf16[4,4,1792]{2,1,0:T(4,128)(2,1)S(1)}, bf16[4,4,1792]{2,1,0:T(4,128)(2,1)S(1)}, u32[]{:S(2)}, u32[]{:S(2)}) collective-permute-start(bf16[4,4,1792]{2,1,0:T(4,128)(2,1)S(1)} %get-tuple-element.49), channel_id=1, source_target_pairs={{0,8},{4,12},{8,0},{12,4},{16,24},{20,28},{24,16},{28,20},{1,9},{5... | collective-permute-start | bytes 172040 | tf_op jit(solution)/shard_map/ppermute | solution.py:30
  47.5 5.6 %collective-permute-start.22 = (bf16[4,1792]{1,0:T(4,128)(2,1)S(1)}, bf16[4,1792]{1,0:T(4,128)(2,1)S(1)}, u32[]{:S(2)}, u32[]{:S(2)}) collective-permute-start(bf16[4,1792]{1,0:T(4,128)(2,1)S(1)} %get-tuple-element.61), channel_id=1, source_target_pairs={{0,3},{1,2},{2,1},{3,0},{4,7},{5,6},{6,5},{7,4},{8,11},{9,10},{10,... | collective-permute-start | bytes 43016 | tf_op jit(solution)/shard_map/ppermute | solution.py:30
  51.2 4.6 %collective-permute-start.21 = (bf16[4,1792]{1,0:T(4,128)(2,1)S(1)}, bf16[4,1792]{1,0:T(4,128)(2,1)S(1)}, u32[]{:S(2)}, u32[]{:S(2)}) collective-permute-start(bf16[4,1792]{1,0:T(4,128)(2,1)S(1)} %get-tuple-element.62), channel_id=1, source_target_pairs={{0,2},{1,3},{2,0},{3,1},{4,6},{5,7},{6,4},{7,5},{8,10},{9,11},{10,... | collective-permute-start | bytes 43016 | tf_op jit(solution)/shard_map/ppermute | solution.py:30
  51.2 4.6 %collective-permute-start.20 = (bf16[4,1792]{1,0:T(4,128)(2,1)S(1)}, bf16[4,1792]{1,0:T(4,128)(2,1)S(1)}, u32[]{:S(2)}, u32[]{:S(2)}) collective-permute-start(bf16[4,1792]{1,0:T(4,128)(2,1)S(1)} %get-tuple-element.60), channel_id=1, source_target_pairs={{0,1},{1,0},{2,3},{3,2},{4,5},{5,4},{6,7},{7,6},{8,9},{9,8},{10,11... | collective-permute-start | bytes 43016 | tf_op jit(solution)/shard_map/ppermute | solution.py:30

commit v9 on v8

--- a/solution.py
+++ b/solution.py
@@ -204,13 +204,13 @@
     return jnp.sum(jnp.where(lane == j, source_ref[:1, :], 0.0)).astype(jnp.int32)
 
 
-def turn_pages(sources, halves, chips):
+def turn_pages(sources, halves, chips, after):
     across = len(halves)
     down = chips // across
     shape = halves[0].shape
 
     def kernel(source_ref, *refs):
-        half_refs, out_refs = refs[:across], refs[across:]
+        half_refs, out_refs = refs[:across], refs[across + len(after) :]
         for row in range(1, down):
             for j in range(2):
                 source = number_at(source_ref, 2 * row + j)
@@ -226,12 +226,12 @@
     return pl.pallas_call(
         kernel,
         out_shape=(one,) * (down - 1),
-        in_specs=[VMEM] * (1 + across),
+        in_specs=[VMEM] * (1 + across) + [ANY] * len(after),
         out_specs=(VMEM,) * (down - 1),
         compiler_params=pltpu.CompilerParams(vmem_limit_bytes=(across + down) * MIB),
         cost_estimate=cost(0, 4 * halves[0].size),
         name="turn_pages",
-    )(sources, *halves)
+    )(sources, *halves, *after)
 
 
 def with_half(source, across, core, half_refs, turned_refs, use):
@@ -346,7 +346,7 @@
     )(keep, got, after)
 
 
-def attend(lengths, new_slot, page_table, sums, bias, tokens, key_pool, value_pool, after):
+def attend(lengths, new_slot, page_table, sums, bias, tokens, key_pool, value_pool, written, after):
     parts = len(sums)
     slots = sums[0].shape[0]
     pages, page, width = key_pool.shape
@@ -368,17 +368,9 @@
     def kernel(*refs):
         length_ref, slot_ref, table_ref = refs[:3]
         sum_refs = refs[3 : 3 + parts]
-        (bias_ref, token_ref, key_ref, value_ref, _, pack_keep, pack_send, patch_ref, value_out) = refs[
-            3 + parts : 12 + parts
+        (bias_ref, token_ref, key_ref, value_ref, _, _, pack_keep, pack_send, patch_ref, score_buffer, mix_buffer) = refs[
+            3 + parts :
         ]
-        score_buffer, mix_buffer, out_sems = refs[12 + parts :]
-        step = pages // 4
-        writes = [
-            pltpu.make_async_copy(value_ref.at[pl.ds(i * step, step)], value_out.at[pl.ds(i * step, step)], out_sems.at[i])
-            for i in range(4)
-        ]
-        for write in writes:
-            write.start()
         here = lax.axis_index("req")
         column_block = lax.axis_index("head")
         leaving = leaving_slot(slot_ref, slots, here)
@@ -536,25 +528,20 @@
                 new = jnp.broadcast_to(new_rows[n][s : s + 1], (tall, width))
                 patch_ref[n, s] = jnp.where(at == offset - first, new, old).astype(BF16)
 
-        for write in writes:
-            write.wait()
-
     packed = jax.ShapeDtypeStruct((parts, pack_rows(slots, strips), PACK), BF16)
-    pool = jax.ShapeDtypeStruct(key_pool.shape, key_pool.dtype)
-    return pl.pallas_call(
-        kernel,
-        out_shape=(packed, packed, jax.ShapeDtypeStruct((2, slots, tall, width), BF16), pool),
-        in_specs=[SMEM] * 3 + [VMEM] * (parts + 4) + [ANY],
-        out_specs=(VMEM, VMEM, VMEM, HBM),
+    return pl.pallas_call(
+        kernel,
+        out_shape=(packed, packed, jax.ShapeDtypeStruct((2, slots, tall, width), BF16)),
+        in_specs=[SMEM] * 3 + [VMEM] * (parts + 4) + [HBM, ANY],
+        out_specs=(VMEM, VMEM, VMEM),
         scratch_shapes=[
             pltpu.VMEM((tall, long_rows), F32),
             pltpu.VMEM((tall, width), F32),
-            pltpu.SemaphoreType.DMA((4,)),
         ],
         compiler_params=pltpu.CompilerParams(vmem_limit_bytes=18 * MIB),
         cost_estimate=cost(4 * tall * (long_rows + short_rows) * width, 4 * (long_rows + short_rows) * width),
         name="attend",
-    )(lengths, new_slot, page_table, *sums, bias, tokens, key_pool, value_pool, after)
+    )(lengths, new_slot, page_table, *sums, bias, tokens, key_pool, value_pool, *in_hbm(written), after)
 
 
 def pack_rows(slots, strips):
@@ -741,20 +728,23 @@
         tokens, norm_gain[None], norm_shift[None], lengths, page_table, new_slot, new_page, key_pool, value_pool
     )
     got = swap(send, "req", 1)
+    across = row_length(chips)
+    send_half, got = lax.optimization_barrier((send_half, got))
     spread = spread_pairs(keep, got)
-    across = row_length(chips)
     halves = [jnp.stack([keep_half, swap(send_half, "req", 1)])]
+    halves[0], *spread = lax.optimization_barrier((halves[0], *spread))
     halves += [swap_pages(halves[0], chips, True, d) for d in range(1, across)]
     flat = out_weight.reshape(-1, out_weight.shape[2])
     keep, send, staged = project(spread, jnp.transpose(qkv_weight, (1, 0, 2)), flat)
     got = swap(send, "req", 1)
     sources = find_sources(spread, keep)
     own, *messages = combine(keep, got, sources)
-    turning = turn_pages(sources, halves, chips)
+    sums = [own] + [swap(messages[d - 1], "req", 2 * d) for d in range(1, chips)]
+    value_out = write_pool(value_pool, own)
+    turning = turn_pages(sources, halves, chips, sums[1:])
     turned = [swap_pages(one, chips, False, row + 1) for row, one in enumerate(turning)]
-    sums = [own] + [swap(messages[d - 1], "req", 2 * d) for d in range(1, chips)]
-
-    pack_keep, pack_send, patches, value_out = attend(
+
+    pack_keep, pack_send, patches = attend(
         lengths,
         new_slot,
         page_table,
@@ -763,6 +753,7 @@
         tokens,
         key_pool,
         value_pool,
+        value_out,
         turning[0],
     )
     packs_got = swap(pack_send, "req", 1)
@@ -794,9 +785,11 @@
         value_out,
     )
     summed, base = lax.optimization_barrier((summed, base))
+    count = head_groups
+    while count > 1:
+        count //= 2
+        summed = summed[:count] + swap(summed[count : 2 * count].astype(BF16), "head", count).astype(F32)
     hidden = summed[0]
-    for j in range(1, head_groups):
-        hidden = hidden + swap(summed[j].astype(BF16), "head", j).astype(F32)
     hidden_out = (hidden + base).astype(BF16)
     return (hidden_out, key_out, value_out)
 

time: 56.4 us -> 58.3 us (1.034)
  Pallas kernels: 14.9 us -> 17.2 us
  starting transfers between devices: 24.1 us -> 23.1 us
  waiting for transfers between devices: 15.2 us -> 16.1 us
    pallas_call x1 -> x2, Pallas kernels: 2.17 us -> 4.54 us  [write_pool(): pl.pallas_call(kernel, out_shape=jax.ShapeDtypeStruct(pool.shape, pool.dt...]
    ppermute x21 -> x20, waiting for transfers between devices: 15.2 us -> 16.1 us  [swap(): return lax.ppermute(value, axis, [(i, i ^ step) for i in range(size)])]
    ppermute x21 -> x20, starting transfers between devices: 21.5 us -> 20.9 us  [swap(): return lax.ppermute(value, axis, [(i, i ^ step) for i in range(size)])]
  transfers between devices with their start and end apart: 23 -> 22, of which waited for: 13 -> 12; matrix products, arithmetic and copies ran while one was open for 1% -> 1% of each run, Pallas kernels for 20% -> 23%
where the time goes in v9:
time: 58.3 us; the launch traced here: 58.6 us
  starting transfers between devices  23.1 us (40%)
  Pallas kernels  17.2 us (30%)
  waiting for transfers between devices  16.1 us (28%)
  between operations  1.04 us (2%)
  other arithmetic  0.98 us (2%)
    ppermute x20, starting transfers between devices, swap(): return lax.ppermute(value, axis, [(i, i ^ step) for i in range(size)])  20.9 us
    ppermute x20, waiting for transfers between devices, swap(): return lax.ppermute(value, axis, [(i, i ^ step) for i in range(size)])  16.1 us
    pallas_call x2, Pallas kernels, write_pool(): pl.pallas_call(kernel, out_shape=jax.ShapeDtypeStruct(pool.shape, pool.dt...  4.54 us
    pallas_call x1, Pallas kernels, attend(): pl.pallas_call(kernel, out_shape=(packed, packed, jax.ShapeDtypeStruct((2...  4.48 us
    pallas_call x1, Pallas kernels, prepare(): pl.pallas_call(kernel, out_shape=(blocks, blocks, halves, halves), in_spe...  2.33 us
    pallas_call x1, Pallas kernels, project(): pl.pallas_call(kernel, out_shape=(shape, shape, jax.ShapeDtypeStruct(late...  2.27 us
    ppermute x2, starting transfers between devices, swap_pages(): lax.ppermute(value, 'req', [(i, i ^ steps[i]) for i in range(2 * chips)])  2.12 us
    pallas_call x1, Pallas kernels, place_page(): pl.pallas_call(kernel, out_shape=(jax.ShapeDtypeStruct((slots, width), F3...  1.76 us
  transfers between devices with their start and end apart: 22, of which 12 were waited for; matrix products, arithmetic and copies ran while one was open for 1% of the time, Pallas kernels for 23%

profile of v9, /device:TPU:0, one launch (start us, length us, event | category | flops | bytes accessed | tf_op | source)
XLA Modules:
  0.0 58.6 jit_solution(5649238534104696672)
XLA Ops:
  0.6 2.3 %prepare.1 = (bf16[4,4,1024]{2,1,0:T(4,128)(2,1)S(1)}, bf16[4,4,1024]{2,1,0:T(4,128)(2,1)S(1)}, bf16[2,32,1792]{2,1,0:T(8,128)(2,1)S(1)}, bf16[2,32,1792]{2,1,0:T(8,128)(2,1)S(1)}) custom-call(bf16[4,7168]{1,0:T(4,128)(2,1)} %refs_4_.1, f32[1,7168]{1,0:T(1,128)} %bitcast.40, f32[1,7168]{1,0:T(1,128)} %bitcast.41, s32[4]{0:T(128)} %length_ref.3, ...), custom_call_target="tpu_custom_call" | custom-call | tf_op jit(solution)/shard_map/prepare/pallas_call | solution.py:129
  3.0 0.5 collective-permute-start
  3.5 0.8 %collective-permute-done = bf16[4,4,1024]{2,1,0:T(4,128)(2,1)S(1)} collective-permute-done((bf16[4,4,1024]{2,1,0:T(4,128)(2,1)S(1)}, bf16[4,4,1024]{2,1,0:T(4,128)(2,1)S(1)}, u32[]{:S(2)}, u32[]{:S(2)}) %collective-permute-start) | collective-permute-done | bytes 32800 | tf_op jit(solution)/shard_map/ppermute | solution.py:30
  4.4 0.3 collective-permute-start.1
  4.7 2.7 %collective-permute-start.2 = (bf16[2,4,1024]{2,1,0:T(4,128)(2,1)S(1)}, bf16[2,4,1024]{2,1,0:T(4,128)(2,1)S(1)}, u32[]{:S(2)}, u32[]{:S(2)}) collective-permute-start(bf16[2,4,1024]{2,1,0:T(4,128)(2,1)S(1)} %pad_maximum_fusion.6), channel_id=1, source_target_pairs={{0,8},{4,12},{8,0},{12,4},{16,24},{20,28},{24,16},{28,20},{1,9},{5... | collective-permute-start | bytes 49160 | tf_op jit(solution)/shard_map/ppermute | solution.py:30
  7.5 1.6 %collective-permute-start.3 = (bf16[2,4,1024]{2,1,0:T(4,128)(2,1)S(1)}, bf16[2,4,1024]{2,1,0:T(4,128)(2,1)S(1)}, u32[]{:S(2)}, u32[]{:S(2)}) collective-permute-start(bf16[2,4,1024]{2,1,0:T(4,128)(2,1)S(1)} %pad_maximum_fusion.7), channel_id=1, source_target_pairs={{0,16},{4,20},{8,24},{12,28},{16,0},{20,4},{24,8},{28,12},{1,17},{... | collective-permute-start | bytes 49160 | tf_op jit(solution)/shard_map/ppermute | solution.py:30
  9.1 0.1 collective-permute-start.4
  9.3 2.0 %collective-permute-done.3.refs_2_ = bf16[2,4,1024]{2,1,0:T(4,128)(2,1)S(1)} collective-permute-done((bf16[2,4,1024]{2,1,0:T(4,128)(2,1)S(1)}, bf16[2,4,1024]{2,1,0:T(4,128)(2,1)S(1)}, u32[]{:S(2)}, u32[]{:S(2)}) %collective-permute-start.3) | collective-permute-done | bytes 16416 | tf_op jit(solution)/shard_map/ppermute | solution.py:30
  11.3 2.5 %collective-permute-done.4.refs_3_ = bf16[2,4,1024]{2,1,0:T(4,128)(2,1)S(1)} collective-permute-done((bf16[2,4,1024]{2,1,0:T(4,128)(2,1)S(1)}, bf16[2,4,1024]{2,1,0:T(4,128)(2,1)S(1)}, u32[]{:S(2)}, u32[]{:S(2)}) %collective-permute-start.4) | collective-permute-done | bytes 16416 | tf_op jit(solution)/shard_map/ppermute | solution.py:30
  13.8 0.5 collective-permute-start.9
  14.3 2.3 %project.1 = (f32[4,4,5376]{2,1,0:T(4,128)S(1)}, f32[4,4,5376]{2,1,0:T(4,128)S(1)}, bf16[224,7168]{1,0:T(8,128)(2,1)S(1)}) custom-call(bf16[2,4,1024]{2,1,0:T(4,128)(2,1)S(1)} %pad_maximum_fusion.5.refs_0_, bf16[2,4,1024]{2,1,0:T(4,128)(2,1)S(1)} %collective-permute-done.2.refs_1_, bf16[2,4,1024]{2,1,0:T(4,128)(2,1)S(1)} %collective-permute-done.3.refs_2_, ...), custom_call_target="tpu_custom_call" | custom-call | tf_op jit(solution)/shard_map/project/pallas_call | solution.py:308
  16.6 0.1 collective-permute-start.5
  16.7 0.3 find_sources.1._.source_ref
  17.0 1.4 %collective-permute-done.5.got_ref = f32[4,4,5376]{2,1,0:T(4,128)S(1)} collective-permute-done((f32[4,4,5376]{2,1,0:T(4,128)S(1)}, f32[4,4,5376]{2,1,0:T(4,128)S(1)}, u32[]{:S(2)}, u32[]{:S(2)}) %collective-permute-start.5) | collective-permute-done | bytes 344096 | tf_op jit(solution)/shard_map/ppermute | solution.py:30
  18.3 0.1 combine.1
  18.4 1.6 %collective-permute-start.6 = (bf16[4,7168]{1,0:T(4,128)(2,1)S(1)}, bf16[4,7168]{1,0:T(4,128)(2,1)S(1)}, u32[]{:S(2)}, u32[]{:S(2)}) collective-permute-start(bf16[4,7168]{1,0:T(4,128)(2,1)S(1)} %get-tuple-element.44), channel_id=1, source_target_pairs={{0,8},{4,12},{8,0},{12,4},{16,24},{20,28},{24,16},{28,20},{1,9},{5... | collective-permute-start | bytes 172040 | tf_op jit(solution)/shard_map/ppermute | solution.py:30
  20.0 0.5 collective-permute-start.7
  20.5 1.5 %collective-permute-start.8 = (bf16[4,7168]{1,0:T(4,128)(2,1)S(1)}, bf16[4,7168]{1,0:T(4,128)(2,1)S(1)}, u32[]{:S(2)}, u32[]{:S(2)}) collective-permute-start(bf16[4,7168]{1,0:T(4,128)(2,1)S(1)} %get-tuple-element.46), channel_id=1, source_target_pairs={{0,24},{4,28},{8,16},{12,20},{16,8},{20,12},{24,0},{28,4},{1,25},{... | collective-permute-start | bytes 172040 | tf_op jit(solution)/shard_map/ppermute | solution.py:30
  22.1 2.4 %write_pool.2.refs_11_ = bf16[20,64,1792]{2,1,0:T(8,128)(2,1)} custom-call(bf16[20,64,1792]{2,1,0:T(8,128)(2,1)S(1)} %bitcast.31, f32[4,5376]{1,0:T(4,128)S(1)} %get-tuple-element.43._.refs_3_), custom_call_target="tpu_custom_call" | custom-call | tf_op jit(solution)/shard_map/write_pool/pallas_call | solution.py:58
  24.5 0.3 collective-permute-done.7.refs_3_.refs_5_
  24.7 0.8 %collective-permute-done.8.refs_4_.refs_6_ = bf16[4,7168]{1,0:T(4,128)(2,1)S(1)} collective-permute-done((bf16[4,7168]{1,0:T(4,128)(2,1)S(1)}, bf16[4,7168]{1,0:T(4,128)(2,1)S(1)}, u32[]{:S(2)}, u32[]{:S(2)}) %collective-permute-start.8) | collective-permute-done | bytes 57376 | tf_op jit(solution)/shard_map/ppermute | solution.py:30
  25.5 0.3 turn_pages.1.refs_12_
  25.9 1.6 %collective-permute-start.14 = (bf16[2,2,32,1792]{3,2,1,0:T(8,128)(2,1)S(1)}, bf16[2,2,32,1792]{3,2,1,0:T(8,128)(2,1)S(1)}, u32[]{:S(2)}, u32[]{:S(2)}) collective-permute-start(bf16[2,2,32,1792]{3,2,1,0:T(8,128)(2,1)S(1)} %turn_pages.1.refs_12_), channel_id=1, source_target_pairs={{0,16},{4,12},{8,24},{12,4},{16,0},{20,28},{24,8},{28,20},{1,17},{... | collective-permute-start | bytes 1376264 | tf_op jit(solution)/shard_map/ppermute | solution.py:163
  27.5 4.5 %attend.1 = (bf16[4,32,256]{2,1,0:T(8,128)(2,1)S(1)}, bf16[4,32,256]{2,1,0:T(8,128)(2,1)S(1)}, bf16[2,4,16,1792]{3,2,1,0:T(8,128)(2,1)S(1)}) custom-call(s32[4]{0:T(128)S(1)} %copy-done.4, s32[4]{0:T(128)S(1)} %copy-done.5, s32[4,16]{1,0:T(4,128)S(1)} %copy-done.3, f32[4,5376]{1,0:T(4,128)S(1)} %get-tuple-element.43._.refs_3_, ...), custom_call_target="tpu_custom_call" | custom-call | tf_op jit(solution)/shard_map/attend/pallas_call | solution.py:532
  32.0 0.1 collective-permute-start.10
  32.1 1.2 %collective-permute-done.10._ = bf16[4,32,256]{2,1,0:T(8,128)(2,1)S(1)} collective-permute-done((bf16[4,32,256]{2,1,0:T(8,128)(2,1)S(1)}, bf16[4,32,256]{2,1,0:T(8,128)(2,1)S(1)}, u32[]{:S(2)}, u32[]{:S(2)}) %collective-permute-start.10) | collective-permute-done | bytes 65568 | tf_op jit(solution)/shard_map/ppermute | solution.py:30
  33.3 0.1 collective-permute-start.11
  33.4 0.6 collective-permute-start.12
  34.0 2.9 %collective-permute-start.13 = (bf16[2,32,256]{2,1,0:T(8,128)(2,1)S(1)}, bf16[2,32,256]{2,1,0:T(8,128)(2,1)S(1)}, u32[]{:S(2)}, u32[]{:S(2)}) collective-permute-start(bf16[2,32,256]{2,1,0:T(8,128)(2,1)S(1)} %pad_maximum_fusion.4), channel_id=1, source_target_pairs={{0,24},{4,28},{8,16},{12,20},{16,8},{20,12},{24,0},{28,4},{1,25},{... | collective-permute-start | bytes 98312 | tf_op jit(solution)/shard_map/ppermute | solution.py:30
  36.9 2.2 %write_pool.3.refs_5_.refs_10_ = bf16[20,64,1792]{2,1,0:T(8,128)(2,1)} custom-call(bf16[20,64,1792]{2,1,0:T(8,128)(2,1)S(1)} %bitcast.33, bf16[4,32,256]{2,1,0:T(8,128)(2,1)S(1)} %collective-permute-done.10._), custom_call_target="tpu_custom_call" | custom-call | tf_op jit(solution)/shard_map/write_pool/pallas_call | solution.py:58
  39.1 1.0 %out_project.1 = (f32[4,4,4,1792]{3,2,1,0:T(4,128)S(1)}, bf16[4,4,4,1792]{3,2,1,0:T(4,128)(2,1)S(1)}) custom-call(bf16[2,32,256]{2,1,0:T(8,128)(2,1)S(1)} %pad_maximum_fusion.1.refs_0_, bf16[2,32,256]{2,1,0:T(8,128)(2,1)S(1)} %collective-permute-done.11.refs_1_, bf16[2,32,256]{2,1,0:T(8,128)(2,1)S(1)} %collective-permute-done.12.refs_2_, ...), custom_call_target="tpu_custom_call" | custom-call | tf_op jit(solution)/shard_map/out_project/pallas_call | solution.py:591
  40.2 0.1 collective-permute-start.15
  40.2 0.2 choose_half.1
  40.4 0.6 collective-permute-start.19
  41.0 0.7 %collective-permute-done.15 = bf16[4,4,4,1792]{3,2,1,0:T(4,128)(2,1)S(1)} collective-permute-done((bf16[4,4,4,1792]{3,2,1,0:T(4,128)(2,1)S(1)}, bf16[4,4,4,1792]{3,2,1,0:T(4,128)(2,1)S(1)}, u32[]{:S(2)}, u32[]{:S(2)}) %collective-permute-start.15) | collective-permute-done | bytes 229408 | tf_op jit(solution)/shard_map/ppermute | solution.py:30
  41.7 0.2 fusion.6
  41.9 0.1 slice_bitcast_fusion.3
  41.9 2.6 %collective-permute-start.18 = (bf16[4,4,1792]{2,1,0:T(4,128)(2,1)S(1)}, bf16[4,4,1792]{2,1,0:T(4,128)(2,1)S(1)}, u32[]{:S(2)}, u32[]{:S(2)}) collective-permute-start(bf16[4,4,1792]{2,1,0:T(4,128)(2,1)S(1)} %get-tuple-element.62), channel_id=1, source_target_pairs={{0,24},{4,28},{8,16},{12,20},{16,8},{20,12},{24,0},{28,4},{1,25},{... | collective-permute-start | bytes 172040 | tf_op jit(solution)/shard_map/ppermute | solution.py:30
  44.6 0.5 collective-permute-start.17
  45.1 0.4 collective-permute-start.16
  45.5 1.8 %place_page.1 = (f32[4,1792]{1,0:T(4,128)S(1)}, bf16[20,64,1792]{2,1,0:T(8,128)(2,1)}, bf16[20,64,1792]{2,1,0:T(8,128)(2,1)}) custom-call(s32[4]{0:T(128)S(1)} %copy-done.4, s32[4]{0:T(128)S(1)} %copy-done.5, s32[4,16]{1,0:T(4,128)S(1)} %copy-done.3, f32[8,128]{1,0:T(8,128)S(1)} %find_sources.1._.source_ref, ...), custom_call_target="tpu_custom_call", output_to_operand_aliasing={{1}: (15, {}), {2}: (16, {})} | custom-call | tf_op jit(solution)/shard_map/place_page/pallas_call | solution.py:687
  47.3 1.5 %collective-permute-done.17 = bf16[4,4,1792]{2,1,0:T(4,128)(2,1)S(1)} collective-permute-done((bf16[4,4,1792]{2,1,0:T(4,128)(2,1)S(1)}, bf16[4,4,1792]{2,1,0:T(4,128)(2,1)S(1)}, u32[]{:S(2)}, u32[]{:S(2)}) %collective-permute-start.17) | collective-permute-done | bytes 57376 | tf_op jit(solution)/shard_map/ppermute | solution.py:30
  48.8 0.5 collective-permute-done.16
  49.4 2.6 %collective-permute-start.20 = (bf16[2,4,1792]{2,1,0:T(4,128)(2,1)S(1)}, bf16[2,4,1792]{2,1,0:T(4,128)(2,1)S(1)}, u32[]{:S(2)}, u32[]{:S(2)}) collective-permute-start(bf16[2,4,1792]{2,1,0:T(4,128)(2,1)S(1)} %slice.132), channel_id=1, source_target_pairs={{0,2},{1,3},{2,0},{3,1},{4,6},{5,7},{6,4},{7,5},{8,10},{9,11},{10,... | collective-permute-start | bytes 86024 | tf_op jit(solution)/shard_map/ppermute | solution.py:30
  52.0 2.2 %collective-permute-done.20 = bf16[2,4,1792]{2,1,0:T(4,128)(2,1)S(1)} collective-permute-done((bf16[2,4,1792]{2,1,0:T(4,128)(2,1)S(1)}, bf16[2,4,1792]{2,1,0:T(4,128)(2,1)S(1)}, u32[]{:S(2)}, u32[]{:S(2)}) %collective-permute-start.20) | collective-permute-done | bytes 28704 | tf_op jit(solution)/shard_map/ppermute | solution.py:30
  54.2 1.6 %collective-permute-start.21 = (bf16[1,4,1792]{2,1,0:T(4,128)(2,1)S(1)}, bf16[1,4,1792]{2,1,0:T(4,128)(2,1)S(1)}, u32[]{:S(2)}, u32[]{:S(2)}) collective-permute-start(bf16[1,4,1792]{2,1,0:T(4,128)(2,1)S(1)} %slice.133), channel_id=1, source_target_pairs={{0,1},{1,0},{2,3},{3,2},{4,5},{5,4},{6,7},{7,6},{8,9},{9,8},{10,11... | collective-permute-start | bytes 43016 | tf_op jit(solution)/shard_map/ppermute | solution.py:30
  55.9 2.1 %collective-permute-done.21 = bf16[1,4,1792]{2,1,0:T(4,128)(2,1)S(1)} collective-permute-done((bf16[1,4,1792]{2,1,0:T(4,128)(2,1)S(1)}, bf16[1,4,1792]{2,1,0:T(4,128)(2,1)S(1)}, u32[]{:S(2)}, u32[]{:S(2)}) %collective-permute-start.21) | collective-permute-done | bytes 14368 | tf_op jit(solution)/shard_map/ppermute | solution.py:30
  58.0 0.6 %fusion.5 = bf16[4,1792]{1,0:T(4,128)(2,1)} fusion(f32[4,1792]{1,0:T(4,128)S(1)} %get-tuple-element.56, f32[2,4,1792]{2,1,0:T(4,128)S(1)} %convert_add_fusion.1, bf16[1,4,1792]{2,1,0:T(4,128)(2,1)S(1)} %collective-permute-done.21), kind=kLoop, calls=%fused_computation.19 | loop fusion | flops 28672 | bytes 86016 | tf_op jit(solution)/shard_map/convert_element_type | solution.py:793
  (52 shorter events, 0.4 us)
Async XLA Ops:
  0.6 13.7 %copy-start = (bf16[896,14,384]{2,0,1:T(8,128)(2,1)S(1)}, bf16[896,14,384]{2,0,1:T(8,128)(2,1)}, u32[]{:S(2)}) copy-start(bf16[896,14,384]{2,0,1:T(8,128)(2,1)} %param.16) | copy-start | bytes 28901380
  3.0 1.4 %collective-permute-start = (bf16[4,4,1024]{2,1,0:T(4,128)(2,1)S(1)}, bf16[4,4,1024]{2,1,0:T(4,128)(2,1)S(1)}, u32[]{:S(2)}, u32[]{:S(2)}) collective-permute-start(bf16[4,4,1024]{2,1,0:T(4,128)(2,1)S(1)} %get-tuple-element.33), channel_id=1, source_target_pairs={{0,4},{4,0},{8,12},{12,8},{16,20},{20,16},{24,28},{28,24},{1,5},{5... | collective-permute-start | bytes 98312 | tf_op jit(solution)/shard_map/ppermute | solution.py:30
  4.4 4.8 %collective-permute-start.1 = (bf16[2,32,1792]{2,1,0:T(8,128)(2,1)S(1)}, bf16[2,32,1792]{2,1,0:T(8,128)(2,1)S(1)}, u32[]{:S(2)}, u32[]{:S(2)}) collective-permute-start(bf16[2,32,1792]{2,1,0:T(8,128)(2,1)S(1)} %get-tuple-element.34), channel_id=1, source_target_pairs={{0,4},{4,0},{8,12},{12,8},{16,20},{20,16},{24,28},{28,24},{1,5},{5... | collective-permute-start | bytes 688136 | tf_op jit(solution)/shard_map/ppermute | solution.py:30
  4.7 4.5 %collective-permute-start.2 = (bf16[2,4,1024]{2,1,0:T(4,128)(2,1)S(1)}, bf16[2,4,1024]{2,1,0:T(4,128)(2,1)S(1)}, u32[]{:S(2)}, u32[]{:S(2)}) collective-permute-start(bf16[2,4,1024]{2,1,0:T(4,128)(2,1)S(1)} %pad_maximum_fusion.6), channel_id=1, source_target_pairs={{0,8},{4,12},{8,0},{12,4},{16,24},{20,28},{24,16},{28,20},{1,9},{5... | collective-permute-start | bytes 49160 | tf_op jit(solution)/shard_map/ppermute | solution.py:30
  7.5 3.8 %collective-permute-start.3 = (bf16[2,4,1024]{2,1,0:T(4,128)(2,1)S(1)}, bf16[2,4,1024]{2,1,0:T(4,128)(2,1)S(1)}, u32[]{:S(2)}, u32[]{:S(2)}) collective-permute-start(bf16[2,4,1024]{2,1,0:T(4,128)(2,1)S(1)} %pad_maximum_fusion.7), channel_id=1, source_target_pairs={{0,16},{4,20},{8,24},{12,28},{16,0},{20,4},{24,8},{28,12},{1,17},{... | collective-permute-start | bytes 49160 | tf_op jit(solution)/shard_map/ppermute | solution.py:30
  9.1 4.7 %collective-permute-start.4 = (bf16[2,4,1024]{2,1,0:T(4,128)(2,1)S(1)}, bf16[2,4,1024]{2,1,0:T(4,128)(2,1)S(1)}, u32[]{:S(2)}, u32[]{:S(2)}) collective-permute-start(bf16[2,4,1024]{2,1,0:T(4,128)(2,1)S(1)} %pad_maximum_fusion.8), channel_id=1, source_target_pairs={{0,24},{4,28},{8,16},{12,20},{16,8},{20,12},{24,0},{28,4},{1,25},{... | collective-permute-start | bytes 49160 | tf_op jit(solution)/shard_map/ppermute | solution.py:30
  9.2 12.8 %slice-start = ((s8[4587520]{0:T(1024)(128)(4,1)}), s8[4194304]{0:T(1024)(128)(4,1)S(1)}, s32[]{:S(2)}) async-start(s8[4587520]{0:T(1024)(128)(4,1)} %bitcast.30), calls=%async_computation | async-start | bytes 8388608
  13.8 11.8 %collective-permute-start.9 = (bf16[2,2,32,1792]{3,2,1,0:T(8,128)(2,1)S(1)}, bf16[2,2,32,1792]{3,2,1,0:T(8,128)(2,1)S(1)}, u32[]{:S(2)}, u32[]{:S(2)}) collective-permute-start(bf16[2,2,32,1792]{3,2,1,0:T(8,128)(2,1)S(1)} %pad_maximum_fusion.refs_0_.refs_6_), channel_id=1, source_target_pairs={{0,8},{4,20},{8,0},{12,28},{16,24},{20,4},{24,16},{28,12},{1,9},{5... | collective-permute-start | bytes 1376264 | tf_op jit(solution)/shard_map/ppermute | solution.py:163
  14.3 7.6 %copy-start.6 = (f32[14,384]{1,0:T(8,128)S(1)}, f32[14,384]{1,0:T(8,128)}, u32[]{:S(2)}) copy-start(f32[14,384]{1,0:T(8,128)} %param.17) | copy-start | bytes 64516
  14.3 7.7 %slice-start.1 = ((s8[4587520]{0:T(1024)(128)(4,1)}), s8[393216]{0:T(1024)(128)(4,1)S(1)}, s32[]{:S(2)}) async-start(s8[4587520]{0:T(1024)(128)(4,1)} %bitcast.30), calls=%async_computation.1 | async-start | bytes 786432
  16.6 1.7 %collective-permute-start.5 = (f32[4,4,5376]{2,1,0:T(4,128)S(1)}, f32[4,4,5376]{2,1,0:T(4,128)S(1)}, u32[]{:S(2)}, u32[]{:S(2)}) collective-permute-start(f32[4,4,5376]{2,1,0:T(4,128)S(1)} %get-tuple-element.42), channel_id=1, source_target_pairs={{0,4},{4,0},{8,12},{12,8},{16,20},{20,16},{24,28},{28,24},{1,5},{5... | collective-permute-start | bytes 1032200 | tf_op jit(solution)/shard_map/ppermute | solution.py:30
  18.4 6.1 %collective-permute-start.6 = (bf16[4,7168]{1,0:T(4,128)(2,1)S(1)}, bf16[4,7168]{1,0:T(4,128)(2,1)S(1)}, u32[]{:S(2)}, u32[]{:S(2)}) collective-permute-start(bf16[4,7168]{1,0:T(4,128)(2,1)S(1)} %get-tuple-element.44), channel_id=1, source_target_pairs={{0,8},{4,12},{8,0},{12,4},{16,24},{20,28},{24,16},{28,20},{1,9},{5... | collective-permute-start | bytes 172040 | tf_op jit(solution)/shard_map/ppermute | solution.py:30
  20.0 4.8 %collective-permute-start.7 = (bf16[4,7168]{1,0:T(4,128)(2,1)S(1)}, bf16[4,7168]{1,0:T(4,128)(2,1)S(1)}, u32[]{:S(2)}, u32[]{:S(2)}) collective-permute-start(bf16[4,7168]{1,0:T(4,128)(2,1)S(1)} %get-tuple-element.45), channel_id=1, source_target_pairs={{0,16},{4,20},{8,24},{12,28},{16,0},{20,4},{24,8},{28,12},{1,17},{... | collective-permute-start | bytes 172040 | tf_op jit(solution)/shard_map/ppermute | solution.py:30
  20.5 5.1 %collective-permute-start.8 = (bf16[4,7168]{1,0:T(4,128)(2,1)S(1)}, bf16[4,7168]{1,0:T(4,128)(2,1)S(1)}, u32[]{:S(2)}, u32[]{:S(2)}) collective-permute-start(bf16[4,7168]{1,0:T(4,128)(2,1)S(1)} %get-tuple-element.46), channel_id=1, source_target_pairs={{0,24},{4,28},{8,16},{12,20},{16,8},{20,12},{24,0},{28,4},{1,25},{... | collective-permute-start | bytes 172040 | tf_op jit(solution)/shard_map/ppermute | solution.py:30
  22.0 5.5 %slice-start.2 = ((s8[4587520]{0:T(1024)(128)(4,1)}), s8[4194304]{0:T(1024)(128)(4,1)S(1)}, s32[]{:S(2)}) async-start(s8[4587520]{0:T(1024)(128)(4,1)} %bitcast.32), calls=%async_computation.2 | async-start | bytes 8388608
  22.0 5.4 %slice-start.3 = ((s8[4587520]{0:T(1024)(128)(4,1)}), s8[393216]{0:T(1024)(128)(4,1)S(1)}, s32[]{:S(2)}) async-start(s8[4587520]{0:T(1024)(128)(4,1)} %bitcast.32), calls=%async_computation.3 | async-start | bytes 786432
  22.0 5.4 %copy-start.1 = (bf16[4,7168]{1,0:T(4,128)(2,1)S(1)}, bf16[4,7168]{1,0:T(4,128)(2,1)}, u32[]{:S(2)}) copy-start(bf16[4,7168]{1,0:T(4,128)(2,1)} %refs_4_.1) | copy-start | bytes 172036
  22.0 5.4 %copy-start.3 = (s32[4,16]{1,0:T(4,128)S(1)}, s32[4,16]{1,0:T(4,128)}, u32[]{:S(2)}) copy-start(s32[4,16]{1,0:T(4,128)} %table_ref.3) | copy-start | bytes 772
  22.1 5.4 %copy-start.4 = (s32[4]{0:T(128)S(1)}, s32[4]{0:T(128)}, u32[]{:S(2)}) copy-start(s32[4]{0:T(128)} %length_ref.3) | copy-start | bytes 52
  22.1 5.4 %copy-start.5 = (s32[4]{0:T(128)S(1)}, s32[4]{0:T(128)}, u32[]{:S(2)}) copy-start(s32[4]{0:T(128)} %slot_ref.3) | copy-start | bytes 52
  25.9 13.2 %collective-permute-start.14 = (bf16[2,2,32,1792]{3,2,1,0:T(8,128)(2,1)S(1)}, bf16[2,2,32,1792]{3,2,1,0:T(8,128)(2,1)S(1)}, u32[]{:S(2)}, u32[]{:S(2)}) collective-permute-start(bf16[2,2,32,1792]{3,2,1,0:T(8,128)(2,1)S(1)} %turn_pages.1.refs_12_), channel_id=1, source_target_pairs={{0,16},{4,12},{8,24},{12,4},{16,0},{20,28},{24,8},{28,20},{1,17},{... | collective-permute-start | bytes 1376264 | tf_op jit(solution)/shard_map/ppermute | solution.py:163
  32.0 1.3 %collective-permute-start.10 = (bf16[4,32,256]{2,1,0:T(8,128)(2,1)S(1)}, bf16[4,32,256]{2,1,0:T(8,128)(2,1)S(1)}, u32[]{:S(2)}, u32[]{:S(2)}) collective-permute-start(bf16[4,32,256]{2,1,0:T(8,128)(2,1)S(1)} %get-tuple-element.49), channel_id=1, source_target_pairs={{0,4},{4,0},{8,12},{12,8},{16,20},{20,16},{24,28},{28,24},{1,5},{5... | collective-permute-start | bytes 196616 | tf_op jit(solution)/shard_map/ppermute | solution.py:30
  33.3 5.7 %collective-permute-start.11 = (bf16[2,32,256]{2,1,0:T(8,128)(2,1)S(1)}, bf16[2,32,256]{2,1,0:T(8,128)(2,1)S(1)}, u32[]{:S(2)}, u32[]{:S(2)}) collective-permute-start(bf16[2,32,256]{2,1,0:T(8,128)(2,1)S(1)} %pad_maximum_fusion.2), channel_id=1, source_target_pairs={{0,8},{4,12},{8,0},{12,4},{16,24},{20,28},{24,16},{28,20},{1,9},{5... | collective-permute-start | bytes 98312 | tf_op jit(solution)/shard_map/ppermute | solution.py:30
  33.4 5.7 %collective-permute-start.12 = (bf16[2,32,256]{2,1,0:T(8,128)(2,1)S(1)}, bf16[2,32,256]{2,1,0:T(8,128)(2,1)S(1)}, u32[]{:S(2)}, u32[]{:S(2)}) collective-permute-start(bf16[2,32,256]{2,1,0:T(8,128)(2,1)S(1)} %pad_maximum_fusion.3), channel_id=1, source_target_pairs={{0,16},{4,20},{8,24},{12,28},{16,0},{20,4},{24,8},{28,12},{1,17},{... | collective-permute-start | bytes 98312 | tf_op jit(solution)/shard_map/ppermute | solution.py:30
  34.0 5.1 %collective-permute-start.13 = (bf16[2,32,256]{2,1,0:T(8,128)(2,1)S(1)}, bf16[2,32,256]{2,1,0:T(8,128)(2,1)S(1)}, u32[]{:S(2)}, u32[]{:S(2)}) collective-permute-start(bf16[2,32,256]{2,1,0:T(8,128)(2,1)S(1)} %pad_maximum_fusion.4), channel_id=1, source_target_pairs={{0,24},{4,28},{8,16},{12,20},{16,8},{20,12},{24,0},{28,4},{1,25},{... | collective-permute-start | bytes 98312 | tf_op jit(solution)/shard_map/ppermute | solution.py:30
  39.1 6.4 %copy-start.2 = (f32[7168]{0:T(1024)S(1)}, f32[7168]{0:T(1024)}, u32[]{:S(2)}) copy-start(f32[7168]{0:T(1024)} %param.19) | copy-start | bytes 86020
  40.2 1.6 %collective-permute-start.15 = (bf16[4,4,4,1792]{3,2,1,0:T(4,128)(2,1)S(1)}, bf16[4,4,4,1792]{3,2,1,0:T(4,128)(2,1)S(1)}, u32[]{:S(2)}, u32[]{:S(2)}) collective-permute-start(bf16[4,4,4,1792]{3,2,1,0:T(4,128)(2,1)S(1)} %get-tuple-element.52), channel_id=1, source_target_pairs={{0,4},{4,0},{8,12},{12,8},{16,20},{20,16},{24,28},{28,24},{1,5},{5... | collective-permute-start | bytes 688136 | tf_op jit(solution)/shard_map/ppermute | solution.py:30
  40.4 5.1 %collective-permute-start.19 = (bf16[2,32,1792]{2,1,0:T(8,128)(2,1)S(1)}, bf16[2,32,1792]{2,1,0:T(8,128)(2,1)S(1)}, u32[]{:S(2)}, u32[]{:S(2)}) collective-permute-start(bf16[2,32,1792]{2,1,0:T(8,128)(2,1)S(1)} %choose_half.1), channel_id=1, source_target_pairs={{0,4},{4,0},{8,12},{12,8},{16,20},{20,16},{24,28},{28,24},{1,5},{5... | collective-permute-start | bytes 688136 | tf_op jit(solution)/shard_map/ppermute | solution.py:30
  41.9 5.3 %collective-permute-start.18 = (bf16[4,4,1792]{2,1,0:T(4,128)(2,1)S(1)}, bf16[4,4,1792]{2,1,0:T(4,128)(2,1)S(1)}, u32[]{:S(2)}, u32[]{:S(2)}) collective-permute-start(bf16[4,4,1792]{2,1,0:T(4,128)(2,1)S(1)} %get-tuple-element.62), channel_id=1, source_target_pairs={{0,24},{4,28},{8,16},{12,20},{16,8},{20,12},{24,0},{28,4},{1,25},{... | collective-permute-start | bytes 172040 | tf_op jit(solution)/shard_map/ppermute | solution.py:30
  44.6 4.2 %collective-permute-start.17 = (bf16[4,4,1792]{2,1,0:T(4,128)(2,1)S(1)}, bf16[4,4,1792]{2,1,0:T(4,128)(2,1)S(1)}, u32[]{:S(2)}, u32[]{:S(2)}) collective-permute-start(bf16[4,4,1792]{2,1,0:T(4,128)(2,1)S(1)} %get-tuple-element.63), channel_id=1, source_target_pairs={{0,16},{4,20},{8,24},{12,28},{16,0},{20,4},{24,8},{28,12},{1,17},{... | collective-permute-start | bytes 172040 | tf_op jit(solution)/shard_map/ppermute | solution.py:30
  45.1 4.2 %collective-permute-start.16 = (bf16[4,4,1792]{2,1,0:T(4,128)(2,1)S(1)}, bf16[4,4,1792]{2,1,0:T(4,128)(2,1)S(1)}, u32[]{:S(2)}, u32[]{:S(2)}) collective-permute-start(bf16[4,4,1792]{2,1,0:T(4,128)(2,1)S(1)} %get-tuple-element.61), channel_id=1, source_target_pairs={{0,8},{4,12},{8,0},{12,4},{16,24},{20,28},{24,16},{28,20},{1,9},{5... | collective-permute-start | bytes 172040 | tf_op jit(solution)/shard_map/ppermute | solution.py:30
  49.4 4.8 %collective-permute-start.20 = (bf16[2,4,1792]{2,1,0:T(4,128)(2,1)S(1)}, bf16[2,4,1792]{2,1,0:T(4,128)(2,1)S(1)}, u32[]{:S(2)}, u32[]{:S(2)}) collective-permute-start(bf16[2,4,1792]{2,1,0:T(4,128)(2,1)S(1)} %slice.132), channel_id=1, source_target_pairs={{0,2},{1,3},{2,0},{3,1},{4,6},{5,7},{6,4},{7,5},{8,10},{9,11},{10,... | collective-permute-start | bytes 86024 | tf_op jit(solution)/shard_map/ppermute | solution.py:30
  54.2 3.8 %collective-permute-start.21 = (bf16[1,4,1792]{2,1,0:T(4,128)(2,1)S(1)}, bf16[1,4,1792]{2,1,0:T(4,128)(2,1)S(1)}, u32[]{:S(2)}, u32[]{:S(2)}) collective-permute-start(bf16[1,4,1792]{2,1,0:T(4,128)(2,1)S(1)} %slice.133), channel_id=1, source_target_pairs={{0,1},{1,0},{2,3},{3,2},{4,5},{5,4},{6,7},{7,6},{8,9},{9,8},{10,11... | collective-permute-start | bytes 43016 | tf_op jit(solution)/shard_map/ppermute | solution.py:30

commit v10 on v8

--- a/solution.py
+++ b/solution.py
@@ -169,7 +169,7 @@
     down = chips // across
 
     def kernel(*refs):
-        block_refs, out_ref = refs[:chips], refs[-1]
+        block_refs, out_ref = refs[:chips][::-1], refs[-1]
         here = lax.axis_index("req")
         lane = lax.broadcasted_iota(jnp.int32, (8, LANES), 1)
         found = jnp.zeros((8, LANES), F32)
@@ -196,7 +196,7 @@
         compiler_params=pltpu.CompilerParams(vmem_limit_bytes=2 * MIB),
         cost_estimate=cost(0, 0),
         name="find_sources",
-    )(*spread, after)
+    )(*spread[::-1], after)
 
 
 def number_at(source_ref, j):
@@ -282,7 +282,7 @@
     rows = chips * 2 * slots
 
     def kernel(*refs):
-        block_refs = refs[:chips]
+        block_refs = refs[:chips][::-1]
         weight_ref, later_ref, keep_ref, send_ref, later_out, left, sem = refs[chips:]
         copy = pltpu.make_async_copy(later_ref, later_out, sem)
         copy.start()
@@ -314,7 +314,7 @@
         compiler_params=pltpu.CompilerParams(vmem_limit_bytes=weight.size * 2 + 12 * MIB),
         cost_estimate=cost(2 * rows * weight.size, 2 * weight.size),
         name="project",
-    )(*blocks, weight, *in_hbm(later))
+    )(*blocks[::-1], weight, *in_hbm(later))
 
 
 def combine(keep, got, after):
@@ -353,10 +353,6 @@
     head = LANES
     heads = width // head
     max_pages = page_table.shape[1]
-    chunk_pages = 4
-    chunk = chunk_pages * page
-    chunks = max_pages // chunk_pages
-    long_rows = max_pages * page
     short_rows = slots * page
     groups = 2 * parts
     share = head // groups
@@ -367,11 +363,11 @@
 
     def kernel(*refs):
         length_ref, slot_ref, table_ref = refs[:3]
-        sum_refs = refs[3 : 3 + parts]
+        sum_refs = refs[3 : 3 + parts][::-1]
         (bias_ref, token_ref, key_ref, value_ref, _, pack_keep, pack_send, patch_ref, value_out) = refs[
             3 + parts : 12 + parts
         ]
-        score_buffer, mix_buffer, out_sems = refs[12 + parts :]
+        attended_ref, out_sems = refs[12 + parts :]
         step = pages // 4
         writes = [
             pltpu.make_async_copy(value_ref.at[pl.ds(i * step, step)], value_out.at[pl.ds(i * step, step)], out_sems.at[i])
@@ -389,7 +385,6 @@
             is_long = lengths[s] >= page
             long_slot = jnp.where(is_long, s, long_slot)
             long_length = jnp.where(is_long, lengths[s], long_length)
-        turns = (long_length + chunk - 1) // chunk
 
         total = sum_refs[0][...] + bias_ref[...]
 
@@ -437,66 +432,50 @@
         own_column = lax.broadcasted_iota(jnp.int32, size, 0) // tall == lax.broadcasted_iota(jnp.int32, size, 1)
         new_score = jnp.sum(jnp.where(own_column, new_scores, 0.0), axis=1, keepdims=True)
 
-        first_pages = lambda ref: jnp.concatenate([ref[table_ref[s, 0]] for s in range(slots)], axis=0)
-        short_scores = lax.dot_general(short_query, first_pages(key_ref), across, preferred_element_type=F32)
-        size = (slots * tall, short_rows)
-        row_slot = lax.broadcasted_iota(jnp.int32, size, 0) // tall
-        column = lax.broadcasted_iota(jnp.int32, size, 1)
-        limit = jnp.zeros(size, jnp.int32)
-        for s in range(slots):
-            limit = jnp.where(row_slot == s, lengths[s], limit)
-        valid = (row_slot == column // page) & (column % page < limit)
-        short_probs, new_prob, short_denom = softmax(short_scores, valid, new_score)
-        new_values = jnp.concatenate(
-            [jnp.broadcast_to(new_rows[1][s : s + 1], (tall, width)) for s in range(slots)], axis=0
-        )
-        short_mix = jnp.dot(short_probs, first_pages(value_ref), preferred_element_type=F32)
-        short_mix = (short_mix + new_prob * new_values) / short_denom
-
-        mix_buffer[...] = jnp.zeros(mix_buffer.shape, F32)
-
-        @pl.when(turns > 0)
-        def _():
-            some_pages = lambda ref, c: jnp.concatenate(
-                [ref[table_ref[long_slot, c * chunk_pages + i]] for i in range(chunk_pages)], axis=0
-            )
-            long_query = blocked(for_slot(long_slot, [query[s : s + 1] for s in range(slots)]))
-            long_new = for_slot(long_slot, [new_score[s * tall : (s + 1) * tall] for s in range(slots)])
-            long_value = for_slot(long_slot, [new_rows[1][s : s + 1] for s in range(slots)])
-            for c in range(chunks):
-
-                @pl.when(c < turns)
-                def _():
-                    score_buffer[:, c * chunk : (c + 1) * chunk] = lax.dot_general(
-                        long_query, some_pages(key_ref, c), across, preferred_element_type=F32
-                    )
-
-                @pl.when(c >= turns)
-                def _():
-                    score_buffer[:, c * chunk : (c + 1) * chunk] = jnp.zeros((tall, chunk), F32)
-
-            position = lax.broadcasted_iota(jnp.int32, (tall, long_rows), 1)
-            long_probs, long_prob, long_denom = softmax(score_buffer[...], position < long_length, long_new)
-            for c in range(chunks):
-
-                @pl.when(c < turns)
-                def _():
-                    mix_buffer[...] += jnp.dot(
-                        long_probs[:, c * chunk : (c + 1) * chunk], some_pages(value_ref, c), preferred_element_type=F32
-                    )
-
-            mix_buffer[...] = (mix_buffer[...] + long_prob * long_value) / long_denom
-
         def fold(mixed):
             return jnp.sum(jnp.where(on_head, mixed, 0.0), axis=0, keepdims=True)
 
-        long_mix = fold(mix_buffer[...])
-        rows = []
-        for s in range(slots):
-            row = fold(short_mix[s * tall : (s + 1) * tall])
-            rows.append(jnp.where(lengths[s] >= page, long_mix, row))
         high = -(-slots // 8) * 8
-        attended = jnp.concatenate(rows + [jnp.zeros((high - slots, width), F32)], axis=0).astype(BF16).astype(F32)
+
+        def attend_all(long_pages):
+            first_pages = lambda ref: jnp.concatenate([ref[table_ref[s, 0]] for s in range(slots)], axis=0)
+            short_scores = lax.dot_general(short_query, first_pages(key_ref), across, preferred_element_type=F32)
+            size = (slots * tall, short_rows)
+            row_slot = lax.broadcasted_iota(jnp.int32, size, 0) // tall
+            column = lax.broadcasted_iota(jnp.int32, size, 1)
+            limit = jnp.zeros(size, jnp.int32)
+            for s in range(slots):
+                limit = jnp.where(row_slot == s, lengths[s], limit)
+            valid = (row_slot == column // page) & (column % page < limit)
+            short_probs, new_prob, short_denom = softmax(short_scores, valid, new_score)
+            new_values = jnp.concatenate(
+                [jnp.broadcast_to(new_rows[1][s : s + 1], (tall, width)) for s in range(slots)], axis=0
+            )
+            short_mix = jnp.dot(short_probs, first_pages(value_ref), preferred_element_type=F32)
+            short_mix = (short_mix + new_prob * new_values) / short_denom
+
+            rows = [fold(short_mix[s * tall : (s + 1) * tall]) for s in range(slots)]
+            if long_pages:
+                some_pages = lambda ref: jnp.concatenate(
+                    [ref[table_ref[long_slot, i]] for i in range(long_pages)], axis=0
+                )
+                long_query = blocked(for_slot(long_slot, [query[s : s + 1] for s in range(slots)]))
+                long_new = for_slot(long_slot, [new_score[s * tall : (s + 1) * tall] for s in range(slots)])
+                long_value = for_slot(long_slot, [new_rows[1][s : s + 1] for s in range(slots)])
+                scores = lax.dot_general(long_query, some_pages(key_ref), across, preferred_element_type=F32)
+                position = lax.broadcasted_iota(jnp.int32, (tall, long_pages * page), 1)
+                long_probs, long_prob, long_denom = softmax(scores, position < long_length, long_new)
+                mixed = jnp.dot(long_probs, some_pages(value_ref), preferred_element_type=F32)
+                long_mix = fold((mixed + long_prob * long_value) / long_denom)
+                rows = [jnp.where(lengths[s] >= page, long_mix, row) for s, row in enumerate(rows)]
+            rows += [jnp.zeros((high - slots, width), F32)]
+            attended_ref[...] = jnp.concatenate(rows, axis=0).astype(BF16).astype(F32)
+
+        half = max_pages // 2
+        pl.when(long_length == 0)(lambda: attend_all(0))
+        pl.when((long_length > 0) & (long_length <= half * page))(lambda: attend_all(half))
+        pl.when(long_length > half * page)(lambda: attend_all(max_pages))
+        attended = attended_ref[...]
 
         token = token_ref[:, pl.ds(pl.multiple_of(column_block * width, LANES), width)].astype(F32)
         extra = []
@@ -547,14 +526,13 @@
         in_specs=[SMEM] * 3 + [VMEM] * (parts + 4) + [ANY],
         out_specs=(VMEM, VMEM, VMEM, HBM),
         scratch_shapes=[
-            pltpu.VMEM((tall, long_rows), F32),
-            pltpu.VMEM((tall, width), F32),
+            pltpu.VMEM((-(-slots // 8) * 8, width), F32),
             pltpu.SemaphoreType.DMA((4,)),
         ],
         compiler_params=pltpu.CompilerParams(vmem_limit_bytes=18 * MIB),
-        cost_estimate=cost(4 * tall * (long_rows + short_rows) * width, 4 * (long_rows + short_rows) * width),
+        cost_estimate=cost(0, 0),
         name="attend",
-    )(lengths, new_slot, page_table, *sums, bias, tokens, key_pool, value_pool, after)
+    )(lengths, new_slot, page_table, *sums[::-1], bias, tokens, key_pool, value_pool, after)
 
 
 def pack_rows(slots, strips):
@@ -570,7 +548,7 @@
     piece = width // pieces
 
     def kernel(*refs):
-        block_refs, weight_ref = refs[:chips], refs[chips]
+        block_refs, weight_ref = refs[:chips][::-1], refs[chips]
         keep_ref, send_ref = refs[chips + 1 + len(after) :]
         gathered = jnp.concatenate(
             [block_refs[d][e, :high, :].astype(F32) for d in range(chips) for e in range(2)], axis=0
@@ -609,7 +587,7 @@
         compiler_params=pltpu.CompilerParams(vmem_limit_bytes=10 * MIB),
         cost_estimate=cost(2 * rows * weight.size, 2 * weight.size),
         name="out_project",
-    )(*blocks, weight, *after)
+    )(*blocks[::-1], weight, *after)
 
 
 def place_page(lengths, new_slot, page_table, sources, patches, packs, tokens, out_bias, halves, turned, from_other, key_out, value_out):
@@ -625,7 +603,7 @@
     tall = patches.shape[2]
 
     def kernel(length_ref, slot_ref, table_ref, source_ref, patch_ref, *refs):
-        pack_refs = refs[:chips]
+        pack_refs = refs[:chips][::-1]
         token_ref, bias_ref = refs[chips : chips + 2]
         half_refs = refs[chips + 2 : chips + 2 + across]
         turned_refs = refs[chips + 2 + across : chips + 2 + across + rows]
@@ -713,7 +691,7 @@
         cost_estimate=cost(0, 8 * page * width),
         name="place_page",
     )(
-        lengths, new_slot, page_table, sources, patches, *packs, tokens, out_bias, *halves, *turned, from_other, key_out, value_out
+        lengths, new_slot, page_table, sources, patches, *packs[::-1], tokens, out_bias, *halves, *turned, from_other, key_out, value_out
     )
 
 

time: 56.4 us -> 53.5 us (0.949); the launches traced: 56.4 us -> 52.9 us
  waiting for transfers between devices: 15.2 us -> 12.5 us
  Pallas kernels: 14.9 us -> 13.2 us
  starting transfers between devices: 24.1 us -> 25.1 us
    ppermute x21, waiting for transfers between devices: 15.2 us -> 12.5 us  [swap(): return lax.ppermute(value, axis, [(i, i ^ step) for i in range(size)])]
    pallas_call x1, Pallas kernels: 4.52 us -> 2.84 us  [attend(): pl.pallas_call(kernel, out_shape=(packed, packed, jax.ShapeDtypeStruct((2...]
    ppermute x2, starting transfers between devices: 2.58 us -> 3.62 us  [swap_pages(): lax.ppermute(value, 'req', [(i, i ^ steps[i]) for i in range(2 * chips)])]
  transfers between devices with their start and end apart: 23 -> 23, of which waited for: 13 -> 14; matrix products, arithmetic and copies ran while one was open for 1% -> 1% of each run, Pallas kernels for 20% -> 19%
where the time goes in v10:
time: 53.5 us; the launch traced here: 52.9 us
  starting transfers between devices  25.1 us (47%)
  Pallas kernels  13.2 us (25%)
  waiting for transfers between devices  12.5 us (23%)
  other arithmetic  1 us (2%)
  between operations  0.95 us (2%)
    ppermute x21, starting transfers between devices, swap(): return lax.ppermute(value, axis, [(i, i ^ step) for i in range(size)])  21.4 us
    ppermute x21, waiting for transfers between devices, swap(): return lax.ppermute(value, axis, [(i, i ^ step) for i in range(size)])  12.5 us
    ppermute x2, starting transfers between devices, swap_pages(): lax.ppermute(value, 'req', [(i, i ^ steps[i]) for i in range(2 * chips)])  3.62 us
    pallas_call x1, Pallas kernels, attend(): pl.pallas_call(kernel, out_shape=(packed, packed, jax.ShapeDtypeStruct((2...  2.84 us
    pallas_call x1, Pallas kernels, prepare(): pl.pallas_call(kernel, out_shape=(blocks, blocks, halves, halves), in_spe...  2.33 us
    pallas_call x1, Pallas kernels, project(): pl.pallas_call(kernel, out_shape=(shape, shape, jax.ShapeDtypeStruct(late...  2.28 us
    pallas_call x1, Pallas kernels, write_pool(): pl.pallas_call(kernel, out_shape=jax.ShapeDtypeStruct(pool.shape, pool.dt...  2.17 us
    pallas_call x1, Pallas kernels, place_page(): pl.pallas_call(kernel, out_shape=(jax.ShapeDtypeStruct((slots, width), F3...  1.76 us
  transfers between devices with their start and end apart: 23, of which 14 were waited for; matrix products, arithmetic and copies ran while one was open for 1% of the time, Pallas kernels for 19%

profile of v10, /device:TPU:0, one launch (start us, length us, event | category | flops | bytes accessed | tf_op | source)
XLA Modules:
  0.0 52.9 jit_solution(8853084267218780151)
XLA Ops:
  0.6 2.3 %prepare.1 = (bf16[4,4,1024]{2,1,0:T(4,128)(2,1)S(1)}, bf16[4,4,1024]{2,1,0:T(4,128)(2,1)S(1)}, bf16[2,32,1792]{2,1,0:T(8,128)(2,1)S(1)}, bf16[2,32,1792]{2,1,0:T(8,128)(2,1)S(1)}) custom-call(bf16[4,7168]{1,0:T(4,128)(2,1)} %refs_4_.1, f32[1,7168]{1,0:T(1,128)} %bitcast.50, f32[1,7168]{1,0:T(1,128)} %bitcast.51, s32[4]{0:T(128)} %length_ref.3, ...), custom_call_target="tpu_custom_call" | custom-call | tf_op jit(solution)/shard_map/prepare/pallas_call | solution.py:129
  3.0 0.5 collective-permute-start
  3.5 0.1 collective-permute-start.8
  3.6 0.8 %collective-permute-done = bf16[4,4,1024]{2,1,0:T(4,128)(2,1)S(1)} collective-permute-done((bf16[4,4,1024]{2,1,0:T(4,128)(2,1)S(1)}, bf16[4,4,1024]{2,1,0:T(4,128)(2,1)S(1)}, u32[]{:S(2)}, u32[]{:S(2)}) %collective-permute-start) | collective-permute-done | bytes 32800 | tf_op jit(solution)/shard_map/ppermute | solution.py:30
  4.4 3.9 %collective-permute-start.1 = (bf16[2,4,1024]{2,1,0:T(4,128)(2,1)S(1)}, bf16[2,4,1024]{2,1,0:T(4,128)(2,1)S(1)}, u32[]{:S(2)}, u32[]{:S(2)}) collective-permute-start(bf16[2,4,1024]{2,1,0:T(4,128)(2,1)S(1)} %pad_maximum_fusion.5), channel_id=1, source_target_pairs={{0,24},{4,28},{8,16},{12,20},{16,8},{20,12},{24,0},{28,4},{1,25},{... | collective-permute-start | bytes 49160 | tf_op jit(solution)/shard_map/ppermute | solution.py:30
  8.3 0.6 %collective-permute-start.2 = (bf16[2,4,1024]{2,1,0:T(4,128)(2,1)S(1)}, bf16[2,4,1024]{2,1,0:T(4,128)(2,1)S(1)}, u32[]{:S(2)}, u32[]{:S(2)}) collective-permute-start(bf16[2,4,1024]{2,1,0:T(4,128)(2,1)S(1)} %pad_maximum_fusion.6), channel_id=1, source_target_pairs={{0,16},{4,20},{8,24},{12,28},{16,0},{20,4},{24,8},{28,12},{1,17},{... | collective-permute-start | bytes 49160 | tf_op jit(solution)/shard_map/ppermute | solution.py:30
  8.9 0.1 collective-permute-start.3
  9.1 2.0 %collective-permute-start.9 = (bf16[2,2,32,1792]{3,2,1,0:T(8,128)(2,1)S(1)}, bf16[2,2,32,1792]{3,2,1,0:T(8,128)(2,1)S(1)}, u32[]{:S(2)}, u32[]{:S(2)}) collective-permute-start(bf16[2,2,32,1792]{3,2,1,0:T(8,128)(2,1)S(1)} %pad_maximum_fusion.refs_0_.refs_6_), channel_id=1, source_target_pairs={{0,8},{4,20},{8,0},{12,28},{16,24},{20,4},{24,16},{28,12},{1,9},{5... | collective-permute-start | bytes 1376264 | tf_op jit(solution)/shard_map/ppermute | solution.py:163
  11.1 1.1 %collective-permute-done.2.refs_1_ = bf16[2,4,1024]{2,1,0:T(4,128)(2,1)S(1)} collective-permute-done((bf16[2,4,1024]{2,1,0:T(4,128)(2,1)S(1)}, bf16[2,4,1024]{2,1,0:T(4,128)(2,1)S(1)}, u32[]{:S(2)}, u32[]{:S(2)}) %collective-permute-start.2) | collective-permute-done | bytes 16416 | tf_op jit(solution)/shard_map/ppermute | solution.py:30
  12.2 0.4 collective-permute-done.3.refs_2_
  12.8 2.3 %project.1 = (f32[4,4,5376]{2,1,0:T(4,128)S(1)}, f32[4,4,5376]{2,1,0:T(4,128)S(1)}, bf16[224,7168]{1,0:T(8,128)(2,1)S(1)}) custom-call(bf16[2,4,1024]{2,1,0:T(4,128)(2,1)S(1)} %collective-permute-done.1.refs_0_, bf16[2,4,1024]{2,1,0:T(4,128)(2,1)S(1)} %collective-permute-done.2.refs_1_, bf16[2,4,1024]{2,1,0:T(4,128)(2,1)S(1)} %collective-permute-done.3.refs_2_, ...), custom_call_target="tpu_custom_call" | custom-call | tf_op jit(solution)/shard_map/project/pallas_call | solution.py:308
  15.0 0.1 collective-permute-start.4
  15.1 0.3 find_sources.1._.source_ref
  15.4 1.4 %collective-permute-done.4.got_ref = f32[4,4,5376]{2,1,0:T(4,128)S(1)} collective-permute-done((f32[4,4,5376]{2,1,0:T(4,128)S(1)}, f32[4,4,5376]{2,1,0:T(4,128)S(1)}, u32[]{:S(2)}, u32[]{:S(2)}) %collective-permute-start.4) | collective-permute-done | bytes 344096 | tf_op jit(solution)/shard_map/ppermute | solution.py:30
  16.8 0.1 combine.1
  16.8 1.6 %collective-permute-start.5 = (bf16[4,7168]{1,0:T(4,128)(2,1)S(1)}, bf16[4,7168]{1,0:T(4,128)(2,1)S(1)}, u32[]{:S(2)}, u32[]{:S(2)}) collective-permute-start(bf16[4,7168]{1,0:T(4,128)(2,1)S(1)} %get-tuple-element.29), channel_id=1, source_target_pairs={{0,24},{4,28},{8,16},{12,20},{16,8},{20,12},{24,0},{28,4},{1,25},{... | collective-permute-start | bytes 172040 | tf_op jit(solution)/shard_map/ppermute | solution.py:30
  18.4 0.1 collective-permute-start.6
  18.5 1.9 %collective-permute-start.7 = (bf16[4,7168]{1,0:T(4,128)(2,1)S(1)}, bf16[4,7168]{1,0:T(4,128)(2,1)S(1)}, u32[]{:S(2)}, u32[]{:S(2)}) collective-permute-start(bf16[4,7168]{1,0:T(4,128)(2,1)S(1)} %get-tuple-element.31), channel_id=1, source_target_pairs={{0,8},{4,12},{8,0},{12,4},{16,24},{20,28},{24,16},{28,20},{1,9},{5... | collective-permute-start | bytes 172040 | tf_op jit(solution)/shard_map/ppermute | solution.py:30
  20.4 0.3 turn_pages.1.refs_11_
  20.7 1.6 %collective-permute-start.14 = (bf16[2,2,32,1792]{3,2,1,0:T(8,128)(2,1)S(1)}, bf16[2,2,32,1792]{3,2,1,0:T(8,128)(2,1)S(1)}, u32[]{:S(2)}, u32[]{:S(2)}) collective-permute-start(bf16[2,2,32,1792]{3,2,1,0:T(8,128)(2,1)S(1)} %turn_pages.1.refs_11_), channel_id=1, source_target_pairs={{0,16},{4,12},{8,24},{12,4},{16,0},{20,28},{24,8},{28,20},{1,17},{... | collective-permute-start | bytes 1376264 | tf_op jit(solution)/shard_map/ppermute | solution.py:163
  22.3 0.6 %collective-permute-done.6.refs_4_ = bf16[4,7168]{1,0:T(4,128)(2,1)S(1)} collective-permute-done((bf16[4,7168]{1,0:T(4,128)(2,1)S(1)}, bf16[4,7168]{1,0:T(4,128)(2,1)S(1)}, u32[]{:S(2)}, u32[]{:S(2)}) %collective-permute-start.6) | collective-permute-done | bytes 57376 | tf_op jit(solution)/shard_map/ppermute | solution.py:30
  23.0 0.4 collective-permute-done.7.refs_5_
  23.5 2.8 %attend.1 = (bf16[4,32,256]{2,1,0:T(8,128)(2,1)S(1)}, bf16[4,32,256]{2,1,0:T(8,128)(2,1)S(1)}, bf16[2,4,16,1792]{3,2,1,0:T(8,128)(2,1)S(1)}, bf16[20,64,1792]{2,1,0:T(8,128)(2,1)}) custom-call(s32[4]{0:T(128)S(1)} %copy-done.4, s32[4]{0:T(128)S(1)} %copy-done.5, s32[4,16]{1,0:T(4,128)S(1)} %copy-done.3, bf16[4,7168]{1,0:T(4,128)(2,1)S(1)} %collective-permute-done.5.refs_3_, ...), custom_call_target="tpu_custom_call" | custom-call | tf_op jit(solution)/shard_map/attend/pallas_call | solution.py:523
  26.3 0.5 collective-permute-start.10
  26.8 0.9 %collective-permute-done.10._ = bf16[4,32,256]{2,1,0:T(8,128)(2,1)S(1)} collective-permute-done((bf16[4,32,256]{2,1,0:T(8,128)(2,1)S(1)}, bf16[4,32,256]{2,1,0:T(8,128)(2,1)S(1)}, u32[]{:S(2)}, u32[]{:S(2)}) %collective-permute-start.10) | collective-permute-done | bytes 65568 | tf_op jit(solution)/shard_map/ppermute | solution.py:30
  27.7 2.7 %collective-permute-start.11 = (bf16[2,32,256]{2,1,0:T(8,128)(2,1)S(1)}, bf16[2,32,256]{2,1,0:T(8,128)(2,1)S(1)}, u32[]{:S(2)}, u32[]{:S(2)}) collective-permute-start(bf16[2,32,256]{2,1,0:T(8,128)(2,1)S(1)} %pad_maximum_fusion.1), channel_id=1, source_target_pairs={{0,24},{4,28},{8,16},{12,20},{16,8},{20,12},{24,0},{28,4},{1,25},{... | collective-permute-start | bytes 98312 | tf_op jit(solution)/shard_map/ppermute | solution.py:30
  30.4 0.6 %collective-permute-start.12 = (bf16[2,32,256]{2,1,0:T(8,128)(2,1)S(1)}, bf16[2,32,256]{2,1,0:T(8,128)(2,1)S(1)}, u32[]{:S(2)}, u32[]{:S(2)}) collective-permute-start(bf16[2,32,256]{2,1,0:T(8,128)(2,1)S(1)} %pad_maximum_fusion.2), channel_id=1, source_target_pairs={{0,16},{4,20},{8,24},{12,28},{16,0},{20,4},{24,8},{28,12},{1,17},{... | collective-permute-start | bytes 98312 | tf_op jit(solution)/shard_map/ppermute | solution.py:30
  31.0 0.2 collective-permute-start.13
  31.3 2.2 %write_pool.1.refs_5_.refs_10_ = bf16[20,64,1792]{2,1,0:T(8,128)(2,1)} custom-call(bf16[20,64,1792]{2,1,0:T(8,128)(2,1)S(1)} %bitcast.41, bf16[4,32,256]{2,1,0:T(8,128)(2,1)S(1)} %collective-permute-done.10._), custom_call_target="tpu_custom_call" | custom-call | tf_op jit(solution)/shard_map/write_pool/pallas_call | solution.py:58
  33.5 0.9 %collective-permute-done.12.refs_1_ = bf16[2,32,256]{2,1,0:T(8,128)(2,1)S(1)} collective-permute-done((bf16[2,32,256]{2,1,0:T(8,128)(2,1)S(1)}, bf16[2,32,256]{2,1,0:T(8,128)(2,1)S(1)}, u32[]{:S(2)}, u32[]{:S(2)}) %collective-permute-start.12) | collective-permute-done | bytes 32800 | tf_op jit(solution)/shard_map/ppermute | solution.py:30
  34.4 0.6 %collective-permute-done.13.refs_2_ = bf16[2,32,256]{2,1,0:T(8,128)(2,1)S(1)} collective-permute-done((bf16[2,32,256]{2,1,0:T(8,128)(2,1)S(1)}, bf16[2,32,256]{2,1,0:T(8,128)(2,1)S(1)}, u32[]{:S(2)}, u32[]{:S(2)}) %collective-permute-start.13) | collective-permute-done | bytes 32800 | tf_op jit(solution)/shard_map/ppermute | solution.py:30
  34.9 1.0 %out_project.1 = (f32[4,4,4,1792]{3,2,1,0:T(4,128)S(1)}, bf16[4,4,4,1792]{3,2,1,0:T(4,128)(2,1)S(1)}) custom-call(bf16[2,32,256]{2,1,0:T(8,128)(2,1)S(1)} %collective-permute-done.11.refs_0_, bf16[2,32,256]{2,1,0:T(8,128)(2,1)S(1)} %collective-permute-done.12.refs_1_, bf16[2,32,256]{2,1,0:T(8,128)(2,1)S(1)} %collective-permute-done.13.refs_2_, ...), custom_call_target="tpu_custom_call" | custom-call | tf_op jit(solution)/shard_map/out_project/pallas_call | solution.py:582
  36.0 0.1 collective-permute-start.15
  36.1 0.2 choose_half.1
  36.2 0.6 %collective-permute-start.19 = (bf16[2,32,1792]{2,1,0:T(8,128)(2,1)S(1)}, bf16[2,32,1792]{2,1,0:T(8,128)(2,1)S(1)}, u32[]{:S(2)}, u32[]{:S(2)}) collective-permute-start(bf16[2,32,1792]{2,1,0:T(8,128)(2,1)S(1)} %choose_half.1), channel_id=1, source_target_pairs={{0,4},{4,0},{8,12},{12,8},{16,20},{20,16},{24,28},{28,24},{1,5},{5... | collective-permute-start | bytes 688136 | tf_op jit(solution)/shard_map/ppermute | solution.py:30
  36.8 0.7 %collective-permute-done.15 = bf16[4,4,4,1792]{3,2,1,0:T(4,128)(2,1)S(1)} collective-permute-done((bf16[4,4,4,1792]{3,2,1,0:T(4,128)(2,1)S(1)}, bf16[4,4,4,1792]{3,2,1,0:T(4,128)(2,1)S(1)}, u32[]{:S(2)}, u32[]{:S(2)}) %collective-permute-start.15) | collective-permute-done | bytes 229408 | tf_op jit(solution)/shard_map/ppermute | solution.py:30
  37.5 0.2 fusion.7
  37.8 1.3 %collective-permute-start.18 = (bf16[4,4,1792]{2,1,0:T(4,128)(2,1)S(1)}, bf16[4,4,1792]{2,1,0:T(4,128)(2,1)S(1)}, u32[]{:S(2)}, u32[]{:S(2)}) collective-permute-start(bf16[4,4,1792]{2,1,0:T(4,128)(2,1)S(1)} %get-tuple-element.50), channel_id=1, source_target_pairs={{0,24},{4,28},{8,16},{12,20},{16,8},{20,12},{24,0},{28,4},{1,25},{... | collective-permute-start | bytes 172040 | tf_op jit(solution)/shard_map/ppermute | solution.py:30
  39.1 0.6 %collective-permute-start.17 = (bf16[4,4,1792]{2,1,0:T(4,128)(2,1)S(1)}, bf16[4,4,1792]{2,1,0:T(4,128)(2,1)S(1)}, u32[]{:S(2)}, u32[]{:S(2)}) collective-permute-start(bf16[4,4,1792]{2,1,0:T(4,128)(2,1)S(1)} %get-tuple-element.51), channel_id=1, source_target_pairs={{0,16},{4,20},{8,24},{12,28},{16,0},{20,4},{24,8},{28,12},{1,17},{... | collective-permute-start | bytes 172040 | tf_op jit(solution)/shard_map/ppermute | solution.py:30
  39.7 1.7 %collective-permute-start.16 = (bf16[4,4,1792]{2,1,0:T(4,128)(2,1)S(1)}, bf16[4,4,1792]{2,1,0:T(4,128)(2,1)S(1)}, u32[]{:S(2)}, u32[]{:S(2)}) collective-permute-start(bf16[4,4,1792]{2,1,0:T(4,128)(2,1)S(1)} %get-tuple-element.49), channel_id=1, source_target_pairs={{0,8},{4,12},{8,0},{12,4},{16,24},{20,28},{24,16},{28,20},{1,9},{5... | collective-permute-start | bytes 172040 | tf_op jit(solution)/shard_map/ppermute | solution.py:30
  41.3 1.8 %place_page.1 = (f32[4,1792]{1,0:T(4,128)S(1)}, bf16[20,64,1792]{2,1,0:T(8,128)(2,1)}, bf16[20,64,1792]{2,1,0:T(8,128)(2,1)}) custom-call(s32[4]{0:T(128)S(1)} %copy-done.4, s32[4]{0:T(128)S(1)} %copy-done.5, s32[4,16]{1,0:T(4,128)S(1)} %copy-done.3, f32[8,128]{1,0:T(8,128)S(1)} %find_sources.1._.source_ref, ...), custom_call_target="tpu_custom_call", output_to_operand_aliasing={{1}: (15, {}), {2}: (16, {})} | custom-call | tf_op jit(solution)/shard_map/place_page/pallas_call | solution.py:678
  43.1 0.1 collective-permute-done.18
  43.2 0.7 %collective-permute-done.17 = bf16[4,4,1792]{2,1,0:T(4,128)(2,1)S(1)} collective-permute-done((bf16[4,4,1792]{2,1,0:T(4,128)(2,1)S(1)}, bf16[4,4,1792]{2,1,0:T(4,128)(2,1)S(1)}, u32[]{:S(2)}, u32[]{:S(2)}) %collective-permute-start.17) | collective-permute-done | bytes 57376 | tf_op jit(solution)/shard_map/ppermute | solution.py:30
  44.1 3.6 %collective-permute-start.22 = (bf16[4,1792]{1,0:T(4,128)(2,1)S(1)}, bf16[4,1792]{1,0:T(4,128)(2,1)S(1)}, u32[]{:S(2)}, u32[]{:S(2)}) collective-permute-start(bf16[4,1792]{1,0:T(4,128)(2,1)S(1)} %get-tuple-element.61), channel_id=1, source_target_pairs={{0,3},{1,2},{2,1},{3,0},{4,7},{5,6},{6,5},{7,4},{8,11},{9,10},{10,... | collective-permute-start | bytes 43016 | tf_op jit(solution)/shard_map/ppermute | solution.py:30
  47.7 0.8 %collective-permute-start.20 = (bf16[4,1792]{1,0:T(4,128)(2,1)S(1)}, bf16[4,1792]{1,0:T(4,128)(2,1)S(1)}, u32[]{:S(2)}, u32[]{:S(2)}) collective-permute-start(bf16[4,1792]{1,0:T(4,128)(2,1)S(1)} %get-tuple-element.60), channel_id=1, source_target_pairs={{0,1},{1,0},{2,3},{3,2},{4,5},{5,4},{6,7},{7,6},{8,9},{9,8},{10,11... | collective-permute-start | bytes 43016 | tf_op jit(solution)/shard_map/ppermute | solution.py:30
  48.5 1.1 %collective-permute-done.22 = bf16[4,1792]{1,0:T(4,128)(2,1)S(1)} collective-permute-done((bf16[4,1792]{1,0:T(4,128)(2,1)S(1)}, bf16[4,1792]{1,0:T(4,128)(2,1)S(1)}, u32[]{:S(2)}, u32[]{:S(2)}) %collective-permute-start.22) | collective-permute-done | bytes 14368 | tf_op jit(solution)/shard_map/ppermute | solution.py:30
  49.6 2.7 %collective-permute-done.21 = bf16[4,1792]{1,0:T(4,128)(2,1)S(1)} collective-permute-done((bf16[4,1792]{1,0:T(4,128)(2,1)S(1)}, bf16[4,1792]{1,0:T(4,128)(2,1)S(1)}, u32[]{:S(2)}, u32[]{:S(2)}) %collective-permute-start.21) | collective-permute-done | bytes 14368 | tf_op jit(solution)/shard_map/ppermute | solution.py:30
  52.3 0.6 %fusion.6 = bf16[4,1792]{1,0:T(4,128)(2,1)} fusion(f32[4,1792]{1,0:T(4,128)S(1)} %get-tuple-element.44, bf16[4,1792]{1,0:T(4,128)(2,1)S(1)} %collective-permute-done.22, bf16[4,1792]{1,0:T(4,128)(2,1)S(1)} %collective-permute-done.21, bf16[4,1792]{1,0:T(4,128)(2,1)S(1)} %collective-permute-done.20, f32[4,4,1792]{2,1,0:T(4,128)S(1)} %fusion.2), kind=kLoop, calls=%fused_computation.17 | loop fusion | flops 57344 | bytes 114688 | tf_op jit(solution)/shard_map/convert_element_type | solution.py:778
  (52 shorter events, 0.4 us)
Async XLA Ops:
  0.6 12.0 %copy-start = (bf16[896,14,384]{2,0,1:T(8,128)(2,1)S(1)}, bf16[896,14,384]{2,0,1:T(8,128)(2,1)}, u32[]{:S(2)}) copy-start(bf16[896,14,384]{2,0,1:T(8,128)(2,1)} %param.16) | copy-start | bytes 28901380
  3.0 1.4 %collective-permute-start = (bf16[4,4,1024]{2,1,0:T(4,128)(2,1)S(1)}, bf16[4,4,1024]{2,1,0:T(4,128)(2,1)S(1)}, u32[]{:S(2)}, u32[]{:S(2)}) collective-permute-start(bf16[4,4,1024]{2,1,0:T(4,128)(2,1)S(1)} %get-tuple-element.26), channel_id=1, source_target_pairs={{0,4},{4,0},{8,12},{12,8},{16,20},{20,16},{24,28},{28,24},{1,5},{5... | collective-permute-start | bytes 98312 | tf_op jit(solution)/shard_map/ppermute | solution.py:30
  3.5 5.5 %collective-permute-start.8 = (bf16[2,32,1792]{2,1,0:T(8,128)(2,1)S(1)}, bf16[2,32,1792]{2,1,0:T(8,128)(2,1)S(1)}, u32[]{:S(2)}, u32[]{:S(2)}) collective-permute-start(bf16[2,32,1792]{2,1,0:T(8,128)(2,1)S(1)} %get-tuple-element.34), channel_id=1, source_target_pairs={{0,4},{4,0},{8,12},{12,8},{16,20},{20,16},{24,28},{28,24},{1,5},{5... | collective-permute-start | bytes 688136 | tf_op jit(solution)/shard_map/ppermute | solution.py:30
  4.4 6.7 %collective-permute-start.1 = (bf16[2,4,1024]{2,1,0:T(4,128)(2,1)S(1)}, bf16[2,4,1024]{2,1,0:T(4,128)(2,1)S(1)}, u32[]{:S(2)}, u32[]{:S(2)}) collective-permute-start(bf16[2,4,1024]{2,1,0:T(4,128)(2,1)S(1)} %pad_maximum_fusion.5), channel_id=1, source_target_pairs={{0,24},{4,28},{8,16},{12,20},{16,8},{20,12},{24,0},{28,4},{1,25},{... | collective-permute-start | bytes 49160 | tf_op jit(solution)/shard_map/ppermute | solution.py:30
  8.3 3.9 %collective-permute-start.2 = (bf16[2,4,1024]{2,1,0:T(4,128)(2,1)S(1)}, bf16[2,4,1024]{2,1,0:T(4,128)(2,1)S(1)}, u32[]{:S(2)}, u32[]{:S(2)}) collective-permute-start(bf16[2,4,1024]{2,1,0:T(4,128)(2,1)S(1)} %pad_maximum_fusion.6), channel_id=1, source_target_pairs={{0,16},{4,20},{8,24},{12,28},{16,0},{20,4},{24,8},{28,12},{1,17},{... | collective-permute-start | bytes 49160 | tf_op jit(solution)/shard_map/ppermute | solution.py:30
  8.9 3.8 %collective-permute-start.3 = (bf16[2,4,1024]{2,1,0:T(4,128)(2,1)S(1)}, bf16[2,4,1024]{2,1,0:T(4,128)(2,1)S(1)}, u32[]{:S(2)}, u32[]{:S(2)}) collective-permute-start(bf16[2,4,1024]{2,1,0:T(4,128)(2,1)S(1)} %pad_maximum_fusion.7), channel_id=1, source_target_pairs={{0,8},{4,12},{8,0},{12,4},{16,24},{20,28},{24,16},{28,20},{1,9},{5... | collective-permute-start | bytes 49160 | tf_op jit(solution)/shard_map/ppermute | solution.py:30
  9.1 11.4 %collective-permute-start.9 = (bf16[2,2,32,1792]{3,2,1,0:T(8,128)(2,1)S(1)}, bf16[2,2,32,1792]{3,2,1,0:T(8,128)(2,1)S(1)}, u32[]{:S(2)}, u32[]{:S(2)}) collective-permute-start(bf16[2,2,32,1792]{3,2,1,0:T(8,128)(2,1)S(1)} %pad_maximum_fusion.refs_0_.refs_6_), channel_id=1, source_target_pairs={{0,8},{4,20},{8,0},{12,28},{16,24},{20,4},{24,16},{28,12},{1,9},{5... | collective-permute-start | bytes 1376264 | tf_op jit(solution)/shard_map/ppermute | solution.py:163
  12.7 10.7 %slice-start = ((s8[4587520]{0:T(1024)(128)(4,1)}), s8[4194304]{0:T(1024)(128)(4,1)S(1)}, s32[]{:S(2)}) async-start(s8[4587520]{0:T(1024)(128)(4,1)} %bitcast.40), calls=%async_computation | async-start | bytes 8388608
  12.7 10.7 %slice-start.2 = ((s8[4587520]{0:T(1024)(128)(4,1)}), s8[4194304]{0:T(1024)(128)(4,1)S(1)}, s32[]{:S(2)}) async-start(s8[4587520]{0:T(1024)(128)(4,1)} %bitcast.42), calls=%async_computation.2 | async-start | bytes 8388608
  12.7 7.7 %copy-start.6 = (f32[14,384]{1,0:T(8,128)S(1)}, f32[14,384]{1,0:T(8,128)}, u32[]{:S(2)}) copy-start(f32[14,384]{1,0:T(8,128)} %param.17) | copy-start | bytes 64516
  12.7 10.7 %slice-start.1 = ((s8[4587520]{0:T(1024)(128)(4,1)}), s8[393216]{0:T(1024)(128)(4,1)S(1)}, s32[]{:S(2)}) async-start(s8[4587520]{0:T(1024)(128)(4,1)} %bitcast.40), calls=%async_computation.1 | async-start | bytes 786432
  12.7 10.7 %slice-start.3 = ((s8[4587520]{0:T(1024)(128)(4,1)}), s8[393216]{0:T(1024)(128)(4,1)S(1)}, s32[]{:S(2)}) async-start(s8[4587520]{0:T(1024)(128)(4,1)} %bitcast.42), calls=%async_computation.3 | async-start | bytes 786432
  12.7 10.7 %copy-start.1 = (bf16[4,7168]{1,0:T(4,128)(2,1)S(1)}, bf16[4,7168]{1,0:T(4,128)(2,1)}, u32[]{:S(2)}) copy-start(bf16[4,7168]{1,0:T(4,128)(2,1)} %refs_4_.1) | copy-start | bytes 172036
  12.7 10.7 %copy-start.3 = (s32[4,16]{1,0:T(4,128)S(1)}, s32[4,16]{1,0:T(4,128)}, u32[]{:S(2)}) copy-start(s32[4,16]{1,0:T(4,128)} %table_ref.3) | copy-start | bytes 772
  12.7 10.7 %copy-start.4 = (s32[4]{0:T(128)S(1)}, s32[4]{0:T(128)}, u32[]{:S(2)}) copy-start(s32[4]{0:T(128)} %length_ref.3) | copy-start | bytes 52
  12.7 10.7 %copy-start.5 = (s32[4]{0:T(128)S(1)}, s32[4]{0:T(128)}, u32[]{:S(2)}) copy-start(s32[4]{0:T(128)} %slot_ref.3) | copy-start | bytes 52
  15.0 1.7 %collective-permute-start.4 = (f32[4,4,5376]{2,1,0:T(4,128)S(1)}, f32[4,4,5376]{2,1,0:T(4,128)S(1)}, u32[]{:S(2)}, u32[]{:S(2)}) collective-permute-start(f32[4,4,5376]{2,1,0:T(4,128)S(1)} %get-tuple-element.28), channel_id=1, source_target_pairs={{0,4},{4,0},{8,12},{12,8},{16,20},{20,16},{24,28},{28,24},{1,5},{5... | collective-permute-start | bytes 1032200 | tf_op jit(solution)/shard_map/ppermute | solution.py:30
  16.8 5.5 %collective-permute-start.5 = (bf16[4,7168]{1,0:T(4,128)(2,1)S(1)}, bf16[4,7168]{1,0:T(4,128)(2,1)S(1)}, u32[]{:S(2)}, u32[]{:S(2)}) collective-permute-start(bf16[4,7168]{1,0:T(4,128)(2,1)S(1)} %get-tuple-element.29), channel_id=1, source_target_pairs={{0,24},{4,28},{8,16},{12,20},{16,8},{20,12},{24,0},{28,4},{1,25},{... | collective-permute-start | bytes 172040 | tf_op jit(solution)/shard_map/ppermute | solution.py:30
  18.4 4.6 %collective-permute-start.6 = (bf16[4,7168]{1,0:T(4,128)(2,1)S(1)}, bf16[4,7168]{1,0:T(4,128)(2,1)S(1)}, u32[]{:S(2)}, u32[]{:S(2)}) collective-permute-start(bf16[4,7168]{1,0:T(4,128)(2,1)S(1)} %get-tuple-element.30), channel_id=1, source_target_pairs={{0,16},{4,20},{8,24},{12,28},{16,0},{20,4},{24,8},{28,12},{1,17},{... | collective-permute-start | bytes 172040 | tf_op jit(solution)/shard_map/ppermute | solution.py:30
  18.5 4.9 %collective-permute-start.7 = (bf16[4,7168]{1,0:T(4,128)(2,1)S(1)}, bf16[4,7168]{1,0:T(4,128)(2,1)S(1)}, u32[]{:S(2)}, u32[]{:S(2)}) collective-permute-start(bf16[4,7168]{1,0:T(4,128)(2,1)S(1)} %get-tuple-element.31), channel_id=1, source_target_pairs={{0,8},{4,12},{8,0},{12,4},{16,24},{20,28},{24,16},{28,20},{1,9},{5... | collective-permute-start | bytes 172040 | tf_op jit(solution)/shard_map/ppermute | solution.py:30
  20.7 14.2 %collective-permute-start.14 = (bf16[2,2,32,1792]{3,2,1,0:T(8,128)(2,1)S(1)}, bf16[2,2,32,1792]{3,2,1,0:T(8,128)(2,1)S(1)}, u32[]{:S(2)}, u32[]{:S(2)}) collective-permute-start(bf16[2,2,32,1792]{3,2,1,0:T(8,128)(2,1)S(1)} %turn_pages.1.refs_11_), channel_id=1, source_target_pairs={{0,16},{4,12},{8,24},{12,4},{16,0},{20,28},{24,8},{28,20},{1,17},{... | collective-permute-start | bytes 1376264 | tf_op jit(solution)/shard_map/ppermute | solution.py:163
  26.3 1.4 %collective-permute-start.10 = (bf16[4,32,256]{2,1,0:T(8,128)(2,1)S(1)}, bf16[4,32,256]{2,1,0:T(8,128)(2,1)S(1)}, u32[]{:S(2)}, u32[]{:S(2)}) collective-permute-start(bf16[4,32,256]{2,1,0:T(8,128)(2,1)S(1)} %get-tuple-element.36), channel_id=1, source_target_pairs={{0,4},{4,0},{8,12},{12,8},{16,20},{20,16},{24,28},{28,24},{1,5},{5... | collective-permute-start | bytes 196616 | tf_op jit(solution)/shard_map/ppermute | solution.py:30
  27.7 5.7 %collective-permute-start.11 = (bf16[2,32,256]{2,1,0:T(8,128)(2,1)S(1)}, bf16[2,32,256]{2,1,0:T(8,128)(2,1)S(1)}, u32[]{:S(2)}, u32[]{:S(2)}) collective-permute-start(bf16[2,32,256]{2,1,0:T(8,128)(2,1)S(1)} %pad_maximum_fusion.1), channel_id=1, source_target_pairs={{0,24},{4,28},{8,16},{12,20},{16,8},{20,12},{24,0},{28,4},{1,25},{... | collective-permute-start | bytes 98312 | tf_op jit(solution)/shard_map/ppermute | solution.py:30
  30.4 3.9 %collective-permute-start.12 = (bf16[2,32,256]{2,1,0:T(8,128)(2,1)S(1)}, bf16[2,32,256]{2,1,0:T(8,128)(2,1)S(1)}, u32[]{:S(2)}, u32[]{:S(2)}) collective-permute-start(bf16[2,32,256]{2,1,0:T(8,128)(2,1)S(1)} %pad_maximum_fusion.2), channel_id=1, source_target_pairs={{0,16},{4,20},{8,24},{12,28},{16,0},{20,4},{24,8},{28,12},{1,17},{... | collective-permute-start | bytes 98312 | tf_op jit(solution)/shard_map/ppermute | solution.py:30
  31.0 3.9 %collective-permute-start.13 = (bf16[2,32,256]{2,1,0:T(8,128)(2,1)S(1)}, bf16[2,32,256]{2,1,0:T(8,128)(2,1)S(1)}, u32[]{:S(2)}, u32[]{:S(2)}) collective-permute-start(bf16[2,32,256]{2,1,0:T(8,128)(2,1)S(1)} %pad_maximum_fusion.3), channel_id=1, source_target_pairs={{0,8},{4,12},{8,0},{12,4},{16,24},{20,28},{24,16},{28,20},{1,9},{5... | collective-permute-start | bytes 98312 | tf_op jit(solution)/shard_map/ppermute | solution.py:30
  34.9 6.4 %copy-start.2 = (f32[7168]{0:T(1024)S(1)}, f32[7168]{0:T(1024)}, u32[]{:S(2)}) copy-start(f32[7168]{0:T(1024)} %param.19) | copy-start | bytes 86020
  36.0 1.6 %collective-permute-start.15 = (bf16[4,4,4,1792]{3,2,1,0:T(4,128)(2,1)S(1)}, bf16[4,4,4,1792]{3,2,1,0:T(4,128)(2,1)S(1)}, u32[]{:S(2)}, u32[]{:S(2)}) collective-permute-start(bf16[4,4,4,1792]{3,2,1,0:T(4,128)(2,1)S(1)} %get-tuple-element.39), channel_id=1, source_target_pairs={{0,4},{4,0},{8,12},{12,8},{16,20},{20,16},{24,28},{28,24},{1,5},{5... | collective-permute-start | bytes 688136 | tf_op jit(solution)/shard_map/ppermute | solution.py:30
  36.2 5.1 %collective-permute-start.19 = (bf16[2,32,1792]{2,1,0:T(8,128)(2,1)S(1)}, bf16[2,32,1792]{2,1,0:T(8,128)(2,1)S(1)}, u32[]{:S(2)}, u32[]{:S(2)}) collective-permute-start(bf16[2,32,1792]{2,1,0:T(8,128)(2,1)S(1)} %choose_half.1), channel_id=1, source_target_pairs={{0,4},{4,0},{8,12},{12,8},{16,20},{20,16},{24,28},{28,24},{1,5},{5... | collective-permute-start | bytes 688136 | tf_op jit(solution)/shard_map/ppermute | solution.py:30
  37.8 5.4 %collective-permute-start.18 = (bf16[4,4,1792]{2,1,0:T(4,128)(2,1)S(1)}, bf16[4,4,1792]{2,1,0:T(4,128)(2,1)S(1)}, u32[]{:S(2)}, u32[]{:S(2)}) collective-permute-start(bf16[4,4,1792]{2,1,0:T(4,128)(2,1)S(1)} %get-tuple-element.50), channel_id=1, source_target_pairs={{0,24},{4,28},{8,16},{12,20},{16,8},{20,12},{24,0},{28,4},{1,25},{... | collective-permute-start | bytes 172040 | tf_op jit(solution)/shard_map/ppermute | solution.py:30
  39.1 4.9 %collective-permute-start.17 = (bf16[4,4,1792]{2,1,0:T(4,128)(2,1)S(1)}, bf16[4,4,1792]{2,1,0:T(4,128)(2,1)S(1)}, u32[]{:S(2)}, u32[]{:S(2)}) collective-permute-start(bf16[4,4,1792]{2,1,0:T(4,128)(2,1)S(1)} %get-tuple-element.51), channel_id=1, source_target_pairs={{0,16},{4,20},{8,24},{12,28},{16,0},{20,4},{24,8},{28,12},{1,17},{... | collective-permute-start | bytes 172040 | tf_op jit(solution)/shard_map/ppermute | solution.py:30
  39.7 4.3 %collective-permute-start.16 = (bf16[4,4,1792]{2,1,0:T(4,128)(2,1)S(1)}, bf16[4,4,1792]{2,1,0:T(4,128)(2,1)S(1)}, u32[]{:S(2)}, u32[]{:S(2)}) collective-permute-start(bf16[4,4,1792]{2,1,0:T(4,128)(2,1)S(1)} %get-tuple-element.49), channel_id=1, source_target_pairs={{0,8},{4,12},{8,0},{12,4},{16,24},{20,28},{24,16},{28,20},{1,9},{5... | collective-permute-start | bytes 172040 | tf_op jit(solution)/shard_map/ppermute | solution.py:30
  44.1 5.6 %collective-permute-start.22 = (bf16[4,1792]{1,0:T(4,128)(2,1)S(1)}, bf16[4,1792]{1,0:T(4,128)(2,1)S(1)}, u32[]{:S(2)}, u32[]{:S(2)}) collective-permute-start(bf16[4,1792]{1,0:T(4,128)(2,1)S(1)} %get-tuple-element.61), channel_id=1, source_target_pairs={{0,3},{1,2},{2,1},{3,0},{4,7},{5,6},{6,5},{7,4},{8,11},{9,10},{10,... | collective-permute-start | bytes 43016 | tf_op jit(solution)/shard_map/ppermute | solution.py:30
  47.7 4.6 %collective-permute-start.21 = (bf16[4,1792]{1,0:T(4,128)(2,1)S(1)}, bf16[4,1792]{1,0:T(4,128)(2,1)S(1)}, u32[]{:S(2)}, u32[]{:S(2)}) collective-permute-start(bf16[4,1792]{1,0:T(4,128)(2,1)S(1)} %get-tuple-element.62), channel_id=1, source_target_pairs={{0,2},{1,3},{2,0},{3,1},{4,6},{5,7},{6,4},{7,5},{8,10},{9,11},{10,... | collective-permute-start | bytes 43016 | tf_op jit(solution)/shard_map/ppermute | solution.py:30
  47.7 4.6 %collective-permute-start.20 = (bf16[4,1792]{1,0:T(4,128)(2,1)S(1)}, bf16[4,1792]{1,0:T(4,128)(2,1)S(1)}, u32[]{:S(2)}, u32[]{:S(2)}) collective-permute-start(bf16[4,1792]{1,0:T(4,128)(2,1)S(1)} %get-tuple-element.60), channel_id=1, source_target_pairs={{0,1},{1,0},{2,3},{3,2},{4,5},{5,4},{6,7},{7,6},{8,9},{9,8},{10,11... | collective-permute-start | bytes 43016 | tf_op jit(solution)/shard_map/ppermute | solution.py:30

commit v11 on v10

--- a/solution.py
+++ b/solution.py
@@ -185,7 +185,6 @@
                 if row == 0 and j == 0:
                     found = put(2 * down, pick(2))
                     found = put(2 * down + 1, pick(3))
-                    found = put(2 * down + 2, source)
         out_ref[...] = found
 
     return pl.pallas_call(
@@ -477,6 +476,9 @@
         pl.when(long_length > half * page)(lambda: attend_all(max_pages))
         attended = attended_ref[...]
 
+        toward = jnp.int32(0)
+        for s in range(slots):
+            toward = jnp.where(leaving == s, slot_ref[s] // slots ^ here, toward)
         token = token_ref[:, pl.ds(pl.multiple_of(column_block * width, LANES), width)].astype(F32)
         extra = []
         for source in new_rows + (token,):
@@ -503,7 +505,7 @@
             for h in range(heads):
                 tiles[h // per] = jnp.where(count == h % per, turned[h], tiles[h // per])
             tiles[-1] = jnp.where((count == per - 1) & (lane % share >= share - 2), goal, tiles[-1])
-            block = jnp.concatenate([jnp.concatenate(tiles, axis=1), extra], axis=0).astype(BF16)
+            block = jnp.concatenate([jnp.concatenate(tiles, axis=1), jnp.where(toward == k, extra, 0.0)], axis=0).astype(BF16)
             (pack_keep, pack_send)[k % 2][k // 2] = block
 
         at = lax.broadcasted_iota(jnp.int32, (tall, width), 0)
@@ -543,7 +545,6 @@
 def out_project(blocks, weight, pieces, slots, *after):
     chips = len(blocks)
     depth, width = weight.shape
-    high = -(-slots // 8) * 8
     rows = 2 * chips * slots
     piece = width // pieces
 
@@ -551,7 +552,7 @@
         block_refs, weight_ref = refs[:chips][::-1], refs[chips]
         keep_ref, send_ref = refs[chips + 1 + len(after) :]
         gathered = jnp.concatenate(
-            [block_refs[d][e, :high, :].astype(F32) for d in range(chips) for e in range(2)], axis=0
+            [block_refs[d][: 2 * slots, :].astype(F32) for d in range(chips)], axis=0
         )
         here = lax.axis_index("req")
         share = LANES // (2 * chips)
@@ -582,7 +583,7 @@
     return pl.pallas_call(
         kernel,
         out_shape=(jax.ShapeDtypeStruct(shape, F32), jax.ShapeDtypeStruct(shape, BF16)),
-        in_specs=[VMEM] * (chips + 1) + [HBM] * min(1, len(after)) + [ANY] * (len(after) - 1),
+        in_specs=[VMEM] * (chips + 1) + [ANY] * len(after),
         out_specs=(VMEM, VMEM),
         compiler_params=pltpu.CompilerParams(vmem_limit_bytes=10 * MIB),
         cost_estimate=cost(2 * rows * weight.size, 2 * weight.size),
@@ -597,9 +598,7 @@
     page, width = key_out.shape[1:]
     half = page // 2
     slots = tokens.shape[0]
-    high = -(-slots // 8) * 8
     strips = width // PACK
-
     tall = patches.shape[2]
 
     def kernel(length_ref, slot_ref, table_ref, source_ref, patch_ref, *refs):
@@ -608,7 +607,7 @@
         half_refs = refs[chips + 2 : chips + 2 + across]
         turned_refs = refs[chips + 2 + across : chips + 2 + across + rows]
         other_ref = refs[chips + 1 + count]
-        _, _, base_ref, key_ref, value_ref, buffer, arrived, out_sems, patch_sems = refs[chips + 2 + count :]
+        _, _, base_ref, key_ref, value_ref, buffer, out_sems, patch_sems = refs[chips + 2 + count :]
         here = lax.axis_index("req")
         leaving = leaving_slot(slot_ref, slots, here)
 
@@ -626,7 +625,7 @@
                     patch(n, s).start()
 
         column = pl.multiple_of(lax.axis_index("head") * width, LANES)
-        page_at, offset, source = [number_at(source_ref, 2 * down + j) for j in range(3)]
+        page_at, offset = [number_at(source_ref, 2 * down + j) for j in range(2)]
         own_rows, other_rows = [pl.ds(pl.multiple_of((here % 2 ^ e) * half, half), half) for e in range(2)]
 
         def use(ref):
@@ -634,16 +633,12 @@
 
         with_half(number_at(source_ref, 0), across, 0, half_refs, turned_refs, use)
         buffer[:, other_rows, :] = other_ref[...]
-        for d in range(chips):
-            for e in range(2):
-
-                @pl.when(source == 2 * d + e)
-                def _():
-                    arrived[...] = pack_refs[d][e].astype(F32)
+        arrived = pack_refs[0][2 * slots :, :].astype(F32)
+        for ref in pack_refs[1:]:
+            arrived = arrived + ref[2 * slots :, :].astype(F32)
 
         def fresh(n):
-            strip = high + n * strips
-            return jnp.concatenate([arrived[strip + i : strip + i + 1, :] for i in range(strips)], axis=1)
+            return jnp.concatenate([arrived[n * strips + i : n * strips + i + 1, :] for i in range(strips)], axis=1)
 
         at = lax.broadcasted_iota(jnp.int32, (slots, width), 0)
         token = jnp.where(
@@ -682,7 +677,6 @@
         out_specs=(VMEM, HBM, HBM),
         scratch_shapes=[
             pltpu.VMEM((2, page, width), BF16),
-            pltpu.VMEM(packs[0].shape[1:], F32),
             pltpu.SemaphoreType.DMA((2,)),
             pltpu.SemaphoreType.DMA((2, slots)),
         ],
@@ -744,18 +738,23 @@
         turning[0],
     )
     packs_got = swap(pack_send, "req", 1)
-    packs = spread_pairs(pack_keep, packs_got)
-    key_out = write_pool(key_pool, packs_got)
-
+    high = -(-slots // 8) * 8
+    merged = [
+        jnp.concatenate([pack_keep[d, :slots], packs_got[d, :slots], pack_keep[d, high:] + packs_got[d, high:]], axis=0)
+        for d in range(chips)
+    ]
+    packs = [merged[0]] + [swap(merged[d], "req", 2 * d) for d in range(1, chips)]
 
     keep, send = out_project(
-        packs, staged, head_groups, slots, *in_hbm(key_out), turned[0]
+        packs, staged, head_groups, slots, turned[0]
     )
     total = keep + swap(send, "req", 1).astype(F32)
     from_other = swap(choose_half(sources, halves, turned, keep), "req", 1)
     summed = total[0]
-    for d in range(1, chips):
+    for d in reversed(range(1, chips)):
         summed = summed + swap(total[d].astype(BF16), "req", 2 * d).astype(F32)
+    key_out = write_pool(key_pool, from_other)
+    summed, key_out = lax.optimization_barrier((summed, key_out))
     base, key_out, value_out = place_page(
         lengths,
         new_slot,
@@ -771,9 +770,8 @@
         key_out,
         value_out,
     )
-    summed, base = lax.optimization_barrier((summed, base))
     hidden = summed[0]
-    for j in range(1, head_groups):
+    for j in [head_groups - 1, *range(1, head_groups - 1)]:
         hidden = hidden + swap(summed[j].astype(BF16), "head", j).astype(F32)
     hidden_out = (hidden + base).astype(BF16)
     return (hidden_out, key_out, value_out)

time: 53.5 us -> 55 us (1.028)
  waiting for transfers between devices: 12.5 us -> 13.6 us
  starting transfers between devices: 25.1 us -> 25.9 us
    ppermute x21, waiting for transfers between devices: 12.5 us -> 13.6 us  [swap(): return lax.ppermute(value, axis, [(i, i ^ step) for i in range(size)])]
    ppermute x21, starting transfers between devices: 21.4 us -> 22.3 us  [swap(): return lax.ppermute(value, axis, [(i, i ^ step) for i in range(size)])]
  transfers between devices with their start and end apart: 23 -> 23, of which waited for: 14 -> 14; matrix products, arithmetic and copies ran while one was open for 1% -> 1% of each run, Pallas kernels for 19% -> 18%
where the time goes in v11:
time: 55 us; the launch traced here: 54.9 us
  starting transfers between devices  25.9 us (47%)
  waiting for transfers between devices  13.6 us (25%)
  Pallas kernels  13.2 us (24%)
  other arithmetic  1.02 us (2%)
  between operations  0.98 us (2%)
    ppermute x21, starting transfers between devices, swap(): return lax.ppermute(value, axis, [(i, i ^ step) for i in range(size)])  22.3 us
    ppermute x21, waiting for transfers between devices, swap(): return lax.ppermute(value, axis, [(i, i ^ step) for i in range(size)])  13.6 us
    ppermute x2, starting transfers between devices, swap_pages(): lax.ppermute(value, 'req', [(i, i ^ steps[i]) for i in range(2 * chips)])  3.62 us
    pallas_call x1, Pallas kernels, attend(): pl.pallas_call(kernel, out_shape=(packed, packed, jax.ShapeDtypeStruct((2...  2.84 us
    pallas_call x1, Pallas kernels, prepare(): pl.pallas_call(kernel, out_shape=(blocks, blocks, halves, halves), in_spe...  2.33 us
    pallas_call x1, Pallas kernels, project(): pl.pallas_call(kernel, out_shape=(shape, shape, jax.ShapeDtypeStruct(late...  2.28 us
    pallas_call x1, Pallas kernels, write_pool(): pl.pallas_call(kernel, out_shape=jax.ShapeDtypeStruct(pool.shape, pool.dt...  2.17 us
    pallas_call x1, Pallas kernels, place_page(): pl.pallas_call(kernel, out_shape=(jax.ShapeDtypeStruct((slots, width), F3...  1.7 us
  transfers between devices with their start and end apart: 23, of which 14 were waited for; matrix products, arithmetic and copies ran while one was open for 1% of the time, Pallas kernels for 18%

profile of v11, /device:TPU:0, one launch (start us, length us, event | category | flops | bytes accessed | tf_op | source)
XLA Modules:
  0.0 54.9 jit_solution(765337341802542923)
XLA Ops:
  0.6 2.3 %prepare.1 = (bf16[4,4,1024]{2,1,0:T(4,128)(2,1)S(1)}, bf16[4,4,1024]{2,1,0:T(4,128)(2,1)S(1)}, bf16[2,32,1792]{2,1,0:T(8,128)(2,1)S(1)}, bf16[2,32,1792]{2,1,0:T(8,128)(2,1)S(1)}) custom-call(bf16[4,7168]{1,0:T(4,128)(2,1)} %refs_4_.1, f32[1,7168]{1,0:T(1,128)} %bitcast.74, f32[1,7168]{1,0:T(1,128)} %bitcast.75, s32[4]{0:T(128)} %length_ref.3, ...), custom_call_target="tpu_custom_call" | custom-call | tf_op jit(solution)/shard_map/prepare/pallas_call | solution.py:129
  3.0 0.5 collective-permute-start
  3.5 0.1 collective-permute-start.8
  3.6 0.8 %collective-permute-done = bf16[4,4,1024]{2,1,0:T(4,128)(2,1)S(1)} collective-permute-done((bf16[4,4,1024]{2,1,0:T(4,128)(2,1)S(1)}, bf16[4,4,1024]{2,1,0:T(4,128)(2,1)S(1)}, u32[]{:S(2)}, u32[]{:S(2)}) %collective-permute-start) | collective-permute-done | bytes 32800 | tf_op jit(solution)/shard_map/ppermute | solution.py:30
  4.4 3.9 %collective-permute-start.1 = (bf16[2,4,1024]{2,1,0:T(4,128)(2,1)S(1)}, bf16[2,4,1024]{2,1,0:T(4,128)(2,1)S(1)}, u32[]{:S(2)}, u32[]{:S(2)}) collective-permute-start(bf16[2,4,1024]{2,1,0:T(4,128)(2,1)S(1)} %pad_maximum_fusion.1), channel_id=1, source_target_pairs={{0,24},{4,28},{8,16},{12,20},{16,8},{20,12},{24,0},{28,4},{1,25},{... | collective-permute-start | bytes 49160 | tf_op jit(solution)/shard_map/ppermute | solution.py:30
  8.3 0.6 %collective-permute-start.2 = (bf16[2,4,1024]{2,1,0:T(4,128)(2,1)S(1)}, bf16[2,4,1024]{2,1,0:T(4,128)(2,1)S(1)}, u32[]{:S(2)}, u32[]{:S(2)}) collective-permute-start(bf16[2,4,1024]{2,1,0:T(4,128)(2,1)S(1)} %pad_maximum_fusion.2), channel_id=1, source_target_pairs={{0,16},{4,20},{8,24},{12,28},{16,0},{20,4},{24,8},{28,12},{1,17},{... | collective-permute-start | bytes 49160 | tf_op jit(solution)/shard_map/ppermute | solution.py:30
  8.9 0.1 collective-permute-start.3
  9.1 2.0 %collective-permute-start.9 = (bf16[2,2,32,1792]{3,2,1,0:T(8,128)(2,1)S(1)}, bf16[2,2,32,1792]{3,2,1,0:T(8,128)(2,1)S(1)}, u32[]{:S(2)}, u32[]{:S(2)}) collective-permute-start(bf16[2,2,32,1792]{3,2,1,0:T(8,128)(2,1)S(1)} %pad_maximum_fusion.refs_0_.refs_6_), channel_id=1, source_target_pairs={{0,8},{4,20},{8,0},{12,28},{16,24},{20,4},{24,16},{28,12},{1,9},{5... | collective-permute-start | bytes 1376264 | tf_op jit(solution)/shard_map/ppermute | solution.py:163
  11.1 1.1 %collective-permute-done.2.refs_1_ = bf16[2,4,1024]{2,1,0:T(4,128)(2,1)S(1)} collective-permute-done((bf16[2,4,1024]{2,1,0:T(4,128)(2,1)S(1)}, bf16[2,4,1024]{2,1,0:T(4,128)(2,1)S(1)}, u32[]{:S(2)}, u32[]{:S(2)}) %collective-permute-start.2) | collective-permute-done | bytes 16416 | tf_op jit(solution)/shard_map/ppermute | solution.py:30
  12.2 0.4 collective-permute-done.3.refs_2_
  12.8 2.3 %project.1 = (f32[4,4,5376]{2,1,0:T(4,128)S(1)}, f32[4,4,5376]{2,1,0:T(4,128)S(1)}, bf16[224,7168]{1,0:T(8,128)(2,1)S(1)}) custom-call(bf16[2,4,1024]{2,1,0:T(4,128)(2,1)S(1)} %collective-permute-done.1.refs_0_, bf16[2,4,1024]{2,1,0:T(4,128)(2,1)S(1)} %collective-permute-done.2.refs_1_, bf16[2,4,1024]{2,1,0:T(4,128)(2,1)S(1)} %collective-permute-done.3.refs_2_, ...), custom_call_target="tpu_custom_call" | custom-call | tf_op jit(solution)/shard_map/project/pallas_call | solution.py:307
  15.0 0.1 collective-permute-start.4
  15.1 0.3 find_sources.1._.source_ref
  15.4 1.4 %collective-permute-done.4.got_ref = f32[4,4,5376]{2,1,0:T(4,128)S(1)} collective-permute-done((f32[4,4,5376]{2,1,0:T(4,128)S(1)}, f32[4,4,5376]{2,1,0:T(4,128)S(1)}, u32[]{:S(2)}, u32[]{:S(2)}) %collective-permute-start.4) | collective-permute-done | bytes 344096 | tf_op jit(solution)/shard_map/ppermute | solution.py:30
  16.8 0.1 combine.1
  16.8 1.6 %collective-permute-start.5 = (bf16[4,7168]{1,0:T(4,128)(2,1)S(1)}, bf16[4,7168]{1,0:T(4,128)(2,1)S(1)}, u32[]{:S(2)}, u32[]{:S(2)}) collective-permute-start(bf16[4,7168]{1,0:T(4,128)(2,1)S(1)} %get-tuple-element.29), channel_id=1, source_target_pairs={{0,24},{4,28},{8,16},{12,20},{16,8},{20,12},{24,0},{28,4},{1,25},{... | collective-permute-start | bytes 172040 | tf_op jit(solution)/shard_map/ppermute | solution.py:30
  18.4 0.1 collective-permute-start.6
  18.5 1.9 %collective-permute-start.7 = (bf16[4,7168]{1,0:T(4,128)(2,1)S(1)}, bf16[4,7168]{1,0:T(4,128)(2,1)S(1)}, u32[]{:S(2)}, u32[]{:S(2)}) collective-permute-start(bf16[4,7168]{1,0:T(4,128)(2,1)S(1)} %get-tuple-element.31), channel_id=1, source_target_pairs={{0,8},{4,12},{8,0},{12,4},{16,24},{20,28},{24,16},{28,20},{1,9},{5... | collective-permute-start | bytes 172040 | tf_op jit(solution)/shard_map/ppermute | solution.py:30
  20.4 0.3 turn_pages.1.refs_11_
  20.7 1.6 %collective-permute-start.14 = (bf16[2,2,32,1792]{3,2,1,0:T(8,128)(2,1)S(1)}, bf16[2,2,32,1792]{3,2,1,0:T(8,128)(2,1)S(1)}, u32[]{:S(2)}, u32[]{:S(2)}) collective-permute-start(bf16[2,2,32,1792]{3,2,1,0:T(8,128)(2,1)S(1)} %turn_pages.1.refs_11_), channel_id=1, source_target_pairs={{0,16},{4,12},{8,24},{12,4},{16,0},{20,28},{24,8},{28,20},{1,17},{... | collective-permute-start | bytes 1376264 | tf_op jit(solution)/shard_map/ppermute | solution.py:163
  22.3 0.6 %collective-permute-done.6.refs_4_ = bf16[4,7168]{1,0:T(4,128)(2,1)S(1)} collective-permute-done((bf16[4,7168]{1,0:T(4,128)(2,1)S(1)}, bf16[4,7168]{1,0:T(4,128)(2,1)S(1)}, u32[]{:S(2)}, u32[]{:S(2)}) %collective-permute-start.6) | collective-permute-done | bytes 57376 | tf_op jit(solution)/shard_map/ppermute | solution.py:30
  23.0 0.4 collective-permute-done.7.refs_5_
  23.5 2.8 %attend.1 = (bf16[4,32,256]{2,1,0:T(8,128)(2,1)S(1)}, bf16[4,32,256]{2,1,0:T(8,128)(2,1)S(1)}, bf16[2,4,16,1792]{3,2,1,0:T(8,128)(2,1)S(1)}, bf16[20,64,1792]{2,1,0:T(8,128)(2,1)}) custom-call(s32[4]{0:T(128)S(1)} %copy-done.4, s32[4]{0:T(128)S(1)} %copy-done.5, s32[4,16]{1,0:T(4,128)S(1)} %copy-done.3, bf16[4,7168]{1,0:T(4,128)(2,1)S(1)} %collective-permute-done.5.refs_3_, ...), custom_call_target="tpu_custom_call" | custom-call | tf_op jit(solution)/shard_map/attend/pallas_call | solution.py:525
  26.3 0.5 collective-permute-start.10
  26.8 0.9 %collective-permute-done.10 = bf16[4,32,256]{2,1,0:T(8,128)(2,1)S(1)} collective-permute-done((bf16[4,32,256]{2,1,0:T(8,128)(2,1)S(1)}, bf16[4,32,256]{2,1,0:T(8,128)(2,1)S(1)}, u32[]{:S(2)}, u32[]{:S(2)}) %collective-permute-start.10) | collective-permute-done | bytes 65568 | tf_op jit(solution)/shard_map/ppermute | solution.py:30
  27.7 3.7 %collective-permute-start.11 = (bf16[32,256]{1,0:T(8,128)(2,1)S(1)}, bf16[32,256]{1,0:T(8,128)(2,1)S(1)}, u32[]{:S(2)}, u32[]{:S(2)}) collective-permute-start(bf16[32,256]{1,0:T(8,128)(2,1)S(1)} %pad_maximum_fusion.5), channel_id=1, source_target_pairs={{0,24},{4,28},{8,16},{12,20},{16,8},{20,12},{24,0},{28,4},{1,25},{... | collective-permute-start | bytes 49160 | tf_op jit(solution)/shard_map/ppermute | solution.py:30
  31.5 0.1 collective-permute-start.12
  31.5 0.6 %collective-permute-start.13 = (bf16[32,256]{1,0:T(8,128)(2,1)S(1)}, bf16[32,256]{1,0:T(8,128)(2,1)S(1)}, u32[]{:S(2)}, u32[]{:S(2)}) collective-permute-start(bf16[32,256]{1,0:T(8,128)(2,1)S(1)} %pad_maximum_fusion.7), channel_id=1, source_target_pairs={{0,8},{4,12},{8,0},{12,4},{16,24},{20,28},{24,16},{28,20},{1,9},{5... | collective-permute-start | bytes 49160 | tf_op jit(solution)/shard_map/ppermute | solution.py:30
  32.2 1.0 %collective-permute-done.11.refs_0_ = bf16[32,256]{1,0:T(8,128)(2,1)S(1)} collective-permute-done((bf16[32,256]{1,0:T(8,128)(2,1)S(1)}, bf16[32,256]{1,0:T(8,128)(2,1)S(1)}, u32[]{:S(2)}, u32[]{:S(2)}) %collective-permute-start.11) | collective-permute-done | bytes 16416 | tf_op jit(solution)/shard_map/ppermute | solution.py:30
  33.2 2.1 %collective-permute-done.12.refs_1_ = bf16[32,256]{1,0:T(8,128)(2,1)S(1)} collective-permute-done((bf16[32,256]{1,0:T(8,128)(2,1)S(1)}, bf16[32,256]{1,0:T(8,128)(2,1)S(1)}, u32[]{:S(2)}, u32[]{:S(2)}) %collective-permute-start.12) | collective-permute-done | bytes 16416 | tf_op jit(solution)/shard_map/ppermute | solution.py:30
  35.2 0.1 collective-permute-done.13.refs_2_
  35.3 1.0 %out_project.1 = (f32[4,4,4,1792]{3,2,1,0:T(4,128)S(1)}, bf16[4,4,4,1792]{3,2,1,0:T(4,128)(2,1)S(1)}) custom-call(bf16[32,256]{1,0:T(8,128)(2,1)S(1)} %collective-permute-done.11.refs_0_, bf16[32,256]{1,0:T(8,128)(2,1)S(1)} %collective-permute-done.12.refs_1_, bf16[32,256]{1,0:T(8,128)(2,1)S(1)} %collective-permute-done.13.refs_2_, ...), custom_call_target="tpu_custom_call" | custom-call | tf_op jit(solution)/shard_map/out_project/pallas_call | solution.py:583
  36.4 0.1 collective-permute-start.15
  36.5 0.2 choose_half.1
  36.6 0.6 %collective-permute-start.19 = (bf16[2,32,1792]{2,1,0:T(8,128)(2,1)S(1)}, bf16[2,32,1792]{2,1,0:T(8,128)(2,1)S(1)}, u32[]{:S(2)}, u32[]{:S(2)}) collective-permute-start(bf16[2,32,1792]{2,1,0:T(8,128)(2,1)S(1)} %choose_half.1), channel_id=1, source_target_pairs={{0,4},{4,0},{8,12},{12,8},{16,20},{20,16},{24,28},{28,24},{1,5},{5... | collective-permute-start | bytes 688136 | tf_op jit(solution)/shard_map/ppermute | solution.py:30
  37.2 0.7 %collective-permute-done.15 = bf16[4,4,4,1792]{3,2,1,0:T(4,128)(2,1)S(1)} collective-permute-done((bf16[4,4,4,1792]{3,2,1,0:T(4,128)(2,1)S(1)}, bf16[4,4,4,1792]{3,2,1,0:T(4,128)(2,1)S(1)}, u32[]{:S(2)}, u32[]{:S(2)}) %collective-permute-start.15) | collective-permute-done | bytes 229408 | tf_op jit(solution)/shard_map/ppermute | solution.py:30
  37.9 0.2 fusion.11
  38.1 0.1 slice_bitcast_fusion.3
  38.2 1.5 %collective-permute-start.16 = (bf16[4,4,1792]{2,1,0:T(4,128)(2,1)S(1)}, bf16[4,4,1792]{2,1,0:T(4,128)(2,1)S(1)}, u32[]{:S(2)}, u32[]{:S(2)}) collective-permute-start(bf16[4,4,1792]{2,1,0:T(4,128)(2,1)S(1)} %get-tuple-element.49), channel_id=1, source_target_pairs={{0,24},{4,28},{8,16},{12,20},{16,8},{20,12},{24,0},{28,4},{1,25},{... | collective-permute-start | bytes 172040 | tf_op jit(solution)/shard_map/ppermute | solution.py:30
  39.7 2.0 %collective-permute-start.18 = (bf16[4,4,1792]{2,1,0:T(4,128)(2,1)S(1)}, bf16[4,4,1792]{2,1,0:T(4,128)(2,1)S(1)}, u32[]{:S(2)}, u32[]{:S(2)}) collective-permute-start(bf16[4,4,1792]{2,1,0:T(4,128)(2,1)S(1)} %get-tuple-element.50), channel_id=1, source_target_pairs={{0,8},{4,12},{8,0},{12,4},{16,24},{20,28},{24,16},{28,20},{1,9},{5... | collective-permute-start | bytes 172040 | tf_op jit(solution)/shard_map/ppermute | solution.py:30
  41.7 2.2 %write_pool.1.refs_10_ = bf16[20,64,1792]{2,1,0:T(8,128)(2,1)} custom-call(bf16[20,64,1792]{2,1,0:T(8,128)(2,1)S(1)} %bitcast.65, bf16[2,32,1792]{2,1,0:T(8,128)(2,1)S(1)} %collective-permute-done.19._.refs_9_), custom_call_target="tpu_custom_call" | custom-call | tf_op jit(solution)/shard_map/write_pool/pallas_call | solution.py:58
  43.9 0.9 %collective-permute-done.18 = bf16[4,4,1792]{2,1,0:T(4,128)(2,1)S(1)} collective-permute-done((bf16[4,4,1792]{2,1,0:T(4,128)(2,1)S(1)}, bf16[4,4,1792]{2,1,0:T(4,128)(2,1)S(1)}, u32[]{:S(2)}, u32[]{:S(2)}) %collective-permute-start.18) | collective-permute-done | bytes 57376 | tf_op jit(solution)/shard_map/ppermute | solution.py:30
  44.9 1.0 %collective-permute-done.17 = bf16[4,4,1792]{2,1,0:T(4,128)(2,1)S(1)} collective-permute-done((bf16[4,4,1792]{2,1,0:T(4,128)(2,1)S(1)}, bf16[4,4,1792]{2,1,0:T(4,128)(2,1)S(1)}, u32[]{:S(2)}, u32[]{:S(2)}) %collective-permute-start.17) | collective-permute-done | bytes 57376 | tf_op jit(solution)/shard_map/ppermute | solution.py:30
  46.0 3.6 %collective-permute-start.20 = (bf16[4,1792]{1,0:T(4,128)(2,1)S(1)}, bf16[4,1792]{1,0:T(4,128)(2,1)S(1)}, u32[]{:S(2)}, u32[]{:S(2)}) collective-permute-start(bf16[4,1792]{1,0:T(4,128)(2,1)S(1)} %get-tuple-element.64), channel_id=1, source_target_pairs={{0,3},{1,2},{2,1},{3,0},{4,7},{5,6},{6,5},{7,4},{8,11},{9,10},{10,... | collective-permute-start | bytes 43016 | tf_op jit(solution)/shard_map/ppermute | solution.py:30
  49.6 0.8 %collective-permute-start.21 = (bf16[4,1792]{1,0:T(4,128)(2,1)S(1)}, bf16[4,1792]{1,0:T(4,128)(2,1)S(1)}, u32[]{:S(2)}, u32[]{:S(2)}) collective-permute-start(bf16[4,1792]{1,0:T(4,128)(2,1)S(1)} %get-tuple-element.66), channel_id=1, source_target_pairs={{0,1},{1,0},{2,3},{3,2},{4,5},{5,4},{6,7},{7,6},{8,9},{9,8},{10,11... | collective-permute-start | bytes 43016 | tf_op jit(solution)/shard_map/ppermute | solution.py:30
  50.5 1.7 %place_page.1 = (f32[4,1792]{1,0:T(4,128)S(1)}, bf16[20,64,1792]{2,1,0:T(8,128)(2,1)}, bf16[20,64,1792]{2,1,0:T(8,128)(2,1)}) custom-call(s32[4]{0:T(128)S(1)} %copy-done.4, s32[4]{0:T(128)S(1)} %copy-done.5, s32[4,16]{1,0:T(4,128)S(1)} %copy-done.3, f32[8,128]{1,0:T(8,128)S(1)} %find_sources.1._.source_ref, ...), custom_call_target="tpu_custom_call", output_to_operand_aliasing={{1}: (15, {}), {2}: (16, {})} | custom-call | tf_op jit(solution)/shard_map/place_page/pallas_call | solution.py:673
  52.2 2.1 %collective-permute-done.22 = bf16[4,1792]{1,0:T(4,128)(2,1)S(1)} collective-permute-done((bf16[4,1792]{1,0:T(4,128)(2,1)S(1)}, bf16[4,1792]{1,0:T(4,128)(2,1)S(1)}, u32[]{:S(2)}, u32[]{:S(2)}) %collective-permute-start.22) | collective-permute-done | bytes 14368 | tf_op jit(solution)/shard_map/ppermute | solution.py:30
  54.3 0.6 %fusion.6 = bf16[4,1792]{1,0:T(4,128)(2,1)} fusion(f32[4,1792]{1,0:T(4,128)S(1)} %get-tuple-element.44, bf16[4,1792]{1,0:T(4,128)(2,1)S(1)} %collective-permute-done.22, bf16[4,1792]{1,0:T(4,128)(2,1)S(1)} %collective-permute-done.21, bf16[4,1792]{1,0:T(4,128)(2,1)S(1)} %collective-permute-done.20, f32[4,4,1792]{2,1,0:T(4,128)S(1)} %fusion.2), kind=kLoop, calls=%fused_computation.13 | loop fusion | flops 57344 | bytes 114688 | tf_op jit(solution)/shard_map/convert_element_type | solution.py:776
  (53 shorter events, 0.4 us)
Async XLA Ops:
  0.6 12.0 %copy-start = (bf16[896,14,384]{2,0,1:T(8,128)(2,1)S(1)}, bf16[896,14,384]{2,0,1:T(8,128)(2,1)}, u32[]{:S(2)}) copy-start(bf16[896,14,384]{2,0,1:T(8,128)(2,1)} %param.16) | copy-start | bytes 28901380
  3.0 1.4 %collective-permute-start = (bf16[4,4,1024]{2,1,0:T(4,128)(2,1)S(1)}, bf16[4,4,1024]{2,1,0:T(4,128)(2,1)S(1)}, u32[]{:S(2)}, u32[]{:S(2)}) collective-permute-start(bf16[4,4,1024]{2,1,0:T(4,128)(2,1)S(1)} %get-tuple-element.26), channel_id=1, source_target_pairs={{0,4},{4,0},{8,12},{12,8},{16,20},{20,16},{24,28},{28,24},{1,5},{5... | collective-permute-start | bytes 98312 | tf_op jit(solution)/shard_map/ppermute | solution.py:30
  3.5 5.5 %collective-permute-start.8 = (bf16[2,32,1792]{2,1,0:T(8,128)(2,1)S(1)}, bf16[2,32,1792]{2,1,0:T(8,128)(2,1)S(1)}, u32[]{:S(2)}, u32[]{:S(2)}) collective-permute-start(bf16[2,32,1792]{2,1,0:T(8,128)(2,1)S(1)} %get-tuple-element.34), channel_id=1, source_target_pairs={{0,4},{4,0},{8,12},{12,8},{16,20},{20,16},{24,28},{28,24},{1,5},{5... | collective-permute-start | bytes 688136 | tf_op jit(solution)/shard_map/ppermute | solution.py:30
  4.4 6.7 %collective-permute-start.1 = (bf16[2,4,1024]{2,1,0:T(4,128)(2,1)S(1)}, bf16[2,4,1024]{2,1,0:T(4,128)(2,1)S(1)}, u32[]{:S(2)}, u32[]{:S(2)}) collective-permute-start(bf16[2,4,1024]{2,1,0:T(4,128)(2,1)S(1)} %pad_maximum_fusion.1), channel_id=1, source_target_pairs={{0,24},{4,28},{8,16},{12,20},{16,8},{20,12},{24,0},{28,4},{1,25},{... | collective-permute-start | bytes 49160 | tf_op jit(solution)/shard_map/ppermute | solution.py:30
  8.3 3.9 %collective-permute-start.2 = (bf16[2,4,1024]{2,1,0:T(4,128)(2,1)S(1)}, bf16[2,4,1024]{2,1,0:T(4,128)(2,1)S(1)}, u32[]{:S(2)}, u32[]{:S(2)}) collective-permute-start(bf16[2,4,1024]{2,1,0:T(4,128)(2,1)S(1)} %pad_maximum_fusion.2), channel_id=1, source_target_pairs={{0,16},{4,20},{8,24},{12,28},{16,0},{20,4},{24,8},{28,12},{1,17},{... | collective-permute-start | bytes 49160 | tf_op jit(solution)/shard_map/ppermute | solution.py:30
  8.9 3.8 %collective-permute-start.3 = (bf16[2,4,1024]{2,1,0:T(4,128)(2,1)S(1)}, bf16[2,4,1024]{2,1,0:T(4,128)(2,1)S(1)}, u32[]{:S(2)}, u32[]{:S(2)}) collective-permute-start(bf16[2,4,1024]{2,1,0:T(4,128)(2,1)S(1)} %pad_maximum_fusion.3), channel_id=1, source_target_pairs={{0,8},{4,12},{8,0},{12,4},{16,24},{20,28},{24,16},{28,20},{1,9},{5... | collective-permute-start | bytes 49160 | tf_op jit(solution)/shard_map/ppermute | solution.py:30
  9.1 11.4 %collective-permute-start.9 = (bf16[2,2,32,1792]{3,2,1,0:T(8,128)(2,1)S(1)}, bf16[2,2,32,1792]{3,2,1,0:T(8,128)(2,1)S(1)}, u32[]{:S(2)}, u32[]{:S(2)}) collective-permute-start(bf16[2,2,32,1792]{3,2,1,0:T(8,128)(2,1)S(1)} %pad_maximum_fusion.refs_0_.refs_6_), channel_id=1, source_target_pairs={{0,8},{4,20},{8,0},{12,28},{16,24},{20,4},{24,16},{28,12},{1,9},{5... | collective-permute-start | bytes 1376264 | tf_op jit(solution)/shard_map/ppermute | solution.py:163
  12.7 10.7 %slice-start = ((s8[4587520]{0:T(1024)(128)(4,1)}), s8[4194304]{0:T(1024)(128)(4,1)S(1)}, s32[]{:S(2)}) async-start(s8[4587520]{0:T(1024)(128)(4,1)} %bitcast.64), calls=%async_computation | async-start | bytes 8388608
  12.7 10.7 %slice-start.2 = ((s8[4587520]{0:T(1024)(128)(4,1)}), s8[4194304]{0:T(1024)(128)(4,1)S(1)}, s32[]{:S(2)}) async-start(s8[4587520]{0:T(1024)(128)(4,1)} %bitcast.66), calls=%async_computation.2 | async-start | bytes 8388608
  12.7 7.7 %copy-start.6 = (f32[14,384]{1,0:T(8,128)S(1)}, f32[14,384]{1,0:T(8,128)}, u32[]{:S(2)}) copy-start(f32[14,384]{1,0:T(8,128)} %param.17) | copy-start | bytes 64516
  12.7 10.7 %slice-start.1 = ((s8[4587520]{0:T(1024)(128)(4,1)}), s8[393216]{0:T(1024)(128)(4,1)S(1)}, s32[]{:S(2)}) async-start(s8[4587520]{0:T(1024)(128)(4,1)} %bitcast.64), calls=%async_computation.1 | async-start | bytes 786432
  12.7 10.7 %slice-start.3 = ((s8[4587520]{0:T(1024)(128)(4,1)}), s8[393216]{0:T(1024)(128)(4,1)S(1)}, s32[]{:S(2)}) async-start(s8[4587520]{0:T(1024)(128)(4,1)} %bitcast.66), calls=%async_computation.3 | async-start | bytes 786432
  12.7 10.7 %copy-start.1 = (bf16[4,7168]{1,0:T(4,128)(2,1)S(1)}, bf16[4,7168]{1,0:T(4,128)(2,1)}, u32[]{:S(2)}) copy-start(bf16[4,7168]{1,0:T(4,128)(2,1)} %refs_4_.1) | copy-start | bytes 172036
  12.7 10.7 %copy-start.3 = (s32[4,16]{1,0:T(4,128)S(1)}, s32[4,16]{1,0:T(4,128)}, u32[]{:S(2)}) copy-start(s32[4,16]{1,0:T(4,128)} %table_ref.3) | copy-start | bytes 772
  12.7 10.7 %copy-start.4 = (s32[4]{0:T(128)S(1)}, s32[4]{0:T(128)}, u32[]{:S(2)}) copy-start(s32[4]{0:T(128)} %length_ref.3) | copy-start | bytes 52
  12.7 10.7 %copy-start.5 = (s32[4]{0:T(128)S(1)}, s32[4]{0:T(128)}, u32[]{:S(2)}) copy-start(s32[4]{0:T(128)} %slot_ref.3) | copy-start | bytes 52
  15.0 1.7 %collective-permute-start.4 = (f32[4,4,5376]{2,1,0:T(4,128)S(1)}, f32[4,4,5376]{2,1,0:T(4,128)S(1)}, u32[]{:S(2)}, u32[]{:S(2)}) collective-permute-start(f32[4,4,5376]{2,1,0:T(4,128)S(1)} %get-tuple-element.28), channel_id=1, source_target_pairs={{0,4},{4,0},{8,12},{12,8},{16,20},{20,16},{24,28},{28,24},{1,5},{5... | collective-permute-start | bytes 1032200 | tf_op jit(solution)/shard_map/ppermute | solution.py:30
  16.8 5.5 %collective-permute-start.5 = (bf16[4,7168]{1,0:T(4,128)(2,1)S(1)}, bf16[4,7168]{1,0:T(4,128)(2,1)S(1)}, u32[]{:S(2)}, u32[]{:S(2)}) collective-permute-start(bf16[4,7168]{1,0:T(4,128)(2,1)S(1)} %get-tuple-element.29), channel_id=1, source_target_pairs={{0,24},{4,28},{8,16},{12,20},{16,8},{20,12},{24,0},{28,4},{1,25},{... | collective-permute-start | bytes 172040 | tf_op jit(solution)/shard_map/ppermute | solution.py:30
  18.4 4.6 %collective-permute-start.6 = (bf16[4,7168]{1,0:T(4,128)(2,1)S(1)}, bf16[4,7168]{1,0:T(4,128)(2,1)S(1)}, u32[]{:S(2)}, u32[]{:S(2)}) collective-permute-start(bf16[4,7168]{1,0:T(4,128)(2,1)S(1)} %get-tuple-element.30), channel_id=1, source_target_pairs={{0,16},{4,20},{8,24},{12,28},{16,0},{20,4},{24,8},{28,12},{1,17},{... | collective-permute-start | bytes 172040 | tf_op jit(solution)/shard_map/ppermute | solution.py:30
  18.5 4.9 %collective-permute-start.7 = (bf16[4,7168]{1,0:T(4,128)(2,1)S(1)}, bf16[4,7168]{1,0:T(4,128)(2,1)S(1)}, u32[]{:S(2)}, u32[]{:S(2)}) collective-permute-start(bf16[4,7168]{1,0:T(4,128)(2,1)S(1)} %get-tuple-element.31), channel_id=1, source_target_pairs={{0,8},{4,12},{8,0},{12,4},{16,24},{20,28},{24,16},{28,20},{1,9},{5... | collective-permute-start | bytes 172040 | tf_op jit(solution)/shard_map/ppermute | solution.py:30
  20.7 14.6 %collective-permute-start.14 = (bf16[2,2,32,1792]{3,2,1,0:T(8,128)(2,1)S(1)}, bf16[2,2,32,1792]{3,2,1,0:T(8,128)(2,1)S(1)}, u32[]{:S(2)}, u32[]{:S(2)}) collective-permute-start(bf16[2,2,32,1792]{3,2,1,0:T(8,128)(2,1)S(1)} %turn_pages.1.refs_11_), channel_id=1, source_target_pairs={{0,16},{4,12},{8,24},{12,4},{16,0},{20,28},{24,8},{28,20},{1,17},{... | collective-permute-start | bytes 1376264 | tf_op jit(solution)/shard_map/ppermute | solution.py:163
  26.3 1.4 %collective-permute-start.10 = (bf16[4,32,256]{2,1,0:T(8,128)(2,1)S(1)}, bf16[4,32,256]{2,1,0:T(8,128)(2,1)S(1)}, u32[]{:S(2)}, u32[]{:S(2)}) collective-permute-start(bf16[4,32,256]{2,1,0:T(8,128)(2,1)S(1)} %get-tuple-element.36), channel_id=1, source_target_pairs={{0,4},{4,0},{8,12},{12,8},{16,20},{20,16},{24,28},{28,24},{1,5},{5... | collective-permute-start | bytes 196616 | tf_op jit(solution)/shard_map/ppermute | solution.py:30
  27.7 5.4 %collective-permute-start.11 = (bf16[32,256]{1,0:T(8,128)(2,1)S(1)}, bf16[32,256]{1,0:T(8,128)(2,1)S(1)}, u32[]{:S(2)}, u32[]{:S(2)}) collective-permute-start(bf16[32,256]{1,0:T(8,128)(2,1)S(1)} %pad_maximum_fusion.5), channel_id=1, source_target_pairs={{0,24},{4,28},{8,16},{12,20},{16,8},{20,12},{24,0},{28,4},{1,25},{... | collective-permute-start | bytes 49160 | tf_op jit(solution)/shard_map/ppermute | solution.py:30
  31.5 3.8 %collective-permute-start.12 = (bf16[32,256]{1,0:T(8,128)(2,1)S(1)}, bf16[32,256]{1,0:T(8,128)(2,1)S(1)}, u32[]{:S(2)}, u32[]{:S(2)}) collective-permute-start(bf16[32,256]{1,0:T(8,128)(2,1)S(1)} %pad_maximum_fusion.6), channel_id=1, source_target_pairs={{0,16},{4,20},{8,24},{12,28},{16,0},{20,4},{24,8},{28,12},{1,17},{... | collective-permute-start | bytes 49160 | tf_op jit(solution)/shard_map/ppermute | solution.py:30
  31.5 3.8 %collective-permute-start.13 = (bf16[32,256]{1,0:T(8,128)(2,1)S(1)}, bf16[32,256]{1,0:T(8,128)(2,1)S(1)}, u32[]{:S(2)}, u32[]{:S(2)}) collective-permute-start(bf16[32,256]{1,0:T(8,128)(2,1)S(1)} %pad_maximum_fusion.7), channel_id=1, source_target_pairs={{0,8},{4,12},{8,0},{12,4},{16,24},{20,28},{24,16},{28,20},{1,9},{5... | collective-permute-start | bytes 49160 | tf_op jit(solution)/shard_map/ppermute | solution.py:30
  36.4 1.6 %collective-permute-start.15 = (bf16[4,4,4,1792]{3,2,1,0:T(4,128)(2,1)S(1)}, bf16[4,4,4,1792]{3,2,1,0:T(4,128)(2,1)S(1)}, u32[]{:S(2)}, u32[]{:S(2)}) collective-permute-start(bf16[4,4,4,1792]{3,2,1,0:T(4,128)(2,1)S(1)} %get-tuple-element.39), channel_id=1, source_target_pairs={{0,4},{4,0},{8,12},{12,8},{16,20},{20,16},{24,28},{28,24},{1,5},{5... | collective-permute-start | bytes 688136 | tf_op jit(solution)/shard_map/ppermute | solution.py:30
  36.6 5.1 %collective-permute-start.19 = (bf16[2,32,1792]{2,1,0:T(8,128)(2,1)S(1)}, bf16[2,32,1792]{2,1,0:T(8,128)(2,1)S(1)}, u32[]{:S(2)}, u32[]{:S(2)}) collective-permute-start(bf16[2,32,1792]{2,1,0:T(8,128)(2,1)S(1)} %choose_half.1), channel_id=1, source_target_pairs={{0,4},{4,0},{8,12},{12,8},{16,20},{20,16},{24,28},{28,24},{1,5},{5... | collective-permute-start | bytes 688136 | tf_op jit(solution)/shard_map/ppermute | solution.py:30
  38.2 5.7 %collective-permute-start.16 = (bf16[4,4,1792]{2,1,0:T(4,128)(2,1)S(1)}, bf16[4,4,1792]{2,1,0:T(4,128)(2,1)S(1)}, u32[]{:S(2)}, u32[]{:S(2)}) collective-permute-start(bf16[4,4,1792]{2,1,0:T(4,128)(2,1)S(1)} %get-tuple-element.49), channel_id=1, source_target_pairs={{0,24},{4,28},{8,16},{12,20},{16,8},{20,12},{24,0},{28,4},{1,25},{... | collective-permute-start | bytes 172040 | tf_op jit(solution)/shard_map/ppermute | solution.py:30
  39.7 5.2 %collective-permute-start.18 = (bf16[4,4,1792]{2,1,0:T(4,128)(2,1)S(1)}, bf16[4,4,1792]{2,1,0:T(4,128)(2,1)S(1)}, u32[]{:S(2)}, u32[]{:S(2)}) collective-permute-start(bf16[4,4,1792]{2,1,0:T(4,128)(2,1)S(1)} %get-tuple-element.50), channel_id=1, source_target_pairs={{0,8},{4,12},{8,0},{12,4},{16,24},{20,28},{24,16},{28,20},{1,9},{5... | collective-permute-start | bytes 172040 | tf_op jit(solution)/shard_map/ppermute | solution.py:30
  41.7 8.8 %copy-start.2 = (f32[7168]{0:T(1024)S(1)}, f32[7168]{0:T(1024)}, u32[]{:S(2)}) copy-start(f32[7168]{0:T(1024)} %param.19) | copy-start | bytes 86020
  41.7 4.2 %collective-permute-start.17 = (bf16[4,4,1792]{2,1,0:T(4,128)(2,1)S(1)}, bf16[4,4,1792]{2,1,0:T(4,128)(2,1)S(1)}, u32[]{:S(2)}, u32[]{:S(2)}) collective-permute-start(bf16[4,4,1792]{2,1,0:T(4,128)(2,1)S(1)} %get-tuple-element.51), channel_id=1, source_target_pairs={{0,16},{4,20},{8,24},{12,28},{16,0},{20,4},{24,8},{28,12},{1,17},{... | collective-permute-start | bytes 172040 | tf_op jit(solution)/shard_map/ppermute | solution.py:30
  46.0 6.2 %collective-permute-start.20 = (bf16[4,1792]{1,0:T(4,128)(2,1)S(1)}, bf16[4,1792]{1,0:T(4,128)(2,1)S(1)}, u32[]{:S(2)}, u32[]{:S(2)}) collective-permute-start(bf16[4,1792]{1,0:T(4,128)(2,1)S(1)} %get-tuple-element.64), channel_id=1, source_target_pairs={{0,3},{1,2},{2,1},{3,0},{4,7},{5,6},{6,5},{7,4},{8,11},{9,10},{10,... | collective-permute-start | bytes 43016 | tf_op jit(solution)/shard_map/ppermute | solution.py:30
  49.6 4.6 %collective-permute-start.22 = (bf16[4,1792]{1,0:T(4,128)(2,1)S(1)}, bf16[4,1792]{1,0:T(4,128)(2,1)S(1)}, u32[]{:S(2)}, u32[]{:S(2)}) collective-permute-start(bf16[4,1792]{1,0:T(4,128)(2,1)S(1)} %get-tuple-element.65), channel_id=1, source_target_pairs={{0,2},{1,3},{2,0},{3,1},{4,6},{5,7},{6,4},{7,5},{8,10},{9,11},{10,... | collective-permute-start | bytes 43016 | tf_op jit(solution)/shard_map/ppermute | solution.py:30
  49.6 4.6 %collective-permute-start.21 = (bf16[4,1792]{1,0:T(4,128)(2,1)S(1)}, bf16[4,1792]{1,0:T(4,128)(2,1)S(1)}, u32[]{:S(2)}, u32[]{:S(2)}) collective-permute-start(bf16[4,1792]{1,0:T(4,128)(2,1)S(1)} %get-tuple-element.66), channel_id=1, source_target_pairs={{0,1},{1,0},{2,3},{3,2},{4,5},{5,4},{6,7},{7,6},{8,9},{9,8},{10,11... | collective-permute-start | bytes 43016 | tf_op jit(solution)/shard_map/ppermute | solution.py:30

commit v12 on v11

--- a/solution.py
+++ b/solution.py
@@ -30,13 +30,6 @@
     return lax.ppermute(value, axis, [(i, i ^ step) for i in range(size)])
 
 
-def spread_pairs(keep, got):
-    chips = keep.shape[0]
-    return [jnp.stack([keep[0], got[0]])] + [
-        swap(jnp.stack([keep[d], got[d]]), "req", 2 * d) for d in range(1, chips)
-    ]
-
-
 def in_hbm(*arrays):
     return [pltpu.with_memory_space_constraint(array, pltpu.HBM) for array in arrays]
 
@@ -74,17 +67,14 @@
     return leaving
 
 
-def prepare(tokens, gain, shift, lengths, page_table, new_slot, new_page, key_pool, value_pool):
-    groups = lax.axis_size("req")
-    chips = groups // 2
-    slots, model = tokens.shape
-    depth = model // groups
+def pick_halves(lengths, page_table, new_slot, new_page, tokens, key_pool, value_pool):
+    slots = new_slot.shape[0]
     page, width = key_pool.shape[1:]
     half = page // 2
 
     def kernel(
-        token_ref, gain_ref, shift_ref, length_ref, table_ref, slot_ref, page_ref, key_ref, value_ref,
-        keep_ref, send_ref, keep_half, send_half, normed, sems,
+        length_ref, table_ref, slot_ref, page_ref, token_ref, key_ref, value_ref,
+        keep_half, send_half, told_ref, token_out, sems,
     ):
         here = lax.axis_index("req")
         leaving = leaving_slot(slot_ref, slots, here)
@@ -97,12 +87,6 @@
                 )
         for copy in copies:
             copy.start()
-        values = token_ref[...].astype(F32)
-        average = jnp.mean(values, axis=1, keepdims=True)
-        centered = values - average
-        variance = jnp.mean(centered * centered, axis=1, keepdims=True)
-        rows = centered * lax.rsqrt(variance + EPSILON) * gain_ref[...] + shift_ref[...]
-        normed[...] = rows.astype(BF16).astype(F32)
         row = lax.broadcasted_iota(jnp.int32, (slots, META), 0)
         lane = lax.broadcasted_iota(jnp.int32, (slots, META), 1)
         told = jnp.zeros((slots, META), F32)
@@ -111,44 +95,75 @@
             numbers = (slot // slots, slot % slots, page_ref[s], length_ref[s] % page)
             for j, number in enumerate(numbers):
                 told = jnp.where((row == s) & (lane == j), number.astype(F32), told)
-        told = told.astype(BF16)
-        for k in range(groups):
-            first = (here ^ k) * depth
+        told_ref[...] = told
+        token_out[...] = token_ref[...]
+        for copy in copies:
+            copy.wait()
+
+    halves = jax.ShapeDtypeStruct((2, half, width), key_pool.dtype)
+    return pl.pallas_call(
+        kernel,
+        out_shape=(
+            halves,
+            halves,
+            jax.ShapeDtypeStruct((slots, META), F32),
+            jax.ShapeDtypeStruct(tokens.shape, tokens.dtype),
+        ),
+        in_specs=[SMEM] * 4 + [VMEM] + [HBM] * 2,
+        out_specs=(VMEM,) * 4,
+        scratch_shapes=[pltpu.SemaphoreType.DMA((2, 2))],
+        compiler_params=pltpu.CompilerParams(vmem_limit_bytes=2 * MIB),
+        cost_estimate=cost(0, 8 * page * width),
+        name="pick_halves",
+    )(*in_hbm(lengths, page_table, new_slot, new_page, tokens, key_pool, value_pool))
+
+
+def prepare(tokens, other_tokens, gain, shift, told):
+    groups = lax.axis_size("req")
+    chips = groups // 2
+    slots, model = tokens.shape
+    depth = model // groups
+
+    def kernel(token_ref, other_ref, gain_ref, shift_ref, told_ref, *refs):
+        out_refs, normed = refs[:chips], refs[chips]
+        here = lax.axis_index("req")
+        values = jnp.concatenate([token_ref[...].astype(F32), other_ref[...].astype(F32)], axis=0)
+        average = jnp.mean(values, axis=1, keepdims=True)
+        centered = values - average
+        variance = jnp.mean(centered * centered, axis=1, keepdims=True)
+        rows = centered * lax.rsqrt(variance + EPSILON) * gain_ref[...] + shift_ref[...]
+        normed[...] = rows.astype(BF16).astype(F32)
+        for d in range(chips):
+            first = (here ^ 2 * d) * depth
             if depth % LANES == 0:
                 block = normed[:, pl.ds(pl.multiple_of(first, LANES), depth)]
             else:
                 block = pltpu.roll(normed[...], lax.rem(model - first, model), 1)[:, :depth]
-            target = (keep_ref, send_ref)[k % 2]
-            target[k // 2, :, :META] = told
-            target[k // 2, :, META:] = block.astype(BF16)
-        for copy in copies:
-            copy.wait()
-
-    blocks = jax.ShapeDtypeStruct((chips, slots, META + depth), BF16)
-    halves = jax.ShapeDtypeStruct((2, half, width), key_pool.dtype)
-    return pl.pallas_call(
-        kernel,
-        out_shape=(blocks, blocks, halves, halves),
-        in_specs=[VMEM] * 3 + [SMEM] * 4 + [HBM] * 2,
-        out_specs=(VMEM,) * 4,
-        scratch_shapes=[pltpu.VMEM((slots, model), F32), pltpu.SemaphoreType.DMA((2, 2))],
+            for e in range(2):
+                out_refs[d][e, :, META:] = block[e * slots : (e + 1) * slots].astype(BF16)
+            out_refs[d][0, :, :META] = told_ref[...].astype(BF16)
+            out_refs[d][1, :, :META] = jnp.zeros((slots, META), BF16)
+
+    return pl.pallas_call(
+        kernel,
+        out_shape=(jax.ShapeDtypeStruct((2, slots, META + depth), BF16),) * chips,
+        in_specs=[VMEM] * 5,
+        out_specs=(VMEM,) * chips,
+        scratch_shapes=[pltpu.VMEM((2 * slots, model), F32)],
         compiler_params=pltpu.CompilerParams(vmem_limit_bytes=4 * MIB),
-        cost_estimate=cost(0, 8 * page * width),
+        cost_estimate=cost(0, 0),
         name="prepare",
-    )(*in_hbm(tokens, gain, shift, lengths, page_table, new_slot, new_page, key_pool, value_pool))
-
-
-def arrivals(block_refs, here, wanted):
-    slots = block_refs[0].shape[1]
+    )(tokens, other_tokens, gain, shift, told)
+
+
+def arrivals(tables, here, wanted):
+    slots = tables[0].shape[0]
     lane = lax.broadcasted_iota(jnp.int32, (slots, META), 1)
     found = jnp.zeros((slots, META), F32)
     goal = here ^ wanted
-    for d, ref in enumerate(block_refs):
-        for e in range(2):
-            k = 2 * d + e
-            told = ref[e, :, :META].astype(F32)
-            numbered = jnp.where(lane == 4, float(k), told)
-            found = jnp.where(told[:, :1] == jnp.where(wanted == k, -1, goal).astype(F32), numbered, found)
+    for k, told in enumerate(tables):
+        numbered = jnp.where(lane == 4, float(k), told)
+        found = jnp.where(told[:, :1] == jnp.where(wanted == k, -1, goal).astype(F32), numbered, found)
     return lambda j: jnp.sum(jnp.where(lane == j, found, 0.0)).astype(jnp.int32)
 
 
@@ -163,21 +178,24 @@
     return lax.ppermute(value, "req", [(i, i ^ steps[i]) for i in range(2 * chips)])
 
 
-def find_sources(spread, after):
+def find_sources(spread, got):
     chips = len(spread)
     across = row_length(chips)
     down = chips // across
 
     def kernel(*refs):
-        block_refs, out_ref = refs[:chips][::-1], refs[-1]
+        block_refs, got_ref, out_ref = refs[:chips][::-1], refs[-2], refs[-1]
         here = lax.axis_index("req")
+        tables = []
+        for d in range(chips):
+            tables += [block_refs[d][0, :, :META].astype(F32), got_ref[d, :, got_ref.shape[2] - META :]]
         lane = lax.broadcasted_iota(jnp.int32, (8, LANES), 1)
         found = jnp.zeros((8, LANES), F32)
         put = lambda j, number: jnp.where(lane == j, number.astype(F32), found)
         turned = (here % 2 == 1) & (across == down)
         for row in range(down):
             for j in range(2):
-                pick = arrivals(block_refs, here, jnp.where(turned, 2 * row, 2 * across * row) + j)
+                pick = arrivals(tables, here, jnp.where(turned, 2 * row, 2 * across * row) + j)
                 source = pick(4)
                 chip = source // 2
                 chip = jnp.where(turned, chip % across * across + chip // across, chip)
@@ -190,12 +208,12 @@
     return pl.pallas_call(
         kernel,
         out_shape=jax.ShapeDtypeStruct((8, LANES), F32),
-        in_specs=[VMEM] * chips + [ANY],
+        in_specs=[VMEM] * (chips + 1),
         out_specs=VMEM,
-        compiler_params=pltpu.CompilerParams(vmem_limit_bytes=2 * MIB),
+        compiler_params=pltpu.CompilerParams(vmem_limit_bytes=4 * MIB),
         cost_estimate=cost(0, 0),
         name="find_sources",
-    )(*spread[::-1], after)
+    )(*spread[::-1], got)
 
 
 def number_at(source_ref, j):
@@ -301,12 +319,15 @@
                 keep_ref[d, :, columns] = total[row : row + slots]
                 send_ref[d, :, columns] = total[row + slots : row + 2 * slots]
 
+        for d in range(chips):
+            send_ref[d, :, heads * width :] = block_refs[d][0, :, :META].astype(F32)
         copy.wait()
 
     shape = jax.ShapeDtypeStruct((chips, slots, heads * width), F32)
-    return pl.pallas_call(
-        kernel,
-        out_shape=(shape, shape, jax.ShapeDtypeStruct(later.shape, later.dtype)),
+    wider = jax.ShapeDtypeStruct((chips, slots, heads * width + META), F32)
+    return pl.pallas_call(
+        kernel,
+        out_shape=(shape, wider, jax.ShapeDtypeStruct(later.shape, later.dtype)),
         in_specs=[VMEM] * (chips + 1) + [HBM],
         out_specs=(VMEM, VMEM, VMEM),
         scratch_shapes=[pltpu.VMEM((rows, depth), F32), pltpu.SemaphoreType.DMA],
@@ -316,12 +337,12 @@
     )(*blocks[::-1], weight, *in_hbm(later))
 
 
-def combine(keep, got, after):
+def combine(keep, got):
     chips, slots, width = keep.shape
     heads = width // (3 * LANES)
 
-    def kernel(keep_ref, got_ref, _, own_ref, *message_refs):
-        own_ref[...] = keep_ref[0] + got_ref[0]
+    def kernel(keep_ref, got_ref, own_ref, *message_refs):
+        own_ref[...] = keep_ref[0] + got_ref[0, :, :width]
         for d in range(1, chips):
             for h in range(heads):
                 total = keep_ref[d, :, 3 * h * LANES : 3 * (h + 1) * LANES] + got_ref[d, :, 3 * h * LANES : 3 * (h + 1) * LANES]
@@ -337,15 +358,15 @@
     return pl.pallas_call(
         kernel,
         out_shape=(jax.ShapeDtypeStruct((slots, width), F32),) + (message,) * (chips - 1),
-        in_specs=[VMEM, VMEM, ANY],
+        in_specs=[VMEM, VMEM],
         out_specs=(VMEM,) * chips,
         compiler_params=pltpu.CompilerParams(vmem_limit_bytes=8 * MIB),
         cost_estimate=cost(0, 8 * keep.size),
         name="combine",
-    )(keep, got, after)
-
-
-def attend(lengths, new_slot, page_table, sums, bias, tokens, key_pool, value_pool, after):
+    )(keep, got)
+
+
+def attend(lengths, new_slot, page_table, sums, bias, tokens, key_pool, value_pool, written, after):
     parts = len(sums)
     slots = sums[0].shape[0]
     pages, page, width = key_pool.shape
@@ -363,17 +384,7 @@
     def kernel(*refs):
         length_ref, slot_ref, table_ref = refs[:3]
         sum_refs = refs[3 : 3 + parts][::-1]
-        (bias_ref, token_ref, key_ref, value_ref, _, pack_keep, pack_send, patch_ref, value_out) = refs[
-            3 + parts : 12 + parts
-        ]
-        attended_ref, out_sems = refs[12 + parts :]
-        step = pages // 4
-        writes = [
-            pltpu.make_async_copy(value_ref.at[pl.ds(i * step, step)], value_out.at[pl.ds(i * step, step)], out_sems.at[i])
-            for i in range(4)
-        ]
-        for write in writes:
-            write.start()
+        (bias_ref, token_ref, key_ref, value_ref, _, _, pack_keep, pack_send, patch_ref, attended_ref) = refs[3 + parts :]
         here = lax.axis_index("req")
         column_block = lax.axis_index("head")
         leaving = leaving_slot(slot_ref, slots, here)
@@ -517,24 +528,17 @@
                 new = jnp.broadcast_to(new_rows[n][s : s + 1], (tall, width))
                 patch_ref[n, s] = jnp.where(at == offset - first, new, old).astype(BF16)
 
-        for write in writes:
-            write.wait()
-
     packed = jax.ShapeDtypeStruct((parts, pack_rows(slots, strips), PACK), BF16)
-    pool = jax.ShapeDtypeStruct(key_pool.shape, key_pool.dtype)
-    return pl.pallas_call(
-        kernel,
-        out_shape=(packed, packed, jax.ShapeDtypeStruct((2, slots, tall, width), BF16), pool),
-        in_specs=[SMEM] * 3 + [VMEM] * (parts + 4) + [ANY],
-        out_specs=(VMEM, VMEM, VMEM, HBM),
-        scratch_shapes=[
-            pltpu.VMEM((-(-slots // 8) * 8, width), F32),
-            pltpu.SemaphoreType.DMA((4,)),
-        ],
+    return pl.pallas_call(
+        kernel,
+        out_shape=(packed, packed, jax.ShapeDtypeStruct((2, slots, tall, width), BF16)),
+        in_specs=[SMEM] * 3 + [VMEM] * (parts + 4) + [HBM, ANY],
+        out_specs=(VMEM, VMEM, VMEM),
+        scratch_shapes=[pltpu.VMEM((-(-slots // 8) * 8, width), F32)],
         compiler_params=pltpu.CompilerParams(vmem_limit_bytes=18 * MIB),
         cost_estimate=cost(0, 0),
         name="attend",
-    )(lengths, new_slot, page_table, *sums[::-1], bias, tokens, key_pool, value_pool, after)
+    )(lengths, new_slot, page_table, *sums[::-1], bias, tokens, key_pool, value_pool, *in_hbm(written), after)
 
 
 def pack_rows(slots, strips):
@@ -709,32 +713,38 @@
     slots = tokens.shape[0]
     chips = groups // 2
 
-    keep, send, keep_half, send_half = prepare(
-        tokens, norm_gain[None], norm_shift[None], lengths, page_table, new_slot, new_page, key_pool, value_pool
+    other_tokens = swap(tokens, "req", 1)
+    keep_half, send_half, told, own_tokens = pick_halves(
+        lengths, page_table, new_slot, new_page, tokens, key_pool, value_pool
     )
-    got = swap(send, "req", 1)
-    spread = spread_pairs(keep, got)
+    blocks = prepare(own_tokens, other_tokens, norm_gain[None], norm_shift[None], told)
+    send_half, *blocks = lax.optimization_barrier((send_half, *blocks))
     across = row_length(chips)
+    spread = [blocks[0]] + [swap(blocks[d], "req", 2 * d) for d in range(1, chips)]
     halves = [jnp.stack([keep_half, swap(send_half, "req", 1)])]
+    halves[0], *spread = lax.optimization_barrier((halves[0], *spread[::-1]))
+    spread = spread[::-1]
     halves += [swap_pages(halves[0], chips, True, d) for d in range(1, across)]
     flat = out_weight.reshape(-1, out_weight.shape[2])
     keep, send, staged = project(spread, jnp.transpose(qkv_weight, (1, 0, 2)), flat)
     got = swap(send, "req", 1)
-    sources = find_sources(spread, keep)
-    own, *messages = combine(keep, got, sources)
+    own, *messages = combine(keep, got)
+    sources = find_sources(spread, got)
+    value_out = write_pool(value_pool, own)
     turning = turn_pages(sources, halves, chips)
     turned = [swap_pages(one, chips, False, row + 1) for row, one in enumerate(turning)]
     sums = [own] + [swap(messages[d - 1], "req", 2 * d) for d in range(1, chips)]
 
-    pack_keep, pack_send, patches, value_out = attend(
+    pack_keep, pack_send, patches = attend(
         lengths,
         new_slot,
         page_table,
         sums,
         qkv_bias.reshape(1, -1),
-        tokens,
+        own_tokens,
         key_pool,
         value_pool,
+        value_out,
         turning[0],
     )
     packs_got = swap(pack_send, "req", 1)
@@ -762,7 +772,7 @@
         sources,
         patches,
         packs,
-        tokens,
+        own_tokens,
         out_bias[None],
         halves,
         turned,

time: 55 us -> 55.8 us (1.015)
  Pallas kernels: 13.2 us -> 15.3 us
  starting transfers between devices: 25.9 us -> 23.8 us
  waiting for transfers between devices: 13.6 us -> 14.5 us
    pallas_call x1 -> x2, Pallas kernels: 2.17 us -> 4.54 us  [write_pool(): pl.pallas_call(kernel, out_shape=jax.ShapeDtypeStruct(pool.shape, pool.dt...]
    ppermute x2, starting transfers between devices: 3.62 us -> 2.05 us  [swap_pages(): lax.ppermute(value, 'req', [(i, i ^ steps[i]) for i in range(2 * chips)])]
    ppermute x21, waiting for transfers between devices: 13.6 us -> 14.5 us  [swap(): return lax.ppermute(value, axis, [(i, i ^ step) for i in range(size)])]
    pallas_call x1, Pallas kernels: 2.84 us -> 2.05 us  [attend(): pl.pallas_call(kernel, out_shape=(packed, packed, jax.ShapeDtypeStruct((2...]
    ppermute x21, starting transfers between devices: 22.3 us -> 21.7 us  [swap(): return lax.ppermute(value, axis, [(i, i ^ step) for i in range(size)])]
    pallas_call x2 -> x3, Pallas kernels: 4.61 us -> 5.16 us  [the longest x1 2.53 us: pick_halves(): pl.pallas_call(kernel, out_shape=(halves, halves, jax.ShapeDtypeStruct((s...]
  transfers between devices with their start and end apart: 23 -> 23, of which waited for: 14 -> 12; matrix products, arithmetic and copies ran while one was open for 1% -> 1% of each run, Pallas kernels for 18% -> 25%
where the time goes in v12:
time: 55.8 us
  starting transfers between devices  23.8 us (43%)
  Pallas kernels  15.3 us (27%)
  waiting for transfers between devices  14.5 us (26%)
  between operations  1.04 us (2%)
  other arithmetic  0.96 us (2%)
    ppermute x21, starting transfers between devices, swap(): return lax.ppermute(value, axis, [(i, i ^ step) for i in range(size)])  21.7 us
    ppermute x21, waiting for transfers between devices, swap(): return lax.ppermute(value, axis, [(i, i ^ step) for i in range(size)])  14.5 us
    pallas_call x2, Pallas kernels, write_pool(): pl.pallas_call(kernel, out_shape=jax.ShapeDtypeStruct(pool.shape, pool.dt...  4.54 us
    pallas_call x1, Pallas kernels, pick_halves(): pl.pallas_call(kernel, out_shape=(halves, halves, jax.ShapeDtypeStruct((s...  2.53 us
    pallas_call x1, Pallas kernels, project(): pl.pallas_call(kernel, out_shape=(shape, wider, jax.ShapeDtypeStruct(late...  2.27 us
    pallas_call x1, Pallas kernels, attend(): pl.pallas_call(kernel, out_shape=(packed, packed, jax.ShapeDtypeStruct((2...  2.05 us
    ppermute x2, starting transfers between devices, swap_pages(): lax.ppermute(value, 'req', [(i, i ^ steps[i]) for i in range(2 * chips)])  2.05 us
    pallas_call x1, Pallas kernels, place_page(): pl.pallas_call(kernel, out_shape=(jax.ShapeDtypeStruct((slots, width), F3...  1.7 us
  transfers between devices with their start and end apart: 23, of which 12 were waited for; matrix products, arithmetic and copies ran while one was open for 1% of the time, Pallas kernels for 25%

profile of v12, /device:TPU:0, one launch (start us, length us, event | category | flops | bytes accessed | tf_op | source)
XLA Modules:
  0.0 55.8 jit_solution(14933008924967695904)
XLA Ops:
  0.7 0.5 collective-permute-start
  1.2 2.5 %pick_halves.1 = (bf16[2,32,1792]{2,1,0:T(8,128)(2,1)S(1)}, bf16[2,32,1792]{2,1,0:T(8,128)(2,1)S(1)}, f32[4,128]{1,0:T(4,128)S(1)}, bf16[4,7168]{1,0:T(4,128)(2,1)S(1)}) custom-call(s32[4]{0:T(128)} %length_ref.3, s32[4,16]{1,0:T(4,128)} %table_ref.3, s32[4]{0:T(128)} %slot_ref.3, s32[4]{0:T(128)} %page_ref.1, bf16[4,7168]{1,0:T(4,128)(2,1)} %token_ref.1, ...), custom_call_target="tpu_custom_call" | custom-call | tf_op jit(solution)/shard_map/pick_halves/pallas_call | solution.py:104
  3.8 0.4 prepare.1
  4.1 0.1 collective-permute-start.1
  4.2 4.0 %collective-permute-start.2 = (bf16[2,4,1024]{2,1,0:T(4,128)(2,1)S(1)}, bf16[2,4,1024]{2,1,0:T(4,128)(2,1)S(1)}, u32[]{:S(2)}, u32[]{:S(2)}) collective-permute-start(bf16[2,4,1024]{2,1,0:T(4,128)(2,1)S(1)} %get-tuple-element.47), channel_id=1, source_target_pairs={{0,24},{4,28},{8,16},{12,20},{16,8},{20,12},{24,0},{28,4},{1,25},{... | collective-permute-start | bytes 49160 | tf_op jit(solution)/shard_map/ppermute | solution.py:30
  8.2 0.5 collective-permute-start.3
  8.7 0.1 collective-permute-start.4
  8.8 1.1 %collective-permute-done.2.refs_0_ = bf16[2,4,1024]{2,1,0:T(4,128)(2,1)S(1)} collective-permute-done((bf16[2,4,1024]{2,1,0:T(4,128)(2,1)S(1)}, bf16[2,4,1024]{2,1,0:T(4,128)(2,1)S(1)}, u32[]{:S(2)}, u32[]{:S(2)}) %collective-permute-start.2) | collective-permute-done | bytes 16416 | tf_op jit(solution)/shard_map/ppermute | solution.py:30
  9.9 2.0 %collective-permute-done.3.refs_1_ = bf16[2,4,1024]{2,1,0:T(4,128)(2,1)S(1)} collective-permute-done((bf16[2,4,1024]{2,1,0:T(4,128)(2,1)S(1)}, bf16[2,4,1024]{2,1,0:T(4,128)(2,1)S(1)}, u32[]{:S(2)}, u32[]{:S(2)}) %collective-permute-start.3) | collective-permute-done | bytes 16416 | tf_op jit(solution)/shard_map/ppermute | solution.py:30
  12.0 0.5 collective-permute-done.4.refs_2_
  12.5 0.1 collective-permute-start.9
  12.5 2.3 %project.1 = (f32[4,4,5376]{2,1,0:T(4,128)S(1)}, f32[4,4,5504]{2,1,0:T(4,128)S(1)}, bf16[224,7168]{1,0:T(8,128)(2,1)S(1)}) custom-call(bf16[2,4,1024]{2,1,0:T(4,128)(2,1)S(1)} %collective-permute-done.2.refs_0_, bf16[2,4,1024]{2,1,0:T(4,128)(2,1)S(1)} %collective-permute-done.3.refs_1_, bf16[2,4,1024]{2,1,0:T(4,128)(2,1)S(1)} %collective-permute-done.4.refs_2_, ...), custom_call_target="tpu_custom_call" | custom-call | tf_op jit(solution)/shard_map/project/pallas_call | solution.py:328
  14.8 0.1 collective-permute-start.5
  14.9 1.7 %collective-permute-done.5.got_ref.refs_4_ = f32[4,4,5504]{2,1,0:T(4,128)S(1)} collective-permute-done((f32[4,4,5504]{2,1,0:T(4,128)S(1)}, f32[4,4,5504]{2,1,0:T(4,128)S(1)}, u32[]{:S(2)}, u32[]{:S(2)}) %collective-permute-start.5) | collective-permute-done | bytes 352288 | tf_op jit(solution)/shard_map/ppermute | solution.py:30
  16.6 0.1 combine.1
  16.6 3.0 %collective-permute-start.6 = (bf16[4,7168]{1,0:T(4,128)(2,1)S(1)}, bf16[4,7168]{1,0:T(4,128)(2,1)S(1)}, u32[]{:S(2)}, u32[]{:S(2)}) collective-permute-start(bf16[4,7168]{1,0:T(4,128)(2,1)S(1)} %get-tuple-element.57), channel_id=1, source_target_pairs={{0,24},{4,28},{8,16},{12,20},{16,8},{20,12},{24,0},{28,4},{1,25},{... | collective-permute-start | bytes 172040 | tf_op jit(solution)/shard_map/ppermute | solution.py:30
  19.6 0.5 collective-permute-start.7
  20.1 0.1 collective-permute-start.8
  20.4 2.4 %write_pool.2.refs_11_ = bf16[20,64,1792]{2,1,0:T(8,128)(2,1)} custom-call(bf16[20,64,1792]{2,1,0:T(8,128)(2,1)S(1)} %bitcast.65, f32[4,5376]{1,0:T(4,128)S(1)} %get-tuple-element.60._.refs_6_), custom_call_target="tpu_custom_call" | custom-call | tf_op jit(solution)/shard_map/write_pool/pallas_call | solution.py:51
  22.8 0.3 find_sources.1.source_ref
  23.0 0.3 turn_pages.1.refs_12_
  23.4 2.0 %collective-permute-start.14 = (bf16[2,2,32,1792]{3,2,1,0:T(8,128)(2,1)S(1)}, bf16[2,2,32,1792]{3,2,1,0:T(8,128)(2,1)S(1)}, u32[]{:S(2)}, u32[]{:S(2)}) collective-permute-start(bf16[2,2,32,1792]{3,2,1,0:T(8,128)(2,1)S(1)} %turn_pages.1.refs_12_), channel_id=1, source_target_pairs={{0,16},{4,12},{8,24},{12,4},{16,0},{20,28},{24,8},{28,20},{1,17},{... | collective-permute-start | bytes 1376264 | tf_op jit(solution)/shard_map/ppermute | solution.py:178
  25.4 2.1 %attend.1 = (bf16[4,32,256]{2,1,0:T(8,128)(2,1)S(1)}, bf16[4,32,256]{2,1,0:T(8,128)(2,1)S(1)}, bf16[2,4,16,1792]{3,2,1,0:T(8,128)(2,1)S(1)}) custom-call(s32[4]{0:T(128)S(1)} %copy-done.5, s32[4]{0:T(128)S(1)} %copy-done.6, s32[4,16]{1,0:T(4,128)S(1)} %copy-done.4, bf16[4,7168]{1,0:T(4,128)(2,1)S(1)} %collective-permute-done.6.refs_3_, ...), custom_call_target="tpu_custom_call" | custom-call | tf_op jit(solution)/shard_map/attend/pallas_call | solution.py:532
  27.5 0.1 collective-permute-start.10
  27.6 1.2 %collective-permute-done.10 = bf16[4,32,256]{2,1,0:T(8,128)(2,1)S(1)} collective-permute-done((bf16[4,32,256]{2,1,0:T(8,128)(2,1)S(1)}, bf16[4,32,256]{2,1,0:T(8,128)(2,1)S(1)}, u32[]{:S(2)}, u32[]{:S(2)}) %collective-permute-start.10) | collective-permute-done | bytes 65568 | tf_op jit(solution)/shard_map/ppermute | solution.py:30
  28.8 3.5 %collective-permute-start.11 = (bf16[32,256]{1,0:T(8,128)(2,1)S(1)}, bf16[32,256]{1,0:T(8,128)(2,1)S(1)}, u32[]{:S(2)}, u32[]{:S(2)}) collective-permute-start(bf16[32,256]{1,0:T(8,128)(2,1)S(1)} %pad_maximum_fusion.1), channel_id=1, source_target_pairs={{0,24},{4,28},{8,16},{12,20},{16,8},{20,12},{24,0},{28,4},{1,25},{... | collective-permute-start | bytes 49160 | tf_op jit(solution)/shard_map/ppermute | solution.py:30
  32.3 0.1 collective-permute-start.12
  32.4 0.6 %collective-permute-start.13 = (bf16[32,256]{1,0:T(8,128)(2,1)S(1)}, bf16[32,256]{1,0:T(8,128)(2,1)S(1)}, u32[]{:S(2)}, u32[]{:S(2)}) collective-permute-start(bf16[32,256]{1,0:T(8,128)(2,1)S(1)} %pad_maximum_fusion.3), channel_id=1, source_target_pairs={{0,8},{4,12},{8,0},{12,4},{16,24},{20,28},{24,16},{28,20},{1,9},{5... | collective-permute-start | bytes 49160 | tf_op jit(solution)/shard_map/ppermute | solution.py:30
  33.0 1.0 %collective-permute-done.11.refs_0_ = bf16[32,256]{1,0:T(8,128)(2,1)S(1)} collective-permute-done((bf16[32,256]{1,0:T(8,128)(2,1)S(1)}, bf16[32,256]{1,0:T(8,128)(2,1)S(1)}, u32[]{:S(2)}, u32[]{:S(2)}) %collective-permute-start.11) | collective-permute-done | bytes 16416 | tf_op jit(solution)/shard_map/ppermute | solution.py:30
  34.0 2.1 %collective-permute-done.12.refs_1_ = bf16[32,256]{1,0:T(8,128)(2,1)S(1)} collective-permute-done((bf16[32,256]{1,0:T(8,128)(2,1)S(1)}, bf16[32,256]{1,0:T(8,128)(2,1)S(1)}, u32[]{:S(2)}, u32[]{:S(2)}) %collective-permute-start.12) | collective-permute-done | bytes 16416 | tf_op jit(solution)/shard_map/ppermute | solution.py:30
  36.1 0.1 collective-permute-done.13.refs_2_
  36.2 1.0 %out_project.1 = (f32[4,4,4,1792]{3,2,1,0:T(4,128)S(1)}, bf16[4,4,4,1792]{3,2,1,0:T(4,128)(2,1)S(1)}) custom-call(bf16[32,256]{1,0:T(8,128)(2,1)S(1)} %collective-permute-done.11.refs_0_, bf16[32,256]{1,0:T(8,128)(2,1)S(1)} %collective-permute-done.12.refs_1_, bf16[32,256]{1,0:T(8,128)(2,1)S(1)} %collective-permute-done.13.refs_2_, ...), custom_call_target="tpu_custom_call" | custom-call | tf_op jit(solution)/shard_map/out_project/pallas_call | solution.py:587
  37.2 0.1 collective-permute-start.15
  37.3 0.2 choose_half.1
  37.5 0.6 %collective-permute-start.19 = (bf16[2,32,1792]{2,1,0:T(8,128)(2,1)S(1)}, bf16[2,32,1792]{2,1,0:T(8,128)(2,1)S(1)}, u32[]{:S(2)}, u32[]{:S(2)}) collective-permute-start(bf16[2,32,1792]{2,1,0:T(8,128)(2,1)S(1)} %choose_half.1), channel_id=1, source_target_pairs={{0,4},{4,0},{8,12},{12,8},{16,20},{20,16},{24,28},{28,24},{1,5},{5... | collective-permute-start | bytes 688136 | tf_op jit(solution)/shard_map/ppermute | solution.py:30
  38.0 0.7 %collective-permute-done.15 = bf16[4,4,4,1792]{3,2,1,0:T(4,128)(2,1)S(1)} collective-permute-done((bf16[4,4,4,1792]{3,2,1,0:T(4,128)(2,1)S(1)}, bf16[4,4,4,1792]{3,2,1,0:T(4,128)(2,1)S(1)}, u32[]{:S(2)}, u32[]{:S(2)}) %collective-permute-start.15) | collective-permute-done | bytes 229408 | tf_op jit(solution)/shard_map/ppermute | solution.py:30
  38.8 0.2 fusion.11
  39.0 0.1 slice_bitcast_fusion.3
  39.0 1.5 %collective-permute-start.16 = (bf16[4,4,1792]{2,1,0:T(4,128)(2,1)S(1)}, bf16[4,4,1792]{2,1,0:T(4,128)(2,1)S(1)}, u32[]{:S(2)}, u32[]{:S(2)}) collective-permute-start(bf16[4,4,1792]{2,1,0:T(4,128)(2,1)S(1)} %get-tuple-element.75), channel_id=1, source_target_pairs={{0,24},{4,28},{8,16},{12,20},{16,8},{20,12},{24,0},{28,4},{1,25},{... | collective-permute-start | bytes 172040 | tf_op jit(solution)/shard_map/ppermute | solution.py:30
  40.5 2.0 %collective-permute-start.18 = (bf16[4,4,1792]{2,1,0:T(4,128)(2,1)S(1)}, bf16[4,4,1792]{2,1,0:T(4,128)(2,1)S(1)}, u32[]{:S(2)}, u32[]{:S(2)}) collective-permute-start(bf16[4,4,1792]{2,1,0:T(4,128)(2,1)S(1)} %get-tuple-element.76), channel_id=1, source_target_pairs={{0,8},{4,12},{8,0},{12,4},{16,24},{20,28},{24,16},{28,20},{1,9},{5... | collective-permute-start | bytes 172040 | tf_op jit(solution)/shard_map/ppermute | solution.py:30
  42.6 2.2 %write_pool.3.refs_10_ = bf16[20,64,1792]{2,1,0:T(8,128)(2,1)} custom-call(bf16[20,64,1792]{2,1,0:T(8,128)(2,1)S(1)} %bitcast.67, bf16[2,32,1792]{2,1,0:T(8,128)(2,1)S(1)} %collective-permute-done.19._.refs_9_), custom_call_target="tpu_custom_call" | custom-call | tf_op jit(solution)/shard_map/write_pool/pallas_call | solution.py:51
  44.8 0.9 %collective-permute-done.18 = bf16[4,4,1792]{2,1,0:T(4,128)(2,1)S(1)} collective-permute-done((bf16[4,4,1792]{2,1,0:T(4,128)(2,1)S(1)}, bf16[4,4,1792]{2,1,0:T(4,128)(2,1)S(1)}, u32[]{:S(2)}, u32[]{:S(2)}) %collective-permute-start.18) | collective-permute-done | bytes 57376 | tf_op jit(solution)/shard_map/ppermute | solution.py:30
  45.7 1.0 %collective-permute-done.17 = bf16[4,4,1792]{2,1,0:T(4,128)(2,1)S(1)} collective-permute-done((bf16[4,4,1792]{2,1,0:T(4,128)(2,1)S(1)}, bf16[4,4,1792]{2,1,0:T(4,128)(2,1)S(1)}, u32[]{:S(2)}, u32[]{:S(2)}) %collective-permute-start.17) | collective-permute-done | bytes 57376 | tf_op jit(solution)/shard_map/ppermute | solution.py:30
  46.9 3.7 %collective-permute-start.20 = (bf16[4,1792]{1,0:T(4,128)(2,1)S(1)}, bf16[4,1792]{1,0:T(4,128)(2,1)S(1)}, u32[]{:S(2)}, u32[]{:S(2)}) collective-permute-start(bf16[4,1792]{1,0:T(4,128)(2,1)S(1)} %get-tuple-element.90), channel_id=1, source_target_pairs={{0,3},{1,2},{2,1},{3,0},{4,7},{5,6},{6,5},{7,4},{8,11},{9,10},{10,... | collective-permute-start | bytes 43016 | tf_op jit(solution)/shard_map/ppermute | solution.py:30
  50.5 0.8 %collective-permute-start.21 = (bf16[4,1792]{1,0:T(4,128)(2,1)S(1)}, bf16[4,1792]{1,0:T(4,128)(2,1)S(1)}, u32[]{:S(2)}, u32[]{:S(2)}) collective-permute-start(bf16[4,1792]{1,0:T(4,128)(2,1)S(1)} %get-tuple-element.92), channel_id=1, source_target_pairs={{0,1},{1,0},{2,3},{3,2},{4,5},{5,4},{6,7},{7,6},{8,9},{9,8},{10,11... | collective-permute-start | bytes 43016 | tf_op jit(solution)/shard_map/ppermute | solution.py:30
  51.3 1.7 %place_page.1 = (f32[4,1792]{1,0:T(4,128)S(1)}, bf16[20,64,1792]{2,1,0:T(8,128)(2,1)}, bf16[20,64,1792]{2,1,0:T(8,128)(2,1)}) custom-call(s32[4]{0:T(128)S(1)} %copy-done.5, s32[4]{0:T(128)S(1)} %copy-done.6, s32[4,16]{1,0:T(4,128)S(1)} %copy-done.4, f32[8,128]{1,0:T(8,128)S(1)} %find_sources.1.source_ref, ...), custom_call_target="tpu_custom_call", output_to_operand_aliasing={{1}: (15, {}), {2}: (16, {})} | custom-call | tf_op jit(solution)/shard_map/place_page/pallas_call | solution.py:677
  53.0 2.1 %collective-permute-done.22 = bf16[4,1792]{1,0:T(4,128)(2,1)S(1)} collective-permute-done((bf16[4,1792]{1,0:T(4,128)(2,1)S(1)}, bf16[4,1792]{1,0:T(4,128)(2,1)S(1)}, u32[]{:S(2)}, u32[]{:S(2)}) %collective-permute-start.22) | collective-permute-done | bytes 14368 | tf_op jit(solution)/shard_map/ppermute | solution.py:30
  55.1 0.6 %fusion.6 = bf16[4,1792]{1,0:T(4,128)(2,1)} fusion(f32[4,1792]{1,0:T(4,128)S(1)} %get-tuple-element.70, bf16[4,1792]{1,0:T(4,128)(2,1)S(1)} %collective-permute-done.22, bf16[4,1792]{1,0:T(4,128)(2,1)S(1)} %collective-permute-done.21, bf16[4,1792]{1,0:T(4,128)(2,1)S(1)} %collective-permute-done.20, f32[4,4,1792]{2,1,0:T(4,128)S(1)} %fusion.2), kind=kLoop, calls=%fused_computation.13 | loop fusion | flops 57344 | bytes 114688 | tf_op jit(solution)/shard_map/convert_element_type | solution.py:786
  (51 shorter events, 0.3 us)
Async XLA Ops:
  0.6 3.1 %copy-start.3 = (f32[7168]{0:T(1024)S(1)}, f32[7168]{0:T(1024)}, u32[]{:S(2)}) copy-start(f32[7168]{0:T(1024)} %param.15) | copy-start | bytes 86020
  0.6 3.1 %copy-start.2 = (f32[7168]{0:T(1024)S(1)}, f32[7168]{0:T(1024)}, u32[]{:S(2)}) copy-start(f32[7168]{0:T(1024)} %param.14) | copy-start | bytes 86020
  0.7 11.9 %copy-start = (bf16[896,14,384]{2,0,1:T(8,128)(2,1)S(1)}, bf16[896,14,384]{2,0,1:T(8,128)(2,1)}, u32[]{:S(2)}) copy-start(bf16[896,14,384]{2,0,1:T(8,128)(2,1)} %param.16) | copy-start | bytes 28901380
  0.7 3.1 %collective-permute-start = (bf16[4,7168]{1,0:T(4,128)(2,1)}, bf16[4,7168]{1,0:T(4,128)(2,1)S(1)}, u32[]{:S(2)}, u32[]{:S(2)}) collective-permute-start(bf16[4,7168]{1,0:T(4,128)(2,1)} %token_ref.1), channel_id=1, source_target_pairs={{0,4},{4,0},{8,12},{12,8},{16,20},{20,16},{24,28},{28,24},{1,5},{5... | collective-permute-start | bytes 172040 | tf_op jit(solution)/shard_map/ppermute | solution.py:30
  4.1 4.7 %collective-permute-start.1 = (bf16[2,32,1792]{2,1,0:T(8,128)(2,1)S(1)}, bf16[2,32,1792]{2,1,0:T(8,128)(2,1)S(1)}, u32[]{:S(2)}, u32[]{:S(2)}) collective-permute-start(bf16[2,32,1792]{2,1,0:T(8,128)(2,1)S(1)} %get-tuple-element.46), channel_id=1, source_target_pairs={{0,4},{4,0},{8,12},{12,8},{16,20},{20,16},{24,28},{28,24},{1,5},{5... | collective-permute-start | bytes 688136 | tf_op jit(solution)/shard_map/ppermute | solution.py:30
  4.2 5.7 %collective-permute-start.2 = (bf16[2,4,1024]{2,1,0:T(4,128)(2,1)S(1)}, bf16[2,4,1024]{2,1,0:T(4,128)(2,1)S(1)}, u32[]{:S(2)}, u32[]{:S(2)}) collective-permute-start(bf16[2,4,1024]{2,1,0:T(4,128)(2,1)S(1)} %get-tuple-element.47), channel_id=1, source_target_pairs={{0,24},{4,28},{8,16},{12,20},{16,8},{20,12},{24,0},{28,4},{1,25},{... | collective-permute-start | bytes 49160 | tf_op jit(solution)/shard_map/ppermute | solution.py:30
  8.2 3.7 %collective-permute-start.3 = (bf16[2,4,1024]{2,1,0:T(4,128)(2,1)S(1)}, bf16[2,4,1024]{2,1,0:T(4,128)(2,1)S(1)}, u32[]{:S(2)}, u32[]{:S(2)}) collective-permute-start(bf16[2,4,1024]{2,1,0:T(4,128)(2,1)S(1)} %get-tuple-element.48), channel_id=1, source_target_pairs={{0,16},{4,20},{8,24},{12,28},{16,0},{20,4},{24,8},{28,12},{1,17},{... | collective-permute-start | bytes 49160 | tf_op jit(solution)/shard_map/ppermute | solution.py:30
  8.7 3.7 %collective-permute-start.4 = (bf16[2,4,1024]{2,1,0:T(4,128)(2,1)S(1)}, bf16[2,4,1024]{2,1,0:T(4,128)(2,1)S(1)}, u32[]{:S(2)}, u32[]{:S(2)}) collective-permute-start(bf16[2,4,1024]{2,1,0:T(4,128)(2,1)S(1)} %get-tuple-element.49), channel_id=1, source_target_pairs={{0,8},{4,12},{8,0},{12,4},{16,24},{20,28},{24,16},{28,20},{1,9},{5... | collective-permute-start | bytes 49160 | tf_op jit(solution)/shard_map/ppermute | solution.py:30
  8.8 11.5 %slice-start = ((s8[4587520]{0:T(1024)(128)(4,1)}), s8[4194304]{0:T(1024)(128)(4,1)S(1)}, s32[]{:S(2)}) async-start(s8[4587520]{0:T(1024)(128)(4,1)} %bitcast.64), calls=%async_computation | async-start | bytes 8388608
  12.5 10.6 %collective-permute-start.9 = (bf16[2,2,32,1792]{3,2,1,0:T(8,128)(2,1)S(1)}, bf16[2,2,32,1792]{3,2,1,0:T(8,128)(2,1)S(1)}, u32[]{:S(2)}, u32[]{:S(2)}) collective-permute-start(bf16[2,2,32,1792]{3,2,1,0:T(8,128)(2,1)S(1)} %pad_maximum_fusion.refs_0_.refs_6_), channel_id=1, source_target_pairs={{0,8},{4,20},{8,0},{12,28},{16,24},{20,4},{24,16},{28,12},{1,9},{5... | collective-permute-start | bytes 1376264 | tf_op jit(solution)/shard_map/ppermute | solution.py:178
  12.5 7.7 %copy-start.7 = (f32[14,384]{1,0:T(8,128)S(1)}, f32[14,384]{1,0:T(8,128)}, u32[]{:S(2)}) copy-start(f32[14,384]{1,0:T(8,128)} %param.17) | copy-start | bytes 64516
  12.5 7.8 %slice-start.1 = ((s8[4587520]{0:T(1024)(128)(4,1)}), s8[393216]{0:T(1024)(128)(4,1)S(1)}, s32[]{:S(2)}) async-start(s8[4587520]{0:T(1024)(128)(4,1)} %bitcast.64), calls=%async_computation.1 | async-start | bytes 786432
  14.8 1.7 %collective-permute-start.5 = (f32[4,4,5504]{2,1,0:T(4,128)S(1)}, f32[4,4,5504]{2,1,0:T(4,128)S(1)}, u32[]{:S(2)}, u32[]{:S(2)}) collective-permute-start(f32[4,4,5504]{2,1,0:T(4,128)S(1)} %get-tuple-element.56), channel_id=1, source_target_pairs={{0,4},{4,0},{8,12},{12,8},{16,20},{20,16},{24,28},{28,24},{1,5},{5... | collective-permute-start | bytes 1056776 | tf_op jit(solution)/shard_map/ppermute | solution.py:30
  16.6 8.7 %collective-permute-start.6 = (bf16[4,7168]{1,0:T(4,128)(2,1)S(1)}, bf16[4,7168]{1,0:T(4,128)(2,1)S(1)}, u32[]{:S(2)}, u32[]{:S(2)}) collective-permute-start(bf16[4,7168]{1,0:T(4,128)(2,1)S(1)} %get-tuple-element.57), channel_id=1, source_target_pairs={{0,24},{4,28},{8,16},{12,20},{16,8},{20,12},{24,0},{28,4},{1,25},{... | collective-permute-start | bytes 172040 | tf_op jit(solution)/shard_map/ppermute | solution.py:30
  19.6 5.7 %collective-permute-start.7 = (bf16[4,7168]{1,0:T(4,128)(2,1)S(1)}, bf16[4,7168]{1,0:T(4,128)(2,1)S(1)}, u32[]{:S(2)}, u32[]{:S(2)}) collective-permute-start(bf16[4,7168]{1,0:T(4,128)(2,1)S(1)} %get-tuple-element.58), channel_id=1, source_target_pairs={{0,16},{4,20},{8,24},{12,28},{16,0},{20,4},{24,8},{28,12},{1,17},{... | collective-permute-start | bytes 172040 | tf_op jit(solution)/shard_map/ppermute | solution.py:30
  20.1 5.2 %collective-permute-start.8 = (bf16[4,7168]{1,0:T(4,128)(2,1)S(1)}, bf16[4,7168]{1,0:T(4,128)(2,1)S(1)}, u32[]{:S(2)}, u32[]{:S(2)}) collective-permute-start(bf16[4,7168]{1,0:T(4,128)(2,1)S(1)} %get-tuple-element.59), channel_id=1, source_target_pairs={{0,8},{4,12},{8,0},{12,4},{16,24},{20,28},{24,16},{28,20},{1,9},{5... | collective-permute-start | bytes 172040 | tf_op jit(solution)/shard_map/ppermute | solution.py:30
  20.3 5.1 %slice-start.2 = ((s8[4587520]{0:T(1024)(128)(4,1)}), s8[4194304]{0:T(1024)(128)(4,1)S(1)}, s32[]{:S(2)}) async-start(s8[4587520]{0:T(1024)(128)(4,1)} %bitcast.66), calls=%async_computation.2 | async-start | bytes 8388608
  20.3 5.0 %slice-start.3 = ((s8[4587520]{0:T(1024)(128)(4,1)}), s8[393216]{0:T(1024)(128)(4,1)S(1)}, s32[]{:S(2)}) async-start(s8[4587520]{0:T(1024)(128)(4,1)} %bitcast.66), calls=%async_computation.3 | async-start | bytes 786432
  20.3 5.0 %copy-start.4 = (s32[4,16]{1,0:T(4,128)S(1)}, s32[4,16]{1,0:T(4,128)}, u32[]{:S(2)}) copy-start(s32[4,16]{1,0:T(4,128)} %table_ref.3) | copy-start | bytes 772
  20.4 5.0 %copy-start.5 = (s32[4]{0:T(128)S(1)}, s32[4]{0:T(128)}, u32[]{:S(2)}) copy-start(s32[4]{0:T(128)} %length_ref.3) | copy-start | bytes 52
  20.4 5.0 %copy-start.6 = (s32[4]{0:T(128)S(1)}, s32[4]{0:T(128)}, u32[]{:S(2)}) copy-start(s32[4]{0:T(128)} %slot_ref.3) | copy-start | bytes 52
  23.4 12.8 %collective-permute-start.14 = (bf16[2,2,32,1792]{3,2,1,0:T(8,128)(2,1)S(1)}, bf16[2,2,32,1792]{3,2,1,0:T(8,128)(2,1)S(1)}, u32[]{:S(2)}, u32[]{:S(2)}) collective-permute-start(bf16[2,2,32,1792]{3,2,1,0:T(8,128)(2,1)S(1)} %turn_pages.1.refs_12_), channel_id=1, source_target_pairs={{0,16},{4,12},{8,24},{12,4},{16,0},{20,28},{24,8},{28,20},{1,17},{... | collective-permute-start | bytes 1376264 | tf_op jit(solution)/shard_map/ppermute | solution.py:178
  27.5 1.3 %collective-permute-start.10 = (bf16[4,32,256]{2,1,0:T(8,128)(2,1)S(1)}, bf16[4,32,256]{2,1,0:T(8,128)(2,1)S(1)}, u32[]{:S(2)}, u32[]{:S(2)}) collective-permute-start(bf16[4,32,256]{2,1,0:T(8,128)(2,1)S(1)} %get-tuple-element.63), channel_id=1, source_target_pairs={{0,4},{4,0},{8,12},{12,8},{16,20},{20,16},{24,28},{28,24},{1,5},{5... | collective-permute-start | bytes 196616 | tf_op jit(solution)/shard_map/ppermute | solution.py:30
  28.8 5.2 %collective-permute-start.11 = (bf16[32,256]{1,0:T(8,128)(2,1)S(1)}, bf16[32,256]{1,0:T(8,128)(2,1)S(1)}, u32[]{:S(2)}, u32[]{:S(2)}) collective-permute-start(bf16[32,256]{1,0:T(8,128)(2,1)S(1)} %pad_maximum_fusion.1), channel_id=1, source_target_pairs={{0,24},{4,28},{8,16},{12,20},{16,8},{20,12},{24,0},{28,4},{1,25},{... | collective-permute-start | bytes 49160 | tf_op jit(solution)/shard_map/ppermute | solution.py:30
  32.3 3.8 %collective-permute-start.12 = (bf16[32,256]{1,0:T(8,128)(2,1)S(1)}, bf16[32,256]{1,0:T(8,128)(2,1)S(1)}, u32[]{:S(2)}, u32[]{:S(2)}) collective-permute-start(bf16[32,256]{1,0:T(8,128)(2,1)S(1)} %pad_maximum_fusion.2), channel_id=1, source_target_pairs={{0,16},{4,20},{8,24},{12,28},{16,0},{20,4},{24,8},{28,12},{1,17},{... | collective-permute-start | bytes 49160 | tf_op jit(solution)/shard_map/ppermute | solution.py:30
  32.4 3.8 %collective-permute-start.13 = (bf16[32,256]{1,0:T(8,128)(2,1)S(1)}, bf16[32,256]{1,0:T(8,128)(2,1)S(1)}, u32[]{:S(2)}, u32[]{:S(2)}) collective-permute-start(bf16[32,256]{1,0:T(8,128)(2,1)S(1)} %pad_maximum_fusion.3), channel_id=1, source_target_pairs={{0,8},{4,12},{8,0},{12,4},{16,24},{20,28},{24,16},{28,20},{1,9},{5... | collective-permute-start | bytes 49160 | tf_op jit(solution)/shard_map/ppermute | solution.py:30
  37.2 1.6 %collective-permute-start.15 = (bf16[4,4,4,1792]{3,2,1,0:T(4,128)(2,1)S(1)}, bf16[4,4,4,1792]{3,2,1,0:T(4,128)(2,1)S(1)}, u32[]{:S(2)}, u32[]{:S(2)}) collective-permute-start(bf16[4,4,4,1792]{3,2,1,0:T(4,128)(2,1)S(1)} %get-tuple-element.66), channel_id=1, source_target_pairs={{0,4},{4,0},{8,12},{12,8},{16,20},{20,16},{24,28},{28,24},{1,5},{5... | collective-permute-start | bytes 688136 | tf_op jit(solution)/shard_map/ppermute | solution.py:30
  37.5 5.1 %collective-permute-start.19 = (bf16[2,32,1792]{2,1,0:T(8,128)(2,1)S(1)}, bf16[2,32,1792]{2,1,0:T(8,128)(2,1)S(1)}, u32[]{:S(2)}, u32[]{:S(2)}) collective-permute-start(bf16[2,32,1792]{2,1,0:T(8,128)(2,1)S(1)} %choose_half.1), channel_id=1, source_target_pairs={{0,4},{4,0},{8,12},{12,8},{16,20},{20,16},{24,28},{28,24},{1,5},{5... | collective-permute-start | bytes 688136 | tf_op jit(solution)/shard_map/ppermute | solution.py:30
  39.0 5.7 %collective-permute-start.16 = (bf16[4,4,1792]{2,1,0:T(4,128)(2,1)S(1)}, bf16[4,4,1792]{2,1,0:T(4,128)(2,1)S(1)}, u32[]{:S(2)}, u32[]{:S(2)}) collective-permute-start(bf16[4,4,1792]{2,1,0:T(4,128)(2,1)S(1)} %get-tuple-element.75), channel_id=1, source_target_pairs={{0,24},{4,28},{8,16},{12,20},{16,8},{20,12},{24,0},{28,4},{1,25},{... | collective-permute-start | bytes 172040 | tf_op jit(solution)/shard_map/ppermute | solution.py:30
  40.5 5.2 %collective-permute-start.18 = (bf16[4,4,1792]{2,1,0:T(4,128)(2,1)S(1)}, bf16[4,4,1792]{2,1,0:T(4,128)(2,1)S(1)}, u32[]{:S(2)}, u32[]{:S(2)}) collective-permute-start(bf16[4,4,1792]{2,1,0:T(4,128)(2,1)S(1)} %get-tuple-element.76), channel_id=1, source_target_pairs={{0,8},{4,12},{8,0},{12,4},{16,24},{20,28},{24,16},{28,20},{1,9},{5... | collective-permute-start | bytes 172040 | tf_op jit(solution)/shard_map/ppermute | solution.py:30
  42.6 8.8 %copy-start.1 = (f32[7168]{0:T(1024)S(1)}, f32[7168]{0:T(1024)}, u32[]{:S(2)}) copy-start(f32[7168]{0:T(1024)} %param.19) | copy-start | bytes 86020
  42.6 4.2 %collective-permute-start.17 = (bf16[4,4,1792]{2,1,0:T(4,128)(2,1)S(1)}, bf16[4,4,1792]{2,1,0:T(4,128)(2,1)S(1)}, u32[]{:S(2)}, u32[]{:S(2)}) collective-permute-start(bf16[4,4,1792]{2,1,0:T(4,128)(2,1)S(1)} %get-tuple-element.77), channel_id=1, source_target_pairs={{0,16},{4,20},{8,24},{12,28},{16,0},{20,4},{24,8},{28,12},{1,17},{... | collective-permute-start | bytes 172040 | tf_op jit(solution)/shard_map/ppermute | solution.py:30
  46.9 6.2 %collective-permute-start.20 = (bf16[4,1792]{1,0:T(4,128)(2,1)S(1)}, bf16[4,1792]{1,0:T(4,128)(2,1)S(1)}, u32[]{:S(2)}, u32[]{:S(2)}) collective-permute-start(bf16[4,1792]{1,0:T(4,128)(2,1)S(1)} %get-tuple-element.90), channel_id=1, source_target_pairs={{0,3},{1,2},{2,1},{3,0},{4,7},{5,6},{6,5},{7,4},{8,11},{9,10},{10,... | collective-permute-start | bytes 43016 | tf_op jit(solution)/shard_map/ppermute | solution.py:30
  50.5 4.6 %collective-permute-start.22 = (bf16[4,1792]{1,0:T(4,128)(2,1)S(1)}, bf16[4,1792]{1,0:T(4,128)(2,1)S(1)}, u32[]{:S(2)}, u32[]{:S(2)}) collective-permute-start(bf16[4,1792]{1,0:T(4,128)(2,1)S(1)} %get-tuple-element.91), channel_id=1, source_target_pairs={{0,2},{1,3},{2,0},{3,1},{4,6},{5,7},{6,4},{7,5},{8,10},{9,11},{10,... | collective-permute-start | bytes 43016 | tf_op jit(solution)/shard_map/ppermute | solution.py:30
  50.5 4.6 %collective-permute-start.21 = (bf16[4,1792]{1,0:T(4,128)(2,1)S(1)}, bf16[4,1792]{1,0:T(4,128)(2,1)S(1)}, u32[]{:S(2)}, u32[]{:S(2)}) collective-permute-start(bf16[4,1792]{1,0:T(4,128)(2,1)S(1)} %get-tuple-element.92), channel_id=1, source_target_pairs={{0,1},{1,0},{2,3},{3,2},{4,5},{5,4},{6,7},{7,6},{8,9},{9,8},{10,11... | collective-permute-start | bytes 43016 | tf_op jit(solution)/shard_map/ppermute | solution.py:30

commit v13 on v12

--- a/solution.py
+++ b/solution.py
@@ -67,26 +67,10 @@
     return leaving
 
 
-def pick_halves(lengths, page_table, new_slot, new_page, tokens, key_pool, value_pool):
+def tell(lengths, new_slot, new_page, tokens, page):
     slots = new_slot.shape[0]
-    page, width = key_pool.shape[1:]
-    half = page // 2
-
-    def kernel(
-        length_ref, table_ref, slot_ref, page_ref, token_ref, key_ref, value_ref,
-        keep_half, send_half, told_ref, token_out, sems,
-    ):
-        here = lax.axis_index("req")
-        leaving = leaving_slot(slot_ref, slots, here)
-        copies = []
-        for n, source in enumerate((key_ref, value_ref)):
-            for e, target in enumerate((keep_half, send_half)):
-                rows = pl.ds(pl.multiple_of((here % 2 ^ e) * half, half), half)
-                copies.append(
-                    pltpu.make_async_copy(source.at[table_ref[leaving, 0], rows], target.at[n], sems.at[n, e])
-                )
-        for copy in copies:
-            copy.start()
+
+    def kernel(length_ref, slot_ref, page_ref, token_ref, told_ref, token_out):
         row = lax.broadcasted_iota(jnp.int32, (slots, META), 0)
         lane = lax.broadcasted_iota(jnp.int32, (slots, META), 1)
         told = jnp.zeros((slots, META), F32)
@@ -97,25 +81,46 @@
                 told = jnp.where((row == s) & (lane == j), number.astype(F32), told)
         told_ref[...] = told
         token_out[...] = token_ref[...]
-        for copy in copies:
-            copy.wait()
-
-    halves = jax.ShapeDtypeStruct((2, half, width), key_pool.dtype)
+
     return pl.pallas_call(
         kernel,
         out_shape=(
-            halves,
-            halves,
             jax.ShapeDtypeStruct((slots, META), F32),
             jax.ShapeDtypeStruct(tokens.shape, tokens.dtype),
         ),
-        in_specs=[SMEM] * 4 + [VMEM] + [HBM] * 2,
-        out_specs=(VMEM,) * 4,
-        scratch_shapes=[pltpu.SemaphoreType.DMA((2, 2))],
+        in_specs=[SMEM] * 3 + [VMEM],
+        out_specs=(VMEM, VMEM),
         compiler_params=pltpu.CompilerParams(vmem_limit_bytes=2 * MIB),
-        cost_estimate=cost(0, 8 * page * width),
-        name="pick_halves",
-    )(*in_hbm(lengths, page_table, new_slot, new_page, tokens, key_pool, value_pool))
+        cost_estimate=cost(0, 0),
+        name="tell",
+    )(*in_hbm(lengths, new_slot, new_page, tokens))
+
+
+def pick_page(new_slot, page_table, key_pool, value_pool, *after):
+    slots = new_slot.shape[0]
+
+    def kernel(slot_ref, table_ref, key_ref, value_ref, *refs):
+        out_ref, sems = refs[len(after) :]
+        leaving = leaving_slot(slot_ref, slots, lax.axis_index("req"))
+        copies = [
+            pltpu.make_async_copy(source.at[table_ref[leaving, 0]], out_ref.at[n], sems.at[n])
+            for n, source in enumerate((key_ref, value_ref))
+        ]
+        for copy in copies:
+            copy.start()
+        for copy in copies:
+            copy.wait()
+
+    return pl.pallas_call(
+        kernel,
+        out_shape=jax.ShapeDtypeStruct((2,) + key_pool.shape[1:], key_pool.dtype),
+        in_specs=[SMEM] * 2 + [HBM] * 2 + [ANY] * len(after),
+        out_specs=VMEM,
+        scratch_shapes=[pltpu.SemaphoreType.DMA((2,))],
+        compiler_params=pltpu.CompilerParams(vmem_limit_bytes=2 * MIB),
+        cost_estimate=cost(0, 0),
+        name="pick_page",
+    )(*in_hbm(new_slot, page_table, key_pool, value_pool), *after)
 
 
 def prepare(tokens, other_tokens, gain, shift, told):
@@ -221,74 +226,72 @@
     return jnp.sum(jnp.where(lane == j, source_ref[:1, :], 0.0)).astype(jnp.int32)
 
 
-def turn_pages(sources, halves, chips):
-    across = len(halves)
+def turn_pages(sources, messages, chips):
+    across = len(messages)
     down = chips // across
-    shape = halves[0].shape
+    shape = (2,) + messages[0].shape
 
     def kernel(source_ref, *refs):
-        half_refs, out_refs = refs[:across], refs[across:]
+        message_refs, out_refs = refs[:across], refs[across:]
         for row in range(1, down):
             for j in range(2):
                 source = number_at(source_ref, 2 * row + j)
-                place = jnp.where(source < 2 * across, source, 0)
+                place = jnp.where((source % 2 == 0) & (source < 2 * across), source // 2, 0)
                 for d in range(across):
-                    for e in range(2):
-
-                        @pl.when(place == 2 * d + e)
-                        def _():
-                            out_refs[row - 1][j] = half_refs[d][e]
-
-    one = jax.ShapeDtypeStruct(shape, halves[0].dtype)
+
+                    @pl.when(place == d)
+                    def _():
+                        out_refs[row - 1][j] = message_refs[d][...]
+
+    one = jax.ShapeDtypeStruct(shape, messages[0].dtype)
     return pl.pallas_call(
         kernel,
         out_shape=(one,) * (down - 1),
         in_specs=[VMEM] * (1 + across),
         out_specs=(VMEM,) * (down - 1),
-        compiler_params=pltpu.CompilerParams(vmem_limit_bytes=(across + down) * MIB),
-        cost_estimate=cost(0, 4 * halves[0].size),
+        compiler_params=pltpu.CompilerParams(vmem_limit_bytes=(across + 2 * down) * MIB),
+        cost_estimate=cost(0, 0),
         name="turn_pages",
-    )(sources, *halves)
-
-
-def with_half(source, across, core, half_refs, turned_refs, use):
-    place = jnp.where(source < 2 * across, source, 2 * across + source // (2 * across))
-    for d, ref in enumerate(half_refs):
-        for e in range(2):
-
-            @pl.when(place == 2 * d + e)
-            def _():
-                use(ref.at[e])
+    )(sources, *messages)
+
+
+def with_page(source, across, core, message_refs, turned_refs, use):
+    place = jnp.where(source < 2 * across, source // 2, across - 1 + source // (2 * across))
+    for d, ref in enumerate(message_refs):
+
+        @pl.when(place == d)
+        def _():
+            use(ref)
 
     for row, ref in enumerate(turned_refs):
 
-        @pl.when(place == 2 * across + row + 1)
+        @pl.when(place == across + row)
         def _():
             use(ref.at[core])
 
 
-def choose_half(sources, halves, turned, after):
-    across, rows = len(halves), len(turned)
+def choose_page(sources, messages, turned, after):
+    across, rows = len(messages), len(turned)
 
     def kernel(source_ref, *refs):
-        half_refs, turned_refs = refs[:across], refs[across : across + rows]
+        message_refs, turned_refs = refs[:across], refs[across : across + rows]
         out_ref = refs[-1]
 
         def use(ref):
             out_ref[...] = ref[...]
 
-        with_half(number_at(source_ref, 1), across, 1, half_refs, turned_refs, use)
-
-    shape = halves[0].shape[1:]
-    return pl.pallas_call(
-        kernel,
-        out_shape=jax.ShapeDtypeStruct(shape, halves[0].dtype),
+        with_page(number_at(source_ref, 1), across, 1, message_refs, turned_refs, use)
+
+    one = messages[0]
+    return pl.pallas_call(
+        kernel,
+        out_shape=jax.ShapeDtypeStruct(one.shape, one.dtype),
         in_specs=[VMEM] * (1 + across + rows) + [ANY],
         out_specs=VMEM,
-        compiler_params=pltpu.CompilerParams(vmem_limit_bytes=(1 + across + rows) * MIB),
-        cost_estimate=cost(0, 2 * halves[0].size),
-        name="choose_half",
-    )(sources, *halves, *turned, after)
+        compiler_params=pltpu.CompilerParams(vmem_limit_bytes=(2 + across + 2 * rows) * MIB),
+        cost_estimate=cost(0, 0),
+        name="choose_page",
+    )(sources, *messages, *turned, after)
 
 
 def project(blocks, weight, later):
@@ -366,7 +369,7 @@
     )(keep, got)
 
 
-def attend(lengths, new_slot, page_table, sums, bias, tokens, key_pool, value_pool, written, after):
+def attend(lengths, new_slot, page_table, sums, bias, tokens, key_pool, value_pool, after):
     parts = len(sums)
     slots = sums[0].shape[0]
     pages, page, width = key_pool.shape
@@ -384,7 +387,17 @@
     def kernel(*refs):
         length_ref, slot_ref, table_ref = refs[:3]
         sum_refs = refs[3 : 3 + parts][::-1]
-        (bias_ref, token_ref, key_ref, value_ref, _, _, pack_keep, pack_send, patch_ref, attended_ref) = refs[3 + parts :]
+        (bias_ref, token_ref, key_ref, value_ref, _, pack_keep, pack_send, patch_ref, value_out) = refs[
+            3 + parts : 12 + parts
+        ]
+        attended_ref, out_sems = refs[12 + parts :]
+        step = pages // 4
+        writes = [
+            pltpu.make_async_copy(value_ref.at[pl.ds(i * step, step)], value_out.at[pl.ds(i * step, step)], out_sems.at[i])
+            for i in range(4)
+        ]
+        for write in writes:
+            write.start()
         here = lax.axis_index("req")
         column_block = lax.axis_index("head")
         leaving = leaving_slot(slot_ref, slots, here)
@@ -528,17 +541,24 @@
                 new = jnp.broadcast_to(new_rows[n][s : s + 1], (tall, width))
                 patch_ref[n, s] = jnp.where(at == offset - first, new, old).astype(BF16)
 
+        for write in writes:
+            write.wait()
+
     packed = jax.ShapeDtypeStruct((parts, pack_rows(slots, strips), PACK), BF16)
-    return pl.pallas_call(
-        kernel,
-        out_shape=(packed, packed, jax.ShapeDtypeStruct((2, slots, tall, width), BF16)),
-        in_specs=[SMEM] * 3 + [VMEM] * (parts + 4) + [HBM, ANY],
-        out_specs=(VMEM, VMEM, VMEM),
-        scratch_shapes=[pltpu.VMEM((-(-slots // 8) * 8, width), F32)],
+    pool = jax.ShapeDtypeStruct(key_pool.shape, key_pool.dtype)
+    return pl.pallas_call(
+        kernel,
+        out_shape=(packed, packed, jax.ShapeDtypeStruct((2, slots, tall, width), BF16), pool),
+        in_specs=[SMEM] * 3 + [VMEM] * (parts + 4) + [ANY],
+        out_specs=(VMEM, VMEM, VMEM, HBM),
+        scratch_shapes=[
+            pltpu.VMEM((-(-slots // 8) * 8, width), F32),
+            pltpu.SemaphoreType.DMA((4,)),
+        ],
         compiler_params=pltpu.CompilerParams(vmem_limit_bytes=18 * MIB),
         cost_estimate=cost(0, 0),
         name="attend",
-    )(lengths, new_slot, page_table, *sums[::-1], bias, tokens, key_pool, value_pool, *in_hbm(written), after)
+    )(lengths, new_slot, page_table, *sums[::-1], bias, tokens, key_pool, value_pool, after)
 
 
 def pack_rows(slots, strips):
@@ -595,12 +615,11 @@
     )(*blocks[::-1], weight, *after)
 
 
-def place_page(lengths, new_slot, page_table, sources, patches, packs, tokens, out_bias, halves, turned, from_other, key_out, value_out):
-    chips, across, rows = len(packs), len(halves), len(turned)
+def place_page(lengths, new_slot, page_table, sources, patches, packs, tokens, out_bias, messages, turned, from_other, key_out, value_out):
+    chips, across, rows = len(packs), len(messages), len(turned)
     down = chips // across
     count = across + rows + 1
     page, width = key_out.shape[1:]
-    half = page // 2
     slots = tokens.shape[0]
     strips = width // PACK
     tall = patches.shape[2]
@@ -608,7 +627,7 @@
     def kernel(length_ref, slot_ref, table_ref, source_ref, patch_ref, *refs):
         pack_refs = refs[:chips][::-1]
         token_ref, bias_ref = refs[chips : chips + 2]
-        half_refs = refs[chips + 2 : chips + 2 + across]
+        message_refs = refs[chips + 2 : chips + 2 + across]
         turned_refs = refs[chips + 2 + across : chips + 2 + across + rows]
         other_ref = refs[chips + 1 + count]
         _, _, base_ref, key_ref, value_ref, buffer, out_sems, patch_sems = refs[chips + 2 + count :]
@@ -630,13 +649,20 @@
 
         column = pl.multiple_of(lax.axis_index("head") * width, LANES)
         page_at, offset = [number_at(source_ref, 2 * down + j) for j in range(2)]
-        own_rows, other_rows = [pl.ds(pl.multiple_of((here % 2 ^ e) * half, half), half) for e in range(2)]
 
         def use(ref):
-            buffer[:, own_rows, :] = ref[...]
-
-        with_half(number_at(source_ref, 0), across, 0, half_refs, turned_refs, use)
-        buffer[:, other_rows, :] = other_ref[...]
+            buffer[...] = ref[...]
+
+        source = number_at(source_ref, 0)
+
+        @pl.when(source % 2 == 0)
+        def _():
+            with_page(source, across, 0, message_refs, turned_refs, use)
+
+        @pl.when(source % 2 == 1)
+        def _():
+            use(other_ref)
+
         arrived = pack_refs[0][2 * slots :, :].astype(F32)
         for ref in pack_refs[1:]:
             arrived = arrived + ref[2 * slots :, :].astype(F32)
@@ -685,11 +711,11 @@
             pltpu.SemaphoreType.DMA((2, slots)),
         ],
         input_output_aliases={chips + 7 + count: 1, chips + 8 + count: 2},
-        compiler_params=pltpu.CompilerParams(vmem_limit_bytes=(6 + count) * MIB),
+        compiler_params=pltpu.CompilerParams(vmem_limit_bytes=(6 + 2 * count) * MIB),
         cost_estimate=cost(0, 8 * page * width),
         name="place_page",
     )(
-        lengths, new_slot, page_table, sources, patches, *packs[::-1], tokens, out_bias, *halves, *turned, from_other, key_out, value_out
+        lengths, new_slot, page_table, sources, patches, *packs[::-1], tokens, out_bias, *messages, *turned, from_other, key_out, value_out
     )
 
 
@@ -714,28 +740,24 @@
     chips = groups // 2
 
     other_tokens = swap(tokens, "req", 1)
-    keep_half, send_half, told, own_tokens = pick_halves(
-        lengths, page_table, new_slot, new_page, tokens, key_pool, value_pool
-    )
+    told, own_tokens = tell(lengths, new_slot, new_page, tokens, key_pool.shape[1])
     blocks = prepare(own_tokens, other_tokens, norm_gain[None], norm_shift[None], told)
-    send_half, *blocks = lax.optimization_barrier((send_half, *blocks))
     across = row_length(chips)
     spread = [blocks[0]] + [swap(blocks[d], "req", 2 * d) for d in range(1, chips)]
-    halves = [jnp.stack([keep_half, swap(send_half, "req", 1)])]
-    halves[0], *spread = lax.optimization_barrier((halves[0], *spread[::-1]))
-    spread = spread[::-1]
-    halves += [swap_pages(halves[0], chips, True, d) for d in range(1, across)]
+    page = pick_page(new_slot, page_table, key_pool, value_pool, *blocks[::-1])
+    page, *spread = lax.optimization_barrier((page, *spread))
+    pages = [page] + [swap_pages(page, chips, True, d) for d in range(1, across)]
+
     flat = out_weight.reshape(-1, out_weight.shape[2])
     keep, send, staged = project(spread, jnp.transpose(qkv_weight, (1, 0, 2)), flat)
     got = swap(send, "req", 1)
     own, *messages = combine(keep, got)
     sources = find_sources(spread, got)
-    value_out = write_pool(value_pool, own)
-    turning = turn_pages(sources, halves, chips)
+    sums = [own] + [swap(messages[d - 1], "req", 2 * d) for d in range(1, chips)]
+    turning = turn_pages(sources, pages, chips)
     turned = [swap_pages(one, chips, False, row + 1) for row, one in enumerate(turning)]
-    sums = [own] + [swap(messages[d - 1], "req", 2 * d) for d in range(1, chips)]
-
-    pack_keep, pack_send, patches = attend(
+
+    pack_keep, pack_send, patches, value_out = attend(
         lengths,
         new_slot,
         page_table,
@@ -744,7 +766,6 @@
         own_tokens,
         key_pool,
         value_pool,
-        value_out,
         turning[0],
     )
     packs_got = swap(pack_send, "req", 1)
@@ -759,12 +780,12 @@
         packs, staged, head_groups, slots, turned[0]
     )
     total = keep + swap(send, "req", 1).astype(F32)
-    from_other = swap(choose_half(sources, halves, turned, keep), "req", 1)
+    from_other = swap(choose_page(sources, pages, turned, keep), "req", 1)
     summed = total[0]
     for d in reversed(range(1, chips)):
         summed = summed + swap(total[d].astype(BF16), "req", 2 * d).astype(F32)
-    key_out = write_pool(key_pool, from_other)
-    summed, key_out = lax.optimization_barrier((summed, key_out))
+    key_out = write_pool(key_pool, total)
+    summed, key_out, from_other = lax.optimization_barrier((summed, key_out, from_other))
     base, key_out, value_out = place_page(
         lengths,
         new_slot,
@@ -774,7 +795,7 @@
         packs,
         own_tokens,
         out_bias[None],
-        halves,
+        pages,
         turned,
         from_other,
         key_out,

time: 55.8 us -> 55.2 us (0.989)
  waiting for transfers between devices: 14.5 us -> 12.8 us
  local copies, waits for them, and re-layouts: 0.18 us -> 1.66 us
  starting transfers between devices: 23.8 us -> 23.2 us
    pallas_call x2 -> x1, Pallas kernels: 4.54 us -> 2.17 us  [write_pool(): pl.pallas_call(kernel, out_shape=jax.ShapeDtypeStruct(pool.shape, pool.dt...]
    pallas_call x1, Pallas kernels: 2.05 us -> 3.83 us  [attend(): pl.pallas_call(kernel, out_shape=(packed, packed, jax.ShapeDtypeStruct((2...]
    ppermute x21 -> x20, waiting for transfers between devices: 14.5 us -> 12.8 us  [swap(): return lax.ppermute(value, axis, [(i, i ^ step) for i in range(size)])]
    unnamed x25, local copies, waits for them, and re-layouts: 0.08 us -> 1.57 us
    ppermute x21 -> x20, starting transfers between devices: 21.7 us -> 20.6 us  [swap(): return lax.ppermute(value, axis, [(i, i ^ step) for i in range(size)])]
    pallas_call x2 -> x3, Pallas kernels: 2.7 us -> 3.32 us  [the longest x1 2.28 us: pick_page(): pl.pallas_call(kernel, out_shape=jax.ShapeDtypeStruct((2,) + key_pool.sha...]
    ppermute x2, starting transfers between devices: 2.05 us -> 2.65 us  [swap_pages(): lax.ppermute(value, 'req', [(i, i ^ steps[i]) for i in range(2 * chips)])]
  transfers between devices with their start and end apart: 23 -> 22, of which waited for: 12 -> 14; matrix products, arithmetic and copies ran while one was open for 1% -> 0% of each run, Pallas kernels for 25% -> 25%
where the time goes in v13:
time: 55.2 us; the launch traced here: 54.9 us
  starting transfers between devices  23.2 us (42%)
  Pallas kernels  15.3 us (28%)
  waiting for transfers between devices  12.8 us (23%)
  local copies, waits for them, and re-layouts  1.66 us (3%)
  between operations  0.97 us (2%)
  other arithmetic  0.91 us (2%)
    ppermute x20, starting transfers between devices, swap(): return lax.ppermute(value, axis, [(i, i ^ step) for i in range(size)])  20.6 us
    ppermute x20, waiting for transfers between devices, swap(): return lax.ppermute(value, axis, [(i, i ^ step) for i in range(size)])  12.8 us
    pallas_call x1, Pallas kernels, attend(): pl.pallas_call(kernel, out_shape=(packed, packed, jax.ShapeDtypeStruct((2...  3.83 us
    ppermute x2, starting transfers between devices, swap_pages(): lax.ppermute(value, 'req', [(i, i ^ steps[i]) for i in range(2 * chips)])  2.65 us
    pallas_call x1, Pallas kernels, project(): pl.pallas_call(kernel, out_shape=(shape, wider, jax.ShapeDtypeStruct(late...  2.28 us
    pallas_call x1, Pallas kernels, pick_page(): pl.pallas_call(kernel, out_shape=jax.ShapeDtypeStruct((2,) + key_pool.sha...  2.28 us
    pallas_call x1, Pallas kernels, write_pool(): pl.pallas_call(kernel, out_shape=jax.ShapeDtypeStruct(pool.shape, pool.dt...  2.17 us
    pallas_call x1, Pallas kernels, place_page(): pl.pallas_call(kernel, out_shape=(jax.ShapeDtypeStruct((slots, width), F3...  1.65 us
  transfers between devices with their start and end apart: 22, of which 14 were waited for; matrix products, arithmetic and copies ran while one was open for 0% of the time, Pallas kernels for 25%

profile of v13, /device:TPU:0, one launch (start us, length us, event | category | flops | bytes accessed | tf_op | source)
XLA Modules:
  0.0 54.9 jit_solution(11929478024155001401)
XLA Ops:
  0.6 0.5 collective-permute-start
  1.1 0.9 %tell.1 = (f32[4,128]{1,0:T(4,128)S(1)}, bf16[4,7168]{1,0:T(4,128)(2,1)S(1)}) custom-call(s32[4]{0:T(128)} %length_ref.3, s32[4]{0:T(128)} %slot_ref.5, s32[4]{0:T(128)} %page_ref.1, bf16[4,7168]{1,0:T(4,128)(2,1)} %token_ref.1), custom_call_target="tpu_custom_call" | custom-call | tf_op jit(solution)/shard_map/tell/pallas_call | solution.py:85
  2.0 0.2 collective-permute-done.other_ref
  2.3 0.7 %copy-done.2 = f32[7168]{0:T(1024)S(1)} copy-done((f32[7168]{0:T(1024)S(1)}, f32[7168]{0:T(1024)}, u32[]{:S(2)}) %copy-start.2) | copy-done | bytes 28696
  3.0 0.7 %copy-done.3 = f32[7168]{0:T(1024)S(1)} copy-done((f32[7168]{0:T(1024)S(1)}, f32[7168]{0:T(1024)}, u32[]{:S(2)}) %copy-start.3) | copy-done | bytes 28696
  3.7 0.4 prepare.1
  4.1 3.9 %collective-permute-start.3 = (bf16[2,4,1024]{2,1,0:T(4,128)(2,1)S(1)}, bf16[2,4,1024]{2,1,0:T(4,128)(2,1)S(1)}, u32[]{:S(2)}, u32[]{:S(2)}) collective-permute-start(bf16[2,4,1024]{2,1,0:T(4,128)(2,1)S(1)} %get-tuple-element.35.refs_0_), channel_id=1, source_target_pairs={{0,24},{4,28},{8,16},{12,20},{16,8},{20,12},{24,0},{28,4},{1,25},{... | collective-permute-start | bytes 49160 | tf_op jit(solution)/shard_map/ppermute | solution.py:30
  8.0 0.5 collective-permute-start.2
  8.5 0.1 collective-permute-start.1
  8.6 2.3 %pick_page.1.refs_0_.refs_6_ = bf16[2,64,1792]{2,1,0:T(8,128)(2,1)S(1)} custom-call(s32[4]{0:T(128)} %slot_ref.5, s32[4,16]{1,0:T(4,128)} %table_ref.3, bf16[20,64,1792]{2,1,0:T(8,128)(2,1)} %pool_ref.1, bf16[20,64,1792]{2,1,0:T(8,128)(2,1)} %refs_10_.1, bf16[2,4,1024]{2,1,0:T(4,128)(2,1)S(1)} %get-tuple-element.35.refs_0_, ...), custom_call_target="tpu_custom_call" | custom-call | tf_op jit(solution)/shard_map/pick_page/pallas_call | solution.py:114
  10.9 0.8 %collective-permute-done.2.refs_1_ = bf16[2,4,1024]{2,1,0:T(4,128)(2,1)S(1)} collective-permute-done((bf16[2,4,1024]{2,1,0:T(4,128)(2,1)S(1)}, bf16[2,4,1024]{2,1,0:T(4,128)(2,1)S(1)}, u32[]{:S(2)}, u32[]{:S(2)}) %collective-permute-start.2) | collective-permute-done | bytes 16416 | tf_op jit(solution)/shard_map/ppermute | solution.py:30
  11.7 0.5 collective-permute-done.1.refs_2_
  12.2 0.7 %collective-permute-start.8 = (bf16[2,64,1792]{2,1,0:T(8,128)(2,1)S(1)}, bf16[2,64,1792]{2,1,0:T(8,128)(2,1)S(1)}, u32[]{:S(2)}, u32[]{:S(2)}) collective-permute-start(bf16[2,64,1792]{2,1,0:T(8,128)(2,1)S(1)} %pick_page.1.refs_0_.refs_6_), channel_id=1, source_target_pairs={{0,8},{4,20},{8,0},{12,28},{16,24},{20,4},{24,16},{28,12},{1,9},{5... | collective-permute-start | bytes 1376264 | tf_op jit(solution)/shard_map/ppermute | solution.py:183
  13.0 2.3 %project.1 = (f32[4,4,5376]{2,1,0:T(4,128)S(1)}, f32[4,4,5504]{2,1,0:T(4,128)S(1)}, bf16[224,7168]{1,0:T(8,128)(2,1)S(1)}) custom-call(bf16[2,4,1024]{2,1,0:T(4,128)(2,1)S(1)} %collective-permute-done.3.refs_0_, bf16[2,4,1024]{2,1,0:T(4,128)(2,1)S(1)} %collective-permute-done.2.refs_1_, bf16[2,4,1024]{2,1,0:T(4,128)(2,1)S(1)} %collective-permute-done.1.refs_2_, ...), custom_call_target="tpu_custom_call" | custom-call | tf_op jit(solution)/shard_map/project/pallas_call | solution.py:331
  15.2 0.1 collective-permute-start.4
  15.3 1.7 %collective-permute-done.4.got_ref.refs_4_ = f32[4,4,5504]{2,1,0:T(4,128)S(1)} collective-permute-done((f32[4,4,5504]{2,1,0:T(4,128)S(1)}, f32[4,4,5504]{2,1,0:T(4,128)S(1)}, u32[]{:S(2)}, u32[]{:S(2)}) %collective-permute-start.4) | collective-permute-done | bytes 352288 | tf_op jit(solution)/shard_map/ppermute | solution.py:30
  17.0 2.6 %collective-permute-start.5 = (bf16[4,7168]{1,0:T(4,128)(2,1)S(1)}, bf16[4,7168]{1,0:T(4,128)(2,1)S(1)}, u32[]{:S(2)}, u32[]{:S(2)}) collective-permute-start(bf16[4,7168]{1,0:T(4,128)(2,1)S(1)} %get-tuple-element.45), channel_id=1, source_target_pairs={{0,24},{4,28},{8,16},{12,20},{16,8},{20,12},{24,0},{28,4},{1,25},{... | collective-permute-start | bytes 172040 | tf_op jit(solution)/shard_map/ppermute | solution.py:30
  19.6 0.5 collective-permute-start.6
  20.1 0.5 collective-permute-start.7
  20.6 0.3 find_sources.1.source_ref
  20.9 0.3 turn_pages.1.refs_11_
  21.2 2.0 %collective-permute-start.13 = (bf16[2,2,64,1792]{3,2,1,0:T(8,128)(2,1)S(1)}, bf16[2,2,64,1792]{3,2,1,0:T(8,128)(2,1)S(1)}, u32[]{:S(2)}, u32[]{:S(2)}) collective-permute-start(bf16[2,2,64,1792]{3,2,1,0:T(8,128)(2,1)S(1)} %turn_pages.1.refs_11_), channel_id=1, source_target_pairs={{0,16},{4,12},{8,24},{12,4},{16,0},{20,28},{24,8},{28,20},{1,17},{... | collective-permute-start | bytes 2752520 | tf_op jit(solution)/shard_map/ppermute | solution.py:183
  23.2 0.7 %collective-permute-done.6.refs_4_ = bf16[4,7168]{1,0:T(4,128)(2,1)S(1)} collective-permute-done((bf16[4,7168]{1,0:T(4,128)(2,1)S(1)}, bf16[4,7168]{1,0:T(4,128)(2,1)S(1)}, u32[]{:S(2)}, u32[]{:S(2)}) %collective-permute-start.6) | collective-permute-done | bytes 57376 | tf_op jit(solution)/shard_map/ppermute | solution.py:30
  23.9 0.9 %collective-permute-done.7.refs_5_ = bf16[4,7168]{1,0:T(4,128)(2,1)S(1)} collective-permute-done((bf16[4,7168]{1,0:T(4,128)(2,1)S(1)}, bf16[4,7168]{1,0:T(4,128)(2,1)S(1)}, u32[]{:S(2)}, u32[]{:S(2)}) %collective-permute-start.7) | collective-permute-done | bytes 57376 | tf_op jit(solution)/shard_map/ppermute | solution.py:30
  24.9 3.8 %attend.1 = (bf16[4,32,256]{2,1,0:T(8,128)(2,1)S(1)}, bf16[4,32,256]{2,1,0:T(8,128)(2,1)S(1)}, bf16[2,4,16,1792]{3,2,1,0:T(8,128)(2,1)S(1)}, bf16[20,64,1792]{2,1,0:T(8,128)(2,1)}) custom-call(s32[4]{0:T(128)S(1)} %copy-done.6, s32[4]{0:T(128)S(1)} %copy-done.5, s32[4,16]{1,0:T(4,128)S(1)} %copy-done.4, bf16[4,7168]{1,0:T(4,128)(2,1)S(1)} %collective-permute-done.5.refs_3_, ...), custom_call_target="tpu_custom_call" | custom-call | tf_op jit(solution)/shard_map/attend/pallas_call | solution.py:549
  28.7 0.1 collective-permute-start.9
  28.8 1.2 %collective-permute-done.9 = bf16[4,32,256]{2,1,0:T(8,128)(2,1)S(1)} collective-permute-done((bf16[4,32,256]{2,1,0:T(8,128)(2,1)S(1)}, bf16[4,32,256]{2,1,0:T(8,128)(2,1)S(1)}, u32[]{:S(2)}, u32[]{:S(2)}) %collective-permute-start.9) | collective-permute-done | bytes 65568 | tf_op jit(solution)/shard_map/ppermute | solution.py:30
  30.1 1.2 %collective-permute-start.10 = (bf16[32,256]{1,0:T(8,128)(2,1)S(1)}, bf16[32,256]{1,0:T(8,128)(2,1)S(1)}, u32[]{:S(2)}, u32[]{:S(2)}) collective-permute-start(bf16[32,256]{1,0:T(8,128)(2,1)S(1)} %pad_maximum_fusion), channel_id=1, source_target_pairs={{0,24},{4,28},{8,16},{12,20},{16,8},{20,12},{24,0},{28,4},{1,25},{... | collective-permute-start | bytes 49160 | tf_op jit(solution)/shard_map/ppermute | solution.py:30
  31.2 0.5 collective-permute-start.11
  31.8 2.0 %collective-permute-start.12 = (bf16[32,256]{1,0:T(8,128)(2,1)S(1)}, bf16[32,256]{1,0:T(8,128)(2,1)S(1)}, u32[]{:S(2)}, u32[]{:S(2)}) collective-permute-start(bf16[32,256]{1,0:T(8,128)(2,1)S(1)} %pad_maximum_fusion.2), channel_id=1, source_target_pairs={{0,8},{4,12},{8,0},{12,4},{16,24},{20,28},{24,16},{28,20},{1,9},{5... | collective-permute-start | bytes 49160 | tf_op jit(solution)/shard_map/ppermute | solution.py:30
  33.8 1.3 %collective-permute-done.10.refs_0_ = bf16[32,256]{1,0:T(8,128)(2,1)S(1)} collective-permute-done((bf16[32,256]{1,0:T(8,128)(2,1)S(1)}, bf16[32,256]{1,0:T(8,128)(2,1)S(1)}, u32[]{:S(2)}, u32[]{:S(2)}) %collective-permute-start.10) | collective-permute-done | bytes 16416 | tf_op jit(solution)/shard_map/ppermute | solution.py:30
  35.1 0.3 collective-permute-done.11.refs_1_
  35.4 0.2 collective-permute-done.12.refs_2_
  35.6 1.0 %out_project.1 = (f32[4,4,4,1792]{3,2,1,0:T(4,128)S(1)}, bf16[4,4,4,1792]{3,2,1,0:T(4,128)(2,1)S(1)}) custom-call(bf16[32,256]{1,0:T(8,128)(2,1)S(1)} %collective-permute-done.10.refs_0_, bf16[32,256]{1,0:T(8,128)(2,1)S(1)} %collective-permute-done.11.refs_1_, bf16[32,256]{1,0:T(8,128)(2,1)S(1)} %collective-permute-done.12.refs_2_, ...), custom_call_target="tpu_custom_call" | custom-call | tf_op jit(solution)/shard_map/out_project/pallas_call | solution.py:607
  36.7 1.5 %collective-permute-done.14 = bf16[4,4,4,1792]{3,2,1,0:T(4,128)(2,1)S(1)} collective-permute-done((bf16[4,4,4,1792]{3,2,1,0:T(4,128)(2,1)S(1)}, bf16[4,4,4,1792]{3,2,1,0:T(4,128)(2,1)S(1)}, u32[]{:S(2)}, u32[]{:S(2)}) %collective-permute-start.14) | collective-permute-done | bytes 229408 | tf_op jit(solution)/shard_map/ppermute | solution.py:30
  38.2 0.2 fusion.11
  38.4 3.0 %collective-permute-start.15 = (bf16[4,4,1792]{2,1,0:T(4,128)(2,1)S(1)}, bf16[4,4,1792]{2,1,0:T(4,128)(2,1)S(1)}, u32[]{:S(2)}, u32[]{:S(2)}) collective-permute-start(bf16[4,4,1792]{2,1,0:T(4,128)(2,1)S(1)} %get-tuple-element.65), channel_id=1, source_target_pairs={{0,24},{4,28},{8,16},{12,20},{16,8},{20,12},{24,0},{28,4},{1,25},{... | collective-permute-start | bytes 172040 | tf_op jit(solution)/shard_map/ppermute | solution.py:30
  41.4 0.3 collective-permute-start.17
  41.7 0.3 collective-permute-start.16
  42.0 0.2 choose_page.1
  42.3 2.2 %write_pool.1.refs_10_ = bf16[20,64,1792]{2,1,0:T(8,128)(2,1)} custom-call(bf16[20,64,1792]{2,1,0:T(8,128)(2,1)S(1)} %bitcast.63, f32[4,4,4,1792]{3,2,1,0:T(4,128)S(1)} %get-tuple-element.64._), custom_call_target="tpu_custom_call" | custom-call | tf_op jit(solution)/shard_map/write_pool/pallas_call | solution.py:51
  44.5 1.1 %collective-permute-done.17 = bf16[4,4,1792]{2,1,0:T(4,128)(2,1)S(1)} collective-permute-done((bf16[4,4,1792]{2,1,0:T(4,128)(2,1)S(1)}, bf16[4,4,1792]{2,1,0:T(4,128)(2,1)S(1)}, u32[]{:S(2)}, u32[]{:S(2)}) %collective-permute-start.17) | collective-permute-done | bytes 57376 | tf_op jit(solution)/shard_map/ppermute | solution.py:30
  45.5 0.3 collective-permute-done.16
  46.0 3.7 %collective-permute-start.19 = (bf16[4,1792]{1,0:T(4,128)(2,1)S(1)}, bf16[4,1792]{1,0:T(4,128)(2,1)S(1)}, u32[]{:S(2)}, u32[]{:S(2)}) collective-permute-start(bf16[4,1792]{1,0:T(4,128)(2,1)S(1)} %get-tuple-element.80), channel_id=1, source_target_pairs={{0,3},{1,2},{2,1},{3,0},{4,7},{5,6},{6,5},{7,4},{8,11},{9,10},{10,... | collective-permute-start | bytes 43016 | tf_op jit(solution)/shard_map/ppermute | solution.py:30
  49.7 0.8 %collective-permute-start.20 = (bf16[4,1792]{1,0:T(4,128)(2,1)S(1)}, bf16[4,1792]{1,0:T(4,128)(2,1)S(1)}, u32[]{:S(2)}, u32[]{:S(2)}) collective-permute-start(bf16[4,1792]{1,0:T(4,128)(2,1)S(1)} %get-tuple-element.82), channel_id=1, source_target_pairs={{0,1},{1,0},{2,3},{3,2},{4,5},{5,4},{6,7},{7,6},{8,9},{9,8},{10,11... | collective-permute-start | bytes 43016 | tf_op jit(solution)/shard_map/ppermute | solution.py:30
  50.5 1.7 %place_page.1 = (f32[4,1792]{1,0:T(4,128)S(1)}, bf16[20,64,1792]{2,1,0:T(8,128)(2,1)}, bf16[20,64,1792]{2,1,0:T(8,128)(2,1)}) custom-call(s32[4]{0:T(128)S(1)} %copy-done.6, s32[4]{0:T(128)S(1)} %copy-done.5, s32[4,16]{1,0:T(4,128)S(1)} %copy-done.4, f32[8,128]{1,0:T(8,128)S(1)} %find_sources.1.source_ref, ...), custom_call_target="tpu_custom_call", output_to_operand_aliasing={{1}: (15, {}), {2}: (16, {})} | custom-call | tf_op jit(solution)/shard_map/place_page/pallas_call | solution.py:703
  52.1 2.2 %collective-permute-done.21 = bf16[4,1792]{1,0:T(4,128)(2,1)S(1)} collective-permute-done((bf16[4,1792]{1,0:T(4,128)(2,1)S(1)}, bf16[4,1792]{1,0:T(4,128)(2,1)S(1)}, u32[]{:S(2)}, u32[]{:S(2)}) %collective-permute-start.21) | collective-permute-done | bytes 14368 | tf_op jit(solution)/shard_map/ppermute | solution.py:30
  54.3 0.6 %fusion.6 = bf16[4,1792]{1,0:T(4,128)(2,1)} fusion(f32[4,1792]{1,0:T(4,128)S(1)} %get-tuple-element.60, bf16[4,1792]{1,0:T(4,128)(2,1)S(1)} %collective-permute-done.21, bf16[4,1792]{1,0:T(4,128)(2,1)S(1)} %collective-permute-done.20, bf16[4,1792]{1,0:T(4,128)(2,1)S(1)} %collective-permute-done.19, f32[4,4,1792]{2,1,0:T(4,128)S(1)} %fusion.2), kind=kLoop, calls=%fused_computation.12 | loop fusion | flops 57344 | bytes 114688 | tf_op jit(solution)/shard_map/convert_element_type | solution.py:807
  (48 shorter events, 0.5 us)
Async XLA Ops:
  0.6 1.6 %collective-permute-start = (bf16[4,7168]{1,0:T(4,128)(2,1)}, bf16[4,7168]{1,0:T(4,128)(2,1)S(1)}, u32[]{:S(2)}, u32[]{:S(2)}) collective-permute-start(bf16[4,7168]{1,0:T(4,128)(2,1)} %token_ref.1), channel_id=1, source_target_pairs={{0,4},{4,0},{8,12},{12,8},{16,20},{20,16},{24,28},{28,24},{1,5},{5... | collective-permute-start | bytes 172040 | tf_op jit(solution)/shard_map/ppermute | solution.py:30
  2.3 0.7 %copy-start.2 = (f32[7168]{0:T(1024)S(1)}, f32[7168]{0:T(1024)}, u32[]{:S(2)}) copy-start(f32[7168]{0:T(1024)} %param.14) | copy-start | bytes 86020
  3.0 0.7 %copy-start.3 = (f32[7168]{0:T(1024)S(1)}, f32[7168]{0:T(1024)}, u32[]{:S(2)}) copy-start(f32[7168]{0:T(1024)} %param.15) | copy-start | bytes 86020
  4.1 6.8 %collective-permute-start.3 = (bf16[2,4,1024]{2,1,0:T(4,128)(2,1)S(1)}, bf16[2,4,1024]{2,1,0:T(4,128)(2,1)S(1)}, u32[]{:S(2)}, u32[]{:S(2)}) collective-permute-start(bf16[2,4,1024]{2,1,0:T(4,128)(2,1)S(1)} %get-tuple-element.35.refs_0_), channel_id=1, source_target_pairs={{0,24},{4,28},{8,16},{12,20},{16,8},{20,12},{24,0},{28,4},{1,25},{... | collective-permute-start | bytes 49160 | tf_op jit(solution)/shard_map/ppermute | solution.py:30
  8.0 3.7 %collective-permute-start.2 = (bf16[2,4,1024]{2,1,0:T(4,128)(2,1)S(1)}, bf16[2,4,1024]{2,1,0:T(4,128)(2,1)S(1)}, u32[]{:S(2)}, u32[]{:S(2)}) collective-permute-start(bf16[2,4,1024]{2,1,0:T(4,128)(2,1)S(1)} %get-tuple-element.36.refs_1_), channel_id=1, source_target_pairs={{0,16},{4,20},{8,24},{12,28},{16,0},{20,4},{24,8},{28,12},{1,17},{... | collective-permute-start | bytes 49160 | tf_op jit(solution)/shard_map/ppermute | solution.py:30
  8.5 3.7 %collective-permute-start.1 = (bf16[2,4,1024]{2,1,0:T(4,128)(2,1)S(1)}, bf16[2,4,1024]{2,1,0:T(4,128)(2,1)S(1)}, u32[]{:S(2)}, u32[]{:S(2)}) collective-permute-start(bf16[2,4,1024]{2,1,0:T(4,128)(2,1)S(1)} %get-tuple-element.37.refs_2_), channel_id=1, source_target_pairs={{0,8},{4,12},{8,0},{12,4},{16,24},{20,28},{24,16},{28,20},{1,9},{5... | collective-permute-start | bytes 49160 | tf_op jit(solution)/shard_map/ppermute | solution.py:30
  8.6 4.3 %copy-start = (bf16[896,14,384]{2,0,1:T(8,128)(2,1)S(1)}, bf16[896,14,384]{2,0,1:T(8,128)(2,1)}, u32[]{:S(2)}) copy-start(bf16[896,14,384]{2,0,1:T(8,128)(2,1)} %param.16) | copy-start | bytes 28901380
  12.2 8.7 %collective-permute-start.8 = (bf16[2,64,1792]{2,1,0:T(8,128)(2,1)S(1)}, bf16[2,64,1792]{2,1,0:T(8,128)(2,1)S(1)}, u32[]{:S(2)}, u32[]{:S(2)}) collective-permute-start(bf16[2,64,1792]{2,1,0:T(8,128)(2,1)S(1)} %pick_page.1.refs_0_.refs_6_), channel_id=1, source_target_pairs={{0,8},{4,20},{8,0},{12,28},{16,24},{20,4},{24,16},{28,12},{1,9},{5... | collective-permute-start | bytes 1376264 | tf_op jit(solution)/shard_map/ppermute | solution.py:183
  12.9 11.9 %slice-start = ((s8[4587520]{0:T(1024)(128)(4,1)}), s8[4194304]{0:T(1024)(128)(4,1)S(1)}, s32[]{:S(2)}) async-start(s8[4587520]{0:T(1024)(128)(4,1)} %bitcast.62), calls=%async_computation | async-start | bytes 8388608
  12.9 11.9 %slice-start.2 = ((s8[4587520]{0:T(1024)(128)(4,1)}), s8[4194304]{0:T(1024)(128)(4,1)S(1)}, s32[]{:S(2)}) async-start(s8[4587520]{0:T(1024)(128)(4,1)} %bitcast.64), calls=%async_computation.2 | async-start | bytes 8388608
  12.9 7.7 %copy-start.7 = (f32[14,384]{1,0:T(8,128)S(1)}, f32[14,384]{1,0:T(8,128)}, u32[]{:S(2)}) copy-start(f32[14,384]{1,0:T(8,128)} %param.17) | copy-start | bytes 64516
  12.9 11.9 %slice-start.1 = ((s8[4587520]{0:T(1024)(128)(4,1)}), s8[393216]{0:T(1024)(128)(4,1)S(1)}, s32[]{:S(2)}) async-start(s8[4587520]{0:T(1024)(128)(4,1)} %bitcast.62), calls=%async_computation.1 | async-start | bytes 786432
  12.9 11.9 %slice-start.3 = ((s8[4587520]{0:T(1024)(128)(4,1)}), s8[393216]{0:T(1024)(128)(4,1)S(1)}, s32[]{:S(2)}) async-start(s8[4587520]{0:T(1024)(128)(4,1)} %bitcast.64), calls=%async_computation.3 | async-start | bytes 786432
  12.9 11.9 %copy-start.4 = (s32[4,16]{1,0:T(4,128)S(1)}, s32[4,16]{1,0:T(4,128)}, u32[]{:S(2)}) copy-start(s32[4,16]{1,0:T(4,128)} %table_ref.3) | copy-start | bytes 772
  12.9 11.9 %copy-start.5 = (s32[4]{0:T(128)S(1)}, s32[4]{0:T(128)}, u32[]{:S(2)}) copy-start(s32[4]{0:T(128)} %slot_ref.5) | copy-start | bytes 52
  12.9 11.9 %copy-start.6 = (s32[4]{0:T(128)S(1)}, s32[4]{0:T(128)}, u32[]{:S(2)}) copy-start(s32[4]{0:T(128)} %length_ref.3) | copy-start | bytes 52
  15.2 1.7 %collective-permute-start.4 = (f32[4,4,5504]{2,1,0:T(4,128)S(1)}, f32[4,4,5504]{2,1,0:T(4,128)S(1)}, u32[]{:S(2)}, u32[]{:S(2)}) collective-permute-start(f32[4,4,5504]{2,1,0:T(4,128)S(1)} %get-tuple-element.44), channel_id=1, source_target_pairs={{0,4},{4,0},{8,12},{12,8},{16,20},{20,16},{24,28},{28,24},{1,5},{5... | collective-permute-start | bytes 1056776 | tf_op jit(solution)/shard_map/ppermute | solution.py:30
  17.0 6.2 %collective-permute-start.5 = (bf16[4,7168]{1,0:T(4,128)(2,1)S(1)}, bf16[4,7168]{1,0:T(4,128)(2,1)S(1)}, u32[]{:S(2)}, u32[]{:S(2)}) collective-permute-start(bf16[4,7168]{1,0:T(4,128)(2,1)S(1)} %get-tuple-element.45), channel_id=1, source_target_pairs={{0,24},{4,28},{8,16},{12,20},{16,8},{20,12},{24,0},{28,4},{1,25},{... | collective-permute-start | bytes 172040 | tf_op jit(solution)/shard_map/ppermute | solution.py:30
  19.6 4.3 %collective-permute-start.6 = (bf16[4,7168]{1,0:T(4,128)(2,1)S(1)}, bf16[4,7168]{1,0:T(4,128)(2,1)S(1)}, u32[]{:S(2)}, u32[]{:S(2)}) collective-permute-start(bf16[4,7168]{1,0:T(4,128)(2,1)S(1)} %get-tuple-element.46), channel_id=1, source_target_pairs={{0,16},{4,20},{8,24},{12,28},{16,0},{20,4},{24,8},{28,12},{1,17},{... | collective-permute-start | bytes 172040 | tf_op jit(solution)/shard_map/ppermute | solution.py:30
  20.1 4.7 %collective-permute-start.7 = (bf16[4,7168]{1,0:T(4,128)(2,1)S(1)}, bf16[4,7168]{1,0:T(4,128)(2,1)S(1)}, u32[]{:S(2)}, u32[]{:S(2)}) collective-permute-start(bf16[4,7168]{1,0:T(4,128)(2,1)S(1)} %get-tuple-element.47), channel_id=1, source_target_pairs={{0,8},{4,12},{8,0},{12,4},{16,24},{20,28},{24,16},{28,20},{1,9},{5... | collective-permute-start | bytes 172040 | tf_op jit(solution)/shard_map/ppermute | solution.py:30
  21.2 14.3 %collective-permute-start.13 = (bf16[2,2,64,1792]{3,2,1,0:T(8,128)(2,1)S(1)}, bf16[2,2,64,1792]{3,2,1,0:T(8,128)(2,1)S(1)}, u32[]{:S(2)}, u32[]{:S(2)}) collective-permute-start(bf16[2,2,64,1792]{3,2,1,0:T(8,128)(2,1)S(1)} %turn_pages.1.refs_11_), channel_id=1, source_target_pairs={{0,16},{4,12},{8,24},{12,4},{16,0},{20,28},{24,8},{28,20},{1,17},{... | collective-permute-start | bytes 2752520 | tf_op jit(solution)/shard_map/ppermute | solution.py:183
  28.7 1.3 %collective-permute-start.9 = (bf16[4,32,256]{2,1,0:T(8,128)(2,1)S(1)}, bf16[4,32,256]{2,1,0:T(8,128)(2,1)S(1)}, u32[]{:S(2)}, u32[]{:S(2)}) collective-permute-start(bf16[4,32,256]{2,1,0:T(8,128)(2,1)S(1)} %get-tuple-element.51), channel_id=1, source_target_pairs={{0,4},{4,0},{8,12},{12,8},{16,20},{20,16},{24,28},{28,24},{1,5},{5... | collective-permute-start | bytes 196616 | tf_op jit(solution)/shard_map/ppermute | solution.py:30
  30.1 5.0 %collective-permute-start.10 = (bf16[32,256]{1,0:T(8,128)(2,1)S(1)}, bf16[32,256]{1,0:T(8,128)(2,1)S(1)}, u32[]{:S(2)}, u32[]{:S(2)}) collective-permute-start(bf16[32,256]{1,0:T(8,128)(2,1)S(1)} %pad_maximum_fusion), channel_id=1, source_target_pairs={{0,24},{4,28},{8,16},{12,20},{16,8},{20,12},{24,0},{28,4},{1,25},{... | collective-permute-start | bytes 49160 | tf_op jit(solution)/shard_map/ppermute | solution.py:30
  31.2 4.2 %collective-permute-start.11 = (bf16[32,256]{1,0:T(8,128)(2,1)S(1)}, bf16[32,256]{1,0:T(8,128)(2,1)S(1)}, u32[]{:S(2)}, u32[]{:S(2)}) collective-permute-start(bf16[32,256]{1,0:T(8,128)(2,1)S(1)} %pad_maximum_fusion.1), channel_id=1, source_target_pairs={{0,16},{4,20},{8,24},{12,28},{16,0},{20,4},{24,8},{28,12},{1,17},{... | collective-permute-start | bytes 49160 | tf_op jit(solution)/shard_map/ppermute | solution.py:30
  31.8 3.8 %collective-permute-start.12 = (bf16[32,256]{1,0:T(8,128)(2,1)S(1)}, bf16[32,256]{1,0:T(8,128)(2,1)S(1)}, u32[]{:S(2)}, u32[]{:S(2)}) collective-permute-start(bf16[32,256]{1,0:T(8,128)(2,1)S(1)} %pad_maximum_fusion.2), channel_id=1, source_target_pairs={{0,8},{4,12},{8,0},{12,4},{16,24},{20,28},{24,16},{28,20},{1,9},{5... | collective-permute-start | bytes 49160 | tf_op jit(solution)/shard_map/ppermute | solution.py:30
  36.6 1.6 %collective-permute-start.14 = (bf16[4,4,4,1792]{3,2,1,0:T(4,128)(2,1)S(1)}, bf16[4,4,4,1792]{3,2,1,0:T(4,128)(2,1)S(1)}, u32[]{:S(2)}, u32[]{:S(2)}) collective-permute-start(bf16[4,4,4,1792]{3,2,1,0:T(4,128)(2,1)S(1)} %get-tuple-element.54), channel_id=1, source_target_pairs={{0,4},{4,0},{8,12},{12,8},{16,20},{20,16},{24,28},{28,24},{1,5},{5... | collective-permute-start | bytes 688136 | tf_op jit(solution)/shard_map/ppermute | solution.py:30
  38.4 6.1 %collective-permute-start.15 = (bf16[4,4,1792]{2,1,0:T(4,128)(2,1)S(1)}, bf16[4,4,1792]{2,1,0:T(4,128)(2,1)S(1)}, u32[]{:S(2)}, u32[]{:S(2)}) collective-permute-start(bf16[4,4,1792]{2,1,0:T(4,128)(2,1)S(1)} %get-tuple-element.65), channel_id=1, source_target_pairs={{0,24},{4,28},{8,16},{12,20},{16,8},{20,12},{24,0},{28,4},{1,25},{... | collective-permute-start | bytes 172040 | tf_op jit(solution)/shard_map/ppermute | solution.py:30
  41.4 4.2 %collective-permute-start.17 = (bf16[4,4,1792]{2,1,0:T(4,128)(2,1)S(1)}, bf16[4,4,1792]{2,1,0:T(4,128)(2,1)S(1)}, u32[]{:S(2)}, u32[]{:S(2)}) collective-permute-start(bf16[4,4,1792]{2,1,0:T(4,128)(2,1)S(1)} %get-tuple-element.66), channel_id=1, source_target_pairs={{0,8},{4,12},{8,0},{12,4},{16,24},{20,28},{24,16},{28,20},{1,9},{5... | collective-permute-start | bytes 172040 | tf_op jit(solution)/shard_map/ppermute | solution.py:30
  41.7 4.2 %collective-permute-start.16 = (bf16[4,4,1792]{2,1,0:T(4,128)(2,1)S(1)}, bf16[4,4,1792]{2,1,0:T(4,128)(2,1)S(1)}, u32[]{:S(2)}, u32[]{:S(2)}) collective-permute-start(bf16[4,4,1792]{2,1,0:T(4,128)(2,1)S(1)} %get-tuple-element.67), channel_id=1, source_target_pairs={{0,16},{4,20},{8,24},{12,28},{16,0},{20,4},{24,8},{28,12},{1,17},{... | collective-permute-start | bytes 172040 | tf_op jit(solution)/shard_map/ppermute | solution.py:30
  42.2 3.8 %collective-permute-start.18 = (bf16[2,64,1792]{2,1,0:T(8,128)(2,1)S(1)}, bf16[2,64,1792]{2,1,0:T(8,128)(2,1)S(1)}, u32[]{:S(2)}, u32[]{:S(2)}) collective-permute-start(bf16[2,64,1792]{2,1,0:T(8,128)(2,1)S(1)} %choose_page.1), channel_id=1, source_target_pairs={{0,4},{4,0},{8,12},{12,8},{16,20},{20,16},{24,28},{28,24},{1,5},{5... | collective-permute-start | bytes 1376264 | tf_op jit(solution)/shard_map/ppermute | solution.py:30
  42.3 8.2 %copy-start.1 = (f32[7168]{0:T(1024)S(1)}, f32[7168]{0:T(1024)}, u32[]{:S(2)}) copy-start(f32[7168]{0:T(1024)} %param.19) | copy-start | bytes 86020
  46.0 6.1 %collective-permute-start.19 = (bf16[4,1792]{1,0:T(4,128)(2,1)S(1)}, bf16[4,1792]{1,0:T(4,128)(2,1)S(1)}, u32[]{:S(2)}, u32[]{:S(2)}) collective-permute-start(bf16[4,1792]{1,0:T(4,128)(2,1)S(1)} %get-tuple-element.80), channel_id=1, source_target_pairs={{0,3},{1,2},{2,1},{3,0},{4,7},{5,6},{6,5},{7,4},{8,11},{9,10},{10,... | collective-permute-start | bytes 43016 | tf_op jit(solution)/shard_map/ppermute | solution.py:30
  49.7 4.6 %collective-permute-start.21 = (bf16[4,1792]{1,0:T(4,128)(2,1)S(1)}, bf16[4,1792]{1,0:T(4,128)(2,1)S(1)}, u32[]{:S(2)}, u32[]{:S(2)}) collective-permute-start(bf16[4,1792]{1,0:T(4,128)(2,1)S(1)} %get-tuple-element.81), channel_id=1, source_target_pairs={{0,2},{1,3},{2,0},{3,1},{4,6},{5,7},{6,4},{7,5},{8,10},{9,11},{10,... | collective-permute-start | bytes 43016 | tf_op jit(solution)/shard_map/ppermute | solution.py:30
  49.7 4.6 %collective-permute-start.20 = (bf16[4,1792]{1,0:T(4,128)(2,1)S(1)}, bf16[4,1792]{1,0:T(4,128)(2,1)S(1)}, u32[]{:S(2)}, u32[]{:S(2)}) collective-permute-start(bf16[4,1792]{1,0:T(4,128)(2,1)S(1)} %get-tuple-element.82), channel_id=1, source_target_pairs={{0,1},{1,0},{2,3},{3,2},{4,5},{5,4},{6,7},{7,6},{8,9},{9,8},{10,11... | collective-permute-start | bytes 43016 | tf_op jit(solution)/shard_map/ppermute | solution.py:30

commit v14 on v13

--- a/solution.py
+++ b/solution.py
@@ -67,10 +67,10 @@
     return leaving
 
 
-def tell(lengths, new_slot, new_page, tokens, page):
+def tell(lengths, new_slot, new_page, tokens, gain, shift, page):
     slots = new_slot.shape[0]
 
-    def kernel(length_ref, slot_ref, page_ref, token_ref, told_ref, token_out):
+    def kernel(length_ref, slot_ref, page_ref, token_ref, gain_ref, shift_ref, told_ref, token_out, gain_out, shift_out):
         row = lax.broadcasted_iota(jnp.int32, (slots, META), 0)
         lane = lax.broadcasted_iota(jnp.int32, (slots, META), 1)
         told = jnp.zeros((slots, META), F32)
@@ -81,19 +81,23 @@
                 told = jnp.where((row == s) & (lane == j), number.astype(F32), told)
         told_ref[...] = told
         token_out[...] = token_ref[...]
+        gain_out[...] = gain_ref[...]
+        shift_out[...] = shift_ref[...]
 
     return pl.pallas_call(
         kernel,
         out_shape=(
             jax.ShapeDtypeStruct((slots, META), F32),
             jax.ShapeDtypeStruct(tokens.shape, tokens.dtype),
+            jax.ShapeDtypeStruct(gain.shape, gain.dtype),
+            jax.ShapeDtypeStruct(shift.shape, shift.dtype),
         ),
-        in_specs=[SMEM] * 3 + [VMEM],
-        out_specs=(VMEM, VMEM),
+        in_specs=[SMEM] * 3 + [VMEM] * 3,
+        out_specs=(VMEM,) * 4,
         compiler_params=pltpu.CompilerParams(vmem_limit_bytes=2 * MIB),
         cost_estimate=cost(0, 0),
         name="tell",
-    )(*in_hbm(lengths, new_slot, new_page, tokens))
+    )(*in_hbm(lengths, new_slot, new_page, tokens, gain, shift))
 
 
 def pick_page(new_slot, page_table, key_pool, value_pool, *after):
@@ -740,8 +744,10 @@
     chips = groups // 2
 
     other_tokens = swap(tokens, "req", 1)
-    told, own_tokens = tell(lengths, new_slot, new_page, tokens, key_pool.shape[1])
-    blocks = prepare(own_tokens, other_tokens, norm_gain[None], norm_shift[None], told)
+    told, own_tokens, gain, shift = tell(
+        lengths, new_slot, new_page, tokens, norm_gain[None], norm_shift[None], key_pool.shape[1]
+    )
+    blocks = prepare(own_tokens, other_tokens, gain, shift, told)
     across = row_length(chips)
     spread = [blocks[0]] + [swap(blocks[d], "req", 2 * d) for d in range(1, chips)]
     page = pick_page(new_slot, page_table, key_pool, value_pool, *blocks[::-1])

time: 55.2 us -> 53.6 us (0.971)
  local copies, waits for them, and re-layouts: 1.66 us -> 0.17 us
    unnamed x25 -> x21, local copies, waits for them, and re-layouts: 1.57 us -> 0.07 us
  transfers between devices with their start and end apart: 22 -> 22, of which waited for: 14 -> 14; matrix products, arithmetic and copies ran while one was open for 0% -> 0% of each run, Pallas kernels for 25% -> 26%
where the time goes in v14:
time: 53.6 us; the launch traced here: 53.4 us
  starting transfers between devices  23.2 us (43%)
  Pallas kernels  15.3 us (29%)
  waiting for transfers between devices  12.9 us (24%)
  between operations  0.97 us (2%)
  other arithmetic  0.91 us (2%)
    ppermute x20, starting transfers between devices, swap(): return lax.ppermute(value, axis, [(i, i ^ step) for i in range(size)])  20.5 us
    ppermute x20, waiting for transfers between devices, swap(): return lax.ppermute(value, axis, [(i, i ^ step) for i in range(size)])  12.9 us
    pallas_call x1, Pallas kernels, attend(): pl.pallas_call(kernel, out_shape=(packed, packed, jax.ShapeDtypeStruct((2...  3.83 us
    ppermute x2, starting transfers between devices, swap_pages(): lax.ppermute(value, 'req', [(i, i ^ steps[i]) for i in range(2 * chips)])  2.65 us
    pallas_call x1, Pallas kernels, project(): pl.pallas_call(kernel, out_shape=(shape, wider, jax.ShapeDtypeStruct(late...  2.28 us
    pallas_call x1, Pallas kernels, pick_page(): pl.pallas_call(kernel, out_shape=jax.ShapeDtypeStruct((2,) + key_pool.sha...  2.28 us
    pallas_call x1, Pallas kernels, write_pool(): pl.pallas_call(kernel, out_shape=jax.ShapeDtypeStruct(pool.shape, pool.dt...  2.17 us
    pallas_call x1, Pallas kernels, place_page(): pl.pallas_call(kernel, out_shape=(jax.ShapeDtypeStruct((slots, width), F3...  1.65 us
  transfers between devices with their start and end apart: 22, of which 14 were waited for; matrix products, arithmetic and copies ran while one was open for 0% of the time, Pallas kernels for 26%

profile of v14, /device:TPU:0, one launch (start us, length us, event | category | flops | bytes accessed | tf_op | source)
XLA Modules:
  0.0 53.4 jit_solution(16378624900402831818)
XLA Ops:
  0.6 0.5 collective-permute-start
  1.1 0.9 %tell.1 = (f32[4,128]{1,0:T(4,128)S(1)}, bf16[4,7168]{1,0:T(4,128)(2,1)S(1)}, f32[1,7168]{1,0:T(1,128)S(1)}, f32[1,7168]{1,0:T(1,128)S(1)}) custom-call(s32[4]{0:T(128)} %length_ref.3, s32[4]{0:T(128)} %slot_ref.5, s32[4]{0:T(128)} %page_ref.1, bf16[4,7168]{1,0:T(4,128)(2,1)} %token_ref.1, f32[1,7168]{1,0:T(1,128)} %bitcast.70, f32[1,7168]{1,0:T(1,128)} %bitcast.71), custom_call_target="tpu_custom_call" | custom-call | tf_op jit(solution)/shard_map/tell/pallas_call | solution.py:87
  2.0 0.2 collective-permute-done.other_ref
  2.3 0.4 prepare.1
  2.6 3.9 %collective-permute-start.3 = (bf16[2,4,1024]{2,1,0:T(4,128)(2,1)S(1)}, bf16[2,4,1024]{2,1,0:T(4,128)(2,1)S(1)}, u32[]{:S(2)}, u32[]{:S(2)}) collective-permute-start(bf16[2,4,1024]{2,1,0:T(4,128)(2,1)S(1)} %get-tuple-element.39.refs_0_), channel_id=1, source_target_pairs={{0,24},{4,28},{8,16},{12,20},{16,8},{20,12},{24,0},{28,4},{1,25},{... | collective-permute-start | bytes 49160 | tf_op jit(solution)/shard_map/ppermute | solution.py:30
  6.5 0.5 collective-permute-start.2
  7.0 0.1 collective-permute-start.1
  7.1 2.3 %pick_page.1.refs_0_.refs_6_ = bf16[2,64,1792]{2,1,0:T(8,128)(2,1)S(1)} custom-call(s32[4]{0:T(128)} %slot_ref.5, s32[4,16]{1,0:T(4,128)} %table_ref.3, bf16[20,64,1792]{2,1,0:T(8,128)(2,1)} %pool_ref.1, bf16[20,64,1792]{2,1,0:T(8,128)(2,1)} %refs_10_.1, bf16[2,4,1024]{2,1,0:T(4,128)(2,1)S(1)} %get-tuple-element.39.refs_0_, ...), custom_call_target="tpu_custom_call" | custom-call | tf_op jit(solution)/shard_map/pick_page/pallas_call | solution.py:118
  9.4 0.8 %collective-permute-done.2.refs_1_ = bf16[2,4,1024]{2,1,0:T(4,128)(2,1)S(1)} collective-permute-done((bf16[2,4,1024]{2,1,0:T(4,128)(2,1)S(1)}, bf16[2,4,1024]{2,1,0:T(4,128)(2,1)S(1)}, u32[]{:S(2)}, u32[]{:S(2)}) %collective-permute-start.2) | collective-permute-done | bytes 16416 | tf_op jit(solution)/shard_map/ppermute | solution.py:30
  10.2 0.5 collective-permute-done.1.refs_2_
  10.7 0.7 %collective-permute-start.8 = (bf16[2,64,1792]{2,1,0:T(8,128)(2,1)S(1)}, bf16[2,64,1792]{2,1,0:T(8,128)(2,1)S(1)}, u32[]{:S(2)}, u32[]{:S(2)}) collective-permute-start(bf16[2,64,1792]{2,1,0:T(8,128)(2,1)S(1)} %pick_page.1.refs_0_.refs_6_), channel_id=1, source_target_pairs={{0,8},{4,20},{8,0},{12,28},{16,24},{20,4},{24,16},{28,12},{1,9},{5... | collective-permute-start | bytes 1376264 | tf_op jit(solution)/shard_map/ppermute | solution.py:187
  11.5 2.3 %project.1 = (f32[4,4,5376]{2,1,0:T(4,128)S(1)}, f32[4,4,5504]{2,1,0:T(4,128)S(1)}, bf16[224,7168]{1,0:T(8,128)(2,1)S(1)}) custom-call(bf16[2,4,1024]{2,1,0:T(4,128)(2,1)S(1)} %collective-permute-done.3.refs_0_, bf16[2,4,1024]{2,1,0:T(4,128)(2,1)S(1)} %collective-permute-done.2.refs_1_, bf16[2,4,1024]{2,1,0:T(4,128)(2,1)S(1)} %collective-permute-done.1.refs_2_, ...), custom_call_target="tpu_custom_call" | custom-call | tf_op jit(solution)/shard_map/project/pallas_call | solution.py:335
  13.7 0.1 collective-permute-start.4
  13.8 1.7 %collective-permute-done.4.got_ref.refs_4_ = f32[4,4,5504]{2,1,0:T(4,128)S(1)} collective-permute-done((f32[4,4,5504]{2,1,0:T(4,128)S(1)}, f32[4,4,5504]{2,1,0:T(4,128)S(1)}, u32[]{:S(2)}, u32[]{:S(2)}) %collective-permute-start.4) | collective-permute-done | bytes 352288 | tf_op jit(solution)/shard_map/ppermute | solution.py:30
  15.5 2.6 %collective-permute-start.5 = (bf16[4,7168]{1,0:T(4,128)(2,1)S(1)}, bf16[4,7168]{1,0:T(4,128)(2,1)S(1)}, u32[]{:S(2)}, u32[]{:S(2)}) collective-permute-start(bf16[4,7168]{1,0:T(4,128)(2,1)S(1)} %get-tuple-element.49), channel_id=1, source_target_pairs={{0,24},{4,28},{8,16},{12,20},{16,8},{20,12},{24,0},{28,4},{1,25},{... | collective-permute-start | bytes 172040 | tf_op jit(solution)/shard_map/ppermute | solution.py:30
  18.1 0.5 collective-permute-start.6
  18.6 0.5 collective-permute-start.7
  19.1 0.3 find_sources.1.source_ref
  19.4 0.3 turn_pages.1.refs_11_
  19.8 2.0 %collective-permute-start.13 = (bf16[2,2,64,1792]{3,2,1,0:T(8,128)(2,1)S(1)}, bf16[2,2,64,1792]{3,2,1,0:T(8,128)(2,1)S(1)}, u32[]{:S(2)}, u32[]{:S(2)}) collective-permute-start(bf16[2,2,64,1792]{3,2,1,0:T(8,128)(2,1)S(1)} %turn_pages.1.refs_11_), channel_id=1, source_target_pairs={{0,16},{4,12},{8,24},{12,4},{16,0},{20,28},{24,8},{28,20},{1,17},{... | collective-permute-start | bytes 2752520 | tf_op jit(solution)/shard_map/ppermute | solution.py:187
  21.7 0.7 %collective-permute-done.6.refs_4_ = bf16[4,7168]{1,0:T(4,128)(2,1)S(1)} collective-permute-done((bf16[4,7168]{1,0:T(4,128)(2,1)S(1)}, bf16[4,7168]{1,0:T(4,128)(2,1)S(1)}, u32[]{:S(2)}, u32[]{:S(2)}) %collective-permute-start.6) | collective-permute-done | bytes 57376 | tf_op jit(solution)/shard_map/ppermute | solution.py:30
  22.4 0.9 %collective-permute-done.7.refs_5_ = bf16[4,7168]{1,0:T(4,128)(2,1)S(1)} collective-permute-done((bf16[4,7168]{1,0:T(4,128)(2,1)S(1)}, bf16[4,7168]{1,0:T(4,128)(2,1)S(1)}, u32[]{:S(2)}, u32[]{:S(2)}) %collective-permute-start.7) | collective-permute-done | bytes 57376 | tf_op jit(solution)/shard_map/ppermute | solution.py:30
  23.4 3.8 %attend.1 = (bf16[4,32,256]{2,1,0:T(8,128)(2,1)S(1)}, bf16[4,32,256]{2,1,0:T(8,128)(2,1)S(1)}, bf16[2,4,16,1792]{3,2,1,0:T(8,128)(2,1)S(1)}, bf16[20,64,1792]{2,1,0:T(8,128)(2,1)}) custom-call(s32[4]{0:T(128)S(1)} %copy-done.4, s32[4]{0:T(128)S(1)} %copy-done.3, s32[4,16]{1,0:T(4,128)S(1)} %copy-done.2, bf16[4,7168]{1,0:T(4,128)(2,1)S(1)} %collective-permute-done.5.refs_3_, ...), custom_call_target="tpu_custom_call" | custom-call | tf_op jit(solution)/shard_map/attend/pallas_call | solution.py:553
  27.2 0.1 collective-permute-start.9
  27.3 1.2 %collective-permute-done.9 = bf16[4,32,256]{2,1,0:T(8,128)(2,1)S(1)} collective-permute-done((bf16[4,32,256]{2,1,0:T(8,128)(2,1)S(1)}, bf16[4,32,256]{2,1,0:T(8,128)(2,1)S(1)}, u32[]{:S(2)}, u32[]{:S(2)}) %collective-permute-start.9) | collective-permute-done | bytes 65568 | tf_op jit(solution)/shard_map/ppermute | solution.py:30
  28.6 1.2 %collective-permute-start.10 = (bf16[32,256]{1,0:T(8,128)(2,1)S(1)}, bf16[32,256]{1,0:T(8,128)(2,1)S(1)}, u32[]{:S(2)}, u32[]{:S(2)}) collective-permute-start(bf16[32,256]{1,0:T(8,128)(2,1)S(1)} %pad_maximum_fusion), channel_id=1, source_target_pairs={{0,24},{4,28},{8,16},{12,20},{16,8},{20,12},{24,0},{28,4},{1,25},{... | collective-permute-start | bytes 49160 | tf_op jit(solution)/shard_map/ppermute | solution.py:30
  29.8 0.4 collective-permute-start.11
  30.2 2.1 %collective-permute-start.12 = (bf16[32,256]{1,0:T(8,128)(2,1)S(1)}, bf16[32,256]{1,0:T(8,128)(2,1)S(1)}, u32[]{:S(2)}, u32[]{:S(2)}) collective-permute-start(bf16[32,256]{1,0:T(8,128)(2,1)S(1)} %pad_maximum_fusion.2), channel_id=1, source_target_pairs={{0,8},{4,12},{8,0},{12,4},{16,24},{20,28},{24,16},{28,20},{1,9},{5... | collective-permute-start | bytes 49160 | tf_op jit(solution)/shard_map/ppermute | solution.py:30
  32.3 1.3 %collective-permute-done.10.refs_0_ = bf16[32,256]{1,0:T(8,128)(2,1)S(1)} collective-permute-done((bf16[32,256]{1,0:T(8,128)(2,1)S(1)}, bf16[32,256]{1,0:T(8,128)(2,1)S(1)}, u32[]{:S(2)}, u32[]{:S(2)}) %collective-permute-start.10) | collective-permute-done | bytes 16416 | tf_op jit(solution)/shard_map/ppermute | solution.py:30
  33.6 0.3 collective-permute-done.11.refs_1_
  33.9 0.1 collective-permute-done.12.refs_2_
  34.0 1.0 %out_project.1 = (f32[4,4,4,1792]{3,2,1,0:T(4,128)S(1)}, bf16[4,4,4,1792]{3,2,1,0:T(4,128)(2,1)S(1)}) custom-call(bf16[32,256]{1,0:T(8,128)(2,1)S(1)} %collective-permute-done.10.refs_0_, bf16[32,256]{1,0:T(8,128)(2,1)S(1)} %collective-permute-done.11.refs_1_, bf16[32,256]{1,0:T(8,128)(2,1)S(1)} %collective-permute-done.12.refs_2_, ...), custom_call_target="tpu_custom_call" | custom-call | tf_op jit(solution)/shard_map/out_project/pallas_call | solution.py:611
  35.0 0.1 collective-permute-start.14
  35.1 1.5 %collective-permute-done.14 = bf16[4,4,4,1792]{3,2,1,0:T(4,128)(2,1)S(1)} collective-permute-done((bf16[4,4,4,1792]{3,2,1,0:T(4,128)(2,1)S(1)}, bf16[4,4,4,1792]{3,2,1,0:T(4,128)(2,1)S(1)}, u32[]{:S(2)}, u32[]{:S(2)}) %collective-permute-start.14) | collective-permute-done | bytes 229408 | tf_op jit(solution)/shard_map/ppermute | solution.py:30
  36.6 0.2 fusion.11
  36.8 2.5 %collective-permute-start.15 = (bf16[4,4,1792]{2,1,0:T(4,128)(2,1)S(1)}, bf16[4,4,1792]{2,1,0:T(4,128)(2,1)S(1)}, u32[]{:S(2)}, u32[]{:S(2)}) collective-permute-start(bf16[4,4,1792]{2,1,0:T(4,128)(2,1)S(1)} %get-tuple-element.69), channel_id=1, source_target_pairs={{0,24},{4,28},{8,16},{12,20},{16,8},{20,12},{24,0},{28,4},{1,25},{... | collective-permute-start | bytes 172040 | tf_op jit(solution)/shard_map/ppermute | solution.py:30
  39.3 0.9 %collective-permute-start.17 = (bf16[4,4,1792]{2,1,0:T(4,128)(2,1)S(1)}, bf16[4,4,1792]{2,1,0:T(4,128)(2,1)S(1)}, u32[]{:S(2)}, u32[]{:S(2)}) collective-permute-start(bf16[4,4,1792]{2,1,0:T(4,128)(2,1)S(1)} %get-tuple-element.70), channel_id=1, source_target_pairs={{0,8},{4,12},{8,0},{12,4},{16,24},{20,28},{24,16},{28,20},{1,9},{5... | collective-permute-start | bytes 172040 | tf_op jit(solution)/shard_map/ppermute | solution.py:30
  40.2 0.2 collective-permute-start.16
  40.4 0.2 choose_page.1
  40.6 0.1 collective-permute-start.18
  40.7 2.2 %write_pool.1.refs_10_ = bf16[20,64,1792]{2,1,0:T(8,128)(2,1)} custom-call(bf16[20,64,1792]{2,1,0:T(8,128)(2,1)S(1)} %bitcast.63, f32[4,4,4,1792]{3,2,1,0:T(4,128)S(1)} %get-tuple-element.68._), custom_call_target="tpu_custom_call" | custom-call | tf_op jit(solution)/shard_map/write_pool/pallas_call | solution.py:51
  42.9 0.7 %collective-permute-done.17 = bf16[4,4,1792]{2,1,0:T(4,128)(2,1)S(1)} collective-permute-done((bf16[4,4,1792]{2,1,0:T(4,128)(2,1)S(1)}, bf16[4,4,1792]{2,1,0:T(4,128)(2,1)S(1)}, u32[]{:S(2)}, u32[]{:S(2)}) %collective-permute-start.17) | collective-permute-done | bytes 57376 | tf_op jit(solution)/shard_map/ppermute | solution.py:30
  43.6 0.8 %collective-permute-done.16 = bf16[4,4,1792]{2,1,0:T(4,128)(2,1)S(1)} collective-permute-done((bf16[4,4,1792]{2,1,0:T(4,128)(2,1)S(1)}, bf16[4,4,1792]{2,1,0:T(4,128)(2,1)S(1)}, u32[]{:S(2)}, u32[]{:S(2)}) %collective-permute-start.16) | collective-permute-done | bytes 57376 | tf_op jit(solution)/shard_map/ppermute | solution.py:30
  44.5 3.7 %collective-permute-start.19 = (bf16[4,1792]{1,0:T(4,128)(2,1)S(1)}, bf16[4,1792]{1,0:T(4,128)(2,1)S(1)}, u32[]{:S(2)}, u32[]{:S(2)}) collective-permute-start(bf16[4,1792]{1,0:T(4,128)(2,1)S(1)} %get-tuple-element.84), channel_id=1, source_target_pairs={{0,3},{1,2},{2,1},{3,0},{4,7},{5,6},{6,5},{7,4},{8,11},{9,10},{10,... | collective-permute-start | bytes 43016 | tf_op jit(solution)/shard_map/ppermute | solution.py:30
  48.2 0.8 %collective-permute-start.20 = (bf16[4,1792]{1,0:T(4,128)(2,1)S(1)}, bf16[4,1792]{1,0:T(4,128)(2,1)S(1)}, u32[]{:S(2)}, u32[]{:S(2)}) collective-permute-start(bf16[4,1792]{1,0:T(4,128)(2,1)S(1)} %get-tuple-element.86), channel_id=1, source_target_pairs={{0,1},{1,0},{2,3},{3,2},{4,5},{5,4},{6,7},{7,6},{8,9},{9,8},{10,11... | collective-permute-start | bytes 43016 | tf_op jit(solution)/shard_map/ppermute | solution.py:30
  49.0 1.7 %place_page.1 = (f32[4,1792]{1,0:T(4,128)S(1)}, bf16[20,64,1792]{2,1,0:T(8,128)(2,1)}, bf16[20,64,1792]{2,1,0:T(8,128)(2,1)}) custom-call(s32[4]{0:T(128)S(1)} %copy-done.4, s32[4]{0:T(128)S(1)} %copy-done.3, s32[4,16]{1,0:T(4,128)S(1)} %copy-done.2, f32[8,128]{1,0:T(8,128)S(1)} %find_sources.1.source_ref, ...), custom_call_target="tpu_custom_call", output_to_operand_aliasing={{1}: (15, {}), {2}: (16, {})} | custom-call | tf_op jit(solution)/shard_map/place_page/pallas_call | solution.py:707
  50.6 2.2 %collective-permute-done.21 = bf16[4,1792]{1,0:T(4,128)(2,1)S(1)} collective-permute-done((bf16[4,1792]{1,0:T(4,128)(2,1)S(1)}, bf16[4,1792]{1,0:T(4,128)(2,1)S(1)}, u32[]{:S(2)}, u32[]{:S(2)}) %collective-permute-start.21) | collective-permute-done | bytes 14368 | tf_op jit(solution)/shard_map/ppermute | solution.py:30
  52.8 0.6 %fusion.6 = bf16[4,1792]{1,0:T(4,128)(2,1)} fusion(f32[4,1792]{1,0:T(4,128)S(1)} %get-tuple-element.64, bf16[4,1792]{1,0:T(4,128)(2,1)S(1)} %collective-permute-done.21, bf16[4,1792]{1,0:T(4,128)(2,1)S(1)} %collective-permute-done.20, bf16[4,1792]{1,0:T(4,128)(2,1)S(1)} %collective-permute-done.19, f32[4,4,1792]{2,1,0:T(4,128)S(1)} %fusion.2), kind=kLoop, calls=%fused_computation.12 | loop fusion | flops 57344 | bytes 114688 | tf_op jit(solution)/shard_map/convert_element_type | solution.py:813
  (44 shorter events, 0.4 us)
Async XLA Ops:
  0.6 1.6 %collective-permute-start = (bf16[4,7168]{1,0:T(4,128)(2,1)}, bf16[4,7168]{1,0:T(4,128)(2,1)S(1)}, u32[]{:S(2)}, u32[]{:S(2)}) collective-permute-start(bf16[4,7168]{1,0:T(4,128)(2,1)} %token_ref.1), channel_id=1, source_target_pairs={{0,4},{4,0},{8,12},{12,8},{16,20},{20,16},{24,28},{28,24},{1,5},{5... | collective-permute-start | bytes 172040 | tf_op jit(solution)/shard_map/ppermute | solution.py:30
  2.6 6.8 %collective-permute-start.3 = (bf16[2,4,1024]{2,1,0:T(4,128)(2,1)S(1)}, bf16[2,4,1024]{2,1,0:T(4,128)(2,1)S(1)}, u32[]{:S(2)}, u32[]{:S(2)}) collective-permute-start(bf16[2,4,1024]{2,1,0:T(4,128)(2,1)S(1)} %get-tuple-element.39.refs_0_), channel_id=1, source_target_pairs={{0,24},{4,28},{8,16},{12,20},{16,8},{20,12},{24,0},{28,4},{1,25},{... | collective-permute-start | bytes 49160 | tf_op jit(solution)/shard_map/ppermute | solution.py:30
  6.5 3.7 %collective-permute-start.2 = (bf16[2,4,1024]{2,1,0:T(4,128)(2,1)S(1)}, bf16[2,4,1024]{2,1,0:T(4,128)(2,1)S(1)}, u32[]{:S(2)}, u32[]{:S(2)}) collective-permute-start(bf16[2,4,1024]{2,1,0:T(4,128)(2,1)S(1)} %get-tuple-element.40.refs_1_), channel_id=1, source_target_pairs={{0,16},{4,20},{8,24},{12,28},{16,0},{20,4},{24,8},{28,12},{1,17},{... | collective-permute-start | bytes 49160 | tf_op jit(solution)/shard_map/ppermute | solution.py:30
  7.0 3.7 %collective-permute-start.1 = (bf16[2,4,1024]{2,1,0:T(4,128)(2,1)S(1)}, bf16[2,4,1024]{2,1,0:T(4,128)(2,1)S(1)}, u32[]{:S(2)}, u32[]{:S(2)}) collective-permute-start(bf16[2,4,1024]{2,1,0:T(4,128)(2,1)S(1)} %get-tuple-element.41.refs_2_), channel_id=1, source_target_pairs={{0,8},{4,12},{8,0},{12,4},{16,24},{20,28},{24,16},{28,20},{1,9},{5... | collective-permute-start | bytes 49160 | tf_op jit(solution)/shard_map/ppermute | solution.py:30
  7.1 4.3 %copy-start = (bf16[896,14,384]{2,0,1:T(8,128)(2,1)S(1)}, bf16[896,14,384]{2,0,1:T(8,128)(2,1)}, u32[]{:S(2)}) copy-start(bf16[896,14,384]{2,0,1:T(8,128)(2,1)} %param.16) | copy-start | bytes 28901380
  10.7 8.7 %collective-permute-start.8 = (bf16[2,64,1792]{2,1,0:T(8,128)(2,1)S(1)}, bf16[2,64,1792]{2,1,0:T(8,128)(2,1)S(1)}, u32[]{:S(2)}, u32[]{:S(2)}) collective-permute-start(bf16[2,64,1792]{2,1,0:T(8,128)(2,1)S(1)} %pick_page.1.refs_0_.refs_6_), channel_id=1, source_target_pairs={{0,8},{4,20},{8,0},{12,28},{16,24},{20,4},{24,16},{28,12},{1,9},{5... | collective-permute-start | bytes 1376264 | tf_op jit(solution)/shard_map/ppermute | solution.py:187
  11.4 11.9 %slice-start = ((s8[4587520]{0:T(1024)(128)(4,1)}), s8[4194304]{0:T(1024)(128)(4,1)S(1)}, s32[]{:S(2)}) async-start(s8[4587520]{0:T(1024)(128)(4,1)} %bitcast.62), calls=%async_computation | async-start | bytes 8388608
  11.4 11.9 %slice-start.2 = ((s8[4587520]{0:T(1024)(128)(4,1)}), s8[4194304]{0:T(1024)(128)(4,1)S(1)}, s32[]{:S(2)}) async-start(s8[4587520]{0:T(1024)(128)(4,1)} %bitcast.64), calls=%async_computation.2 | async-start | bytes 8388608
  11.4 7.7 %copy-start.5 = (f32[14,384]{1,0:T(8,128)S(1)}, f32[14,384]{1,0:T(8,128)}, u32[]{:S(2)}) copy-start(f32[14,384]{1,0:T(8,128)} %param.17) | copy-start | bytes 64516
  11.4 11.9 %slice-start.1 = ((s8[4587520]{0:T(1024)(128)(4,1)}), s8[393216]{0:T(1024)(128)(4,1)S(1)}, s32[]{:S(2)}) async-start(s8[4587520]{0:T(1024)(128)(4,1)} %bitcast.62), calls=%async_computation.1 | async-start | bytes 786432
  11.4 11.9 %slice-start.3 = ((s8[4587520]{0:T(1024)(128)(4,1)}), s8[393216]{0:T(1024)(128)(4,1)S(1)}, s32[]{:S(2)}) async-start(s8[4587520]{0:T(1024)(128)(4,1)} %bitcast.64), calls=%async_computation.3 | async-start | bytes 786432
  11.4 11.9 %copy-start.2 = (s32[4,16]{1,0:T(4,128)S(1)}, s32[4,16]{1,0:T(4,128)}, u32[]{:S(2)}) copy-start(s32[4,16]{1,0:T(4,128)} %table_ref.3) | copy-start | bytes 772
  11.4 11.9 %copy-start.3 = (s32[4]{0:T(128)S(1)}, s32[4]{0:T(128)}, u32[]{:S(2)}) copy-start(s32[4]{0:T(128)} %slot_ref.5) | copy-start | bytes 52
  11.4 11.9 %copy-start.4 = (s32[4]{0:T(128)S(1)}, s32[4]{0:T(128)}, u32[]{:S(2)}) copy-start(s32[4]{0:T(128)} %length_ref.3) | copy-start | bytes 52
  13.7 1.7 %collective-permute-start.4 = (f32[4,4,5504]{2,1,0:T(4,128)S(1)}, f32[4,4,5504]{2,1,0:T(4,128)S(1)}, u32[]{:S(2)}, u32[]{:S(2)}) collective-permute-start(f32[4,4,5504]{2,1,0:T(4,128)S(1)} %get-tuple-element.48), channel_id=1, source_target_pairs={{0,4},{4,0},{8,12},{12,8},{16,20},{20,16},{24,28},{28,24},{1,5},{5... | collective-permute-start | bytes 1056776 | tf_op jit(solution)/shard_map/ppermute | solution.py:30
  15.5 6.2 %collective-permute-start.5 = (bf16[4,7168]{1,0:T(4,128)(2,1)S(1)}, bf16[4,7168]{1,0:T(4,128)(2,1)S(1)}, u32[]{:S(2)}, u32[]{:S(2)}) collective-permute-start(bf16[4,7168]{1,0:T(4,128)(2,1)S(1)} %get-tuple-element.49), channel_id=1, source_target_pairs={{0,24},{4,28},{8,16},{12,20},{16,8},{20,12},{24,0},{28,4},{1,25},{... | collective-permute-start | bytes 172040 | tf_op jit(solution)/shard_map/ppermute | solution.py:30
  18.1 4.3 %collective-permute-start.6 = (bf16[4,7168]{1,0:T(4,128)(2,1)S(1)}, bf16[4,7168]{1,0:T(4,128)(2,1)S(1)}, u32[]{:S(2)}, u32[]{:S(2)}) collective-permute-start(bf16[4,7168]{1,0:T(4,128)(2,1)S(1)} %get-tuple-element.50), channel_id=1, source_target_pairs={{0,16},{4,20},{8,24},{12,28},{16,0},{20,4},{24,8},{28,12},{1,17},{... | collective-permute-start | bytes 172040 | tf_op jit(solution)/shard_map/ppermute | solution.py:30
  18.6 4.7 %collective-permute-start.7 = (bf16[4,7168]{1,0:T(4,128)(2,1)S(1)}, bf16[4,7168]{1,0:T(4,128)(2,1)S(1)}, u32[]{:S(2)}, u32[]{:S(2)}) collective-permute-start(bf16[4,7168]{1,0:T(4,128)(2,1)S(1)} %get-tuple-element.51), channel_id=1, source_target_pairs={{0,8},{4,12},{8,0},{12,4},{16,24},{20,28},{24,16},{28,20},{1,9},{5... | collective-permute-start | bytes 172040 | tf_op jit(solution)/shard_map/ppermute | solution.py:30
  19.8 14.2 %collective-permute-start.13 = (bf16[2,2,64,1792]{3,2,1,0:T(8,128)(2,1)S(1)}, bf16[2,2,64,1792]{3,2,1,0:T(8,128)(2,1)S(1)}, u32[]{:S(2)}, u32[]{:S(2)}) collective-permute-start(bf16[2,2,64,1792]{3,2,1,0:T(8,128)(2,1)S(1)} %turn_pages.1.refs_11_), channel_id=1, source_target_pairs={{0,16},{4,12},{8,24},{12,4},{16,0},{20,28},{24,8},{28,20},{1,17},{... | collective-permute-start | bytes 2752520 | tf_op jit(solution)/shard_map/ppermute | solution.py:187
  27.2 1.3 %collective-permute-start.9 = (bf16[4,32,256]{2,1,0:T(8,128)(2,1)S(1)}, bf16[4,32,256]{2,1,0:T(8,128)(2,1)S(1)}, u32[]{:S(2)}, u32[]{:S(2)}) collective-permute-start(bf16[4,32,256]{2,1,0:T(8,128)(2,1)S(1)} %get-tuple-element.55), channel_id=1, source_target_pairs={{0,4},{4,0},{8,12},{12,8},{16,20},{20,16},{24,28},{28,24},{1,5},{5... | collective-permute-start | bytes 196616 | tf_op jit(solution)/shard_map/ppermute | solution.py:30
  28.6 5.0 %collective-permute-start.10 = (bf16[32,256]{1,0:T(8,128)(2,1)S(1)}, bf16[32,256]{1,0:T(8,128)(2,1)S(1)}, u32[]{:S(2)}, u32[]{:S(2)}) collective-permute-start(bf16[32,256]{1,0:T(8,128)(2,1)S(1)} %pad_maximum_fusion), channel_id=1, source_target_pairs={{0,24},{4,28},{8,16},{12,20},{16,8},{20,12},{24,0},{28,4},{1,25},{... | collective-permute-start | bytes 49160 | tf_op jit(solution)/shard_map/ppermute | solution.py:30
  29.8 4.2 %collective-permute-start.11 = (bf16[32,256]{1,0:T(8,128)(2,1)S(1)}, bf16[32,256]{1,0:T(8,128)(2,1)S(1)}, u32[]{:S(2)}, u32[]{:S(2)}) collective-permute-start(bf16[32,256]{1,0:T(8,128)(2,1)S(1)} %pad_maximum_fusion.1), channel_id=1, source_target_pairs={{0,16},{4,20},{8,24},{12,28},{16,0},{20,4},{24,8},{28,12},{1,17},{... | collective-permute-start | bytes 49160 | tf_op jit(solution)/shard_map/ppermute | solution.py:30
  30.2 3.8 %collective-permute-start.12 = (bf16[32,256]{1,0:T(8,128)(2,1)S(1)}, bf16[32,256]{1,0:T(8,128)(2,1)S(1)}, u32[]{:S(2)}, u32[]{:S(2)}) collective-permute-start(bf16[32,256]{1,0:T(8,128)(2,1)S(1)} %pad_maximum_fusion.2), channel_id=1, source_target_pairs={{0,8},{4,12},{8,0},{12,4},{16,24},{20,28},{24,16},{28,20},{1,9},{5... | collective-permute-start | bytes 49160 | tf_op jit(solution)/shard_map/ppermute | solution.py:30
  35.0 1.6 %collective-permute-start.14 = (bf16[4,4,4,1792]{3,2,1,0:T(4,128)(2,1)S(1)}, bf16[4,4,4,1792]{3,2,1,0:T(4,128)(2,1)S(1)}, u32[]{:S(2)}, u32[]{:S(2)}) collective-permute-start(bf16[4,4,4,1792]{3,2,1,0:T(4,128)(2,1)S(1)} %get-tuple-element.58), channel_id=1, source_target_pairs={{0,4},{4,0},{8,12},{12,8},{16,20},{20,16},{24,28},{28,24},{1,5},{5... | collective-permute-start | bytes 688136 | tf_op jit(solution)/shard_map/ppermute | solution.py:30
  36.8 6.0 %collective-permute-start.15 = (bf16[4,4,1792]{2,1,0:T(4,128)(2,1)S(1)}, bf16[4,4,1792]{2,1,0:T(4,128)(2,1)S(1)}, u32[]{:S(2)}, u32[]{:S(2)}) collective-permute-start(bf16[4,4,1792]{2,1,0:T(4,128)(2,1)S(1)} %get-tuple-element.69), channel_id=1, source_target_pairs={{0,24},{4,28},{8,16},{12,20},{16,8},{20,12},{24,0},{28,4},{1,25},{... | collective-permute-start | bytes 172040 | tf_op jit(solution)/shard_map/ppermute | solution.py:30
  39.3 4.3 %collective-permute-start.17 = (bf16[4,4,1792]{2,1,0:T(4,128)(2,1)S(1)}, bf16[4,4,1792]{2,1,0:T(4,128)(2,1)S(1)}, u32[]{:S(2)}, u32[]{:S(2)}) collective-permute-start(bf16[4,4,1792]{2,1,0:T(4,128)(2,1)S(1)} %get-tuple-element.70), channel_id=1, source_target_pairs={{0,8},{4,12},{8,0},{12,4},{16,24},{20,28},{24,16},{28,20},{1,9},{5... | collective-permute-start | bytes 172040 | tf_op jit(solution)/shard_map/ppermute | solution.py:30
  40.2 4.2 %collective-permute-start.16 = (bf16[4,4,1792]{2,1,0:T(4,128)(2,1)S(1)}, bf16[4,4,1792]{2,1,0:T(4,128)(2,1)S(1)}, u32[]{:S(2)}, u32[]{:S(2)}) collective-permute-start(bf16[4,4,1792]{2,1,0:T(4,128)(2,1)S(1)} %get-tuple-element.71), channel_id=1, source_target_pairs={{0,16},{4,20},{8,24},{12,28},{16,0},{20,4},{24,8},{28,12},{1,17},{... | collective-permute-start | bytes 172040 | tf_op jit(solution)/shard_map/ppermute | solution.py:30
  40.6 3.9 %collective-permute-start.18 = (bf16[2,64,1792]{2,1,0:T(8,128)(2,1)S(1)}, bf16[2,64,1792]{2,1,0:T(8,128)(2,1)S(1)}, u32[]{:S(2)}, u32[]{:S(2)}) collective-permute-start(bf16[2,64,1792]{2,1,0:T(8,128)(2,1)S(1)} %choose_page.1), channel_id=1, source_target_pairs={{0,4},{4,0},{8,12},{12,8},{16,20},{20,16},{24,28},{28,24},{1,5},{5... | collective-permute-start | bytes 1376264 | tf_op jit(solution)/shard_map/ppermute | solution.py:30
  40.6 8.3 %copy-start.1 = (f32[7168]{0:T(1024)S(1)}, f32[7168]{0:T(1024)}, u32[]{:S(2)}) copy-start(f32[7168]{0:T(1024)} %param.19) | copy-start | bytes 86020
  44.5 6.1 %collective-permute-start.19 = (bf16[4,1792]{1,0:T(4,128)(2,1)S(1)}, bf16[4,1792]{1,0:T(4,128)(2,1)S(1)}, u32[]{:S(2)}, u32[]{:S(2)}) collective-permute-start(bf16[4,1792]{1,0:T(4,128)(2,1)S(1)} %get-tuple-element.84), channel_id=1, source_target_pairs={{0,3},{1,2},{2,1},{3,0},{4,7},{5,6},{6,5},{7,4},{8,11},{9,10},{10,... | collective-permute-start | bytes 43016 | tf_op jit(solution)/shard_map/ppermute | solution.py:30
  48.2 4.6 %collective-permute-start.21 = (bf16[4,1792]{1,0:T(4,128)(2,1)S(1)}, bf16[4,1792]{1,0:T(4,128)(2,1)S(1)}, u32[]{:S(2)}, u32[]{:S(2)}) collective-permute-start(bf16[4,1792]{1,0:T(4,128)(2,1)S(1)} %get-tuple-element.85), channel_id=1, source_target_pairs={{0,2},{1,3},{2,0},{3,1},{4,6},{5,7},{6,4},{7,5},{8,10},{9,11},{10,... | collective-permute-start | bytes 43016 | tf_op jit(solution)/shard_map/ppermute | solution.py:30
  48.2 4.6 %collective-permute-start.20 = (bf16[4,1792]{1,0:T(4,128)(2,1)S(1)}, bf16[4,1792]{1,0:T(4,128)(2,1)S(1)}, u32[]{:S(2)}, u32[]{:S(2)}) collective-permute-start(bf16[4,1792]{1,0:T(4,128)(2,1)S(1)} %get-tuple-element.86), channel_id=1, source_target_pairs={{0,1},{1,0},{2,3},{3,2},{4,5},{5,4},{6,7},{7,6},{8,9},{9,8},{10,11... | collective-permute-start | bytes 43016 | tf_op jit(solution)/shard_map/ppermute | solution.py:30

commit v15 on v14

--- a/solution.py
+++ b/solution.py
@@ -577,7 +577,7 @@
     piece = width // pieces
 
     def kernel(*refs):
-        block_refs, weight_ref = refs[:chips][::-1], refs[chips]
+        block_refs, weight_ref = refs[:chips], refs[chips]
         keep_ref, send_ref = refs[chips + 1 + len(after) :]
         gathered = jnp.concatenate(
             [block_refs[d][: 2 * slots, :].astype(F32) for d in range(chips)], axis=0
@@ -616,7 +616,7 @@
         compiler_params=pltpu.CompilerParams(vmem_limit_bytes=10 * MIB),
         cost_estimate=cost(2 * rows * weight.size, 2 * weight.size),
         name="out_project",
-    )(*blocks[::-1], weight, *after)
+    )(*blocks, weight, *after)
 
 
 def place_page(lengths, new_slot, page_table, sources, patches, packs, tokens, out_bias, messages, turned, from_other, key_out, value_out):

time: 53.6 us -> 53.6 us (level)
  Pallas kernels: 15.3 us -> 14.4 us
    pallas_call x1, Pallas kernels: 3.83 us -> 2.84 us  [attend(): pl.pallas_call(kernel, out_shape=(packed, packed, jax.ShapeDtypeStruct((2...]
  transfers between devices with their start and end apart: 22 -> 22, of which waited for: 14 -> 12; matrix products, arithmetic and copies ran while one was open for 0% -> 0% of each run, Pallas kernels for 26% -> 24%
where the time goes in v15:
time: 53.6 us; the launch traced here: 53.4 us
  starting transfers between devices  23.7 us (44%)
  Pallas kernels  14.4 us (27%)
  waiting for transfers between devices  13.3 us (25%)
  between operations  0.98 us (2%)
  other arithmetic  0.91 us (2%)
    ppermute x20, starting transfers between devices, swap(): return lax.ppermute(value, axis, [(i, i ^ step) for i in range(size)])  21 us
    ppermute x20, waiting for transfers between devices, swap(): return lax.ppermute(value, axis, [(i, i ^ step) for i in range(size)])  13.3 us
    pallas_call x1, Pallas kernels, attend(): pl.pallas_call(kernel, out_shape=(packed, packed, jax.ShapeDtypeStruct((2...  2.84 us
    ppermute x2, starting transfers between devices, swap_pages(): lax.ppermute(value, 'req', [(i, i ^ steps[i]) for i in range(2 * chips)])  2.65 us
    pallas_call x1, Pallas kernels, project(): pl.pallas_call(kernel, out_shape=(shape, wider, jax.ShapeDtypeStruct(late...  2.28 us
    pallas_call x1, Pallas kernels, pick_page(): pl.pallas_call(kernel, out_shape=jax.ShapeDtypeStruct((2,) + key_pool.sha...  2.28 us
    pallas_call x1, Pallas kernels, write_pool(): pl.pallas_call(kernel, out_shape=jax.ShapeDtypeStruct(pool.shape, pool.dt...  2.17 us
    pallas_call x1, Pallas kernels, place_page(): pl.pallas_call(kernel, out_shape=(jax.ShapeDtypeStruct((slots, width), F3...  1.68 us
  transfers between devices with their start and end apart: 22, of which 12 were waited for; matrix products, arithmetic and copies ran while one was open for 0% of the time, Pallas kernels for 24%

profile of v15, /device:TPU:0, one launch (start us, length us, event | category | flops | bytes accessed | tf_op | source)
XLA Modules:
  0.0 53.4 jit_solution(9645529674847638800)
XLA Ops:
  0.6 0.5 collective-permute-start
  1.1 0.9 %tell.1 = (f32[4,128]{1,0:T(4,128)S(1)}, bf16[4,7168]{1,0:T(4,128)(2,1)S(1)}, f32[1,7168]{1,0:T(1,128)S(1)}, f32[1,7168]{1,0:T(1,128)S(1)}) custom-call(s32[4]{0:T(128)} %length_ref.3, s32[4]{0:T(128)} %slot_ref.5, s32[4]{0:T(128)} %page_ref.1, bf16[4,7168]{1,0:T(4,128)(2,1)} %token_ref.1, f32[1,7168]{1,0:T(1,128)} %bitcast.70, f32[1,7168]{1,0:T(1,128)} %bitcast.71), custom_call_target="tpu_custom_call" | custom-call | tf_op jit(solution)/shard_map/tell/pallas_call | solution.py:87
  2.0 0.2 collective-permute-done.other_ref
  2.3 0.4 prepare.1
  2.6 3.9 %collective-permute-start.3 = (bf16[2,4,1024]{2,1,0:T(4,128)(2,1)S(1)}, bf16[2,4,1024]{2,1,0:T(4,128)(2,1)S(1)}, u32[]{:S(2)}, u32[]{:S(2)}) collective-permute-start(bf16[2,4,1024]{2,1,0:T(4,128)(2,1)S(1)} %get-tuple-element.39.refs_0_), channel_id=1, source_target_pairs={{0,24},{4,28},{8,16},{12,20},{16,8},{20,12},{24,0},{28,4},{1,25},{... | collective-permute-start | bytes 49160 | tf_op jit(solution)/shard_map/ppermute | solution.py:30
  6.5 0.5 collective-permute-start.2
  7.0 0.1 collective-permute-start.1
  7.1 2.3 %pick_page.1.refs_0_.refs_6_ = bf16[2,64,1792]{2,1,0:T(8,128)(2,1)S(1)} custom-call(s32[4]{0:T(128)} %slot_ref.5, s32[4,16]{1,0:T(4,128)} %table_ref.3, bf16[20,64,1792]{2,1,0:T(8,128)(2,1)} %pool_ref.1, bf16[20,64,1792]{2,1,0:T(8,128)(2,1)} %refs_10_.1, bf16[2,4,1024]{2,1,0:T(4,128)(2,1)S(1)} %get-tuple-element.39.refs_0_, ...), custom_call_target="tpu_custom_call" | custom-call | tf_op jit(solution)/shard_map/pick_page/pallas_call | solution.py:118
  9.4 0.8 %collective-permute-done.2.refs_1_ = bf16[2,4,1024]{2,1,0:T(4,128)(2,1)S(1)} collective-permute-done((bf16[2,4,1024]{2,1,0:T(4,128)(2,1)S(1)}, bf16[2,4,1024]{2,1,0:T(4,128)(2,1)S(1)}, u32[]{:S(2)}, u32[]{:S(2)}) %collective-permute-start.2) | collective-permute-done | bytes 16416 | tf_op jit(solution)/shard_map/ppermute | solution.py:30
  10.2 0.5 collective-permute-done.1.refs_2_
  10.7 0.7 %collective-permute-start.8 = (bf16[2,64,1792]{2,1,0:T(8,128)(2,1)S(1)}, bf16[2,64,1792]{2,1,0:T(8,128)(2,1)S(1)}, u32[]{:S(2)}, u32[]{:S(2)}) collective-permute-start(bf16[2,64,1792]{2,1,0:T(8,128)(2,1)S(1)} %pick_page.1.refs_0_.refs_6_), channel_id=1, source_target_pairs={{0,8},{4,20},{8,0},{12,28},{16,24},{20,4},{24,16},{28,12},{1,9},{5... | collective-permute-start | bytes 1376264 | tf_op jit(solution)/shard_map/ppermute | solution.py:187
  11.5 2.3 %project.1 = (f32[4,4,5376]{2,1,0:T(4,128)S(1)}, f32[4,4,5504]{2,1,0:T(4,128)S(1)}, bf16[224,7168]{1,0:T(8,128)(2,1)S(1)}) custom-call(bf16[2,4,1024]{2,1,0:T(4,128)(2,1)S(1)} %collective-permute-done.3.refs_0_, bf16[2,4,1024]{2,1,0:T(4,128)(2,1)S(1)} %collective-permute-done.2.refs_1_, bf16[2,4,1024]{2,1,0:T(4,128)(2,1)S(1)} %collective-permute-done.1.refs_2_, ...), custom_call_target="tpu_custom_call" | custom-call | tf_op jit(solution)/shard_map/project/pallas_call | solution.py:335
  13.7 0.1 collective-permute-start.4
  13.8 1.7 %collective-permute-done.4.got_ref.refs_4_ = f32[4,4,5504]{2,1,0:T(4,128)S(1)} collective-permute-done((f32[4,4,5504]{2,1,0:T(4,128)S(1)}, f32[4,4,5504]{2,1,0:T(4,128)S(1)}, u32[]{:S(2)}, u32[]{:S(2)}) %collective-permute-start.4) | collective-permute-done | bytes 352288 | tf_op jit(solution)/shard_map/ppermute | solution.py:30
  15.5 0.1 combine.1
  15.5 2.6 %collective-permute-start.5 = (bf16[4,7168]{1,0:T(4,128)(2,1)S(1)}, bf16[4,7168]{1,0:T(4,128)(2,1)S(1)}, u32[]{:S(2)}, u32[]{:S(2)}) collective-permute-start(bf16[4,7168]{1,0:T(4,128)(2,1)S(1)} %get-tuple-element.49), channel_id=1, source_target_pairs={{0,24},{4,28},{8,16},{12,20},{16,8},{20,12},{24,0},{28,4},{1,25},{... | collective-permute-start | bytes 172040 | tf_op jit(solution)/shard_map/ppermute | solution.py:30
  18.1 0.5 collective-permute-start.6
  18.6 0.5 collective-permute-start.7
  19.1 0.3 find_sources.1.source_ref
  19.4 0.3 turn_pages.1.refs_11_
  19.8 2.0 %collective-permute-start.13 = (bf16[2,2,64,1792]{3,2,1,0:T(8,128)(2,1)S(1)}, bf16[2,2,64,1792]{3,2,1,0:T(8,128)(2,1)S(1)}, u32[]{:S(2)}, u32[]{:S(2)}) collective-permute-start(bf16[2,2,64,1792]{3,2,1,0:T(8,128)(2,1)S(1)} %turn_pages.1.refs_11_), channel_id=1, source_target_pairs={{0,16},{4,12},{8,24},{12,4},{16,0},{20,28},{24,8},{28,20},{1,17},{... | collective-permute-start | bytes 2752520 | tf_op jit(solution)/shard_map/ppermute | solution.py:187
  21.7 0.7 %collective-permute-done.6.refs_4_ = bf16[4,7168]{1,0:T(4,128)(2,1)S(1)} collective-permute-done((bf16[4,7168]{1,0:T(4,128)(2,1)S(1)}, bf16[4,7168]{1,0:T(4,128)(2,1)S(1)}, u32[]{:S(2)}, u32[]{:S(2)}) %collective-permute-start.6) | collective-permute-done | bytes 57376 | tf_op jit(solution)/shard_map/ppermute | solution.py:30
  22.4 0.9 %collective-permute-done.7.refs_5_ = bf16[4,7168]{1,0:T(4,128)(2,1)S(1)} collective-permute-done((bf16[4,7168]{1,0:T(4,128)(2,1)S(1)}, bf16[4,7168]{1,0:T(4,128)(2,1)S(1)}, u32[]{:S(2)}, u32[]{:S(2)}) %collective-permute-start.7) | collective-permute-done | bytes 57376 | tf_op jit(solution)/shard_map/ppermute | solution.py:30
  23.4 2.8 %attend.1 = (bf16[4,32,256]{2,1,0:T(8,128)(2,1)S(1)}, bf16[4,32,256]{2,1,0:T(8,128)(2,1)S(1)}, bf16[2,4,16,1792]{3,2,1,0:T(8,128)(2,1)S(1)}, bf16[20,64,1792]{2,1,0:T(8,128)(2,1)}) custom-call(s32[4]{0:T(128)S(1)} %copy-done.4, s32[4]{0:T(128)S(1)} %copy-done.3, s32[4,16]{1,0:T(4,128)S(1)} %copy-done.2, bf16[4,7168]{1,0:T(4,128)(2,1)S(1)} %collective-permute-done.5.refs_3_, ...), custom_call_target="tpu_custom_call" | custom-call | tf_op jit(solution)/shard_map/attend/pallas_call | solution.py:553
  26.3 0.1 collective-permute-start.9
  26.3 1.2 %collective-permute-done.9 = bf16[4,32,256]{2,1,0:T(8,128)(2,1)S(1)} collective-permute-done((bf16[4,32,256]{2,1,0:T(8,128)(2,1)S(1)}, bf16[4,32,256]{2,1,0:T(8,128)(2,1)S(1)}, u32[]{:S(2)}, u32[]{:S(2)}) %collective-permute-start.9) | collective-permute-done | bytes 65568 | tf_op jit(solution)/shard_map/ppermute | solution.py:30
  27.6 0.5 %collective-permute-start.10 = (bf16[32,256]{1,0:T(8,128)(2,1)S(1)}, bf16[32,256]{1,0:T(8,128)(2,1)S(1)}, u32[]{:S(2)}, u32[]{:S(2)}) collective-permute-start(bf16[32,256]{1,0:T(8,128)(2,1)S(1)} %pad_maximum_fusion.1), channel_id=1, source_target_pairs={{0,8},{4,12},{8,0},{12,4},{16,24},{20,28},{24,16},{28,20},{1,9},{5... | collective-permute-start | bytes 49160 | tf_op jit(solution)/shard_map/ppermute | solution.py:30
  28.2 2.1 %collective-permute-start.11 = (bf16[32,256]{1,0:T(8,128)(2,1)S(1)}, bf16[32,256]{1,0:T(8,128)(2,1)S(1)}, u32[]{:S(2)}, u32[]{:S(2)}) collective-permute-start(bf16[32,256]{1,0:T(8,128)(2,1)S(1)} %pad_maximum_fusion.2), channel_id=1, source_target_pairs={{0,16},{4,20},{8,24},{12,28},{16,0},{20,4},{24,8},{28,12},{1,17},{... | collective-permute-start | bytes 49160 | tf_op jit(solution)/shard_map/ppermute | solution.py:30
  30.3 1.5 %collective-permute-start.12 = (bf16[32,256]{1,0:T(8,128)(2,1)S(1)}, bf16[32,256]{1,0:T(8,128)(2,1)S(1)}, u32[]{:S(2)}, u32[]{:S(2)}) collective-permute-start(bf16[32,256]{1,0:T(8,128)(2,1)S(1)} %pad_maximum_fusion.3), channel_id=1, source_target_pairs={{0,24},{4,28},{8,16},{12,20},{16,8},{20,12},{24,0},{28,4},{1,25},{... | collective-permute-start | bytes 49160 | tf_op jit(solution)/shard_map/ppermute | solution.py:30
  31.8 1.8 %collective-permute-done.11.refs_2_.refs_1_ = bf16[32,256]{1,0:T(8,128)(2,1)S(1)} collective-permute-done((bf16[32,256]{1,0:T(8,128)(2,1)S(1)}, bf16[32,256]{1,0:T(8,128)(2,1)S(1)}, u32[]{:S(2)}, u32[]{:S(2)}) %collective-permute-start.11) | collective-permute-done | bytes 16416 | tf_op jit(solution)/shard_map/ppermute | solution.py:30
  33.6 1.4 %collective-permute-done.12.refs_3_.refs_0_ = bf16[32,256]{1,0:T(8,128)(2,1)S(1)} collective-permute-done((bf16[32,256]{1,0:T(8,128)(2,1)S(1)}, bf16[32,256]{1,0:T(8,128)(2,1)S(1)}, u32[]{:S(2)}, u32[]{:S(2)}) %collective-permute-start.12) | collective-permute-done | bytes 16416 | tf_op jit(solution)/shard_map/ppermute | solution.py:30
  35.0 1.0 %out_project.1 = (f32[4,4,4,1792]{3,2,1,0:T(4,128)S(1)}, bf16[4,4,4,1792]{3,2,1,0:T(4,128)(2,1)S(1)}) custom-call(bf16[32,256]{1,0:T(8,128)(2,1)S(1)} %pad_maximum_fusion.refs_0_.refs_3_, bf16[32,256]{1,0:T(8,128)(2,1)S(1)} %collective-permute-done.10.refs_1_.refs_2_, bf16[32,256]{1,0:T(8,128)(2,1)S(1)} %collective-permute-done.11.refs_2_.refs_1_, ...), custom_call_target="tpu_custom_call" | custom-call | tf_op jit(solution)/shard_map/out_project/pallas_call | solution.py:611
  36.0 0.1 collective-permute-start.14
  36.1 1.5 %collective-permute-done.14 = bf16[4,4,4,1792]{3,2,1,0:T(4,128)(2,1)S(1)} collective-permute-done((bf16[4,4,4,1792]{3,2,1,0:T(4,128)(2,1)S(1)}, bf16[4,4,4,1792]{3,2,1,0:T(4,128)(2,1)S(1)}, u32[]{:S(2)}, u32[]{:S(2)}) %collective-permute-start.14) | collective-permute-done | bytes 229408 | tf_op jit(solution)/shard_map/ppermute | solution.py:30
  37.6 0.2 fusion.11
  37.7 0.1 slice_bitcast_fusion.3
  37.8 1.5 %collective-permute-start.15 = (bf16[4,4,1792]{2,1,0:T(4,128)(2,1)S(1)}, bf16[4,4,1792]{2,1,0:T(4,128)(2,1)S(1)}, u32[]{:S(2)}, u32[]{:S(2)}) collective-permute-start(bf16[4,4,1792]{2,1,0:T(4,128)(2,1)S(1)} %get-tuple-element.69), channel_id=1, source_target_pairs={{0,24},{4,28},{8,16},{12,20},{16,8},{20,12},{24,0},{28,4},{1,25},{... | collective-permute-start | bytes 172040 | tf_op jit(solution)/shard_map/ppermute | solution.py:30
  39.3 0.9 %collective-permute-start.17 = (bf16[4,4,1792]{2,1,0:T(4,128)(2,1)S(1)}, bf16[4,4,1792]{2,1,0:T(4,128)(2,1)S(1)}, u32[]{:S(2)}, u32[]{:S(2)}) collective-permute-start(bf16[4,4,1792]{2,1,0:T(4,128)(2,1)S(1)} %get-tuple-element.70), channel_id=1, source_target_pairs={{0,8},{4,12},{8,0},{12,4},{16,24},{20,28},{24,16},{28,20},{1,9},{5... | collective-permute-start | bytes 172040 | tf_op jit(solution)/shard_map/ppermute | solution.py:30
  40.2 1.2 %collective-permute-start.16 = (bf16[4,4,1792]{2,1,0:T(4,128)(2,1)S(1)}, bf16[4,4,1792]{2,1,0:T(4,128)(2,1)S(1)}, u32[]{:S(2)}, u32[]{:S(2)}) collective-permute-start(bf16[4,4,1792]{2,1,0:T(4,128)(2,1)S(1)} %get-tuple-element.71), channel_id=1, source_target_pairs={{0,16},{4,20},{8,24},{12,28},{16,0},{20,4},{24,8},{28,12},{1,17},{... | collective-permute-start | bytes 172040 | tf_op jit(solution)/shard_map/ppermute | solution.py:30
  41.4 0.2 choose_page.1
  41.5 0.1 collective-permute-start.18
  41.6 2.2 %write_pool.1.refs_10_ = bf16[20,64,1792]{2,1,0:T(8,128)(2,1)} custom-call(bf16[20,64,1792]{2,1,0:T(8,128)(2,1)S(1)} %bitcast.63, f32[4,4,4,1792]{3,2,1,0:T(4,128)S(1)} %get-tuple-element.68._), custom_call_target="tpu_custom_call" | custom-call | tf_op jit(solution)/shard_map/write_pool/pallas_call | solution.py:51
  43.8 0.6 %collective-permute-done.16 = bf16[4,4,1792]{2,1,0:T(4,128)(2,1)S(1)} collective-permute-done((bf16[4,4,1792]{2,1,0:T(4,128)(2,1)S(1)}, bf16[4,4,1792]{2,1,0:T(4,128)(2,1)S(1)}, u32[]{:S(2)}, u32[]{:S(2)}) %collective-permute-start.16) | collective-permute-done | bytes 57376 | tf_op jit(solution)/shard_map/ppermute | solution.py:30
  44.5 3.7 %collective-permute-start.19 = (bf16[4,1792]{1,0:T(4,128)(2,1)S(1)}, bf16[4,1792]{1,0:T(4,128)(2,1)S(1)}, u32[]{:S(2)}, u32[]{:S(2)}) collective-permute-start(bf16[4,1792]{1,0:T(4,128)(2,1)S(1)} %get-tuple-element.84), channel_id=1, source_target_pairs={{0,3},{1,2},{2,1},{3,0},{4,7},{5,6},{6,5},{7,4},{8,11},{9,10},{10,... | collective-permute-start | bytes 43016 | tf_op jit(solution)/shard_map/ppermute | solution.py:30
  48.2 0.8 %collective-permute-start.20 = (bf16[4,1792]{1,0:T(4,128)(2,1)S(1)}, bf16[4,1792]{1,0:T(4,128)(2,1)S(1)}, u32[]{:S(2)}, u32[]{:S(2)}) collective-permute-start(bf16[4,1792]{1,0:T(4,128)(2,1)S(1)} %get-tuple-element.86), channel_id=1, source_target_pairs={{0,1},{1,0},{2,3},{3,2},{4,5},{5,4},{6,7},{7,6},{8,9},{9,8},{10,11... | collective-permute-start | bytes 43016 | tf_op jit(solution)/shard_map/ppermute | solution.py:30
  49.0 1.7 %place_page.1 = (f32[4,1792]{1,0:T(4,128)S(1)}, bf16[20,64,1792]{2,1,0:T(8,128)(2,1)}, bf16[20,64,1792]{2,1,0:T(8,128)(2,1)}) custom-call(s32[4]{0:T(128)S(1)} %copy-done.4, s32[4]{0:T(128)S(1)} %copy-done.3, s32[4,16]{1,0:T(4,128)S(1)} %copy-done.2, f32[8,128]{1,0:T(8,128)S(1)} %find_sources.1.source_ref, ...), custom_call_target="tpu_custom_call", output_to_operand_aliasing={{1}: (15, {}), {2}: (16, {})} | custom-call | tf_op jit(solution)/shard_map/place_page/pallas_call | solution.py:707
  50.7 2.1 %collective-permute-done.21 = bf16[4,1792]{1,0:T(4,128)(2,1)S(1)} collective-permute-done((bf16[4,1792]{1,0:T(4,128)(2,1)S(1)}, bf16[4,1792]{1,0:T(4,128)(2,1)S(1)}, u32[]{:S(2)}, u32[]{:S(2)}) %collective-permute-start.21) | collective-permute-done | bytes 14368 | tf_op jit(solution)/shard_map/ppermute | solution.py:30
  52.8 0.6 %fusion.6 = bf16[4,1792]{1,0:T(4,128)(2,1)} fusion(f32[4,1792]{1,0:T(4,128)S(1)} %get-tuple-element.64, bf16[4,1792]{1,0:T(4,128)(2,1)S(1)} %collective-permute-done.21, bf16[4,1792]{1,0:T(4,128)(2,1)S(1)} %collective-permute-done.20, bf16[4,1792]{1,0:T(4,128)(2,1)S(1)} %collective-permute-done.19, f32[4,4,1792]{2,1,0:T(4,128)S(1)} %fusion.2), kind=kLoop, calls=%fused_computation.12 | loop fusion | flops 57344 | bytes 114688 | tf_op jit(solution)/shard_map/convert_element_type | solution.py:813
  (44 shorter events, 0.3 us)
Async XLA Ops:
  0.6 1.6 %collective-permute-start = (bf16[4,7168]{1,0:T(4,128)(2,1)}, bf16[4,7168]{1,0:T(4,128)(2,1)S(1)}, u32[]{:S(2)}, u32[]{:S(2)}) collective-permute-start(bf16[4,7168]{1,0:T(4,128)(2,1)} %token_ref.1), channel_id=1, source_target_pairs={{0,4},{4,0},{8,12},{12,8},{16,20},{20,16},{24,28},{28,24},{1,5},{5... | collective-permute-start | bytes 172040 | tf_op jit(solution)/shard_map/ppermute | solution.py:30
  2.6 6.8 %collective-permute-start.3 = (bf16[2,4,1024]{2,1,0:T(4,128)(2,1)S(1)}, bf16[2,4,1024]{2,1,0:T(4,128)(2,1)S(1)}, u32[]{:S(2)}, u32[]{:S(2)}) collective-permute-start(bf16[2,4,1024]{2,1,0:T(4,128)(2,1)S(1)} %get-tuple-element.39.refs_0_), channel_id=1, source_target_pairs={{0,24},{4,28},{8,16},{12,20},{16,8},{20,12},{24,0},{28,4},{1,25},{... | collective-permute-start | bytes 49160 | tf_op jit(solution)/shard_map/ppermute | solution.py:30
  6.5 3.7 %collective-permute-start.2 = (bf16[2,4,1024]{2,1,0:T(4,128)(2,1)S(1)}, bf16[2,4,1024]{2,1,0:T(4,128)(2,1)S(1)}, u32[]{:S(2)}, u32[]{:S(2)}) collective-permute-start(bf16[2,4,1024]{2,1,0:T(4,128)(2,1)S(1)} %get-tuple-element.40.refs_1_), channel_id=1, source_target_pairs={{0,16},{4,20},{8,24},{12,28},{16,0},{20,4},{24,8},{28,12},{1,17},{... | collective-permute-start | bytes 49160 | tf_op jit(solution)/shard_map/ppermute | solution.py:30
  7.0 3.7 %collective-permute-start.1 = (bf16[2,4,1024]{2,1,0:T(4,128)(2,1)S(1)}, bf16[2,4,1024]{2,1,0:T(4,128)(2,1)S(1)}, u32[]{:S(2)}, u32[]{:S(2)}) collective-permute-start(bf16[2,4,1024]{2,1,0:T(4,128)(2,1)S(1)} %get-tuple-element.41.refs_2_), channel_id=1, source_target_pairs={{0,8},{4,12},{8,0},{12,4},{16,24},{20,28},{24,16},{28,20},{1,9},{5... | collective-permute-start | bytes 49160 | tf_op jit(solution)/shard_map/ppermute | solution.py:30
  7.1 4.3 %copy-start = (bf16[896,14,384]{2,0,1:T(8,128)(2,1)S(1)}, bf16[896,14,384]{2,0,1:T(8,128)(2,1)}, u32[]{:S(2)}) copy-start(bf16[896,14,384]{2,0,1:T(8,128)(2,1)} %param.16) | copy-start | bytes 28901380
  10.7 8.7 %collective-permute-start.8 = (bf16[2,64,1792]{2,1,0:T(8,128)(2,1)S(1)}, bf16[2,64,1792]{2,1,0:T(8,128)(2,1)S(1)}, u32[]{:S(2)}, u32[]{:S(2)}) collective-permute-start(bf16[2,64,1792]{2,1,0:T(8,128)(2,1)S(1)} %pick_page.1.refs_0_.refs_6_), channel_id=1, source_target_pairs={{0,8},{4,20},{8,0},{12,28},{16,24},{20,4},{24,16},{28,12},{1,9},{5... | collective-permute-start | bytes 1376264 | tf_op jit(solution)/shard_map/ppermute | solution.py:187
  11.4 11.9 %slice-start = ((s8[4587520]{0:T(1024)(128)(4,1)}), s8[4194304]{0:T(1024)(128)(4,1)S(1)}, s32[]{:S(2)}) async-start(s8[4587520]{0:T(1024)(128)(4,1)} %bitcast.62), calls=%async_computation | async-start | bytes 8388608
  11.4 11.9 %slice-start.2 = ((s8[4587520]{0:T(1024)(128)(4,1)}), s8[4194304]{0:T(1024)(128)(4,1)S(1)}, s32[]{:S(2)}) async-start(s8[4587520]{0:T(1024)(128)(4,1)} %bitcast.64), calls=%async_computation.2 | async-start | bytes 8388608
  11.4 7.7 %copy-start.5 = (f32[14,384]{1,0:T(8,128)S(1)}, f32[14,384]{1,0:T(8,128)}, u32[]{:S(2)}) copy-start(f32[14,384]{1,0:T(8,128)} %param.17) | copy-start | bytes 64516
  11.4 11.9 %slice-start.1 = ((s8[4587520]{0:T(1024)(128)(4,1)}), s8[393216]{0:T(1024)(128)(4,1)S(1)}, s32[]{:S(2)}) async-start(s8[4587520]{0:T(1024)(128)(4,1)} %bitcast.62), calls=%async_computation.1 | async-start | bytes 786432
  11.4 11.9 %slice-start.3 = ((s8[4587520]{0:T(1024)(128)(4,1)}), s8[393216]{0:T(1024)(128)(4,1)S(1)}, s32[]{:S(2)}) async-start(s8[4587520]{0:T(1024)(128)(4,1)} %bitcast.64), calls=%async_computation.3 | async-start | bytes 786432
  11.4 11.9 %copy-start.2 = (s32[4,16]{1,0:T(4,128)S(1)}, s32[4,16]{1,0:T(4,128)}, u32[]{:S(2)}) copy-start(s32[4,16]{1,0:T(4,128)} %table_ref.3) | copy-start | bytes 772
  11.4 11.9 %copy-start.3 = (s32[4]{0:T(128)S(1)}, s32[4]{0:T(128)}, u32[]{:S(2)}) copy-start(s32[4]{0:T(128)} %slot_ref.5) | copy-start | bytes 52
  11.4 11.9 %copy-start.4 = (s32[4]{0:T(128)S(1)}, s32[4]{0:T(128)}, u32[]{:S(2)}) copy-start(s32[4]{0:T(128)} %length_ref.3) | copy-start | bytes 52
  13.7 1.7 %collective-permute-start.4 = (f32[4,4,5504]{2,1,0:T(4,128)S(1)}, f32[4,4,5504]{2,1,0:T(4,128)S(1)}, u32[]{:S(2)}, u32[]{:S(2)}) collective-permute-start(f32[4,4,5504]{2,1,0:T(4,128)S(1)} %get-tuple-element.48), channel_id=1, source_target_pairs={{0,4},{4,0},{8,12},{12,8},{16,20},{20,16},{24,28},{28,24},{1,5},{5... | collective-permute-start | bytes 1056776 | tf_op jit(solution)/shard_map/ppermute | solution.py:30
  15.5 6.2 %collective-permute-start.5 = (bf16[4,7168]{1,0:T(4,128)(2,1)S(1)}, bf16[4,7168]{1,0:T(4,128)(2,1)S(1)}, u32[]{:S(2)}, u32[]{:S(2)}) collective-permute-start(bf16[4,7168]{1,0:T(4,128)(2,1)S(1)} %get-tuple-element.49), channel_id=1, source_target_pairs={{0,24},{4,28},{8,16},{12,20},{16,8},{20,12},{24,0},{28,4},{1,25},{... | collective-permute-start | bytes 172040 | tf_op jit(solution)/shard_map/ppermute | solution.py:30
  18.1 4.3 %collective-permute-start.6 = (bf16[4,7168]{1,0:T(4,128)(2,1)S(1)}, bf16[4,7168]{1,0:T(4,128)(2,1)S(1)}, u32[]{:S(2)}, u32[]{:S(2)}) collective-permute-start(bf16[4,7168]{1,0:T(4,128)(2,1)S(1)} %get-tuple-element.50), channel_id=1, source_target_pairs={{0,16},{4,20},{8,24},{12,28},{16,0},{20,4},{24,8},{28,12},{1,17},{... | collective-permute-start | bytes 172040 | tf_op jit(solution)/shard_map/ppermute | solution.py:30
  18.6 4.7 %collective-permute-start.7 = (bf16[4,7168]{1,0:T(4,128)(2,1)S(1)}, bf16[4,7168]{1,0:T(4,128)(2,1)S(1)}, u32[]{:S(2)}, u32[]{:S(2)}) collective-permute-start(bf16[4,7168]{1,0:T(4,128)(2,1)S(1)} %get-tuple-element.51), channel_id=1, source_target_pairs={{0,8},{4,12},{8,0},{12,4},{16,24},{20,28},{24,16},{28,20},{1,9},{5... | collective-permute-start | bytes 172040 | tf_op jit(solution)/shard_map/ppermute | solution.py:30
  19.8 15.2 %collective-permute-start.13 = (bf16[2,2,64,1792]{3,2,1,0:T(8,128)(2,1)S(1)}, bf16[2,2,64,1792]{3,2,1,0:T(8,128)(2,1)S(1)}, u32[]{:S(2)}, u32[]{:S(2)}) collective-permute-start(bf16[2,2,64,1792]{3,2,1,0:T(8,128)(2,1)S(1)} %turn_pages.1.refs_11_), channel_id=1, source_target_pairs={{0,16},{4,12},{8,24},{12,4},{16,0},{20,28},{24,8},{28,20},{1,17},{... | collective-permute-start | bytes 2752520 | tf_op jit(solution)/shard_map/ppermute | solution.py:187
  26.3 1.3 %collective-permute-start.9 = (bf16[4,32,256]{2,1,0:T(8,128)(2,1)S(1)}, bf16[4,32,256]{2,1,0:T(8,128)(2,1)S(1)}, u32[]{:S(2)}, u32[]{:S(2)}) collective-permute-start(bf16[4,32,256]{2,1,0:T(8,128)(2,1)S(1)} %get-tuple-element.55), channel_id=1, source_target_pairs={{0,4},{4,0},{8,12},{12,8},{16,20},{20,16},{24,28},{28,24},{1,5},{5... | collective-permute-start | bytes 196616 | tf_op jit(solution)/shard_map/ppermute | solution.py:30
  27.6 4.2 %collective-permute-start.10 = (bf16[32,256]{1,0:T(8,128)(2,1)S(1)}, bf16[32,256]{1,0:T(8,128)(2,1)S(1)}, u32[]{:S(2)}, u32[]{:S(2)}) collective-permute-start(bf16[32,256]{1,0:T(8,128)(2,1)S(1)} %pad_maximum_fusion.1), channel_id=1, source_target_pairs={{0,8},{4,12},{8,0},{12,4},{16,24},{20,28},{24,16},{28,20},{1,9},{5... | collective-permute-start | bytes 49160 | tf_op jit(solution)/shard_map/ppermute | solution.py:30
  28.2 5.4 %collective-permute-start.11 = (bf16[32,256]{1,0:T(8,128)(2,1)S(1)}, bf16[32,256]{1,0:T(8,128)(2,1)S(1)}, u32[]{:S(2)}, u32[]{:S(2)}) collective-permute-start(bf16[32,256]{1,0:T(8,128)(2,1)S(1)} %pad_maximum_fusion.2), channel_id=1, source_target_pairs={{0,16},{4,20},{8,24},{12,28},{16,0},{20,4},{24,8},{28,12},{1,17},{... | collective-permute-start | bytes 49160 | tf_op jit(solution)/shard_map/ppermute | solution.py:30
  30.3 4.7 %collective-permute-start.12 = (bf16[32,256]{1,0:T(8,128)(2,1)S(1)}, bf16[32,256]{1,0:T(8,128)(2,1)S(1)}, u32[]{:S(2)}, u32[]{:S(2)}) collective-permute-start(bf16[32,256]{1,0:T(8,128)(2,1)S(1)} %pad_maximum_fusion.3), channel_id=1, source_target_pairs={{0,24},{4,28},{8,16},{12,20},{16,8},{20,12},{24,0},{28,4},{1,25},{... | collective-permute-start | bytes 49160 | tf_op jit(solution)/shard_map/ppermute | solution.py:30
  36.0 1.6 %collective-permute-start.14 = (bf16[4,4,4,1792]{3,2,1,0:T(4,128)(2,1)S(1)}, bf16[4,4,4,1792]{3,2,1,0:T(4,128)(2,1)S(1)}, u32[]{:S(2)}, u32[]{:S(2)}) collective-permute-start(bf16[4,4,4,1792]{3,2,1,0:T(4,128)(2,1)S(1)} %get-tuple-element.58), channel_id=1, source_target_pairs={{0,4},{4,0},{8,12},{12,8},{16,20},{20,16},{24,28},{28,24},{1,5},{5... | collective-permute-start | bytes 688136 | tf_op jit(solution)/shard_map/ppermute | solution.py:30
  37.8 6.0 %collective-permute-start.15 = (bf16[4,4,1792]{2,1,0:T(4,128)(2,1)S(1)}, bf16[4,4,1792]{2,1,0:T(4,128)(2,1)S(1)}, u32[]{:S(2)}, u32[]{:S(2)}) collective-permute-start(bf16[4,4,1792]{2,1,0:T(4,128)(2,1)S(1)} %get-tuple-element.69), channel_id=1, source_target_pairs={{0,24},{4,28},{8,16},{12,20},{16,8},{20,12},{24,0},{28,4},{1,25},{... | collective-permute-start | bytes 172040 | tf_op jit(solution)/shard_map/ppermute | solution.py:30
  39.3 4.5 %collective-permute-start.17 = (bf16[4,4,1792]{2,1,0:T(4,128)(2,1)S(1)}, bf16[4,4,1792]{2,1,0:T(4,128)(2,1)S(1)}, u32[]{:S(2)}, u32[]{:S(2)}) collective-permute-start(bf16[4,4,1792]{2,1,0:T(4,128)(2,1)S(1)} %get-tuple-element.70), channel_id=1, source_target_pairs={{0,8},{4,12},{8,0},{12,4},{16,24},{20,28},{24,16},{28,20},{1,9},{5... | collective-permute-start | bytes 172040 | tf_op jit(solution)/shard_map/ppermute | solution.py:30
  40.2 4.2 %collective-permute-start.16 = (bf16[4,4,1792]{2,1,0:T(4,128)(2,1)S(1)}, bf16[4,4,1792]{2,1,0:T(4,128)(2,1)S(1)}, u32[]{:S(2)}, u32[]{:S(2)}) collective-permute-start(bf16[4,4,1792]{2,1,0:T(4,128)(2,1)S(1)} %get-tuple-element.71), channel_id=1, source_target_pairs={{0,16},{4,20},{8,24},{12,28},{16,0},{20,4},{24,8},{28,12},{1,17},{... | collective-permute-start | bytes 172040 | tf_op jit(solution)/shard_map/ppermute | solution.py:30
  41.5 2.9 %collective-permute-start.18 = (bf16[2,64,1792]{2,1,0:T(8,128)(2,1)S(1)}, bf16[2,64,1792]{2,1,0:T(8,128)(2,1)S(1)}, u32[]{:S(2)}, u32[]{:S(2)}) collective-permute-start(bf16[2,64,1792]{2,1,0:T(8,128)(2,1)S(1)} %choose_page.1), channel_id=1, source_target_pairs={{0,4},{4,0},{8,12},{12,8},{16,20},{20,16},{24,28},{28,24},{1,5},{5... | collective-permute-start | bytes 1376264 | tf_op jit(solution)/shard_map/ppermute | solution.py:30
  41.6 7.3 %copy-start.1 = (f32[7168]{0:T(1024)S(1)}, f32[7168]{0:T(1024)}, u32[]{:S(2)}) copy-start(f32[7168]{0:T(1024)} %param.19) | copy-start | bytes 86020
  44.5 6.1 %collective-permute-start.19 = (bf16[4,1792]{1,0:T(4,128)(2,1)S(1)}, bf16[4,1792]{1,0:T(4,128)(2,1)S(1)}, u32[]{:S(2)}, u32[]{:S(2)}) collective-permute-start(bf16[4,1792]{1,0:T(4,128)(2,1)S(1)} %get-tuple-element.84), channel_id=1, source_target_pairs={{0,3},{1,2},{2,1},{3,0},{4,7},{5,6},{6,5},{7,4},{8,11},{9,10},{10,... | collective-permute-start | bytes 43016 | tf_op jit(solution)/shard_map/ppermute | solution.py:30
  48.2 4.6 %collective-permute-start.21 = (bf16[4,1792]{1,0:T(4,128)(2,1)S(1)}, bf16[4,1792]{1,0:T(4,128)(2,1)S(1)}, u32[]{:S(2)}, u32[]{:S(2)}) collective-permute-start(bf16[4,1792]{1,0:T(4,128)(2,1)S(1)} %get-tuple-element.85), channel_id=1, source_target_pairs={{0,2},{1,3},{2,0},{3,1},{4,6},{5,7},{6,4},{7,5},{8,10},{9,11},{10,... | collective-permute-start | bytes 43016 | tf_op jit(solution)/shard_map/ppermute | solution.py:30
  48.2 4.6 %collective-permute-start.20 = (bf16[4,1792]{1,0:T(4,128)(2,1)S(1)}, bf16[4,1792]{1,0:T(4,128)(2,1)S(1)}, u32[]{:S(2)}, u32[]{:S(2)}) collective-permute-start(bf16[4,1792]{1,0:T(4,128)(2,1)S(1)} %get-tuple-element.86), channel_id=1, source_target_pairs={{0,1},{1,0},{2,3},{3,2},{4,5},{5,4},{6,7},{7,6},{8,9},{9,8},{10,11... | collective-permute-start | bytes 43016 | tf_op jit(solution)/shard_map/ppermute | solution.py:30
